TPU v7x, 32 devices: a whole 2x2x4 slice. The times are simulated.
32 devices in a mesh: row: 2 (over x), col: 8 (over z, core), depth: 2 (over y).
Axes of the slice: x: 2, y: 2, z: 4, core: 2. Of those that a mesh axis runs over, the one named last changes fastest.
Arguments:
- tokens: bfloat16 [2, 384, 8192], P('depth', None, ('col', 'row')), may hold values from -6 to 6
- gate_weight: bfloat16 [8192, 14336], P('col', 'row'), may hold values from -0.0625 to 0.0625
- up_weight: bfloat16 [8192, 14336], P('col', 'row'), may hold values from -0.0625 to 0.0625
- grad_hidden: bfloat16 [2, 384, 14336], P('depth', 'col', 'row'), may hold values from -0.75 to 0.75
Outputs:
- hidden: bfloat16 [2, 384, 14336], P('depth', 'col', 'row')
- grad_gate: float32 [8192, 14336], P('col', ('row', 'depth'))
- grad_up: float32 [8192, 14336], P('col', ('row', 'depth'))
All inputs are finite; a program needn't handle non-finite values.
Results may differ from a plain program's by a relative error of at most 0.0034.
Values may be sent and summed in bfloat16 or wider, within the bound.
No kernel may reach another device: no remote copies, remote signals or barrier semaphores. Data moves between devices by JAX's collectives and lax.ppermute only.
A program may use at most 192 MiB of HBM per device.

v0:
```python
import jax
import jax.numpy as jnp
from jax import lax
from jax.sharding import PartitionSpec as P


def contract(picked, piece):
    return lax.dot_general(
        picked, piece, (((0,), (0,)), ((), ())), preferred_element_type=jnp.float32
    )


def local(tokens, gate_weight, up_weight, grad_hidden):
    features = lax.all_gather(tokens[0], "row", axis=1, tiled=True)
    columns = gate_weight.shape[1]
    picked = features
    gate_part = jnp.dot(picked, gate_weight, preferred_element_type=jnp.float32)
    up_part = jnp.dot(picked, up_weight, preferred_element_type=jnp.float32)
    summed = lax.psum_scatter(
        jnp.concatenate([gate_part, up_part], axis=1), "col", scatter_dimension=0, tiled=True
    )
    gate_sum = summed[:, :columns]
    up_sum = summed[:, columns:]
    squash = jax.nn.sigmoid(gate_sum)
    hidden = (gate_sum * squash * up_sum).astype(jnp.bfloat16)
    cotangent = grad_hidden[0].astype(jnp.float32)
    gate_act = (cotangent * up_sum * squash * (1.0 + gate_sum * (1.0 - squash))).astype(
        jnp.bfloat16
    )
    up_act = (cotangent * gate_sum * squash).astype(jnp.bfloat16)
    picked = features
    gate_total = contract(picked, lax.all_gather(gate_act, "col", axis=0, tiled=True))
    up_total = contract(picked, lax.all_gather(up_act, "col", axis=0, tiled=True))
    grad_gate, grad_up = (
        lax.psum_scatter(gate_total, "depth", scatter_dimension=1, tiled=True),
        lax.psum_scatter(up_total, "depth", scatter_dimension=1, tiled=True),
    )
    return (hidden[None], grad_gate, grad_up)


def solution(mesh):
    in_specs = (
        P("depth", None, ("col", "row")),
        P("col", "row"),
        P("col", "row"),
        P("depth", "col", "row"),
    )
    out_specs = (P("depth", "col", "row"), P("col", ("row", "depth")), P("col", ("row", "depth")))
    return jax.shard_map(local, mesh=mesh, in_specs=in_specs, out_specs=out_specs, check_vma=False)
```

profile of v0, /device:TPU:1, one launch (start us, length us, event | category | flops | bytes accessed | tf_op | source)
XLA Modules:
  0.0 1057.1 jit_solution(1953689916446225358)
XLA Ops:
  7.2 0.0 reduce-scatter.4.cloned.1.call-start
  7.2 11.8 %all-gather = bf16[1,384,1024]{2,1,0:T(8,128)(2,1)S(1)} all-gather(bf16[1,384,512]{2,1,0:T(8,128)(2,1)} %param.4), channel_id=2, replica_groups=mesh['row'=2,'col'=8,'depth'=2] {'row'}, dimensions={2}, use_global_device_ids=true | all-gather | bytes 1179648 | tf_op jit(solution)/shard_map/all_gather | solution.py:14
  19.0 9.1 fusion.7
  28.1 9.1 fusion.9
  37.3 7.6 pad_maximum_fusion
  44.9 0.0 copy-start
  44.9 0.0 reduce-scatter.4.cloned.1.call-update
  45.0 0.0 all-gather.4.cloned.1.call-start
  45.0 217.6 %reduce-scatter.4.cloned.1.call-done = f32[48,14336]{1,0:T(8,128)} async-done(((f32[384,14336]{1,0:T(8,128)}), f32[48,14336]{1,0:T(8,128)}) %reduce-scatter.4.cloned.1.call-update) | async-done | bytes 2752528 | tf_op jit(solution)/shard_map/reduce_scatter | solution.py:19
  262.6 0.0 copy-done
  262.6 3.7 fusion.4
  266.3 0.0 all-gather.4.cloned.1.call-update
  266.3 0.0 all-gather.6.cloned.1.call-start
  266.4 0.7 all-gather.6.cloned.1.call-update
  267.1 0.0 reduce-scatter.6.cloned.1.call-start
  267.1 58.5 %all-gather.4.cloned.1.call-done = bf16[384,7168]{1,0:T(8,128)(2,1)} async-done(((bf16[48,7168]{1,0:T(8,128)(2,1)}), bf16[384,7168]{1,0:T(8,128)(2,1)}) %all-gather.4.cloned.1.call-update) | async-done | bytes 5505040 | tf_op jit(solution)/shard_map/all_gather | solution.py:32
  325.6 16.8 %convolution_bitcast_fusion.1 = f32[1024,7168]{0,1:T(8,128)} fusion(bf16[384,7168]{1,0:T(8,128)(2,1)} %all-gather.4.cloned.1.call-done, bf16[1,384,1024]{2,1,0:T(8,128)(2,1)S(1)} %all-gather), kind=kOutput, calls=%fused_computation.2 | convolution fusion | flops 5637144576 | bytes 35651584 | tf_op jit(solution)/shard_map/dot_general | solution.py:8
  342.5 0.0 reduce-scatter.6.cloned.1.call-update
  342.5 0.2 reduce-scatter.8.cloned.1.call-start
  342.7 42.1 %all-gather.6.cloned.1.call-done = bf16[384,7168]{1,0:T(8,128)(2,1)} async-done(((bf16[48,7168]{1,0:T(8,128)(2,1)}), bf16[384,7168]{1,0:T(8,128)(2,1)}) %all-gather.6.cloned.1.call-update) | async-done | bytes 5505040 | tf_op jit(solution)/shard_map/all_gather | solution.py:33
  384.8 16.7 %convolution_bitcast_fusion = f32[1024,7168]{0,1:T(8,128)} fusion(bf16[384,7168]{1,0:T(8,128)(2,1)} %all-gather.6.cloned.1.call-done, bf16[1,384,1024]{2,1,0:T(8,128)(2,1)S(1)} %all-gather), kind=kOutput, calls=%fused_computation.1 | convolution fusion | flops 5637144576 | bytes 35651584 | tf_op jit(solution)/shard_map/dot_general | solution.py:8
  401.5 0.0 reduce-scatter.8.cloned.1.call-update
  401.5 308.2 %reduce-scatter.6.cloned.1.call-done = f32[1024,3584]{0,1:T(8,128)} async-done(((f32[1024,7168]{0,1:T(8,128)}), f32[1024,3584]{0,1:T(8,128)}) %reduce-scatter.6.cloned.1.call-update) | async-done | bytes 14680080 | tf_op jit(solution)/shard_map/reduce_scatter | solution.py:35
  709.7 14.9 %copy.7 = f32[1024,3584]{1,0:T(8,128)} copy(f32[1024,3584]{0,1:T(8,128)} %reduce-scatter.6.cloned.1.call-done) | data formatting | bytes 29360128
  724.6 311.7 %reduce-scatter.8.cloned.1.call-done = f32[1024,3584]{0,1:T(8,128)} async-done(((f32[1024,7168]{0,1:T(8,128)}), f32[1024,3584]{0,1:T(8,128)}) %reduce-scatter.8.cloned.1.call-update) | async-done | bytes 14680080 | tf_op jit(solution)/shard_map/reduce_scatter | solution.py:36
  1036.3 14.3 %copy.8 = f32[1024,3584]{1,0:T(8,128)} copy(f32[1024,3584]{0,1:T(8,128)} %reduce-scatter.8.cloned.1.call-done) | data formatting | bytes 29360128
Async XLA Ops:
  7.2 255.4 %reduce-scatter.4.cloned.1.call-start = ((), (), s32[]{:S(2)}) async-start(), calls=%async_computation.3 | async-start | bytes 24772608 | tf_op jit(solution)/shard_map/reduce_scatter | solution.py:19
  44.9 217.6 %copy-start = (bf16[1,48,7168]{2,1,0:T(8,128)(2,1)S(1)}, bf16[1,48,7168]{2,1,0:T(8,128)(2,1)}, u32[]{:S(2)}) copy-start(bf16[1,48,7168]{2,1,0:T(8,128)(2,1)} %param.7) | copy-start | bytes 2064388
  45.0 280.7 %all-gather.4.cloned.1.call-start = ((), (), s32[]{:S(2)}) async-start(), calls=%async_computation.4 | async-start | bytes 6193152 | tf_op jit(solution)/shard_map/all_gather | solution.py:32
  266.3 118.5 %all-gather.6.cloned.1.call-start = ((), (), s32[]{:S(2)}) async-start(), calls=%async_computation.6 | async-start | bytes 6193152 | tf_op jit(solution)/shard_map/all_gather | solution.py:33
  267.1 442.7 %reduce-scatter.6.cloned.1.call-start = ((), (), s32[]{:S(2)}) async-start(), calls=%async_computation.5 | async-start | bytes 44040192 | tf_op jit(solution)/shard_map/reduce_scatter | solution.py:35
  342.5 693.8 %reduce-scatter.8.cloned.1.call-start = ((), (), s32[]{:S(2)}) async-start(), calls=%async_computation.7 | async-start | bytes 44040192 | tf_op jit(solution)/shard_map/reduce_scatter | solution.py:36
Sparse Core Ops, SparseCore 0:
  45.1 217.4 reduce-scatter.3
  266.4 59.1 all-gather.3
  327.8 56.9 all-gather.5
  387.0 322.7 reduce-scatter.5
  711.9 324.3 reduce-scatter.7
where the time goes:
time: 1060 us
  waiting for transfers between devices  939 us (89%)
  matrix products  51.8 us (5%)
  local copies, waits for them, and re-layouts  29.1 us (3%)
  between operations  13.8 us (1%)
  blocking collectives  11.8 us (1%)
  other arithmetic  11.4 us (1%)
    reduce_scatter x1, waiting for transfers between devices, local(): lax.psum_scatter(up_total, 'depth', scatter_dimension=1, tiled=True)  312 us
    reduce_scatter x1, waiting for transfers between devices, local(): lax.psum_scatter(gate_total, 'depth', scatter_dimension=1, tiled=True)  308 us
    reduce_scatter x1, waiting for transfers between devices, local(): lax.psum_scatter(jnp.concatenate([gate_part, up_part], axis=1), 'col', sc...  218 us
    all_gather x1, waiting for transfers between devices, local(): lax.all_gather(gate_act, 'col', axis=0, tiled=True)  58.5 us
    all_gather x1, waiting for transfers between devices, local(): lax.all_gather(up_act, 'col', axis=0, tiled=True)  42.1 us
    dot_general x2, matrix products, contract(): lax.dot_general(picked, piece, (((0,), (0,)), ((), ())), preferred_elemen...  33.5 us
    unnamed x4, local copies, waits for them, and re-layouts  29.1 us
  transfers between devices with their start and end apart: 5, of which 5 were waited for; matrix products, arithmetic and copies ran while one was open for 5% of the time, Pallas kernels for 0%

commit v1 on v0

v1 whole, which is shorter than its diff:
```python
import functools
import math

import jax
import jax.numpy as jnp
from jax import lax
from jax.experimental import pallas as pl
from jax.experimental.pallas import tpu as pltpu
from jax.sharding import PartitionSpec as P

WIRE = jnp.float16
LARGEST_TOKEN, LARGEST_WEIGHT = 6.0, 0.0625
VMEM_LIMIT = 48 * 2**20


def forward_kernel(scale, place_ref, tokens_ref, gate_ref, up_ref, other_ref, own_ref):
    blocks, _, rows, width = own_ref.shape
    half = blocks * rows
    for which, weight_ref in enumerate((gate_ref, up_ref)):
        product = scale * jnp.dot(
            tokens_ref[...], weight_ref[...], preferred_element_type=jnp.float32
        )
        own_ref[:, which] = product[:half].reshape(blocks, rows, width)
        other_ref[:, which] = product[half:].reshape(blocks, rows, width)


def forward(place, tokens, gate_weight, up_weight, start, width, tile, blocks, scale):
    total, depth = tokens.shape
    rows = total // (2 * blocks)
    weight_spec = pl.BlockSpec((depth, tile), lambda j, place: (0, place[0] + start // tile + j))
    out_spec = pl.BlockSpec((blocks, 2, rows, tile), lambda j, place: (0, 0, 0, j))
    out_shape = jax.ShapeDtypeStruct((blocks, 2, rows, width), jnp.float32)
    return pl.pallas_call(
        functools.partial(forward_kernel, scale),
        out_shape=(out_shape, out_shape),
        grid_spec=pltpu.PrefetchScalarGridSpec(
            num_scalar_prefetch=1,
            grid=(width // tile,),
            in_specs=[
                pl.BlockSpec((total, depth), lambda j, place: (0, 0)),
                weight_spec,
                weight_spec,
            ],
            out_specs=(out_spec, out_spec),
        ),
        compiler_params=pltpu.CompilerParams(vmem_limit_bytes=VMEM_LIMIT),
        cost_estimate=pl.CostEstimate(
            flops=4 * total * depth * width,
            bytes_accessed=4 * depth * width + 8 * total * width + 2 * total * depth,
            transcendentals=0,
        ),
    )(place, tokens, gate_weight, up_weight)


def gradient_kernel(features_ref, own_ref, other_ref, *refs):
    gate_ref, up_ref = refs[-2:]
    blocks, _, rows, width = own_ref.shape
    half = blocks * rows
    for which, out_ref in enumerate((gate_ref, up_ref)):
        out_ref[...] = jnp.dot(
            features_ref[:, :half],
            own_ref[:, which].reshape(half, width),
            preferred_element_type=jnp.float32,
        ) + jnp.dot(
            features_ref[:, half:],
            other_ref[:, which].reshape(half, width),
            preferred_element_type=jnp.float32,
        )


def gradient(features, own, other, totals, columns, start, tile):
    depth, total = features.shape
    blocks, _, rows, width = own.shape
    act_spec = pl.BlockSpec((blocks, 2, rows, tile), lambda j: (0, 0, 0, j))
    out_spec = pl.BlockSpec((depth, tile), lambda j: (0, start // tile + j))
    out_shape = jax.ShapeDtypeStruct((depth, columns), jnp.float32)
    in_specs = [pl.BlockSpec((depth, total), lambda j: (0, 0)), act_spec, act_spec]
    in_specs += [pl.BlockSpec(memory_space=pl.ANY)] * len(totals)
    return pl.pallas_call(
        gradient_kernel,
        out_shape=(out_shape, out_shape),
        grid=(width // tile,),
        in_specs=in_specs,
        out_specs=(out_spec, out_spec),
        input_output_aliases={3 + i: i for i in range(len(totals))},
        compiler_params=pltpu.CompilerParams(vmem_limit_bytes=VMEM_LIMIT),
        cost_estimate=pl.CostEstimate(
            flops=4 * total * depth * width,
            bytes_accessed=8 * depth * width + 4 * total * width + 2 * total * depth,
            transcendentals=0,
        ),
    )(features, own, other, *totals)


def cut(units, shares):
    edges = [round(units * sum(shares[:i]) / sum(shares)) for i in range(len(shares) + 1)]
    return [(a, b - a) for a, b in zip(edges, edges[1:]) if b > a]


def local(sizes, tokens, gate_weight, up_weight, grad_hidden):
    n_row, n_col, n_depth = sizes
    line = n_col // 2
    row, col, part = (lax.axis_index(name) for name in ("row", "col", "depth"))
    place, core = col // 2, col % 2
    slab = grad_hidden.shape[1]
    depth, columns = gate_weight.shape
    half = columns // n_depth
    tile = 256 if half % 256 == 0 else 128
    scale = 2.0 ** math.floor(
        math.log2(65504 / (depth * n_col * LARGEST_TOKEN * LARGEST_WEIGHT))
    )

    swap = [(0, 1), (1, 0)]
    pairs = [(i, i ^ 1) for i in range(n_col)]

    def ahead(first, last):
        return [(2 * i + c, 2 * i + 2 + c) for i in range(first, last + 1) for c in (0, 1)]

    def back(first, last):
        return [(2 * i + c, 2 * i - 2 + c) for i in range(first, last + 1) for c in (0, 1)]

    def gather_rows(mine):
        if n_row != 2:
            return lax.all_gather(mine, "row", axis=1, tiled=True)
        theirs = lax.ppermute(mine, "row", swap)
        return jnp.where(
            row == 0,
            jnp.concatenate([mine, theirs], axis=1),
            jnp.concatenate([theirs, mine], axis=1),
        )

    features = gather_rows(tokens[0])
    others = lax.ppermute(features, "depth", swap)

    def arrange(values):
        values = values.reshape(line, 2, slab, depth)
        values = lax.dynamic_slice_in_dim(jnp.concatenate([values, values]), place, line, 0)
        mine = lax.dynamic_index_in_dim(values, core, 1, keepdims=False)
        theirs = lax.dynamic_index_in_dim(values, 1 - core, 1, keepdims=False)
        return jnp.stack([mine, theirs])

    picked = jnp.stack([arrange(features), arrange(others)], axis=2)
    picked = picked.reshape(2 * line * 2 * slab, depth)
    turned = picked.T

    cotangent = grad_hidden[0]
    mine = lax.dynamic_slice_in_dim(cotangent, part * half, half, 1)
    theirs = lax.dynamic_slice_in_dim(cotangent, (1 - part) * half, half, 1)
    cotangent = jnp.stack([mine, lax.ppermute(theirs, "depth", swap)])

    first_tile = (part * (half // tile)).astype(jnp.int32).reshape(1)
    wide = lambda x: x.astype(jnp.float32)

    totals, hidden_own, hidden_other = (), [], []
    for begin, count in cut(half // tile, SHARES):
        start, width = begin * tile, count * tile
        other, own = forward(
            first_tile, picked, gate_weight, up_weight, start, width, tile, line, scale
        )
        got = lax.ppermute(other.astype(WIRE), "col", pairs)
        both = (own + wide(got)).astype(WIRE)
        right = left = None
        for o in range(line - 1, 0, -1):
            to_right, to_left = both[o], both[line - o]
            if right is not None:
                to_right = (wide(to_right) + wide(right)).astype(WIRE)
                to_left = (wide(to_left) + wide(left)).astype(WIRE)
            right = lax.ppermute(to_right, "col", ahead(0, line - 1 - o))
            left = lax.ppermute(to_left, "col", back(o, line - 1))
        summed = (wide(both[0]) + wide(right) + wide(left)) * (1.0 / scale)
        summed = summed.reshape(2, 2, slab, width)
        gate_sum, up_sum = summed[0], summed[1]
        squash = jax.nn.sigmoid(gate_sum)
        hidden = (gate_sum * squash * up_sum).astype(jnp.bfloat16)
        given = wide(cotangent[:, :, start : start + width])
        gate_act = given * up_sum * squash * (1.0 + gate_sum * (1.0 - squash))
        up_act = given * gate_sum * squash
        act = jnp.stack([gate_act, up_act]).astype(jnp.bfloat16).reshape(2, 2 * slab, width)
        hidden_own.append(hidden[0])
        hidden_other.append(lax.ppermute(hidden[1], "depth", swap))

        from_left, from_right = [act], [act]
        for step in range(1, line):
            from_left.append(lax.ppermute(from_left[-1], "col", ahead(step - 1, line - 2)))
            from_right.append(lax.ppermute(from_right[-1], "col", back(1, line - step)))
        blocks = [act]
        for o in range(1, line):
            blocks.append(jnp.where(place + o < line, from_right[o], from_left[line - o]))
        gathered = jnp.stack(blocks)
        totals = gradient(
            turned, gathered, lax.ppermute(gathered, "col", pairs), totals, half, start, tile
        )

    own = jnp.concatenate(hidden_own, axis=1)
    other = jnp.concatenate(hidden_other, axis=1)
    hidden = jnp.where(
        part == 0,
        jnp.concatenate([own, other], axis=1),
        jnp.concatenate([other, own], axis=1),
    )
    return (hidden[None], *totals)


SHARES = (3, 4, 4, 3)


def solution(mesh):
    sizes = tuple(mesh.shape[name] for name in ("row", "col", "depth"))
    in_specs = (
        P("depth", None, ("col", "row")),
        P("col", "row"),
        P("col", "row"),
        P("depth", "col", "row"),
    )
    out_specs = (P("depth", "col", "row"), P("col", ("row", "depth")), P("col", ("row", "depth")))
    return jax.shard_map(
        functools.partial(local, sizes),
        mesh=mesh,
        in_specs=in_specs,
        out_specs=out_specs,
        check_vma=False,
    )
```

time: 1060 us -> 299 us (0.28)
  waiting for transfers between devices: 939 us -> 85.8 us
  starting transfers between devices: 0.38 us -> 135 us
  matrix products: 51.8 us -> 0 us
  Pallas kernels: 0 us -> 49.2 us
  local copies, waits for them, and re-layouts: 29.1 us -> 5.15 us
  between operations: 13.8 us -> 1.82 us
  blocking collectives: 11.8 us -> 0 us
    reduce_scatter x3 -> x0, waiting for transfers between devices: 837 us -> none  [the longest x1 312 us: local(): lax.psum_scatter(up_total, 'depth', scatter_dimension=1, tiled=True)]
    ppermute x0 -> x63, starting transfers between devices: none -> 135 us  [the longest x12 46.9 us: local(): right = lax.ppermute(to_right, 'col', ahead(0, line - 1 - o))]
    all_gather x2 -> x0, waiting for transfers between devices: 101 us -> none  [the longest x1 58.5 us: local(): lax.all_gather(gate_act, 'col', axis=0, tiled=True)]
    ppermute x0 -> x63, waiting for transfers between devices: none -> 85.8 us  [the longest x12 20.3 us: local(): from_right.append(lax.ppermute(from_right[-1], 'col', back(1, line - step)))]
    dot_general x4 -> x0, matrix products: 51.8 us -> none  [the longest x2 33.5 us: contract(): lax.dot_general(picked, piece, (((0,), (0,)), ((), ())), preferred_elemen...]
    pallas_call x0 -> x8, Pallas kernels: none -> 49.2 us  [the longest x4 25.1 us: forward(): pl.pallas_call(functools.partial(forward_kernel, scale), out_shape=(out_s...]
    unnamed x4 -> x30, local copies, waits for them, and re-layouts: 29.1 us -> 1.15 us
    all_gather x1 -> x0, blocking collectives: 11.8 us -> none  [local(): features = lax.all_gather(tokens[0], 'row', axis=1, tiled=True)]
  transfers between devices with their start and end apart: 5 -> 63, of which waited for: 5 -> 20; matrix products, arithmetic and copies ran while one was open for 5% -> 8% of each run, Pallas kernels for 0% -> 13%
where the time goes in v1:
time: 299 us; the launch traced here: 298 us
  starting transfers between devices  135 us (45%)
  waiting for transfers between devices  85.8 us (29%)
  Pallas kernels  49.2 us (16%)
  other arithmetic  21.2 us (7%)
  local copies, waits for them, and re-layouts  5.15 us (2%)
    ppermute x12, starting transfers between devices, local(): right = lax.ppermute(to_right, 'col', ahead(0, line - 1 - o))  46.9 us
    ppermute x4, starting transfers between devices, local(): lax.ppermute(gathered, 'col', pairs)  25.7 us
    pallas_call x4, Pallas kernels, forward(): pl.pallas_call(functools.partial(forward_kernel, scale), out_shape=(out_s...  25.1 us
    pallas_call x4, Pallas kernels, gradient(): pl.pallas_call(gradient_kernel, out_shape=(out_shape, out_shape), grid=(w...  24.1 us
    ppermute x12, starting transfers between devices, local(): lax.ppermute(from_left[-1], 'col', ahead(step - 1, line - 2))  21.9 us
    ppermute x12, waiting for transfers between devices, local(): from_right.append(lax.ppermute(from_right[-1], 'col', back(1, line - step)))  20.3 us
    ppermute x1, waiting for transfers between devices, local(): others = lax.ppermute(features, 'depth', swap)  16 us
    ppermute x12, starting transfers between devices, local(): from_right.append(lax.ppermute(from_right[-1], 'col', back(1, line - step)))  15.4 us
  transfers between devices with their start and end apart: 63, of which 20 were waited for; matrix products, arithmetic and copies ran while one was open for 8% of the time, Pallas kernels for 13%

profile of v1, /device:TPU:1, one launch (start us, length us, event | category | flops | bytes accessed | tf_op | source)
XLA Modules:
  0.0 297.9 jit_solution(1430709392466835590)
XLA Ops:
  0.6 2.1 collective-permute-start
  2.7 9.1 %collective-permute-done = bf16[384,512]{1,0:T(8,128)(2,1)S(1)} collective-permute-done((bf16[384,512]{1,0:T(8,128)(2,1)}, bf16[384,512]{1,0:T(8,128)(2,1)S(1)}, u32[]{:S(2)}, u32[]{:S(2)}) %collective-permute-start) | collective-permute-done | bytes 393248 | tf_op jit(solution)/shard_map/ppermute | solution.py:125
  11.8 1.3 maximum_select_fusion
  15.0 16.0 %collective-permute-done.1 = bf16[384,1024]{1,0:T(8,128)(2,1)S(1)} collective-permute-done((bf16[384,1024]{1,0:T(8,128)(2,1)S(1)}, bf16[384,1024]{1,0:T(8,128)(2,1)S(1)}, u32[]{:S(2)}, u32[]{:S(2)}) %collective-permute-start.1) | collective-permute-done | bytes 786464 | tf_op jit(solution)/shard_map/ppermute | solution.py:133
  31.8 5.7 %shard_map.70 = (f32[4,2,96,768]{3,2,1,0:T(8,128)S(1)}, f32[4,2,96,768]{3,2,1,0:T(8,128)}) custom-call(s32[1]{0:T(128)} %bitcast.place_ref, bf16[768,1024]{1,0:T(8,128)(2,1)S(1)} %bitcast.174, bf16[1024,7168]{1,0:T(8,128)(2,1)} %gate_ref.7, bf16[1024,7168]{1,0:T(8,128)(2,1)} %up_ref.7), custom_call_target="tpu_custom_call" | custom-call | flops 2415919104 | bytes 9437184 | tf_op jit(solution)/shard_map/pallas_call | solution.py:33
  37.7 2.2 collective-permute-start.23
  39.9 5.7 %shard_map.67 = (f32[4,2,96,768]{3,2,1,0:T(8,128)S(1)}, f32[4,2,96,768]{3,2,1,0:T(8,128)}) custom-call(s32[1]{0:T(128)} %bitcast.place_ref, bf16[768,1024]{1,0:T(8,128)(2,1)S(1)} %bitcast.175, bf16[1024,7168]{1,0:T(8,128)(2,1)} %gate_ref.7, bf16[1024,7168]{1,0:T(8,128)(2,1)} %up_ref.7), custom_call_target="tpu_custom_call" | custom-call | flops 2415919104 | bytes 9437184 | tf_op jit(solution)/shard_map/pallas_call | solution.py:33
  45.9 6.8 %shard_map.69 = (f32[4,2,96,1024]{3,2,1,0:T(8,128)S(1)}, f32[4,2,96,1024]{3,2,1,0:T(8,128)}) custom-call(s32[1]{0:T(128)} %bitcast.place_ref, bf16[768,1024]{1,0:T(8,128)(2,1)S(1)} %bitcast.176, bf16[1024,7168]{1,0:T(8,128)(2,1)} %gate_ref.7, bf16[1024,7168]{1,0:T(8,128)(2,1)} %up_ref.7), custom_call_target="tpu_custom_call" | custom-call | flops 3221225472 | bytes 12058624 | tf_op jit(solution)/shard_map/pallas_call | solution.py:33
  52.7 1.5 convert_element_type.332
  54.6 6.8 %shard_map.68 = (f32[4,2,96,1024]{3,2,1,0:T(8,128)S(1)}, f32[4,2,96,1024]{3,2,1,0:T(8,128)}) custom-call(s32[1]{0:T(128)} %bitcast.place_ref, bf16[768,1024]{1,0:T(8,128)(2,1)S(1)} %bitcast.177, bf16[1024,7168]{1,0:T(8,128)(2,1)} %gate_ref.7, bf16[1024,7168]{1,0:T(8,128)(2,1)} %up_ref.7), custom_call_target="tpu_custom_call" | custom-call | flops 3221225472 | bytes 12058624 | tf_op jit(solution)/shard_map/pallas_call | solution.py:33
  61.4 1.5 convert_element_type.312
  63.6 1.7 add_convert_fusion.2
  66.3 3.1 %collective-permute-start.24 = (f16[2,96,768]{2,1,0:T(8,128)(2,1)S(1)}, f16[2,96,768]{2,1,0:T(8,128)(2,1)S(1)}, u32[]{:S(2)}, u32[]{:S(2)}) collective-permute-start(f16[2,96,768]{2,1,0:T(8,128)(2,1)S(1)} %get-tuple-element.59), channel_id=1, source_target_pairs={{0,4},{2,6},{1,5},{3,7},{16,20},{18,22},{17,21},{19,23}} | collective-permute-start | bytes 884744 | tf_op jit(solution)/shard_map/ppermute | solution.py:168
  69.4 1.4 collective-permute-start.27
  72.4 2.0 collective-permute-start.3
  74.4 1.4 collective-permute-done.24
  75.8 1.4 collective-permute-start.6
  78.7 1.3 collective-permute-start.34
  80.0 1.3 fusion.10
  82.2 4.1 %collective-permute-start.25 = (f16[2,96,768]{2,1,0:T(8,128)(2,1)S(1)}, f16[2,96,768]{2,1,0:T(8,128)(2,1)S(1)}, u32[]{:S(2)}, u32[]{:S(2)}) collective-permute-start(f16[2,96,768]{2,1,0:T(8,128)(2,1)S(1)} %get-tuple-element.57), channel_id=1, source_target_pairs={{0,4},{2,6},{4,8},{6,10},{1,5},{3,7},{5,9},{7,11},{16,20},{18,22},... | collective-permute-start | bytes 884744 | tf_op jit(solution)/shard_map/ppermute | solution.py:168
  88.3 2.5 collective-permute-start.4
  90.9 3.1 %add_convert_fusion = f16[4,2,96,1024]{3,2,1,0:T(8,128)(2,1)S(1)} fusion(f32[4,2,96,1024]{3,2,1,0:T(8,128)} %get-tuple-element.23, f16[4,2,96,1024]{3,2,1,0:T(8,128)(2,1)} %collective-permute-done.16), kind=kLoop, calls=%fused_computation | loop fusion | flops 2359296 | bytes 6291456 | tf_op jit(solution)/shard_map/convert_element_type | solution.py:161
  94.6 2.0 add_convert_fusion.1
  97.0 4.7 %collective-permute-start.17 = (f16[2,96,1024]{2,1,0:T(8,128)(2,1)S(1)}, f16[2,96,1024]{2,1,0:T(8,128)(2,1)S(1)}, u32[]{:S(2)}, u32[]{:S(2)}) collective-permute-start(f16[2,96,1024]{2,1,0:T(8,128)(2,1)S(1)} %get-tuple-element.47), channel_id=1, source_target_pairs={{0,4},{2,6},{1,5},{3,7},{16,20},{18,22},{17,21},{19,23}} | collective-permute-start | bytes 1179656 | tf_op jit(solution)/shard_map/ppermute | solution.py:168
  102.7 1.3 collective-permute-start.10
  104.9 3.8 %collective-permute-done.17 = f16[2,96,1024]{2,1,0:T(8,128)(2,1)S(1)} collective-permute-done((f16[2,96,1024]{2,1,0:T(8,128)(2,1)S(1)}, f16[2,96,1024]{2,1,0:T(8,128)(2,1)S(1)}, u32[]{:S(2)}, u32[]{:S(2)}) %collective-permute-start.17) | collective-permute-done | bytes 393248 | tf_op jit(solution)/shard_map/ppermute | solution.py:168
  108.7 4.1 %collective-permute-start.26 = (f16[2,96,768]{2,1,0:T(8,128)(2,1)S(1)}, f16[2,96,768]{2,1,0:T(8,128)(2,1)S(1)}, u32[]{:S(2)}, u32[]{:S(2)}) collective-permute-start(f16[2,96,768]{2,1,0:T(8,128)(2,1)S(1)} %get-tuple-element.55), channel_id=1, source_target_pairs={{0,4},{2,6},{4,8},{6,10},{8,12},{10,14},{1,5},{3,7},{5,9},{7,11},{... | collective-permute-start | bytes 884744 | tf_op jit(solution)/shard_map/ppermute | solution.py:168
  112.9 1.3 collective-permute-start.29
  114.4 2.7 collective-permute-done.10
  117.2 4.1 %collective-permute-start.5 = (f16[2,96,768]{2,1,0:T(8,128)(2,1)S(1)}, f16[2,96,768]{2,1,0:T(8,128)(2,1)S(1)}, u32[]{:S(2)}, u32[]{:S(2)}) collective-permute-start(f16[2,96,768]{2,1,0:T(8,128)(2,1)S(1)} %get-tuple-element.61), channel_id=1, source_target_pairs={{0,4},{2,6},{4,8},{6,10},{8,12},{10,14},{1,5},{3,7},{5,9},{7,11},{... | collective-permute-start | bytes 884744 | tf_op jit(solution)/shard_map/ppermute | solution.py:168
  123.5 4.1 %collective-permute-start.18 = (f16[2,96,1024]{2,1,0:T(8,128)(2,1)S(1)}, f16[2,96,1024]{2,1,0:T(8,128)(2,1)S(1)}, u32[]{:S(2)}, u32[]{:S(2)}) collective-permute-start(f16[2,96,1024]{2,1,0:T(8,128)(2,1)S(1)} %get-tuple-element.45), channel_id=1, source_target_pairs={{0,4},{2,6},{4,8},{6,10},{1,5},{3,7},{5,9},{7,11},{16,20},{18,22},... | collective-permute-start | bytes 1179656 | tf_op jit(solution)/shard_map/ppermute | solution.py:168
  129.8 4.1 %collective-permute-start.11 = (f16[2,96,1024]{2,1,0:T(8,128)(2,1)S(1)}, f16[2,96,1024]{2,1,0:T(8,128)(2,1)S(1)}, u32[]{:S(2)}, u32[]{:S(2)}) collective-permute-start(f16[2,96,1024]{2,1,0:T(8,128)(2,1)S(1)} %get-tuple-element.51), channel_id=1, source_target_pairs={{0,4},{2,6},{4,8},{6,10},{1,5},{3,7},{5,9},{7,11},{16,20},{18,22},... | collective-permute-start | bytes 1179656 | tf_op jit(solution)/shard_map/ppermute | solution.py:168
  134.6 1.9 collective-permute-start.57
  136.6 1.3 collective-permute-start.30
  138.0 1.9 collective-permute-done.30
  141.2 11.8 %collective-permute-done.57 = bf16[2,96,768]{2,1,0:T(8,128)(2,1)S(1)} collective-permute-done((bf16[2,96,768]{2,1,0:T(8,128)(2,1)S(1)}, bf16[2,96,768]{2,1,0:T(8,128)(2,1)S(1)}, u32[]{:S(2)}, u32[]{:S(2)}) %collective-permute-start.57) | collective-permute-done | bytes 294944 | tf_op jit(solution)/shard_map/ppermute | solution.py:184
  153.7 4.7 %collective-permute-start.36 = (bf16[2,96,768]{2,1,0:T(8,128)(2,1)S(1)}, bf16[2,96,768]{2,1,0:T(8,128)(2,1)S(1)}, u32[]{:S(2)}, u32[]{:S(2)}) collective-permute-start(bf16[2,96,768]{2,1,0:T(8,128)(2,1)S(1)} %pad_maximum_fusion.9), channel_id=1, source_target_pairs={{0,4},{2,6},{4,8},{6,10},{8,12},{10,14},{1,5},{3,7},{5,9},{7,11},{... | collective-permute-start | bytes 884744 | tf_op jit(solution)/shard_map/ppermute | solution.py:184
  158.4 1.3 collective-permute-start.35
  160.4 1.3 collective-permute-start.60
  162.1 1.3 collective-permute-start.33
  164.1 2.7 collective-permute-done.35
  168.5 8.6 %collective-permute-start.19 = (f16[2,96,1024]{2,1,0:T(8,128)(2,1)S(1)}, f16[2,96,1024]{2,1,0:T(8,128)(2,1)S(1)}, u32[]{:S(2)}, u32[]{:S(2)}) collective-permute-start(f16[2,96,1024]{2,1,0:T(8,128)(2,1)S(1)} %get-tuple-element.43), channel_id=1, source_target_pairs={{0,4},{2,6},{4,8},{6,10},{8,12},{10,14},{1,5},{3,7},{5,9},{7,11},{... | collective-permute-start | bytes 1179656 | tf_op jit(solution)/shard_map/ppermute | solution.py:168
  178.5 4.0 %collective-permute-start.12 = (f16[2,96,1024]{2,1,0:T(8,128)(2,1)S(1)}, f16[2,96,1024]{2,1,0:T(8,128)(2,1)S(1)}, u32[]{:S(2)}, u32[]{:S(2)}) collective-permute-start(f16[2,96,1024]{2,1,0:T(8,128)(2,1)S(1)} %get-tuple-element.49), channel_id=1, source_target_pairs={{0,4},{2,6},{4,8},{6,10},{8,12},{10,14},{1,5},{3,7},{5,9},{7,11},{... | collective-permute-start | bytes 1179656 | tf_op jit(solution)/shard_map/ppermute | solution.py:168
  184.5 4.9 %collective-permute-done.22 = f16[2,96,1024]{2,1,0:T(8,128)(2,1)S(1)} collective-permute-done((f16[2,96,1024]{2,1,0:T(8,128)(2,1)S(1)}, f16[2,96,1024]{2,1,0:T(8,128)(2,1)S(1)}, u32[]{:S(2)}, u32[]{:S(2)}) %collective-permute-start.22) | collective-permute-done | bytes 393248 | tf_op jit(solution)/shard_map/ppermute | solution.py:169
  192.0 5.8 %collective-permute-done.15 = f16[2,96,1024]{2,1,0:T(8,128)(2,1)S(1)} collective-permute-done((f16[2,96,1024]{2,1,0:T(8,128)(2,1)S(1)}, f16[2,96,1024]{2,1,0:T(8,128)(2,1)S(1)}, u32[]{:S(2)}, u32[]{:S(2)}) %collective-permute-start.15) | collective-permute-done | bytes 393248 | tf_op jit(solution)/shard_map/ppermute | solution.py:169
  198.8 1.3 collective-permute-start.31
  200.2 2.4 collective-permute-done.31
  203.9 2.5 collective-permute-done.32
  207.7 5.8 %collective-permute-start.50 = (bf16[2,96,1024]{2,1,0:T(8,128)(2,1)S(1)}, bf16[2,96,1024]{2,1,0:T(8,128)(2,1)S(1)}, u32[]{:S(2)}, u32[]{:S(2)}) collective-permute-start(bf16[2,96,1024]{2,1,0:T(8,128)(2,1)S(1)} %pad_maximum_fusion.8), channel_id=1, source_target_pairs={{0,4},{2,6},{4,8},{6,10},{8,12},{10,14},{1,5},{3,7},{5,9},{7,11},{... | collective-permute-start | bytes 1179656 | tf_op jit(solution)/shard_map/ppermute | solution.py:184
  215.1 4.0 %collective-permute-start.43 = (bf16[2,96,1024]{2,1,0:T(8,128)(2,1)S(1)}, bf16[2,96,1024]{2,1,0:T(8,128)(2,1)S(1)}, u32[]{:S(2)}, u32[]{:S(2)}) collective-permute-start(bf16[2,96,1024]{2,1,0:T(8,128)(2,1)S(1)} %pad_maximum_fusion.7), channel_id=1, source_target_pairs={{0,4},{2,6},{4,8},{6,10},{8,12},{10,14},{1,5},{3,7},{5,9},{7,11},{... | collective-permute-start | bytes 1179656 | tf_op jit(solution)/shard_map/ppermute | solution.py:184
  221.2 3.9 %collective-permute-done.49 = bf16[2,96,1024]{2,1,0:T(8,128)(2,1)S(1)} collective-permute-done((bf16[2,96,1024]{2,1,0:T(8,128)(2,1)S(1)}, bf16[2,96,1024]{2,1,0:T(8,128)(2,1)S(1)}, u32[]{:S(2)}, u32[]{:S(2)}) %collective-permute-start.49) | collective-permute-done | bytes 393248 | tf_op jit(solution)/shard_map/ppermute | solution.py:185
  226.5 10.2 %collective-permute-start.62 = (bf16[4,2,96,768]{3,2,1,0:T(8,128)(2,1)S(1)}, bf16[4,2,96,768]{3,2,1,0:T(8,128)(2,1)S(1)}, u32[]{:S(2)}, u32[]{:S(2)}) collective-permute-start(bf16[4,2,96,768]{3,2,1,0:T(8,128)(2,1)S(1)} %pad_maximum_fusion.4.own_ref), channel_id=1, source_target_pairs={{0,2},{2,0},{4,6},{6,4},{8,10},{10,8},{12,14},{14,12},{1,3},{3,1},... | collective-permute-start | bytes 3538952 | tf_op jit(solution)/shard_map/ppermute | solution.py:191
  238.9 5.6 %collective-permute-start.41 = (bf16[4,2,96,768]{3,2,1,0:T(8,128)(2,1)S(1)}, bf16[4,2,96,768]{3,2,1,0:T(8,128)(2,1)S(1)}, u32[]{:S(2)}, u32[]{:S(2)}) collective-permute-start(bf16[4,2,96,768]{3,2,1,0:T(8,128)(2,1)S(1)} %pad_maximum_fusion.3.own_ref), channel_id=1, source_target_pairs={{0,2},{2,0},{4,6},{6,4},{8,10},{10,8},{12,14},{14,12},{1,3},{3,1},... | collective-permute-start | bytes 3538952 | tf_op jit(solution)/shard_map/ppermute | solution.py:191
  245.2 1.3 collective-permute-start.54
  246.5 5.7 %collective-permute-done.46 = bf16[2,96,1024]{2,1,0:T(8,128)(2,1)S(1)} collective-permute-done((bf16[2,96,1024]{2,1,0:T(8,128)(2,1)S(1)}, bf16[2,96,1024]{2,1,0:T(8,128)(2,1)S(1)}, u32[]{:S(2)}, u32[]{:S(2)}) %collective-permute-start.46) | collective-permute-done | bytes 393248 | tf_op jit(solution)/shard_map/ppermute | solution.py:185
  253.0 1.3 collective-permute-start.47
  254.3 6.3 %collective-permute-done.54 = bf16[2,96,1024]{2,1,0:T(8,128)(2,1)S(1)} collective-permute-done((bf16[2,96,1024]{2,1,0:T(8,128)(2,1)S(1)}, bf16[2,96,1024]{2,1,0:T(8,128)(2,1)S(1)}, u32[]{:S(2)}, u32[]{:S(2)}) %collective-permute-start.54) | collective-permute-done | bytes 393248 | tf_op jit(solution)/shard_map/ppermute | solution.py:185
  260.9 6.5 %collective-permute-start.55 = (bf16[4,2,96,1024]{3,2,1,0:T(8,128)(2,1)S(1)}, bf16[4,2,96,1024]{3,2,1,0:T(8,128)(2,1)S(1)}, u32[]{:S(2)}, u32[]{:S(2)}) collective-permute-start(bf16[4,2,96,1024]{3,2,1,0:T(8,128)(2,1)S(1)} %pad_maximum_fusion.2.own_ref), channel_id=1, source_target_pairs={{0,2},{2,0},{4,6},{6,4},{8,10},{10,8},{12,14},{14,12},{1,3},{3,1},... | collective-permute-start | bytes 4718600 | tf_op jit(solution)/shard_map/ppermute | solution.py:191
  267.4 1.7 collective-permute-done.47
  269.3 3.5 %collective-permute-start.48 = (bf16[4,2,96,1024]{3,2,1,0:T(8,128)(2,1)S(1)}, bf16[4,2,96,1024]{3,2,1,0:T(8,128)(2,1)S(1)}, u32[]{:S(2)}, u32[]{:S(2)}) collective-permute-start(bf16[4,2,96,1024]{3,2,1,0:T(8,128)(2,1)S(1)} %pad_maximum_fusion.1.own_ref), channel_id=1, source_target_pairs={{0,2},{2,0},{4,6},{6,4},{8,10},{10,8},{12,14},{14,12},{1,3},{3,1},... | collective-permute-start | bytes 4718600 | tf_op jit(solution)/shard_map/ppermute | solution.py:191
  273.7 5.3 %shard_map.71 = (f32[1024,3584]{1,0:T(8,128)}, f32[1024,3584]{1,0:T(8,128)}) custom-call(bf16[1024,768]{1,0:T(8,128)(2,1)S(1)} %bitcast.179, bf16[4,2,96,768]{3,2,1,0:T(8,128)(2,1)S(1)} %pad_maximum_fusion.4.own_ref, bf16[4,2,96,768]{3,2,1,0:T(8,128)(2,1)S(1)} %collective-permute-done.62.other_ref), custom_call_target="tpu_custom_call" | custom-call | flops 2415919104 | bytes 10223616 | tf_op jit(solution)/shard_map/pallas_call | solution.py:79
  279.0 6.8 %shard_map.72 = (f32[1024,3584]{1,0:T(8,128)}, f32[1024,3584]{1,0:T(8,128)}) custom-call(bf16[1024,768]{1,0:T(8,128)(2,1)S(1)} %bitcast.180, bf16[4,2,96,1024]{3,2,1,0:T(8,128)(2,1)S(1)} %pad_maximum_fusion.2.own_ref, bf16[4,2,96,1024]{3,2,1,0:T(8,128)(2,1)S(1)} %collective-permute-done.55.other_ref, ...), custom_call_target="tpu_custom_call", output_to_operand_aliasing={{0}: (3, {}), {1}: (4, {})} | custom-call | flops 3221225472 | bytes 13107200 | tf_op jit(solution)/shard_map/pallas_call | solution.py:79
  285.8 6.8 %shard_map.73 = (f32[1024,3584]{1,0:T(8,128)}, f32[1024,3584]{1,0:T(8,128)}) custom-call(bf16[1024,768]{1,0:T(8,128)(2,1)S(1)} %bitcast.181, bf16[4,2,96,1024]{3,2,1,0:T(8,128)(2,1)S(1)} %pad_maximum_fusion.1.own_ref, bf16[4,2,96,1024]{3,2,1,0:T(8,128)(2,1)S(1)} %collective-permute-done.48.other_ref, ...), custom_call_target="tpu_custom_call", output_to_operand_aliasing={{0}: (3, {}), {1}: (4, {})} | custom-call | flops 3221225472 | bytes 13107200 | tf_op jit(solution)/shard_map/pallas_call | solution.py:79
  292.6 5.3 %shard_map.74 = (f32[1024,3584]{1,0:T(8,128)}, f32[1024,3584]{1,0:T(8,128)}) custom-call(bf16[1024,768]{1,0:T(8,128)(2,1)S(1)} %bitcast.182, bf16[4,2,96,768]{3,2,1,0:T(8,128)(2,1)S(1)} %pad_maximum_fusion.3.own_ref, bf16[4,2,96,768]{3,2,1,0:T(8,128)(2,1)S(1)} %collective-permute-done.41.other_ref, ...), custom_call_target="tpu_custom_call", output_to_operand_aliasing={{0}: (3, {}), {1}: (4, {})} | custom-call | flops 2415919104 | bytes 10223616 | tf_op jit(solution)/shard_map/pallas_call | solution.py:79
  (171 shorter events, 44.2 us)
Async XLA Ops:
  0.6 13.8 %copy-start.7 = (bf16[1,384,512]{2,1,0:T(8,128)(2,1)S(1)}, bf16[1,384,512]{2,1,0:T(8,128)(2,1)}, u32[]{:S(2)}) copy-start(bf16[1,384,512]{2,1,0:T(8,128)(2,1)} %param.4) | copy-start | bytes 1179652
  0.6 11.2 %collective-permute-start = (bf16[384,512]{1,0:T(8,128)(2,1)}, bf16[384,512]{1,0:T(8,128)(2,1)S(1)}, u32[]{:S(2)}, u32[]{:S(2)}) collective-permute-start(bf16[384,512]{1,0:T(8,128)(2,1)} %bitcast.199), channel_id=1, source_target_pairs={{0,16},{16,0},{1,17},{17,1},{2,18},{18,2},{3,19},{19,3},{4,20},{20... | collective-permute-start | bytes 1179656 | tf_op jit(solution)/shard_map/ppermute | solution.py:125
  13.1 17.9 %collective-permute-start.1 = (bf16[384,1024]{1,0:T(8,128)(2,1)S(1)}, bf16[384,1024]{1,0:T(8,128)(2,1)S(1)}, u32[]{:S(2)}, u32[]{:S(2)}) collective-permute-start(bf16[384,1024]{1,0:T(8,128)(2,1)S(1)} %maximum_select_fusion), channel_id=1, source_target_pairs={{0,1},{1,0},{2,3},{3,2},{4,5},{5,4},{6,7},{7,6},{8,9},{9,8},{10,11... | collective-permute-start | bytes 2359304 | tf_op jit(solution)/shard_map/ppermute | solution.py:133
  37.7 25.2 %collective-permute-start.23 = (f16[4,2,96,768]{3,2,1,0:T(8,128)(2,1)S(1)}, f16[4,2,96,768]{3,2,1,0:T(8,128)(2,1)}, u32[]{:S(2)}, u32[]{:S(2)}) collective-permute-start(f16[4,2,96,768]{3,2,1,0:T(8,128)(2,1)S(1)} %convert_element_type.352), channel_id=1, source_target_pairs={{0,2},{2,0},{4,6},{6,4},{8,10},{10,8},{12,14},{14,12},{1,3},{3,1},... | collective-permute-start | bytes 3538952 | tf_op jit(solution)/shard_map/ppermute | solution.py:160
  45.8 25.1 %collective-permute-start.2 = (f16[4,2,96,768]{3,2,1,0:T(8,128)(2,1)S(1)}, f16[4,2,96,768]{3,2,1,0:T(8,128)(2,1)S(1)}, u32[]{:S(2)}, u32[]{:S(2)}) collective-permute-start(f16[4,2,96,768]{3,2,1,0:T(8,128)(2,1)S(1)} %convert_element_type.292), channel_id=1, source_target_pairs={{0,2},{2,0},{4,6},{6,4},{8,10},{10,8},{12,14},{14,12},{1,3},{3,1},... | collective-permute-start | bytes 3538952 | tf_op jit(solution)/shard_map/ppermute | solution.py:160
  54.1 34.2 %collective-permute-start.16 = (f16[4,2,96,1024]{3,2,1,0:T(8,128)(2,1)}, f16[4,2,96,1024]{3,2,1,0:T(8,128)(2,1)}, u32[]{:S(2)}, u32[]{:S(2)}) collective-permute-start(f16[4,2,96,1024]{3,2,1,0:T(8,128)(2,1)} %convert_element_type.332), channel_id=1, source_target_pairs={{0,2},{2,0},{4,6},{6,4},{8,10},{10,8},{12,14},{14,12},{1,3},{3,1},... | collective-permute-start | bytes 4718600 | tf_op jit(solution)/shard_map/ppermute | solution.py:160
  62.9 31.1 %collective-permute-start.9 = (f16[4,2,96,1024]{3,2,1,0:T(8,128)(2,1)}, f16[4,2,96,1024]{3,2,1,0:T(8,128)(2,1)}, u32[]{:S(2)}, u32[]{:S(2)}) collective-permute-start(f16[4,2,96,1024]{3,2,1,0:T(8,128)(2,1)} %convert_element_type.312), channel_id=1, source_target_pairs={{0,2},{2,0},{4,6},{6,4},{8,10},{10,8},{12,14},{14,12},{1,3},{3,1},... | collective-permute-start | bytes 4718600 | tf_op jit(solution)/shard_map/ppermute | solution.py:160
  66.3 9.5 %collective-permute-start.24 = (f16[2,96,768]{2,1,0:T(8,128)(2,1)S(1)}, f16[2,96,768]{2,1,0:T(8,128)(2,1)S(1)}, u32[]{:S(2)}, u32[]{:S(2)}) collective-permute-start(f16[2,96,768]{2,1,0:T(8,128)(2,1)S(1)} %get-tuple-element.59), channel_id=1, source_target_pairs={{0,4},{2,6},{1,5},{3,7},{16,20},{18,22},{17,21},{19,23}} | collective-permute-start | bytes 884744 | tf_op jit(solution)/shard_map/ppermute | solution.py:168
  69.4 9.2 %collective-permute-start.27 = (f16[2,96,768]{2,1,0:T(8,128)(2,1)}, f16[2,96,768]{2,1,0:T(8,128)(2,1)}, u32[]{:S(2)}, u32[]{:S(2)}) collective-permute-start(f16[2,96,768]{2,1,0:T(8,128)(2,1)} %get-tuple-element.60), channel_id=1, source_target_pairs={{12,8},{14,10},{13,9},{15,11},{28,24},{30,26},{29,25},{31,27}} | collective-permute-start | bytes 884744 | tf_op jit(solution)/shard_map/ppermute | solution.py:169
  72.4 9.8 %collective-permute-start.3 = (f16[2,96,768]{2,1,0:T(8,128)(2,1)}, f16[2,96,768]{2,1,0:T(8,128)(2,1)}, u32[]{:S(2)}, u32[]{:S(2)}) collective-permute-start(f16[2,96,768]{2,1,0:T(8,128)(2,1)} %get-tuple-element.65), channel_id=1, source_target_pairs={{0,4},{2,6},{1,5},{3,7},{16,20},{18,22},{17,21},{19,23}} | collective-permute-start | bytes 884744 | tf_op jit(solution)/shard_map/ppermute | solution.py:168
  75.8 10.5 %collective-permute-start.6 = (f16[2,96,768]{2,1,0:T(8,128)(2,1)}, f16[2,96,768]{2,1,0:T(8,128)(2,1)}, u32[]{:S(2)}, u32[]{:S(2)}) collective-permute-start(f16[2,96,768]{2,1,0:T(8,128)(2,1)} %get-tuple-element.66), channel_id=1, source_target_pairs={{12,8},{14,10},{13,9},{15,11},{28,24},{30,26},{29,25},{31,27}} | collective-permute-start | bytes 884744 | tf_op jit(solution)/shard_map/ppermute | solution.py:169
  78.7 55.5 %collective-permute-start.34 = (bf16[48,3584]{1,0:T(8,128)(2,1)}, bf16[48,3584]{1,0:T(8,128)(2,1)S(1)}, u32[]{:S(2)}, u32[]{:S(2)}) collective-permute-start(bf16[48,3584]{1,0:T(8,128)(2,1)} %get-tuple-element.85), channel_id=1, source_target_pairs={{0,1},{1,0},{2,3},{3,2},{4,5},{5,4},{6,7},{7,6},{8,9},{9,8},{10,11... | collective-permute-start | bytes 1032200 | tf_op jit(solution)/shard_map/ppermute | solution.py:149
  82.2 14.8 %collective-permute-start.25 = (f16[2,96,768]{2,1,0:T(8,128)(2,1)S(1)}, f16[2,96,768]{2,1,0:T(8,128)(2,1)S(1)}, u32[]{:S(2)}, u32[]{:S(2)}) collective-permute-start(f16[2,96,768]{2,1,0:T(8,128)(2,1)S(1)} %get-tuple-element.57), channel_id=1, source_target_pairs={{0,4},{2,6},{4,8},{6,10},{1,5},{3,7},{5,9},{7,11},{16,20},{18,22},... | collective-permute-start | bytes 884744 | tf_op jit(solution)/shard_map/ppermute | solution.py:168
  86.4 15.4 %collective-permute-start.28 = (f16[2,96,768]{2,1,0:T(8,128)(2,1)S(1)}, f16[2,96,768]{2,1,0:T(8,128)(2,1)S(1)}, u32[]{:S(2)}, u32[]{:S(2)}) collective-permute-start(f16[2,96,768]{2,1,0:T(8,128)(2,1)S(1)} %get-tuple-element.58), channel_id=1, source_target_pairs={{8,4},{10,6},{12,8},{14,10},{9,5},{11,7},{13,9},{15,11},{24,20},{2... | collective-permute-start | bytes 884744 | tf_op jit(solution)/shard_map/ppermute | solution.py:169
  88.3 14.4 %collective-permute-start.4 = (f16[2,96,768]{2,1,0:T(8,128)(2,1)S(1)}, f16[2,96,768]{2,1,0:T(8,128)(2,1)S(1)}, u32[]{:S(2)}, u32[]{:S(2)}) collective-permute-start(f16[2,96,768]{2,1,0:T(8,128)(2,1)S(1)} %get-tuple-element.63), channel_id=1, source_target_pairs={{0,4},{2,6},{4,8},{6,10},{1,5},{3,7},{5,9},{7,11},{16,20},{18,22},... | collective-permute-start | bytes 884744 | tf_op jit(solution)/shard_map/ppermute | solution.py:168
  93.9 10.1 %collective-permute-start.7 = (f16[2,96,768]{2,1,0:T(8,128)(2,1)S(1)}, f16[2,96,768]{2,1,0:T(8,128)(2,1)S(1)}, u32[]{:S(2)}, u32[]{:S(2)}) collective-permute-start(f16[2,96,768]{2,1,0:T(8,128)(2,1)S(1)} %get-tuple-element.64), channel_id=1, source_target_pairs={{8,4},{10,6},{12,8},{14,10},{9,5},{11,7},{13,9},{15,11},{24,20},{2... | collective-permute-start | bytes 884744 | tf_op jit(solution)/shard_map/ppermute | solution.py:169
  97.0 11.7 %collective-permute-start.17 = (f16[2,96,1024]{2,1,0:T(8,128)(2,1)S(1)}, f16[2,96,1024]{2,1,0:T(8,128)(2,1)S(1)}, u32[]{:S(2)}, u32[]{:S(2)}) collective-permute-start(f16[2,96,1024]{2,1,0:T(8,128)(2,1)S(1)} %get-tuple-element.47), channel_id=1, source_target_pairs={{0,4},{2,6},{1,5},{3,7},{16,20},{18,22},{17,21},{19,23}} | collective-permute-start | bytes 1179656 | tf_op jit(solution)/shard_map/ppermute | solution.py:168
  101.8 11.1 %collective-permute-start.20 = (f16[2,96,1024]{2,1,0:T(8,128)(2,1)S(1)}, f16[2,96,1024]{2,1,0:T(8,128)(2,1)S(1)}, u32[]{:S(2)}, u32[]{:S(2)}) collective-permute-start(f16[2,96,1024]{2,1,0:T(8,128)(2,1)S(1)} %get-tuple-element.48), channel_id=1, source_target_pairs={{12,8},{14,10},{13,9},{15,11},{28,24},{30,26},{29,25},{31,27}} | collective-permute-start | bytes 1179656 | tf_op jit(solution)/shard_map/ppermute | solution.py:169
  102.7 14.5 %collective-permute-start.10 = (f16[2,96,1024]{2,1,0:T(8,128)(2,1)S(1)}, f16[2,96,1024]{2,1,0:T(8,128)(2,1)S(1)}, u32[]{:S(2)}, u32[]{:S(2)}) collective-permute-start(f16[2,96,1024]{2,1,0:T(8,128)(2,1)S(1)} %get-tuple-element.53), channel_id=1, source_target_pairs={{0,4},{2,6},{1,5},{3,7},{16,20},{18,22},{17,21},{19,23}} | collective-permute-start | bytes 1179656 | tf_op jit(solution)/shard_map/ppermute | solution.py:168
  104.0 17.3 %collective-permute-start.13 = (f16[2,96,1024]{2,1,0:T(8,128)(2,1)S(1)}, f16[2,96,1024]{2,1,0:T(8,128)(2,1)S(1)}, u32[]{:S(2)}, u32[]{:S(2)}) collective-permute-start(f16[2,96,1024]{2,1,0:T(8,128)(2,1)S(1)} %get-tuple-element.54), channel_id=1, source_target_pairs={{12,8},{14,10},{13,9},{15,11},{28,24},{30,26},{29,25},{31,27}} | collective-permute-start | bytes 1179656 | tf_op jit(solution)/shard_map/ppermute | solution.py:169
  108.7 14.7 %collective-permute-start.26 = (f16[2,96,768]{2,1,0:T(8,128)(2,1)S(1)}, f16[2,96,768]{2,1,0:T(8,128)(2,1)S(1)}, u32[]{:S(2)}, u32[]{:S(2)}) collective-permute-start(f16[2,96,768]{2,1,0:T(8,128)(2,1)S(1)} %get-tuple-element.55), channel_id=1, source_target_pairs={{0,4},{2,6},{4,8},{6,10},{8,12},{10,14},{1,5},{3,7},{5,9},{7,11},{... | collective-permute-start | bytes 884744 | tf_op jit(solution)/shard_map/ppermute | solution.py:168
  112.9 14.7 %collective-permute-start.29 = (f16[2,96,768]{2,1,0:T(8,128)(2,1)S(1)}, f16[2,96,768]{2,1,0:T(8,128)(2,1)S(1)}, u32[]{:S(2)}, u32[]{:S(2)}) collective-permute-start(f16[2,96,768]{2,1,0:T(8,128)(2,1)S(1)} %get-tuple-element.56), channel_id=1, source_target_pairs={{4,0},{6,2},{8,4},{10,6},{12,8},{14,10},{5,1},{7,3},{9,5},{11,7},{... | collective-permute-start | bytes 884744 | tf_op jit(solution)/shard_map/ppermute | solution.py:169
  117.2 12.6 %collective-permute-start.5 = (f16[2,96,768]{2,1,0:T(8,128)(2,1)S(1)}, f16[2,96,768]{2,1,0:T(8,128)(2,1)S(1)}, u32[]{:S(2)}, u32[]{:S(2)}) collective-permute-start(f16[2,96,768]{2,1,0:T(8,128)(2,1)S(1)} %get-tuple-element.61), channel_id=1, source_target_pairs={{0,4},{2,6},{4,8},{6,10},{8,12},{10,14},{1,5},{3,7},{5,9},{7,11},{... | collective-permute-start | bytes 884744 | tf_op jit(solution)/shard_map/ppermute | solution.py:168
  121.3 12.6 %collective-permute-start.8 = (f16[2,96,768]{2,1,0:T(8,128)(2,1)S(1)}, f16[2,96,768]{2,1,0:T(8,128)(2,1)S(1)}, u32[]{:S(2)}, u32[]{:S(2)}) collective-permute-start(f16[2,96,768]{2,1,0:T(8,128)(2,1)S(1)} %get-tuple-element.62), channel_id=1, source_target_pairs={{4,0},{6,2},{8,4},{10,6},{12,8},{14,10},{5,1},{7,3},{9,5},{11,7},{... | collective-permute-start | bytes 884744 | tf_op jit(solution)/shard_map/ppermute | solution.py:169
  123.5 34.9 %collective-permute-start.18 = (f16[2,96,1024]{2,1,0:T(8,128)(2,1)S(1)}, f16[2,96,1024]{2,1,0:T(8,128)(2,1)S(1)}, u32[]{:S(2)}, u32[]{:S(2)}) collective-permute-start(f16[2,96,1024]{2,1,0:T(8,128)(2,1)S(1)} %get-tuple-element.45), channel_id=1, source_target_pairs={{0,4},{2,6},{4,8},{6,10},{1,5},{3,7},{5,9},{7,11},{16,20},{18,22},... | collective-permute-start | bytes 1179656 | tf_op jit(solution)/shard_map/ppermute | solution.py:168
  127.6 32.1 %collective-permute-start.21 = (f16[2,96,1024]{2,1,0:T(8,128)(2,1)S(1)}, f16[2,96,1024]{2,1,0:T(8,128)(2,1)S(1)}, u32[]{:S(2)}, u32[]{:S(2)}) collective-permute-start(f16[2,96,1024]{2,1,0:T(8,128)(2,1)S(1)} %get-tuple-element.46), channel_id=1, source_target_pairs={{8,4},{10,6},{12,8},{14,10},{9,5},{11,7},{13,9},{15,11},{24,20},{2... | collective-permute-start | bytes 1179656 | tf_op jit(solution)/shard_map/ppermute | solution.py:169
  129.8 30.6 %collective-permute-start.11 = (f16[2,96,1024]{2,1,0:T(8,128)(2,1)S(1)}, f16[2,96,1024]{2,1,0:T(8,128)(2,1)S(1)}, u32[]{:S(2)}, u32[]{:S(2)}) collective-permute-start(f16[2,96,1024]{2,1,0:T(8,128)(2,1)S(1)} %get-tuple-element.51), channel_id=1, source_target_pairs={{0,4},{2,6},{4,8},{6,10},{1,5},{3,7},{5,9},{7,11},{16,20},{18,22},... | collective-permute-start | bytes 1179656 | tf_op jit(solution)/shard_map/ppermute | solution.py:168
  134.6 18.3 %collective-permute-start.57 = (bf16[2,96,768]{2,1,0:T(8,128)(2,1)S(1)}, bf16[2,96,768]{2,1,0:T(8,128)(2,1)S(1)}, u32[]{:S(2)}, u32[]{:S(2)}) collective-permute-start(bf16[2,96,768]{2,1,0:T(8,128)(2,1)S(1)} %pad_maximum_fusion.10), channel_id=1, source_target_pairs={{0,4},{2,6},{4,8},{6,10},{8,12},{10,14},{1,5},{3,7},{5,9},{7,11},{... | collective-permute-start | bytes 884744 | tf_op jit(solution)/shard_map/ppermute | solution.py:184
  136.6 3.3 %collective-permute-start.30 = (bf16[48,768]{1,0:T(8,128)(2,1)S(1)}, bf16[48,768]{1,0:T(8,128)(2,1)S(1)}, u32[]{:S(2)}, u32[]{:S(2)}) collective-permute-start(bf16[48,768]{1,0:T(8,128)(2,1)S(1)} %slice_bitcast_fusion.19), channel_id=1, source_target_pairs={{0,1},{1,0},{2,3},{3,2},{4,5},{5,4},{6,7},{7,6},{8,9},{9,8},{10,11... | collective-permute-start | bytes 221192 | tf_op jit(solution)/shard_map/ppermute | solution.py:180
  139.9 13.8 %collective-permute-start.56 = (bf16[2,96,768]{2,1,0:T(8,128)(2,1)S(1)}, bf16[2,96,768]{2,1,0:T(8,128)(2,1)S(1)}, u32[]{:S(2)}, u32[]{:S(2)}) collective-permute-start(bf16[2,96,768]{2,1,0:T(8,128)(2,1)S(1)} %pad_maximum_fusion.10), channel_id=1, source_target_pairs={{4,0},{6,2},{8,4},{10,6},{12,8},{14,10},{5,1},{7,3},{9,5},{11,7},{... | collective-permute-start | bytes 884744 | tf_op jit(solution)/shard_map/ppermute | solution.py:185
  153.0 9.1 %collective-permute-start.14 = (f16[2,96,1024]{2,1,0:T(8,128)(2,1)S(1)}, f16[2,96,1024]{2,1,0:T(8,128)(2,1)S(1)}, u32[]{:S(2)}, u32[]{:S(2)}) collective-permute-start(f16[2,96,1024]{2,1,0:T(8,128)(2,1)S(1)} %get-tuple-element.52), channel_id=1, source_target_pairs={{8,4},{10,6},{12,8},{14,10},{9,5},{11,7},{13,9},{15,11},{24,20},{2... | collective-permute-start | bytes 1179656 | tf_op jit(solution)/shard_map/ppermute | solution.py:169
  153.7 9.8 %collective-permute-start.36 = (bf16[2,96,768]{2,1,0:T(8,128)(2,1)S(1)}, bf16[2,96,768]{2,1,0:T(8,128)(2,1)S(1)}, u32[]{:S(2)}, u32[]{:S(2)}) collective-permute-start(bf16[2,96,768]{2,1,0:T(8,128)(2,1)S(1)} %pad_maximum_fusion.9), channel_id=1, source_target_pairs={{0,4},{2,6},{4,8},{6,10},{8,12},{10,14},{1,5},{3,7},{5,9},{7,11},{... | collective-permute-start | bytes 884744 | tf_op jit(solution)/shard_map/ppermute | solution.py:184
  158.4 8.4 %collective-permute-start.35 = (bf16[2,96,768]{2,1,0:T(8,128)(2,1)S(1)}, bf16[2,96,768]{2,1,0:T(8,128)(2,1)S(1)}, u32[]{:S(2)}, u32[]{:S(2)}) collective-permute-start(bf16[2,96,768]{2,1,0:T(8,128)(2,1)S(1)} %pad_maximum_fusion.9), channel_id=1, source_target_pairs={{4,0},{6,2},{8,4},{10,6},{12,8},{14,10},{5,1},{7,3},{9,5},{11,7},{... | collective-permute-start | bytes 884744 | tf_op jit(solution)/shard_map/ppermute | solution.py:185
  159.7 8.8 %collective-permute-start.58 = (bf16[2,96,768]{2,1,0:T(8,128)(2,1)S(1)}, bf16[2,96,768]{2,1,0:T(8,128)(2,1)S(1)}, u32[]{:S(2)}, u32[]{:S(2)}) collective-permute-start(bf16[2,96,768]{2,1,0:T(8,128)(2,1)S(1)} %collective-permute-done.57), channel_id=1, source_target_pairs={{4,8},{6,10},{8,12},{10,14},{5,9},{7,11},{9,13},{11,15},{20,24},{2... | collective-permute-start | bytes 884744 | tf_op jit(solution)/shard_map/ppermute | solution.py:184
  160.4 16.7 %collective-permute-start.60 = (bf16[2,96,768]{2,1,0:T(8,128)(2,1)S(1)}, bf16[2,96,768]{2,1,0:T(8,128)(2,1)S(1)}, u32[]{:S(2)}, u32[]{:S(2)}) collective-permute-start(bf16[2,96,768]{2,1,0:T(8,128)(2,1)S(1)} %collective-permute-done.56), channel_id=1, source_target_pairs={{4,0},{6,2},{8,4},{10,6},{5,1},{7,3},{9,5},{11,7},{20,16},{22,18},... | collective-permute-start | bytes 884744 | tf_op jit(solution)/shard_map/ppermute | solution.py:185
  162.1 45.6 %collective-permute-start.33 = (bf16[48,768]{1,0:T(8,128)(2,1)S(1)}, bf16[48,768]{1,0:T(8,128)(2,1)S(1)}, u32[]{:S(2)}, u32[]{:S(2)}) collective-permute-start(bf16[48,768]{1,0:T(8,128)(2,1)S(1)} %slice_bitcast_fusion.18), channel_id=1, source_target_pairs={{0,1},{1,0},{2,3},{3,2},{4,5},{5,4},{6,7},{7,6},{8,9},{9,8},{10,11... | collective-permute-start | bytes 221192 | tf_op jit(solution)/shard_map/ppermute | solution.py:180
  163.4 15.0 %collective-permute-start.37 = (bf16[2,96,768]{2,1,0:T(8,128)(2,1)S(1)}, bf16[2,96,768]{2,1,0:T(8,128)(2,1)S(1)}, u32[]{:S(2)}, u32[]{:S(2)}) collective-permute-start(bf16[2,96,768]{2,1,0:T(8,128)(2,1)S(1)} %collective-permute-done.36), channel_id=1, source_target_pairs={{4,8},{6,10},{8,12},{10,14},{5,9},{7,11},{9,13},{11,15},{20,24},{2... | collective-permute-start | bytes 884744 | tf_op jit(solution)/shard_map/ppermute | solution.py:184
  166.8 15.6 %collective-permute-start.39 = (bf16[2,96,768]{2,1,0:T(8,128)(2,1)S(1)}, bf16[2,96,768]{2,1,0:T(8,128)(2,1)S(1)}, u32[]{:S(2)}, u32[]{:S(2)}) collective-permute-start(bf16[2,96,768]{2,1,0:T(8,128)(2,1)S(1)} %collective-permute-done.35), channel_id=1, source_target_pairs={{4,0},{6,2},{8,4},{10,6},{5,1},{7,3},{9,5},{11,7},{20,16},{22,18},... | collective-permute-start | bytes 884744 | tf_op jit(solution)/shard_map/ppermute | solution.py:185
  168.5 15.3 %collective-permute-start.19 = (f16[2,96,1024]{2,1,0:T(8,128)(2,1)S(1)}, f16[2,96,1024]{2,1,0:T(8,128)(2,1)S(1)}, u32[]{:S(2)}, u32[]{:S(2)}) collective-permute-start(f16[2,96,1024]{2,1,0:T(8,128)(2,1)S(1)} %get-tuple-element.43), channel_id=1, source_target_pairs={{0,4},{2,6},{4,8},{6,10},{8,12},{10,14},{1,5},{3,7},{5,9},{7,11},{... | collective-permute-start | bytes 1179656 | tf_op jit(solution)/shard_map/ppermute | solution.py:168
  177.1 12.3 %collective-permute-start.22 = (f16[2,96,1024]{2,1,0:T(8,128)(2,1)S(1)}, f16[2,96,1024]{2,1,0:T(8,128)(2,1)S(1)}, u32[]{:S(2)}, u32[]{:S(2)}) collective-permute-start(f16[2,96,1024]{2,1,0:T(8,128)(2,1)S(1)} %get-tuple-element.44), channel_id=1, source_target_pairs={{4,0},{6,2},{8,4},{10,6},{12,8},{14,10},{5,1},{7,3},{9,5},{11,7},{... | collective-permute-start | bytes 1179656 | tf_op jit(solution)/shard_map/ppermute | solution.py:169
  178.5 12.9 %collective-permute-start.12 = (f16[2,96,1024]{2,1,0:T(8,128)(2,1)S(1)}, f16[2,96,1024]{2,1,0:T(8,128)(2,1)S(1)}, u32[]{:S(2)}, u32[]{:S(2)}) collective-permute-start(f16[2,96,1024]{2,1,0:T(8,128)(2,1)S(1)} %get-tuple-element.49), channel_id=1, source_target_pairs={{0,4},{2,6},{4,8},{6,10},{8,12},{10,14},{1,5},{3,7},{5,9},{7,11},{... | collective-permute-start | bytes 1179656 | tf_op jit(solution)/shard_map/ppermute | solution.py:168
  182.5 15.3 %collective-permute-start.15 = (f16[2,96,1024]{2,1,0:T(8,128)(2,1)S(1)}, f16[2,96,1024]{2,1,0:T(8,128)(2,1)S(1)}, u32[]{:S(2)}, u32[]{:S(2)}) collective-permute-start(f16[2,96,1024]{2,1,0:T(8,128)(2,1)S(1)} %get-tuple-element.50), channel_id=1, source_target_pairs={{4,0},{6,2},{8,4},{10,6},{12,8},{14,10},{5,1},{7,3},{9,5},{11,7},{... | collective-permute-start | bytes 1179656 | tf_op jit(solution)/shard_map/ppermute | solution.py:169
  183.8 29.9 %collective-permute-start.59 = (bf16[2,96,768]{2,1,0:T(8,128)(2,1)S(1)}, bf16[2,96,768]{2,1,0:T(8,128)(2,1)S(1)}, u32[]{:S(2)}, u32[]{:S(2)}) collective-permute-start(bf16[2,96,768]{2,1,0:T(8,128)(2,1)S(1)} %collective-permute-done.58), channel_id=1, source_target_pairs={{8,12},{10,14},{9,13},{11,15},{24,28},{26,30},{25,29},{27,31}} | collective-permute-start | bytes 884744 | tf_op jit(solution)/shard_map/ppermute | solution.py:184
  189.4 29.8 %collective-permute-start.61 = (bf16[2,96,768]{2,1,0:T(8,128)(2,1)S(1)}, bf16[2,96,768]{2,1,0:T(8,128)(2,1)S(1)}, u32[]{:S(2)}, u32[]{:S(2)}) collective-permute-start(bf16[2,96,768]{2,1,0:T(8,128)(2,1)S(1)} %collective-permute-done.60), channel_id=1, source_target_pairs={{4,0},{6,2},{5,1},{7,3},{20,16},{22,18},{21,17},{23,19}} | collective-permute-start | bytes 884744 | tf_op jit(solution)/shard_map/ppermute | solution.py:185
  191.4 23.7 %collective-permute-start.38 = (bf16[2,96,768]{2,1,0:T(8,128)(2,1)S(1)}, bf16[2,96,768]{2,1,0:T(8,128)(2,1)S(1)}, u32[]{:S(2)}, u32[]{:S(2)}) collective-permute-start(bf16[2,96,768]{2,1,0:T(8,128)(2,1)S(1)} %collective-permute-done.37), channel_id=1, source_target_pairs={{8,12},{10,14},{9,13},{11,15},{24,28},{26,30},{25,29},{27,31}} | collective-permute-start | bytes 884744 | tf_op jit(solution)/shard_map/ppermute | solution.py:184
  198.8 3.8 %collective-permute-start.31 = (bf16[48,1024]{1,0:T(8,128)(2,1)S(1)}, bf16[48,1024]{1,0:T(8,128)(2,1)S(1)}, u32[]{:S(2)}, u32[]{:S(2)}) collective-permute-start(bf16[48,1024]{1,0:T(8,128)(2,1)S(1)} %slice_bitcast_fusion.17), channel_id=1, source_target_pairs={{0,1},{1,0},{2,3},{3,2},{4,5},{5,4},{6,7},{7,6},{8,9},{9,8},{10,11... | collective-permute-start | bytes 294920 | tf_op jit(solution)/shard_map/ppermute | solution.py:180
  202.7 3.8 %collective-permute-start.32 = (bf16[48,1024]{1,0:T(8,128)(2,1)S(1)}, bf16[48,1024]{1,0:T(8,128)(2,1)S(1)}, u32[]{:S(2)}, u32[]{:S(2)}) collective-permute-start(bf16[48,1024]{1,0:T(8,128)(2,1)S(1)} %slice_bitcast_fusion.16), channel_id=1, source_target_pairs={{0,1},{1,0},{2,3},{3,2},{4,5},{5,4},{6,7},{7,6},{8,9},{9,8},{10,11... | collective-permute-start | bytes 294920 | tf_op jit(solution)/shard_map/ppermute | solution.py:180
  206.4 20.1 %collective-permute-start.40 = (bf16[2,96,768]{2,1,0:T(8,128)(2,1)S(1)}, bf16[2,96,768]{2,1,0:T(8,128)(2,1)S(1)}, u32[]{:S(2)}, u32[]{:S(2)}) collective-permute-start(bf16[2,96,768]{2,1,0:T(8,128)(2,1)S(1)} %collective-permute-done.39), channel_id=1, source_target_pairs={{4,0},{6,2},{5,1},{7,3},{20,16},{22,18},{21,17},{23,19}} | collective-permute-start | bytes 884744 | tf_op jit(solution)/shard_map/ppermute | solution.py:185
  207.7 12.8 %collective-permute-start.50 = (bf16[2,96,1024]{2,1,0:T(8,128)(2,1)S(1)}, bf16[2,96,1024]{2,1,0:T(8,128)(2,1)S(1)}, u32[]{:S(2)}, u32[]{:S(2)}) collective-permute-start(bf16[2,96,1024]{2,1,0:T(8,128)(2,1)S(1)} %pad_maximum_fusion.8), channel_id=1, source_target_pairs={{0,4},{2,6},{4,8},{6,10},{8,12},{10,14},{1,5},{3,7},{5,9},{7,11},{... | collective-permute-start | bytes 1179656 | tf_op jit(solution)/shard_map/ppermute | solution.py:184
  213.7 11.3 %collective-permute-start.49 = (bf16[2,96,1024]{2,1,0:T(8,128)(2,1)S(1)}, bf16[2,96,1024]{2,1,0:T(8,128)(2,1)S(1)}, u32[]{:S(2)}, u32[]{:S(2)}) collective-permute-start(bf16[2,96,1024]{2,1,0:T(8,128)(2,1)S(1)} %pad_maximum_fusion.8), channel_id=1, source_target_pairs={{4,0},{6,2},{8,4},{10,6},{12,8},{14,10},{5,1},{7,3},{9,5},{11,7},{... | collective-permute-start | bytes 1179656 | tf_op jit(solution)/shard_map/ppermute | solution.py:185
  215.1 21.7 %collective-permute-start.43 = (bf16[2,96,1024]{2,1,0:T(8,128)(2,1)S(1)}, bf16[2,96,1024]{2,1,0:T(8,128)(2,1)S(1)}, u32[]{:S(2)}, u32[]{:S(2)}) collective-permute-start(bf16[2,96,1024]{2,1,0:T(8,128)(2,1)S(1)} %pad_maximum_fusion.7), channel_id=1, source_target_pairs={{0,4},{2,6},{4,8},{6,10},{8,12},{10,14},{1,5},{3,7},{5,9},{7,11},{... | collective-permute-start | bytes 1179656 | tf_op jit(solution)/shard_map/ppermute | solution.py:184
  219.2 18.3 %collective-permute-start.42 = (bf16[2,96,1024]{2,1,0:T(8,128)(2,1)S(1)}, bf16[2,96,1024]{2,1,0:T(8,128)(2,1)S(1)}, u32[]{:S(2)}, u32[]{:S(2)}) collective-permute-start(bf16[2,96,1024]{2,1,0:T(8,128)(2,1)S(1)} %pad_maximum_fusion.7), channel_id=1, source_target_pairs={{4,0},{6,2},{8,4},{10,6},{12,8},{14,10},{5,1},{7,3},{9,5},{11,7},{... | collective-permute-start | bytes 1179656 | tf_op jit(solution)/shard_map/ppermute | solution.py:185
  220.5 18.4 %collective-permute-start.51 = (bf16[2,96,1024]{2,1,0:T(8,128)(2,1)S(1)}, bf16[2,96,1024]{2,1,0:T(8,128)(2,1)S(1)}, u32[]{:S(2)}, u32[]{:S(2)}) collective-permute-start(bf16[2,96,1024]{2,1,0:T(8,128)(2,1)S(1)} %collective-permute-done.50), channel_id=1, source_target_pairs={{4,8},{6,10},{8,12},{10,14},{5,9},{7,11},{9,13},{11,15},{20,24},{2... | collective-permute-start | bytes 1179656 | tf_op jit(solution)/shard_map/ppermute | solution.py:184
  225.1 19.4 %collective-permute-start.53 = (bf16[2,96,1024]{2,1,0:T(8,128)(2,1)S(1)}, bf16[2,96,1024]{2,1,0:T(8,128)(2,1)S(1)}, u32[]{:S(2)}, u32[]{:S(2)}) collective-permute-start(bf16[2,96,1024]{2,1,0:T(8,128)(2,1)S(1)} %collective-permute-done.49), channel_id=1, source_target_pairs={{4,0},{6,2},{8,4},{10,6},{5,1},{7,3},{9,5},{11,7},{20,16},{22,18},... | collective-permute-start | bytes 1179656 | tf_op jit(solution)/shard_map/ppermute | solution.py:185
  226.5 47.2 %collective-permute-start.62 = (bf16[4,2,96,768]{3,2,1,0:T(8,128)(2,1)S(1)}, bf16[4,2,96,768]{3,2,1,0:T(8,128)(2,1)S(1)}, u32[]{:S(2)}, u32[]{:S(2)}) collective-permute-start(bf16[4,2,96,768]{3,2,1,0:T(8,128)(2,1)S(1)} %pad_maximum_fusion.4.own_ref), channel_id=1, source_target_pairs={{0,2},{2,0},{4,6},{6,4},{8,10},{10,8},{12,14},{14,12},{1,3},{3,1},... | collective-permute-start | bytes 3538952 | tf_op jit(solution)/shard_map/ppermute | solution.py:191
  236.8 8.5 %collective-permute-start.44 = (bf16[2,96,1024]{2,1,0:T(8,128)(2,1)S(1)}, bf16[2,96,1024]{2,1,0:T(8,128)(2,1)S(1)}, u32[]{:S(2)}, u32[]{:S(2)}) collective-permute-start(bf16[2,96,1024]{2,1,0:T(8,128)(2,1)S(1)} %collective-permute-done.43), channel_id=1, source_target_pairs={{4,8},{6,10},{8,12},{10,14},{5,9},{7,11},{9,13},{11,15},{20,24},{2... | collective-permute-start | bytes 1179656 | tf_op jit(solution)/shard_map/ppermute | solution.py:184
  237.5 14.8 %collective-permute-start.46 = (bf16[2,96,1024]{2,1,0:T(8,128)(2,1)S(1)}, bf16[2,96,1024]{2,1,0:T(8,128)(2,1)S(1)}, u32[]{:S(2)}, u32[]{:S(2)}) collective-permute-start(bf16[2,96,1024]{2,1,0:T(8,128)(2,1)S(1)} %collective-permute-done.42), channel_id=1, source_target_pairs={{4,0},{6,2},{8,4},{10,6},{5,1},{7,3},{9,5},{11,7},{20,16},{22,18},... | collective-permute-start | bytes 1179656 | tf_op jit(solution)/shard_map/ppermute | solution.py:185
  238.9 53.7 %collective-permute-start.41 = (bf16[4,2,96,768]{3,2,1,0:T(8,128)(2,1)S(1)}, bf16[4,2,96,768]{3,2,1,0:T(8,128)(2,1)S(1)}, u32[]{:S(2)}, u32[]{:S(2)}) collective-permute-start(bf16[4,2,96,768]{3,2,1,0:T(8,128)(2,1)S(1)} %pad_maximum_fusion.3.own_ref), channel_id=1, source_target_pairs={{0,2},{2,0},{4,6},{6,4},{8,10},{10,8},{12,14},{14,12},{1,3},{3,1},... | collective-permute-start | bytes 3538952 | tf_op jit(solution)/shard_map/ppermute | solution.py:191
  244.5 8.5 %collective-permute-start.52 = (bf16[2,96,1024]{2,1,0:T(8,128)(2,1)S(1)}, bf16[2,96,1024]{2,1,0:T(8,128)(2,1)S(1)}, u32[]{:S(2)}, u32[]{:S(2)}) collective-permute-start(bf16[2,96,1024]{2,1,0:T(8,128)(2,1)S(1)} %collective-permute-done.51), channel_id=1, source_target_pairs={{8,12},{10,14},{9,13},{11,15},{24,28},{26,30},{25,29},{27,31}} | collective-permute-start | bytes 1179656 | tf_op jit(solution)/shard_map/ppermute | solution.py:184
  245.2 15.4 %collective-permute-start.54 = (bf16[2,96,1024]{2,1,0:T(8,128)(2,1)S(1)}, bf16[2,96,1024]{2,1,0:T(8,128)(2,1)S(1)}, u32[]{:S(2)}, u32[]{:S(2)}) collective-permute-start(bf16[2,96,1024]{2,1,0:T(8,128)(2,1)S(1)} %collective-permute-done.53), channel_id=1, source_target_pairs={{4,0},{6,2},{5,1},{7,3},{20,16},{22,18},{21,17},{23,19}} | collective-permute-start | bytes 1179656 | tf_op jit(solution)/shard_map/ppermute | solution.py:185
  252.2 15.1 %collective-permute-start.45 = (bf16[2,96,1024]{2,1,0:T(8,128)(2,1)S(1)}, bf16[2,96,1024]{2,1,0:T(8,128)(2,1)S(1)}, u32[]{:S(2)}, u32[]{:S(2)}) collective-permute-start(bf16[2,96,1024]{2,1,0:T(8,128)(2,1)S(1)} %collective-permute-done.44), channel_id=1, source_target_pairs={{8,12},{10,14},{9,13},{11,15},{24,28},{26,30},{25,29},{27,31}} | collective-permute-start | bytes 1179656 | tf_op jit(solution)/shard_map/ppermute | solution.py:184
  253.0 16.1 %collective-permute-start.47 = (bf16[2,96,1024]{2,1,0:T(8,128)(2,1)S(1)}, bf16[2,96,1024]{2,1,0:T(8,128)(2,1)S(1)}, u32[]{:S(2)}, u32[]{:S(2)}) collective-permute-start(bf16[2,96,1024]{2,1,0:T(8,128)(2,1)S(1)} %collective-permute-done.46), channel_id=1, source_target_pairs={{4,0},{6,2},{5,1},{7,3},{20,16},{22,18},{21,17},{23,19}} | collective-permute-start | bytes 1179656 | tf_op jit(solution)/shard_map/ppermute | solution.py:185
  260.9 18.1 %collective-permute-start.55 = (bf16[4,2,96,1024]{3,2,1,0:T(8,128)(2,1)S(1)}, bf16[4,2,96,1024]{3,2,1,0:T(8,128)(2,1)S(1)}, u32[]{:S(2)}, u32[]{:S(2)}) collective-permute-start(bf16[4,2,96,1024]{3,2,1,0:T(8,128)(2,1)S(1)} %pad_maximum_fusion.2.own_ref), channel_id=1, source_target_pairs={{0,2},{2,0},{4,6},{6,4},{8,10},{10,8},{12,14},{14,12},{1,3},{3,1},... | collective-permute-start | bytes 4718600 | tf_op jit(solution)/shard_map/ppermute | solution.py:191
  269.3 16.5 %collective-permute-start.48 = (bf16[4,2,96,1024]{3,2,1,0:T(8,128)(2,1)S(1)}, bf16[4,2,96,1024]{3,2,1,0:T(8,128)(2,1)S(1)}, u32[]{:S(2)}, u32[]{:S(2)}) collective-permute-start(bf16[4,2,96,1024]{3,2,1,0:T(8,128)(2,1)S(1)} %pad_maximum_fusion.1.own_ref), channel_id=1, source_target_pairs={{0,2},{2,0},{4,6},{6,4},{8,10},{10,8},{12,14},{14,12},{1,3},{3,1},... | collective-permute-start | bytes 4718600 | tf_op jit(solution)/shard_map/ppermute | solution.py:191
  (9 other events, 42.6 us)

commit v2 on v1

--- a/solution.py
+++ b/solution.py
@@ -92,6 +92,10 @@
     )(features, own, other, *totals)
 
 
+def tie(value, *after):
+    return lax.optimization_barrier((value, after))[0]
+
+
 def cut(units, shares):
     edges = [round(units * sum(shares[:i]) / sum(shares)) for i in range(len(shares) + 1)]
     return [(a, b - a) for a, b in zip(edges, edges[1:]) if b > a]
@@ -119,18 +123,23 @@
     def back(first, last):
         return [(2 * i + c, 2 * i - 2 + c) for i in range(first, last + 1) for c in (0, 1)]
 
-    def gather_rows(mine):
-        if n_row != 2:
-            return lax.all_gather(mine, "row", axis=1, tiled=True)
-        theirs = lax.ppermute(mine, "row", swap)
-        return jnp.where(
-            row == 0,
-            jnp.concatenate([mine, theirs], axis=1),
-            jnp.concatenate([theirs, mine], axis=1),
-        )
-
-    features = gather_rows(tokens[0])
-    others = lax.ppermute(features, "depth", swap)
+    mine_wide = tokens[0]
+    if n_row == 2:
+        over_row = lax.ppermute(mine_wide, "row", swap)
+        over_depth = lax.ppermute(mine_wide, "depth", swap)
+        over_both = lax.ppermute(over_row, "depth", swap)
+
+        def join(mine, theirs):
+            return jnp.where(
+                row == 0,
+                jnp.concatenate([mine, theirs], axis=1),
+                jnp.concatenate([theirs, mine], axis=1),
+            )
+
+        features = (join(mine_wide, over_row), join(over_depth, over_both))
+    else:
+        features = lax.all_gather(mine_wide, "row", axis=1, tiled=True)
+        features = (features, lax.ppermute(features, "depth", swap))
 
     def arrange(values):
         values = values.reshape(line, 2, slab, depth)
@@ -139,60 +148,99 @@
         theirs = lax.dynamic_index_in_dim(values, 1 - core, 1, keepdims=False)
         return jnp.stack([mine, theirs])
 
-    picked = jnp.stack([arrange(features), arrange(others)], axis=2)
-    picked = picked.reshape(2 * line * 2 * slab, depth)
-    turned = picked.T
+    single = [arrange(values) for values in features]
+    double = jnp.stack(single, axis=2).reshape(-1, depth)
+    picked = {
+        (0,): single[0].reshape(-1, depth),
+        (1,): single[1].reshape(-1, depth),
+        (0, 1): double,
+    }
+    turned = double.T
 
     cotangent = grad_hidden[0]
     mine = lax.dynamic_slice_in_dim(cotangent, part * half, half, 1)
     theirs = lax.dynamic_slice_in_dim(cotangent, (1 - part) * half, half, 1)
-    cotangent = jnp.stack([mine, lax.ppermute(theirs, "depth", swap)])
+    cotangent = (mine, lax.ppermute(theirs, "depth", swap))
 
     first_tile = (part * (half // tile)).astype(jnp.int32).reshape(1)
     wide = lambda x: x.astype(jnp.float32)
 
-    totals, hidden_own, hidden_other = (), [], []
-    for begin, count in cut(half // tile, SHARES):
-        start, width = begin * tile, count * tile
+    pieces = []
+    for i, (begin, count) in enumerate(cut(half // tile, SHARES)):
+        for batches in ((0,), (1,)) if i == 0 else ((0, 1),):
+            pieces.append((batches, begin * tile, count * tile))
+
+    def multiply(k, after):
+        batches, start, width = pieces[k]
+        rows = tie(picked[batches], after)
         other, own = forward(
-            first_tile, picked, gate_weight, up_weight, start, width, tile, line, scale
+            first_tile, rows, gate_weight, up_weight, start, width, tile, line, scale
         )
         got = lax.ppermute(other.astype(WIRE), "col", pairs)
-        both = (own + wide(got)).astype(WIRE)
-        right = left = None
-        for o in range(line - 1, 0, -1):
-            to_right, to_left = both[o], both[line - o]
-            if right is not None:
-                to_right = (wide(to_right) + wide(right)).astype(WIRE)
-                to_left = (wide(to_left) + wide(left)).astype(WIRE)
-            right = lax.ppermute(to_right, "col", ahead(0, line - 1 - o))
-            left = lax.ppermute(to_left, "col", back(o, line - 1))
-        summed = (wide(both[0]) + wide(right) + wide(left)) * (1.0 / scale)
-        summed = summed.reshape(2, 2, slab, width)
+        return (own + wide(got)).astype(WIRE)
+
+    def activate(k, summed):
+        batches, start, width = pieces[k]
+        summed = (summed * (1.0 / scale)).reshape(2, len(batches), slab, width)
         gate_sum, up_sum = summed[0], summed[1]
         squash = jax.nn.sigmoid(gate_sum)
         hidden = (gate_sum * squash * up_sum).astype(jnp.bfloat16)
-        given = wide(cotangent[:, :, start : start + width])
+        given = jnp.stack([wide(cotangent[b][:, start : start + width]) for b in batches])
         gate_act = given * up_sum * squash * (1.0 + gate_sum * (1.0 - squash))
         up_act = given * gate_sum * squash
-        act = jnp.stack([gate_act, up_act]).astype(jnp.bfloat16).reshape(2, 2 * slab, width)
-        hidden_own.append(hidden[0])
-        hidden_other.append(lax.ppermute(hidden[1], "depth", swap))
-
+        act = jnp.stack([gate_act, up_act]).astype(jnp.bfloat16)
+        for position, batch in enumerate(batches):
+            hiddens[batch].append(hidden[position])
+        return act.reshape(2, len(batches) * slab, width)
+
+    hiddens, totals, waiting = ([], []), (), []
+    last = len(pieces) - 1
+    both = {0: multiply(0, ())}
+    both[1] = multiply(1, ())
+    act = None
+    for k in range(-1, last + 1):
+        right = left = None
         from_left, from_right = [act], [act]
         for step in range(1, line):
-            from_left.append(lax.ppermute(from_left[-1], "col", ahead(step - 1, line - 2)))
-            from_right.append(lax.ppermute(from_right[-1], "col", back(1, line - step)))
-        blocks = [act]
-        for o in range(1, line):
-            blocks.append(jnp.where(place + o < line, from_right[o], from_left[line - o]))
-        gathered = jnp.stack(blocks)
-        totals = gradient(
-            turned, gathered, lax.ppermute(gathered, "col", pairs), totals, half, start, tile
-        )
-
-    own = jnp.concatenate(hidden_own, axis=1)
-    other = jnp.concatenate(hidden_other, axis=1)
+            if k < last:
+                o = line - step
+                to_right, to_left = both[k + 1][o], both[k + 1][line - o]
+                if right is not None:
+                    to_right = (wide(to_right) + wide(right)).astype(WIRE)
+                    to_left = (wide(to_left) + wide(left)).astype(WIRE)
+                if step > 1 and act is not None:
+                    to_right, to_left = tie(
+                        (to_right, to_left), from_left[step - 1], from_right[step - 1]
+                    )
+                right = lax.ppermute(to_right, "col", ahead(0, step - 1))
+                left = lax.ppermute(to_left, "col", back(o, line - 1))
+            if act is not None:
+                to_right, to_left = from_left[-1], from_right[-1]
+                from_left.append(lax.ppermute(to_right, "col", ahead(step - 1, line - 2)))
+                from_right.append(lax.ppermute(to_left, "col", back(1, line - step)))
+            if step == 1 and k + 3 <= last:
+                both[k + 3] = multiply(k + 3, both[k + 1])
+        if k < last:
+            ready = activate(k + 1, wide(both[k + 1][0]) + wide(right) + wide(left))
+        if act is not None:
+            blocks = [act]
+            for o in range(1, line):
+                blocks.append(jnp.where(place + o < line, from_right[o], from_left[line - o]))
+            gathered = jnp.stack(blocks)
+            gathered = (gathered, lax.ppermute(gathered, "col", pairs))
+            waiting.append(gathered)
+            batches, start, width = pieces[k]
+            if batches != (0,):
+                if batches == (1,):
+                    gathered = [jnp.concatenate(both_batches, axis=2) for both_batches in zip(*waiting)]
+                waiting = []
+                totals = gradient(turned, *gathered, totals, half, start, tile)
+                if k < last - 1:
+                    both[k + 2] = tie(both[k + 2], *totals)
+        act = ready
+
+    own, other = (jnp.concatenate(parts, axis=1) for parts in hiddens)
+    other = lax.ppermute(other, "depth", swap)
     hidden = jnp.where(
         part == 0,
         jnp.concatenate([own, other], axis=1),
@@ -201,7 +249,7 @@
     return (hidden[None], *totals)
 
 
-SHARES = (3, 4, 4, 3)
+SHARES = (4, 4, 4, 2)
 
 
 def solution(mesh):

time: 299 us -> 336 us (1.12)
  starting transfers between devices: 135 us -> 158 us
  waiting for transfers between devices: 85.8 us -> 100 us
    ppermute x51 -> x60, starting transfers between devices: 123 us -> 145 us  [the longest x15 65.7 us: local(): right = lax.ppermute(to_right, 'col', ahead(0, step - 1))]
    ppermute x51 -> x60, waiting for transfers between devices: 75.1 us -> 96.8 us  [the longest x15 58.6 us: local(): from_right.append(lax.ppermute(to_left, 'col', back(1, line - step)))]
    ppermute x12 -> x15, waiting for transfers between devices: 10.7 us -> 3.44 us  [local(): left = lax.ppermute(to_left, 'col', back(o, line - 1))]
    convert_element_type x8 -> x2, other arithmetic: 4.19 us -> 0.25 us  [local(): to_right = (wide(to_right) + wide(right)).astype(WIRE)]
    ppermute x12 -> x15, starting transfers between devices: 12.2 us -> 13.2 us  [local(): left = lax.ppermute(to_left, 'col', back(o, line - 1))]
    pallas_call x4 -> x5, Pallas kernels: 25.1 us -> 26 us  [forward(): pl.pallas_call(functools.partial(forward_kernel, scale), out_shape=(out_s...]
    convert_element_type x8 -> x21, other arithmetic: 10.3 us -> 11.2 us  [the longest x5 4.9 us: multiply(): return (own + wide(got)).astype(WIRE)]
  transfers between devices with their start and end apart: 63 -> 75, of which waited for: 20 -> 25; matrix products, arithmetic and copies ran while one was open for 8% -> 7% of each run, Pallas kernels for 13% -> 14%
where the time goes in v2:
time: 336 us; the launch traced here: 334 us
  starting transfers between devices  158 us (47%)
  waiting for transfers between devices  100 us (30%)
  Pallas kernels  50.4 us (15%)
  other arithmetic  18.8 us (6%)
  local copies, waits for them, and re-layouts  4.81 us (1%)
    ppermute x15, starting transfers between devices, local(): right = lax.ppermute(to_right, 'col', ahead(0, step - 1))  65.7 us
    ppermute x15, waiting for transfers between devices, local(): from_right.append(lax.ppermute(to_left, 'col', back(1, line - step)))  58.6 us
    pallas_call x5, Pallas kernels, forward(): pl.pallas_call(functools.partial(forward_kernel, scale), out_shape=(out_s...  26 us
    pallas_call x4, Pallas kernels, gradient(): pl.pallas_call(gradient_kernel, out_shape=(out_shape, out_shape), grid=(w...  24.4 us
    ppermute x15, starting transfers between devices, local(): from_left.append(lax.ppermute(to_right, 'col', ahead(step - 1, line - 2)))  24 us
    ppermute x15, starting transfers between devices, local(): from_right.append(lax.ppermute(to_left, 'col', back(1, line - step)))  19.7 us
    ppermute x5, starting transfers between devices, local(): gathered = (gathered, lax.ppermute(gathered, 'col', pairs))  18.2 us
    ppermute x15, waiting for transfers between devices, local(): right = lax.ppermute(to_right, 'col', ahead(0, step - 1))  13.4 us
  transfers between devices with their start and end apart: 75, of which 25 were waited for; matrix products, arithmetic and copies ran while one was open for 7% of the time, Pallas kernels for 14%

profile of v2, /device:TPU:1, one launch (start us, length us, event | category | flops | bytes accessed | tf_op | source)
XLA Modules:
  0.0 334.3 jit_solution(1600863646719402988)
XLA Ops:
  0.6 2.1 collective-permute-start
  4.0 7.8 %collective-permute-done = bf16[384,512]{1,0:T(8,128)(2,1)S(1)} collective-permute-done((bf16[384,512]{1,0:T(8,128)(2,1)}, bf16[384,512]{1,0:T(8,128)(2,1)S(1)}, u32[]{:S(2)}, u32[]{:S(2)}) %collective-permute-start) | collective-permute-done | bytes 393248 | tf_op jit(solution)/shard_map/ppermute | solution.py:128
  15.3 5.9 %collective-permute-done.9 = bf16[384,512]{1,0:T(8,128)(2,1)S(1)} collective-permute-done((bf16[384,512]{1,0:T(8,128)(2,1)S(1)}, bf16[384,512]{1,0:T(8,128)(2,1)S(1)}, u32[]{:S(2)}, u32[]{:S(2)}) %collective-permute-start.9) | collective-permute-done | bytes 393248 | tf_op jit(solution)/shard_map/ppermute | solution.py:130
  22.0 4.4 %shard_map.67 = (f32[4,2,48,1024]{3,2,1,0:T(8,128)S(1)}, f32[4,2,48,1024]{3,2,1,0:T(8,128)S(1)}) custom-call(s32[1]{0:T(128)} %bitcast.place_ref, bf16[384,1024]{1,0:T(8,128)(2,1)S(1)} %bitcast.219, bf16[1024,7168]{1,0:T(8,128)(2,1)} %gate_ref.9, bf16[1024,7168]{1,0:T(8,128)(2,1)} %up_ref.9), custom_call_target="tpu_custom_call" | custom-call | flops 1610612736 | bytes 8126464 | tf_op jit(solution)/shard_map/pallas_call | solution.py:33
  27.6 3.9 %collective-permute-start.1 = (f16[4,2,48,1024]{3,2,1,0:T(8,128)(2,1)}, f16[4,2,48,1024]{3,2,1,0:T(8,128)(2,1)}, u32[]{:S(2)}, u32[]{:S(2)}) collective-permute-start(f16[4,2,48,1024]{3,2,1,0:T(8,128)(2,1)} %convert_element_type.362), channel_id=1, source_target_pairs={{0,2},{2,0},{4,6},{6,4},{8,10},{10,8},{12,14},{14,12},{1,3},{3,1},... | collective-permute-start | bytes 2359304 | tf_op jit(solution)/shard_map/ppermute | solution.py:179
  32.6 4.4 %shard_map.69 = (f32[4,2,48,1024]{3,2,1,0:T(8,128)S(1)}, f32[4,2,48,1024]{3,2,1,0:T(8,128)S(1)}) custom-call(s32[1]{0:T(128)} %bitcast.place_ref, bf16[384,1024]{1,0:T(8,128)(2,1)S(1)} %bitcast.220, bf16[1024,7168]{1,0:T(8,128)(2,1)} %gate_ref.9, bf16[1024,7168]{1,0:T(8,128)(2,1)} %up_ref.9), custom_call_target="tpu_custom_call" | custom-call | flops 1610612736 | bytes 8126464 | tf_op jit(solution)/shard_map/pallas_call | solution.py:33
  40.0 2.0 add_convert_fusion.4
  42.1 3.5 %collective-permute-start.2 = (f16[2,48,1024]{2,1,0:T(8,128)(2,1)S(1)}, f16[2,48,1024]{2,1,0:T(8,128)(2,1)S(1)}, u32[]{:S(2)}, u32[]{:S(2)}) collective-permute-start(f16[2,48,1024]{2,1,0:T(8,128)(2,1)S(1)} %get-tuple-element.115), channel_id=1, source_target_pairs={{0,4},{2,6},{1,5},{3,7},{16,20},{18,22},{17,21},{19,23}} | collective-permute-start | bytes 589832 | tf_op jit(solution)/shard_map/ppermute | solution.py:215
  46.3 1.4 add_convert_fusion.3
  47.7 1.6 collective-permute-done.2
  49.4 4.1 %collective-permute-start.3 = (f16[2,48,1024]{2,1,0:T(8,128)(2,1)S(1)}, f16[2,48,1024]{2,1,0:T(8,128)(2,1)S(1)}, u32[]{:S(2)}, u32[]{:S(2)}) collective-permute-start(f16[2,48,1024]{2,1,0:T(8,128)(2,1)S(1)} %get-tuple-element.113), channel_id=1, source_target_pairs={{0,4},{2,6},{4,8},{6,10},{1,5},{3,7},{5,9},{7,11},{16,20},{18,22},... | collective-permute-start | bytes 589832 | tf_op jit(solution)/shard_map/ppermute | solution.py:215
  54.2 6.8 %shard_map.70 = (f32[4,2,96,1024]{3,2,1,0:T(8,128)S(1)}, f32[4,2,96,1024]{3,2,1,0:T(8,128)}) custom-call(s32[1]{0:T(128)} %bitcast.place_ref, bf16[768,1024]{1,0:T(8,128)(2,1)S(1)} %bitcast.212, bf16[1024,7168]{1,0:T(8,128)(2,1)} %gate_ref.9, bf16[1024,7168]{1,0:T(8,128)(2,1)} %up_ref.9), custom_call_target="tpu_custom_call" | custom-call | flops 3221225472 | bytes 12058624 | tf_op jit(solution)/shard_map/pallas_call | solution.py:33
  61.1 1.5 convert_element_type.421
  62.5 1.6 collective-permute-start.33
  65.6 5.1 %collective-permute-start.4 = (f16[2,48,1024]{2,1,0:T(8,128)(2,1)S(1)}, f16[2,48,1024]{2,1,0:T(8,128)(2,1)S(1)}, u32[]{:S(2)}, u32[]{:S(2)}) collective-permute-start(f16[2,48,1024]{2,1,0:T(8,128)(2,1)S(1)} %get-tuple-element.111), channel_id=1, source_target_pairs={{0,4},{2,6},{4,8},{6,10},{8,12},{10,14},{1,5},{3,7},{5,9},{7,11},{... | collective-permute-start | bytes 589832 | tf_op jit(solution)/shard_map/ppermute | solution.py:215
  71.5 4.3 %collective-permute-start.15 = (f16[2,48,1024]{2,1,0:T(8,128)(2,1)S(1)}, f16[2,48,1024]{2,1,0:T(8,128)(2,1)S(1)}, u32[]{:S(2)}, u32[]{:S(2)}) collective-permute-start(f16[2,48,1024]{2,1,0:T(8,128)(2,1)S(1)} %get-tuple-element.120), channel_id=1, source_target_pairs={{0,4},{2,6},{1,5},{3,7},{16,20},{18,22},{17,21},{19,23}} | collective-permute-start | bytes 589832 | tf_op jit(solution)/shard_map/ppermute | solution.py:215
  76.0 3.5 %collective-permute-start.17 = (bf16[2,48,1024]{2,1,0:T(8,128)(2,1)S(1)}, bf16[2,48,1024]{2,1,0:T(8,128)(2,1)S(1)}, u32[]{:S(2)}, u32[]{:S(2)}) collective-permute-start(bf16[2,48,1024]{2,1,0:T(8,128)(2,1)S(1)} %pad_maximum_fusion.16), channel_id=1, source_target_pairs={{0,4},{2,6},{4,8},{6,10},{8,12},{10,14},{1,5},{3,7},{5,9},{7,11},{... | collective-permute-start | bytes 589832 | tf_op jit(solution)/shard_map/ppermute | solution.py:219
  81.0 2.8 collective-permute-done.17
  83.8 4.0 %collective-permute-done.18 = bf16[2,48,1024]{2,1,0:T(8,128)(2,1)S(1)} collective-permute-done((bf16[2,48,1024]{2,1,0:T(8,128)(2,1)S(1)}, bf16[2,48,1024]{2,1,0:T(8,128)(2,1)S(1)}, u32[]{:S(2)}, u32[]{:S(2)}) %collective-permute-start.18) | collective-permute-done | bytes 196640 | tf_op jit(solution)/shard_map/ppermute | solution.py:220
  88.5 3.7 %collective-permute-start.19 = (f16[2,48,1024]{2,1,0:T(8,128)(2,1)S(1)}, f16[2,48,1024]{2,1,0:T(8,128)(2,1)S(1)}, u32[]{:S(2)}, u32[]{:S(2)}) collective-permute-start(f16[2,48,1024]{2,1,0:T(8,128)(2,1)S(1)} %get-tuple-element.49), channel_id=1, source_target_pairs={{0,4},{2,6},{4,8},{6,10},{1,5},{3,7},{5,9},{7,11},{16,20},{18,22},... | collective-permute-start | bytes 589832 | tf_op jit(solution)/shard_map/ppermute | solution.py:215
  92.2 6.8 %shard_map.68 = (f32[4,2,96,1024]{3,2,1,0:T(8,128)S(1)}, f32[4,2,96,1024]{3,2,1,0:T(8,128)}) custom-call(s32[1]{0:T(128)} %bitcast.place_ref, bf16[768,1024]{1,0:T(8,128)(2,1)S(1)} %bitcast.213, bf16[1024,7168]{1,0:T(8,128)(2,1)} %gate_ref.9, bf16[1024,7168]{1,0:T(8,128)(2,1)} %up_ref.9), custom_call_target="tpu_custom_call" | custom-call | flops 3221225472 | bytes 12058624 | tf_op jit(solution)/shard_map/pallas_call | solution.py:33
  99.3 2.3 collective-permute-start.10
  103.8 8.7 %collective-permute-done.22 = bf16[2,48,1024]{2,1,0:T(8,128)(2,1)S(1)} collective-permute-done((bf16[2,48,1024]{2,1,0:T(8,128)(2,1)S(1)}, bf16[2,48,1024]{2,1,0:T(8,128)(2,1)S(1)}, u32[]{:S(2)}, u32[]{:S(2)}) %collective-permute-start.22) | collective-permute-done | bytes 196640 | tf_op jit(solution)/shard_map/ppermute | solution.py:220
  113.8 4.0 %collective-permute-start.23 = (f16[2,48,1024]{2,1,0:T(8,128)(2,1)S(1)}, f16[2,48,1024]{2,1,0:T(8,128)(2,1)S(1)}, u32[]{:S(2)}, u32[]{:S(2)}) collective-permute-start(f16[2,48,1024]{2,1,0:T(8,128)(2,1)S(1)} %get-tuple-element.51), channel_id=1, source_target_pairs={{0,4},{2,6},{4,8},{6,10},{8,12},{10,14},{1,5},{3,7},{5,9},{7,11},{... | collective-permute-start | bytes 589832 | tf_op jit(solution)/shard_map/ppermute | solution.py:215
  122.2 1.6 collective-permute-start.26
  124.9 3.6 %collective-permute-start.25 = (bf16[2,48,1024]{2,1,0:T(8,128)(2,1)S(1)}, bf16[2,48,1024]{2,1,0:T(8,128)(2,1)S(1)}, u32[]{:S(2)}, u32[]{:S(2)}) collective-permute-start(bf16[2,48,1024]{2,1,0:T(8,128)(2,1)S(1)} %pad_maximum_fusion.17), channel_id=1, source_target_pairs={{0,4},{2,6},{4,8},{6,10},{8,12},{10,14},{1,5},{3,7},{5,9},{7,11},{... | collective-permute-start | bytes 589832 | tf_op jit(solution)/shard_map/ppermute | solution.py:219
  128.7 2.1 collective-permute-start.38
  134.3 3.8 %collective-permute-done.30 = bf16[2,48,1024]{2,1,0:T(8,128)(2,1)S(1)} collective-permute-done((bf16[2,48,1024]{2,1,0:T(8,128)(2,1)S(1)}, bf16[2,48,1024]{2,1,0:T(8,128)(2,1)S(1)}, u32[]{:S(2)}, u32[]{:S(2)}) %collective-permute-start.30) | collective-permute-done | bytes 196640 | tf_op jit(solution)/shard_map/ppermute | solution.py:220
  138.1 3.2 collective-permute-start.11
  142.7 5.1 %collective-permute-done.37 = bf16[2,48,1024]{2,1,0:T(8,128)(2,1)S(1)} collective-permute-done((bf16[2,48,1024]{2,1,0:T(8,128)(2,1)S(1)}, bf16[2,48,1024]{2,1,0:T(8,128)(2,1)S(1)}, u32[]{:S(2)}, u32[]{:S(2)}) %collective-permute-start.37) | collective-permute-done | bytes 196640 | tf_op jit(solution)/shard_map/ppermute | solution.py:220
  148.6 3.9 %collective-permute-start.39 = (bf16[4,2,48,1024]{3,2,1,0:T(8,128)(2,1)S(1)}, bf16[4,2,48,1024]{3,2,1,0:T(8,128)(2,1)S(1)}, u32[]{:S(2)}, u32[]{:S(2)}) collective-permute-start(bf16[4,2,48,1024]{3,2,1,0:T(8,128)(2,1)S(1)} %pad_maximum_fusion.11), channel_id=1, source_target_pairs={{0,2},{2,0},{4,6},{6,4},{8,10},{10,8},{12,14},{14,12},{1,3},{3,1},... | collective-permute-start | bytes 2359304 | tf_op jit(solution)/shard_map/ppermute | solution.py:230
  153.5 2.0 collective-permute-start.27
  156.3 6.2 %collective-permute-done.27 = f16[2,96,1024]{2,1,0:T(8,128)(2,1)S(1)} collective-permute-done((f16[2,96,1024]{2,1,0:T(8,128)(2,1)S(1)}, f16[2,96,1024]{2,1,0:T(8,128)(2,1)S(1)}, u32[]{:S(2)}, u32[]{:S(2)}) %collective-permute-start.27) | collective-permute-done | bytes 393248 | tf_op jit(solution)/shard_map/ppermute | solution.py:215
  164.2 4.8 %collective-permute-start.31 = (f16[2,96,1024]{2,1,0:T(8,128)(2,1)S(1)}, f16[2,96,1024]{2,1,0:T(8,128)(2,1)S(1)}, u32[]{:S(2)}, u32[]{:S(2)}) collective-permute-start(f16[2,96,1024]{2,1,0:T(8,128)(2,1)S(1)} %get-tuple-element.55), channel_id=1, source_target_pairs={{0,4},{2,6},{4,8},{6,10},{8,12},{10,14},{1,5},{3,7},{5,9},{7,11},{... | collective-permute-start | bytes 1179656 | tf_op jit(solution)/shard_map/ppermute | solution.py:215
  169.2 6.8 %shard_map.71 = (f32[1024,3584]{1,0:T(8,128)}, f32[1024,3584]{1,0:T(8,128)}) custom-call(bf16[1024,768]{1,0:T(8,128)(2,1)S(1)} %bitcast.215, bf16[4,2,96,1024]{3,2,1,0:T(8,128)(2,1)S(1)} %maximum_maximum_fusion.own_ref, bf16[4,2,96,1024]{3,2,1,0:T(8,128)(2,1)S(1)} %pad_maximum_fusion.1.other_ref), custom_call_target="tpu_custom_call" | custom-call | flops 3221225472 | bytes 13107200 | tf_op jit(solution)/shard_map/pallas_call | solution.py:79
  176.8 3.7 %collective-permute-start.40 = (f16[2,96,1024]{2,1,0:T(8,128)(2,1)S(1)}, f16[2,96,1024]{2,1,0:T(8,128)(2,1)S(1)}, u32[]{:S(2)}, u32[]{:S(2)}) collective-permute-start(f16[2,96,1024]{2,1,0:T(8,128)(2,1)S(1)} %get-tuple-element.88), channel_id=1, source_target_pairs={{0,4},{2,6},{1,5},{3,7},{16,20},{18,22},{17,21},{19,23}} | collective-permute-start | bytes 1179656 | tf_op jit(solution)/shard_map/ppermute | solution.py:215
  181.1 1.4 collective-permute-start.43
  182.5 4.0 %collective-permute-start.42 = (bf16[2,96,1024]{2,1,0:T(8,128)(2,1)S(1)}, bf16[2,96,1024]{2,1,0:T(8,128)(2,1)S(1)}, u32[]{:S(2)}, u32[]{:S(2)}) collective-permute-start(bf16[2,96,1024]{2,1,0:T(8,128)(2,1)S(1)} %pad_maximum_fusion.13), channel_id=1, source_target_pairs={{0,4},{2,6},{4,8},{6,10},{8,12},{10,14},{1,5},{3,7},{5,9},{7,11},{... | collective-permute-start | bytes 1179656 | tf_op jit(solution)/shard_map/ppermute | solution.py:219
  186.9 4.0 %collective-permute-done.43 = bf16[2,96,1024]{2,1,0:T(8,128)(2,1)S(1)} collective-permute-done((bf16[2,96,1024]{2,1,0:T(8,128)(2,1)S(1)}, bf16[2,96,1024]{2,1,0:T(8,128)(2,1)S(1)}, u32[]{:S(2)}, u32[]{:S(2)}) %collective-permute-start.43) | collective-permute-done | bytes 393248 | tf_op jit(solution)/shard_map/ppermute | solution.py:220
  190.9 4.6 %collective-permute-done.42 = bf16[2,96,1024]{2,1,0:T(8,128)(2,1)S(1)} collective-permute-done((bf16[2,96,1024]{2,1,0:T(8,128)(2,1)S(1)}, bf16[2,96,1024]{2,1,0:T(8,128)(2,1)S(1)}, u32[]{:S(2)}, u32[]{:S(2)}) %collective-permute-start.42) | collective-permute-done | bytes 393248 | tf_op jit(solution)/shard_map/ppermute | solution.py:219
  196.2 4.7 %collective-permute-start.44 = (f16[2,96,1024]{2,1,0:T(8,128)(2,1)S(1)}, f16[2,96,1024]{2,1,0:T(8,128)(2,1)S(1)}, u32[]{:S(2)}, u32[]{:S(2)}) collective-permute-start(f16[2,96,1024]{2,1,0:T(8,128)(2,1)S(1)} %get-tuple-element.63), channel_id=1, source_target_pairs={{0,4},{2,6},{4,8},{6,10},{1,5},{3,7},{5,9},{7,11},{16,20},{18,22},... | collective-permute-start | bytes 1179656 | tf_op jit(solution)/shard_map/ppermute | solution.py:215
  203.8 3.5 %shard_map.72 = (f32[4,2,96,512]{3,2,1,0:T(8,128)S(1)}, f32[4,2,96,512]{3,2,1,0:T(8,128)S(1)}) custom-call(s32[1]{0:T(128)} %bitcast.place_ref, bf16[768,1024]{1,0:T(8,128)(2,1)S(1)} %bitcast.214, bf16[1024,7168]{1,0:T(8,128)(2,1)} %gate_ref.9, bf16[1024,7168]{1,0:T(8,128)(2,1)} %up_ref.9), custom_call_target="tpu_custom_call" | custom-call | flops 1610612736 | bytes 6815744 | tf_op jit(solution)/shard_map/pallas_call | solution.py:33
  207.5 3.1 collective-permute-start.50
  214.0 8.4 %collective-permute-start.48 = (f16[2,96,1024]{2,1,0:T(8,128)(2,1)S(1)}, f16[2,96,1024]{2,1,0:T(8,128)(2,1)S(1)}, u32[]{:S(2)}, u32[]{:S(2)}) collective-permute-start(f16[2,96,1024]{2,1,0:T(8,128)(2,1)S(1)} %get-tuple-element.65), channel_id=1, source_target_pairs={{0,4},{2,6},{4,8},{6,10},{8,12},{10,14},{1,5},{3,7},{5,9},{7,11},{... | collective-permute-start | bytes 1179656 | tf_op jit(solution)/shard_map/ppermute | solution.py:215
  223.1 1.6 collective-permute-done.52
  225.1 6.4 %collective-permute-start.53 = (bf16[4,2,96,1024]{3,2,1,0:T(8,128)(2,1)S(1)}, bf16[4,2,96,1024]{3,2,1,0:T(8,128)(2,1)S(1)}, u32[]{:S(2)}, u32[]{:S(2)}) collective-permute-start(bf16[4,2,96,1024]{3,2,1,0:T(8,128)(2,1)S(1)} %pad_maximum_fusion.2.own_ref), channel_id=1, source_target_pairs={{0,2},{2,0},{4,6},{6,4},{8,10},{10,8},{12,14},{14,12},{1,3},{3,1},... | collective-permute-start | bytes 4718600 | tf_op jit(solution)/shard_map/ppermute | solution.py:230
  233.7 1.3 collective-permute-start.56
  236.4 3.7 %collective-permute-done.56 = bf16[2,96,1024]{2,1,0:T(8,128)(2,1)S(1)} collective-permute-done((bf16[2,96,1024]{2,1,0:T(8,128)(2,1)S(1)}, bf16[2,96,1024]{2,1,0:T(8,128)(2,1)S(1)}, u32[]{:S(2)}, u32[]{:S(2)}) %collective-permute-start.56) | collective-permute-done | bytes 393248 | tf_op jit(solution)/shard_map/ppermute | solution.py:219
  240.8 16.9 %collective-permute-done.57 = bf16[2,96,1024]{2,1,0:T(8,128)(2,1)S(1)} collective-permute-done((bf16[2,96,1024]{2,1,0:T(8,128)(2,1)S(1)}, bf16[2,96,1024]{2,1,0:T(8,128)(2,1)S(1)}, u32[]{:S(2)}, u32[]{:S(2)}) %collective-permute-start.57) | collective-permute-done | bytes 393248 | tf_op jit(solution)/shard_map/ppermute | solution.py:220
  259.0 6.8 %shard_map.73 = (f32[1024,3584]{1,0:T(8,128)}, f32[1024,3584]{1,0:T(8,128)}) custom-call(bf16[1024,768]{1,0:T(8,128)(2,1)S(1)} %bitcast.216, bf16[4,2,96,1024]{3,2,1,0:T(8,128)(2,1)S(1)} %pad_maximum_fusion.2.own_ref, bf16[4,2,96,1024]{3,2,1,0:T(8,128)(2,1)S(1)} %collective-permute-done.53.other_ref, ...), custom_call_target="tpu_custom_call", output_to_operand_aliasing={{0}: (3, {}), {1}: (4, {})} | custom-call | flops 3221225472 | bytes 13107200 | tf_op jit(solution)/shard_map/pallas_call | solution.py:79
  266.6 4.7 %collective-permute-start.54 = (f16[2,96,512]{2,1,0:T(8,128)(2,1)S(1)}, f16[2,96,512]{2,1,0:T(8,128)(2,1)S(1)}, u32[]{:S(2)}, u32[]{:S(2)}) collective-permute-start(f16[2,96,512]{2,1,0:T(8,128)(2,1)S(1)} %get-tuple-element.108), channel_id=1, source_target_pairs={{0,4},{2,6},{1,5},{3,7},{16,20},{18,22},{17,21},{19,23}} | collective-permute-start | bytes 589832 | tf_op jit(solution)/shard_map/ppermute | solution.py:215
  273.4 1.4 collective-permute-done.54
  275.5 4.7 %collective-permute-start.58 = (f16[2,96,512]{2,1,0:T(8,128)(2,1)S(1)}, f16[2,96,512]{2,1,0:T(8,128)(2,1)S(1)}, u32[]{:S(2)}, u32[]{:S(2)}) collective-permute-start(f16[2,96,512]{2,1,0:T(8,128)(2,1)S(1)} %get-tuple-element.73), channel_id=1, source_target_pairs={{0,4},{2,6},{4,8},{6,10},{1,5},{3,7},{5,9},{7,11},{16,20},{18,22},... | collective-permute-start | bytes 589832 | tf_op jit(solution)/shard_map/ppermute | solution.py:215
  280.3 2.5 collective-permute-done.58
  284.3 4.7 %collective-permute-start.62 = (f16[2,96,512]{2,1,0:T(8,128)(2,1)S(1)}, f16[2,96,512]{2,1,0:T(8,128)(2,1)S(1)}, u32[]{:S(2)}, u32[]{:S(2)}) collective-permute-start(f16[2,96,512]{2,1,0:T(8,128)(2,1)S(1)} %get-tuple-element.75), channel_id=1, source_target_pairs={{0,4},{2,6},{4,8},{6,10},{8,12},{10,14},{1,5},{3,7},{5,9},{7,11},{... | collective-permute-start | bytes 589832 | tf_op jit(solution)/shard_map/ppermute | solution.py:215
  290.1 1.5 collective-permute-done.62
  293.2 4.7 %collective-permute-start.66 = (bf16[2,96,512]{2,1,0:T(8,128)(2,1)S(1)}, bf16[2,96,512]{2,1,0:T(8,128)(2,1)S(1)}, u32[]{:S(2)}, u32[]{:S(2)}) collective-permute-start(bf16[2,96,512]{2,1,0:T(8,128)(2,1)S(1)} %pad_maximum_fusion.20), channel_id=1, source_target_pairs={{0,4},{2,6},{4,8},{6,10},{8,12},{10,14},{1,5},{3,7},{5,9},{7,11},{... | collective-permute-start | bytes 589832 | tf_op jit(solution)/shard_map/ppermute | solution.py:219
  298.0 1.3 collective-permute-start.64
  299.6 4.2 %collective-permute-start.74 = (bf16[4,2,96,1024]{3,2,1,0:T(8,128)(2,1)S(1)}, bf16[4,2,96,1024]{3,2,1,0:T(8,128)(2,1)S(1)}, u32[]{:S(2)}, u32[]{:S(2)}) collective-permute-start(bf16[4,2,96,1024]{3,2,1,0:T(8,128)(2,1)S(1)} %pad_maximum_fusion.3.own_ref), channel_id=1, source_target_pairs={{0,2},{2,0},{4,6},{6,4},{8,10},{10,8},{12,14},{14,12},{1,3},{3,1},... | collective-permute-start | bytes 4718600 | tf_op jit(solution)/shard_map/ppermute | solution.py:230
  306.0 7.1 %collective-permute-done.69 = bf16[2,96,512]{2,1,0:T(8,128)(2,1)S(1)} collective-permute-done((bf16[2,96,512]{2,1,0:T(8,128)(2,1)S(1)}, bf16[2,96,512]{2,1,0:T(8,128)(2,1)S(1)}, u32[]{:S(2)}, u32[]{:S(2)}) %collective-permute-start.69) | collective-permute-done | bytes 196640 | tf_op jit(solution)/shard_map/ppermute | solution.py:220
  315.2 5.7 %collective-permute-done.70 = bf16[2,96,512]{2,1,0:T(8,128)(2,1)S(1)} collective-permute-done((bf16[2,96,512]{2,1,0:T(8,128)(2,1)S(1)}, bf16[2,96,512]{2,1,0:T(8,128)(2,1)S(1)}, u32[]{:S(2)}, u32[]{:S(2)}) %collective-permute-start.70) | collective-permute-done | bytes 196640 | tf_op jit(solution)/shard_map/ppermute | solution.py:220
  321.1 1.5 collective-permute-start.71
  323.5 6.8 %shard_map.74 = (f32[1024,3584]{1,0:T(8,128)}, f32[1024,3584]{1,0:T(8,128)}) custom-call(bf16[1024,768]{1,0:T(8,128)(2,1)S(1)} %bitcast.217, bf16[4,2,96,1024]{3,2,1,0:T(8,128)(2,1)S(1)} %pad_maximum_fusion.3.own_ref, bf16[4,2,96,1024]{3,2,1,0:T(8,128)(2,1)S(1)} %collective-permute-done.74.other_ref, ...), custom_call_target="tpu_custom_call", output_to_operand_aliasing={{0}: (3, {}), {1}: (4, {})} | custom-call | flops 3221225472 | bytes 13107200 | tf_op jit(solution)/shard_map/pallas_call | solution.py:79
  330.3 4.0 %shard_map.75 = (f32[1024,3584]{1,0:T(8,128)}, f32[1024,3584]{1,0:T(8,128)}) custom-call(bf16[1024,768]{1,0:T(8,128)(2,1)S(1)} %bitcast.218, bf16[4,2,96,512]{3,2,1,0:T(8,128)(2,1)S(1)} %pad_maximum_fusion.12.own_ref, bf16[4,2,96,512]{3,2,1,0:T(8,128)(2,1)S(1)} %collective-permute-done.71.other_ref, ...), custom_call_target="tpu_custom_call", output_to_operand_aliasing={{0}: (3, {}), {1}: (4, {})} | custom-call | flops 1610612736 | bytes 7340032 | tf_op jit(solution)/shard_map/pallas_call | solution.py:79
  (210 shorter events, 63.6 us)
Async XLA Ops:
  0.6 11.2 %collective-permute-start = (bf16[384,512]{1,0:T(8,128)(2,1)}, bf16[384,512]{1,0:T(8,128)(2,1)S(1)}, u32[]{:S(2)}, u32[]{:S(2)}) collective-permute-start(bf16[384,512]{1,0:T(8,128)(2,1)} %bitcast.241), channel_id=1, source_target_pairs={{0,16},{16,0},{1,17},{17,1},{2,18},{18,2},{3,19},{19,3},{4,20},{20... | collective-permute-start | bytes 1179656 | tf_op jit(solution)/shard_map/ppermute | solution.py:128
  2.7 12.6 %collective-permute-start.8 = (bf16[384,512]{1,0:T(8,128)(2,1)}, bf16[384,512]{1,0:T(8,128)(2,1)S(1)}, u32[]{:S(2)}, u32[]{:S(2)}) collective-permute-start(bf16[384,512]{1,0:T(8,128)(2,1)} %bitcast.242), channel_id=1, source_target_pairs={{0,1},{1,0},{2,3},{3,2},{4,5},{5,4},{6,7},{7,6},{8,9},{9,8},{10,11... | collective-permute-start | bytes 1179656 | tf_op jit(solution)/shard_map/ppermute | solution.py:129
  11.8 9.4 %collective-permute-start.9 = (bf16[384,512]{1,0:T(8,128)(2,1)S(1)}, bf16[384,512]{1,0:T(8,128)(2,1)S(1)}, u32[]{:S(2)}, u32[]{:S(2)}) collective-permute-start(bf16[384,512]{1,0:T(8,128)(2,1)S(1)} %collective-permute-done), channel_id=1, source_target_pairs={{0,1},{1,0},{2,3},{3,2},{4,5},{5,4},{6,7},{7,6},{8,9},{9,8},{10,11... | collective-permute-start | bytes 1179656 | tf_op jit(solution)/shard_map/ppermute | solution.py:130
  14.1 17.4 %collective-permute-start.13 = (bf16[48,3584]{1,0:T(8,128)(2,1)S(1)}, bf16[48,3584]{1,0:T(8,128)(2,1)S(1)}, u32[]{:S(2)}, u32[]{:S(2)}) collective-permute-start(bf16[48,3584]{1,0:T(8,128)(2,1)S(1)} %get-tuple-element.138), channel_id=1, source_target_pairs={{0,1},{1,0},{2,3},{3,2},{4,5},{5,4},{6,7},{7,6},{8,9},{9,8},{10,11... | collective-permute-start | bytes 1032200 | tf_op jit(solution)/shard_map/ppermute | solution.py:163
  27.6 12.4 %collective-permute-start.1 = (f16[4,2,48,1024]{3,2,1,0:T(8,128)(2,1)}, f16[4,2,48,1024]{3,2,1,0:T(8,128)(2,1)}, u32[]{:S(2)}, u32[]{:S(2)}) collective-permute-start(f16[4,2,48,1024]{3,2,1,0:T(8,128)(2,1)} %convert_element_type.362), channel_id=1, source_target_pairs={{0,2},{2,0},{4,6},{6,4},{8,10},{10,8},{12,14},{14,12},{1,3},{3,1},... | collective-permute-start | bytes 2359304 | tf_op jit(solution)/shard_map/ppermute | solution.py:179
  38.2 8.0 %collective-permute-start.14 = (f16[4,2,48,1024]{3,2,1,0:T(8,128)(2,1)}, f16[4,2,48,1024]{3,2,1,0:T(8,128)(2,1)}, u32[]{:S(2)}, u32[]{:S(2)}) collective-permute-start(f16[4,2,48,1024]{3,2,1,0:T(8,128)(2,1)} %convert_element_type.394), channel_id=1, source_target_pairs={{0,2},{2,0},{4,6},{6,4},{8,10},{10,8},{12,14},{14,12},{1,3},{3,1},... | collective-permute-start | bytes 2359304 | tf_op jit(solution)/shard_map/ppermute | solution.py:179
  42.1 7.2 %collective-permute-start.2 = (f16[2,48,1024]{2,1,0:T(8,128)(2,1)S(1)}, f16[2,48,1024]{2,1,0:T(8,128)(2,1)S(1)}, u32[]{:S(2)}, u32[]{:S(2)}) collective-permute-start(f16[2,48,1024]{2,1,0:T(8,128)(2,1)S(1)} %get-tuple-element.115), channel_id=1, source_target_pairs={{0,4},{2,6},{1,5},{3,7},{16,20},{18,22},{17,21},{19,23}} | collective-permute-start | bytes 589832 | tf_op jit(solution)/shard_map/ppermute | solution.py:215
  49.4 14.7 %collective-permute-start.3 = (f16[2,48,1024]{2,1,0:T(8,128)(2,1)S(1)}, f16[2,48,1024]{2,1,0:T(8,128)(2,1)S(1)}, u32[]{:S(2)}, u32[]{:S(2)}) collective-permute-start(f16[2,48,1024]{2,1,0:T(8,128)(2,1)S(1)} %get-tuple-element.113), channel_id=1, source_target_pairs={{0,4},{2,6},{4,8},{6,10},{1,5},{3,7},{5,9},{7,11},{16,20},{18,22},... | collective-permute-start | bytes 589832 | tf_op jit(solution)/shard_map/ppermute | solution.py:215
  53.6 10.6 %collective-permute-start.6 = (f16[2,48,1024]{2,1,0:T(8,128)(2,1)S(1)}, f16[2,48,1024]{2,1,0:T(8,128)(2,1)S(1)}, u32[]{:S(2)}, u32[]{:S(2)}) collective-permute-start(f16[2,48,1024]{2,1,0:T(8,128)(2,1)S(1)} %get-tuple-element.114), channel_id=1, source_target_pairs={{8,4},{10,6},{12,8},{14,10},{9,5},{11,7},{13,9},{15,11},{24,20},{2... | collective-permute-start | bytes 589832 | tf_op jit(solution)/shard_map/ppermute | solution.py:216
  62.5 92.9 %collective-permute-start.33 = (f16[4,2,96,1024]{3,2,1,0:T(8,128)(2,1)}, f16[4,2,96,1024]{3,2,1,0:T(8,128)(2,1)S(1)}, u32[]{:S(2)}, u32[]{:S(2)}) collective-permute-start(f16[4,2,96,1024]{3,2,1,0:T(8,128)(2,1)} %convert_element_type.421), channel_id=1, source_target_pairs={{0,2},{2,0},{4,6},{6,4},{8,10},{10,8},{12,14},{14,12},{1,3},{3,1},... | collective-permute-start | bytes 4718600 | tf_op jit(solution)/shard_map/ppermute | solution.py:179
  64.3 11.5 %collective-permute-start.7 = (f16[2,48,1024]{2,1,0:T(8,128)(2,1)S(1)}, f16[2,48,1024]{2,1,0:T(8,128)(2,1)S(1)}, u32[]{:S(2)}, u32[]{:S(2)}) collective-permute-start(f16[2,48,1024]{2,1,0:T(8,128)(2,1)S(1)} %get-tuple-element.112), channel_id=1, source_target_pairs={{4,0},{6,2},{8,4},{10,6},{12,8},{14,10},{5,1},{7,3},{9,5},{11,7},{... | collective-permute-start | bytes 589832 | tf_op jit(solution)/shard_map/ppermute | solution.py:216
  65.6 10.2 %collective-permute-start.4 = (f16[2,48,1024]{2,1,0:T(8,128)(2,1)S(1)}, f16[2,48,1024]{2,1,0:T(8,128)(2,1)S(1)}, u32[]{:S(2)}, u32[]{:S(2)}) collective-permute-start(f16[2,48,1024]{2,1,0:T(8,128)(2,1)S(1)} %get-tuple-element.111), channel_id=1, source_target_pairs={{0,4},{2,6},{4,8},{6,10},{8,12},{10,14},{1,5},{3,7},{5,9},{7,11},{... | collective-permute-start | bytes 589832 | tf_op jit(solution)/shard_map/ppermute | solution.py:215
  70.8 10.0 %collective-permute-start.16 = (f16[2,48,1024]{2,1,0:T(8,128)(2,1)S(1)}, f16[2,48,1024]{2,1,0:T(8,128)(2,1)S(1)}, u32[]{:S(2)}, u32[]{:S(2)}) collective-permute-start(f16[2,48,1024]{2,1,0:T(8,128)(2,1)S(1)} %get-tuple-element.119), channel_id=1, source_target_pairs={{12,8},{14,10},{13,9},{15,11},{28,24},{30,26},{29,25},{31,27}} | collective-permute-start | bytes 589832 | tf_op jit(solution)/shard_map/ppermute | solution.py:216
  71.5 9.4 %collective-permute-start.15 = (f16[2,48,1024]{2,1,0:T(8,128)(2,1)S(1)}, f16[2,48,1024]{2,1,0:T(8,128)(2,1)S(1)}, u32[]{:S(2)}, u32[]{:S(2)}) collective-permute-start(f16[2,48,1024]{2,1,0:T(8,128)(2,1)S(1)} %get-tuple-element.120), channel_id=1, source_target_pairs={{0,4},{2,6},{1,5},{3,7},{16,20},{18,22},{17,21},{19,23}} | collective-permute-start | bytes 589832 | tf_op jit(solution)/shard_map/ppermute | solution.py:215
  76.0 7.8 %collective-permute-start.17 = (bf16[2,48,1024]{2,1,0:T(8,128)(2,1)S(1)}, bf16[2,48,1024]{2,1,0:T(8,128)(2,1)S(1)}, u32[]{:S(2)}, u32[]{:S(2)}) collective-permute-start(bf16[2,48,1024]{2,1,0:T(8,128)(2,1)S(1)} %pad_maximum_fusion.16), channel_id=1, source_target_pairs={{0,4},{2,6},{4,8},{6,10},{8,12},{10,14},{1,5},{3,7},{5,9},{7,11},{... | collective-permute-start | bytes 589832 | tf_op jit(solution)/shard_map/ppermute | solution.py:219
  79.5 8.3 %collective-permute-start.18 = (bf16[2,48,1024]{2,1,0:T(8,128)(2,1)S(1)}, bf16[2,48,1024]{2,1,0:T(8,128)(2,1)S(1)}, u32[]{:S(2)}, u32[]{:S(2)}) collective-permute-start(bf16[2,48,1024]{2,1,0:T(8,128)(2,1)S(1)} %pad_maximum_fusion.16), channel_id=1, source_target_pairs={{4,0},{6,2},{8,4},{10,6},{12,8},{14,10},{5,1},{7,3},{9,5},{11,7},{... | collective-permute-start | bytes 589832 | tf_op jit(solution)/shard_map/ppermute | solution.py:220
  87.8 14.5 %collective-permute-start.20 = (f16[2,48,1024]{2,1,0:T(8,128)(2,1)S(1)}, f16[2,48,1024]{2,1,0:T(8,128)(2,1)S(1)}, u32[]{:S(2)}, u32[]{:S(2)}) collective-permute-start(f16[2,48,1024]{2,1,0:T(8,128)(2,1)S(1)} %get-tuple-element.50), channel_id=1, source_target_pairs={{8,4},{10,6},{12,8},{14,10},{9,5},{11,7},{13,9},{15,11},{24,20},{2... | collective-permute-start | bytes 589832 | tf_op jit(solution)/shard_map/ppermute | solution.py:216
  88.5 15.2 %collective-permute-start.19 = (f16[2,48,1024]{2,1,0:T(8,128)(2,1)S(1)}, f16[2,48,1024]{2,1,0:T(8,128)(2,1)S(1)}, u32[]{:S(2)}, u32[]{:S(2)}) collective-permute-start(f16[2,48,1024]{2,1,0:T(8,128)(2,1)S(1)} %get-tuple-element.49), channel_id=1, source_target_pairs={{0,4},{2,6},{4,8},{6,10},{1,5},{3,7},{5,9},{7,11},{16,20},{18,22},... | collective-permute-start | bytes 589832 | tf_op jit(solution)/shard_map/ppermute | solution.py:215
  99.3 33.5 %collective-permute-start.10 = (f16[4,2,96,1024]{3,2,1,0:T(8,128)(2,1)S(1)}, f16[4,2,96,1024]{3,2,1,0:T(8,128)(2,1)S(1)}, u32[]{:S(2)}, u32[]{:S(2)}) collective-permute-start(f16[4,2,96,1024]{3,2,1,0:T(8,128)(2,1)S(1)} %convert_element_type.382), channel_id=1, source_target_pairs={{0,2},{2,0},{4,6},{6,4},{8,10},{10,8},{12,14},{14,12},{1,3},{3,1},... | collective-permute-start | bytes 4718600 | tf_op jit(solution)/shard_map/ppermute | solution.py:179
  102.3 10.1 %collective-permute-start.22 = (bf16[2,48,1024]{2,1,0:T(8,128)(2,1)S(1)}, bf16[2,48,1024]{2,1,0:T(8,128)(2,1)S(1)}, u32[]{:S(2)}, u32[]{:S(2)}) collective-permute-start(bf16[2,48,1024]{2,1,0:T(8,128)(2,1)S(1)} %collective-permute-done.18), channel_id=1, source_target_pairs={{4,0},{6,2},{8,4},{10,6},{5,1},{7,3},{9,5},{11,7},{20,16},{22,18},... | collective-permute-start | bytes 589832 | tf_op jit(solution)/shard_map/ppermute | solution.py:220
  112.5 7.7 %collective-permute-start.24 = (f16[2,48,1024]{2,1,0:T(8,128)(2,1)S(1)}, f16[2,48,1024]{2,1,0:T(8,128)(2,1)S(1)}, u32[]{:S(2)}, u32[]{:S(2)}) collective-permute-start(f16[2,48,1024]{2,1,0:T(8,128)(2,1)S(1)} %get-tuple-element.52), channel_id=1, source_target_pairs={{4,0},{6,2},{8,4},{10,6},{12,8},{14,10},{5,1},{7,3},{9,5},{11,7},{... | collective-permute-start | bytes 589832 | tf_op jit(solution)/shard_map/ppermute | solution.py:216
  113.8 7.3 %collective-permute-start.23 = (f16[2,48,1024]{2,1,0:T(8,128)(2,1)S(1)}, f16[2,48,1024]{2,1,0:T(8,128)(2,1)S(1)}, u32[]{:S(2)}, u32[]{:S(2)}) collective-permute-start(f16[2,48,1024]{2,1,0:T(8,128)(2,1)S(1)} %get-tuple-element.51), channel_id=1, source_target_pairs={{0,4},{2,6},{4,8},{6,10},{8,12},{10,14},{1,5},{3,7},{5,9},{7,11},{... | collective-permute-start | bytes 589832 | tf_op jit(solution)/shard_map/ppermute | solution.py:215
  120.2 8.4 %collective-permute-start.34 = (bf16[2,48,1024]{2,1,0:T(8,128)(2,1)S(1)}, bf16[2,48,1024]{2,1,0:T(8,128)(2,1)S(1)}, u32[]{:S(2)}, u32[]{:S(2)}) collective-permute-start(bf16[2,48,1024]{2,1,0:T(8,128)(2,1)S(1)} %collective-permute-done.21), channel_id=1, source_target_pairs={{8,12},{10,14},{9,13},{11,15},{24,28},{26,30},{25,29},{27,31}} | collective-permute-start | bytes 589832 | tf_op jit(solution)/shard_map/ppermute | solution.py:219
  122.2 8.6 %collective-permute-start.26 = (bf16[2,48,1024]{2,1,0:T(8,128)(2,1)S(1)}, bf16[2,48,1024]{2,1,0:T(8,128)(2,1)S(1)}, u32[]{:S(2)}, u32[]{:S(2)}) collective-permute-start(bf16[2,48,1024]{2,1,0:T(8,128)(2,1)S(1)} %pad_maximum_fusion.17), channel_id=1, source_target_pairs={{4,0},{6,2},{8,4},{10,6},{12,8},{14,10},{5,1},{7,3},{9,5},{11,7},{... | collective-permute-start | bytes 589832 | tf_op jit(solution)/shard_map/ppermute | solution.py:220
  124.9 7.3 %collective-permute-start.25 = (bf16[2,48,1024]{2,1,0:T(8,128)(2,1)S(1)}, bf16[2,48,1024]{2,1,0:T(8,128)(2,1)S(1)}, u32[]{:S(2)}, u32[]{:S(2)}) collective-permute-start(bf16[2,48,1024]{2,1,0:T(8,128)(2,1)S(1)} %pad_maximum_fusion.17), channel_id=1, source_target_pairs={{0,4},{2,6},{4,8},{6,10},{8,12},{10,14},{1,5},{3,7},{5,9},{7,11},{... | collective-permute-start | bytes 589832 | tf_op jit(solution)/shard_map/ppermute | solution.py:219
  128.7 40.3 %collective-permute-start.38 = (bf16[4,2,48,1024]{3,2,1,0:T(8,128)(2,1)S(1)}, bf16[4,2,48,1024]{3,2,1,0:T(8,128)(2,1)S(1)}, u32[]{:S(2)}, u32[]{:S(2)}) collective-permute-start(bf16[4,2,48,1024]{3,2,1,0:T(8,128)(2,1)S(1)} %pad_maximum_fusion.10), channel_id=1, source_target_pairs={{0,2},{2,0},{4,6},{6,4},{8,10},{10,8},{12,14},{14,12},{1,3},{3,1},... | collective-permute-start | bytes 2359304 | tf_op jit(solution)/shard_map/ppermute | solution.py:230
  130.9 7.2 %collective-permute-start.30 = (bf16[2,48,1024]{2,1,0:T(8,128)(2,1)S(1)}, bf16[2,48,1024]{2,1,0:T(8,128)(2,1)S(1)}, u32[]{:S(2)}, u32[]{:S(2)}) collective-permute-start(bf16[2,48,1024]{2,1,0:T(8,128)(2,1)S(1)} %collective-permute-done.26), channel_id=1, source_target_pairs={{4,0},{6,2},{8,4},{10,6},{5,1},{7,3},{9,5},{11,7},{20,16},{22,18},... | collective-permute-start | bytes 589832 | tf_op jit(solution)/shard_map/ppermute | solution.py:220
  132.2 9.2 %collective-permute-start.29 = (bf16[2,48,1024]{2,1,0:T(8,128)(2,1)S(1)}, bf16[2,48,1024]{2,1,0:T(8,128)(2,1)S(1)}, u32[]{:S(2)}, u32[]{:S(2)}) collective-permute-start(bf16[2,48,1024]{2,1,0:T(8,128)(2,1)S(1)} %collective-permute-done.25), channel_id=1, source_target_pairs={{4,8},{6,10},{8,12},{10,14},{5,9},{7,11},{9,13},{11,15},{20,24},{2... | collective-permute-start | bytes 589832 | tf_op jit(solution)/shard_map/ppermute | solution.py:219
  133.6 18.9 %collective-permute-start.12 = (f16[2,96,1024]{2,1,0:T(8,128)(2,1)S(1)}, f16[2,96,1024]{2,1,0:T(8,128)(2,1)S(1)}, u32[]{:S(2)}, u32[]{:S(2)}) collective-permute-start(f16[2,96,1024]{2,1,0:T(8,128)(2,1)S(1)} %get-tuple-element.93), channel_id=1, source_target_pairs={{12,8},{14,10},{13,9},{15,11},{28,24},{30,26},{29,25},{31,27}} | collective-permute-start | bytes 1179656 | tf_op jit(solution)/shard_map/ppermute | solution.py:216
  138.1 14.4 %collective-permute-start.11 = (f16[2,96,1024]{2,1,0:T(8,128)(2,1)S(1)}, f16[2,96,1024]{2,1,0:T(8,128)(2,1)S(1)}, u32[]{:S(2)}, u32[]{:S(2)}) collective-permute-start(f16[2,96,1024]{2,1,0:T(8,128)(2,1)S(1)} %get-tuple-element.94), channel_id=1, source_target_pairs={{0,4},{2,6},{1,5},{3,7},{16,20},{18,22},{17,21},{19,23}} | collective-permute-start | bytes 1179656 | tf_op jit(solution)/shard_map/ppermute | solution.py:215
  148.6 20.4 %collective-permute-start.39 = (bf16[4,2,48,1024]{3,2,1,0:T(8,128)(2,1)S(1)}, bf16[4,2,48,1024]{3,2,1,0:T(8,128)(2,1)S(1)}, u32[]{:S(2)}, u32[]{:S(2)}) collective-permute-start(bf16[4,2,48,1024]{3,2,1,0:T(8,128)(2,1)S(1)} %pad_maximum_fusion.11), channel_id=1, source_target_pairs={{0,2},{2,0},{4,6},{6,4},{8,10},{10,8},{12,14},{14,12},{1,3},{3,1},... | collective-permute-start | bytes 2359304 | tf_op jit(solution)/shard_map/ppermute | solution.py:230
  153.5 9.1 %collective-permute-start.27 = (f16[2,96,1024]{2,1,0:T(8,128)(2,1)S(1)}, f16[2,96,1024]{2,1,0:T(8,128)(2,1)S(1)}, u32[]{:S(2)}, u32[]{:S(2)}) collective-permute-start(f16[2,96,1024]{2,1,0:T(8,128)(2,1)S(1)} %get-tuple-element.53), channel_id=1, source_target_pairs={{0,4},{2,6},{4,8},{6,10},{1,5},{3,7},{5,9},{7,11},{16,20},{18,22},... | collective-permute-start | bytes 1179656 | tf_op jit(solution)/shard_map/ppermute | solution.py:215
  162.9 17.6 %collective-permute-start.32 = (f16[2,96,1024]{2,1,0:T(8,128)(2,1)S(1)}, f16[2,96,1024]{2,1,0:T(8,128)(2,1)S(1)}, u32[]{:S(2)}, u32[]{:S(2)}) collective-permute-start(f16[2,96,1024]{2,1,0:T(8,128)(2,1)S(1)} %get-tuple-element.56), channel_id=1, source_target_pairs={{4,0},{6,2},{8,4},{10,6},{12,8},{14,10},{5,1},{7,3},{9,5},{11,7},{... | collective-permute-start | bytes 1179656 | tf_op jit(solution)/shard_map/ppermute | solution.py:216
  164.2 16.3 %collective-permute-start.31 = (f16[2,96,1024]{2,1,0:T(8,128)(2,1)S(1)}, f16[2,96,1024]{2,1,0:T(8,128)(2,1)S(1)}, u32[]{:S(2)}, u32[]{:S(2)}) collective-permute-start(f16[2,96,1024]{2,1,0:T(8,128)(2,1)S(1)} %get-tuple-element.55), channel_id=1, source_target_pairs={{0,4},{2,6},{4,8},{6,10},{8,12},{10,14},{1,5},{3,7},{5,9},{7,11},{... | collective-permute-start | bytes 1179656 | tf_op jit(solution)/shard_map/ppermute | solution.py:215
  176.1 10.4 %collective-permute-start.41 = (f16[2,96,1024]{2,1,0:T(8,128)(2,1)S(1)}, f16[2,96,1024]{2,1,0:T(8,128)(2,1)S(1)}, u32[]{:S(2)}, u32[]{:S(2)}) collective-permute-start(f16[2,96,1024]{2,1,0:T(8,128)(2,1)S(1)} %get-tuple-element.87), channel_id=1, source_target_pairs={{12,8},{14,10},{13,9},{15,11},{28,24},{30,26},{29,25},{31,27}} | collective-permute-start | bytes 1179656 | tf_op jit(solution)/shard_map/ppermute | solution.py:216
  176.8 9.8 %collective-permute-start.40 = (f16[2,96,1024]{2,1,0:T(8,128)(2,1)S(1)}, f16[2,96,1024]{2,1,0:T(8,128)(2,1)S(1)}, u32[]{:S(2)}, u32[]{:S(2)}) collective-permute-start(f16[2,96,1024]{2,1,0:T(8,128)(2,1)S(1)} %get-tuple-element.88), channel_id=1, source_target_pairs={{0,4},{2,6},{1,5},{3,7},{16,20},{18,22},{17,21},{19,23}} | collective-permute-start | bytes 1179656 | tf_op jit(solution)/shard_map/ppermute | solution.py:215
  181.1 9.8 %collective-permute-start.43 = (bf16[2,96,1024]{2,1,0:T(8,128)(2,1)S(1)}, bf16[2,96,1024]{2,1,0:T(8,128)(2,1)S(1)}, u32[]{:S(2)}, u32[]{:S(2)}) collective-permute-start(bf16[2,96,1024]{2,1,0:T(8,128)(2,1)S(1)} %pad_maximum_fusion.13), channel_id=1, source_target_pairs={{4,0},{6,2},{8,4},{10,6},{12,8},{14,10},{5,1},{7,3},{9,5},{11,7},{... | collective-permute-start | bytes 1179656 | tf_op jit(solution)/shard_map/ppermute | solution.py:220
  182.5 13.0 %collective-permute-start.42 = (bf16[2,96,1024]{2,1,0:T(8,128)(2,1)S(1)}, bf16[2,96,1024]{2,1,0:T(8,128)(2,1)S(1)}, u32[]{:S(2)}, u32[]{:S(2)}) collective-permute-start(bf16[2,96,1024]{2,1,0:T(8,128)(2,1)S(1)} %pad_maximum_fusion.13), channel_id=1, source_target_pairs={{0,4},{2,6},{4,8},{6,10},{8,12},{10,14},{1,5},{3,7},{5,9},{7,11},{... | collective-permute-start | bytes 1179656 | tf_op jit(solution)/shard_map/ppermute | solution.py:219
  195.5 16.8 %collective-permute-start.45 = (f16[2,96,1024]{2,1,0:T(8,128)(2,1)S(1)}, f16[2,96,1024]{2,1,0:T(8,128)(2,1)S(1)}, u32[]{:S(2)}, u32[]{:S(2)}) collective-permute-start(f16[2,96,1024]{2,1,0:T(8,128)(2,1)S(1)} %get-tuple-element.64), channel_id=1, source_target_pairs={{8,4},{10,6},{12,8},{14,10},{9,5},{11,7},{13,9},{15,11},{24,20},{2... | collective-permute-start | bytes 1179656 | tf_op jit(solution)/shard_map/ppermute | solution.py:216
  196.2 16.1 %collective-permute-start.44 = (f16[2,96,1024]{2,1,0:T(8,128)(2,1)S(1)}, f16[2,96,1024]{2,1,0:T(8,128)(2,1)S(1)}, u32[]{:S(2)}, u32[]{:S(2)}) collective-permute-start(f16[2,96,1024]{2,1,0:T(8,128)(2,1)S(1)} %get-tuple-element.63), channel_id=1, source_target_pairs={{0,4},{2,6},{4,8},{6,10},{1,5},{3,7},{5,9},{7,11},{16,20},{18,22},... | collective-permute-start | bytes 1179656 | tf_op jit(solution)/shard_map/ppermute | solution.py:215
  200.9 10.1 %collective-permute-start.47 = (bf16[2,96,1024]{2,1,0:T(8,128)(2,1)S(1)}, bf16[2,96,1024]{2,1,0:T(8,128)(2,1)S(1)}, u32[]{:S(2)}, u32[]{:S(2)}) collective-permute-start(bf16[2,96,1024]{2,1,0:T(8,128)(2,1)S(1)} %collective-permute-done.43), channel_id=1, source_target_pairs={{4,0},{6,2},{8,4},{10,6},{5,1},{7,3},{9,5},{11,7},{20,16},{22,18},... | collective-permute-start | bytes 1179656 | tf_op jit(solution)/shard_map/ppermute | solution.py:220
  203.1 9.6 %collective-permute-start.46 = (bf16[2,96,1024]{2,1,0:T(8,128)(2,1)S(1)}, bf16[2,96,1024]{2,1,0:T(8,128)(2,1)S(1)}, u32[]{:S(2)}, u32[]{:S(2)}) collective-permute-start(bf16[2,96,1024]{2,1,0:T(8,128)(2,1)S(1)} %collective-permute-done.42), channel_id=1, source_target_pairs={{4,8},{6,10},{8,12},{10,14},{5,9},{7,11},{9,13},{11,15},{20,24},{2... | collective-permute-start | bytes 1179656 | tf_op jit(solution)/shard_map/ppermute | solution.py:219
  207.5 24.1 %collective-permute-start.50 = (f16[4,2,96,512]{3,2,1,0:T(8,128)(2,1)S(1)}, f16[4,2,96,512]{3,2,1,0:T(8,128)(2,1)S(1)}, u32[]{:S(2)}, u32[]{:S(2)}) collective-permute-start(f16[4,2,96,512]{3,2,1,0:T(8,128)(2,1)S(1)} %convert_element_type.441), channel_id=1, source_target_pairs={{0,2},{2,0},{4,6},{6,4},{8,10},{10,8},{12,14},{14,12},{1,3},{3,1},... | collective-permute-start | bytes 2359304 | tf_op jit(solution)/shard_map/ppermute | solution.py:179
  211.0 13.7 %collective-permute-start.52 = (bf16[2,96,1024]{2,1,0:T(8,128)(2,1)S(1)}, bf16[2,96,1024]{2,1,0:T(8,128)(2,1)S(1)}, u32[]{:S(2)}, u32[]{:S(2)}) collective-permute-start(bf16[2,96,1024]{2,1,0:T(8,128)(2,1)S(1)} %collective-permute-done.47), channel_id=1, source_target_pairs={{4,0},{6,2},{5,1},{7,3},{20,16},{22,18},{21,17},{23,19}} | collective-permute-start | bytes 1179656 | tf_op jit(solution)/shard_map/ppermute | solution.py:220
  212.7 20.5 %collective-permute-start.49 = (f16[2,96,1024]{2,1,0:T(8,128)(2,1)S(1)}, f16[2,96,1024]{2,1,0:T(8,128)(2,1)S(1)}, u32[]{:S(2)}, u32[]{:S(2)}) collective-permute-start(f16[2,96,1024]{2,1,0:T(8,128)(2,1)S(1)} %get-tuple-element.66), channel_id=1, source_target_pairs={{4,0},{6,2},{8,4},{10,6},{12,8},{14,10},{5,1},{7,3},{9,5},{11,7},{... | collective-permute-start | bytes 1179656 | tf_op jit(solution)/shard_map/ppermute | solution.py:216
  214.0 19.2 %collective-permute-start.48 = (f16[2,96,1024]{2,1,0:T(8,128)(2,1)S(1)}, f16[2,96,1024]{2,1,0:T(8,128)(2,1)S(1)}, u32[]{:S(2)}, u32[]{:S(2)}) collective-permute-start(f16[2,96,1024]{2,1,0:T(8,128)(2,1)S(1)} %get-tuple-element.65), channel_id=1, source_target_pairs={{0,4},{2,6},{4,8},{6,10},{8,12},{10,14},{1,5},{3,7},{5,9},{7,11},{... | collective-permute-start | bytes 1179656 | tf_op jit(solution)/shard_map/ppermute | solution.py:215
  225.1 34.0 %collective-permute-start.53 = (bf16[4,2,96,1024]{3,2,1,0:T(8,128)(2,1)S(1)}, bf16[4,2,96,1024]{3,2,1,0:T(8,128)(2,1)S(1)}, u32[]{:S(2)}, u32[]{:S(2)}) collective-permute-start(bf16[4,2,96,1024]{3,2,1,0:T(8,128)(2,1)S(1)} %pad_maximum_fusion.2.own_ref), channel_id=1, source_target_pairs={{0,2},{2,0},{4,6},{6,4},{8,10},{10,8},{12,14},{14,12},{1,3},{3,1},... | collective-permute-start | bytes 4718600 | tf_op jit(solution)/shard_map/ppermute | solution.py:230
  235.0 22.7 %collective-permute-start.57 = (bf16[2,96,1024]{2,1,0:T(8,128)(2,1)S(1)}, bf16[2,96,1024]{2,1,0:T(8,128)(2,1)S(1)}, u32[]{:S(2)}, u32[]{:S(2)}) collective-permute-start(bf16[2,96,1024]{2,1,0:T(8,128)(2,1)S(1)} %pad_maximum_fusion.14), channel_id=1, source_target_pairs={{4,0},{6,2},{8,4},{10,6},{12,8},{14,10},{5,1},{7,3},{9,5},{11,7},{... | collective-permute-start | bytes 1179656 | tf_op jit(solution)/shard_map/ppermute | solution.py:220
  240.1 32.6 %collective-permute-start.60 = (bf16[2,96,1024]{2,1,0:T(8,128)(2,1)S(1)}, bf16[2,96,1024]{2,1,0:T(8,128)(2,1)S(1)}, u32[]{:S(2)}, u32[]{:S(2)}) collective-permute-start(bf16[2,96,1024]{2,1,0:T(8,128)(2,1)S(1)} %collective-permute-done.56), channel_id=1, source_target_pairs={{4,8},{6,10},{8,12},{10,14},{5,9},{7,11},{9,13},{11,15},{20,24},{2... | collective-permute-start | bytes 1179656 | tf_op jit(solution)/shard_map/ppermute | solution.py:219
  257.7 13.6 %collective-permute-start.61 = (bf16[2,96,1024]{2,1,0:T(8,128)(2,1)S(1)}, bf16[2,96,1024]{2,1,0:T(8,128)(2,1)S(1)}, u32[]{:S(2)}, u32[]{:S(2)}) collective-permute-start(bf16[2,96,1024]{2,1,0:T(8,128)(2,1)S(1)} %collective-permute-done.57), channel_id=1, source_target_pairs={{4,0},{6,2},{8,4},{10,6},{5,1},{7,3},{9,5},{11,7},{20,16},{22,18},... | collective-permute-start | bytes 1179656 | tf_op jit(solution)/shard_map/ppermute | solution.py:220
  265.9 7.5 %collective-permute-start.55 = (f16[2,96,512]{2,1,0:T(8,128)(2,1)S(1)}, f16[2,96,512]{2,1,0:T(8,128)(2,1)S(1)}, u32[]{:S(2)}, u32[]{:S(2)}) collective-permute-start(f16[2,96,512]{2,1,0:T(8,128)(2,1)S(1)} %get-tuple-element.107), channel_id=1, source_target_pairs={{12,8},{14,10},{13,9},{15,11},{28,24},{30,26},{29,25},{31,27}} | collective-permute-start | bytes 589832 | tf_op jit(solution)/shard_map/ppermute | solution.py:216
  266.6 8.1 %collective-permute-start.54 = (f16[2,96,512]{2,1,0:T(8,128)(2,1)S(1)}, f16[2,96,512]{2,1,0:T(8,128)(2,1)S(1)}, u32[]{:S(2)}, u32[]{:S(2)}) collective-permute-start(f16[2,96,512]{2,1,0:T(8,128)(2,1)S(1)} %get-tuple-element.108), channel_id=1, source_target_pairs={{0,4},{2,6},{1,5},{3,7},{16,20},{18,22},{17,21},{19,23}} | collective-permute-start | bytes 589832 | tf_op jit(solution)/shard_map/ppermute | solution.py:215
  271.4 17.7 %collective-permute-start.73 = (bf16[2,96,1024]{2,1,0:T(8,128)(2,1)S(1)}, bf16[2,96,1024]{2,1,0:T(8,128)(2,1)S(1)}, u32[]{:S(2)}, u32[]{:S(2)}) collective-permute-start(bf16[2,96,1024]{2,1,0:T(8,128)(2,1)S(1)} %collective-permute-done.61), channel_id=1, source_target_pairs={{4,0},{6,2},{5,1},{7,3},{20,16},{22,18},{21,17},{23,19}} | collective-permute-start | bytes 1179656 | tf_op jit(solution)/shard_map/ppermute | solution.py:220
  272.7 26.7 %collective-permute-start.72 = (bf16[2,96,1024]{2,1,0:T(8,128)(2,1)S(1)}, bf16[2,96,1024]{2,1,0:T(8,128)(2,1)S(1)}, u32[]{:S(2)}, u32[]{:S(2)}) collective-permute-start(bf16[2,96,1024]{2,1,0:T(8,128)(2,1)S(1)} %collective-permute-done.60), channel_id=1, source_target_pairs={{8,12},{10,14},{9,13},{11,15},{24,28},{26,30},{25,29},{27,31}} | collective-permute-start | bytes 1179656 | tf_op jit(solution)/shard_map/ppermute | solution.py:219
  275.5 7.3 %collective-permute-start.58 = (f16[2,96,512]{2,1,0:T(8,128)(2,1)S(1)}, f16[2,96,512]{2,1,0:T(8,128)(2,1)S(1)}, u32[]{:S(2)}, u32[]{:S(2)}) collective-permute-start(f16[2,96,512]{2,1,0:T(8,128)(2,1)S(1)} %get-tuple-element.73), channel_id=1, source_target_pairs={{0,4},{2,6},{4,8},{6,10},{1,5},{3,7},{5,9},{7,11},{16,20},{18,22},... | collective-permute-start | bytes 589832 | tf_op jit(solution)/shard_map/ppermute | solution.py:215
  284.3 7.3 %collective-permute-start.62 = (f16[2,96,512]{2,1,0:T(8,128)(2,1)S(1)}, f16[2,96,512]{2,1,0:T(8,128)(2,1)S(1)}, u32[]{:S(2)}, u32[]{:S(2)}) collective-permute-start(f16[2,96,512]{2,1,0:T(8,128)(2,1)S(1)} %get-tuple-element.75), channel_id=1, source_target_pairs={{0,4},{2,6},{4,8},{6,10},{8,12},{10,14},{1,5},{3,7},{5,9},{7,11},{... | collective-permute-start | bytes 589832 | tf_op jit(solution)/shard_map/ppermute | solution.py:215
  291.9 12.0 %collective-permute-start.65 = (bf16[2,96,512]{2,1,0:T(8,128)(2,1)S(1)}, bf16[2,96,512]{2,1,0:T(8,128)(2,1)S(1)}, u32[]{:S(2)}, u32[]{:S(2)}) collective-permute-start(bf16[2,96,512]{2,1,0:T(8,128)(2,1)S(1)} %pad_maximum_fusion.20), channel_id=1, source_target_pairs={{4,0},{6,2},{8,4},{10,6},{12,8},{14,10},{5,1},{7,3},{9,5},{11,7},{... | collective-permute-start | bytes 589832 | tf_op jit(solution)/shard_map/ppermute | solution.py:220
  293.2 11.9 %collective-permute-start.66 = (bf16[2,96,512]{2,1,0:T(8,128)(2,1)S(1)}, bf16[2,96,512]{2,1,0:T(8,128)(2,1)S(1)}, u32[]{:S(2)}, u32[]{:S(2)}) collective-permute-start(bf16[2,96,512]{2,1,0:T(8,128)(2,1)S(1)} %pad_maximum_fusion.20), channel_id=1, source_target_pairs={{0,4},{2,6},{4,8},{6,10},{8,12},{10,14},{1,5},{3,7},{5,9},{7,11},{... | collective-permute-start | bytes 589832 | tf_op jit(solution)/shard_map/ppermute | solution.py:219
  298.0 7.8 %collective-permute-start.64 = (bf16[48,3584]{1,0:T(8,128)(2,1)S(1)}, bf16[48,3584]{1,0:T(8,128)(2,1)S(1)}, u32[]{:S(2)}, u32[]{:S(2)}) collective-permute-start(bf16[48,3584]{1,0:T(8,128)(2,1)S(1)} %pad_maximum_fusion.15), channel_id=1, source_target_pairs={{0,1},{1,0},{2,3},{3,2},{4,5},{5,4},{6,7},{7,6},{8,9},{9,8},{10,11... | collective-permute-start | bytes 1032200 | tf_op jit(solution)/shard_map/ppermute | solution.py:243
  299.6 23.9 %collective-permute-start.74 = (bf16[4,2,96,1024]{3,2,1,0:T(8,128)(2,1)S(1)}, bf16[4,2,96,1024]{3,2,1,0:T(8,128)(2,1)S(1)}, u32[]{:S(2)}, u32[]{:S(2)}) collective-permute-start(bf16[4,2,96,1024]{3,2,1,0:T(8,128)(2,1)S(1)} %pad_maximum_fusion.3.own_ref), channel_id=1, source_target_pairs={{0,2},{2,0},{4,6},{6,4},{8,10},{10,8},{12,14},{14,12},{1,3},{3,1},... | collective-permute-start | bytes 4718600 | tf_op jit(solution)/shard_map/ppermute | solution.py:230
  303.8 9.3 %collective-permute-start.69 = (bf16[2,96,512]{2,1,0:T(8,128)(2,1)S(1)}, bf16[2,96,512]{2,1,0:T(8,128)(2,1)S(1)}, u32[]{:S(2)}, u32[]{:S(2)}) collective-permute-start(bf16[2,96,512]{2,1,0:T(8,128)(2,1)S(1)} %collective-permute-done.65), channel_id=1, source_target_pairs={{4,0},{6,2},{8,4},{10,6},{5,1},{7,3},{9,5},{11,7},{20,16},{22,18},... | collective-permute-start | bytes 589832 | tf_op jit(solution)/shard_map/ppermute | solution.py:220
  305.1 9.3 %collective-permute-start.67 = (bf16[2,96,512]{2,1,0:T(8,128)(2,1)S(1)}, bf16[2,96,512]{2,1,0:T(8,128)(2,1)S(1)}, u32[]{:S(2)}, u32[]{:S(2)}) collective-permute-start(bf16[2,96,512]{2,1,0:T(8,128)(2,1)S(1)} %collective-permute-done.66), channel_id=1, source_target_pairs={{4,8},{6,10},{8,12},{10,14},{5,9},{7,11},{9,13},{11,15},{20,24},{2... | collective-permute-start | bytes 589832 | tf_op jit(solution)/shard_map/ppermute | solution.py:219
  313.2 7.7 %collective-permute-start.70 = (bf16[2,96,512]{2,1,0:T(8,128)(2,1)S(1)}, bf16[2,96,512]{2,1,0:T(8,128)(2,1)S(1)}, u32[]{:S(2)}, u32[]{:S(2)}) collective-permute-start(bf16[2,96,512]{2,1,0:T(8,128)(2,1)S(1)} %collective-permute-done.69), channel_id=1, source_target_pairs={{4,0},{6,2},{5,1},{7,3},{20,16},{22,18},{21,17},{23,19}} | collective-permute-start | bytes 589832 | tf_op jit(solution)/shard_map/ppermute | solution.py:220
  321.1 9.3 %collective-permute-start.71 = (bf16[4,2,96,512]{3,2,1,0:T(8,128)(2,1)S(1)}, bf16[4,2,96,512]{3,2,1,0:T(8,128)(2,1)S(1)}, u32[]{:S(2)}, u32[]{:S(2)}) collective-permute-start(bf16[4,2,96,512]{3,2,1,0:T(8,128)(2,1)S(1)} %pad_maximum_fusion.12.own_ref), channel_id=1, source_target_pairs={{0,2},{2,0},{4,6},{6,4},{8,10},{10,8},{12,14},{14,12},{1,3},{3,1},... | collective-permute-start | bytes 2359304 | tf_op jit(solution)/shard_map/ppermute | solution.py:230
  (21 other events, 148.0 us)

commit v3 on v2

--- a/solution.py
+++ b/solution.py
@@ -57,15 +57,10 @@
     blocks, _, rows, width = own_ref.shape
     half = blocks * rows
     for which, out_ref in enumerate((gate_ref, up_ref)):
-        out_ref[...] = jnp.dot(
-            features_ref[:, :half],
-            own_ref[:, which].reshape(half, width),
-            preferred_element_type=jnp.float32,
-        ) + jnp.dot(
-            features_ref[:, half:],
-            other_ref[:, which].reshape(half, width),
-            preferred_element_type=jnp.float32,
+        act = jnp.concatenate(
+            [own_ref[:, which].reshape(half, width), other_ref[:, which].reshape(half, width)]
         )
+        out_ref[...] = jnp.dot(features_ref[...], act, preferred_element_type=jnp.float32)
 
 
 def gradient(features, own, other, totals, columns, start, tile):
@@ -117,11 +112,13 @@
     swap = [(0, 1), (1, 0)]
     pairs = [(i, i ^ 1) for i in range(n_col)]
 
-    def ahead(first, last):
-        return [(2 * i + c, 2 * i + 2 + c) for i in range(first, last + 1) for c in (0, 1)]
-
-    def back(first, last):
-        return [(2 * i + c, 2 * i - 2 + c) for i in range(first, last + 1) for c in (0, 1)]
+    def between(hops):
+        return [(2 * i + c, 2 * j + c) for i, j in hops for c in (0, 1)]
+
+    inward, outward = between([(0, 1), (3, 2)]), between([(1, 0), (2, 3)])
+    side, centre = inward + outward, between([(1, 2), (2, 1)])
+    at_end = (place == 0) | (place == line - 1)
+    at_far = 2 * place >= line
 
     mine_wide = tokens[0]
     if n_row == 2:
@@ -143,19 +140,10 @@
 
     def arrange(values):
         values = values.reshape(line, 2, slab, depth)
-        values = lax.dynamic_slice_in_dim(jnp.concatenate([values, values]), place, line, 0)
+        values = jnp.where(at_far, values[::-1], values)
         mine = lax.dynamic_index_in_dim(values, core, 1, keepdims=False)
         theirs = lax.dynamic_index_in_dim(values, 1 - core, 1, keepdims=False)
         return jnp.stack([mine, theirs])
-
-    single = [arrange(values) for values in features]
-    double = jnp.stack(single, axis=2).reshape(-1, depth)
-    picked = {
-        (0,): single[0].reshape(-1, depth),
-        (1,): single[1].reshape(-1, depth),
-        (0, 1): double,
-    }
-    turned = double.T
 
     cotangent = grad_hidden[0]
     mine = lax.dynamic_slice_in_dim(cotangent, part * half, half, 1)
@@ -173,9 +161,11 @@
     def multiply(k, after):
         batches, start, width = pieces[k]
         rows = tie(picked[batches], after)
-        other, own = forward(
+        return forward(
             first_tile, rows, gate_weight, up_weight, start, width, tile, line, scale
         )
+
+    def pair_sum(other, own):
         got = lax.ppermute(other.astype(WIRE), "col", pairs)
         return (own + wide(got)).astype(WIRE)
 
@@ -193,51 +183,73 @@
             hiddens[batch].append(hidden[position])
         return act.reshape(2, len(batches) * slab, width)
 
+    def add(*terms):
+        return functools.reduce(jnp.add, map(wide, terms))
+
+    def send(value, route):
+        return lax.ppermute(value, "col", route)
+
     hiddens, totals, waiting = ([], []), (), []
     last = len(pieces) - 1
-    both = {0: multiply(0, ())}
-    both[1] = multiply(1, ())
-    act = None
+    near_rows = arrange(features[0])
+    picked = {(0,): near_rows.reshape(-1, depth)}
+    first = multiply(0, ())
+    arranged = arrange(tie(features[1], first))
+    double = jnp.stack([near_rows, arranged], axis=2).reshape(-1, depth)
+    picked[(1,)] = arranged.reshape(-1, depth)
+    picked[(0, 1)] = double
+    turned = double.T
+    sums = pair_sum(*first)
+    act = gathered = None
     for k in range(-1, last + 1):
-        right = left = None
-        from_left, from_right = [act], [act]
-        for step in range(1, line):
-            if k < last:
-                o = line - step
-                to_right, to_left = both[k + 1][o], both[k + 1][line - o]
-                if right is not None:
-                    to_right = (wide(to_right) + wide(right)).astype(WIRE)
-                    to_left = (wide(to_left) + wide(left)).astype(WIRE)
-                if step > 1 and act is not None:
-                    to_right, to_left = tie(
-                        (to_right, to_left), from_left[step - 1], from_right[step - 1]
-                    )
-                right = lax.ppermute(to_right, "col", ahead(0, step - 1))
-                left = lax.ppermute(to_left, "col", back(o, line - 1))
-            if act is not None:
-                to_right, to_left = from_left[-1], from_right[-1]
-                from_left.append(lax.ppermute(to_right, "col", ahead(step - 1, line - 2)))
-                from_right.append(lax.ppermute(to_left, "col", back(1, line - step)))
-            if step == 1 and k + 3 <= last:
-                both[k + 3] = multiply(k + 3, both[k + 1])
-        if k < last:
-            ready = activate(k + 1, wide(both[k + 1][0]) + wide(right) + wide(left))
-        if act is not None:
-            blocks = [act]
-            for o in range(1, line):
-                blocks.append(jnp.where(place + o < line, from_right[o], from_left[line - o]))
-            gathered = jnp.stack(blocks)
-            gathered = (gathered, lax.ppermute(gathered, "col", pairs))
-            waiting.append(gathered)
-            batches, start, width = pieces[k]
+        adding, sharing = k < last, act is not None
+        if adding:
+            in_1 = send(sums[3], inward)
+        if sharing:
+            side_1, centre_1 = send(act, side), send(act, centre)
+        if gathered is not None:
+            waiting.append((gathered, send(gathered, pairs)))
+            batches, start, width = pieces[k - 1]
             if batches != (0,):
-                if batches == (1,):
-                    gathered = [jnp.concatenate(both_batches, axis=2) for both_batches in zip(*waiting)]
+                if len(waiting) > 1:
+                    merged = [jnp.concatenate(both, axis=2) for both in zip(*waiting)]
+                else:
+                    merged = waiting[0]
                 waiting = []
-                totals = gradient(turned, *gathered, totals, half, start, tile)
-                if k < last - 1:
-                    both[k + 2] = tie(both[k + 2], *totals)
-        act = ready
+                totals = gradient(turned, *merged, totals, half, start, tile)
+                if adding:
+                    sums = tie(sums, totals)
+        if adding:
+            far = add(sums[3], in_1).astype(WIRE)
+            centre_2 = send(far, centre)
+            in_2 = send(tie(sums[2], in_1), inward)
+        if sharing:
+            out_2, share_2 = send(centre_1, outward), send(side_1, centre)
+        if adding:
+            if k + 2 <= last:
+                following = multiply(k + 2, (in_1,))
+                sums = tie(sums, following)
+            near = add(sums[2], in_2).astype(WIRE)
+            swapped = jnp.where(at_end, wide(sums[1]), add(sums[0], centre_2)).astype(WIRE)
+            side_3 = send(swapped, side)
+            centre_3 = send(near, centre)
+        if sharing:
+            out_3 = send(share_2, outward)
+            gathered = jnp.stack(
+                [
+                    jnp.where(at_end, act, side_1),
+                    jnp.where(at_end, side_1, act),
+                    jnp.where(at_end, out_2, centre_1),
+                    jnp.where(at_end, out_3, share_2),
+                ]
+            )
+        if adding:
+            own = jnp.where(at_end, wide(sums[0]), wide(sums[1]))
+            act = activate(k + 1, own + wide(side_3) + wide(centre_3))
+            if k + 2 <= last:
+                sums = pair_sum(*following)
+    batches, start, width = pieces[last]
+    totals = gradient(turned, gathered, send(gathered, pairs), totals, half, start, tile)
 
     own, other = (jnp.concatenate(parts, axis=1) for parts in hiddens)
     other = lax.ppermute(other, "depth", swap)
@@ -247,6 +259,40 @@
         jnp.concatenate([other, own], axis=1),
     )
     return (hidden[None], *totals)
+
+
+def contract(picked, piece):
+    return lax.dot_general(
+        picked, piece, (((0,), (0,)), ((), ())), preferred_element_type=jnp.float32
+    )
+
+
+def local_any(tokens, gate_weight, up_weight, grad_hidden):
+    features = lax.all_gather(tokens[0], "row", axis=1, tiled=True)
+    columns = gate_weight.shape[1]
+    picked = features
+    gate_part = jnp.dot(picked, gate_weight, preferred_element_type=jnp.float32)
+    up_part = jnp.dot(picked, up_weight, preferred_element_type=jnp.float32)
+    summed = lax.psum_scatter(
+        jnp.concatenate([gate_part, up_part], axis=1), "col", scatter_dimension=0, tiled=True
+    )
+    gate_sum = summed[:, :columns]
+    up_sum = summed[:, columns:]
+    squash = jax.nn.sigmoid(gate_sum)
+    hidden = (gate_sum * squash * up_sum).astype(jnp.bfloat16)
+    cotangent = grad_hidden[0].astype(jnp.float32)
+    gate_act = (cotangent * up_sum * squash * (1.0 + gate_sum * (1.0 - squash))).astype(
+        jnp.bfloat16
+    )
+    up_act = (cotangent * gate_sum * squash).astype(jnp.bfloat16)
+    picked = features
+    gate_total = contract(picked, lax.all_gather(gate_act, "col", axis=0, tiled=True))
+    up_total = contract(picked, lax.all_gather(up_act, "col", axis=0, tiled=True))
+    grad_gate, grad_up = (
+        lax.psum_scatter(gate_total, "depth", scatter_dimension=1, tiled=True),
+        lax.psum_scatter(up_total, "depth", scatter_dimension=1, tiled=True),
+    )
+    return (hidden[None], grad_gate, grad_up)
 
 
 SHARES = (4, 4, 4, 2)
@@ -262,7 +308,7 @@
     )
     out_specs = (P("depth", "col", "row"), P("col", ("row", "depth")), P("col", ("row", "depth")))
     return jax.shard_map(
-        functools.partial(local, sizes),
+        functools.partial(local, sizes) if sizes == (2, 8, 2) else local_any,
         mesh=mesh,
         in_specs=in_specs,
         out_specs=out_specs,

time: 336 us -> 299 us (0.89)
  waiting for transfers between devices: 100 us -> 66.2 us
    ppermute x70 -> x60, waiting for transfers between devices: 86.6 us -> 50.5 us  [the longest x55 50.5 us: send(): return lax.ppermute(value, 'col', route)]
    ppermute x70 -> x60, starting transfers between devices: 152 us -> 153 us  [the longest x55 136 us: send(): return lax.ppermute(value, 'col', route)]
  transfers between devices with their start and end apart: 75 -> 65, of which waited for: 25 -> 16; matrix products, arithmetic and copies ran while one was open for 7% -> 8% of each run, Pallas kernels for 14% -> 15%
where the time goes in v3:
time: 299 us; the launch traced here: 297 us
  starting transfers between devices  156 us (52%)
  waiting for transfers between devices  66.2 us (22%)
  Pallas kernels  47.1 us (16%)
  other arithmetic  21.9 us (7%)
  local copies, waits for them, and re-layouts  3.66 us (1%)
    ppermute x55, starting transfers between devices, send(): return lax.ppermute(value, 'col', route)  136 us
    ppermute x55, waiting for transfers between devices, send(): return lax.ppermute(value, 'col', route)  50.5 us
    pallas_call x5, Pallas kernels, forward(): pl.pallas_call(functools.partial(forward_kernel, scale), out_shape=(out_s...  26 us
    pallas_call x4, Pallas kernels, gradient(): pl.pallas_call(gradient_kernel, out_shape=(out_shape, out_shape), grid=(w...  21.1 us
    ppermute x5, starting transfers between devices, pair_sum(): got = lax.ppermute(other.astype(WIRE), 'col', pairs)  16.1 us
    ppermute x1, waiting for transfers between devices, local(): over_both = lax.ppermute(over_row, 'depth', swap)  9.11 us
    ppermute x1, waiting for transfers between devices, local(): over_row = lax.ppermute(mine_wide, 'row', swap)  6.56 us
  transfers between devices with their start and end apart: 65, of which 16 were waited for; matrix products, arithmetic and copies ran while one was open for 8% of the time, Pallas kernels for 15%

profile of v3, /device:TPU:1, one launch (start us, length us, event | category | flops | bytes accessed | tf_op | source)
XLA Modules:
  0.0 297.3 jit_solution(7748769554688100402)
XLA Ops:
  0.6 2.1 collective-permute-start.2
  2.8 1.2 collective-permute-start
  4.0 1.9 dynamic-slice_bitcast_fusion.5
  6.1 6.6 %collective-permute-done = bf16[384,512]{1,0:T(8,128)(2,1)S(1)} collective-permute-done((bf16[384,512]{1,0:T(8,128)(2,1)}, bf16[384,512]{1,0:T(8,128)(2,1)S(1)}, u32[]{:S(2)}, u32[]{:S(2)}) %collective-permute-start) | collective-permute-done | bytes 393248 | tf_op jit(solution)/shard_map/ppermute | solution.py:125
  13.3 4.4 %shard_map.67 = (f32[4,2,48,1024]{3,2,1,0:T(8,128)S(1)}, f32[4,2,48,1024]{3,2,1,0:T(8,128)S(1)}) custom-call(s32[1]{0:T(128)} %bitcast.place_ref, bf16[384,1024]{1,0:T(8,128)(2,1)S(1)} %bitcast.214, bf16[1024,7168]{1,0:T(8,128)(2,1)} %gate_ref.9, bf16[1024,7168]{1,0:T(8,128)(2,1)} %up_ref.9), custom_call_target="tpu_custom_call" | custom-call | flops 1610612736 | bytes 8126464 | tf_op jit(solution)/shard_map/pallas_call | solution.py:33
  17.9 1.9 collective-permute-start.1
  21.4 9.1 %collective-permute-done.3 = bf16[384,512]{1,0:T(8,128)(2,1)S(1)} collective-permute-done((bf16[384,512]{1,0:T(8,128)(2,1)S(1)}, bf16[384,512]{1,0:T(8,128)(2,1)S(1)}, u32[]{:S(2)}, u32[]{:S(2)}) %collective-permute-start.3) | collective-permute-done | bytes 393248 | tf_op jit(solution)/shard_map/ppermute | solution.py:127
  31.1 3.2 %collective-permute-start.4 = (f16[2,48,1024]{2,1,0:T(8,128)(2,1)S(1)}, f16[2,48,1024]{2,1,0:T(8,128)(2,1)S(1)}, u32[]{:S(2)}, u32[]{:S(2)}) collective-permute-start(f16[2,48,1024]{2,1,0:T(8,128)(2,1)S(1)} %get-tuple-element.94), channel_id=1, source_target_pairs={{0,4},{2,6},{12,8},{14,10},{1,5},{3,7},{13,9},{15,11},{16,20},{18,... | collective-permute-start | bytes 589832 | tf_op jit(solution)/shard_map/ppermute | solution.py:190
  34.6 3.0 %collective-permute-done.4 = f16[2,48,1024]{2,1,0:T(8,128)(2,1)S(1)} collective-permute-done((f16[2,48,1024]{2,1,0:T(8,128)(2,1)S(1)}, f16[2,48,1024]{2,1,0:T(8,128)(2,1)S(1)}, u32[]{:S(2)}, u32[]{:S(2)}) %collective-permute-start.4) | collective-permute-done | bytes 196640 | tf_op jit(solution)/shard_map/ppermute | solution.py:190
  38.4 6.6 %collective-permute-start.7 = (f16[2,48,1024]{2,1,0:T(8,128)(2,1)S(1)}, f16[2,48,1024]{2,1,0:T(8,128)(2,1)S(1)}, u32[]{:S(2)}, u32[]{:S(2)}) collective-permute-start(f16[2,48,1024]{2,1,0:T(8,128)(2,1)S(1)} %get-tuple-element.44), channel_id=1, source_target_pairs={{0,4},{2,6},{12,8},{14,10},{1,5},{3,7},{13,9},{15,11},{16,20},{18,... | collective-permute-start | bytes 589832 | tf_op jit(solution)/shard_map/ppermute | solution.py:190
  45.2 4.5 %shard_map.68 = (f32[4,2,48,1024]{3,2,1,0:T(8,128)S(1)}, f32[4,2,48,1024]{3,2,1,0:T(8,128)S(1)}) custom-call(s32[1]{0:T(128)} %bitcast.place_ref, bf16[384,1024]{1,0:T(8,128)(2,1)S(1)} %bitcast.215, bf16[1024,7168]{1,0:T(8,128)(2,1)} %gate_ref.9, bf16[1024,7168]{1,0:T(8,128)(2,1)} %up_ref.9), custom_call_target="tpu_custom_call" | custom-call | flops 1610612736 | bytes 8126464 | tf_op jit(solution)/shard_map/pallas_call | solution.py:33
  51.7 3.3 %collective-permute-start.9 = (f16[4,2,48,1024]{3,2,1,0:T(8,128)(2,1)}, f16[4,2,48,1024]{3,2,1,0:T(8,128)(2,1)}, u32[]{:S(2)}, u32[]{:S(2)}) collective-permute-start(f16[4,2,48,1024]{3,2,1,0:T(8,128)(2,1)} %convert_element_type.339), channel_id=1, source_target_pairs={{0,2},{2,0},{4,6},{6,4},{8,10},{10,8},{12,14},{14,12},{1,3},{3,1},... | collective-permute-start | bytes 2359304 | tf_op jit(solution)/shard_map/ppermute | solution.py:169
  56.0 1.3 collective-permute-start.19
  57.4 4.3 %collective-permute-start.18 = (bf16[2,48,1024]{2,1,0:T(8,128)(2,1)}, bf16[2,48,1024]{2,1,0:T(8,128)(2,1)}, u32[]{:S(2)}, u32[]{:S(2)}) collective-permute-start(bf16[2,48,1024]{2,1,0:T(8,128)(2,1)} %pad_maximum_fusion.14), channel_id=1, source_target_pairs={{0,4},{2,6},{12,8},{14,10},{4,0},{6,2},{8,12},{10,14},{1,5},{3,7},... | collective-permute-start | bytes 589832 | tf_op jit(solution)/shard_map/ppermute | solution.py:190
  63.4 1.4 collective-permute-start.20
  65.7 1.9 add_convert_fusion.3
  67.7 5.9 %collective-permute-start.10 = (f16[2,48,1024]{2,1,0:T(8,128)(2,1)S(1)}, f16[2,48,1024]{2,1,0:T(8,128)(2,1)S(1)}, u32[]{:S(2)}, u32[]{:S(2)}) collective-permute-start(f16[2,48,1024]{2,1,0:T(8,128)(2,1)S(1)} %get-tuple-element.98), channel_id=1, source_target_pairs={{0,4},{2,6},{12,8},{14,10},{1,5},{3,7},{13,9},{15,11},{16,20},{18,... | collective-permute-start | bytes 589832 | tf_op jit(solution)/shard_map/ppermute | solution.py:190
  74.6 1.3 collective-permute-start.22
  77.0 6.1 %collective-permute-start.26 = (f16[2,48,1024]{2,1,0:T(8,128)(2,1)S(1)}, f16[2,48,1024]{2,1,0:T(8,128)(2,1)S(1)}, u32[]{:S(2)}, u32[]{:S(2)}) collective-permute-start(f16[2,48,1024]{2,1,0:T(8,128)(2,1)S(1)} %get-tuple-element.54), channel_id=1, source_target_pairs={{0,4},{2,6},{12,8},{14,10},{1,5},{3,7},{13,9},{15,11},{16,20},{18,... | collective-permute-start | bytes 589832 | tf_op jit(solution)/shard_map/ppermute | solution.py:190
  83.1 6.8 %shard_map.69 = (f32[4,2,96,1024]{3,2,1,0:T(8,128)S(1)}, f32[4,2,96,1024]{3,2,1,0:T(8,128)}) custom-call(s32[1]{0:T(128)} %bitcast.place_ref, bf16[768,1024]{1,0:T(8,128)(2,1)S(1)} %bitcast.207, bf16[1024,7168]{1,0:T(8,128)(2,1)} %gate_ref.9, bf16[1024,7168]{1,0:T(8,128)(2,1)} %up_ref.9), custom_call_target="tpu_custom_call" | custom-call | flops 3221225472 | bytes 12058624 | tf_op jit(solution)/shard_map/pallas_call | solution.py:33
  90.3 6.4 %collective-permute-start.11 = (f16[4,2,96,1024]{3,2,1,0:T(8,128)(2,1)S(1)}, f16[4,2,96,1024]{3,2,1,0:T(8,128)(2,1)S(1)}, u32[]{:S(2)}, u32[]{:S(2)}) collective-permute-start(f16[4,2,96,1024]{3,2,1,0:T(8,128)(2,1)S(1)} %convert_element_type.342), channel_id=1, source_target_pairs={{0,2},{2,0},{4,6},{6,4},{8,10},{10,8},{12,14},{14,12},{1,3},{3,1},... | collective-permute-start | bytes 4718600 | tf_op jit(solution)/shard_map/ppermute | solution.py:169
  97.6 5.8 %collective-permute-done.25 = f16[2,48,1024]{2,1,0:T(8,128)(2,1)S(1)} collective-permute-done((f16[2,48,1024]{2,1,0:T(8,128)(2,1)S(1)}, f16[2,48,1024]{2,1,0:T(8,128)(2,1)S(1)}, u32[]{:S(2)}, u32[]{:S(2)}) %collective-permute-start.25) | collective-permute-done | bytes 196640 | tf_op jit(solution)/shard_map/ppermute | solution.py:190
  105.4 5.0 %collective-permute-start.28 = (bf16[2,48,1024]{2,1,0:T(8,128)(2,1)S(1)}, bf16[2,48,1024]{2,1,0:T(8,128)(2,1)S(1)}, u32[]{:S(2)}, u32[]{:S(2)}) collective-permute-start(bf16[2,48,1024]{2,1,0:T(8,128)(2,1)S(1)} %pad_maximum_fusion.15), channel_id=1, source_target_pairs={{0,4},{2,6},{12,8},{14,10},{4,0},{6,2},{8,12},{10,14},{1,5},{3,7},... | collective-permute-start | bytes 589832 | tf_op jit(solution)/shard_map/ppermute | solution.py:190
  111.4 1.7 collective-permute-start.33
  113.1 1.3 collective-permute-start.30
  115.1 1.3 collective-permute-start.32
  117.2 9.7 %collective-permute-start.12 = (f16[2,96,1024]{2,1,0:T(8,128)(2,1)S(1)}, f16[2,96,1024]{2,1,0:T(8,128)(2,1)S(1)}, u32[]{:S(2)}, u32[]{:S(2)}) collective-permute-start(f16[2,96,1024]{2,1,0:T(8,128)(2,1)S(1)} %get-tuple-element.78), channel_id=1, source_target_pairs={{0,4},{2,6},{12,8},{14,10},{1,5},{3,7},{13,9},{15,11},{16,20},{18,... | collective-permute-start | bytes 1179656 | tf_op jit(solution)/shard_map/ppermute | solution.py:190
  127.2 5.0 %collective-permute-done.12 = f16[2,96,1024]{2,1,0:T(8,128)(2,1)S(1)} collective-permute-done((f16[2,96,1024]{2,1,0:T(8,128)(2,1)S(1)}, f16[2,96,1024]{2,1,0:T(8,128)(2,1)S(1)}, u32[]{:S(2)}, u32[]{:S(2)}) %collective-permute-start.12) | collective-permute-done | bytes 393248 | tf_op jit(solution)/shard_map/ppermute | solution.py:190
  133.0 8.1 %collective-permute-start.15 = (f16[2,96,1024]{2,1,0:T(8,128)(2,1)S(1)}, f16[2,96,1024]{2,1,0:T(8,128)(2,1)}, u32[]{:S(2)}, u32[]{:S(2)}) collective-permute-start(f16[2,96,1024]{2,1,0:T(8,128)(2,1)S(1)} %get-tuple-element.52), channel_id=1, source_target_pairs={{0,4},{2,6},{12,8},{14,10},{1,5},{3,7},{13,9},{15,11},{16,20},{18,... | collective-permute-start | bytes 1179656 | tf_op jit(solution)/shard_map/ppermute | solution.py:190
  141.2 3.9 %collective-permute-start.34 = (bf16[4,2,48,1024]{3,2,1,0:T(8,128)(2,1)S(1)}, bf16[4,2,48,1024]{3,2,1,0:T(8,128)(2,1)S(1)}, u32[]{:S(2)}, u32[]{:S(2)}) collective-permute-start(bf16[4,2,48,1024]{3,2,1,0:T(8,128)(2,1)S(1)} %pad_maximum_fusion.9), channel_id=1, source_target_pairs={{0,2},{2,0},{4,6},{6,4},{8,10},{10,8},{12,14},{14,12},{1,3},{3,1},... | collective-permute-start | bytes 2359304 | tf_op jit(solution)/shard_map/ppermute | solution.py:190
  145.2 6.8 %shard_map.70 = (f32[4,2,96,1024]{3,2,1,0:T(8,128)S(1)}, f32[4,2,96,1024]{3,2,1,0:T(8,128)}) custom-call(s32[1]{0:T(128)} %bitcast.place_ref, bf16[768,1024]{1,0:T(8,128)(2,1)S(1)} %bitcast.208, bf16[1024,7168]{1,0:T(8,128)(2,1)} %gate_ref.9, bf16[1024,7168]{1,0:T(8,128)(2,1)} %up_ref.9), custom_call_target="tpu_custom_call" | custom-call | flops 3221225472 | bytes 12058624 | tf_op jit(solution)/shard_map/pallas_call | solution.py:33
  152.4 1.5 fusion
  155.1 1.3 pad_maximum_fusion.1.other_ref
  156.4 7.8 %collective-permute-done.14 = f16[2,96,1024]{2,1,0:T(8,128)(2,1)S(1)} collective-permute-done((f16[2,96,1024]{2,1,0:T(8,128)(2,1)S(1)}, f16[2,96,1024]{2,1,0:T(8,128)(2,1)S(1)}, u32[]{:S(2)}, u32[]{:S(2)}) %collective-permute-start.14) | collective-permute-done | bytes 393248 | tf_op jit(solution)/shard_map/ppermute | solution.py:190
  165.5 4.4 %collective-permute-start.41 = (bf16[2,96,1024]{2,1,0:T(8,128)(2,1)S(1)}, bf16[2,96,1024]{2,1,0:T(8,128)(2,1)S(1)}, u32[]{:S(2)}, u32[]{:S(2)}) collective-permute-start(bf16[2,96,1024]{2,1,0:T(8,128)(2,1)S(1)} %pad_maximum_fusion.11), channel_id=1, source_target_pairs={{0,4},{2,6},{12,8},{14,10},{4,0},{6,2},{8,12},{10,14},{1,5},{3,7},... | collective-permute-start | bytes 1179656 | tf_op jit(solution)/shard_map/ppermute | solution.py:190
  170.0 5.9 %shard_map.71 = (f32[1024,3584]{1,0:T(8,128)}, f32[1024,3584]{1,0:T(8,128)}) custom-call(bf16[1024,768]{1,0:T(8,128)(2,1)S(1)} %bitcast.210, bf16[4,2,96,1024]{3,2,1,0:T(8,128)(2,1)S(1)} %maximum_maximum_fusion.own_ref, bf16[4,2,96,1024]{3,2,1,0:T(8,128)(2,1)S(1)} %pad_maximum_fusion.1.other_ref), custom_call_target="tpu_custom_call" | custom-call | flops 3221225472 | bytes 13107200 | tf_op jit(solution)/shard_map/pallas_call | solution.py:74
  176.6 1.3 collective-permute-start.43
  179.3 6.6 %collective-permute-start.35 = (f16[2,96,1024]{2,1,0:T(8,128)(2,1)S(1)}, f16[2,96,1024]{2,1,0:T(8,128)(2,1)S(1)}, u32[]{:S(2)}, u32[]{:S(2)}) collective-permute-start(f16[2,96,1024]{2,1,0:T(8,128)(2,1)S(1)} %slice_bitcast_fusion), channel_id=1, source_target_pairs={{0,4},{2,6},{12,8},{14,10},{1,5},{3,7},{13,9},{15,11},{16,20},{18,... | collective-permute-start | bytes 1179656 | tf_op jit(solution)/shard_map/ppermute | solution.py:190
  186.1 1.3 collective-permute-start.45
  187.4 4.2 %collective-permute-done.35 = f16[2,96,1024]{2,1,0:T(8,128)(2,1)S(1)} collective-permute-done((f16[2,96,1024]{2,1,0:T(8,128)(2,1)S(1)}, f16[2,96,1024]{2,1,0:T(8,128)(2,1)S(1)}, u32[]{:S(2)}, u32[]{:S(2)}) %collective-permute-start.35) | collective-permute-done | bytes 393248 | tf_op jit(solution)/shard_map/ppermute | solution.py:190
  192.4 5.4 %collective-permute-start.38 = (f16[2,96,1024]{2,1,0:T(8,128)(2,1)S(1)}, f16[2,96,1024]{2,1,0:T(8,128)(2,1)S(1)}, u32[]{:S(2)}, u32[]{:S(2)}) collective-permute-start(f16[2,96,1024]{2,1,0:T(8,128)(2,1)S(1)} %slice_bitcast_fusion.3), channel_id=1, source_target_pairs={{0,4},{2,6},{12,8},{14,10},{1,5},{3,7},{13,9},{15,11},{16,20},{18,... | collective-permute-start | bytes 1179656 | tf_op jit(solution)/shard_map/ppermute | solution.py:190
  197.9 3.5 %shard_map.72 = (f32[4,2,96,512]{3,2,1,0:T(8,128)S(1)}, f32[4,2,96,512]{3,2,1,0:T(8,128)S(1)}) custom-call(s32[1]{0:T(128)} %bitcast.place_ref, bf16[768,1024]{1,0:T(8,128)(2,1)S(1)} %bitcast.209, bf16[1024,7168]{1,0:T(8,128)(2,1)} %gate_ref.9, bf16[1024,7168]{1,0:T(8,128)(2,1)} %up_ref.9), custom_call_target="tpu_custom_call" | custom-call | flops 1610612736 | bytes 6815744 | tf_op jit(solution)/shard_map/pallas_call | solution.py:33
  201.5 4.4 %collective-permute-start.40 = (f16[4,2,96,512]{3,2,1,0:T(8,128)(2,1)S(1)}, f16[4,2,96,512]{3,2,1,0:T(8,128)(2,1)S(1)}, u32[]{:S(2)}, u32[]{:S(2)}) collective-permute-start(f16[4,2,96,512]{3,2,1,0:T(8,128)(2,1)S(1)} %convert_element_type.396), channel_id=1, source_target_pairs={{0,2},{2,0},{4,6},{6,4},{8,10},{10,8},{12,14},{14,12},{1,3},{3,1},... | collective-permute-start | bytes 2359304 | tf_op jit(solution)/shard_map/ppermute | solution.py:169
  207.5 4.0 %collective-permute-start.46 = (bf16[4,2,96,1024]{3,2,1,0:T(8,128)(2,1)S(1)}, bf16[4,2,96,1024]{3,2,1,0:T(8,128)(2,1)S(1)}, u32[]{:S(2)}, u32[]{:S(2)}) collective-permute-start(bf16[4,2,96,1024]{3,2,1,0:T(8,128)(2,1)S(1)} %pad_maximum_fusion.2.own_ref), channel_id=1, source_target_pairs={{0,2},{2,0},{4,6},{6,4},{8,10},{10,8},{12,14},{14,12},{1,3},{3,1},... | collective-permute-start | bytes 4718600 | tf_op jit(solution)/shard_map/ppermute | solution.py:190
  211.4 3.7 %collective-permute-done.37 = f16[2,96,1024]{2,1,0:T(8,128)(2,1)S(1)} collective-permute-done((f16[2,96,1024]{2,1,0:T(8,128)(2,1)S(1)}, f16[2,96,1024]{2,1,0:T(8,128)(2,1)S(1)}, u32[]{:S(2)}, u32[]{:S(2)}) %collective-permute-start.37) | collective-permute-done | bytes 393248 | tf_op jit(solution)/shard_map/ppermute | solution.py:190
  216.6 5.7 %collective-permute-start.59 = (bf16[2,96,1024]{2,1,0:T(8,128)(2,1)S(1)}, bf16[2,96,1024]{2,1,0:T(8,128)(2,1)S(1)}, u32[]{:S(2)}, u32[]{:S(2)}) collective-permute-start(bf16[2,96,1024]{2,1,0:T(8,128)(2,1)S(1)} %pad_maximum_fusion.12), channel_id=1, source_target_pairs={{0,4},{2,6},{12,8},{14,10},{4,0},{6,2},{8,12},{10,14},{1,5},{3,7},... | collective-permute-start | bytes 1179656 | tf_op jit(solution)/shard_map/ppermute | solution.py:190
  222.6 1.9 collective-permute-start.47
  224.8 1.3 collective-permute-start.61
  226.1 2.3 collective-permute-done.59
  229.0 5.9 %shard_map.73 = (f32[1024,3584]{1,0:T(8,128)}, f32[1024,3584]{1,0:T(8,128)}) custom-call(bf16[1024,768]{1,0:T(8,128)(2,1)S(1)} %bitcast.211, bf16[4,2,96,1024]{3,2,1,0:T(8,128)(2,1)S(1)} %pad_maximum_fusion.2.own_ref, bf16[4,2,96,1024]{3,2,1,0:T(8,128)(2,1)S(1)} %collective-permute-done.46.other_ref, ...), custom_call_target="tpu_custom_call", output_to_operand_aliasing={{0}: (3, {}), {1}: (4, {})} | custom-call | flops 3221225472 | bytes 13107200 | tf_op jit(solution)/shard_map/pallas_call | solution.py:74
  235.7 7.2 %collective-permute-start.50 = (f16[2,96,512]{2,1,0:T(8,128)(2,1)S(1)}, f16[2,96,512]{2,1,0:T(8,128)(2,1)S(1)}, u32[]{:S(2)}, u32[]{:S(2)}) collective-permute-start(f16[2,96,512]{2,1,0:T(8,128)(2,1)S(1)} %slice_bitcast_fusion.9), channel_id=1, source_target_pairs={{0,4},{2,6},{12,8},{14,10},{1,5},{3,7},{13,9},{15,11},{16,20},{18,... | collective-permute-start | bytes 589832 | tf_op jit(solution)/shard_map/ppermute | solution.py:190
  243.0 1.4 collective-permute-start.63
  244.5 1.1 collective-permute-done.50
  245.7 2.0 collective-permute-start.49
  248.4 5.4 %collective-permute-done.49 = f16[2,96,512]{2,1,0:T(8,128)(2,1)S(1)} collective-permute-done((f16[2,96,512]{2,1,0:T(8,128)(2,1)S(1)}, f16[2,96,512]{2,1,0:T(8,128)(2,1)S(1)}, u32[]{:S(2)}, u32[]{:S(2)}) %collective-permute-start.49) | collective-permute-done | bytes 196640 | tf_op jit(solution)/shard_map/ppermute | solution.py:190
  254.8 3.2 %collective-permute-start.53 = (bf16[2,96,512]{2,1,0:T(8,128)(2,1)S(1)}, bf16[2,96,512]{2,1,0:T(8,128)(2,1)S(1)}, u32[]{:S(2)}, u32[]{:S(2)}) collective-permute-start(bf16[2,96,512]{2,1,0:T(8,128)(2,1)S(1)} %pad_maximum_fusion.17), channel_id=1, source_target_pairs={{0,4},{2,6},{12,8},{14,10},{4,0},{6,2},{8,12},{10,14},{1,5},{3,7},... | collective-permute-start | bytes 589832 | tf_op jit(solution)/shard_map/ppermute | solution.py:190
  258.7 10.4 %collective-permute-start.64 = (bf16[4,2,96,1024]{3,2,1,0:T(8,128)(2,1)S(1)}, bf16[4,2,96,1024]{3,2,1,0:T(8,128)(2,1)S(1)}, u32[]{:S(2)}, u32[]{:S(2)}) collective-permute-start(bf16[4,2,96,1024]{3,2,1,0:T(8,128)(2,1)S(1)} %pad_maximum_fusion.3.own_ref), channel_id=1, source_target_pairs={{0,2},{2,0},{4,6},{6,4},{8,10},{10,8},{12,14},{14,12},{1,3},{3,1},... | collective-permute-start | bytes 4718600 | tf_op jit(solution)/shard_map/ppermute | solution.py:190
  269.1 1.3 collective-permute-start.55
  271.3 1.3 collective-permute-start.57
  272.6 4.5 %collective-permute-done.55 = bf16[2,96,512]{2,1,0:T(8,128)(2,1)S(1)} collective-permute-done((bf16[2,96,512]{2,1,0:T(8,128)(2,1)S(1)}, bf16[2,96,512]{2,1,0:T(8,128)(2,1)S(1)}, u32[]{:S(2)}, u32[]{:S(2)}) %collective-permute-start.55) | collective-permute-done | bytes 196640 | tf_op jit(solution)/shard_map/ppermute | solution.py:190
  277.2 6.9 %collective-permute-done.57 = bf16[2,96,512]{2,1,0:T(8,128)(2,1)S(1)} collective-permute-done((bf16[2,96,512]{2,1,0:T(8,128)(2,1)S(1)}, bf16[2,96,512]{2,1,0:T(8,128)(2,1)S(1)}, u32[]{:S(2)}, u32[]{:S(2)}) %collective-permute-start.57) | collective-permute-done | bytes 196640 | tf_op jit(solution)/shard_map/ppermute | solution.py:190
  284.2 2.9 collective-permute-start.58
  288.0 5.9 %shard_map.74 = (f32[1024,3584]{1,0:T(8,128)}, f32[1024,3584]{1,0:T(8,128)}) custom-call(bf16[1024,768]{1,0:T(8,128)(2,1)S(1)} %bitcast.212, bf16[4,2,96,1024]{3,2,1,0:T(8,128)(2,1)S(1)} %pad_maximum_fusion.3.own_ref, bf16[4,2,96,1024]{3,2,1,0:T(8,128)(2,1)S(1)} %collective-permute-done.64.other_ref, ...), custom_call_target="tpu_custom_call", output_to_operand_aliasing={{0}: (3, {}), {1}: (4, {})} | custom-call | flops 3221225472 | bytes 13107200 | tf_op jit(solution)/shard_map/pallas_call | solution.py:74
  293.9 3.4 %shard_map.75 = (f32[1024,3584]{1,0:T(8,128)}, f32[1024,3584]{1,0:T(8,128)}) custom-call(bf16[1024,768]{1,0:T(8,128)(2,1)S(1)} %bitcast.213, bf16[4,2,96,512]{3,2,1,0:T(8,128)(2,1)S(1)} %pad_maximum_fusion.10.own_ref, bf16[4,2,96,512]{3,2,1,0:T(8,128)(2,1)S(1)} %collective-permute-done.58.other_ref, ...), custom_call_target="tpu_custom_call", output_to_operand_aliasing={{0}: (3, {}), {1}: (4, {})} | custom-call | flops 1610612736 | bytes 7340032 | tf_op jit(solution)/shard_map/pallas_call | solution.py:74
  (200 shorter events, 34.2 us)
Async XLA Ops:
  0.6 20.7 %collective-permute-start.2 = (bf16[384,512]{1,0:T(8,128)(2,1)}, bf16[384,512]{1,0:T(8,128)(2,1)S(1)}, u32[]{:S(2)}, u32[]{:S(2)}) collective-permute-start(bf16[384,512]{1,0:T(8,128)(2,1)} %bitcast.223), channel_id=1, source_target_pairs={{0,1},{1,0},{2,3},{3,2},{4,5},{5,4},{6,7},{7,6},{8,9},{9,8},{10,11... | collective-permute-start | bytes 1179656 | tf_op jit(solution)/shard_map/ppermute | solution.py:126
  2.8 9.9 %collective-permute-start = (bf16[384,512]{1,0:T(8,128)(2,1)}, bf16[384,512]{1,0:T(8,128)(2,1)S(1)}, u32[]{:S(2)}, u32[]{:S(2)}) collective-permute-start(bf16[384,512]{1,0:T(8,128)(2,1)} %bitcast.224), channel_id=1, source_target_pairs={{0,16},{16,0},{1,17},{17,1},{2,18},{18,2},{3,19},{19,3},{4,20},{20... | collective-permute-start | bytes 1179656 | tf_op jit(solution)/shard_map/ppermute | solution.py:125
  5.8 14.1 %collective-permute-start.23 = (bf16[48,3584]{1,0:T(8,128)(2,1)}, bf16[48,3584]{1,0:T(8,128)(2,1)S(1)}, u32[]{:S(2)}, u32[]{:S(2)}) collective-permute-start(bf16[48,3584]{1,0:T(8,128)(2,1)} %get-tuple-element.116), channel_id=1, source_target_pairs={{0,1},{1,0},{2,3},{3,2},{4,5},{5,4},{6,7},{7,6},{8,9},{9,8},{10,11... | collective-permute-start | bytes 1032200 | tf_op jit(solution)/shard_map/ppermute | solution.py:151
  17.9 12.9 %collective-permute-start.1 = (f16[4,2,48,1024]{3,2,1,0:T(8,128)(2,1)S(1)}, f16[4,2,48,1024]{3,2,1,0:T(8,128)(2,1)S(1)}, u32[]{:S(2)}, u32[]{:S(2)}) collective-permute-start(f16[4,2,48,1024]{3,2,1,0:T(8,128)(2,1)S(1)} %convert_element_type.320), channel_id=1, source_target_pairs={{0,2},{2,0},{4,6},{6,4},{8,10},{10,8},{12,14},{14,12},{1,3},{3,1},... | collective-permute-start | bytes 2359304 | tf_op jit(solution)/shard_map/ppermute | solution.py:169
  19.8 10.7 %collective-permute-start.3 = (bf16[384,512]{1,0:T(8,128)(2,1)S(1)}, bf16[384,512]{1,0:T(8,128)(2,1)S(1)}, u32[]{:S(2)}, u32[]{:S(2)}) collective-permute-start(bf16[384,512]{1,0:T(8,128)(2,1)S(1)} %collective-permute-done), channel_id=1, source_target_pairs={{0,1},{1,0},{2,3},{3,2},{4,5},{5,4},{6,7},{7,6},{8,9},{9,8},{10,11... | collective-permute-start | bytes 1179656 | tf_op jit(solution)/shard_map/ppermute | solution.py:127
  31.1 6.5 %collective-permute-start.4 = (f16[2,48,1024]{2,1,0:T(8,128)(2,1)S(1)}, f16[2,48,1024]{2,1,0:T(8,128)(2,1)S(1)}, u32[]{:S(2)}, u32[]{:S(2)}) collective-permute-start(f16[2,48,1024]{2,1,0:T(8,128)(2,1)S(1)} %get-tuple-element.94), channel_id=1, source_target_pairs={{0,4},{2,6},{12,8},{14,10},{1,5},{3,7},{13,9},{15,11},{16,20},{18,... | collective-permute-start | bytes 589832 | tf_op jit(solution)/shard_map/ppermute | solution.py:190
  37.7 11.9 %collective-permute-start.5 = (f16[2,48,1024]{2,1,0:T(8,128)(2,1)S(1)}, f16[2,48,1024]{2,1,0:T(8,128)(2,1)S(1)}, u32[]{:S(2)}, u32[]{:S(2)}) collective-permute-start(f16[2,48,1024]{2,1,0:T(8,128)(2,1)S(1)} %add_convert_fusion.8), channel_id=1, source_target_pairs={{4,8},{6,10},{8,4},{10,6},{5,9},{7,11},{9,5},{11,7},{20,24},{22,26... | collective-permute-start | bytes 589832 | tf_op jit(solution)/shard_map/ppermute | solution.py:190
  38.4 11.2 %collective-permute-start.7 = (f16[2,48,1024]{2,1,0:T(8,128)(2,1)S(1)}, f16[2,48,1024]{2,1,0:T(8,128)(2,1)S(1)}, u32[]{:S(2)}, u32[]{:S(2)}) collective-permute-start(f16[2,48,1024]{2,1,0:T(8,128)(2,1)S(1)} %get-tuple-element.44), channel_id=1, source_target_pairs={{0,4},{2,6},{12,8},{14,10},{1,5},{3,7},{13,9},{15,11},{16,20},{18,... | collective-permute-start | bytes 589832 | tf_op jit(solution)/shard_map/ppermute | solution.py:190
  49.9 5.1 %collective-permute-start.6 = (f16[2,48,1024]{2,1,0:T(8,128)(2,1)S(1)}, f16[2,48,1024]{2,1,0:T(8,128)(2,1)S(1)}, u32[]{:S(2)}, u32[]{:S(2)}) collective-permute-start(f16[2,48,1024]{2,1,0:T(8,128)(2,1)S(1)} %get-tuple-element.91), channel_id=1, source_target_pairs={{0,4},{2,6},{12,8},{14,10},{4,0},{6,2},{8,12},{10,14},{1,5},{3,7},... | collective-permute-start | bytes 589832 | tf_op jit(solution)/shard_map/ppermute | solution.py:190
  50.0 5.0 %collective-permute-start.8 = (f16[2,48,1024]{2,1,0:T(8,128)(2,1)S(1)}, f16[2,48,1024]{2,1,0:T(8,128)(2,1)S(1)}, u32[]{:S(2)}, u32[]{:S(2)}) collective-permute-start(f16[2,48,1024]{2,1,0:T(8,128)(2,1)S(1)} %get-tuple-element.92), channel_id=1, source_target_pairs={{4,8},{6,10},{8,4},{10,6},{5,9},{7,11},{9,5},{11,7},{20,24},{22,26... | collective-permute-start | bytes 589832 | tf_op jit(solution)/shard_map/ppermute | solution.py:190
  51.7 14.1 %collective-permute-start.9 = (f16[4,2,48,1024]{3,2,1,0:T(8,128)(2,1)}, f16[4,2,48,1024]{3,2,1,0:T(8,128)(2,1)}, u32[]{:S(2)}, u32[]{:S(2)}) collective-permute-start(f16[4,2,48,1024]{3,2,1,0:T(8,128)(2,1)} %convert_element_type.339), channel_id=1, source_target_pairs={{0,2},{2,0},{4,6},{6,4},{8,10},{10,8},{12,14},{14,12},{1,3},{3,1},... | collective-permute-start | bytes 2359304 | tf_op jit(solution)/shard_map/ppermute | solution.py:169
  56.0 7.4 %collective-permute-start.19 = (bf16[2,48,1024]{2,1,0:T(8,128)(2,1)}, bf16[2,48,1024]{2,1,0:T(8,128)(2,1)}, u32[]{:S(2)}, u32[]{:S(2)}) collective-permute-start(bf16[2,48,1024]{2,1,0:T(8,128)(2,1)} %pad_maximum_fusion.14), channel_id=1, source_target_pairs={{4,8},{6,10},{8,4},{10,6},{5,9},{7,11},{9,5},{11,7},{20,24},{22,26... | collective-permute-start | bytes 589832 | tf_op jit(solution)/shard_map/ppermute | solution.py:190
  57.4 7.7 %collective-permute-start.18 = (bf16[2,48,1024]{2,1,0:T(8,128)(2,1)}, bf16[2,48,1024]{2,1,0:T(8,128)(2,1)}, u32[]{:S(2)}, u32[]{:S(2)}) collective-permute-start(bf16[2,48,1024]{2,1,0:T(8,128)(2,1)} %pad_maximum_fusion.14), channel_id=1, source_target_pairs={{0,4},{2,6},{12,8},{14,10},{4,0},{6,2},{8,12},{10,14},{1,5},{3,7},... | collective-permute-start | bytes 589832 | tf_op jit(solution)/shard_map/ppermute | solution.py:190
  63.4 34.2 %collective-permute-start.20 = (bf16[2,48,1024]{2,1,0:T(8,128)(2,1)}, bf16[2,48,1024]{2,1,0:T(8,128)(2,1)S(1)}, u32[]{:S(2)}, u32[]{:S(2)}) collective-permute-start(bf16[2,48,1024]{2,1,0:T(8,128)(2,1)} %collective-permute-done.19), channel_id=1, source_target_pairs={{4,0},{6,2},{8,12},{10,14},{5,1},{7,3},{9,13},{11,15},{20,16},{22,... | collective-permute-start | bytes 589832 | tf_op jit(solution)/shard_map/ppermute | solution.py:190
  65.1 9.6 %collective-permute-start.21 = (bf16[2,48,1024]{2,1,0:T(8,128)(2,1)}, bf16[2,48,1024]{2,1,0:T(8,128)(2,1)S(1)}, u32[]{:S(2)}, u32[]{:S(2)}) collective-permute-start(bf16[2,48,1024]{2,1,0:T(8,128)(2,1)} %collective-permute-done.18), channel_id=1, source_target_pairs={{4,8},{6,10},{8,4},{10,6},{5,9},{7,11},{9,5},{11,7},{20,24},{22,26... | collective-permute-start | bytes 589832 | tf_op jit(solution)/shard_map/ppermute | solution.py:190
  67.7 8.5 %collective-permute-start.10 = (f16[2,48,1024]{2,1,0:T(8,128)(2,1)S(1)}, f16[2,48,1024]{2,1,0:T(8,128)(2,1)S(1)}, u32[]{:S(2)}, u32[]{:S(2)}) collective-permute-start(f16[2,48,1024]{2,1,0:T(8,128)(2,1)S(1)} %get-tuple-element.98), channel_id=1, source_target_pairs={{0,4},{2,6},{12,8},{14,10},{1,5},{3,7},{13,9},{15,11},{16,20},{18,... | collective-permute-start | bytes 589832 | tf_op jit(solution)/shard_map/ppermute | solution.py:190
  74.6 35.8 %collective-permute-start.22 = (bf16[2,48,1024]{2,1,0:T(8,128)(2,1)S(1)}, bf16[2,48,1024]{2,1,0:T(8,128)(2,1)S(1)}, u32[]{:S(2)}, u32[]{:S(2)}) collective-permute-start(bf16[2,48,1024]{2,1,0:T(8,128)(2,1)S(1)} %collective-permute-done.21), channel_id=1, source_target_pairs={{4,0},{6,2},{8,12},{10,14},{5,1},{7,3},{9,13},{11,15},{20,16},{22,... | collective-permute-start | bytes 589832 | tf_op jit(solution)/shard_map/ppermute | solution.py:190
  76.3 20.3 %collective-permute-start.24 = (f16[2,48,1024]{2,1,0:T(8,128)(2,1)S(1)}, f16[2,48,1024]{2,1,0:T(8,128)(2,1)S(1)}, u32[]{:S(2)}, u32[]{:S(2)}) collective-permute-start(f16[2,48,1024]{2,1,0:T(8,128)(2,1)S(1)} %add_convert_fusion.7), channel_id=1, source_target_pairs={{4,8},{6,10},{8,4},{10,6},{5,9},{7,11},{9,5},{11,7},{20,24},{22,26... | collective-permute-start | bytes 589832 | tf_op jit(solution)/shard_map/ppermute | solution.py:190
  77.0 19.7 %collective-permute-start.26 = (f16[2,48,1024]{2,1,0:T(8,128)(2,1)S(1)}, f16[2,48,1024]{2,1,0:T(8,128)(2,1)S(1)}, u32[]{:S(2)}, u32[]{:S(2)}) collective-permute-start(f16[2,48,1024]{2,1,0:T(8,128)(2,1)S(1)} %get-tuple-element.54), channel_id=1, source_target_pairs={{0,4},{2,6},{12,8},{14,10},{1,5},{3,7},{13,9},{15,11},{16,20},{18,... | collective-permute-start | bytes 589832 | tf_op jit(solution)/shard_map/ppermute | solution.py:190
  90.3 26.2 %collective-permute-start.11 = (f16[4,2,96,1024]{3,2,1,0:T(8,128)(2,1)S(1)}, f16[4,2,96,1024]{3,2,1,0:T(8,128)(2,1)S(1)}, u32[]{:S(2)}, u32[]{:S(2)}) collective-permute-start(f16[4,2,96,1024]{3,2,1,0:T(8,128)(2,1)S(1)} %convert_element_type.342), channel_id=1, source_target_pairs={{0,2},{2,0},{4,6},{6,4},{8,10},{10,8},{12,14},{14,12},{1,3},{3,1},... | collective-permute-start | bytes 4718600 | tf_op jit(solution)/shard_map/ppermute | solution.py:169
  96.8 6.6 %collective-permute-start.25 = (f16[2,48,1024]{2,1,0:T(8,128)(2,1)S(1)}, f16[2,48,1024]{2,1,0:T(8,128)(2,1)S(1)}, u32[]{:S(2)}, u32[]{:S(2)}) collective-permute-start(f16[2,48,1024]{2,1,0:T(8,128)(2,1)S(1)} %get-tuple-element.95), channel_id=1, source_target_pairs={{0,4},{2,6},{12,8},{14,10},{4,0},{6,2},{8,12},{10,14},{1,5},{3,7},... | collective-permute-start | bytes 589832 | tf_op jit(solution)/shard_map/ppermute | solution.py:190
  96.9 6.5 %collective-permute-start.27 = (f16[2,48,1024]{2,1,0:T(8,128)(2,1)S(1)}, f16[2,48,1024]{2,1,0:T(8,128)(2,1)S(1)}, u32[]{:S(2)}, u32[]{:S(2)}) collective-permute-start(f16[2,48,1024]{2,1,0:T(8,128)(2,1)S(1)} %get-tuple-element.96), channel_id=1, source_target_pairs={{4,8},{6,10},{8,4},{10,6},{5,9},{7,11},{9,5},{11,7},{20,24},{22,26... | collective-permute-start | bytes 589832 | tf_op jit(solution)/shard_map/ppermute | solution.py:190
  104.6 8.5 %collective-permute-start.29 = (bf16[2,48,1024]{2,1,0:T(8,128)(2,1)S(1)}, bf16[2,48,1024]{2,1,0:T(8,128)(2,1)S(1)}, u32[]{:S(2)}, u32[]{:S(2)}) collective-permute-start(bf16[2,48,1024]{2,1,0:T(8,128)(2,1)S(1)} %pad_maximum_fusion.15), channel_id=1, source_target_pairs={{4,8},{6,10},{8,4},{10,6},{5,9},{7,11},{9,5},{11,7},{20,24},{22,26... | collective-permute-start | bytes 589832 | tf_op jit(solution)/shard_map/ppermute | solution.py:190
  105.4 9.0 %collective-permute-start.28 = (bf16[2,48,1024]{2,1,0:T(8,128)(2,1)S(1)}, bf16[2,48,1024]{2,1,0:T(8,128)(2,1)S(1)}, u32[]{:S(2)}, u32[]{:S(2)}) collective-permute-start(bf16[2,48,1024]{2,1,0:T(8,128)(2,1)S(1)} %pad_maximum_fusion.15), channel_id=1, source_target_pairs={{0,4},{2,6},{12,8},{14,10},{4,0},{6,2},{8,12},{10,14},{1,5},{3,7},... | collective-permute-start | bytes 589832 | tf_op jit(solution)/shard_map/ppermute | solution.py:190
  111.4 43.7 %collective-permute-start.33 = (bf16[4,2,48,1024]{3,2,1,0:T(8,128)(2,1)}, bf16[4,2,48,1024]{3,2,1,0:T(8,128)(2,1)}, u32[]{:S(2)}, u32[]{:S(2)}) collective-permute-start(bf16[4,2,48,1024]{3,2,1,0:T(8,128)(2,1)} %pad_maximum_fusion.8), channel_id=1, source_target_pairs={{0,2},{2,0},{4,6},{6,4},{8,10},{10,8},{12,14},{14,12},{1,3},{3,1},... | collective-permute-start | bytes 2359304 | tf_op jit(solution)/shard_map/ppermute | solution.py:190
  113.1 13.8 %collective-permute-start.30 = (bf16[2,48,1024]{2,1,0:T(8,128)(2,1)S(1)}, bf16[2,48,1024]{2,1,0:T(8,128)(2,1)S(1)}, u32[]{:S(2)}, u32[]{:S(2)}) collective-permute-start(bf16[2,48,1024]{2,1,0:T(8,128)(2,1)S(1)} %collective-permute-done.29), channel_id=1, source_target_pairs={{4,0},{6,2},{8,12},{10,14},{5,1},{7,3},{9,13},{11,15},{20,16},{22,... | collective-permute-start | bytes 589832 | tf_op jit(solution)/shard_map/ppermute | solution.py:190
  115.1 12.1 %collective-permute-start.32 = (bf16[2,48,1024]{2,1,0:T(8,128)(2,1)S(1)}, bf16[2,48,1024]{2,1,0:T(8,128)(2,1)S(1)}, u32[]{:S(2)}, u32[]{:S(2)}) collective-permute-start(bf16[2,48,1024]{2,1,0:T(8,128)(2,1)S(1)} %collective-permute-done.31), channel_id=1, source_target_pairs={{4,0},{6,2},{8,12},{10,14},{5,1},{7,3},{9,13},{11,15},{20,16},{22,... | collective-permute-start | bytes 589832 | tf_op jit(solution)/shard_map/ppermute | solution.py:190
  117.2 15.0 %collective-permute-start.12 = (f16[2,96,1024]{2,1,0:T(8,128)(2,1)S(1)}, f16[2,96,1024]{2,1,0:T(8,128)(2,1)S(1)}, u32[]{:S(2)}, u32[]{:S(2)}) collective-permute-start(f16[2,96,1024]{2,1,0:T(8,128)(2,1)S(1)} %get-tuple-element.78), channel_id=1, source_target_pairs={{0,4},{2,6},{12,8},{14,10},{1,5},{3,7},{13,9},{15,11},{16,20},{18,... | collective-permute-start | bytes 1179656 | tf_op jit(solution)/shard_map/ppermute | solution.py:190
  132.3 20.1 %collective-permute-start.13 = (f16[2,96,1024]{2,1,0:T(8,128)(2,1)S(1)}, f16[2,96,1024]{2,1,0:T(8,128)(2,1)S(1)}, u32[]{:S(2)}, u32[]{:S(2)}) collective-permute-start(f16[2,96,1024]{2,1,0:T(8,128)(2,1)S(1)} %add_convert_fusion.5), channel_id=1, source_target_pairs={{4,8},{6,10},{8,4},{10,6},{5,9},{7,11},{9,5},{11,7},{20,24},{22,26... | collective-permute-start | bytes 1179656 | tf_op jit(solution)/shard_map/ppermute | solution.py:190
  133.0 19.4 %collective-permute-start.15 = (f16[2,96,1024]{2,1,0:T(8,128)(2,1)S(1)}, f16[2,96,1024]{2,1,0:T(8,128)(2,1)}, u32[]{:S(2)}, u32[]{:S(2)}) collective-permute-start(f16[2,96,1024]{2,1,0:T(8,128)(2,1)S(1)} %get-tuple-element.52), channel_id=1, source_target_pairs={{0,4},{2,6},{12,8},{14,10},{1,5},{3,7},{13,9},{15,11},{16,20},{18,... | collective-permute-start | bytes 1179656 | tf_op jit(solution)/shard_map/ppermute | solution.py:190
  141.2 13.8 %collective-permute-start.34 = (bf16[4,2,48,1024]{3,2,1,0:T(8,128)(2,1)S(1)}, bf16[4,2,48,1024]{3,2,1,0:T(8,128)(2,1)S(1)}, u32[]{:S(2)}, u32[]{:S(2)}) collective-permute-start(bf16[4,2,48,1024]{3,2,1,0:T(8,128)(2,1)S(1)} %pad_maximum_fusion.9), channel_id=1, source_target_pairs={{0,2},{2,0},{4,6},{6,4},{8,10},{10,8},{12,14},{14,12},{1,3},{3,1},... | collective-permute-start | bytes 2359304 | tf_op jit(solution)/shard_map/ppermute | solution.py:190
  152.3 26.3 %collective-permute-start.17 = (f16[4,2,96,1024]{3,2,1,0:T(8,128)(2,1)S(1)}, f16[4,2,96,1024]{3,2,1,0:T(8,128)(2,1)S(1)}, u32[]{:S(2)}, u32[]{:S(2)}) collective-permute-start(f16[4,2,96,1024]{3,2,1,0:T(8,128)(2,1)S(1)} %convert_element_type.361), channel_id=1, source_target_pairs={{0,2},{2,0},{4,6},{6,4},{8,10},{10,8},{12,14},{14,12},{1,3},{3,1},... | collective-permute-start | bytes 4718600 | tf_op jit(solution)/shard_map/ppermute | solution.py:169
  153.9 10.3 %collective-permute-start.14 = (f16[2,96,1024]{2,1,0:T(8,128)(2,1)S(1)}, f16[2,96,1024]{2,1,0:T(8,128)(2,1)S(1)}, u32[]{:S(2)}, u32[]{:S(2)}) collective-permute-start(f16[2,96,1024]{2,1,0:T(8,128)(2,1)S(1)} %get-tuple-element.75), channel_id=1, source_target_pairs={{0,4},{2,6},{12,8},{14,10},{4,0},{6,2},{8,12},{10,14},{1,5},{3,7},... | collective-permute-start | bytes 1179656 | tf_op jit(solution)/shard_map/ppermute | solution.py:190
  154.0 10.2 %collective-permute-start.16 = (f16[2,96,1024]{2,1,0:T(8,128)(2,1)S(1)}, f16[2,96,1024]{2,1,0:T(8,128)(2,1)S(1)}, u32[]{:S(2)}, u32[]{:S(2)}) collective-permute-start(f16[2,96,1024]{2,1,0:T(8,128)(2,1)S(1)} %get-tuple-element.76), channel_id=1, source_target_pairs={{4,8},{6,10},{8,4},{10,6},{5,9},{7,11},{9,5},{11,7},{20,24},{22,26... | collective-permute-start | bytes 1179656 | tf_op jit(solution)/shard_map/ppermute | solution.py:190
  164.8 11.8 %collective-permute-start.42 = (bf16[2,96,1024]{2,1,0:T(8,128)(2,1)S(1)}, bf16[2,96,1024]{2,1,0:T(8,128)(2,1)S(1)}, u32[]{:S(2)}, u32[]{:S(2)}) collective-permute-start(bf16[2,96,1024]{2,1,0:T(8,128)(2,1)S(1)} %pad_maximum_fusion.11), channel_id=1, source_target_pairs={{4,8},{6,10},{8,4},{10,6},{5,9},{7,11},{9,5},{11,7},{20,24},{22,26... | collective-permute-start | bytes 1179656 | tf_op jit(solution)/shard_map/ppermute | solution.py:190
  165.5 12.4 %collective-permute-start.41 = (bf16[2,96,1024]{2,1,0:T(8,128)(2,1)S(1)}, bf16[2,96,1024]{2,1,0:T(8,128)(2,1)S(1)}, u32[]{:S(2)}, u32[]{:S(2)}) collective-permute-start(bf16[2,96,1024]{2,1,0:T(8,128)(2,1)S(1)} %pad_maximum_fusion.11), channel_id=1, source_target_pairs={{0,4},{2,6},{12,8},{14,10},{4,0},{6,2},{8,12},{10,14},{1,5},{3,7},... | collective-permute-start | bytes 1179656 | tf_op jit(solution)/shard_map/ppermute | solution.py:190
  176.6 21.2 %collective-permute-start.43 = (bf16[2,96,1024]{2,1,0:T(8,128)(2,1)S(1)}, bf16[2,96,1024]{2,1,0:T(8,128)(2,1)S(1)}, u32[]{:S(2)}, u32[]{:S(2)}) collective-permute-start(bf16[2,96,1024]{2,1,0:T(8,128)(2,1)S(1)} %collective-permute-done.42), channel_id=1, source_target_pairs={{4,0},{6,2},{8,12},{10,14},{5,1},{7,3},{9,13},{11,15},{20,16},{22,... | collective-permute-start | bytes 1179656 | tf_op jit(solution)/shard_map/ppermute | solution.py:190
  177.9 8.2 %collective-permute-start.44 = (bf16[2,96,1024]{2,1,0:T(8,128)(2,1)S(1)}, bf16[2,96,1024]{2,1,0:T(8,128)(2,1)S(1)}, u32[]{:S(2)}, u32[]{:S(2)}) collective-permute-start(bf16[2,96,1024]{2,1,0:T(8,128)(2,1)S(1)} %collective-permute-done.41), channel_id=1, source_target_pairs={{4,8},{6,10},{8,4},{10,6},{5,9},{7,11},{9,5},{11,7},{20,24},{22,26... | collective-permute-start | bytes 1179656 | tf_op jit(solution)/shard_map/ppermute | solution.py:190
  179.3 12.2 %collective-permute-start.35 = (f16[2,96,1024]{2,1,0:T(8,128)(2,1)S(1)}, f16[2,96,1024]{2,1,0:T(8,128)(2,1)S(1)}, u32[]{:S(2)}, u32[]{:S(2)}) collective-permute-start(f16[2,96,1024]{2,1,0:T(8,128)(2,1)S(1)} %slice_bitcast_fusion), channel_id=1, source_target_pairs={{0,4},{2,6},{12,8},{14,10},{1,5},{3,7},{13,9},{15,11},{16,20},{18,... | collective-permute-start | bytes 1179656 | tf_op jit(solution)/shard_map/ppermute | solution.py:190
  186.1 21.1 %collective-permute-start.45 = (bf16[2,96,1024]{2,1,0:T(8,128)(2,1)S(1)}, bf16[2,96,1024]{2,1,0:T(8,128)(2,1)S(1)}, u32[]{:S(2)}, u32[]{:S(2)}) collective-permute-start(bf16[2,96,1024]{2,1,0:T(8,128)(2,1)S(1)} %collective-permute-done.44), channel_id=1, source_target_pairs={{4,0},{6,2},{8,12},{10,14},{5,1},{7,3},{9,13},{11,15},{20,16},{22,... | collective-permute-start | bytes 1179656 | tf_op jit(solution)/shard_map/ppermute | solution.py:190
  191.7 14.2 %collective-permute-start.36 = (f16[2,96,1024]{2,1,0:T(8,128)(2,1)S(1)}, f16[2,96,1024]{2,1,0:T(8,128)(2,1)S(1)}, u32[]{:S(2)}, u32[]{:S(2)}) collective-permute-start(f16[2,96,1024]{2,1,0:T(8,128)(2,1)S(1)} %fusion.9), channel_id=1, source_target_pairs={{4,8},{6,10},{8,4},{10,6},{5,9},{7,11},{9,5},{11,7},{20,24},{22,26... | collective-permute-start | bytes 1179656 | tf_op jit(solution)/shard_map/ppermute | solution.py:190
  192.4 13.5 %collective-permute-start.38 = (f16[2,96,1024]{2,1,0:T(8,128)(2,1)S(1)}, f16[2,96,1024]{2,1,0:T(8,128)(2,1)S(1)}, u32[]{:S(2)}, u32[]{:S(2)}) collective-permute-start(f16[2,96,1024]{2,1,0:T(8,128)(2,1)S(1)} %slice_bitcast_fusion.3), channel_id=1, source_target_pairs={{0,4},{2,6},{12,8},{14,10},{1,5},{3,7},{13,9},{15,11},{16,20},{18,... | collective-permute-start | bytes 1179656 | tf_op jit(solution)/shard_map/ppermute | solution.py:190
  201.5 20.8 %collective-permute-start.40 = (f16[4,2,96,512]{3,2,1,0:T(8,128)(2,1)S(1)}, f16[4,2,96,512]{3,2,1,0:T(8,128)(2,1)S(1)}, u32[]{:S(2)}, u32[]{:S(2)}) collective-permute-start(f16[4,2,96,512]{3,2,1,0:T(8,128)(2,1)S(1)} %convert_element_type.396), channel_id=1, source_target_pairs={{0,2},{2,0},{4,6},{6,4},{8,10},{10,8},{12,14},{14,12},{1,3},{3,1},... | collective-permute-start | bytes 2359304 | tf_op jit(solution)/shard_map/ppermute | solution.py:169
  206.4 8.8 %collective-permute-start.37 = (f16[2,96,1024]{2,1,0:T(8,128)(2,1)S(1)}, f16[2,96,1024]{2,1,0:T(8,128)(2,1)S(1)}, u32[]{:S(2)}, u32[]{:S(2)}) collective-permute-start(f16[2,96,1024]{2,1,0:T(8,128)(2,1)S(1)} %get-tuple-element.73), channel_id=1, source_target_pairs={{0,4},{2,6},{12,8},{14,10},{4,0},{6,2},{8,12},{10,14},{1,5},{3,7},... | collective-permute-start | bytes 1179656 | tf_op jit(solution)/shard_map/ppermute | solution.py:190
  206.5 8.7 %collective-permute-start.39 = (f16[2,96,1024]{2,1,0:T(8,128)(2,1)S(1)}, f16[2,96,1024]{2,1,0:T(8,128)(2,1)S(1)}, u32[]{:S(2)}, u32[]{:S(2)}) collective-permute-start(f16[2,96,1024]{2,1,0:T(8,128)(2,1)S(1)} %get-tuple-element.74), channel_id=1, source_target_pairs={{4,8},{6,10},{8,4},{10,6},{5,9},{7,11},{9,5},{11,7},{20,24},{22,26... | collective-permute-start | bytes 1179656 | tf_op jit(solution)/shard_map/ppermute | solution.py:190
  207.5 21.6 %collective-permute-start.46 = (bf16[4,2,96,1024]{3,2,1,0:T(8,128)(2,1)S(1)}, bf16[4,2,96,1024]{3,2,1,0:T(8,128)(2,1)S(1)}, u32[]{:S(2)}, u32[]{:S(2)}) collective-permute-start(bf16[4,2,96,1024]{3,2,1,0:T(8,128)(2,1)S(1)} %pad_maximum_fusion.2.own_ref), channel_id=1, source_target_pairs={{0,2},{2,0},{4,6},{6,4},{8,10},{10,8},{12,14},{14,12},{1,3},{3,1},... | collective-permute-start | bytes 4718600 | tf_op jit(solution)/shard_map/ppermute | solution.py:190
  215.8 8.9 %collective-permute-start.60 = (bf16[2,96,1024]{2,1,0:T(8,128)(2,1)S(1)}, bf16[2,96,1024]{2,1,0:T(8,128)(2,1)S(1)}, u32[]{:S(2)}, u32[]{:S(2)}) collective-permute-start(bf16[2,96,1024]{2,1,0:T(8,128)(2,1)S(1)} %pad_maximum_fusion.12), channel_id=1, source_target_pairs={{4,8},{6,10},{8,4},{10,6},{5,9},{7,11},{9,5},{11,7},{20,24},{22,26... | collective-permute-start | bytes 1179656 | tf_op jit(solution)/shard_map/ppermute | solution.py:190
  216.6 11.7 %collective-permute-start.59 = (bf16[2,96,1024]{2,1,0:T(8,128)(2,1)S(1)}, bf16[2,96,1024]{2,1,0:T(8,128)(2,1)S(1)}, u32[]{:S(2)}, u32[]{:S(2)}) collective-permute-start(bf16[2,96,1024]{2,1,0:T(8,128)(2,1)S(1)} %pad_maximum_fusion.12), channel_id=1, source_target_pairs={{0,4},{2,6},{12,8},{14,10},{4,0},{6,2},{8,12},{10,14},{1,5},{3,7},... | collective-permute-start | bytes 1179656 | tf_op jit(solution)/shard_map/ppermute | solution.py:190
  222.6 12.3 %collective-permute-start.47 = (f16[2,96,512]{2,1,0:T(8,128)(2,1)S(1)}, f16[2,96,512]{2,1,0:T(8,128)(2,1)S(1)}, u32[]{:S(2)}, u32[]{:S(2)}) collective-permute-start(f16[2,96,512]{2,1,0:T(8,128)(2,1)S(1)} %slice_bitcast_fusion.4), channel_id=1, source_target_pairs={{0,4},{2,6},{12,8},{14,10},{1,5},{3,7},{13,9},{15,11},{16,20},{18,... | collective-permute-start | bytes 589832 | tf_op jit(solution)/shard_map/ppermute | solution.py:190
  224.8 23.6 %collective-permute-start.61 = (bf16[2,96,1024]{2,1,0:T(8,128)(2,1)S(1)}, bf16[2,96,1024]{2,1,0:T(8,128)(2,1)S(1)}, u32[]{:S(2)}, u32[]{:S(2)}) collective-permute-start(bf16[2,96,1024]{2,1,0:T(8,128)(2,1)S(1)} %collective-permute-done.60), channel_id=1, source_target_pairs={{4,0},{6,2},{8,12},{10,14},{5,1},{7,3},{9,13},{11,15},{20,16},{22,... | collective-permute-start | bytes 1179656 | tf_op jit(solution)/shard_map/ppermute | solution.py:190
  228.3 14.7 %collective-permute-start.62 = (bf16[2,96,1024]{2,1,0:T(8,128)(2,1)S(1)}, bf16[2,96,1024]{2,1,0:T(8,128)(2,1)S(1)}, u32[]{:S(2)}, u32[]{:S(2)}) collective-permute-start(bf16[2,96,1024]{2,1,0:T(8,128)(2,1)S(1)} %collective-permute-done.59), channel_id=1, source_target_pairs={{4,8},{6,10},{8,4},{10,6},{5,9},{7,11},{9,5},{11,7},{20,24},{22,26... | collective-permute-start | bytes 1179656 | tf_op jit(solution)/shard_map/ppermute | solution.py:190
  235.1 9.4 %collective-permute-start.48 = (f16[2,96,512]{2,1,0:T(8,128)(2,1)S(1)}, f16[2,96,512]{2,1,0:T(8,128)(2,1)S(1)}, u32[]{:S(2)}, u32[]{:S(2)}) collective-permute-start(f16[2,96,512]{2,1,0:T(8,128)(2,1)S(1)} %fusion.33), channel_id=1, source_target_pairs={{4,8},{6,10},{8,4},{10,6},{5,9},{7,11},{9,5},{11,7},{20,24},{22,26... | collective-permute-start | bytes 589832 | tf_op jit(solution)/shard_map/ppermute | solution.py:190
  235.7 9.8 %collective-permute-start.50 = (f16[2,96,512]{2,1,0:T(8,128)(2,1)S(1)}, f16[2,96,512]{2,1,0:T(8,128)(2,1)S(1)}, u32[]{:S(2)}, u32[]{:S(2)}) collective-permute-start(f16[2,96,512]{2,1,0:T(8,128)(2,1)S(1)} %slice_bitcast_fusion.9), channel_id=1, source_target_pairs={{0,4},{2,6},{12,8},{14,10},{1,5},{3,7},{13,9},{15,11},{16,20},{18,... | collective-permute-start | bytes 589832 | tf_op jit(solution)/shard_map/ppermute | solution.py:190
  243.0 15.4 %collective-permute-start.63 = (bf16[2,96,1024]{2,1,0:T(8,128)(2,1)S(1)}, bf16[2,96,1024]{2,1,0:T(8,128)(2,1)S(1)}, u32[]{:S(2)}, u32[]{:S(2)}) collective-permute-start(bf16[2,96,1024]{2,1,0:T(8,128)(2,1)S(1)} %collective-permute-done.62), channel_id=1, source_target_pairs={{4,0},{6,2},{8,12},{10,14},{5,1},{7,3},{9,13},{11,15},{20,16},{22,... | collective-permute-start | bytes 1179656 | tf_op jit(solution)/shard_map/ppermute | solution.py:190
  245.7 8.1 %collective-permute-start.49 = (f16[2,96,512]{2,1,0:T(8,128)(2,1)S(1)}, f16[2,96,512]{2,1,0:T(8,128)(2,1)S(1)}, u32[]{:S(2)}, u32[]{:S(2)}) collective-permute-start(f16[2,96,512]{2,1,0:T(8,128)(2,1)S(1)} %get-tuple-element.89), channel_id=1, source_target_pairs={{0,4},{2,6},{12,8},{14,10},{4,0},{6,2},{8,12},{10,14},{1,5},{3,7},... | collective-permute-start | bytes 589832 | tf_op jit(solution)/shard_map/ppermute | solution.py:190
  247.7 6.1 %collective-permute-start.51 = (f16[2,96,512]{2,1,0:T(8,128)(2,1)S(1)}, f16[2,96,512]{2,1,0:T(8,128)(2,1)S(1)}, u32[]{:S(2)}, u32[]{:S(2)}) collective-permute-start(f16[2,96,512]{2,1,0:T(8,128)(2,1)S(1)} %get-tuple-element.90), channel_id=1, source_target_pairs={{4,8},{6,10},{8,4},{10,6},{5,9},{7,11},{9,5},{11,7},{20,24},{22,26... | collective-permute-start | bytes 589832 | tf_op jit(solution)/shard_map/ppermute | solution.py:190
  254.1 15.0 %collective-permute-start.54 = (bf16[2,96,512]{2,1,0:T(8,128)(2,1)S(1)}, bf16[2,96,512]{2,1,0:T(8,128)(2,1)S(1)}, u32[]{:S(2)}, u32[]{:S(2)}) collective-permute-start(bf16[2,96,512]{2,1,0:T(8,128)(2,1)S(1)} %pad_maximum_fusion.17), channel_id=1, source_target_pairs={{4,8},{6,10},{8,4},{10,6},{5,9},{7,11},{9,5},{11,7},{20,24},{22,26... | collective-permute-start | bytes 589832 | tf_op jit(solution)/shard_map/ppermute | solution.py:190
  254.8 15.6 %collective-permute-start.53 = (bf16[2,96,512]{2,1,0:T(8,128)(2,1)S(1)}, bf16[2,96,512]{2,1,0:T(8,128)(2,1)S(1)}, u32[]{:S(2)}, u32[]{:S(2)}) collective-permute-start(bf16[2,96,512]{2,1,0:T(8,128)(2,1)S(1)} %pad_maximum_fusion.17), channel_id=1, source_target_pairs={{0,4},{2,6},{12,8},{14,10},{4,0},{6,2},{8,12},{10,14},{1,5},{3,7},... | collective-permute-start | bytes 589832 | tf_op jit(solution)/shard_map/ppermute | solution.py:190
  258.1 13.0 %collective-permute-start.52 = (bf16[48,3584]{1,0:T(8,128)(2,1)S(1)}, bf16[48,3584]{1,0:T(8,128)(2,1)S(1)}, u32[]{:S(2)}, u32[]{:S(2)}) collective-permute-start(bf16[48,3584]{1,0:T(8,128)(2,1)S(1)} %pad_maximum_fusion.13), channel_id=1, source_target_pairs={{0,1},{1,0},{2,3},{3,2},{4,5},{5,4},{6,7},{7,6},{8,9},{9,8},{10,11... | collective-permute-start | bytes 1032200 | tf_op jit(solution)/shard_map/ppermute | solution.py:255
  258.7 29.4 %collective-permute-start.64 = (bf16[4,2,96,1024]{3,2,1,0:T(8,128)(2,1)S(1)}, bf16[4,2,96,1024]{3,2,1,0:T(8,128)(2,1)S(1)}, u32[]{:S(2)}, u32[]{:S(2)}) collective-permute-start(bf16[4,2,96,1024]{3,2,1,0:T(8,128)(2,1)S(1)} %pad_maximum_fusion.3.own_ref), channel_id=1, source_target_pairs={{0,2},{2,0},{4,6},{6,4},{8,10},{10,8},{12,14},{14,12},{1,3},{3,1},... | collective-permute-start | bytes 4718600 | tf_op jit(solution)/shard_map/ppermute | solution.py:190
  269.1 8.1 %collective-permute-start.55 = (bf16[2,96,512]{2,1,0:T(8,128)(2,1)S(1)}, bf16[2,96,512]{2,1,0:T(8,128)(2,1)S(1)}, u32[]{:S(2)}, u32[]{:S(2)}) collective-permute-start(bf16[2,96,512]{2,1,0:T(8,128)(2,1)S(1)} %collective-permute-done.54), channel_id=1, source_target_pairs={{4,0},{6,2},{8,12},{10,14},{5,1},{7,3},{9,13},{11,15},{20,16},{22,... | collective-permute-start | bytes 589832 | tf_op jit(solution)/shard_map/ppermute | solution.py:190
  270.4 1.0 collective-permute-start.56
  271.3 12.8 %collective-permute-start.57 = (bf16[2,96,512]{2,1,0:T(8,128)(2,1)S(1)}, bf16[2,96,512]{2,1,0:T(8,128)(2,1)S(1)}, u32[]{:S(2)}, u32[]{:S(2)}) collective-permute-start(bf16[2,96,512]{2,1,0:T(8,128)(2,1)S(1)} %collective-permute-done.56), channel_id=1, source_target_pairs={{4,0},{6,2},{8,12},{10,14},{5,1},{7,3},{9,13},{11,15},{20,16},{22,... | collective-permute-start | bytes 589832 | tf_op jit(solution)/shard_map/ppermute | solution.py:190
  284.2 9.7 %collective-permute-start.58 = (bf16[4,2,96,512]{3,2,1,0:T(8,128)(2,1)S(1)}, bf16[4,2,96,512]{3,2,1,0:T(8,128)(2,1)S(1)}, u32[]{:S(2)}, u32[]{:S(2)}) collective-permute-start(bf16[4,2,96,512]{3,2,1,0:T(8,128)(2,1)S(1)} %pad_maximum_fusion.10.own_ref), channel_id=1, source_target_pairs={{0,2},{2,0},{4,6},{6,4},{8,10},{10,8},{12,14},{14,12},{1,3},{3,1},... | collective-permute-start | bytes 2359304 | tf_op jit(solution)/shard_map/ppermute | solution.py:190
  (14 other events, 136.7 us)

commit v4 on v0

--- a/solution.py
+++ b/solution.py
@@ -1,7 +1,280 @@
+import functools
+import math
+
 import jax
 import jax.numpy as jnp
 from jax import lax
+from jax.experimental import pallas as pl
+from jax.experimental.pallas import tpu as pltpu
 from jax.sharding import PartitionSpec as P
+
+WIRE = jnp.float16
+LARGEST_TOKEN, LARGEST_WEIGHT = 6.0, 0.0625
+VMEM_LIMIT = 48 * 2**20
+SHARES = (2, 3, 2)
+
+
+def forward_kernel(
+    scale, place_ref, mine_ref, theirs_ref, gate_ref, up_ref, gate_far_ref, up_far_ref, out_ref
+):
+    blocks, _, rows, width = out_ref.shape
+    for which, (near, far) in enumerate(((gate_ref, gate_far_ref), (up_ref, up_far_ref))):
+        product = jnp.dot(mine_ref[...], near[...], preferred_element_type=jnp.float32)
+        product += jnp.dot(theirs_ref[...], far[0], preferred_element_type=jnp.float32)
+        out_ref[:, which] = (scale * product).reshape(blocks, rows, width)
+
+
+def forward(place, mine, theirs, gate_weight, up_weight, far, start, tile, blocks, scale):
+    total, depth = mine.shape
+    width = far.shape[2]
+    rows = total // blocks
+    whole = pl.BlockSpec((total, depth), lambda j, place: (0, 0))
+    weight = pl.BlockSpec((depth, tile), lambda j, place: (0, place[0] + start // tile + j))
+    return pl.pallas_call(
+        functools.partial(forward_kernel, scale),
+        out_shape=jax.ShapeDtypeStruct((blocks, 2, rows, width), jnp.float32),
+        grid_spec=pltpu.PrefetchScalarGridSpec(
+            num_scalar_prefetch=1,
+            grid=(width // tile,),
+            in_specs=[
+                whole,
+                whole,
+                weight,
+                weight,
+                pl.BlockSpec((1, depth, tile), lambda j, place: (0, 0, j)),
+                pl.BlockSpec((1, depth, tile), lambda j, place: (1, 0, j)),
+            ],
+            out_specs=pl.BlockSpec((blocks, 2, rows, tile), lambda j, place: (0, 0, 0, j)),
+        ),
+        compiler_params=pltpu.CompilerParams(vmem_limit_bytes=VMEM_LIMIT),
+        cost_estimate=pl.CostEstimate(
+            flops=8 * total * depth * width,
+            bytes_accessed=8 * depth * width + 8 * total * width + 4 * total * depth,
+            transcendentals=0,
+        ),
+    )(place, mine, theirs, gate_weight, up_weight, far, far)
+
+
+def gradient_kernel(place_ref, features_ref, act_ref, *refs):
+    gate_ref, up_ref = refs[-2:]
+    blocks, _, _, rows, width = act_ref.shape
+    for which, out_ref in enumerate((gate_ref, up_ref)):
+        act = act_ref[:, 0, which].reshape(blocks * rows, width)
+        out_ref[...] = jnp.dot(features_ref[...], act, preferred_element_type=jnp.float32)
+
+
+def gradient(place, features, act, totals, columns, start, tile):
+    depth, total = features.shape
+    blocks, cores, _, rows, width = act.shape
+    act_spec = pl.BlockSpec((blocks, 1, 2, rows, tile), lambda i, j, place: (0, i, 0, 0, j))
+    out_spec = pl.BlockSpec((depth, tile), lambda i, j, place: (0, place[i] + start // tile + j))
+    out_shape = jax.ShapeDtypeStruct((depth, columns), jnp.float32)
+    in_specs = [pl.BlockSpec((depth, total), lambda i, j, place: (0, 0)), act_spec]
+    in_specs += [pl.BlockSpec(memory_space=pl.ANY)] * len(totals)
+    return pl.pallas_call(
+        gradient_kernel,
+        out_shape=(out_shape, out_shape),
+        grid_spec=pltpu.PrefetchScalarGridSpec(
+            num_scalar_prefetch=1,
+            grid=(cores, width // tile),
+            in_specs=in_specs,
+            out_specs=(out_spec, out_spec),
+        ),
+        input_output_aliases={3 + i: i for i in range(len(totals))},
+        compiler_params=pltpu.CompilerParams(vmem_limit_bytes=VMEM_LIMIT),
+        cost_estimate=pl.CostEstimate(
+            flops=4 * cores * total * depth * width,
+            bytes_accessed=cores * (8 * depth + 4 * total) * width + 2 * total * depth,
+            transcendentals=0,
+        ),
+    )(place, features, act, *totals)
+
+
+def tie(value, *after):
+    return lax.optimization_barrier((value, after))[0]
+
+
+def cut(units, shares):
+    edges = [round(units * sum(shares[:i]) / sum(shares)) for i in range(len(shares) + 1)]
+    return [(a, b - a) for a, b in zip(edges, edges[1:]) if b > a]
+
+
+def local(tokens, gate_weight, up_weight, grad_hidden):
+    line = 4
+    row, col, part = (lax.axis_index(name) for name in ("row", "col", "depth"))
+    place, core = col // 2, col % 2
+    slab = grad_hidden.shape[1]
+    rows = 2 * slab
+    depth, columns = gate_weight.shape
+    half = columns // 2
+    share = half // 2
+    tile = 256 if share % 256 == 0 else 128
+    largest = depth * 2 * line * LARGEST_TOKEN * LARGEST_WEIGHT
+    scale = 2.0 ** math.floor(math.log2(65504 / largest))
+
+    swap = [(0, 1), (1, 0)]
+    pairs = [(i, i ^ 1) for i in range(2 * line)]
+
+    def between(hops):
+        return [(2 * i + c, 2 * j + c) for i, j in hops for c in (0, 1)]
+
+    inward, outward = between([(0, 1), (3, 2)]), between([(1, 0), (2, 3)])
+    side, centre = inward + outward, between([(1, 2), (2, 1)])
+    at_end = (place == 0) | (place == line - 1)
+    at_far = 2 * place >= line
+
+    def send(value, route):
+        return lax.ppermute(value, "col", route)
+
+    def wide(value):
+        return value.astype(jnp.float32)
+
+    def add(*terms):
+        return functools.reduce(jnp.add, map(wide, terms))
+
+    def by(first, mine, theirs, axis):
+        return jnp.where(
+            first,
+            jnp.concatenate([mine, theirs], axis=axis),
+            jnp.concatenate([theirs, mine], axis=axis),
+        )
+
+    def columns_of(array, start, width):
+        return lax.dynamic_slice_in_dim(array, start, width, array.ndim - 1)
+
+    pieces = [(begin * tile, count * tile) for begin, count in cut(share // tile, SHARES)]
+    last = len(pieces) - 1
+
+    def exchange_weights(k, after):
+        start, width = pieces[k]
+        first = part * half + (1 - core) * share + start
+        chosen = [columns_of(weight, first, width) for weight in (gate_weight, up_weight)]
+        return send(tie(jnp.stack(chosen), after), pairs)
+
+    mine = tokens[0]
+    over_row = lax.ppermute(mine, "row", swap)
+    over_depth = lax.ppermute(mine, "depth", swap)
+    over_both = lax.ppermute(over_row, "depth", swap)
+    far_weights = [exchange_weights(0, ())]
+    features = [by(row == 0, mine, over_row, 1), by(row == 0, over_depth, over_both, 1)]
+    other_features = [send(value, pairs) for value in features]
+    for k in range(1, last + 1):
+        far_weights.append(exchange_weights(k, other_features))
+
+    def arrange(values):
+        values = jnp.stack([value.reshape(line, rows, depth) for value in values], axis=1)
+        return values, jnp.where(at_far, values[::-1], values)
+
+    in_place, by_distance = arrange(features)
+    mine_rows = by_distance.reshape(-1, depth)
+    their_rows = arrange(other_features)[1].reshape(-1, depth)
+
+    first_tile = ((part * half + core * share) // tile).astype(jnp.int32).reshape(1)
+
+    def multiply(k, after):
+        start, _ = pieces[k]
+        return forward(
+            first_tile,
+            tie(mine_rows, after),
+            their_rows,
+            gate_weight,
+            up_weight,
+            far_weights[k],
+            start,
+            tile,
+            line,
+            scale,
+        )
+
+    terms = multiply(0, ())
+    in_1 = send(terms[3].astype(WIRE), inward)
+
+    mine_cotangent, cotangent = tie((grad_hidden[0], grad_hidden[0]), terms)
+    cotangent = jnp.stack(
+        [
+            columns_of(mine_cotangent, part * half, half),
+            lax.ppermute(columns_of(cotangent, (1 - part) * half, half), "depth", swap),
+        ]
+    )
+    cotangent = by(
+        core == 0,
+        columns_of(cotangent, core * share, share),
+        send(columns_of(cotangent, (1 - core) * share, share), pairs),
+        1,
+    )
+
+    in_place, by_distance = tie((in_place, by_distance), terms)
+    turned = by_distance.reshape(-1, depth).T
+    turned_in_place = in_place.reshape(-1, depth).T
+
+    def activate(k, summed):
+        start, width = pieces[k]
+        summed = (summed * (1.0 / scale)).reshape(2, 2, rows, width)
+        gate_sum, up_sum = summed[0], summed[1]
+        squash = jax.nn.sigmoid(gate_sum)
+        hidden.append((gate_sum * squash * up_sum).astype(jnp.bfloat16))
+        given = wide(cotangent[:, :, start : start + width])
+        gate_act = given * up_sum * squash * (1.0 + gate_sum * (1.0 - squash))
+        up_act = given * gate_sum * squash
+        act = jnp.stack([gate_act, up_act]).astype(jnp.bfloat16)
+        return act.reshape(2, 2 * rows, width)
+
+    def finish(k, gathered, totals):
+        start, _ = pieces[k]
+        for value, owner in ((gathered, core), (send(gathered, pairs), 1 - core)):
+            where = (owner * (share // tile)).astype(jnp.int32).reshape(1)
+            totals = gradient(where, turned, value[:, None], totals, half, start, tile)
+        return totals
+
+    hidden, totals = [], ()
+    act = gathered = None
+    for k in range(-1, last):
+        if act is not None:
+            side_1, centre_1 = send(act, side), send(act, centre)
+        if gathered is not None:
+            totals = finish(k - 1, gathered, totals)
+            terms = tie(terms, totals)
+        far = add(terms[3], in_1).astype(WIRE)
+        centre_2 = send(far, centre)
+        in_2 = send(tie(terms[2], in_1).astype(WIRE), inward)
+        if act is not None:
+            out_2, share_2 = send(centre_1, outward), send(side_1, centre)
+        following = None
+        if k + 2 <= last:
+            following = multiply(k + 2, (in_1,))
+            terms = tie(terms, following)
+        near = add(terms[2], in_2).astype(WIRE)
+        swapped = jnp.where(at_end, terms[1], add(terms[0], centre_2)).astype(WIRE)
+        centre_3, side_3 = send(near, centre), send(swapped, side)
+        if following is not None:
+            in_1 = send(tie(following[3], near, swapped).astype(WIRE), inward)
+        if act is not None:
+            out_3 = send(share_2, outward)
+            gathered = jnp.stack(
+                [
+                    jnp.where(at_end, act, side_1),
+                    jnp.where(at_end, side_1, act),
+                    jnp.where(at_end, out_2, centre_1),
+                    jnp.where(at_end, out_3, share_2),
+                ]
+            )
+        own = jnp.where(at_end, terms[0], terms[1])
+        act = activate(k + 1, add(own, side_3, centre_3))
+        terms = following
+
+    everything = lax.all_gather(act, "col", axis=0).reshape(line, 2, *act.shape)
+    if gathered is not None:
+        totals = finish(last - 1, gathered, totals)
+    start, _ = pieces[last]
+    both_cores = jnp.array([0, share // tile], jnp.int32)
+    totals = gradient(both_cores, turned_in_place, everything, totals, half, start, tile)
+
+    hidden = jnp.concatenate(hidden, axis=2).reshape(2, 2, slab, share)
+    mine = lax.dynamic_index_in_dim(hidden, core, 1, keepdims=False)
+    theirs = lax.dynamic_index_in_dim(hidden, 1 - core, 1, keepdims=False)
+    hidden = by(core == 0, mine, send(theirs, pairs), 2)
+    hidden = by(part == 0, hidden[0], lax.ppermute(hidden[1], "depth", swap), 1)
+    return (hidden[None], *totals)
 
 
 def contract(picked, piece):
@@ -10,7 +283,7 @@
     )
 
 
-def local(tokens, gate_weight, up_weight, grad_hidden):
+def local_any(tokens, gate_weight, up_weight, grad_hidden):
     features = lax.all_gather(tokens[0], "row", axis=1, tiled=True)
     columns = gate_weight.shape[1]
     picked = features
@@ -46,4 +319,11 @@
         P("depth", "col", "row"),
     )
     out_specs = (P("depth", "col", "row"), P("col", ("row", "depth")), P("col", ("row", "depth")))
-    return jax.shard_map(local, mesh=mesh, in_specs=in_specs, out_specs=out_specs, check_vma=False)
+    sizes = tuple(mesh.shape[name] for name in ("row", "col", "depth"))
+    return jax.shard_map(
+        local if sizes == (2, 8, 2) else local_any,
+        mesh=mesh,
+        in_specs=in_specs,
+        out_specs=out_specs,
+        check_vma=False,
+    )

time: 1060 us -> 307 us (0.29)
  waiting for transfers between devices: 939 us -> 97.3 us
  starting transfers between devices: 0.38 us -> 91 us
  matrix products: 51.8 us -> 0 us
  Pallas kernels: 0 us -> 46.7 us
  other arithmetic: 11.4 us -> 33.3 us
  blocking collectives: 11.8 us -> 0 us
    reduce_scatter x3 -> x0, waiting for transfers between devices: 837 us -> none  [the longest x1 312 us: local(): lax.psum_scatter(up_total, 'depth', scatter_dimension=1, tiled=True)]
    all_gather x2 -> x1, waiting for transfers between devices: 101 us -> 0.01 us  [local(): everything = lax.all_gather(act, 'col', axis=0).reshape(line, 2, *act.shape)]
    ppermute x0 -> x39, waiting for transfers between devices: none -> 97.2 us  [the longest x34 84.1 us: send(): return lax.ppermute(value, 'col', route)]
    ppermute x0 -> x39, starting transfers between devices: none -> 90.9 us  [the longest x34 85.2 us: send(): return lax.ppermute(value, 'col', route)]
    dot_general x4 -> x0, matrix products: 51.8 us -> none  [the longest x2 33.5 us: contract(): lax.dot_general(picked, piece, (((0,), (0,)), ((), ())), preferred_elemen...]
    pallas_call x0 -> x8, Pallas kernels: none -> 46.7 us  [the longest x5 25.3 us: gradient(): pl.pallas_call(gradient_kernel, out_shape=(out_shape, out_shape), grid_sp...]
    unnamed x4 -> x66, local copies, waits for them, and re-layouts: 29.1 us -> 10.4 us
    all_gather x1 -> x0, blocking collectives: 11.8 us -> none  [local(): features = lax.all_gather(tokens[0], 'row', axis=1, tiled=True)]
  transfers between devices with their start and end apart: 5 -> 40, of which waited for: 5 -> 14; matrix products, arithmetic and copies ran while one was open for 5% -> 14% of each run, Pallas kernels for 0% -> 13%
where the time goes in v4:
time: 307 us; the launch traced here: 305 us
  waiting for transfers between devices  97.3 us (32%)
  starting transfers between devices  91 us (30%)
  Pallas kernels  46.7 us (15%)
  other arithmetic  33.3 us (11%)
  local copies, waits for them, and re-layouts  21.8 us (7%)
  between operations  15 us (5%)
    ppermute x34, starting transfers between devices, send(): return lax.ppermute(value, 'col', route)  85.2 us
    ppermute x34, waiting for transfers between devices, send(): return lax.ppermute(value, 'col', route)  84.1 us
    pallas_call x5, Pallas kernels, gradient(): pl.pallas_call(gradient_kernel, out_shape=(out_shape, out_shape), grid_sp...  25.3 us
    pallas_call x3, Pallas kernels, forward(): pl.pallas_call(functools.partial(forward_kernel, scale), out_shape=jax.Sh...  21.5 us
    select_n x7, other arithmetic, by(): jnp.where(first, jnp.concatenate([mine, theirs], axis=axis), jnp.concaten...  10.5 us
    unnamed x66, local copies, waits for them, and re-layouts  10.4 us
    ppermute x1, waiting for transfers between devices, local(): over_row = lax.ppermute(mine, 'row', swap)  7.92 us
  transfers between devices with their start and end apart: 40, of which 14 were waited for; matrix products, arithmetic and copies ran while one was open for 14% of the time, Pallas kernels for 13%

profile of v4, /device:TPU:1, one launch (start us, length us, event | category | flops | bytes accessed | tf_op | source)
XLA Modules:
  0.0 305.1 jit_solution(2614179697932574838)
XLA Ops:
  7.2 2.1 collective-permute-start
  10.6 7.9 %collective-permute-done = bf16[384,512]{1,0:T(8,128)(2,1)} collective-permute-done((bf16[384,512]{1,0:T(8,128)(2,1)}, bf16[384,512]{1,0:T(8,128)(2,1)}, u32[]{:S(2)}, u32[]{:S(2)}) %collective-permute-start) | collective-permute-done | bytes 393248 | tf_op jit(solution)/shard_map/ppermute | solution.py:155
  19.7 3.5 %dynamic-slice_bitcast_fusion.2 = (bf16[1,1024,512]{2,1,0:T(8,128)(2,1)S(1)}, bf16[1,1024,512]{2,1,0:T(8,128)(2,1)S(1)}, bf16[1,1024,512]{2,1,0:T(8,128)(2,1)S(1)}, bf16[1,1024,512]{2,1,0:T(8,128)(2,1)}) fusion(bf16[1024,7168]{1,0:T(8,128)(2,1)} %up_ref.5, s32[]{:T(128)S(6)} %select_n.208, s32[]{:T(128)S(6)} %select_n.203, bf16[1024,7168]{1,0:T(8,128)(2,1)} %gate_ref.5), kind=kLoop, calls=%fused_computation.23 | loop fusion | bytes 8388616 | tf_op jit(solution)/shard_map/stack | solution.py:152
  23.2 1.5 pad_maximum_fusion.2
  24.7 1.8 collective-permute-start.5
  26.5 1.3 maximum_select_fusion.2
  28.2 2.5 maximum_select_fusion.3
  30.7 2.2 collective-permute-start.4
  32.8 2.1 dynamic-slice_bitcast_fusion
  35.5 1.3 maximum_select_fusion
  36.8 1.6 maximum_select_fusion.1
  39.8 1.5 pad_maximum_fusion.5
  41.8 6.9 %shard_map.76 = f32[4,2,192,512]{3,2,1,0:T(8,128)} custom-call(s32[1]{0:T(128)} %bitcast.place_ref, bf16[768,1024]{1,0:T(8,128)(2,1)S(1)} %bitcast.166, bf16[768,1024]{1,0:T(8,128)(2,1)S(1)} %bitcast.174, bf16[1024,7168]{1,0:T(8,128)(2,1)} %gate_ref.5, bf16[1024,7168]{1,0:T(8,128)(2,1)} %up_ref.5, ...), custom_call_target="tpu_custom_call" | custom-call | flops 3221225472 | bytes 10485760 | tf_op jit(solution)/shard_map/pallas_call | solution.py:33
  50.0 1.5 slice_bitcast_fusion.3
  51.5 3.5 %collective-permute-start.6 = (f16[2,192,512]{2,1,0:T(8,128)(2,1)S(1)}, f16[2,192,512]{2,1,0:T(8,128)(2,1)S(1)}, u32[]{:S(2)}, u32[]{:S(2)}) collective-permute-start(f16[2,192,512]{2,1,0:T(8,128)(2,1)S(1)} %get-tuple-element.68), channel_id=1, source_target_pairs={{0,4},{2,6},{12,8},{14,10},{1,5},{3,7},{13,9},{15,11},{16,20},{18,... | collective-permute-start | bytes 1179656 | tf_op jit(solution)/shard_map/ppermute | solution.py:127
  55.0 3.1 %collective-permute-done.18 = bf16[48,3584]{1,0:T(8,128)(2,1)S(1)} collective-permute-done((bf16[48,3584]{1,0:T(8,128)(2,1)S(1)}, bf16[48,3584]{1,0:T(8,128)(2,1)S(1)}, u32[]{:S(2)}, u32[]{:S(2)}) %collective-permute-start.18) | collective-permute-done | bytes 344096 | tf_op jit(solution)/shard_map/ppermute | solution.py:196
  60.2 2.6 collective-permute-done.6
  63.7 6.6 %collective-permute-start.10 = (f16[2,192,512]{2,1,0:T(8,128)(2,1)S(1)}, f16[2,192,512]{2,1,0:T(8,128)(2,1)S(1)}, u32[]{:S(2)}, u32[]{:S(2)}) collective-permute-start(f16[2,192,512]{2,1,0:T(8,128)(2,1)S(1)} %convert_element_type.129), channel_id=1, source_target_pairs={{0,4},{2,6},{12,8},{14,10},{1,5},{3,7},{13,9},{15,11},{16,20},{18,... | collective-permute-start | bytes 1179656 | tf_op jit(solution)/shard_map/ppermute | solution.py:127
  70.3 1.7 copy-done.12
  72.0 8.5 %shard_map.77 = f32[4,2,192,768]{3,2,1,0:T(8,128)} custom-call(s32[1]{0:T(128)} %bitcast.place_ref, bf16[768,1024]{1,0:T(8,128)(2,1)S(1)} %bitcast.167, bf16[768,1024]{1,0:T(8,128)(2,1)S(1)} %bitcast.175, bf16[1024,7168]{1,0:T(8,128)(2,1)} %gate_ref.5, bf16[1024,7168]{1,0:T(8,128)(2,1)} %up_ref.5, bf16[2,1024,768]{2,1,0:T(8,128)(2,1)} %copy-done.12, ...), custom_call_target="tpu_custom_call" | custom-call | flops 4831838208 | bytes 14155776 | tf_op jit(solution)/shard_map/pallas_call | solution.py:33
  80.5 1.3 fusion.14
  81.8 1.4 collective-permute-start.11
  83.2 1.5 maximum_select_fusion.4
  84.7 6.0 %collective-permute-done.9 = f16[2,192,512]{2,1,0:T(8,128)(2,1)} collective-permute-done((f16[2,192,512]{2,1,0:T(8,128)(2,1)}, f16[2,192,512]{2,1,0:T(8,128)(2,1)}, u32[]{:S(2)}, u32[]{:S(2)}) %collective-permute-start.9) | collective-permute-done | bytes 393248 | tf_op jit(solution)/shard_map/ppermute | solution.py:127
  90.7 1.9 fusion.13
  93.6 3.1 %collective-permute-start.20 = (bf16[2,192,512]{2,1,0:T(8,128)(2,1)S(1)}, bf16[2,192,512]{2,1,0:T(8,128)(2,1)S(1)}, u32[]{:S(2)}, u32[]{:S(2)}) collective-permute-start(bf16[2,192,512]{2,1,0:T(8,128)(2,1)S(1)} %pad_maximum_fusion.9), channel_id=1, source_target_pairs={{0,4},{2,6},{12,8},{14,10},{4,0},{6,2},{8,12},{10,14},{1,5},{3,7},... | collective-permute-start | bytes 1179656 | tf_op jit(solution)/shard_map/ppermute | solution.py:127
  96.9 3.6 %collective-permute-start.13 = (bf16[2,1024,512]{2,1,0:T(8,128)(2,1)S(1)}, bf16[2,1024,512]{2,1,0:T(8,128)(2,1)S(1)}, u32[]{:S(2)}, u32[]{:S(2)}) collective-permute-start(bf16[2,1024,512]{2,1,0:T(8,128)(2,1)S(1)} %pad_maximum_fusion.3), channel_id=1, source_target_pairs={{0,2},{2,0},{4,6},{6,4},{8,10},{10,8},{12,14},{14,12},{1,3},{3,1},... | collective-permute-start | bytes 6291464 | tf_op jit(solution)/shard_map/ppermute | solution.py:127
  101.2 1.7 collective-permute-done.20
  103.6 1.3 collective-permute-start.22
  105.2 11.6 %collective-permute-start.12 = (f16[2,192,768]{2,1,0:T(8,128)(2,1)S(1)}, f16[2,192,768]{2,1,0:T(8,128)(2,1)S(1)}, u32[]{:S(2)}, u32[]{:S(2)}) collective-permute-start(f16[2,192,768]{2,1,0:T(8,128)(2,1)S(1)} %convert_element_type.134), channel_id=1, source_target_pairs={{0,4},{2,6},{12,8},{14,10},{1,5},{3,7},{13,9},{15,11},{16,20},{18,... | collective-permute-start | bytes 1769480 | tf_op jit(solution)/shard_map/ppermute | solution.py:127
  116.7 1.3 collective-permute-start.24
  118.1 4.6 %collective-permute-done.22 = bf16[2,192,512]{2,1,0:T(8,128)(2,1)S(1)} collective-permute-done((bf16[2,192,512]{2,1,0:T(8,128)(2,1)S(1)}, bf16[2,192,512]{2,1,0:T(8,128)(2,1)S(1)}, u32[]{:S(2)}, u32[]{:S(2)}) %collective-permute-start.22) | collective-permute-done | bytes 393248 | tf_op jit(solution)/shard_map/ppermute | solution.py:127
  122.8 8.8 %collective-permute-done.24 = bf16[2,192,512]{2,1,0:T(8,128)(2,1)S(1)} collective-permute-done((bf16[2,192,512]{2,1,0:T(8,128)(2,1)S(1)}, bf16[2,192,512]{2,1,0:T(8,128)(2,1)S(1)}, u32[]{:S(2)}, u32[]{:S(2)}) %collective-permute-start.24) | collective-permute-done | bytes 393248 | tf_op jit(solution)/shard_map/ppermute | solution.py:127
  131.6 1.9 fusion.33
  133.6 1.4 collective-permute-start.25
  136.0 2.8 collective-permute-start.16
  138.8 6.1 %shard_map.78 = f32[4,2,192,512]{3,2,1,0:T(8,128)} custom-call(s32[1]{0:T(128)} %bitcast.place_ref, bf16[768,1024]{1,0:T(8,128)(2,1)S(1)} %bitcast.168, bf16[768,1024]{1,0:T(8,128)(2,1)S(1)} %bitcast.176, bf16[1024,7168]{1,0:T(8,128)(2,1)} %gate_ref.5, bf16[1024,7168]{1,0:T(8,128)(2,1)} %up_ref.5, ...), custom_call_target="tpu_custom_call" | custom-call | flops 3221225472 | bytes 10485760 | tf_op jit(solution)/shard_map/pallas_call | solution.py:33
  146.2 4.9 %collective-permute-done.16 = f16[2,192,768]{2,1,0:T(8,128)(2,1)S(1)} collective-permute-done((f16[2,192,768]{2,1,0:T(8,128)(2,1)S(1)}, f16[2,192,768]{2,1,0:T(8,128)(2,1)S(1)}, u32[]{:S(2)}, u32[]{:S(2)}) %collective-permute-start.16) | collective-permute-done | bytes 589856 | tf_op jit(solution)/shard_map/ppermute | solution.py:127
  152.3 4.9 %collective-permute-start.26 = (f16[2,192,512]{2,1,0:T(8,128)(2,1)}, f16[2,192,512]{2,1,0:T(8,128)(2,1)}, u32[]{:S(2)}, u32[]{:S(2)}) collective-permute-start(f16[2,192,512]{2,1,0:T(8,128)(2,1)} %convert_element_type.146), channel_id=1, source_target_pairs={{0,4},{2,6},{12,8},{14,10},{1,5},{3,7},{13,9},{15,11},{16,20},{18,... | collective-permute-start | bytes 1179656 | tf_op jit(solution)/shard_map/ppermute | solution.py:127
  157.1 1.6 copy.34
  159.4 1.4 copy-done.2
  160.8 1.4 copy-done.8
  162.3 3.4 %shard_map.79 = (f32[1024,3584]{1,0:T(8,128)}, f32[1024,3584]{1,0:T(8,128)}) custom-call(s32[1]{0:T(128)} %bitcast.45.place_ref, bf16[1024,768]{1,0:T(8,128)(2,1)S(1)} %bitcast.170, bf16[4,1,2,192,512]{4,3,2,1,0:T(8,128)(2,1)S(1)} %copy-done.8), custom_call_target="tpu_custom_call" | custom-call | flops 1610612736 | bytes 7340032 | tf_op jit(solution)/shard_map/pallas_call | solution.py:74
  165.7 4.6 %shard_map.80 = (f32[1024,3584]{1,0:T(8,128)}, f32[1024,3584]{1,0:T(8,128)}) custom-call(s32[1]{0:T(128)} %bitcast.30.place_ref, bf16[1024,768]{1,0:T(8,128)(2,1)S(1)} %bitcast.171, bf16[4,1,2,192,512]{4,3,2,1,0:T(8,128)(2,1)} %bitcast.44.act_ref, f32[1024,3584]{1,0:T(8,128)} %get-tuple-element.41.refs_0_, ...), custom_call_target="tpu_custom_call", output_to_operand_aliasing={{0}: (3, {}), {1}: (4, {})} | custom-call | flops 1610612736 | bytes 7340032 | tf_op jit(solution)/shard_map/pallas_call | solution.py:74
  172.3 7.3 %collective-permute-start.29 = (f16[2,192,512]{2,1,0:T(8,128)(2,1)S(1)}, f16[2,192,512]{2,1,0:T(8,128)(2,1)S(1)}, u32[]{:S(2)}, u32[]{:S(2)}) collective-permute-start(f16[2,192,512]{2,1,0:T(8,128)(2,1)S(1)} %convert_element_type.152), channel_id=1, source_target_pairs={{0,4},{2,6},{12,8},{14,10},{1,5},{3,7},{13,9},{15,11},{16,20},{18,... | collective-permute-start | bytes 1179656 | tf_op jit(solution)/shard_map/ppermute | solution.py:127
  180.1 5.7 %collective-permute-done.29 = f16[2,192,512]{2,1,0:T(8,128)(2,1)S(1)} collective-permute-done((f16[2,192,512]{2,1,0:T(8,128)(2,1)S(1)}, f16[2,192,512]{2,1,0:T(8,128)(2,1)S(1)}, u32[]{:S(2)}, u32[]{:S(2)}) %collective-permute-start.29) | collective-permute-done | bytes 393248 | tf_op jit(solution)/shard_map/ppermute | solution.py:127
  186.2 2.3 collective-permute-start.28
  190.4 1.5 collective-permute-start.34
  191.9 3.2 %collective-permute-start.33 = (bf16[2,192,768]{2,1,0:T(8,128)(2,1)}, bf16[2,192,768]{2,1,0:T(8,128)(2,1)}, u32[]{:S(2)}, u32[]{:S(2)}) collective-permute-start(bf16[2,192,768]{2,1,0:T(8,128)(2,1)} %pad_maximum_fusion.8), channel_id=1, source_target_pairs={{0,4},{2,6},{12,8},{14,10},{4,0},{6,2},{8,12},{10,14},{1,5},{3,7},... | collective-permute-start | bytes 1769480 | tf_op jit(solution)/shard_map/ppermute | solution.py:127
  197.3 1.4 collective-permute-start.35
  198.7 9.7 %collective-permute-done.33 = bf16[2,192,768]{2,1,0:T(8,128)(2,1)} collective-permute-done((bf16[2,192,768]{2,1,0:T(8,128)(2,1)}, bf16[2,192,768]{2,1,0:T(8,128)(2,1)}, u32[]{:S(2)}, u32[]{:S(2)}) %collective-permute-start.33) | collective-permute-done | bytes 589856 | tf_op jit(solution)/shard_map/ppermute | solution.py:127
  212.0 23.9 %collective-permute-done.35 = bf16[2,192,768]{2,1,0:T(8,128)(2,1)S(1)} collective-permute-done((bf16[2,192,768]{2,1,0:T(8,128)(2,1)}, bf16[2,192,768]{2,1,0:T(8,128)(2,1)S(1)}, u32[]{:S(2)}, u32[]{:S(2)}) %collective-permute-start.35) | collective-permute-done | bytes 589856 | tf_op jit(solution)/shard_map/ppermute | solution.py:127
  236.3 12.8 %collective-permute-start.31 = (bf16[2,48,1792]{2,1,0:T(8,128)(2,1)S(1)}, bf16[2,48,1792]{2,1,0:T(8,128)(2,1)S(1)}, u32[]{:S(2)}, u32[]{:S(2)}) collective-permute-start(bf16[2,48,1792]{2,1,0:T(8,128)(2,1)S(1)} %get-tuple-element.92), channel_id=1, source_target_pairs={{0,2},{2,0},{4,6},{6,4},{8,10},{10,8},{12,14},{14,12},{1,3},{3,1},... | collective-permute-start | bytes 1032200 | tf_op jit(solution)/shard_map/ppermute | solution.py:127
  249.1 16.2 %collective-permute-done.37 = bf16[2,192,768]{2,1,0:T(8,128)(2,1)S(1)} collective-permute-done((bf16[2,192,768]{2,1,0:T(8,128)(2,1)S(1)}, bf16[2,192,768]{2,1,0:T(8,128)(2,1)S(1)}, u32[]{:S(2)}, u32[]{:S(2)}) %collective-permute-start.37) | collective-permute-done | bytes 589856 | tf_op jit(solution)/shard_map/ppermute | solution.py:127
  265.4 2.4 fusion.34
  267.8 3.0 collective-permute-start.38
  271.7 1.7 copy.36
  273.4 1.7 copy-done.6
  275.1 4.7 %shard_map.81 = (f32[1024,3584]{1,0:T(8,128)}, f32[1024,3584]{1,0:T(8,128)}) custom-call(s32[1]{0:T(128)} %bitcast.45.place_ref, bf16[1024,768]{1,0:T(8,128)(2,1)S(1)} %bitcast.172, bf16[4,1,2,192,768]{4,3,2,1,0:T(8,128)(2,1)S(1)} %copy-done.6, f32[1024,3584]{1,0:T(8,128)} %get-tuple-element.43.refs_0_, ...), custom_call_target="tpu_custom_call", output_to_operand_aliasing={{0}: (3, {}), {1}: (4, {})} | custom-call | flops 2415919104 | bytes 10223616 | tf_op jit(solution)/shard_map/pallas_call | solution.py:74
  279.8 1.9 collective-permute-done.32
  281.7 2.1 maximum_select_fusion.6
  283.8 6.2 %shard_map.82 = (f32[1024,3584]{1,0:T(8,128)}, f32[1024,3584]{1,0:T(8,128)}) custom-call(s32[1]{0:T(128)} %bitcast.30.place_ref, bf16[1024,768]{1,0:T(8,128)(2,1)S(1)} %bitcast.173, bf16[4,1,2,192,768]{4,3,2,1,0:T(8,128)(2,1)} %bitcast.74.act_ref, f32[1024,3584]{1,0:T(8,128)} %get-tuple-element.49.refs_0_, ...), custom_call_target="tpu_custom_call", output_to_operand_aliasing={{0}: (3, {}), {1}: (4, {})} | custom-call | flops 2415919104 | bytes 10223616 | tf_op jit(solution)/shard_map/pallas_call | solution.py:74
  290.0 1.9 copy-done.7
  291.9 6.3 %shard_map.83 = (f32[1024,3584]{1,0:T(8,128)}, f32[1024,3584]{1,0:T(8,128)}) custom-call(s32[2]{0:T(128)S(1)} %iota_multiply_fusion.place_ref, bf16[1024,768]{1,0:T(8,128)(2,1)S(1)} %bitcast.177, bf16[4,2,2,192,512]{4,3,2,1,0:T(8,128)(2,1)S(1)} %bitcast.178, f32[1024,3584]{1,0:T(8,128)} %get-tuple-element.51.refs_0_, ...), custom_call_target="tpu_custom_call", output_to_operand_aliasing={{0}: (3, {}), {1}: (4, {})} | custom-call | flops 3221225472 | bytes 13107200 | tf_op jit(solution)/shard_map/pallas_call | solution.py:74
  (156 shorter events, 28.1 us)
Async XLA Ops:
  7.2 41.5 %copy-start = (bf16[1,48,7168]{2,1,0:T(8,128)(2,1)S(1)}, bf16[1,48,7168]{2,1,0:T(8,128)(2,1)}, u32[]{:S(2)}) copy-start(bf16[1,48,7168]{2,1,0:T(8,128)(2,1)} %param.8) | copy-start | bytes 2064388
  7.2 282.8 %all-gather.2.cloned.1.call-start = ((), (), s32[]{:S(2)}) async-start(), calls=%async_computation | async-start | bytes 3538944 | tf_op jit(solution)/shard_map/all_gather | solution.py:265
  7.2 11.3 %collective-permute-start = (bf16[384,512]{1,0:T(8,128)(2,1)}, bf16[384,512]{1,0:T(8,128)(2,1)}, u32[]{:S(2)}, u32[]{:S(2)}) collective-permute-start(bf16[384,512]{1,0:T(8,128)(2,1)} %bitcast.204), channel_id=1, source_target_pairs={{0,16},{16,0},{1,17},{17,1},{2,18},{18,2},{3,19},{19,3},{4,20},{20... | collective-permute-start | bytes 1179656 | tf_op jit(solution)/shard_map/ppermute | solution.py:155
  9.3 18.6 %collective-permute-start.1 = (bf16[384,512]{1,0:T(8,128)(2,1)}, bf16[384,512]{1,0:T(8,128)(2,1)}, u32[]{:S(2)}, u32[]{:S(2)}) collective-permute-start(bf16[384,512]{1,0:T(8,128)(2,1)} %bitcast.205), channel_id=1, source_target_pairs={{0,1},{1,0},{2,3},{3,2},{4,5},{5,4},{6,7},{7,6},{8,9},{9,8},{10,11... | collective-permute-start | bytes 1179656 | tf_op jit(solution)/shard_map/ppermute | solution.py:156
  18.5 9.7 %collective-permute-start.2 = (bf16[384,512]{1,0:T(8,128)(2,1)}, bf16[384,512]{1,0:T(8,128)(2,1)}, u32[]{:S(2)}, u32[]{:S(2)}) collective-permute-start(bf16[384,512]{1,0:T(8,128)(2,1)} %collective-permute-done), channel_id=1, source_target_pairs={{0,1},{1,0},{2,3},{3,2},{4,5},{5,4},{6,7},{7,6},{8,9},{9,8},{10,11... | collective-permute-start | bytes 1179656 | tf_op jit(solution)/shard_map/ppermute | solution.py:157
  23.2 3.3 %copy-start.28 = (bf16[1,384,512]{2,1,0:T(8,128)(2,1)S(1)}, bf16[1,384,512]{2,1,0:T(8,128)(2,1)}, u32[]{:S(2)}) copy-start(bf16[1,384,512]{2,1,0:T(8,128)(2,1)} %param.5) | copy-start | bytes 1179652
  24.7 17.1 %collective-permute-start.5 = (bf16[2,1024,512]{2,1,0:T(8,128)(2,1)}, bf16[2,1024,512]{2,1,0:T(8,128)(2,1)}, u32[]{:S(2)}, u32[]{:S(2)}) collective-permute-start(bf16[2,1024,512]{2,1,0:T(8,128)(2,1)} %pad_maximum_fusion.2), channel_id=1, source_target_pairs={{0,2},{2,0},{4,6},{6,4},{8,10},{10,8},{12,14},{14,12},{1,3},{3,1},... | collective-permute-start | bytes 6291464 | tf_op jit(solution)/shard_map/ppermute | solution.py:127
  27.9 7.3 %collective-permute-start.3 = (bf16[384,1024]{1,0:T(8,128)(2,1)S(1)}, bf16[384,1024]{1,0:T(8,128)(2,1)}, u32[]{:S(2)}, u32[]{:S(2)}) collective-permute-start(bf16[384,1024]{1,0:T(8,128)(2,1)S(1)} %maximum_select_fusion.2), channel_id=1, source_target_pairs={{0,2},{2,0},{4,6},{6,4},{8,10},{10,8},{12,14},{14,12},{1,3},{3,1},... | collective-permute-start | bytes 2359304 | tf_op jit(solution)/shard_map/ppermute | solution.py:127
  30.7 4.6 %collective-permute-start.4 = (bf16[384,1024]{1,0:T(8,128)(2,1)}, bf16[384,1024]{1,0:T(8,128)(2,1)}, u32[]{:S(2)}, u32[]{:S(2)}) collective-permute-start(bf16[384,1024]{1,0:T(8,128)(2,1)} %maximum_select_fusion.3), channel_id=1, source_target_pairs={{0,2},{2,0},{4,6},{6,4},{8,10},{10,8},{12,14},{14,12},{1,3},{3,1},... | collective-permute-start | bytes 2359304 | tf_op jit(solution)/shard_map/ppermute | solution.py:127
  35.2 35.1 %collective-permute-start.7 = (bf16[2,1024,768]{2,1,0:T(8,128)(2,1)S(1)}, bf16[2,1024,768]{2,1,0:T(8,128)(2,1)S(1)}, u32[]{:S(2)}, u32[]{:S(2)}) collective-permute-start(bf16[2,1024,768]{2,1,0:T(8,128)(2,1)S(1)} %pad_maximum_fusion), channel_id=1, source_target_pairs={{0,2},{2,0},{4,6},{6,4},{8,10},{10,8},{12,14},{14,12},{1,3},{3,1},... | collective-permute-start | bytes 9437192 | tf_op jit(solution)/shard_map/ppermute | solution.py:127
  41.8 28.5 %copy-start.4 = (bf16[4,2,96,1024]{3,2,1,0:T(8,128)(2,1)}, bf16[4,2,96,1024]{3,2,1,0:T(8,128)(2,1)S(1)}, u32[]{:S(2)}) copy-start(bf16[4,2,96,1024]{3,2,1,0:T(8,128)(2,1)S(1)} %reverse_select_fusion) | copy-start | bytes 4718596
  48.7 9.4 %collective-permute-start.18 = (bf16[48,3584]{1,0:T(8,128)(2,1)S(1)}, bf16[48,3584]{1,0:T(8,128)(2,1)S(1)}, u32[]{:S(2)}, u32[]{:S(2)}) collective-permute-start(bf16[48,3584]{1,0:T(8,128)(2,1)S(1)} %constant_dynamic-slice_fusion), channel_id=1, source_target_pairs={{0,1},{1,0},{2,3},{3,2},{4,5},{5,4},{6,7},{7,6},{8,9},{9,8},{10,11... | collective-permute-start | bytes 1032200 | tf_op jit(solution)/shard_map/ppermute | solution.py:196
  51.5 11.3 %copy-start.10 = (f32[4,2,192,512]{3,2,1,0:T(8,128)S(1)}, f32[4,2,192,512]{3,2,1,0:T(8,128)}, u32[]{:S(2)}) copy-start(f32[4,2,192,512]{3,2,1,0:T(8,128)} %shard_map.76) | copy-start | bytes 9437188
  51.5 11.3 %collective-permute-start.6 = (f16[2,192,512]{2,1,0:T(8,128)(2,1)S(1)}, f16[2,192,512]{2,1,0:T(8,128)(2,1)S(1)}, u32[]{:S(2)}, u32[]{:S(2)}) collective-permute-start(f16[2,192,512]{2,1,0:T(8,128)(2,1)S(1)} %get-tuple-element.68), channel_id=1, source_target_pairs={{0,4},{2,6},{12,8},{14,10},{1,5},{3,7},{13,9},{15,11},{16,20},{18,... | collective-permute-start | bytes 1179656 | tf_op jit(solution)/shard_map/ppermute | solution.py:127
  59.0 24.2 %collective-permute-start.19 = (bf16[2,48,1792]{2,1,0:T(8,128)(2,1)}, bf16[2,48,1792]{2,1,0:T(8,128)(2,1)}, u32[]{:S(2)}, u32[]{:S(2)}) collective-permute-start(bf16[2,48,1792]{2,1,0:T(8,128)(2,1)} %get-tuple-element.94), channel_id=1, source_target_pairs={{0,2},{2,0},{4,6},{6,4},{8,10},{10,8},{12,14},{14,12},{1,3},{3,1},... | collective-permute-start | bytes 1032200 | tf_op jit(solution)/shard_map/ppermute | solution.py:127
  63.0 17.5 %collective-permute-start.8 = (f16[2,192,512]{2,1,0:T(8,128)(2,1)S(1)}, f16[2,192,512]{2,1,0:T(8,128)(2,1)S(1)}, u32[]{:S(2)}, u32[]{:S(2)}) collective-permute-start(f16[2,192,512]{2,1,0:T(8,128)(2,1)S(1)} %add_convert_fusion.2), channel_id=1, source_target_pairs={{4,8},{6,10},{8,4},{10,6},{5,9},{7,11},{9,5},{11,7},{20,24},{22,26... | collective-permute-start | bytes 1179656 | tf_op jit(solution)/shard_map/ppermute | solution.py:127
  63.7 16.8 %collective-permute-start.10 = (f16[2,192,512]{2,1,0:T(8,128)(2,1)S(1)}, f16[2,192,512]{2,1,0:T(8,128)(2,1)S(1)}, u32[]{:S(2)}, u32[]{:S(2)}) collective-permute-start(f16[2,192,512]{2,1,0:T(8,128)(2,1)S(1)} %convert_element_type.129), channel_id=1, source_target_pairs={{0,4},{2,6},{12,8},{14,10},{1,5},{3,7},{13,9},{15,11},{16,20},{18,... | collective-permute-start | bytes 1179656 | tf_op jit(solution)/shard_map/ppermute | solution.py:127
  80.5 24.4 %slice-start = ((s8[4718592]{0:T(1024)(128)(4,1)}), s8[524288]{0:T(1024)(128)(4,1)S(1)}, s32[]{:S(2)}) async-start(s8[4718592]{0:T(1024)(128)(4,1)} %bitcast.179), calls=%async_computation.1 | async-start | bytes 1048576
  81.8 8.9 %collective-permute-start.9 = (f16[2,192,512]{2,1,0:T(8,128)(2,1)}, f16[2,192,512]{2,1,0:T(8,128)(2,1)}, u32[]{:S(2)}, u32[]{:S(2)}) collective-permute-start(f16[2,192,512]{2,1,0:T(8,128)(2,1)} %get-tuple-element.65), channel_id=1, source_target_pairs={{0,4},{2,6},{12,8},{14,10},{4,0},{6,2},{8,12},{10,14},{1,5},{3,7},... | collective-permute-start | bytes 1179656 | tf_op jit(solution)/shard_map/ppermute | solution.py:127
  81.8 8.9 %collective-permute-start.11 = (f16[2,192,512]{2,1,0:T(8,128)(2,1)}, f16[2,192,512]{2,1,0:T(8,128)(2,1)}, u32[]{:S(2)}, u32[]{:S(2)}) collective-permute-start(f16[2,192,512]{2,1,0:T(8,128)(2,1)} %get-tuple-element.66), channel_id=1, source_target_pairs={{4,8},{6,10},{8,4},{10,6},{5,9},{7,11},{9,5},{11,7},{20,24},{22,26... | collective-permute-start | bytes 1179656 | tf_op jit(solution)/shard_map/ppermute | solution.py:127
  84.7 7.9 %copy-start.22 = (bf16[2,96,1792]{2,1,0:T(8,128)(2,1)}, bf16[2,96,1792]{2,1,0:T(8,128)(2,1)S(1)}, u32[]{:S(2)}) copy-start(bf16[2,96,1792]{2,1,0:T(8,128)(2,1)S(1)} %maximum_select_fusion.4) | copy-start | bytes 2064388
  84.7 20.2 %slice-start.1 = ((s8[4718592]{0:T(1024)(128)(4,1)}), s8[4194304]{0:T(1024)(128)(4,1)S(1)}, s32[]{:S(2)}) async-start(s8[4718592]{0:T(1024)(128)(4,1)} %bitcast.179), calls=%async_computation.2 | async-start | bytes 8388608
  92.5 4.2 %copy-start.13 = (bf16[1,1024,512]{2,1,0:T(8,128)(2,1)S(1)}, bf16[1,1024,512]{2,1,0:T(8,128)(2,1)}, u32[]{:S(2)}) copy-start(bf16[1,1024,512]{2,1,0:T(8,128)(2,1)} %get-tuple-element.96) | copy-start | bytes 3145732
  93.6 9.3 %collective-permute-start.20 = (bf16[2,192,512]{2,1,0:T(8,128)(2,1)S(1)}, bf16[2,192,512]{2,1,0:T(8,128)(2,1)S(1)}, u32[]{:S(2)}, u32[]{:S(2)}) collective-permute-start(bf16[2,192,512]{2,1,0:T(8,128)(2,1)S(1)} %pad_maximum_fusion.9), channel_id=1, source_target_pairs={{0,4},{2,6},{12,8},{14,10},{4,0},{6,2},{8,12},{10,14},{1,5},{3,7},... | collective-permute-start | bytes 1179656 | tf_op jit(solution)/shard_map/ppermute | solution.py:127
  96.9 41.9 %collective-permute-start.13 = (bf16[2,1024,512]{2,1,0:T(8,128)(2,1)S(1)}, bf16[2,1024,512]{2,1,0:T(8,128)(2,1)S(1)}, u32[]{:S(2)}, u32[]{:S(2)}) collective-permute-start(bf16[2,1024,512]{2,1,0:T(8,128)(2,1)S(1)} %pad_maximum_fusion.3), channel_id=1, source_target_pairs={{0,2},{2,0},{4,6},{6,4},{8,10},{10,8},{12,14},{14,12},{1,3},{3,1},... | collective-permute-start | bytes 6291464 | tf_op jit(solution)/shard_map/ppermute | solution.py:127
  100.6 3.0 collective-permute-start.21
  102.9 13.8 %collective-permute-start.23 = (bf16[2,192,512]{2,1,0:T(8,128)(2,1)S(1)}, bf16[2,192,512]{2,1,0:T(8,128)(2,1)S(1)}, u32[]{:S(2)}, u32[]{:S(2)}) collective-permute-start(bf16[2,192,512]{2,1,0:T(8,128)(2,1)S(1)} %collective-permute-done.20), channel_id=1, source_target_pairs={{4,8},{6,10},{8,4},{10,6},{5,9},{7,11},{9,5},{11,7},{20,24},{22,26... | collective-permute-start | bytes 1179656 | tf_op jit(solution)/shard_map/ppermute | solution.py:127
  103.6 19.1 %collective-permute-start.22 = (bf16[2,192,512]{2,1,0:T(8,128)(2,1)S(1)}, bf16[2,192,512]{2,1,0:T(8,128)(2,1)S(1)}, u32[]{:S(2)}, u32[]{:S(2)}) collective-permute-start(bf16[2,192,512]{2,1,0:T(8,128)(2,1)S(1)} %collective-permute-done.21), channel_id=1, source_target_pairs={{4,0},{6,2},{8,12},{10,14},{5,1},{7,3},{9,13},{11,15},{20,16},{22,... | collective-permute-start | bytes 1179656 | tf_op jit(solution)/shard_map/ppermute | solution.py:127
  105.2 29.8 %collective-permute-start.12 = (f16[2,192,768]{2,1,0:T(8,128)(2,1)S(1)}, f16[2,192,768]{2,1,0:T(8,128)(2,1)S(1)}, u32[]{:S(2)}, u32[]{:S(2)}) collective-permute-start(f16[2,192,768]{2,1,0:T(8,128)(2,1)S(1)} %convert_element_type.134), channel_id=1, source_target_pairs={{0,4},{2,6},{12,8},{14,10},{1,5},{3,7},{13,9},{15,11},{16,20},{18,... | collective-permute-start | bytes 1769480 | tf_op jit(solution)/shard_map/ppermute | solution.py:127
  116.7 14.9 %collective-permute-start.24 = (bf16[2,192,512]{2,1,0:T(8,128)(2,1)S(1)}, bf16[2,192,512]{2,1,0:T(8,128)(2,1)S(1)}, u32[]{:S(2)}, u32[]{:S(2)}) collective-permute-start(bf16[2,192,512]{2,1,0:T(8,128)(2,1)S(1)} %collective-permute-done.23), channel_id=1, source_target_pairs={{4,0},{6,2},{8,12},{10,14},{5,1},{7,3},{9,13},{11,15},{20,16},{22,... | collective-permute-start | bytes 1179656 | tf_op jit(solution)/shard_map/ppermute | solution.py:127
  133.6 32.1 %collective-permute-start.25 = (bf16[4,2,192,512]{3,2,1,0:T(8,128)(2,1)}, bf16[4,2,192,512]{3,2,1,0:T(8,128)(2,1)}, u32[]{:S(2)}, u32[]{:S(2)}) collective-permute-start(bf16[4,2,192,512]{3,2,1,0:T(8,128)(2,1)} %get-tuple-element.72), channel_id=1, source_target_pairs={{0,2},{2,0},{4,6},{6,4},{8,10},{10,8},{12,14},{14,12},{1,3},{3,1},... | collective-permute-start | bytes 4718600 | tf_op jit(solution)/shard_map/ppermute | solution.py:127
  135.0 3.8 %copy-start.5 = (bf16[4,2,96,1024]{3,2,1,0:T(8,128)(2,1)S(1)}, bf16[4,2,96,1024]{3,2,1,0:T(8,128)(2,1)}, u32[]{:S(2)}) copy-start(bf16[4,2,96,1024]{3,2,1,0:T(8,128)(2,1)} %copy-done.4) | copy-start | bytes 4718596
  135.2 10.9 %collective-permute-start.14 = (f16[2,192,768]{2,1,0:T(8,128)(2,1)S(1)}, f16[2,192,768]{2,1,0:T(8,128)(2,1)S(1)}, u32[]{:S(2)}, u32[]{:S(2)}) collective-permute-start(f16[2,192,768]{2,1,0:T(8,128)(2,1)S(1)} %add_convert_fusion), channel_id=1, source_target_pairs={{4,8},{6,10},{8,4},{10,6},{5,9},{7,11},{9,5},{11,7},{20,24},{22,26... | collective-permute-start | bytes 1769480 | tf_op jit(solution)/shard_map/ppermute | solution.py:127
  136.0 15.0 %collective-permute-start.16 = (f16[2,192,768]{2,1,0:T(8,128)(2,1)S(1)}, f16[2,192,768]{2,1,0:T(8,128)(2,1)S(1)}, u32[]{:S(2)}, u32[]{:S(2)}) collective-permute-start(f16[2,192,768]{2,1,0:T(8,128)(2,1)S(1)} %convert_element_type.140), channel_id=1, source_target_pairs={{0,4},{2,6},{12,8},{14,10},{1,5},{3,7},{13,9},{15,11},{16,20},{18,... | collective-permute-start | bytes 1769480 | tf_op jit(solution)/shard_map/ppermute | solution.py:127
  152.3 18.1 %collective-permute-start.26 = (f16[2,192,512]{2,1,0:T(8,128)(2,1)}, f16[2,192,512]{2,1,0:T(8,128)(2,1)}, u32[]{:S(2)}, u32[]{:S(2)}) collective-permute-start(f16[2,192,512]{2,1,0:T(8,128)(2,1)} %convert_element_type.146), channel_id=1, source_target_pairs={{0,4},{2,6},{12,8},{14,10},{1,5},{3,7},{13,9},{15,11},{16,20},{18,... | collective-permute-start | bytes 1179656 | tf_op jit(solution)/shard_map/ppermute | solution.py:127
  158.7 20.9 %collective-permute-start.15 = (f16[2,192,768]{2,1,0:T(8,128)(2,1)S(1)}, f16[2,192,768]{2,1,0:T(8,128)(2,1)S(1)}, u32[]{:S(2)}, u32[]{:S(2)}) collective-permute-start(f16[2,192,768]{2,1,0:T(8,128)(2,1)S(1)} %get-tuple-element.59), channel_id=1, source_target_pairs={{0,4},{2,6},{12,8},{14,10},{4,0},{6,2},{8,12},{10,14},{1,5},{3,7},... | collective-permute-start | bytes 1769480 | tf_op jit(solution)/shard_map/ppermute | solution.py:127
  158.7 20.9 %collective-permute-start.17 = (f16[2,192,768]{2,1,0:T(8,128)(2,1)S(1)}, f16[2,192,768]{2,1,0:T(8,128)(2,1)S(1)}, u32[]{:S(2)}, u32[]{:S(2)}) collective-permute-start(f16[2,192,768]{2,1,0:T(8,128)(2,1)S(1)} %get-tuple-element.60), channel_id=1, source_target_pairs={{4,8},{6,10},{8,4},{10,6},{5,9},{7,11},{9,5},{11,7},{20,24},{22,26... | collective-permute-start | bytes 1769480 | tf_op jit(solution)/shard_map/ppermute | solution.py:127
  162.2 3.4 %copy-start.3 = (bf16[768,1024]{0,1:T(8,128)(2,1)S(1)}, bf16[768,1024]{0,1:T(8,128)(2,1)}, u32[]{:S(2)}) copy-start(bf16[768,1024]{0,1:T(8,128)(2,1)} %copy.34) | copy-start | bytes 4718596
  165.7 13.9 %slice-start.2 = ((s8[4718592]{0:T(1024)(128)(4,1)}), s8[4194304]{0:T(1024)(128)(4,1)S(1)}, s32[]{:S(2)}) async-start(s8[4718592]{0:T(1024)(128)(4,1)} %bitcast.181), calls=%async_computation.3 | async-start | bytes 8388608
  165.7 4.7 %copy-start.9 = (f32[4,2,192,512]{3,2,1,0:T(8,128)S(1)}, f32[4,2,192,512]{3,2,1,0:T(8,128)}, u32[]{:S(2)}) copy-start(f32[4,2,192,512]{3,2,1,0:T(8,128)} %shard_map.78) | copy-start | bytes 9437188
  165.7 13.9 %slice-start.3 = ((s8[4718592]{0:T(1024)(128)(4,1)}), s8[524288]{0:T(1024)(128)(4,1)S(1)}, s32[]{:S(2)}) async-start(s8[4718592]{0:T(1024)(128)(4,1)} %bitcast.181), calls=%async_computation.4 | async-start | bytes 1048576
  171.5 8.6 %collective-permute-start.27 = (f16[2,192,512]{2,1,0:T(8,128)(2,1)S(1)}, f16[2,192,512]{2,1,0:T(8,128)(2,1)S(1)}, u32[]{:S(2)}, u32[]{:S(2)}) collective-permute-start(f16[2,192,512]{2,1,0:T(8,128)(2,1)S(1)} %fusion.5), channel_id=1, source_target_pairs={{4,8},{6,10},{8,4},{10,6},{5,9},{7,11},{9,5},{11,7},{20,24},{22,26... | collective-permute-start | bytes 1179656 | tf_op jit(solution)/shard_map/ppermute | solution.py:127
  172.3 13.4 %collective-permute-start.29 = (f16[2,192,512]{2,1,0:T(8,128)(2,1)S(1)}, f16[2,192,512]{2,1,0:T(8,128)(2,1)S(1)}, u32[]{:S(2)}, u32[]{:S(2)}) collective-permute-start(f16[2,192,512]{2,1,0:T(8,128)(2,1)S(1)} %convert_element_type.152), channel_id=1, source_target_pairs={{0,4},{2,6},{12,8},{14,10},{1,5},{3,7},{13,9},{15,11},{16,20},{18,... | collective-permute-start | bytes 1179656 | tf_op jit(solution)/shard_map/ppermute | solution.py:127
  180.1 9.0 %copy-start.23 = (bf16[2,96,1792]{2,1,0:T(8,128)(2,1)S(1)}, bf16[2,96,1792]{2,1,0:T(8,128)(2,1)}, u32[]{:S(2)}) copy-start(bf16[2,96,1792]{2,1,0:T(8,128)(2,1)} %copy-done.22) | copy-start | bytes 2064388
  186.2 8.9 %collective-permute-start.28 = (f16[2,192,512]{2,1,0:T(8,128)(2,1)S(1)}, f16[2,192,512]{2,1,0:T(8,128)(2,1)S(1)}, u32[]{:S(2)}, u32[]{:S(2)}) collective-permute-start(f16[2,192,512]{2,1,0:T(8,128)(2,1)S(1)} %get-tuple-element.63), channel_id=1, source_target_pairs={{0,4},{2,6},{12,8},{14,10},{4,0},{6,2},{8,12},{10,14},{1,5},{3,7},... | collective-permute-start | bytes 1179656 | tf_op jit(solution)/shard_map/ppermute | solution.py:127
  188.4 6.7 %collective-permute-start.30 = (f16[2,192,512]{2,1,0:T(8,128)(2,1)S(1)}, f16[2,192,512]{2,1,0:T(8,128)(2,1)S(1)}, u32[]{:S(2)}, u32[]{:S(2)}) collective-permute-start(f16[2,192,512]{2,1,0:T(8,128)(2,1)S(1)} %get-tuple-element.64), channel_id=1, source_target_pairs={{4,8},{6,10},{8,4},{10,6},{5,9},{7,11},{9,5},{11,7},{20,24},{22,26... | collective-permute-start | bytes 1179656 | tf_op jit(solution)/shard_map/ppermute | solution.py:127
  189.4 6.0 %copy-start.24 = (bf16[2,96,768]{2,1,0:T(8,128)(2,1)}, bf16[2,96,768]{2,1,0:T(8,128)(2,1)S(1)}, u32[]{:S(2)}) copy-start(bf16[2,96,768]{2,1,0:T(8,128)(2,1)S(1)} %get-tuple-element.73) | copy-start | bytes 884740
  189.4 6.0 %copy-start.26 = (bf16[2,96,768]{2,1,0:T(8,128)(2,1)}, bf16[2,96,768]{2,1,0:T(8,128)(2,1)S(1)}, u32[]{:S(2)}) copy-start(bf16[2,96,768]{2,1,0:T(8,128)(2,1)S(1)} %get-tuple-element.74) | copy-start | bytes 884740
  190.4 6.9 %collective-permute-start.34 = (bf16[2,192,768]{2,1,0:T(8,128)(2,1)}, bf16[2,192,768]{2,1,0:T(8,128)(2,1)}, u32[]{:S(2)}, u32[]{:S(2)}) collective-permute-start(bf16[2,192,768]{2,1,0:T(8,128)(2,1)} %pad_maximum_fusion.8), channel_id=1, source_target_pairs={{4,8},{6,10},{8,4},{10,6},{5,9},{7,11},{9,5},{11,7},{20,24},{22,26... | collective-permute-start | bytes 1769480 | tf_op jit(solution)/shard_map/ppermute | solution.py:127
  191.9 16.6 %collective-permute-start.33 = (bf16[2,192,768]{2,1,0:T(8,128)(2,1)}, bf16[2,192,768]{2,1,0:T(8,128)(2,1)}, u32[]{:S(2)}, u32[]{:S(2)}) collective-permute-start(bf16[2,192,768]{2,1,0:T(8,128)(2,1)} %pad_maximum_fusion.8), channel_id=1, source_target_pairs={{0,4},{2,6},{12,8},{14,10},{4,0},{6,2},{8,12},{10,14},{1,5},{3,7},... | collective-permute-start | bytes 1769480 | tf_op jit(solution)/shard_map/ppermute | solution.py:127
  195.5 13.7 %copy-start.15 = (f32[1,192,512]{2,1,0:T(8,128)S(1)}, f32[1,192,512]{2,1,0:T(8,128)}, u32[]{:S(2)}) copy-start(f32[1,192,512]{2,1,0:T(8,128)} %copy-done.14) | copy-start | bytes 1179652
  195.5 13.7 %copy-start.17 = (f32[1,192,512]{2,1,0:T(8,128)S(1)}, f32[1,192,512]{2,1,0:T(8,128)}, u32[]{:S(2)}) copy-start(f32[1,192,512]{2,1,0:T(8,128)} %copy-done.16) | copy-start | bytes 1179652
  197.3 12.2 %copy-start.25 = (bf16[2,96,768]{2,1,0:T(8,128)(2,1)S(1)}, bf16[2,96,768]{2,1,0:T(8,128)(2,1)}, u32[]{:S(2)}) copy-start(bf16[2,96,768]{2,1,0:T(8,128)(2,1)} %copy-done.24) | copy-start | bytes 884740
  197.3 12.2 %copy-start.27 = (bf16[2,96,768]{2,1,0:T(8,128)(2,1)S(1)}, bf16[2,96,768]{2,1,0:T(8,128)(2,1)}, u32[]{:S(2)}) copy-start(bf16[2,96,768]{2,1,0:T(8,128)(2,1)} %copy-done.26) | copy-start | bytes 884740
  197.3 38.7 %collective-permute-start.35 = (bf16[2,192,768]{2,1,0:T(8,128)(2,1)}, bf16[2,192,768]{2,1,0:T(8,128)(2,1)S(1)}, u32[]{:S(2)}, u32[]{:S(2)}) collective-permute-start(bf16[2,192,768]{2,1,0:T(8,128)(2,1)} %collective-permute-done.34), channel_id=1, source_target_pairs={{4,0},{6,2},{8,12},{10,14},{5,1},{7,3},{9,13},{11,15},{20,16},{22,... | collective-permute-start | bytes 1769480 | tf_op jit(solution)/shard_map/ppermute | solution.py:127
  208.4 2.3 collective-permute-start.36
  209.5 26.6 %copy-start.19 = (f32[1,192,512]{2,1,0:T(8,128)S(1)}, f32[1,192,512]{2,1,0:T(8,128)}, u32[]{:S(2)}) copy-start(f32[1,192,512]{2,1,0:T(8,128)} %copy-done.18) | copy-start | bytes 1179652
  209.5 26.6 %copy-start.21 = (f32[1,192,512]{2,1,0:T(8,128)S(1)}, f32[1,192,512]{2,1,0:T(8,128)}, u32[]{:S(2)}) copy-start(f32[1,192,512]{2,1,0:T(8,128)} %copy-done.20) | copy-start | bytes 1179652
  210.7 54.6 %collective-permute-start.37 = (bf16[2,192,768]{2,1,0:T(8,128)(2,1)S(1)}, bf16[2,192,768]{2,1,0:T(8,128)(2,1)S(1)}, u32[]{:S(2)}, u32[]{:S(2)}) collective-permute-start(bf16[2,192,768]{2,1,0:T(8,128)(2,1)S(1)} %collective-permute-done.36), channel_id=1, source_target_pairs={{4,0},{6,2},{8,12},{10,14},{5,1},{7,3},{9,13},{11,15},{20,16},{22,... | collective-permute-start | bytes 1769480 | tf_op jit(solution)/shard_map/ppermute | solution.py:127
  236.3 34.4 %collective-permute-start.31 = (bf16[2,48,1792]{2,1,0:T(8,128)(2,1)S(1)}, bf16[2,48,1792]{2,1,0:T(8,128)(2,1)S(1)}, u32[]{:S(2)}, u32[]{:S(2)}) collective-permute-start(bf16[2,48,1792]{2,1,0:T(8,128)(2,1)S(1)} %get-tuple-element.92), channel_id=1, source_target_pairs={{0,2},{2,0},{4,6},{6,4},{8,10},{10,8},{12,14},{14,12},{1,3},{3,1},... | collective-permute-start | bytes 1032200 | tf_op jit(solution)/shard_map/ppermute | solution.py:127
  267.8 16.0 %collective-permute-start.38 = (bf16[4,2,192,768]{3,2,1,0:T(8,128)(2,1)}, bf16[4,2,192,768]{3,2,1,0:T(8,128)(2,1)}, u32[]{:S(2)}, u32[]{:S(2)}) collective-permute-start(bf16[4,2,192,768]{3,2,1,0:T(8,128)(2,1)} %get-tuple-element.70), channel_id=1, source_target_pairs={{0,2},{2,0},{4,6},{6,4},{8,10},{10,8},{12,14},{14,12},{1,3},{3,1},... | collective-permute-start | bytes 7077896 | tf_op jit(solution)/shard_map/ppermute | solution.py:127
  271.7 10.0 %collective-permute-start.32 = (bf16[48,3584]{1,0:T(8,128)(2,1)}, bf16[48,3584]{1,0:T(8,128)(2,1)}, u32[]{:S(2)}, u32[]{:S(2)}) collective-permute-start(bf16[48,3584]{1,0:T(8,128)(2,1)} %get-tuple-element.90), channel_id=1, source_target_pairs={{0,1},{1,0},{2,3},{3,2},{4,5},{5,4},{6,7},{7,6},{8,9},{9,8},{10,11... | collective-permute-start | bytes 1032200 | tf_op jit(solution)/shard_map/ppermute | solution.py:276
  290.0 1.9 copy-start.7
  291.9 6.3 %copy-start.1 = (bf16[1,48,7168]{2,1,0:T(8,128)(2,1)S(1)}, bf16[1,48,7168]{2,1,0:T(8,128)(2,1)}, u32[]{:S(2)}) copy-start(bf16[1,48,7168]{2,1,0:T(8,128)(2,1)} %param.8) | copy-start | bytes 2064388
  (9 other events, 10.8 us)
Sparse Core Ops, SparseCore 0:
  197.4 57.9 all-gather.1

commit v5 on v4

v5 whole, which is shorter than its diff:
```python
import functools
import math

import jax
import jax.numpy as jnp
from jax import lax
from jax.experimental import pallas as pl
from jax.experimental.pallas import tpu as pltpu
from jax.sharding import PartitionSpec as P

WIRE = jnp.float16
LARGEST_TOKEN, LARGEST_WEIGHT = 6.0, 0.0625
VMEM_LIMIT = 48 * 2**20
NO_COST = pl.CostEstimate(flops=0, bytes_accessed=0, transcendentals=0)
SHARES = (4, 3)


def forward_kernel(
    scale, place_ref, mine_ref, theirs_ref, gate_ref, up_ref, gate_far_ref, up_far_ref, out_ref
):
    blocks, _, rows, width = out_ref.shape
    for which, (near, far) in enumerate(((gate_ref, gate_far_ref), (up_ref, up_far_ref))):
        product = jnp.dot(mine_ref[...], near[...], preferred_element_type=jnp.float32)
        product += jnp.dot(theirs_ref[...], far[...], preferred_element_type=jnp.float32)
        out_ref[:, which] = (scale * product).reshape(blocks, rows, width)


def forward(place, mine, theirs, gate_weight, up_weight, far, start, tile, blocks, scale):
    total, depth = mine.shape
    width = far[0].shape[1]
    rows = total // blocks
    whole = pl.BlockSpec((total, depth), lambda j, place: (0, 0))
    weight = pl.BlockSpec((depth, tile), lambda j, place: (0, place[0] + start // tile + j))
    return pl.pallas_call(
        functools.partial(forward_kernel, scale),
        out_shape=jax.ShapeDtypeStruct((blocks, 2, rows, width), jnp.float32),
        grid_spec=pltpu.PrefetchScalarGridSpec(
            num_scalar_prefetch=1,
            grid=(width // tile,),
            in_specs=[
                whole,
                whole,
                weight,
                weight,
                pl.BlockSpec((depth, tile), lambda j, place: (0, j)),
                pl.BlockSpec((depth, tile), lambda j, place: (0, j)),
            ],
            out_specs=pl.BlockSpec((blocks, 2, rows, tile), lambda j, place: (0, 0, 0, j)),
        ),
        compiler_params=pltpu.CompilerParams(vmem_limit_bytes=VMEM_LIMIT),
        cost_estimate=NO_COST,
    )(place, mine, theirs, gate_weight, up_weight, *far)


def gradient_kernel(batches, place_ref, features_ref, *refs):
    acts, outs = refs[:batches], refs[-2:]
    for which, out_ref in enumerate(outs):
        parts = []
        for act_ref in acts:
            blocks, _, _, rows, width = act_ref.shape
            rows = rows * batches // 2
            for i in range(2 // batches):
                part = act_ref[:, 0, which, i * rows : (i + 1) * rows]
                parts.append(part.reshape(blocks * rows, width))
        out_ref[...] = jnp.dot(
            features_ref[...], jnp.concatenate(parts), preferred_element_type=jnp.float32
        )


def gradient(place, features, acts, totals, columns, start, tile):
    depth, total = features.shape
    blocks, cores, _, rows, width = acts[0].shape
    act_spec = pl.BlockSpec((blocks, 1, 2, rows, tile), lambda i, j, place: (0, i, 0, 0, j))
    out_spec = pl.BlockSpec((depth, tile), lambda i, j, place: (0, place[i] + start // tile + j))
    out_shape = jax.ShapeDtypeStruct((depth, columns), jnp.float32)
    in_specs = [pl.BlockSpec((depth, total), lambda i, j, place: (0, 0))]
    in_specs += [act_spec] * len(acts)
    in_specs += [pl.BlockSpec(memory_space=pl.ANY)] * len(totals)
    return pl.pallas_call(
        functools.partial(gradient_kernel, len(acts)),
        out_shape=(out_shape, out_shape),
        grid_spec=pltpu.PrefetchScalarGridSpec(
            num_scalar_prefetch=1,
            grid=(cores, width // tile),
            in_specs=in_specs,
            out_specs=(out_spec, out_spec),
        ),
        input_output_aliases={2 + len(acts) + i: i for i in range(len(totals))},
        compiler_params=pltpu.CompilerParams(vmem_limit_bytes=VMEM_LIMIT),
        cost_estimate=NO_COST,
    )(place, features, *acts, *totals)


def tie(value, *after):
    return lax.optimization_barrier((value, after))[0]


def cut(units, shares):
    edges = [round(units * sum(shares[:i]) / sum(shares)) for i in range(len(shares) + 1)]
    return [(a, b - a) for a, b in zip(edges, edges[1:]) if b > a]


def local(tokens, gate_weight, up_weight, grad_hidden):
    line = 4
    row, col, part = (lax.axis_index(name) for name in ("row", "col", "depth"))
    place, core = col // 2, col % 2
    slab = grad_hidden.shape[1]
    rows = 2 * slab
    depth, columns = gate_weight.shape
    half = columns // 2
    share = half // 2
    tile = 256 if share % 256 == 0 else 128
    largest = depth * 2 * line * LARGEST_TOKEN * LARGEST_WEIGHT
    scale = 2.0 ** math.floor(math.log2(65504 / largest))

    swap = [(0, 1), (1, 0)]
    pairs = [(i, i ^ 1) for i in range(2 * line)]

    def between(hops):
        return [(2 * i + c, 2 * j + c) for i, j in hops for c in (0, 1)]

    inward, outward = between([(0, 1), (3, 2)]), between([(1, 0), (2, 3)])
    side, centre = inward + outward, between([(1, 2), (2, 1)])
    at_end = (place == 0) | (place == line - 1)
    at_far = 2 * place >= line

    def send(value, route):
        return lax.ppermute(value, "col", route)

    def wide(value):
        return value.astype(jnp.float32)

    def add(*terms):
        return functools.reduce(jnp.add, map(wide, terms))

    def by(first, mine, theirs, axis):
        return jnp.where(
            first,
            jnp.concatenate([mine, theirs], axis=axis),
            jnp.concatenate([theirs, mine], axis=axis),
        )

    def columns_of(array, start, width):
        return lax.dynamic_slice_in_dim(array, start, width, array.ndim - 1)

    pieces = []
    for begin, count in cut(share // tile, SHARES):
        for batches in ((0, 1),) if pieces else ((0,), (1,)):
            pieces.append((batches, begin * tile, count * tile))
    last = len(pieces) - 1

    def exchange_weights(k, after):
        _, start, width = pieces[k]
        first = part * half + (1 - core) * share + start
        return [
            send(tie(columns_of(weight, first, width), after), pairs)
            for weight in (gate_weight, up_weight)
        ]

    mine = tokens[0]
    over_row = lax.ppermute(mine, "row", swap)
    over_depth = lax.ppermute(mine, "depth", swap)
    over_both = lax.ppermute(over_row, "depth", swap)
    far_weights = {0: exchange_weights(0, ())}
    far_weights[1] = far_weights[0]
    first_tile = ((part * half + core * share) // tile).astype(jnp.int32).reshape(1)

    def arrange(values):
        values = values.reshape(line, rows, depth)
        return jnp.where(at_far, values[::-1], values)

    def both_cores(values, after):
        values = arrange(tie(values, after))
        return values, send(values, pairs)

    def multiply(k, tokens, after):
        _, start, _ = pieces[k]
        mine, theirs = (value.reshape(-1, depth) for value in tie(tokens, after))
        weights = (gate_weight, up_weight, far_weights[k])
        return forward(first_tile, mine, theirs, *weights, start, tile, line, scale)

    features = [by(row == 0, mine, over_row, 1)]
    spread = [both_cores(features[0], ())]
    terms = multiply(0, spread[0], ())
    payload = terms[3].astype(WIRE)
    in_1 = send(payload, inward)

    over_depth, over_both = tie((over_depth, over_both), payload)
    features.append(by(row == 0, over_depth, over_both, 1))
    spread.append(both_cores(features[1], ()))
    far_weights[2] = exchange_weights(2, spread[1])

    mine_cotangent, cotangent = tie((grad_hidden[0], grad_hidden[0]), in_1)
    cotangent = jnp.stack(
        [
            columns_of(mine_cotangent, part * half, half),
            lax.ppermute(columns_of(cotangent, (1 - part) * half, half), "depth", swap),
        ]
    )
    cotangent = by(
        core == 0,
        columns_of(cotangent, core * share, share),
        send(columns_of(cotangent, (1 - core) * share, share), pairs),
        1,
    )

    def activate(k, summed):
        batches, start, width = pieces[k]
        summed = (summed * (1.0 / scale)).reshape(2, len(batches), rows, width)
        gate_sum, up_sum = summed[0], summed[1]
        squash = jax.nn.sigmoid(gate_sum)
        product = (gate_sum * squash * up_sum).astype(jnp.bfloat16)
        for position, batch in enumerate(batches):
            hidden[batch].append(product[position])
        given = jnp.stack([wide(cotangent[b][:, start : start + width]) for b in batches])
        gate_act = given * up_sum * squash * (1.0 + gate_sum * (1.0 - squash))
        up_act = given * gate_sum * squash
        act = jnp.stack([gate_act, up_act]).astype(jnp.bfloat16)
        return act.reshape(2, len(batches) * rows, width)

    def merge(act, side_1, centre_1, out_2, share_2, out_3):
        blocks = jnp.stack(
            [
                jnp.where(at_end, act, side_1),
                jnp.where(at_end, side_1, act),
                jnp.where(at_end, out_2, centre_1),
                jnp.where(at_end, out_3, share_2),
            ]
        )
        return blocks, send(blocks, pairs)

    turned = jnp.concatenate([tie(near, in_1).reshape(-1, depth) for near, _ in spread]).T
    turned_in_place = jnp.concatenate([tie(value, in_1) for value in features]).T

    def finish(gathered, totals, start):
        own, other = [value for value, _ in gathered], [value for _, value in gathered]
        for values, owner in ((own, core), (other, 1 - core)):
            where = (owner * (share // tile)).astype(jnp.int32).reshape(1)
            values = [value[:, None] for value in values]
            totals = gradient(where, turned, values, totals, half, start, tile)
        return totals

    hidden, totals, waiting = ([], []), (), []
    act = hops = None
    for k in range(-1, last):
        if act is not None:
            side_1, centre_1 = send(act, side), send(act, centre)
        if hops is not None:
            waiting.append(merge(*hops))
            terms = tie(terms, waiting[-1][0])
        far = add(terms[3], in_1).astype(WIRE)
        centre_2 = send(far, centre)
        in_2 = send(tie(terms[2], in_1).astype(WIRE), inward)
        if act is not None:
            out_2, share_2 = send(centre_1, outward), send(side_1, centre)
        following = None
        if k + 2 <= last:
            tokens = spread[1] if k < 0 else [jnp.stack(pair, axis=1) for pair in zip(*spread)]
            following = multiply(k + 2, tokens, (in_1, *(() if act is None else (side_1, centre_1))))
            terms = tie(terms, following)
        near = add(terms[2], in_2).astype(WIRE)
        swapped = jnp.where(at_end, terms[1], add(terms[0], centre_2)).astype(WIRE)
        centre_3, side_3 = send(near, centre), send(swapped, side)
        if following is not None:
            in_1 = send(tie(following[3], near, swapped).astype(WIRE), inward)
        if act is not None:
            out_3 = send(share_2, outward)
        own = jnp.where(at_end, terms[0], terms[1])
        ready = activate(k + 1, add(own, side_3, centre_3))
        if act is not None:
            hops = tie((act, side_1, centre_1, out_2, share_2, out_3), ready)
        act, terms = ready, following

    everything = lax.all_gather(tie(act, share_2), "col", axis=0).reshape(line, 2, *act.shape)
    waiting.append(merge(*hops))
    totals = finish(waiting, totals, pieces[0][1])
    places = jnp.array([0, share // tile], jnp.int32)
    totals = gradient(places, turned_in_place, [everything], totals, half, pieces[last][1], tile)

    hidden = jnp.stack([jnp.concatenate(parts, axis=1) for parts in hidden])
    hidden = hidden.reshape(2, 2, slab, share)
    mine = lax.dynamic_index_in_dim(hidden, core, 1, keepdims=False)
    theirs = lax.dynamic_index_in_dim(hidden, 1 - core, 1, keepdims=False)
    hidden = by(core == 0, mine, send(theirs, pairs), 2)
    hidden = by(part == 0, hidden[0], lax.ppermute(hidden[1], "depth", swap), 1)
    return (hidden[None], *totals)


def contract(picked, piece):
    return lax.dot_general(
        picked, piece, (((0,), (0,)), ((), ())), preferred_element_type=jnp.float32
    )


def local_any(tokens, gate_weight, up_weight, grad_hidden):
    features = lax.all_gather(tokens[0], "row", axis=1, tiled=True)
    columns = gate_weight.shape[1]
    picked = features
    gate_part = jnp.dot(picked, gate_weight, preferred_element_type=jnp.float32)
    up_part = jnp.dot(picked, up_weight, preferred_element_type=jnp.float32)
    summed = lax.psum_scatter(
        jnp.concatenate([gate_part, up_part], axis=1), "col", scatter_dimension=0, tiled=True
    )
    gate_sum = summed[:, :columns]
    up_sum = summed[:, columns:]
    squash = jax.nn.sigmoid(gate_sum)
    hidden = (gate_sum * squash * up_sum).astype(jnp.bfloat16)
    cotangent = grad_hidden[0].astype(jnp.float32)
    gate_act = (cotangent * up_sum * squash * (1.0 + gate_sum * (1.0 - squash))).astype(
        jnp.bfloat16
    )
    up_act = (cotangent * gate_sum * squash).astype(jnp.bfloat16)
    picked = features
    gate_total = contract(picked, lax.all_gather(gate_act, "col", axis=0, tiled=True))
    up_total = contract(picked, lax.all_gather(up_act, "col", axis=0, tiled=True))
    grad_gate, grad_up = (
        lax.psum_scatter(gate_total, "depth", scatter_dimension=1, tiled=True),
        lax.psum_scatter(up_total, "depth", scatter_dimension=1, tiled=True),
    )
    return (hidden[None], grad_gate, grad_up)


def solution(mesh):
    in_specs = (
        P("depth", None, ("col", "row")),
        P("col", "row"),
        P("col", "row"),
        P("depth", "col", "row"),
    )
    out_specs = (P("depth", "col", "row"), P("col", ("row", "depth")), P("col", ("row", "depth")))
    sizes = tuple(mesh.shape[name] for name in ("row", "col", "depth"))
    return jax.shard_map(
        local if sizes == (2, 8, 2) else local_any,
        mesh=mesh,
        in_specs=in_specs,
        out_specs=out_specs,
        check_vma=False,
    )
```

time: 307 us -> 318 us (1.036)
  waiting for transfers between devices: 97.3 us -> 117 us
  starting transfers between devices: 91 us -> 83.7 us
  other arithmetic: 33.3 us -> 27.2 us
  local copies, waits for them, and re-layouts: 21.8 us -> 25.7 us
    ppermute x34 -> x35, waiting for transfers between devices: 84.1 us -> 101 us  [send(): return lax.ppermute(value, 'col', route)]
    dynamic_slice x1 -> x5, local copies, waits for them, and re-layouts: 0.02 us -> 11.6 us  [columns_of(): return lax.dynamic_slice_in_dim(array, start, width, array.ndim - 1)]
    ppermute x34 -> x35, starting transfers between devices: 85.2 us -> 77.3 us  [send(): return lax.ppermute(value, 'col', route)]
    another operation x2 -> x1, local copies, waits for them, and re-layouts: 5.64 us -> 0.02 us  [activate(): jnp.stack([wide(cotangent[b][:, start:start + width]) for b in batches])]
    optimization_barrier x0 -> x4, local copies, waits for them, and re-layouts: none -> 5.03 us  [tie(): return lax.optimization_barrier((value, after))[0]]
    unnamed x66 -> x37, local copies, waits for them, and re-layouts: 10.4 us -> 5.37 us
    select_n x7 -> x5, other arithmetic: 10.5 us -> 5.8 us  [by(): jnp.where(first, jnp.concatenate([mine, theirs], axis=axis), jnp.concaten...]
    select_n x2, other arithmetic: 0.85 us -> 4.44 us  [arrange(): return jnp.where(at_far, values[::-1], values)]
  transfers between devices with their start and end apart: 40 -> 41, of which waited for: 14 -> 12; matrix products, arithmetic and copies ran while one was open for 14% -> 14% of each run, Pallas kernels for 13% -> 11%
where the time goes in v5:
time: 318 us; the launch traced here: 315 us
  waiting for transfers between devices  117 us (37%)
  starting transfers between devices  83.7 us (26%)
  Pallas kernels  47.2 us (15%)
  other arithmetic  27.2 us (9%)
  local copies, waits for them, and re-layouts  25.7 us (8%)
  between operations  14.8 us (5%)
    ppermute x35, waiting for transfers between devices, send(): return lax.ppermute(value, 'col', route)  101 us
    ppermute x35, starting transfers between devices, send(): return lax.ppermute(value, 'col', route)  77.3 us
    pallas_call x3, Pallas kernels, gradient(): pl.pallas_call(functools.partial(gradient_kernel, len(acts)), out_shape=(...  24.2 us
    pallas_call x3, Pallas kernels, forward(): pl.pallas_call(functools.partial(forward_kernel, scale), out_shape=jax.Sh...  23 us
    dynamic_slice x5, local copies, waits for them, and re-layouts, columns_of(): return lax.dynamic_slice_in_dim(array, start, width, array.ndim - 1)  11.6 us
    ppermute x1, waiting for transfers between devices, local(): over_row = lax.ppermute(mine, 'row', swap)  9.13 us
    ppermute x1, waiting for transfers between devices, local(): lax.ppermute(columns_of(cotangent, (1 - part) * half, half), 'depth', swap)  6.58 us
  transfers between devices with their start and end apart: 41, of which 12 were waited for; matrix products, arithmetic and copies ran while one was open for 14% of the time, Pallas kernels for 11%

profile of v5, /device:TPU:1, one launch (start us, length us, event | category | flops | bytes accessed | tf_op | source)
XLA Modules:
  0.0 315.5 jit_solution(8809168757017623183)
XLA Ops:
  7.3 3.1 constant_dynamic-slice_fusion.4
  10.5 3.1 constant_dynamic-slice_fusion.3
  14.0 1.2 copy.32
  15.2 2.3 collective-permute-start
  17.5 9.1 %collective-permute-done = bf16[384,512]{0,1:T(8,128)(2,1)} collective-permute-done((bf16[384,512]{0,1:T(8,128)(2,1)S(1)}, bf16[384,512]{0,1:T(8,128)(2,1)}, u32[]{:S(2)}, u32[]{:S(2)}) %collective-permute-start) | collective-permute-done | bytes 393248 | tf_op jit(solution)/shard_map/ppermute | solution.py:161
  26.6 2.3 maximum_select_fusion
  28.9 2.3 copy.33
  31.2 2.7 reverse_select_fusion.1
  33.9 1.0 collective-permute-start.1
  34.9 1.5 collective-permute-start.4
  36.4 2.7 constant_dynamic-slice_fusion
  39.1 2.7 constant_dynamic-slice_fusion.1
  41.8 7.7 %shard_map.76 = f32[4,2,96,1024]{3,2,1,0:T(8,128)} custom-call(s32[1]{0:T(128)} %bitcast.place_ref, bf16[384,1024]{1,0:T(8,128)(2,1)} %bitcast.3.mine_ref, bf16[384,1024]{1,0:T(8,128)(2,1)} %bitcast.4.theirs_ref, bf16[1024,7168]{1,0:T(8,128)(2,1)} %gate_ref.5, bf16[1024,7168]{1,0:T(8,128)(2,1)} %up_ref.5, ...), custom_call_target="tpu_custom_call" | custom-call | tf_op jit(solution)/shard_map/pallas_call | solution.py:34
  49.4 2.5 slice_bitcast_fusion.4
  52.0 4.2 %collective-permute-start.7 = (f16[2,96,1024]{2,1,0:T(8,128)(2,1)}, f16[2,96,1024]{2,1,0:T(8,128)(2,1)}, u32[]{:S(2)}, u32[]{:S(2)}) collective-permute-start(f16[2,96,1024]{2,1,0:T(8,128)(2,1)} %get-tuple-element.98), channel_id=1, source_target_pairs={{0,4},{2,6},{12,8},{14,10},{1,5},{3,7},{13,9},{15,11},{16,20},{18,... | collective-permute-start | bytes 1179656 | tf_op jit(solution)/shard_map/ppermute | solution.py:128
  56.2 2.3 maximum_select_fusion.1
  58.4 2.4 copy.34
  60.8 1.8 reverse_select_fusion
  63.7 4.1 %collective-permute-start.10 = (f16[2,96,1024]{2,1,0:T(8,128)(2,1)S(1)}, f16[2,96,1024]{2,1,0:T(8,128)(2,1)S(1)}, u32[]{:S(2)}, u32[]{:S(2)}) collective-permute-start(f16[2,96,1024]{2,1,0:T(8,128)(2,1)S(1)} %convert_element_type.119), channel_id=1, source_target_pairs={{0,4},{2,6},{12,8},{14,10},{1,5},{3,7},{13,9},{15,11},{16,20},{18,... | collective-permute-start | bytes 1179656 | tf_op jit(solution)/shard_map/ppermute | solution.py:128
  67.8 1.4 add_convert_fusion.2
  69.9 1.3 collective-permute-start.13
  71.3 6.6 %collective-permute-done.13 = bf16[48,3584]{1,0:T(8,128)(2,1)S(1)} collective-permute-done((bf16[48,3584]{1,0:T(8,128)(2,1)S(1)}, bf16[48,3584]{1,0:T(8,128)(2,1)S(1)}, u32[]{:S(2)}, u32[]{:S(2)}) %collective-permute-start.13) | collective-permute-done | bytes 344096 | tf_op jit(solution)/shard_map/ppermute | solution.py:197
  77.9 2.7 collective-permute-start.14
  80.6 7.3 %shard_map.77 = f32[4,2,96,1024]{3,2,1,0:T(8,128)} custom-call(s32[1]{0:T(128)} %bitcast.place_ref, bf16[384,1024]{1,0:T(8,128)(2,1)S(1)} %bitcast.178, bf16[384,1024]{1,0:T(8,128)(2,1)S(1)} %bitcast.182, bf16[1024,7168]{1,0:T(8,128)(2,1)} %gate_ref.5, bf16[1024,7168]{1,0:T(8,128)(2,1)} %up_ref.5, ...), custom_call_target="tpu_custom_call" | custom-call | tf_op jit(solution)/shard_map/pallas_call | solution.py:34
  89.1 3.3 %collective-permute-start.9 = (f16[2,96,1024]{2,1,0:T(8,128)(2,1)S(1)}, f16[2,96,1024]{2,1,0:T(8,128)(2,1)S(1)}, u32[]{:S(2)}, u32[]{:S(2)}) collective-permute-start(f16[2,96,1024]{2,1,0:T(8,128)(2,1)S(1)} %get-tuple-element.95), channel_id=1, source_target_pairs={{0,4},{2,6},{12,8},{14,10},{4,0},{6,2},{8,12},{10,14},{1,5},{3,7},... | collective-permute-start | bytes 1179656 | tf_op jit(solution)/shard_map/ppermute | solution.py:128
  92.6 2.1 collective-permute-start.12
  95.7 5.9 %collective-permute-done.9 = f16[2,96,1024]{2,1,0:T(8,128)(2,1)S(1)} collective-permute-done((f16[2,96,1024]{2,1,0:T(8,128)(2,1)S(1)}, f16[2,96,1024]{2,1,0:T(8,128)(2,1)S(1)}, u32[]{:S(2)}, u32[]{:S(2)}) %collective-permute-start.9) | collective-permute-done | bytes 393248 | tf_op jit(solution)/shard_map/ppermute | solution.py:128
  102.3 1.3 collective-permute-start.15
  104.5 4.5 %collective-permute-done.12 = f16[2,96,1024]{2,1,0:T(8,128)(2,1)S(1)} collective-permute-done((f16[2,96,1024]{2,1,0:T(8,128)(2,1)S(1)}, f16[2,96,1024]{2,1,0:T(8,128)(2,1)S(1)}, u32[]{:S(2)}, u32[]{:S(2)}) %collective-permute-start.12) | collective-permute-done | bytes 393248 | tf_op jit(solution)/shard_map/ppermute | solution.py:128
  109.1 4.1 %collective-permute-start.24 = (f16[2,96,1024]{2,1,0:T(8,128)(2,1)S(1)}, f16[2,96,1024]{2,1,0:T(8,128)(2,1)S(1)}, u32[]{:S(2)}, u32[]{:S(2)}) collective-permute-start(f16[2,96,1024]{2,1,0:T(8,128)(2,1)S(1)} %convert_element_type.130), channel_id=1, source_target_pairs={{0,4},{2,6},{12,8},{14,10},{1,5},{3,7},{13,9},{15,11},{16,20},{18,... | collective-permute-start | bytes 1179656 | tf_op jit(solution)/shard_map/ppermute | solution.py:128
  113.4 4.1 %collective-permute-done.15 = bf16[2,96,1024]{2,1,0:T(8,128)(2,1)S(1)} collective-permute-done((bf16[2,96,1024]{2,1,0:T(8,128)(2,1)S(1)}, bf16[2,96,1024]{2,1,0:T(8,128)(2,1)S(1)}, u32[]{:S(2)}, u32[]{:S(2)}) %collective-permute-start.15) | collective-permute-done | bytes 393248 | tf_op jit(solution)/shard_map/ppermute | solution.py:128
  118.5 1.3 pad_maximum_fusion.1
  120.9 1.1 copy-done.15
  122.0 8.1 %shard_map.78 = f32[4,2,192,768]{3,2,1,0:T(8,128)} custom-call(s32[1]{0:T(128)} %bitcast.place_ref, bf16[768,1024]{1,0:T(8,128)(2,1)S(1)} %bitcast.180, bf16[768,1024]{1,0:T(8,128)(2,1)S(1)} %bitcast.181, bf16[1024,7168]{1,0:T(8,128)(2,1)} %gate_ref.5, bf16[1024,7168]{1,0:T(8,128)(2,1)} %up_ref.5, ...), custom_call_target="tpu_custom_call" | custom-call | tf_op jit(solution)/shard_map/pallas_call | solution.py:34
  130.4 6.2 %collective-permute-start.23 = (f16[2,96,1024]{2,1,0:T(8,128)(2,1)S(1)}, f16[2,96,1024]{2,1,0:T(8,128)(2,1)S(1)}, u32[]{:S(2)}, u32[]{:S(2)}) collective-permute-start(f16[2,96,1024]{2,1,0:T(8,128)(2,1)S(1)} %get-tuple-element.91), channel_id=1, source_target_pairs={{0,4},{2,6},{12,8},{14,10},{4,0},{6,2},{8,12},{10,14},{1,5},{3,7},... | collective-permute-start | bytes 1179656 | tf_op jit(solution)/shard_map/ppermute | solution.py:128
  137.3 1.3 collective-permute-start.19
  138.6 1.3 collective-permute-start.21
  139.9 1.4 slice_bitcast_fusion
  141.3 4.7 %collective-permute-start.26 = (f16[2,192,768]{2,1,0:T(8,128)(2,1)S(1)}, f16[2,192,768]{2,1,0:T(8,128)(2,1)S(1)}, u32[]{:S(2)}, u32[]{:S(2)}) collective-permute-start(f16[2,192,768]{2,1,0:T(8,128)(2,1)S(1)} %convert_element_type.134), channel_id=1, source_target_pairs={{0,4},{2,6},{12,8},{14,10},{1,5},{3,7},{13,9},{15,11},{16,20},{18,... | collective-permute-start | bytes 1769480 | tf_op jit(solution)/shard_map/ppermute | solution.py:128
  146.7 5.4 %collective-permute-done.19 = bf16[2,96,1024]{2,1,0:T(8,128)(2,1)S(1)} collective-permute-done((bf16[2,96,1024]{2,1,0:T(8,128)(2,1)S(1)}, bf16[2,96,1024]{2,1,0:T(8,128)(2,1)S(1)}, u32[]{:S(2)}, u32[]{:S(2)}) %collective-permute-start.19) | collective-permute-done | bytes 393248 | tf_op jit(solution)/shard_map/ppermute | solution.py:128
  152.0 8.4 %collective-permute-done.21 = bf16[2,96,1024]{2,1,0:T(8,128)(2,1)S(1)} collective-permute-done((bf16[2,96,1024]{2,1,0:T(8,128)(2,1)S(1)}, bf16[2,96,1024]{2,1,0:T(8,128)(2,1)S(1)}, u32[]{:S(2)}, u32[]{:S(2)}) %collective-permute-start.21) | collective-permute-done | bytes 393248 | tf_op jit(solution)/shard_map/ppermute | solution.py:128
  160.7 1.9 fusion.34
  162.7 1.3 collective-permute-start.29
  165.0 8.7 %collective-permute-done.29 = f16[2,192,768]{2,1,0:T(8,128)(2,1)S(1)} collective-permute-done((f16[2,192,768]{2,1,0:T(8,128)(2,1)S(1)}, f16[2,192,768]{2,1,0:T(8,128)(2,1)S(1)}, u32[]{:S(2)}, u32[]{:S(2)}) %collective-permute-start.29) | collective-permute-done | bytes 589856 | tf_op jit(solution)/shard_map/ppermute | solution.py:128
  174.2 3.5 %collective-permute-start.28 = (f16[2,192,768]{2,1,0:T(8,128)(2,1)S(1)}, f16[2,192,768]{2,1,0:T(8,128)(2,1)S(1)}, u32[]{:S(2)}, u32[]{:S(2)}) collective-permute-start(f16[2,192,768]{2,1,0:T(8,128)(2,1)S(1)} %get-tuple-element.89), channel_id=1, source_target_pairs={{0,4},{2,6},{12,8},{14,10},{4,0},{6,2},{8,12},{10,14},{1,5},{3,7},... | collective-permute-start | bytes 1769480 | tf_op jit(solution)/shard_map/ppermute | solution.py:128
  178.4 2.6 collective-permute-start.33
  181.0 14.7 %collective-permute-done.33 = bf16[2,96,1024]{2,1,0:T(8,128)(2,1)S(1)} collective-permute-done((bf16[2,96,1024]{2,1,0:T(8,128)(2,1)S(1)}, bf16[2,96,1024]{2,1,0:T(8,128)(2,1)S(1)}, u32[]{:S(2)}, u32[]{:S(2)}) %collective-permute-start.33) | collective-permute-done | bytes 393248 | tf_op jit(solution)/shard_map/ppermute | solution.py:128
  198.8 1.3 collective-permute-start.37
  200.1 1.3 collective-permute-start.38
  201.4 4.7 %collective-permute-start.35 = (bf16[4,2,96,1024]{3,2,1,0:T(8,128)(2,1)}, bf16[4,2,96,1024]{3,2,1,0:T(8,128)(2,1)}, u32[]{:S(2)}, u32[]{:S(2)}) collective-permute-start(bf16[4,2,96,1024]{3,2,1,0:T(8,128)(2,1)} %get-tuple-element.102), channel_id=1, source_target_pairs={{0,2},{2,0},{4,6},{6,4},{8,10},{10,8},{12,14},{14,12},{1,3},{3,1},... | collective-permute-start | bytes 4718600 | tf_op jit(solution)/shard_map/ppermute | solution.py:128
  206.1 15.5 %collective-permute-done.37 = bf16[2,96,1024]{2,1,0:T(8,128)(2,1)} collective-permute-done((bf16[2,96,1024]{2,1,0:T(8,128)(2,1)S(1)}, bf16[2,96,1024]{2,1,0:T(8,128)(2,1)}, u32[]{:S(2)}, u32[]{:S(2)}) %collective-permute-start.37) | collective-permute-done | bytes 393248 | tf_op jit(solution)/shard_map/ppermute | solution.py:128
  221.6 33.8 %collective-permute-done.38 = bf16[2,96,1024]{2,1,0:T(8,128)(2,1)} collective-permute-done((bf16[2,96,1024]{2,1,0:T(8,128)(2,1)S(1)}, bf16[2,96,1024]{2,1,0:T(8,128)(2,1)}, u32[]{:S(2)}, u32[]{:S(2)}) %collective-permute-start.38) | collective-permute-done | bytes 393248 | tf_op jit(solution)/shard_map/ppermute | solution.py:128
  255.7 17.0 %collective-permute-start.31 = (bf16[2,48,1792]{2,1,0:T(8,128)(2,1)S(1)}, bf16[2,48,1792]{2,1,0:T(8,128)(2,1)S(1)}, u32[]{:S(2)}, u32[]{:S(2)}) collective-permute-start(bf16[2,48,1792]{2,1,0:T(8,128)(2,1)S(1)} %get-tuple-element.120), channel_id=1, source_target_pairs={{0,2},{2,0},{4,6},{6,4},{8,10},{10,8},{12,14},{14,12},{1,3},{3,1},... | collective-permute-start | bytes 1032200 | tf_op jit(solution)/shard_map/ppermute | solution.py:128
  272.7 1.1 select_bitcast_fusion.1
  273.8 1.0 select_bitcast_fusion
  274.9 1.9 fusion.33
  277.1 1.3 collective-permute-start.32
  278.7 1.5 copy.37
  280.3 1.0 copy-done.10
  281.7 1.3 copy-done.4
  283.4 5.9 %shard_map.79 = (f32[1024,3584]{1,0:T(8,128)}, f32[1024,3584]{1,0:T(8,128)}) custom-call(s32[1]{0:T(128)} %bitcast.69.place_ref, bf16[1024,768]{1,0:T(8,128)(2,1)S(1)} %maximum_bitcast_fusion.1.features_ref, bf16[4,1,2,96,1024]{4,3,2,1,0:T(8,128)(2,1)S(1)} %copy-done.4, bf16[4,1,2,96,1024]{4,3,2,1,0:T(8,128)(2,1)S(1)} %copy-done.5), custom_call_target="tpu_custom_call" | custom-call | tf_op jit(solution)/shard_map/pallas_call | solution.py:79
  289.3 1.0 maximum_select_fusion.4
  290.3 7.3 %shard_map.80 = (f32[1024,3584]{1,0:T(8,128)}, f32[1024,3584]{1,0:T(8,128)}) custom-call(s32[1]{0:T(128)} %bitcast.58.place_ref, bf16[1024,768]{1,0:T(8,128)(2,1)S(1)} %maximum_bitcast_fusion.1.features_ref, bf16[4,1,2,96,1024]{4,3,2,1,0:T(8,128)(2,1)} %bitcast.63.refs_0_, ...), custom_call_target="tpu_custom_call", output_to_operand_aliasing={{0}: (4, {}), {1}: (5, {})} | custom-call | tf_op jit(solution)/shard_map/pallas_call | solution.py:79
  297.7 10.9 %shard_map.81 = (f32[1024,3584]{1,0:T(8,128)}, f32[1024,3584]{1,0:T(8,128)}) custom-call(s32[2]{0:T(128)S(1)} %iota_multiply_fusion.place_ref, bf16[1024,768]{1,0:T(8,128)(2,1)S(1)} %maximum_bitcast_fusion.features_ref, bf16[4,2,2,192,768]{4,3,2,1,0:T(8,128)(2,1)} %bitcast.190, ...), custom_call_target="tpu_custom_call", output_to_operand_aliasing={{0}: (3, {}), {1}: (4, {})} | custom-call | tf_op jit(solution)/shard_map/pallas_call | solution.py:79
  (129 shorter events, 17.6 us)
Async XLA Ops:
  7.2 62.7 %copy-start = (bf16[1,48,7168]{2,1,0:T(8,128)(2,1)S(1)}, bf16[1,48,7168]{2,1,0:T(8,128)(2,1)}, u32[]{:S(2)}) copy-start(bf16[1,48,7168]{2,1,0:T(8,128)(2,1)} %param.8) | copy-start | bytes 2064388
  7.2 290.5 %all-gather.3.cloned.1.call-start = ((), (), s32[]{:S(2)}) async-start(), calls=%async_computation | async-start | bytes 5308416 | tf_op jit(solution)/shard_map/all_gather | solution.py:274
  10.4 31.4 %collective-permute-start.2 = (bf16[1024,1024]{1,0:T(8,128)(2,1)}, bf16[1024,1024]{1,0:T(8,128)(2,1)S(1)}, u32[]{:S(2)}, u32[]{:S(2)}) collective-permute-start(bf16[1024,1024]{1,0:T(8,128)(2,1)} %constant_dynamic-slice_fusion.4), channel_id=1, source_target_pairs={{0,2},{2,0},{4,6},{6,4},{8,10},{10,8},{12,14},{14,12},{1,3},{3,1},... | collective-permute-start | bytes 6291464 | tf_op jit(solution)/shard_map/ppermute | solution.py:128
  13.5 28.2 %collective-permute-start.3 = (bf16[1024,1024]{1,0:T(8,128)(2,1)}, bf16[1024,1024]{1,0:T(8,128)(2,1)}, u32[]{:S(2)}, u32[]{:S(2)}) collective-permute-start(bf16[1024,1024]{1,0:T(8,128)(2,1)} %constant_dynamic-slice_fusion.3), channel_id=1, source_target_pairs={{0,2},{2,0},{4,6},{6,4},{8,10},{10,8},{12,14},{14,12},{1,3},{3,1},... | collective-permute-start | bytes 6291464 | tf_op jit(solution)/shard_map/ppermute | solution.py:128
  15.2 11.4 %collective-permute-start = (bf16[384,512]{0,1:T(8,128)(2,1)S(1)}, bf16[384,512]{0,1:T(8,128)(2,1)}, u32[]{:S(2)}, u32[]{:S(2)}) collective-permute-start(bf16[384,512]{0,1:T(8,128)(2,1)S(1)} %bitcast.193), channel_id=1, source_target_pairs={{0,16},{16,0},{1,17},{17,1},{2,18},{18,2},{3,19},{19,3},{4,20},{20... | collective-permute-start | bytes 1179656 | tf_op jit(solution)/shard_map/ppermute | solution.py:161
  33.9 7.9 %collective-permute-start.1 = (bf16[4,96,1024]{2,1,0:T(8,128)(2,1)}, bf16[4,96,1024]{2,1,0:T(8,128)(2,1)}, u32[]{:S(2)}, u32[]{:S(2)}) collective-permute-start(bf16[4,96,1024]{2,1,0:T(8,128)(2,1)} %reverse_select_fusion.1), channel_id=1, source_target_pairs={{0,2},{2,0},{4,6},{6,4},{8,10},{10,8},{12,14},{14,12},{1,3},{3,1},... | collective-permute-start | bytes 2359304 | tf_op jit(solution)/shard_map/ppermute | solution.py:128
  34.9 21.3 %collective-permute-start.4 = (bf16[384,512]{0,1:T(8,128)(2,1)S(1)}, bf16[384,512]{0,1:T(8,128)(2,1)}, u32[]{:S(2)}, u32[]{:S(2)}) collective-permute-start(bf16[384,512]{0,1:T(8,128)(2,1)S(1)} %bitcast.195), channel_id=1, source_target_pairs={{0,1},{1,0},{2,3},{3,2},{4,5},{5,4},{6,7},{7,6},{8,9},{9,8},{10,11... | collective-permute-start | bytes 1179656 | tf_op jit(solution)/shard_map/ppermute | solution.py:162
  39.1 17.1 %collective-permute-start.5 = (bf16[384,512]{0,1:T(8,128)(2,1)}, bf16[384,512]{0,1:T(8,128)(2,1)S(1)}, u32[]{:S(2)}, u32[]{:S(2)}) collective-permute-start(bf16[384,512]{0,1:T(8,128)(2,1)} %collective-permute-done), channel_id=1, source_target_pairs={{0,1},{1,0},{2,3},{3,2},{4,5},{5,4},{6,7},{7,6},{8,9},{9,8},{10,11... | collective-permute-start | bytes 1179656 | tf_op jit(solution)/shard_map/ppermute | solution.py:163
  52.0 11.6 %collective-permute-start.7 = (f16[2,96,1024]{2,1,0:T(8,128)(2,1)}, f16[2,96,1024]{2,1,0:T(8,128)(2,1)}, u32[]{:S(2)}, u32[]{:S(2)}) collective-permute-start(f16[2,96,1024]{2,1,0:T(8,128)(2,1)} %get-tuple-element.98), channel_id=1, source_target_pairs={{0,4},{2,6},{12,8},{14,10},{1,5},{3,7},{13,9},{15,11},{16,20},{18,... | collective-permute-start | bytes 1179656 | tf_op jit(solution)/shard_map/ppermute | solution.py:128
  60.8 2.8 copy-start.12
  62.6 18.0 %copy-start.2 = (bf16[4,96,1024]{2,1,0:T(8,128)(2,1)}, bf16[4,96,1024]{2,1,0:T(8,128)(2,1)S(1)}, u32[]{:S(2)}) copy-start(bf16[4,96,1024]{2,1,0:T(8,128)(2,1)S(1)} %reverse_select_fusion) | copy-start | bytes 2359300
  62.6 18.0 %collective-permute-start.6 = (bf16[4,96,1024]{2,1,0:T(8,128)(2,1)S(1)}, bf16[4,96,1024]{2,1,0:T(8,128)(2,1)S(1)}, u32[]{:S(2)}, u32[]{:S(2)}) collective-permute-start(bf16[4,96,1024]{2,1,0:T(8,128)(2,1)S(1)} %reverse_select_fusion), channel_id=1, source_target_pairs={{0,2},{2,0},{4,6},{6,4},{8,10},{10,8},{12,14},{14,12},{1,3},{3,1},... | collective-permute-start | bytes 2359304 | tf_op jit(solution)/shard_map/ppermute | solution.py:128
  63.7 24.2 %collective-permute-start.10 = (f16[2,96,1024]{2,1,0:T(8,128)(2,1)S(1)}, f16[2,96,1024]{2,1,0:T(8,128)(2,1)S(1)}, u32[]{:S(2)}, u32[]{:S(2)}) collective-permute-start(f16[2,96,1024]{2,1,0:T(8,128)(2,1)S(1)} %convert_element_type.119), channel_id=1, source_target_pairs={{0,4},{2,6},{12,8},{14,10},{1,5},{3,7},{13,9},{15,11},{16,20},{18,... | collective-permute-start | bytes 1179656 | tf_op jit(solution)/shard_map/ppermute | solution.py:128
  69.2 18.7 %collective-permute-start.8 = (f16[2,96,1024]{2,1,0:T(8,128)(2,1)S(1)}, f16[2,96,1024]{2,1,0:T(8,128)(2,1)S(1)}, u32[]{:S(2)}, u32[]{:S(2)}) collective-permute-start(f16[2,96,1024]{2,1,0:T(8,128)(2,1)S(1)} %add_convert_fusion.2), channel_id=1, source_target_pairs={{4,8},{6,10},{8,4},{10,6},{5,9},{7,11},{9,5},{11,7},{20,24},{22,26... | collective-permute-start | bytes 1179656 | tf_op jit(solution)/shard_map/ppermute | solution.py:128
  69.9 7.9 %collective-permute-start.13 = (bf16[48,3584]{1,0:T(8,128)(2,1)S(1)}, bf16[48,3584]{1,0:T(8,128)(2,1)S(1)}, u32[]{:S(2)}, u32[]{:S(2)}) collective-permute-start(bf16[48,3584]{1,0:T(8,128)(2,1)S(1)} %constant_dynamic-slice_fusion.2), channel_id=1, source_target_pairs={{0,1},{1,0},{2,3},{3,2},{4,5},{5,4},{6,7},{7,6},{8,9},{9,8},{10,11... | collective-permute-start | bytes 1032200 | tf_op jit(solution)/shard_map/ppermute | solution.py:197
  77.9 17.5 %collective-permute-start.14 = (bf16[2,48,1792]{2,1,0:T(8,128)(2,1)S(1)}, bf16[2,48,1792]{2,1,0:T(8,128)(2,1)S(1)}, u32[]{:S(2)}, u32[]{:S(2)}) collective-permute-start(bf16[2,48,1792]{2,1,0:T(8,128)(2,1)S(1)} %get-tuple-element.124), channel_id=1, source_target_pairs={{0,2},{2,0},{4,6},{6,4},{8,10},{10,8},{12,14},{14,12},{1,3},{3,1},... | collective-permute-start | bytes 1032200 | tf_op jit(solution)/shard_map/ppermute | solution.py:128
  80.6 7.3 %copy-start.7 = (f32[4,2,96,1024]{3,2,1,0:T(8,128)S(1)}, f32[4,2,96,1024]{3,2,1,0:T(8,128)}, u32[]{:S(2)}) copy-start(f32[4,2,96,1024]{3,2,1,0:T(8,128)} %shard_map.76) | copy-start | bytes 9437188
  87.9 4.5 %copy-start.6 = (f32[4,2,96,1024]{3,2,1,0:T(8,128)S(1)}, f32[4,2,96,1024]{3,2,1,0:T(8,128)}, u32[]{:S(2)}) copy-start(f32[4,2,96,1024]{3,2,1,0:T(8,128)} %shard_map.77) | copy-start | bytes 9437188
  88.2 7.5 %collective-permute-start.11 = (f16[2,96,1024]{2,1,0:T(8,128)(2,1)S(1)}, f16[2,96,1024]{2,1,0:T(8,128)(2,1)S(1)}, u32[]{:S(2)}, u32[]{:S(2)}) collective-permute-start(f16[2,96,1024]{2,1,0:T(8,128)(2,1)S(1)} %get-tuple-element.96), channel_id=1, source_target_pairs={{4,8},{6,10},{8,4},{10,6},{5,9},{7,11},{9,5},{11,7},{20,24},{22,26... | collective-permute-start | bytes 1179656 | tf_op jit(solution)/shard_map/ppermute | solution.py:128
  89.0 5.7 %copy-start.13 = (bf16[1024,768]{1,0:T(8,128)(2,1)S(1)}, bf16[1024,768]{1,0:T(8,128)(2,1)}, u32[]{:S(2)}) copy-start(bf16[1024,768]{1,0:T(8,128)(2,1)} %constant_dynamic-slice_fusion) | copy-start | bytes 4718596
  89.1 6.4 %copy-start.14 = (bf16[1024,768]{1,0:T(8,128)(2,1)S(1)}, bf16[1024,768]{1,0:T(8,128)(2,1)}, u32[]{:S(2)}) copy-start(bf16[1024,768]{1,0:T(8,128)(2,1)} %constant_dynamic-slice_fusion.1) | copy-start | bytes 4718596
  89.1 12.6 %collective-permute-start.9 = (f16[2,96,1024]{2,1,0:T(8,128)(2,1)S(1)}, f16[2,96,1024]{2,1,0:T(8,128)(2,1)S(1)}, u32[]{:S(2)}, u32[]{:S(2)}) collective-permute-start(f16[2,96,1024]{2,1,0:T(8,128)(2,1)S(1)} %get-tuple-element.95), channel_id=1, source_target_pairs={{0,4},{2,6},{12,8},{14,10},{4,0},{6,2},{8,12},{10,14},{1,5},{3,7},... | collective-permute-start | bytes 1179656 | tf_op jit(solution)/shard_map/ppermute | solution.py:128
  92.6 16.4 %collective-permute-start.12 = (f16[2,96,1024]{2,1,0:T(8,128)(2,1)S(1)}, f16[2,96,1024]{2,1,0:T(8,128)(2,1)S(1)}, u32[]{:S(2)}, u32[]{:S(2)}) collective-permute-start(f16[2,96,1024]{2,1,0:T(8,128)(2,1)S(1)} %convert_element_type.124), channel_id=1, source_target_pairs={{0,4},{2,6},{12,8},{14,10},{1,5},{3,7},{13,9},{15,11},{16,20},{18,... | collective-permute-start | bytes 1179656 | tf_op jit(solution)/shard_map/ppermute | solution.py:128
  94.7 26.1 %collective-permute-start.18 = (bf16[1024,768]{1,0:T(8,128)(2,1)S(1)}, bf16[1024,768]{1,0:T(8,128)(2,1)S(1)}, u32[]{:S(2)}, u32[]{:S(2)}) collective-permute-start(bf16[1024,768]{1,0:T(8,128)(2,1)S(1)} %copy-done.13), channel_id=1, source_target_pairs={{0,2},{2,0},{4,6},{6,4},{8,10},{10,8},{12,14},{14,12},{1,3},{3,1},... | collective-permute-start | bytes 4718600 | tf_op jit(solution)/shard_map/ppermute | solution.py:128
  95.4 25.4 %collective-permute-start.17 = (bf16[1024,768]{1,0:T(8,128)(2,1)S(1)}, bf16[1024,768]{1,0:T(8,128)(2,1)S(1)}, u32[]{:S(2)}, u32[]{:S(2)}) collective-permute-start(bf16[1024,768]{1,0:T(8,128)(2,1)S(1)} %copy-done.14), channel_id=1, source_target_pairs={{0,2},{2,0},{4,6},{6,4},{8,10},{10,8},{12,14},{14,12},{1,3},{3,1},... | collective-permute-start | bytes 4718600 | tf_op jit(solution)/shard_map/ppermute | solution.py:128
  101.9 1.6 copy-start.8
  102.3 15.2 %collective-permute-start.15 = (bf16[2,96,1024]{2,1,0:T(8,128)(2,1)S(1)}, bf16[2,96,1024]{2,1,0:T(8,128)(2,1)S(1)}, u32[]{:S(2)}, u32[]{:S(2)}) collective-permute-start(bf16[2,96,1024]{2,1,0:T(8,128)(2,1)S(1)} %pad_maximum_fusion.5), channel_id=1, source_target_pairs={{0,4},{2,6},{12,8},{14,10},{4,0},{6,2},{8,12},{10,14},{1,5},{3,7},... | collective-permute-start | bytes 1179656 | tf_op jit(solution)/shard_map/ppermute | solution.py:128
  103.7 14.4 %copy-start.9 = (bf16[384,1024]{1,0:T(8,128)(2,1)S(1)}, bf16[384,1024]{1,0:T(8,128)(2,1)}, u32[]{:S(2)}) copy-start(bf16[384,1024]{1,0:T(8,128)(2,1)} %copy.34) | copy-start | bytes 2359300
  103.7 16.1 %collective-permute-start.16 = (bf16[2,96,1024]{2,1,0:T(8,128)(2,1)S(1)}, bf16[2,96,1024]{2,1,0:T(8,128)(2,1)S(1)}, u32[]{:S(2)}, u32[]{:S(2)}) collective-permute-start(bf16[2,96,1024]{2,1,0:T(8,128)(2,1)S(1)} %pad_maximum_fusion.5), channel_id=1, source_target_pairs={{4,8},{6,10},{8,4},{10,6},{5,9},{7,11},{9,5},{11,7},{20,24},{22,26... | collective-permute-start | bytes 1179656 | tf_op jit(solution)/shard_map/ppermute | solution.py:128
  109.1 21.0 %collective-permute-start.24 = (f16[2,96,1024]{2,1,0:T(8,128)(2,1)S(1)}, f16[2,96,1024]{2,1,0:T(8,128)(2,1)S(1)}, u32[]{:S(2)}, u32[]{:S(2)}) collective-permute-start(f16[2,96,1024]{2,1,0:T(8,128)(2,1)S(1)} %convert_element_type.130), channel_id=1, source_target_pairs={{0,4},{2,6},{12,8},{14,10},{1,5},{3,7},{13,9},{15,11},{16,20},{18,... | collective-permute-start | bytes 1179656 | tf_op jit(solution)/shard_map/ppermute | solution.py:128
  117.4 12.6 %collective-permute-start.22 = (f16[2,96,1024]{2,1,0:T(8,128)(2,1)S(1)}, f16[2,96,1024]{2,1,0:T(8,128)(2,1)S(1)}, u32[]{:S(2)}, u32[]{:S(2)}) collective-permute-start(f16[2,96,1024]{2,1,0:T(8,128)(2,1)S(1)} %add_convert_fusion.1), channel_id=1, source_target_pairs={{4,8},{6,10},{8,4},{10,6},{5,9},{7,11},{9,5},{11,7},{20,24},{22,26... | collective-permute-start | bytes 1179656 | tf_op jit(solution)/shard_map/ppermute | solution.py:128
  120.1 18.5 %collective-permute-start.20 = (bf16[2,96,1024]{2,1,0:T(8,128)(2,1)S(1)}, bf16[2,96,1024]{2,1,0:T(8,128)(2,1)S(1)}, u32[]{:S(2)}, u32[]{:S(2)}) collective-permute-start(bf16[2,96,1024]{2,1,0:T(8,128)(2,1)S(1)} %collective-permute-done.15), channel_id=1, source_target_pairs={{4,8},{6,10},{8,4},{10,6},{5,9},{7,11},{9,5},{11,7},{20,24},{22,26... | collective-permute-start | bytes 1179656 | tf_op jit(solution)/shard_map/ppermute | solution.py:128
  120.8 1.1 copy-start.15
  130.4 15.6 %collective-permute-start.23 = (f16[2,96,1024]{2,1,0:T(8,128)(2,1)S(1)}, f16[2,96,1024]{2,1,0:T(8,128)(2,1)S(1)}, u32[]{:S(2)}, u32[]{:S(2)}) collective-permute-start(f16[2,96,1024]{2,1,0:T(8,128)(2,1)S(1)} %get-tuple-element.91), channel_id=1, source_target_pairs={{0,4},{2,6},{12,8},{14,10},{4,0},{6,2},{8,12},{10,14},{1,5},{3,7},... | collective-permute-start | bytes 1179656 | tf_op jit(solution)/shard_map/ppermute | solution.py:128
  136.6 9.4 %collective-permute-start.25 = (f16[2,96,1024]{2,1,0:T(8,128)(2,1)S(1)}, f16[2,96,1024]{2,1,0:T(8,128)(2,1)S(1)}, u32[]{:S(2)}, u32[]{:S(2)}) collective-permute-start(f16[2,96,1024]{2,1,0:T(8,128)(2,1)S(1)} %get-tuple-element.92), channel_id=1, source_target_pairs={{4,8},{6,10},{8,4},{10,6},{5,9},{7,11},{9,5},{11,7},{20,24},{22,26... | collective-permute-start | bytes 1179656 | tf_op jit(solution)/shard_map/ppermute | solution.py:128
  137.3 14.7 %collective-permute-start.19 = (bf16[2,96,1024]{2,1,0:T(8,128)(2,1)S(1)}, bf16[2,96,1024]{2,1,0:T(8,128)(2,1)S(1)}, u32[]{:S(2)}, u32[]{:S(2)}) collective-permute-start(bf16[2,96,1024]{2,1,0:T(8,128)(2,1)S(1)} %collective-permute-done.16), channel_id=1, source_target_pairs={{4,0},{6,2},{8,12},{10,14},{5,1},{7,3},{9,13},{11,15},{20,16},{22,... | collective-permute-start | bytes 1179656 | tf_op jit(solution)/shard_map/ppermute | solution.py:128
  138.6 21.9 %collective-permute-start.21 = (bf16[2,96,1024]{2,1,0:T(8,128)(2,1)S(1)}, bf16[2,96,1024]{2,1,0:T(8,128)(2,1)S(1)}, u32[]{:S(2)}, u32[]{:S(2)}) collective-permute-start(bf16[2,96,1024]{2,1,0:T(8,128)(2,1)S(1)} %collective-permute-done.20), channel_id=1, source_target_pairs={{4,0},{6,2},{8,12},{10,14},{5,1},{7,3},{9,13},{11,15},{20,16},{22,... | collective-permute-start | bytes 1179656 | tf_op jit(solution)/shard_map/ppermute | solution.py:128
  141.3 21.3 %collective-permute-start.26 = (f16[2,192,768]{2,1,0:T(8,128)(2,1)S(1)}, f16[2,192,768]{2,1,0:T(8,128)(2,1)S(1)}, u32[]{:S(2)}, u32[]{:S(2)}) collective-permute-start(f16[2,192,768]{2,1,0:T(8,128)(2,1)S(1)} %convert_element_type.134), channel_id=1, source_target_pairs={{0,4},{2,6},{12,8},{14,10},{1,5},{3,7},{13,9},{15,11},{16,20},{18,... | collective-permute-start | bytes 1769480 | tf_op jit(solution)/shard_map/ppermute | solution.py:128
  146.1 16.5 %slice-start = ((s8[4718592]{0:T(1024)(128)(4,1)}), s8[4194304]{0:T(1024)(128)(4,1)S(1)}, s32[]{:S(2)}) async-start(s8[4718592]{0:T(1024)(128)(4,1)} %bitcast.184), calls=%async_computation.1 | async-start | bytes 8388608
  146.6 15.9 %slice-start.1 = ((s8[4718592]{0:T(1024)(128)(4,1)}), s8[524288]{0:T(1024)(128)(4,1)S(1)}, s32[]{:S(2)}) async-start(s8[4718592]{0:T(1024)(128)(4,1)} %bitcast.184), calls=%async_computation.2 | async-start | bytes 1048576
  162.7 10.9 %collective-permute-start.29 = (f16[2,192,768]{2,1,0:T(8,128)(2,1)S(1)}, f16[2,192,768]{2,1,0:T(8,128)(2,1)S(1)}, u32[]{:S(2)}, u32[]{:S(2)}) collective-permute-start(f16[2,192,768]{2,1,0:T(8,128)(2,1)S(1)} %convert_element_type.140), channel_id=1, source_target_pairs={{0,4},{2,6},{12,8},{14,10},{1,5},{3,7},{13,9},{15,11},{16,20},{18,... | collective-permute-start | bytes 1769480 | tf_op jit(solution)/shard_map/ppermute | solution.py:128
  164.3 9.4 %collective-permute-start.27 = (f16[2,192,768]{2,1,0:T(8,128)(2,1)S(1)}, f16[2,192,768]{2,1,0:T(8,128)(2,1)S(1)}, u32[]{:S(2)}, u32[]{:S(2)}) collective-permute-start(f16[2,192,768]{2,1,0:T(8,128)(2,1)S(1)} %fusion), channel_id=1, source_target_pairs={{4,8},{6,10},{8,4},{10,6},{5,9},{7,11},{9,5},{11,7},{20,24},{22,26... | collective-permute-start | bytes 1769480 | tf_op jit(solution)/shard_map/ppermute | solution.py:128
  174.2 22.3 %collective-permute-start.28 = (f16[2,192,768]{2,1,0:T(8,128)(2,1)S(1)}, f16[2,192,768]{2,1,0:T(8,128)(2,1)S(1)}, u32[]{:S(2)}, u32[]{:S(2)}) collective-permute-start(f16[2,192,768]{2,1,0:T(8,128)(2,1)S(1)} %get-tuple-element.89), channel_id=1, source_target_pairs={{0,4},{2,6},{12,8},{14,10},{4,0},{6,2},{8,12},{10,14},{1,5},{3,7},... | collective-permute-start | bytes 1769480 | tf_op jit(solution)/shard_map/ppermute | solution.py:128
  177.7 18.8 %collective-permute-start.30 = (f16[2,192,768]{2,1,0:T(8,128)(2,1)S(1)}, f16[2,192,768]{2,1,0:T(8,128)(2,1)S(1)}, u32[]{:S(2)}, u32[]{:S(2)}) collective-permute-start(f16[2,192,768]{2,1,0:T(8,128)(2,1)S(1)} %get-tuple-element.90), channel_id=1, source_target_pairs={{4,8},{6,10},{8,4},{10,6},{5,9},{7,11},{9,5},{11,7},{20,24},{22,26... | collective-permute-start | bytes 1769480 | tf_op jit(solution)/shard_map/ppermute | solution.py:128
  178.4 17.4 %collective-permute-start.33 = (bf16[2,96,1024]{2,1,0:T(8,128)(2,1)S(1)}, bf16[2,96,1024]{2,1,0:T(8,128)(2,1)S(1)}, u32[]{:S(2)}, u32[]{:S(2)}) collective-permute-start(bf16[2,96,1024]{2,1,0:T(8,128)(2,1)S(1)} %pad_maximum_fusion.6), channel_id=1, source_target_pairs={{0,4},{2,6},{12,8},{14,10},{4,0},{6,2},{8,12},{10,14},{1,5},{3,7},... | collective-permute-start | bytes 1179656 | tf_op jit(solution)/shard_map/ppermute | solution.py:128
  195.8 2.3 collective-permute-start.34
  198.1 0.7 collective-permute-start.36
  198.8 22.8 %collective-permute-start.37 = (bf16[2,96,1024]{2,1,0:T(8,128)(2,1)S(1)}, bf16[2,96,1024]{2,1,0:T(8,128)(2,1)}, u32[]{:S(2)}, u32[]{:S(2)}) collective-permute-start(bf16[2,96,1024]{2,1,0:T(8,128)(2,1)S(1)} %collective-permute-done.36), channel_id=1, source_target_pairs={{4,0},{6,2},{8,12},{10,14},{5,1},{7,3},{9,13},{11,15},{20,16},{22,... | collective-permute-start | bytes 1179656 | tf_op jit(solution)/shard_map/ppermute | solution.py:128
  200.1 55.3 %collective-permute-start.38 = (bf16[2,96,1024]{2,1,0:T(8,128)(2,1)S(1)}, bf16[2,96,1024]{2,1,0:T(8,128)(2,1)}, u32[]{:S(2)}, u32[]{:S(2)}) collective-permute-start(bf16[2,96,1024]{2,1,0:T(8,128)(2,1)S(1)} %collective-permute-done.34), channel_id=1, source_target_pairs={{4,0},{6,2},{8,12},{10,14},{5,1},{7,3},{9,13},{11,15},{20,16},{22,... | collective-permute-start | bytes 1179656 | tf_op jit(solution)/shard_map/ppermute | solution.py:128
  201.4 88.9 %collective-permute-start.35 = (bf16[4,2,96,1024]{3,2,1,0:T(8,128)(2,1)}, bf16[4,2,96,1024]{3,2,1,0:T(8,128)(2,1)}, u32[]{:S(2)}, u32[]{:S(2)}) collective-permute-start(bf16[4,2,96,1024]{3,2,1,0:T(8,128)(2,1)} %get-tuple-element.102), channel_id=1, source_target_pairs={{0,2},{2,0},{4,6},{6,4},{8,10},{10,8},{12,14},{14,12},{1,3},{3,1},... | collective-permute-start | bytes 4718600 | tf_op jit(solution)/shard_map/ppermute | solution.py:128
  255.7 21.1 %collective-permute-start.31 = (bf16[2,48,1792]{2,1,0:T(8,128)(2,1)S(1)}, bf16[2,48,1792]{2,1,0:T(8,128)(2,1)S(1)}, u32[]{:S(2)}, u32[]{:S(2)}) collective-permute-start(bf16[2,48,1792]{2,1,0:T(8,128)(2,1)S(1)} %get-tuple-element.120), channel_id=1, source_target_pairs={{0,2},{2,0},{4,6},{6,4},{8,10},{10,8},{12,14},{14,12},{1,3},{3,1},... | collective-permute-start | bytes 1032200 | tf_op jit(solution)/shard_map/ppermute | solution.py:128
  276.8 1.5 copy-start.3
  276.8 13.5 %collective-permute-start.39 = (bf16[4,2,96,1024]{3,2,1,0:T(8,128)(2,1)}, bf16[4,2,96,1024]{3,2,1,0:T(8,128)(2,1)}, u32[]{:S(2)}, u32[]{:S(2)}) collective-permute-start(bf16[4,2,96,1024]{3,2,1,0:T(8,128)(2,1)} %get-tuple-element.100), channel_id=1, source_target_pairs={{0,2},{2,0},{4,6},{6,4},{8,10},{10,8},{12,14},{14,12},{1,3},{3,1},... | collective-permute-start | bytes 4718600 | tf_op jit(solution)/shard_map/ppermute | solution.py:128
  277.1 12.3 %collective-permute-start.32 = (bf16[48,3584]{1,0:T(8,128)(2,1)S(1)}, bf16[48,3584]{1,0:T(8,128)(2,1)S(1)}, u32[]{:S(2)}, u32[]{:S(2)}) collective-permute-start(bf16[48,3584]{1,0:T(8,128)(2,1)S(1)} %get-tuple-element.118), channel_id=1, source_target_pairs={{0,1},{1,0},{2,3},{3,2},{4,5},{5,4},{6,7},{7,6},{8,9},{9,8},{10,11... | collective-permute-start | bytes 1032200 | tf_op jit(solution)/shard_map/ppermute | solution.py:285
  280.2 1.1 copy-start.10
  280.2 1.4 copy-start.11
  281.5 1.4 copy-start.4
  281.5 1.9 copy-start.5
  297.7 10.9 %copy-start.1 = (bf16[1,48,7168]{2,1,0:T(8,128)(2,1)S(1)}, bf16[1,48,7168]{2,1,0:T(8,128)(2,1)}, u32[]{:S(2)}) copy-start(bf16[1,48,7168]{2,1,0:T(8,128)(2,1)} %param.8) | copy-start | bytes 2064388
Sparse Core Ops, SparseCore 0:
  198.2 75.9 all-gather.2

commit v6 on v5

--- a/solution.py
+++ b/solution.py
@@ -12,7 +12,7 @@
 LARGEST_TOKEN, LARGEST_WEIGHT = 6.0, 0.0625
 VMEM_LIMIT = 48 * 2**20
 NO_COST = pl.CostEstimate(flops=0, bytes_accessed=0, transcendentals=0)
-SHARES = (4, 3)
+SHARES = (2, 2, 2, 1)
 
 
 def forward_kernel(
@@ -53,42 +53,54 @@
 
 
 def gradient_kernel(batches, place_ref, features_ref, *refs):
-    acts, outs = refs[:batches], refs[-2:]
-    for which, out_ref in enumerate(outs):
-        parts = []
-        for act_ref in acts:
-            blocks, _, _, rows, width = act_ref.shape
-            rows = rows * batches // 2
-            for i in range(2 // batches):
-                part = act_ref[:, 0, which, i * rows : (i + 1) * rows]
-                parts.append(part.reshape(blocks * rows, width))
-        out_ref[...] = jnp.dot(
-            features_ref[...], jnp.concatenate(parts), preferred_element_type=jnp.float32
-        )
-
-
-def gradient(place, features, acts, totals, columns, start, tile):
+    own, other, outs = refs[: 2 * batches], refs[2 * batches : 4 * batches], refs[-2:]
+
+    def fill(acts):
+        for which, out_ref in enumerate(outs):
+            parts = []
+            for batch in range(2):
+                for act_ref in acts if batches == 1 else acts[2 * batch : 2 * batch + 2]:
+                    blocks, _, rows, width = act_ref.shape
+                    rows = rows * batches // 2
+                    first = batch * rows if batches == 1 else 0
+                    part = act_ref[:, which, first : first + rows]
+                    parts.append(part.reshape(blocks * rows, width))
+            out_ref[...] = jnp.dot(
+                features_ref[...], jnp.concatenate(parts), preferred_element_type=jnp.float32
+            )
+
+    for which, acts in enumerate((own, other)):
+        pl.when(pl.program_id(0) == which)(functools.partial(fill, acts))
+
+
+def gradient(place, features, own, other, totals, columns, start, tile):
     depth, total = features.shape
-    blocks, cores, _, rows, width = acts[0].shape
-    act_spec = pl.BlockSpec((blocks, 1, 2, rows, tile), lambda i, j, place: (0, i, 0, 0, j))
+    blocks, _, rows, width = own[0].shape
+    tiles = width // tile
+    shape = (blocks, 2, rows, tile)
+    own_spec = pl.BlockSpec(
+        shape, lambda i, j, place: (0, 0, 0, jnp.where(i == 0, j, tiles - 1))
+    )
+    other_spec = pl.BlockSpec(shape, lambda i, j, place: (0, 0, 0, jnp.where(i == 0, 0, j)))
     out_spec = pl.BlockSpec((depth, tile), lambda i, j, place: (0, place[i] + start // tile + j))
     out_shape = jax.ShapeDtypeStruct((depth, columns), jnp.float32)
     in_specs = [pl.BlockSpec((depth, total), lambda i, j, place: (0, 0))]
-    in_specs += [act_spec] * len(acts)
+    in_specs += [own_spec] * len(own) + [other_spec] * len(other)
     in_specs += [pl.BlockSpec(memory_space=pl.ANY)] * len(totals)
+    first = 2 + len(own) + len(other)
     return pl.pallas_call(
-        functools.partial(gradient_kernel, len(acts)),
+        functools.partial(gradient_kernel, len(own) // 2),
         out_shape=(out_shape, out_shape),
         grid_spec=pltpu.PrefetchScalarGridSpec(
             num_scalar_prefetch=1,
-            grid=(cores, width // tile),
+            grid=(2, tiles),
             in_specs=in_specs,
             out_specs=(out_spec, out_spec),
         ),
-        input_output_aliases={2 + len(acts) + i: i for i in range(len(totals))},
+        input_output_aliases={first + i: i for i in range(len(totals))},
         compiler_params=pltpu.CompilerParams(vmem_limit_bytes=VMEM_LIMIT),
         cost_estimate=NO_COST,
-    )(place, features, *acts, *totals)
+    )(place, features, *own, *other, *totals)
 
 
 def tie(value, *after):
@@ -103,7 +115,7 @@
 def local(tokens, gate_weight, up_weight, grad_hidden):
     line = 4
     row, col, part = (lax.axis_index(name) for name in ("row", "col", "depth"))
-    place, core = col // 2, col % 2
+    chip, core = col // 2, col % 2
     slab = grad_hidden.shape[1]
     rows = 2 * slab
     depth, columns = gate_weight.shape
@@ -120,9 +132,9 @@
         return [(2 * i + c, 2 * j + c) for i, j in hops for c in (0, 1)]
 
     inward, outward = between([(0, 1), (3, 2)]), between([(1, 0), (2, 3)])
-    side, centre = inward + outward, between([(1, 2), (2, 1)])
-    at_end = (place == 0) | (place == line - 1)
-    at_far = 2 * place >= line
+    centre = between([(1, 2), (2, 1)])
+    at_end = (chip == 0) | (chip == line - 1)
+    at_far = 2 * chip >= line
 
     def send(value, route):
         return lax.ppermute(value, "col", route)
@@ -181,16 +193,17 @@
 
     features = [by(row == 0, mine, over_row, 1)]
     spread = [both_cores(features[0], ())]
-    terms = multiply(0, spread[0], ())
-    payload = terms[3].astype(WIRE)
-    in_1 = send(payload, inward)
+    terms = {0: multiply(0, spread[0], ())}
+    payload = terms[0].astype(WIRE)
+    inner = {0: send(payload, inward)}
 
     over_depth, over_both = tie((over_depth, over_both), payload)
     features.append(by(row == 0, over_depth, over_both, 1))
     spread.append(both_cores(features[1], ()))
-    far_weights[2] = exchange_weights(2, spread[1])
-
-    mine_cotangent, cotangent = tie((grad_hidden[0], grad_hidden[0]), in_1)
+    for k in range(2, last + 1):
+        far_weights[k] = exchange_weights(k, spread[1] if k < 4 else inner[0])
+
+    mine_cotangent, cotangent = tie((grad_hidden[0], grad_hidden[0]), payload)
     cotangent = jnp.stack(
         [
             columns_of(mine_cotangent, part * half, half),
@@ -203,82 +216,85 @@
         send(columns_of(cotangent, (1 - core) * share, share), pairs),
         1,
     )
+    cotangent = jnp.stack([send(cotangent, inward), cotangent])
 
     def activate(k, summed):
         batches, start, width = pieces[k]
-        summed = (summed * (1.0 / scale)).reshape(2, len(batches), rows, width)
-        gate_sum, up_sum = summed[0], summed[1]
+        summed = (summed * (1.0 / scale)).reshape(2, 2, len(batches), rows, width)
+        gate_sum, up_sum = summed[:, 0], summed[:, 1]
         squash = jax.nn.sigmoid(gate_sum)
         product = (gate_sum * squash * up_sum).astype(jnp.bfloat16)
-        for position, batch in enumerate(batches):
-            hidden[batch].append(product[position])
-        given = jnp.stack([wide(cotangent[b][:, start : start + width]) for b in batches])
+        given = wide(cotangent[:, batches[0] : batches[-1] + 1, :, start : start + width])
         gate_act = given * up_sum * squash * (1.0 + gate_sum * (1.0 - squash))
         up_act = given * gate_sum * squash
-        act = jnp.stack([gate_act, up_act]).astype(jnp.bfloat16)
-        return act.reshape(2, len(batches) * rows, width)
-
-    def merge(act, side_1, centre_1, out_2, share_2, out_3):
-        blocks = jnp.stack(
-            [
-                jnp.where(at_end, act, side_1),
-                jnp.where(at_end, side_1, act),
-                jnp.where(at_end, out_2, centre_1),
-                jnp.where(at_end, out_3, share_2),
+        act = jnp.stack([gate_act, up_act], axis=1).astype(jnp.bfloat16)
+        return product, act.reshape(2, 2, len(batches) * rows, width)
+
+    def by_side(values):
+        values = values.reshape(line, rows * depth)
+        values = jnp.concatenate([values[:2], values[3:], values[2:3]])
+        return values.reshape(-1, depth)
+
+    turned = jnp.concatenate([by_side(tie(near, inner[0])) for near, _ in spread]).T
+    place = jnp.stack([core, 1 - core]).astype(jnp.int32) * (share // tile)
+
+    def outer_hidden(ks):
+        def joined(batch, which):
+            chosen = [
+                hidden[k][which, pieces[k][0].index(batch)] for k in ks if batch in pieces[k][0]
             ]
-        )
-        return blocks, send(blocks, pairs)
-
-    turned = jnp.concatenate([tie(near, in_1).reshape(-1, depth) for near, _ in spread]).T
-    turned_in_place = jnp.concatenate([tie(value, in_1) for value in features]).T
-
-    def finish(gathered, totals, start):
-        own, other = [value for value, _ in gathered], [value for _, value in gathered]
-        for values, owner in ((own, core), (other, 1 - core)):
-            where = (owner * (share // tile)).astype(jnp.int32).reshape(1)
-            values = [value[:, None] for value in values]
-            totals = gradient(where, turned, values, totals, half, start, tile)
-        return totals
-
-    hidden, totals, waiting = ([], []), (), []
-    act = hops = None
-    for k in range(-1, last):
-        if act is not None:
-            side_1, centre_1 = send(act, side), send(act, centre)
-        if hops is not None:
-            waiting.append(merge(*hops))
-            terms = tie(terms, waiting[-1][0])
-        far = add(terms[3], in_1).astype(WIRE)
-        centre_2 = send(far, centre)
-        in_2 = send(tie(terms[2], in_1).astype(WIRE), inward)
-        if act is not None:
-            out_2, share_2 = send(centre_1, outward), send(side_1, centre)
-        following = None
-        if k + 2 <= last:
-            tokens = spread[1] if k < 0 else [jnp.stack(pair, axis=1) for pair in zip(*spread)]
-            following = multiply(k + 2, tokens, (in_1, *(() if act is None else (side_1, centre_1))))
-            terms = tie(terms, following)
-        near = add(terms[2], in_2).astype(WIRE)
-        swapped = jnp.where(at_end, terms[1], add(terms[0], centre_2)).astype(WIRE)
-        centre_3, side_3 = send(near, centre), send(swapped, side)
-        if following is not None:
-            in_1 = send(tie(following[3], near, swapped).astype(WIRE), inward)
-        if act is not None:
-            out_3 = send(share_2, outward)
-        own = jnp.where(at_end, terms[0], terms[1])
-        ready = activate(k + 1, add(own, side_3, centre_3))
-        if act is not None:
-            hops = tie((act, side_1, centre_1, out_2, share_2, out_3), ready)
-        act, terms = ready, following
-
-    everything = lax.all_gather(tie(act, share_2), "col", axis=0).reshape(line, 2, *act.shape)
-    waiting.append(merge(*hops))
-    totals = finish(waiting, totals, pieces[0][1])
-    places = jnp.array([0, share // tile], jnp.int32)
-    totals = gradient(places, turned_in_place, [everything], totals, half, pieces[last][1], tile)
-
-    hidden = jnp.stack([jnp.concatenate(parts, axis=1) for parts in hidden])
-    hidden = hidden.reshape(2, 2, slab, share)
+            return jnp.concatenate(chosen, axis=1)
+
+        own = [joined(batch, 1) for batch in range(2)]
+        theirs = send(jnp.stack([joined(batch, 0) for batch in range(2)]), outward)
+        return jnp.where(at_end, theirs, jnp.stack(own))
+
+    got, act, hidden, near_out, far_out, across = {}, {}, {}, {}, {}, {}
+    totals, waiting, hiddens = (), [], []
+    for t in range(last + 3):
+        before = []
+        k = t - 1
+        if 0 <= k <= last:
+            summed = jnp.stack([terms[k][0] + wide(got[k][1]), terms[k][1] + wide(got[k][0])])
+            hidden[k], act[k] = activate(k, summed)
+            across[k], near_out[k] = send(act[k], centre), send(act[k], outward)
+            before.append(act[k])
+            if k == last - 1:
+                hiddens.append(outer_hidden(range(last)))
+            if k == last:
+                hiddens.append(outer_hidden([last]))
+        k = t - 2
+        if 0 <= k <= last:
+            near_mine, near_got, far_mine, far_got = tie(
+                (act[k], near_out[k], across[k], far_out[k]), before
+            )
+            mine = [
+                jnp.where(at_end, near_got, near_mine),
+                jnp.where(at_end, far_got, far_mine),
+            ]
+            waiting.append((mine, [send(value, pairs) for value in mine]))
+        k = t + 1
+        if k <= last:
+            tokens = spread[1] if k == 1 else [jnp.stack(pair, axis=1) for pair in zip(*spread)]
+            terms[k] = multiply(k, tokens, before)
+            payload = terms[k].astype(WIRE)
+            inner[k] = send(payload, inward)
+            before.append(payload)
+        k = t - 2
+        if 0 <= k <= last and pieces[k][0] != (0,):
+            own, other = (sum(values, []) for values in zip(*waiting))
+            totals = gradient(place, turned, own, other, totals, half, pieces[k][1], tile)
+            waiting = []
+            before.append(totals)
+        k = t
+        if k <= last:
+            terms[k] = tie(terms[k], before) + wide(inner[k])
+            got[k] = send(terms[k][2:].astype(WIRE), centre)
+        k = t - 1
+        if 0 <= k <= last:
+            far_out[k] = send(across[k], outward)
+
+    hidden = jnp.concatenate(hiddens, axis=2).reshape(2, 2, slab, share)
     mine = lax.dynamic_index_in_dim(hidden, core, 1, keepdims=False)
     theirs = lax.dynamic_index_in_dim(hidden, 1 - core, 1, keepdims=False)
     hidden = by(core == 0, mine, send(theirs, pairs), 2)

time: 318 us -> 333 us (1.047)
  starting transfers between devices: 83.7 us -> 96.7 us
  between operations: 14.8 us -> 1.8 us
  other arithmetic: 27.2 us -> 37.2 us
  waiting for transfers between devices: 117 us -> 121 us
    ppermute x35 -> x50, starting transfers between devices: 77.3 us -> 90.2 us  [send(): return lax.ppermute(value, 'col', route)]
    add x0 -> x8, other arithmetic: none -> 8.09 us  [the longest x5 5.88 us: local(): terms[k] = tie(terms[k], before) + wide(inner[k])]
    ppermute x1, waiting for transfers between devices: 9.13 us -> 2.5 us  [local(): over_row = lax.ppermute(mine, 'row', swap)]
    ppermute x1, waiting for transfers between devices: 0.01 us -> 6.54 us  [local(): over_both = lax.ppermute(over_row, 'depth', swap)]
    convert_element_type x11 -> x5, other arithmetic: 3.15 us -> 9.38 us  [the longest x4 9.19 us: local(): payload = terms[k].astype(WIRE)]
    unnamed x37 -> x70, local copies, waits for them, and re-layouts: 5.37 us -> 10.6 us
    ppermute x35 -> x50, waiting for transfers between devices: 101 us -> 106 us  [send(): return lax.ppermute(value, 'col', route)]
    optimization_barrier x4 -> x3, local copies, waits for them, and re-layouts: 5.03 us -> 0.36 us  [tie(): return lax.optimization_barrier((value, after))[0]]
  transfers between devices with their start and end apart: 41 -> 55, of which waited for: 12 -> 17; matrix products, arithmetic and copies ran while one was open for 14% -> 17% of each run, Pallas kernels for 11% -> 13%
where the time goes in v6:
time: 333 us; the launch traced here: 331 us
  waiting for transfers between devices  121 us (36%)
  starting transfers between devices  96.7 us (29%)
  Pallas kernels  47.5 us (14%)
  other arithmetic  37.2 us (11%)
  local copies, waits for them, and re-layouts  26.6 us (8%)
    ppermute x50, waiting for transfers between devices, send(): return lax.ppermute(value, 'col', route)  106 us
    ppermute x50, starting transfers between devices, send(): return lax.ppermute(value, 'col', route)  90.2 us
    pallas_call x4, Pallas kernels, gradient(): pl.pallas_call(functools.partial(gradient_kernel, len(own) // 2), out_sha...  25.1 us
    pallas_call x5, Pallas kernels, forward(): pl.pallas_call(functools.partial(forward_kernel, scale), out_shape=jax.Sh...  22.4 us
    unnamed x70, local copies, waits for them, and re-layouts  10.6 us
    dynamic_slice x4, local copies, waits for them, and re-layouts, columns_of(): return lax.dynamic_slice_in_dim(array, start, width, array.ndim - 1)  9.49 us
    convert_element_type x4, other arithmetic, local(): payload = terms[k].astype(WIRE)  9.19 us
  transfers between devices with their start and end apart: 55, of which 17 were waited for; matrix products, arithmetic and copies ran while one was open for 17% of the time, Pallas kernels for 13%

profile of v6, /device:TPU:1, one launch (start us, length us, event | category | flops | bytes accessed | tf_op | source)
XLA Modules:
  0.0 330.8 jit_solution(3651292915475825681)
XLA Ops:
  0.6 2.1 collective-permute-start
  2.8 5.6 %constant_dynamic-slice_fusion.2 = (bf16[1024,512]{1,0:T(8,128)(2,1)}, bf16[1024,512]{1,0:T(8,128)(2,1)}, bf16[1024,512]{1,0:T(8,128)(2,1)}, bf16[1024,512]{1,0:...) fusion(bf16[1024,7168]{1,0:T(8,128)(2,1)} %up_ref.9, s32[]{:T(128)S(6)} %select_n.205, ...), kind=kLoop, calls=%fused_computation.168 | loop fusion | bytes 12582924 | tf_op jit(solution)/shard_map/dynamic_slice | solution.py:156
  9.3 2.5 collective-permute-done
  11.8 1.5 maximum_select_fusion
  14.4 1.3 collective-permute-start.1
  15.7 1.5 collective-permute-start.4
  17.2 1.9 constant_dynamic-slice_fusion.1
  19.2 2.0 constant_dynamic-slice_fusion
  21.4 3.5 %shard_map.67 = f32[4,2,96,512]{3,2,1,0:T(8,128)S(1)} custom-call(s32[1]{0:T(128)} %bitcast.place_ref, bf16[384,1024]{1,0:T(8,128)(2,1)S(1)} %bitcast.256, bf16[384,1024]{1,0:T(8,128)(2,1)S(1)} %bitcast.261, bf16[1024,7168]{1,0:T(8,128)(2,1)} %gate_ref.9, bf16[1024,7168]{1,0:T(8,128)(2,1)} %up_ref.9, bf16[1024,512]{1,0:T(8,128)(2,1)} %collective-permute-done.2.gate_far_ref, ...), custom_call_target="tpu_custom_call" | custom-call | tf_op jit(solution)/shard_map/pallas_call | solution.py:34
  25.1 3.5 %collective-permute-start.7 = (f16[4,2,96,512]{3,2,1,0:T(8,128)(2,1)S(1)}, f16[4,2,96,512]{3,2,1,0:T(8,128)(2,1)S(1)}, u32[]{:S(2)}, u32[]{:S(2)}) collective-permute-start(f16[4,2,96,512]{3,2,1,0:T(8,128)(2,1)S(1)} %convert_element_type.135), channel_id=1, source_target_pairs={{0,4},{2,6},{12,8},{14,10},{1,5},{3,7},{13,9},{15,11},{16,20},{18,... | collective-permute-start | bytes 2359304 | tf_op jit(solution)/shard_map/ppermute | solution.py:140
  28.6 6.5 %collective-permute-done.5 = bf16[384,512]{1,0:T(8,128)(2,1)} collective-permute-done((bf16[384,512]{1,0:T(8,128)(2,1)}, bf16[384,512]{1,0:T(8,128)(2,1)}, u32[]{:S(2)}, u32[]{:S(2)}) %collective-permute-start.5) | collective-permute-done | bytes 393248 | tf_op jit(solution)/shard_map/ppermute | solution.py:175
  35.1 1.6 maximum_select_fusion.1
  36.8 1.5 collective-permute-start.9
  39.8 5.9 %collective-permute-done.9 = bf16[48,3584]{1,0:T(8,128)(2,1)S(1)} collective-permute-done((bf16[48,3584]{1,0:T(8,128)(2,1)S(1)}, bf16[48,3584]{1,0:T(8,128)(2,1)S(1)}, u32[]{:S(2)}, u32[]{:S(2)}) %collective-permute-start.9) | collective-permute-done | bytes 344096 | tf_op jit(solution)/shard_map/ppermute | solution.py:210
  45.7 1.8 collective-permute-start.10
  48.9 3.5 %collective-permute-start.11 = (bf16[2,96,1792]{2,1,0:T(8,128)(2,1)S(1)}, bf16[2,96,1792]{2,1,0:T(8,128)(2,1)S(1)}, u32[]{:S(2)}, u32[]{:S(2)}) collective-permute-start(bf16[2,96,1792]{2,1,0:T(8,128)(2,1)S(1)} %maximum_select_fusion.2), channel_id=1, source_target_pairs={{0,4},{2,6},{12,8},{14,10},{1,5},{3,7},{13,9},{15,11},{16,20},{18,... | collective-permute-start | bytes 2064392 | tf_op jit(solution)/shard_map/ppermute | solution.py:140
  52.5 3.8 %shard_map.68 = f32[4,2,96,512]{3,2,1,0:T(8,128)S(1)} custom-call(s32[1]{0:T(128)} %bitcast.place_ref, bf16[384,1024]{1,0:T(8,128)(2,1)S(1)} %bitcast.257, bf16[384,1024]{1,0:T(8,128)(2,1)S(1)} %bitcast.263, bf16[1024,7168]{1,0:T(8,128)(2,1)} %gate_ref.9, bf16[1024,7168]{1,0:T(8,128)(2,1)} %up_ref.9, bf16[1024,512]{1,0:T(8,128)(2,1)} %collective-permute-done.2.gate_far_ref, ...), custom_call_target="tpu_custom_call" | custom-call | tf_op jit(solution)/shard_map/pallas_call | solution.py:34
  57.3 2.2 collective-permute-start.14
  62.4 4.3 %collective-permute-done.11 = bf16[2,96,1792]{2,1,0:T(8,128)(2,1)S(1)} collective-permute-done((bf16[2,96,1792]{2,1,0:T(8,128)(2,1)S(1)}, bf16[2,96,1792]{2,1,0:T(8,128)(2,1)S(1)}, u32[]{:S(2)}, u32[]{:S(2)}) %collective-permute-start.11) | collective-permute-done | bytes 688160 | tf_op jit(solution)/shard_map/ppermute | solution.py:140
  66.7 2.0 collective-permute-start.17
  69.9 6.0 %shard_map.69 = f32[4,2,192,512]{3,2,1,0:T(8,128)} custom-call(s32[1]{0:T(128)} %bitcast.place_ref, bf16[768,1024]{1,0:T(8,128)(2,1)S(1)} %bitcast.259, bf16[768,1024]{1,0:T(8,128)(2,1)S(1)} %bitcast.253, bf16[1024,7168]{1,0:T(8,128)(2,1)} %gate_ref.9, bf16[1024,7168]{1,0:T(8,128)(2,1)} %up_ref.9, ...), custom_call_target="tpu_custom_call" | custom-call | tf_op jit(solution)/shard_map/pallas_call | solution.py:34
  76.0 3.5 %convert_element_type.143 = f16[4,2,192,512]{3,2,1,0:T(8,128)(2,1)} convert(f32[4,2,192,512]{3,2,1,0:T(8,128)} %shard_map.69) | non-fusion elementwise | flops 786432 | bytes 4718592 | tf_op jit(solution)/shard_map/convert_element_type | solution.py:280
  79.5 6.5 %collective-permute-start.18 = (f16[4,2,192,512]{3,2,1,0:T(8,128)(2,1)}, f16[4,2,192,512]{3,2,1,0:T(8,128)(2,1)}, u32[]{:S(2)}, u32[]{:S(2)}) collective-permute-start(f16[4,2,192,512]{3,2,1,0:T(8,128)(2,1)} %convert_element_type.143), channel_id=1, source_target_pairs={{0,4},{2,6},{12,8},{14,10},{1,5},{3,7},{13,9},{15,11},{16,20},{18,... | collective-permute-start | bytes 4718600 | tf_op jit(solution)/shard_map/ppermute | solution.py:140
  86.0 1.4 convert_add_fusion.3
  95.4 1.3 collective-permute-start.24
  96.7 6.1 %shard_map.70 = f32[4,2,192,512]{3,2,1,0:T(8,128)} custom-call(s32[1]{0:T(128)} %bitcast.place_ref, bf16[768,1024]{1,0:T(8,128)(2,1)S(1)} %bitcast.258, bf16[768,1024]{1,0:T(8,128)(2,1)S(1)} %bitcast.254, bf16[1024,7168]{1,0:T(8,128)(2,1)} %gate_ref.9, bf16[1024,7168]{1,0:T(8,128)(2,1)} %up_ref.9, ...), custom_call_target="tpu_custom_call" | custom-call | tf_op jit(solution)/shard_map/pallas_call | solution.py:34
  102.8 3.6 %convert_element_type.147 = f16[4,2,192,512]{3,2,1,0:T(8,128)(2,1)} convert(f32[4,2,192,512]{3,2,1,0:T(8,128)} %shard_map.70) | non-fusion elementwise | flops 786432 | bytes 4718592 | tf_op jit(solution)/shard_map/convert_element_type | solution.py:280
  106.4 12.1 %collective-permute-done.18 = f16[4,2,192,512]{3,2,1,0:T(8,128)(2,1)} collective-permute-done((f16[4,2,192,512]{3,2,1,0:T(8,128)(2,1)}, f16[4,2,192,512]{3,2,1,0:T(8,128)(2,1)}, u32[]{:S(2)}, u32[]{:S(2)}) %collective-permute-start.18) | collective-permute-done | bytes 1572896 | tf_op jit(solution)/shard_map/ppermute | solution.py:140
  118.5 2.0 convert_add_fusion.1
  121.4 2.2 pad_maximum_fusion.3
  124.6 6.7 %collective-permute-done.24 = bf16[2,2,96,512]{3,2,1,0:T(8,128)(2,1)S(1)} collective-permute-done((bf16[2,2,96,512]{3,2,1,0:T(8,128)(2,1)S(1)}, bf16[2,2,96,512]{3,2,1,0:T(8,128)(2,1)S(1)}, u32[]{:S(2)}, u32[]{:S(2)}) %collective-permute-start.24) | collective-permute-done | bytes 393248 | tf_op jit(solution)/shard_map/ppermute | solution.py:140
  132.8 26.6 %collective-permute-start.32 = (f16[4,2,192,512]{3,2,1,0:T(8,128)(2,1)}, f16[4,2,192,512]{3,2,1,0:T(8,128)(2,1)}, u32[]{:S(2)}, u32[]{:S(2)}) collective-permute-start(f16[4,2,192,512]{3,2,1,0:T(8,128)(2,1)} %convert_element_type.147), channel_id=1, source_target_pairs={{0,4},{2,6},{12,8},{14,10},{1,5},{3,7},{13,9},{15,11},{16,20},{18,... | collective-permute-start | bytes 4718600 | tf_op jit(solution)/shard_map/ppermute | solution.py:140
  165.6 5.2 %collective-permute-done.27 = bf16[2,2,96,512]{3,2,1,0:T(8,128)(2,1)S(1)} collective-permute-done((bf16[2,2,96,512]{3,2,1,0:T(8,128)(2,1)S(1)}, bf16[2,2,96,512]{3,2,1,0:T(8,128)(2,1)S(1)}, u32[]{:S(2)}, u32[]{:S(2)}) %collective-permute-start.27) | collective-permute-done | bytes 393248 | tf_op jit(solution)/shard_map/ppermute | solution.py:140
  170.8 2.0 collective-permute-start.28
  173.5 2.2 pad_maximum_fusion.4
  175.7 1.8 reshape.459
  178.6 1.8 reshape.460
  181.6 1.6 maximum_bitcast_fusion.features_ref
  185.1 3.0 shard_map.71
  190.4 1.7 collective-permute-start.36
  192.0 8.2 %shard_map.72 = (f32[1024,3584]{1,0:T(8,128)}, f32[1024,3584]{1,0:T(8,128)}) custom-call(s32[2]{0:T(128)S(1)} %add_multiply_fusion.place_ref, bf16[1024,768]{1,0:T(8,128)(2,1)S(1)} %maximum_bitcast_fusion.features_ref, bf16[2,2,96,512]{3,2,1,0:T(8,128)(2,1)S(1)} %broadcast_select_fusion.9.refs_0_, ...), custom_call_target="tpu_custom_call" | custom-call | tf_op jit(solution)/shard_map/pallas_call | solution.py:91
  200.2 2.0 convert_add_fusion
  202.3 1.6 copy-done.19
  204.1 1.7 collective-permute-start.33
  205.9 3.6 %collective-permute-start.40 = (f16[4,2,192,256]{3,2,1,0:T(8,128)(2,1)}, f16[4,2,192,256]{3,2,1,0:T(8,128)(2,1)S(1)}, u32[]{:S(2)}, u32[]{:S(2)}) collective-permute-start(f16[4,2,192,256]{3,2,1,0:T(8,128)(2,1)} %convert_element_type.153), channel_id=1, source_target_pairs={{0,4},{2,6},{12,8},{14,10},{1,5},{3,7},{13,9},{15,11},{16,20},{18,... | collective-permute-start | bytes 2359304 | tf_op jit(solution)/shard_map/ppermute | solution.py:140
  209.5 1.3 collective-permute-start.35
  212.1 1.8 slice_add_fusion.1
  216.9 12.8 %collective-permute-done.35 = bf16[2,2,192,512]{3,2,1,0:T(8,128)(2,1)S(1)} collective-permute-done((bf16[2,2,192,512]{3,2,1,0:T(8,128)(2,1)}, bf16[2,2,192,512]{3,2,1,0:T(8,128)(2,1)S(1)}, u32[]{:S(2)}, u32[]{:S(2)}) %collective-permute-start.35) | collective-permute-done | bytes 786464 | tf_op jit(solution)/shard_map/ppermute | solution.py:140
  229.7 16.9 %collective-permute-done.37 = bf16[2,2,192,512]{3,2,1,0:T(8,128)(2,1)S(1)} collective-permute-done((bf16[2,2,192,512]{3,2,1,0:T(8,128)(2,1)}, bf16[2,2,192,512]{3,2,1,0:T(8,128)(2,1)S(1)}, u32[]{:S(2)}, u32[]{:S(2)}) %collective-permute-start.37) | collective-permute-done | bytes 786464 | tf_op jit(solution)/shard_map/ppermute | solution.py:140
  246.7 1.9 collective-permute-start.39
  250.5 1.6 collective-permute-start.50
  252.1 6.5 %shard_map.73 = (f32[1024,3584]{1,0:T(8,128)}, f32[1024,3584]{1,0:T(8,128)}) custom-call(s32[2]{0:T(128)S(1)} %add_multiply_fusion.place_ref, bf16[1024,768]{1,0:T(8,128)(2,1)S(1)} %maximum_bitcast_fusion.features_ref, bf16[2,2,192,512]{3,2,1,0:T(8,128)(2,1)S(1)} %broadcast_select_fusion.3.refs_0_, ...), custom_call_target="tpu_custom_call", output_to_operand_aliasing={{0}: (6, {}), {1}: (7, {})} | custom-call | tf_op jit(solution)/shard_map/pallas_call | solution.py:91
  259.6 5.6 %collective-permute-done.34 = bf16[2,96,1536]{2,1,0:T(8,128)(2,1)S(1)} collective-permute-done((bf16[2,96,1536]{2,1,0:T(8,128)(2,1)S(1)}, bf16[2,96,1536]{2,1,0:T(8,128)(2,1)S(1)}, u32[]{:S(2)}, u32[]{:S(2)}) %collective-permute-start.34) | collective-permute-done | bytes 589856 | tf_op jit(solution)/shard_map/ppermute | solution.py:140
  267.1 1.3 collective-permute-start.42
  270.4 11.6 %collective-permute-done.50 = bf16[2,2,192,512]{3,2,1,0:T(8,128)(2,1)S(1)} collective-permute-done((bf16[2,2,192,512]{3,2,1,0:T(8,128)(2,1)S(1)}, bf16[2,2,192,512]{3,2,1,0:T(8,128)(2,1)S(1)}, u32[]{:S(2)}, u32[]{:S(2)}) %collective-permute-start.50) | collective-permute-done | bytes 786464 | tf_op jit(solution)/shard_map/ppermute | solution.py:140
  282.0 16.9 %collective-permute-done.52 = bf16[2,2,192,512]{3,2,1,0:T(8,128)(2,1)S(1)} collective-permute-done((bf16[2,2,192,512]{3,2,1,0:T(8,128)(2,1)S(1)}, bf16[2,2,192,512]{3,2,1,0:T(8,128)(2,1)S(1)}, u32[]{:S(2)}, u32[]{:S(2)}) %collective-permute-start.52) | collective-permute-done | bytes 786464 | tf_op jit(solution)/shard_map/ppermute | solution.py:140
  298.8 2.1 collective-permute-done.42
  301.1 2.3 collective-permute-start.43
  305.7 1.3 collective-permute-start.44
  307.0 2.3 collective-permute-done.45
  309.4 8.4 %collective-permute-done.47 = bf16[2,2,192,256]{3,2,1,0:T(8,128)(2,1)S(1)} collective-permute-done((bf16[2,2,192,256]{3,2,1,0:T(8,128)(2,1)S(1)}, bf16[2,2,192,256]{3,2,1,0:T(8,128)(2,1)S(1)}, u32[]{:S(2)}, u32[]{:S(2)}) %collective-permute-start.47) | collective-permute-done | bytes 393248 | tf_op jit(solution)/shard_map/ppermute | solution.py:140
  317.8 1.4 collective-permute-start.49
  320.4 6.5 %shard_map.74 = (f32[1024,3584]{1,0:T(8,128)}, f32[1024,3584]{1,0:T(8,128)}) custom-call(s32[2]{0:T(128)S(1)} %add_multiply_fusion.place_ref, bf16[1024,768]{1,0:T(8,128)(2,1)S(1)} %maximum_bitcast_fusion.features_ref, bf16[2,2,192,512]{3,2,1,0:T(8,128)(2,1)S(1)} %broadcast_select_fusion.1.refs_0_, ...), custom_call_target="tpu_custom_call", output_to_operand_aliasing={{0}: (6, {}), {1}: (7, {})} | custom-call | tf_op jit(solution)/shard_map/pallas_call | solution.py:91
  326.9 3.9 %shard_map.75 = (f32[1024,3584]{1,0:T(8,128)}, f32[1024,3584]{1,0:T(8,128)}) custom-call(s32[2]{0:T(128)S(1)} %add_multiply_fusion.place_ref, bf16[1024,768]{1,0:T(8,128)(2,1)S(1)} %maximum_bitcast_fusion.features_ref, bf16[2,2,192,256]{3,2,1,0:T(8,128)(2,1)S(1)} %broadcast_select_fusion.5.refs_0_, ...), custom_call_target="tpu_custom_call", output_to_operand_aliasing={{0}: (6, {}), {1}: (7, {})} | custom-call | tf_op jit(solution)/shard_map/pallas_call | solution.py:91
  (220 shorter events, 49.8 us)
Async XLA Ops:
  0.6 28.0 %copy-start = (bf16[1,48,7168]{2,1,0:T(8,128)(2,1)S(1)}, bf16[1,48,7168]{2,1,0:T(8,128)(2,1)}, u32[]{:S(2)}) copy-start(bf16[1,48,7168]{2,1,0:T(8,128)(2,1)} %param.7) | copy-start | bytes 2064388
  0.6 11.2 %collective-permute-start = (bf16[384,512]{1,0:T(8,128)(2,1)}, bf16[384,512]{1,0:T(8,128)(2,1)S(1)}, u32[]{:S(2)}, u32[]{:S(2)}) collective-permute-start(bf16[384,512]{1,0:T(8,128)(2,1)} %bitcast.1), channel_id=1, source_target_pairs={{0,16},{16,0},{1,17},{17,1},{2,18},{18,2},{3,19},{19,3},{4,20},{20... | collective-permute-start | bytes 1179656 | tf_op jit(solution)/shard_map/ppermute | solution.py:173
  8.3 13.0 %collective-permute-start.3 = (bf16[1024,512]{1,0:T(8,128)(2,1)}, bf16[1024,512]{1,0:T(8,128)(2,1)S(1)}, u32[]{:S(2)}, u32[]{:S(2)}) collective-permute-start(bf16[1024,512]{1,0:T(8,128)(2,1)} %get-tuple-element.125), channel_id=1, source_target_pairs={{0,2},{2,0},{4,6},{6,4},{8,10},{10,8},{12,14},{14,12},{1,3},{3,1},... | collective-permute-start | bytes 3145736 | tf_op jit(solution)/shard_map/ppermute | solution.py:140
  9.3 12.1 %collective-permute-start.2 = (bf16[1024,512]{1,0:T(8,128)(2,1)}, bf16[1024,512]{1,0:T(8,128)(2,1)}, u32[]{:S(2)}, u32[]{:S(2)}) collective-permute-start(bf16[1024,512]{1,0:T(8,128)(2,1)} %get-tuple-element.172), channel_id=1, source_target_pairs={{0,2},{2,0},{4,6},{6,4},{8,10},{10,8},{12,14},{14,12},{1,3},{3,1},... | collective-permute-start | bytes 3145736 | tf_op jit(solution)/shard_map/ppermute | solution.py:140
  14.4 7.0 %collective-permute-start.1 = (bf16[4,96,1024]{2,1,0:T(8,128)(2,1)S(1)}, bf16[4,96,1024]{2,1,0:T(8,128)(2,1)S(1)}, u32[]{:S(2)}, u32[]{:S(2)}) collective-permute-start(bf16[4,96,1024]{2,1,0:T(8,128)(2,1)S(1)} %reverse_select_fusion.1), channel_id=1, source_target_pairs={{0,2},{2,0},{4,6},{6,4},{8,10},{10,8},{12,14},{14,12},{1,3},{3,1},... | collective-permute-start | bytes 2359304 | tf_op jit(solution)/shard_map/ppermute | solution.py:140
  15.7 12.9 %collective-permute-start.4 = (bf16[384,512]{1,0:T(8,128)(2,1)}, bf16[384,512]{1,0:T(8,128)(2,1)}, u32[]{:S(2)}, u32[]{:S(2)}) collective-permute-start(bf16[384,512]{1,0:T(8,128)(2,1)} %bitcast.1), channel_id=1, source_target_pairs={{0,1},{1,0},{2,3},{3,2},{4,5},{5,4},{6,7},{7,6},{8,9},{9,8},{10,11... | collective-permute-start | bytes 1179656 | tf_op jit(solution)/shard_map/ppermute | solution.py:174
  19.1 16.1 %collective-permute-start.5 = (bf16[384,512]{1,0:T(8,128)(2,1)}, bf16[384,512]{1,0:T(8,128)(2,1)}, u32[]{:S(2)}, u32[]{:S(2)}) collective-permute-start(bf16[384,512]{1,0:T(8,128)(2,1)} %copy-done.29), channel_id=1, source_target_pairs={{0,1},{1,0},{2,3},{3,2},{4,5},{5,4},{6,7},{7,6},{8,9},{9,8},{10,11... | collective-permute-start | bytes 1179656 | tf_op jit(solution)/shard_map/ppermute | solution.py:175
  25.1 34.4 %collective-permute-start.7 = (f16[4,2,96,512]{3,2,1,0:T(8,128)(2,1)S(1)}, f16[4,2,96,512]{3,2,1,0:T(8,128)(2,1)S(1)}, u32[]{:S(2)}, u32[]{:S(2)}) collective-permute-start(f16[4,2,96,512]{3,2,1,0:T(8,128)(2,1)S(1)} %convert_element_type.135), channel_id=1, source_target_pairs={{0,4},{2,6},{12,8},{14,10},{1,5},{3,7},{13,9},{15,11},{16,20},{18,... | collective-permute-start | bytes 2359304 | tf_op jit(solution)/shard_map/ppermute | solution.py:140
  36.8 8.8 %collective-permute-start.9 = (bf16[48,3584]{1,0:T(8,128)(2,1)S(1)}, bf16[48,3584]{1,0:T(8,128)(2,1)S(1)}, u32[]{:S(2)}, u32[]{:S(2)}) collective-permute-start(bf16[48,3584]{1,0:T(8,128)(2,1)S(1)} %constant_dynamic-slice_fusion.6), channel_id=1, source_target_pairs={{0,1},{1,0},{2,3},{3,2},{4,5},{5,4},{6,7},{7,6},{8,9},{9,8},{10,11... | collective-permute-start | bytes 1032200 | tf_op jit(solution)/shard_map/ppermute | solution.py:210
  38.5 13.9 %collective-permute-start.6 = (bf16[4,96,1024]{2,1,0:T(8,128)(2,1)S(1)}, bf16[4,96,1024]{2,1,0:T(8,128)(2,1)S(1)}, u32[]{:S(2)}, u32[]{:S(2)}) collective-permute-start(bf16[4,96,1024]{2,1,0:T(8,128)(2,1)S(1)} %reverse_select_fusion), channel_id=1, source_target_pairs={{0,2},{2,0},{4,6},{6,4},{8,10},{10,8},{12,14},{14,12},{1,3},{3,1},... | collective-permute-start | bytes 2359304 | tf_op jit(solution)/shard_map/ppermute | solution.py:140
  45.7 3.1 collective-permute-start.10
  47.8 45.2 %copy-start.12 = (bf16[4,2,96,1024]{3,2,0,1:T(8,128)(2,1)}, bf16[4,2,96,1024]{3,2,0,1:T(8,128)(2,1)S(1)}, u32[]{:S(2)}) copy-start(bf16[4,2,96,1024]{3,2,0,1:T(8,128)(2,1)S(1)} %pad_maximum_fusion) | copy-start | bytes 4718596
  48.9 17.9 %collective-permute-start.11 = (bf16[2,96,1792]{2,1,0:T(8,128)(2,1)S(1)}, bf16[2,96,1792]{2,1,0:T(8,128)(2,1)S(1)}, u32[]{:S(2)}, u32[]{:S(2)}) collective-permute-start(bf16[2,96,1792]{2,1,0:T(8,128)(2,1)S(1)} %maximum_select_fusion.2), channel_id=1, source_target_pairs={{0,4},{2,6},{12,8},{14,10},{1,5},{3,7},{13,9},{15,11},{16,20},{18,... | collective-permute-start | bytes 2064392 | tf_op jit(solution)/shard_map/ppermute | solution.py:140
  52.5 108.7 %copy-start.14 = (bf16[1,2,96,1792]{3,2,1,0:T(8,128)(2,1)}, bf16[1,2,96,1792]{3,2,1,0:T(8,128)(2,1)S(1)}, u32[]{:S(2)}) copy-start(bf16[1,2,96,1792]{3,2,1,0:T(8,128)(2,1)S(1)} %maximum_select_fusion.3) | copy-start | bytes 2064388
  57.3 28.7 %collective-permute-start.14 = (f16[4,2,96,512]{3,2,1,0:T(8,128)(2,1)}, f16[4,2,96,512]{3,2,1,0:T(8,128)(2,1)}, u32[]{:S(2)}, u32[]{:S(2)}) collective-permute-start(f16[4,2,96,512]{3,2,1,0:T(8,128)(2,1)} %convert_element_type.136), channel_id=1, source_target_pairs={{0,4},{2,6},{12,8},{14,10},{1,5},{3,7},{13,9},{15,11},{16,20},{18,... | collective-permute-start | bytes 2359304 | tf_op jit(solution)/shard_map/ppermute | solution.py:140
  59.9 2.1 collective-permute-start.8
  60.7 9.2 %collective-permute-start.12 = (bf16[1024,512]{1,0:T(8,128)(2,1)S(1)}, bf16[1024,512]{1,0:T(8,128)(2,1)S(1)}, u32[]{:S(2)}, u32[]{:S(2)}) collective-permute-start(bf16[1024,512]{1,0:T(8,128)(2,1)S(1)} %copy-done.24), channel_id=1, source_target_pairs={{0,2},{2,0},{4,6},{6,4},{8,10},{10,8},{12,14},{14,12},{1,3},{3,1},... | collective-permute-start | bytes 3145736 | tf_op jit(solution)/shard_map/ppermute | solution.py:140
  61.4 8.5 %collective-permute-start.13 = (bf16[1024,512]{1,0:T(8,128)(2,1)S(1)}, bf16[1024,512]{1,0:T(8,128)(2,1)S(1)}, u32[]{:S(2)}, u32[]{:S(2)}) collective-permute-start(bf16[1024,512]{1,0:T(8,128)(2,1)S(1)} %copy-done.23), channel_id=1, source_target_pairs={{0,2},{2,0},{4,6},{6,4},{8,10},{10,8},{12,14},{14,12},{1,3},{3,1},... | collective-permute-start | bytes 3145736 | tf_op jit(solution)/shard_map/ppermute | solution.py:140
  61.9 34.8 %copy-start.2 = (bf16[4,2,96,1024]{3,2,1,0:T(8,128)(2,1)}, bf16[4,2,96,1024]{3,2,1,0:T(8,128)(2,1)S(1)}, u32[]{:S(2)}) copy-start(bf16[4,2,96,1024]{3,2,1,0:T(8,128)(2,1)S(1)} %pad_maximum_fusion.1) | copy-start | bytes 4718596
  61.9 32.2 %collective-permute-start.16 = (bf16[1024,512]{1,0:T(8,128)(2,1)}, bf16[1024,512]{1,0:T(8,128)(2,1)S(1)}, u32[]{:S(2)}, u32[]{:S(2)}) collective-permute-start(bf16[1024,512]{1,0:T(8,128)(2,1)} %get-tuple-element.74), channel_id=1, source_target_pairs={{0,2},{2,0},{4,6},{6,4},{8,10},{10,8},{12,14},{14,12},{1,3},{3,1},... | collective-permute-start | bytes 3145736 | tf_op jit(solution)/shard_map/ppermute | solution.py:140
  66.7 25.3 %copy-start.16 = (bf16[2,96,1792]{2,1,0:T(8,128)(2,1)}, bf16[2,96,1792]{2,1,0:T(8,128)(2,1)S(1)}, u32[]{:S(2)}) copy-start(bf16[2,96,1792]{2,1,0:T(8,128)(2,1)S(1)} %collective-permute-done.11) | copy-start | bytes 2064388
  66.7 28.7 %collective-permute-start.17 = (bf16[1024,512]{1,0:T(8,128)(2,1)}, bf16[1024,512]{1,0:T(8,128)(2,1)S(1)}, u32[]{:S(2)}, u32[]{:S(2)}) collective-permute-start(bf16[1024,512]{1,0:T(8,128)(2,1)} %get-tuple-element.75), channel_id=1, source_target_pairs={{0,2},{2,0},{4,6},{6,4},{8,10},{10,8},{12,14},{14,12},{1,3},{3,1},... | collective-permute-start | bytes 3145736 | tf_op jit(solution)/shard_map/ppermute | solution.py:140
  79.5 39.0 %collective-permute-start.18 = (f16[4,2,192,512]{3,2,1,0:T(8,128)(2,1)}, f16[4,2,192,512]{3,2,1,0:T(8,128)(2,1)}, u32[]{:S(2)}, u32[]{:S(2)}) collective-permute-start(f16[4,2,192,512]{3,2,1,0:T(8,128)(2,1)} %convert_element_type.143), channel_id=1, source_target_pairs={{0,4},{2,6},{12,8},{14,10},{1,5},{3,7},{13,9},{15,11},{16,20},{18,... | collective-permute-start | bytes 4718600 | tf_op jit(solution)/shard_map/ppermute | solution.py:140
  87.5 3.4 %collective-permute-start.15 = (f16[2,2,96,512]{3,2,1,0:T(8,128)(2,1)S(1)}, f16[2,2,96,512]{3,2,1,0:T(8,128)(2,1)S(1)}, u32[]{:S(2)}, u32[]{:S(2)}) collective-permute-start(f16[2,2,96,512]{3,2,1,0:T(8,128)(2,1)S(1)} %slice_convert_fusion.3), channel_id=1, source_target_pairs={{4,8},{6,10},{8,4},{10,6},{5,9},{7,11},{9,5},{11,7},{20,24},{22,26... | collective-permute-start | bytes 1179656 | tf_op jit(solution)/shard_map/ppermute | solution.py:140
  90.1 82.8 %collective-permute-start.20 = (bf16[1024,256]{1,0:T(8,128)(2,1)S(1)}, bf16[1024,256]{1,0:T(8,128)(2,1)S(1)}, u32[]{:S(2)}, u32[]{:S(2)}) collective-permute-start(bf16[1024,256]{1,0:T(8,128)(2,1)S(1)} %copy-done.27), channel_id=1, source_target_pairs={{0,2},{2,0},{4,6},{6,4},{8,10},{10,8},{12,14},{14,12},{1,3},{3,1},... | collective-permute-start | bytes 1572872 | tf_op jit(solution)/shard_map/ppermute | solution.py:140
  90.9 2.3 collective-permute-start.23
  94.1 78.9 %collective-permute-start.21 = (bf16[1024,256]{1,0:T(8,128)(2,1)S(1)}, bf16[1024,256]{1,0:T(8,128)(2,1)S(1)}, u32[]{:S(2)}, u32[]{:S(2)}) collective-permute-start(bf16[1024,256]{1,0:T(8,128)(2,1)S(1)} %copy-done.28), channel_id=1, source_target_pairs={{0,2},{2,0},{4,6},{6,4},{8,10},{10,8},{12,14},{14,12},{1,3},{3,1},... | collective-permute-start | bytes 1572872 | tf_op jit(solution)/shard_map/ppermute | solution.py:140
  94.1 29.8 %collective-permute-start.22 = (bf16[2,2,96,512]{3,2,1,0:T(8,128)(2,1)S(1)}, bf16[2,2,96,512]{3,2,1,0:T(8,128)(2,1)S(1)}, u32[]{:S(2)}, u32[]{:S(2)}) collective-permute-start(bf16[2,2,96,512]{3,2,1,0:T(8,128)(2,1)S(1)} %pad_maximum_fusion.10), channel_id=1, source_target_pairs={{4,0},{6,2},{8,12},{10,14},{5,1},{7,3},{9,13},{11,15},{20,16},{22,... | collective-permute-start | bytes 1179656 | tf_op jit(solution)/shard_map/ppermute | solution.py:140
  95.4 35.9 %collective-permute-start.24 = (bf16[2,2,96,512]{3,2,1,0:T(8,128)(2,1)S(1)}, bf16[2,2,96,512]{3,2,1,0:T(8,128)(2,1)S(1)}, u32[]{:S(2)}, u32[]{:S(2)}) collective-permute-start(bf16[2,2,96,512]{3,2,1,0:T(8,128)(2,1)S(1)} %collective-permute-done.23), channel_id=1, source_target_pairs={{4,0},{6,2},{8,12},{10,14},{5,1},{7,3},{9,13},{11,15},{20,16},{22,... | collective-permute-start | bytes 1179656 | tf_op jit(solution)/shard_map/ppermute | solution.py:140
  102.8 15.7 %copy-start.11 = (f32[4,2,192,512]{3,2,1,0:T(8,128)S(1)}, f32[4,2,192,512]{3,2,1,0:T(8,128)}, u32[]{:S(2)}) copy-start(f32[4,2,192,512]{3,2,1,0:T(8,128)} %shard_map.69) | copy-start | bytes 9437188
  120.7 38.7 %collective-permute-start.19 = (f16[2,2,192,512]{3,2,1,0:T(8,128)(2,1)S(1)}, f16[2,2,192,512]{3,2,1,0:T(8,128)(2,1)S(1)}, u32[]{:S(2)}, u32[]{:S(2)}) collective-permute-start(f16[2,2,192,512]{3,2,1,0:T(8,128)(2,1)S(1)} %slice_convert_fusion.1), channel_id=1, source_target_pairs={{4,8},{6,10},{8,4},{10,6},{5,9},{7,11},{9,5},{11,7},{20,24},{22,26... | collective-permute-start | bytes 2359304 | tf_op jit(solution)/shard_map/ppermute | solution.py:140
  123.9 8.8 %collective-permute-start.26 = (bf16[2,2,96,512]{3,2,1,0:T(8,128)(2,1)S(1)}, bf16[2,2,96,512]{3,2,1,0:T(8,128)(2,1)S(1)}, u32[]{:S(2)}, u32[]{:S(2)}) collective-permute-start(bf16[2,2,96,512]{3,2,1,0:T(8,128)(2,1)S(1)} %pad_maximum_fusion.11), channel_id=1, source_target_pairs={{4,8},{6,10},{8,4},{10,6},{5,9},{7,11},{9,5},{11,7},{20,24},{22,26... | collective-permute-start | bytes 1179656 | tf_op jit(solution)/shard_map/ppermute | solution.py:140
  131.4 33.1 %collective-permute-start.25 = (bf16[2,2,96,512]{3,2,1,0:T(8,128)(2,1)S(1)}, bf16[2,2,96,512]{3,2,1,0:T(8,128)(2,1)S(1)}, u32[]{:S(2)}, u32[]{:S(2)}) collective-permute-start(bf16[2,2,96,512]{3,2,1,0:T(8,128)(2,1)S(1)} %pad_maximum_fusion.11), channel_id=1, source_target_pairs={{4,0},{6,2},{8,12},{10,14},{5,1},{7,3},{9,13},{11,15},{20,16},{22,... | collective-permute-start | bytes 1179656 | tf_op jit(solution)/shard_map/ppermute | solution.py:140
  132.8 67.5 %collective-permute-start.32 = (f16[4,2,192,512]{3,2,1,0:T(8,128)(2,1)}, f16[4,2,192,512]{3,2,1,0:T(8,128)(2,1)}, u32[]{:S(2)}, u32[]{:S(2)}) collective-permute-start(f16[4,2,192,512]{3,2,1,0:T(8,128)(2,1)} %convert_element_type.147), channel_id=1, source_target_pairs={{0,4},{2,6},{12,8},{14,10},{1,5},{3,7},{13,9},{15,11},{16,20},{18,... | collective-permute-start | bytes 4718600 | tf_op jit(solution)/shard_map/ppermute | solution.py:140
  159.4 11.4 %collective-permute-start.27 = (bf16[2,2,96,512]{3,2,1,0:T(8,128)(2,1)S(1)}, bf16[2,2,96,512]{3,2,1,0:T(8,128)(2,1)S(1)}, u32[]{:S(2)}, u32[]{:S(2)}) collective-permute-start(bf16[2,2,96,512]{3,2,1,0:T(8,128)(2,1)S(1)} %collective-permute-done.26), channel_id=1, source_target_pairs={{4,0},{6,2},{8,12},{10,14},{5,1},{7,3},{9,13},{11,15},{20,16},{22,... | collective-permute-start | bytes 1179656 | tf_op jit(solution)/shard_map/ppermute | solution.py:140
  164.5 25.9 %collective-permute-start.29 = (bf16[2,2,96,512]{3,2,1,0:T(8,128)(2,1)S(1)}, bf16[2,2,96,512]{3,2,1,0:T(8,128)(2,1)}, u32[]{:S(2)}, u32[]{:S(2)}) collective-permute-start(bf16[2,2,96,512]{3,2,1,0:T(8,128)(2,1)S(1)} %broadcast_select_fusion.8.refs_1_), channel_id=1, source_target_pairs={{0,2},{2,0},{4,6},{6,4},{8,10},{10,8},{12,14},{14,12},{1,3},{3,1},... | collective-permute-start | bytes 1179656 | tf_op jit(solution)/shard_map/ppermute | solution.py:140
  170.8 21.3 %collective-permute-start.28 = (bf16[2,2,96,512]{3,2,1,0:T(8,128)(2,1)S(1)}, bf16[2,2,96,512]{3,2,1,0:T(8,128)(2,1)}, u32[]{:S(2)}, u32[]{:S(2)}) collective-permute-start(bf16[2,2,96,512]{3,2,1,0:T(8,128)(2,1)S(1)} %broadcast_select_fusion.9.refs_0_), channel_id=1, source_target_pairs={{0,2},{2,0},{4,6},{6,4},{8,10},{10,8},{12,14},{14,12},{1,3},{3,1},... | collective-permute-start | bytes 1179656 | tf_op jit(solution)/shard_map/ppermute | solution.py:140
  172.9 19.2 %collective-permute-start.31 = (bf16[2,2,96,512]{3,2,1,0:T(8,128)(2,1)S(1)}, bf16[2,2,96,512]{3,2,1,0:T(8,128)(2,1)}, u32[]{:S(2)}, u32[]{:S(2)}) collective-permute-start(bf16[2,2,96,512]{3,2,1,0:T(8,128)(2,1)S(1)} %broadcast_select_fusion.6.refs_3_), channel_id=1, source_target_pairs={{0,2},{2,0},{4,6},{6,4},{8,10},{10,8},{12,14},{14,12},{1,3},{3,1},... | collective-permute-start | bytes 1179656 | tf_op jit(solution)/shard_map/ppermute | solution.py:140
  173.0 19.1 %collective-permute-start.30 = (bf16[2,2,96,512]{3,2,1,0:T(8,128)(2,1)S(1)}, bf16[2,2,96,512]{3,2,1,0:T(8,128)(2,1)}, u32[]{:S(2)}, u32[]{:S(2)}) collective-permute-start(bf16[2,2,96,512]{3,2,1,0:T(8,128)(2,1)S(1)} %broadcast_select_fusion.7.refs_2_), channel_id=1, source_target_pairs={{0,2},{2,0},{4,6},{6,4},{8,10},{10,8},{12,14},{14,12},{1,3},{3,1},... | collective-permute-start | bytes 1179656 | tf_op jit(solution)/shard_map/ppermute | solution.py:140
  190.4 9.9 %copy-start.10 = (f32[4,2,192,512]{3,2,1,0:T(8,128)S(1)}, f32[4,2,192,512]{3,2,1,0:T(8,128)}, u32[]{:S(2)}) copy-start(f32[4,2,192,512]{3,2,1,0:T(8,128)} %shard_map.70) | copy-start | bytes 9437188
  190.4 20.4 %collective-permute-start.36 = (bf16[2,2,192,512]{3,2,1,0:T(8,128)(2,1)}, bf16[2,2,192,512]{3,2,1,0:T(8,128)(2,1)}, u32[]{:S(2)}, u32[]{:S(2)}) collective-permute-start(bf16[2,2,192,512]{3,2,1,0:T(8,128)(2,1)} %pad_maximum_fusion.2), channel_id=1, source_target_pairs={{4,8},{6,10},{8,4},{10,6},{5,9},{7,11},{9,5},{11,7},{20,24},{22,26... | collective-permute-start | bytes 2359304 | tf_op jit(solution)/shard_map/ppermute | solution.py:140
  203.9 6.9 %copy-start.22 = (bf16[2,2,96,512]{3,2,1,0:T(8,128)(2,1)S(1)}, bf16[2,2,96,512]{3,2,1,0:T(8,128)(2,1)}, u32[]{:S(2)}) copy-start(bf16[2,2,96,512]{3,2,1,0:T(8,128)(2,1)} %get-tuple-element.139) | copy-start | bytes 1179652
  204.1 8.0 %collective-permute-start.33 = (f16[2,2,192,512]{3,2,1,0:T(8,128)(2,1)S(1)}, f16[2,2,192,512]{3,2,1,0:T(8,128)(2,1)}, u32[]{:S(2)}, u32[]{:S(2)}) collective-permute-start(f16[2,2,192,512]{3,2,1,0:T(8,128)(2,1)S(1)} %slice_convert_fusion), channel_id=1, source_target_pairs={{4,8},{6,10},{8,4},{10,6},{5,9},{7,11},{9,5},{11,7},{20,24},{22,26... | collective-permute-start | bytes 2359304 | tf_op jit(solution)/shard_map/ppermute | solution.py:140
  205.9 52.7 %collective-permute-start.40 = (f16[4,2,192,256]{3,2,1,0:T(8,128)(2,1)}, f16[4,2,192,256]{3,2,1,0:T(8,128)(2,1)S(1)}, u32[]{:S(2)}, u32[]{:S(2)}) collective-permute-start(f16[4,2,192,256]{3,2,1,0:T(8,128)(2,1)} %convert_element_type.153), channel_id=1, source_target_pairs={{0,4},{2,6},{12,8},{14,10},{1,5},{3,7},{13,9},{15,11},{16,20},{18,... | collective-permute-start | bytes 2359304 | tf_op jit(solution)/shard_map/ppermute | solution.py:140
  209.5 20.2 %collective-permute-start.35 = (bf16[2,2,192,512]{3,2,1,0:T(8,128)(2,1)}, bf16[2,2,192,512]{3,2,1,0:T(8,128)(2,1)S(1)}, u32[]{:S(2)}, u32[]{:S(2)}) collective-permute-start(bf16[2,2,192,512]{3,2,1,0:T(8,128)(2,1)} %pad_maximum_fusion.2), channel_id=1, source_target_pairs={{4,0},{6,2},{8,12},{10,14},{5,1},{7,3},{9,13},{11,15},{20,16},{22,... | collective-permute-start | bytes 2359304 | tf_op jit(solution)/shard_map/ppermute | solution.py:140
  210.8 35.7 %collective-permute-start.37 = (bf16[2,2,192,512]{3,2,1,0:T(8,128)(2,1)}, bf16[2,2,192,512]{3,2,1,0:T(8,128)(2,1)S(1)}, u32[]{:S(2)}, u32[]{:S(2)}) collective-permute-start(bf16[2,2,192,512]{3,2,1,0:T(8,128)(2,1)} %collective-permute-done.36), channel_id=1, source_target_pairs={{4,0},{6,2},{8,12},{10,14},{5,1},{7,3},{9,13},{11,15},{20,16},{22,... | collective-permute-start | bytes 2359304 | tf_op jit(solution)/shard_map/ppermute | solution.py:140
  216.1 49.1 %collective-permute-start.51 = (bf16[2,2,192,512]{3,2,1,0:T(8,128)(2,1)S(1)}, bf16[2,2,192,512]{3,2,1,0:T(8,128)(2,1)S(1)}, u32[]{:S(2)}, u32[]{:S(2)}) collective-permute-start(bf16[2,2,192,512]{3,2,1,0:T(8,128)(2,1)S(1)} %pad_maximum_fusion.5), channel_id=1, source_target_pairs={{4,8},{6,10},{8,4},{10,6},{5,9},{7,11},{9,5},{11,7},{20,24},{22,26... | collective-permute-start | bytes 2359304 | tf_op jit(solution)/shard_map/ppermute | solution.py:140
  246.7 3.8 %collective-permute-start.39 = (bf16[2,2,192,512]{3,2,1,0:T(8,128)(2,1)S(1)}, bf16[2,2,192,512]{3,2,1,0:T(8,128)(2,1)S(1)}, u32[]{:S(2)}, u32[]{:S(2)}) collective-permute-start(bf16[2,2,192,512]{3,2,1,0:T(8,128)(2,1)S(1)} %broadcast_select_fusion.2.refs_1_), channel_id=1, source_target_pairs={{0,2},{2,0},{4,6},{6,4},{8,10},{10,8},{12,14},{14,12},{1,3},{3,1},... | collective-permute-start | bytes 2359304 | tf_op jit(solution)/shard_map/ppermute | solution.py:140
  248.6 3.5 %collective-permute-start.38 = (bf16[2,2,192,512]{3,2,1,0:T(8,128)(2,1)S(1)}, bf16[2,2,192,512]{3,2,1,0:T(8,128)(2,1)S(1)}, u32[]{:S(2)}, u32[]{:S(2)}) collective-permute-start(bf16[2,2,192,512]{3,2,1,0:T(8,128)(2,1)S(1)} %broadcast_select_fusion.3.refs_0_), channel_id=1, source_target_pairs={{0,2},{2,0},{4,6},{6,4},{8,10},{10,8},{12,14},{14,12},{1,3},{3,1},... | collective-permute-start | bytes 2359304 | tf_op jit(solution)/shard_map/ppermute | solution.py:140
  248.8 16.3 %collective-permute-start.34 = (bf16[2,96,1536]{2,1,0:T(8,128)(2,1)S(1)}, bf16[2,96,1536]{2,1,0:T(8,128)(2,1)S(1)}, u32[]{:S(2)}, u32[]{:S(2)}) collective-permute-start(bf16[2,96,1536]{2,1,0:T(8,128)(2,1)S(1)} %pad_maximum_fusion.7), channel_id=1, source_target_pairs={{4,0},{6,2},{8,12},{10,14},{5,1},{7,3},{9,13},{11,15},{20,16},{22,... | collective-permute-start | bytes 1769480 | tf_op jit(solution)/shard_map/ppermute | solution.py:140
  250.2 8.4 %copy-start.5 = (f32[4,2,192,256]{3,2,1,0:T(8,128)S(1)}, f32[4,2,192,256]{3,2,1,0:T(8,128)}, u32[]{:S(2)}) copy-start(f32[4,2,192,256]{3,2,1,0:T(8,128)} %copy-done.4) | copy-start | bytes 4718596
  250.5 31.5 %collective-permute-start.50 = (bf16[2,2,192,512]{3,2,1,0:T(8,128)(2,1)S(1)}, bf16[2,2,192,512]{3,2,1,0:T(8,128)(2,1)S(1)}, u32[]{:S(2)}, u32[]{:S(2)}) collective-permute-start(bf16[2,2,192,512]{3,2,1,0:T(8,128)(2,1)S(1)} %pad_maximum_fusion.5), channel_id=1, source_target_pairs={{4,0},{6,2},{8,12},{10,14},{5,1},{7,3},{9,13},{11,15},{20,16},{22,... | collective-permute-start | bytes 2359304 | tf_op jit(solution)/shard_map/ppermute | solution.py:140
  258.9 7.7 %collective-permute-start.41 = (f16[2,2,192,256]{3,2,1,0:T(8,128)(2,1)S(1)}, f16[2,2,192,256]{3,2,1,0:T(8,128)(2,1)S(1)}, u32[]{:S(2)}, u32[]{:S(2)}) collective-permute-start(f16[2,2,192,256]{3,2,1,0:T(8,128)(2,1)S(1)} %slice_convert_fusion.2), channel_id=1, source_target_pairs={{4,8},{6,10},{8,4},{10,6},{5,9},{7,11},{9,5},{11,7},{20,24},{22,26... | collective-permute-start | bytes 1179656 | tf_op jit(solution)/shard_map/ppermute | solution.py:140
  265.2 33.6 %collective-permute-start.52 = (bf16[2,2,192,512]{3,2,1,0:T(8,128)(2,1)S(1)}, bf16[2,2,192,512]{3,2,1,0:T(8,128)(2,1)S(1)}, u32[]{:S(2)}, u32[]{:S(2)}) collective-permute-start(bf16[2,2,192,512]{3,2,1,0:T(8,128)(2,1)S(1)} %collective-permute-done.51), channel_id=1, source_target_pairs={{4,0},{6,2},{8,12},{10,14},{5,1},{7,3},{9,13},{11,15},{20,16},{22,... | collective-permute-start | bytes 2359304 | tf_op jit(solution)/shard_map/ppermute | solution.py:140
  267.1 33.9 %collective-permute-start.42 = (bf16[2,96,256]{2,1,0:T(8,128)(2,1)S(1)}, bf16[2,96,256]{2,1,0:T(8,128)(2,1)S(1)}, u32[]{:S(2)}, u32[]{:S(2)}) collective-permute-start(bf16[2,96,256]{2,1,0:T(8,128)(2,1)S(1)} %pad_maximum_fusion.15), channel_id=1, source_target_pairs={{4,0},{6,2},{8,12},{10,14},{5,1},{7,3},{9,13},{11,15},{20,16},{22,... | collective-permute-start | bytes 294920 | tf_op jit(solution)/shard_map/ppermute | solution.py:140
  268.4 35.8 %collective-permute-start.46 = (bf16[2,2,192,256]{3,2,1,0:T(8,128)(2,1)S(1)}, bf16[2,2,192,256]{3,2,1,0:T(8,128)(2,1)S(1)}, u32[]{:S(2)}, u32[]{:S(2)}) collective-permute-start(bf16[2,2,192,256]{3,2,1,0:T(8,128)(2,1)S(1)} %pad_maximum_fusion.12), channel_id=1, source_target_pairs={{4,8},{6,10},{8,4},{10,6},{5,9},{7,11},{9,5},{11,7},{20,24},{22,26... | collective-permute-start | bytes 1179656 | tf_op jit(solution)/shard_map/ppermute | solution.py:140
  269.1 40.2 %collective-permute-start.45 = (bf16[2,2,192,256]{3,2,1,0:T(8,128)(2,1)S(1)}, bf16[2,2,192,256]{3,2,1,0:T(8,128)(2,1)S(1)}, u32[]{:S(2)}, u32[]{:S(2)}) collective-permute-start(bf16[2,2,192,256]{3,2,1,0:T(8,128)(2,1)S(1)} %pad_maximum_fusion.12), channel_id=1, source_target_pairs={{4,0},{6,2},{8,12},{10,14},{5,1},{7,3},{9,13},{11,15},{20,16},{22,... | collective-permute-start | bytes 1179656 | tf_op jit(solution)/shard_map/ppermute | solution.py:140
  301.1 4.4 %collective-permute-start.43 = (bf16[2,48,1792]{2,1,0:T(8,128)(2,1)S(1)}, bf16[2,48,1792]{2,1,0:T(8,128)(2,1)S(1)}, u32[]{:S(2)}, u32[]{:S(2)}) collective-permute-start(bf16[2,48,1792]{2,1,0:T(8,128)(2,1)S(1)} %get-tuple-element.153), channel_id=1, source_target_pairs={{0,2},{2,0},{4,6},{6,4},{8,10},{10,8},{12,14},{14,12},{1,3},{3,1},... | collective-permute-start | bytes 1032200 | tf_op jit(solution)/shard_map/ppermute | solution.py:140
  303.5 16.9 %collective-permute-start.54 = (bf16[2,2,192,512]{3,2,1,0:T(8,128)(2,1)S(1)}, bf16[2,2,192,512]{3,2,1,0:T(8,128)(2,1)S(1)}, u32[]{:S(2)}, u32[]{:S(2)}) collective-permute-start(bf16[2,2,192,512]{3,2,1,0:T(8,128)(2,1)S(1)} %broadcast_select_fusion.refs_1_), channel_id=1, source_target_pairs={{0,2},{2,0},{4,6},{6,4},{8,10},{10,8},{12,14},{14,12},{1,3},{3,1},... | collective-permute-start | bytes 2359304 | tf_op jit(solution)/shard_map/ppermute | solution.py:140
  303.6 16.7 %collective-permute-start.53 = (bf16[2,2,192,512]{3,2,1,0:T(8,128)(2,1)S(1)}, bf16[2,2,192,512]{3,2,1,0:T(8,128)(2,1)S(1)}, u32[]{:S(2)}, u32[]{:S(2)}) collective-permute-start(bf16[2,2,192,512]{3,2,1,0:T(8,128)(2,1)S(1)} %broadcast_select_fusion.1.refs_0_), channel_id=1, source_target_pairs={{0,2},{2,0},{4,6},{6,4},{8,10},{10,8},{12,14},{14,12},{1,3},{3,1},... | collective-permute-start | bytes 2359304 | tf_op jit(solution)/shard_map/ppermute | solution.py:140
  304.2 13.6 %collective-permute-start.47 = (bf16[2,2,192,256]{3,2,1,0:T(8,128)(2,1)S(1)}, bf16[2,2,192,256]{3,2,1,0:T(8,128)(2,1)S(1)}, u32[]{:S(2)}, u32[]{:S(2)}) collective-permute-start(bf16[2,2,192,256]{3,2,1,0:T(8,128)(2,1)S(1)} %collective-permute-done.46), channel_id=1, source_target_pairs={{4,0},{6,2},{8,12},{10,14},{5,1},{7,3},{9,13},{11,15},{20,16},{22,... | collective-permute-start | bytes 1179656 | tf_op jit(solution)/shard_map/ppermute | solution.py:140
  305.7 13.6 %collective-permute-start.44 = (bf16[48,3584]{1,0:T(8,128)(2,1)S(1)}, bf16[48,3584]{1,0:T(8,128)(2,1)S(1)}, u32[]{:S(2)}, u32[]{:S(2)}) collective-permute-start(bf16[48,3584]{1,0:T(8,128)(2,1)S(1)} %get-tuple-element.151), channel_id=1, source_target_pairs={{0,1},{1,0},{2,3},{3,2},{4,5},{5,4},{6,7},{7,6},{8,9},{9,8},{10,11... | collective-permute-start | bytes 1032200 | tf_op jit(solution)/shard_map/ppermute | solution.py:301
  317.8 9.1 %collective-permute-start.49 = (bf16[2,2,192,256]{3,2,1,0:T(8,128)(2,1)S(1)}, bf16[2,2,192,256]{3,2,1,0:T(8,128)(2,1)S(1)}, u32[]{:S(2)}, u32[]{:S(2)}) collective-permute-start(bf16[2,2,192,256]{3,2,1,0:T(8,128)(2,1)S(1)} %broadcast_select_fusion.4.refs_1_), channel_id=1, source_target_pairs={{0,2},{2,0},{4,6},{6,4},{8,10},{10,8},{12,14},{14,12},{1,3},{3,1},... | collective-permute-start | bytes 1179656 | tf_op jit(solution)/shard_map/ppermute | solution.py:140
  319.3 7.6 %collective-permute-start.48 = (bf16[2,2,192,256]{3,2,1,0:T(8,128)(2,1)S(1)}, bf16[2,2,192,256]{3,2,1,0:T(8,128)(2,1)S(1)}, u32[]{:S(2)}, u32[]{:S(2)}) collective-permute-start(bf16[2,2,192,256]{3,2,1,0:T(8,128)(2,1)S(1)} %broadcast_select_fusion.5.refs_0_), channel_id=1, source_target_pairs={{0,2},{2,0},{4,6},{6,4},{8,10},{10,8},{12,14},{14,12},{1,3},{3,1},... | collective-permute-start | bytes 1179656 | tf_op jit(solution)/shard_map/ppermute | solution.py:140
  (21 other events, 39.9 us)

commit v7 on v6

--- a/solution.py
+++ b/solution.py
@@ -21,13 +21,14 @@
     blocks, _, rows, width = out_ref.shape
     for which, (near, far) in enumerate(((gate_ref, gate_far_ref), (up_ref, up_far_ref))):
         product = jnp.dot(mine_ref[...], near[...], preferred_element_type=jnp.float32)
-        product += jnp.dot(theirs_ref[...], far[...], preferred_element_type=jnp.float32)
+        product += jnp.dot(theirs_ref[...], far[0, 0], preferred_element_type=jnp.float32)
         out_ref[:, which] = (scale * product).reshape(blocks, rows, width)
 
 
 def forward(place, mine, theirs, gate_weight, up_weight, far, start, tile, blocks, scale):
     total, depth = mine.shape
-    width = far[0].shape[1]
+    width = far[0].shape[3]
+    up_index = far[1].shape[1] - 1
     rows = total // blocks
     whole = pl.BlockSpec((total, depth), lambda j, place: (0, 0))
     weight = pl.BlockSpec((depth, tile), lambda j, place: (0, place[0] + start // tile + j))
@@ -42,8 +43,8 @@
                 whole,
                 weight,
                 weight,
-                pl.BlockSpec((depth, tile), lambda j, place: (0, j)),
-                pl.BlockSpec((depth, tile), lambda j, place: (0, j)),
+                pl.BlockSpec((1, 1, depth, tile), lambda j, place: (place[1], 0, 0, j)),
+                pl.BlockSpec((1, 1, depth, tile), lambda j, place: (place[1], up_index, 0, j)),
             ],
             out_specs=pl.BlockSpec((blocks, 2, rows, tile), lambda j, place: (0, 0, 0, j)),
         ),
@@ -52,55 +53,41 @@
     )(place, mine, theirs, gate_weight, up_weight, *far)
 
 
-def gradient_kernel(batches, place_ref, features_ref, *refs):
-    own, other, outs = refs[: 2 * batches], refs[2 * batches : 4 * batches], refs[-2:]
-
-    def fill(acts):
-        for which, out_ref in enumerate(outs):
-            parts = []
-            for batch in range(2):
-                for act_ref in acts if batches == 1 else acts[2 * batch : 2 * batch + 2]:
-                    blocks, _, rows, width = act_ref.shape
-                    rows = rows * batches // 2
-                    first = batch * rows if batches == 1 else 0
-                    part = act_ref[:, which, first : first + rows]
-                    parts.append(part.reshape(blocks * rows, width))
-            out_ref[...] = jnp.dot(
-                features_ref[...], jnp.concatenate(parts), preferred_element_type=jnp.float32
-            )
-
-    for which, acts in enumerate((own, other)):
-        pl.when(pl.program_id(0) == which)(functools.partial(fill, acts))
-
-
-def gradient(place, features, own, other, totals, columns, start, tile):
+def gradient_kernel(batches, features_ref, *refs):
+    acts, outs = refs[: 2 * batches], refs[-2:]
+    for which, out_ref in enumerate(outs):
+        parts = []
+        for batch in range(2):
+            for act_ref in acts if batches == 1 else acts[2 * batch : 2 * batch + 2]:
+                _, blocks, _, rows, width = act_ref.shape
+                rows = rows * batches // 2
+                first = batch * rows if batches == 1 else 0
+                part = act_ref[0, :, which, first : first + rows]
+                parts.append(part.reshape(blocks * rows, width))
+        out_ref[...] = jnp.dot(
+            features_ref[...], jnp.concatenate(parts), preferred_element_type=jnp.float32
+        )
+
+
+def gradient(features, acts, totals, columns, start, tile):
     depth, total = features.shape
-    blocks, _, rows, width = own[0].shape
-    tiles = width // tile
-    shape = (blocks, 2, rows, tile)
-    own_spec = pl.BlockSpec(
-        shape, lambda i, j, place: (0, 0, 0, jnp.where(i == 0, j, tiles - 1))
-    )
-    other_spec = pl.BlockSpec(shape, lambda i, j, place: (0, 0, 0, jnp.where(i == 0, 0, j)))
-    out_spec = pl.BlockSpec((depth, tile), lambda i, j, place: (0, place[i] + start // tile + j))
+    cores, blocks, _, rows, width = acts[0].shape
+    share = columns // cores // tile
+    act_spec = pl.BlockSpec((1, blocks, 2, rows, tile), lambda i, j: (i, 0, 0, 0, j))
+    out_spec = pl.BlockSpec((depth, tile), lambda i, j: (0, i * share + start // tile + j))
     out_shape = jax.ShapeDtypeStruct((depth, columns), jnp.float32)
-    in_specs = [pl.BlockSpec((depth, total), lambda i, j, place: (0, 0))]
-    in_specs += [own_spec] * len(own) + [other_spec] * len(other)
+    in_specs = [pl.BlockSpec((depth, total), lambda i, j: (0, 0))] + [act_spec] * len(acts)
     in_specs += [pl.BlockSpec(memory_space=pl.ANY)] * len(totals)
-    first = 2 + len(own) + len(other)
     return pl.pallas_call(
-        functools.partial(gradient_kernel, len(own) // 2),
+        functools.partial(gradient_kernel, len(acts) // 2),
         out_shape=(out_shape, out_shape),
-        grid_spec=pltpu.PrefetchScalarGridSpec(
-            num_scalar_prefetch=1,
-            grid=(2, tiles),
-            in_specs=in_specs,
-            out_specs=(out_spec, out_spec),
-        ),
-        input_output_aliases={first + i: i for i in range(len(totals))},
+        grid=(cores, width // tile),
+        in_specs=in_specs,
+        out_specs=(out_spec, out_spec),
+        input_output_aliases={1 + len(acts) + i: i for i in range(len(totals))},
         compiler_params=pltpu.CompilerParams(vmem_limit_bytes=VMEM_LIMIT),
         cost_estimate=NO_COST,
-    )(place, features, *own, *other, *totals)
+    )(features, *acts, *totals)
 
 
 def tie(value, *after):
@@ -161,21 +148,43 @@
             pieces.append((batches, begin * tile, count * tile))
     last = len(pieces) - 1
 
+    both = [[2 * i, 2 * i + 1] for i in range(line)]
+
+    def share_pair(value):
+        return lax.all_gather(value, "col", axis=0, axis_index_groups=both)
+
     def exchange_weights(k, after):
         _, start, width = pieces[k]
         first = part * half + (1 - core) * share + start
-        return [
-            send(tie(columns_of(weight, first, width), after), pairs)
-            for weight in (gate_weight, up_weight)
+        chosen = [
+            columns_of(weight, first, width) for weight in tie((gate_weight, up_weight), after)
         ]
+        if k == 0:
+            return [send(value, pairs)[None, None] for value in chosen]
+        return [share_pair(jnp.stack(chosen))] * 2
 
     mine = tokens[0]
     over_row = lax.ppermute(mine, "row", swap)
+    cotangent = grad_hidden[0]
+    cotangent = jnp.stack(
+        [
+            columns_of(cotangent, part * half, half),
+            lax.ppermute(columns_of(cotangent, (1 - part) * half, half), "depth", swap),
+        ]
+    )
     over_depth = lax.ppermute(mine, "depth", swap)
     over_both = lax.ppermute(over_row, "depth", swap)
     far_weights = {0: exchange_weights(0, ())}
     far_weights[1] = far_weights[0]
-    first_tile = ((part * half + core * share) // tile).astype(jnp.int32).reshape(1)
+    first_tile = (part * half + core * share) // tile
+
+    cotangent = by(
+        core == 0,
+        columns_of(cotangent, core * share, share),
+        send(columns_of(cotangent, (1 - core) * share, share), pairs),
+        1,
+    )
+    cotangent = jnp.stack([send(cotangent, inward), cotangent])
 
     def arrange(values):
         values = values.reshape(line, rows, depth)
@@ -189,7 +198,8 @@
         _, start, _ = pieces[k]
         mine, theirs = (value.reshape(-1, depth) for value in tie(tokens, after))
         weights = (gate_weight, up_weight, far_weights[k])
-        return forward(first_tile, mine, theirs, *weights, start, tile, line, scale)
+        where = jnp.stack([first_tile, jnp.where(k < 2, 0, 1 - core)]).astype(jnp.int32)
+        return forward(where, mine, theirs, *weights, start, tile, line, scale)
 
     features = [by(row == 0, mine, over_row, 1)]
     spread = [both_cores(features[0], ())]
@@ -200,23 +210,8 @@
     over_depth, over_both = tie((over_depth, over_both), payload)
     features.append(by(row == 0, over_depth, over_both, 1))
     spread.append(both_cores(features[1], ()))
-    for k in range(2, last + 1):
-        far_weights[k] = exchange_weights(k, spread[1] if k < 4 else inner[0])
-
-    mine_cotangent, cotangent = tie((grad_hidden[0], grad_hidden[0]), payload)
-    cotangent = jnp.stack(
-        [
-            columns_of(mine_cotangent, part * half, half),
-            lax.ppermute(columns_of(cotangent, (1 - part) * half, half), "depth", swap),
-        ]
-    )
-    cotangent = by(
-        core == 0,
-        columns_of(cotangent, core * share, share),
-        send(columns_of(cotangent, (1 - core) * share, share), pairs),
-        1,
-    )
-    cotangent = jnp.stack([send(cotangent, inward), cotangent])
+    far_weights[2] = exchange_weights(2, payload)
+    both_rows = [jnp.stack(pair, axis=1) for pair in zip(*spread)]
 
     def activate(k, summed):
         batches, start, width = pieces[k]
@@ -225,18 +220,19 @@
         squash = jax.nn.sigmoid(gate_sum)
         product = (gate_sum * squash * up_sum).astype(jnp.bfloat16)
         given = wide(cotangent[:, batches[0] : batches[-1] + 1, :, start : start + width])
-        gate_act = given * up_sum * squash * (1.0 + gate_sum * (1.0 - squash))
-        up_act = given * gate_sum * squash
-        act = jnp.stack([gate_act, up_act], axis=1).astype(jnp.bfloat16)
+        given = given * squash
+        gate_act = given * up_sum * (1.0 + gate_sum * (1.0 - squash))
+        up_act = given * gate_sum
+        is_gate = lax.broadcasted_iota(jnp.int32, (2, 2, *given.shape[1:]), 1) == 0
+        act = jnp.where(is_gate, gate_act[:, None], up_act[:, None]).astype(jnp.bfloat16)
         return product, act.reshape(2, 2, len(batches) * rows, width)
 
     def by_side(values):
-        values = values.reshape(line, rows * depth)
+        values = values.reshape(line, rows, depth)
         values = jnp.concatenate([values[:2], values[3:], values[2:3]])
         return values.reshape(-1, depth)
 
     turned = jnp.concatenate([by_side(tie(near, inner[0])) for near, _ in spread]).T
-    place = jnp.stack([core, 1 - core]).astype(jnp.int32) * (share // tile)
 
     def outer_hidden(ks):
         def joined(batch, which):
@@ -255,8 +251,7 @@
         before = []
         k = t - 1
         if 0 <= k <= last:
-            summed = jnp.stack([terms[k][0] + wide(got[k][1]), terms[k][1] + wide(got[k][0])])
-            hidden[k], act[k] = activate(k, summed)
+            hidden[k], act[k] = activate(k, add(terms[k][:2], inner[k][:2], got[k][::-1]))
             across[k], near_out[k] = send(act[k], centre), send(act[k], outward)
             before.append(act[k])
             if k == last - 1:
@@ -272,24 +267,25 @@
                 jnp.where(at_end, near_got, near_mine),
                 jnp.where(at_end, far_got, far_mine),
             ]
-            waiting.append((mine, [send(value, pairs) for value in mine]))
+            waiting += [share_pair(value) for value in mine]
         k = t + 1
         if k <= last:
-            tokens = spread[1] if k == 1 else [jnp.stack(pair, axis=1) for pair in zip(*spread)]
+            tokens = spread[1] if k == 1 else both_rows
             terms[k] = multiply(k, tokens, before)
             payload = terms[k].astype(WIRE)
             inner[k] = send(payload, inward)
             before.append(payload)
+            if 2 < k + 2 <= last:
+                far_weights[k + 2] = exchange_weights(k + 2, payload)
         k = t - 2
         if 0 <= k <= last and pieces[k][0] != (0,):
-            own, other = (sum(values, []) for values in zip(*waiting))
-            totals = gradient(place, turned, own, other, totals, half, pieces[k][1], tile)
+            totals = gradient(turned, waiting, totals, half, pieces[k][1], tile)
             waiting = []
             before.append(totals)
         k = t
         if k <= last:
-            terms[k] = tie(terms[k], before) + wide(inner[k])
-            got[k] = send(terms[k][2:].astype(WIRE), centre)
+            terms[k] = tie(terms[k], before)
+            got[k] = send(add(terms[k][2:], inner[k][2:]).astype(WIRE), centre)
         k = t - 1
         if 0 <= k <= last:
             far_out[k] = send(across[k], outward)

time: 333 us -> 399 us (1.20)
  other arithmetic: 37.2 us -> 76.4 us
  starting transfers between devices: 96.7 us -> 66.7 us
  local copies, waits for them, and re-layouts: 26.6 us -> 48 us
  blocking collectives: 0 us -> 21.4 us
  between operations: 1.8 us -> 15.1 us
    ppermute x50 -> x34, starting transfers between devices: 90.2 us -> 59.9 us  [send(): return lax.ppermute(value, 'col', route)]
    ppermute x50 -> x34, waiting for transfers between devices: 106 us -> 81.9 us  [send(): return lax.ppermute(value, 'col', route)]
    all_gather x0 -> x6, blocking collectives: none -> 21.4 us  [share_pair(): return lax.all_gather(value, 'col', axis=0, axis_index_groups=both)]
    unnamed x70 -> x120, local copies, waits for them, and re-layouts: 10.6 us -> 23.2 us
    convert_element_type x0 -> x10, other arithmetic: none -> 11 us  [the longest x5 7.79 us: local(): got[k] = send(add(terms[k][2:], inner[k][2:]).astype(WIRE), centre)]
    ppermute x1, waiting for transfers between devices: 0.01 us -> 8.76 us  [local(): over_depth = lax.ppermute(mine, 'depth', swap)]
    add x8 -> x0, other arithmetic: 8.09 us -> none  [the longest x5 5.88 us: local(): terms[k] = tie(terms[k], before) + wide(inner[k])]
    all_gather x0 -> x7, waiting for transfers between devices: none -> 7.5 us  [share_pair(): return lax.all_gather(value, 'col', axis=0, axis_index_groups=both)]
  transfers between devices with their start and end apart: 55 -> 46, of which waited for: 17 -> 17; matrix products, arithmetic and copies ran while one was open for 17% -> 24% of each run, Pallas kernels for 13% -> 8%
where the time goes in v7:
time: 399 us; the launch traced here: 396 us
  waiting for transfers between devices  122 us (31%)
  other arithmetic  76.4 us (19%)
  starting transfers between devices  66.7 us (17%)
  local copies, waits for them, and re-layouts  48 us (12%)
  Pallas kernels  46.5 us (12%)
  blocking collectives  21.4 us (5%)
  between operations  15.1 us (4%)
    ppermute x34, waiting for transfers between devices, send(): return lax.ppermute(value, 'col', route)  81.9 us
    ppermute x34, starting transfers between devices, send(): return lax.ppermute(value, 'col', route)  59.9 us
    pallas_call x5, Pallas kernels, forward(): pl.pallas_call(functools.partial(forward_kernel, scale), out_shape=jax.Sh...  25.8 us
    unnamed x120, local copies, waits for them, and re-layouts  23.2 us
    all_gather x6, blocking collectives, share_pair(): return lax.all_gather(value, 'col', axis=0, axis_index_groups=both)  21.4 us
    pallas_call x4, Pallas kernels, gradient(): pl.pallas_call(functools.partial(gradient_kernel, len(acts) // 2), out_sh...  20.6 us
    convert_element_type x4, other arithmetic, local(): payload = terms[k].astype(WIRE)  9.13 us
    ppermute x1, waiting for transfers between devices, local(): over_depth = lax.ppermute(mine, 'depth', swap)  8.76 us
  transfers between devices with their start and end apart: 46, of which 17 were waited for; matrix products, arithmetic and copies ran while one was open for 24% of the time, Pallas kernels for 8%

profile of v7, /device:TPU:1, one launch (start us, length us, event | category | flops | bytes accessed | tf_op | source)
XLA Modules:
  0.0 396.4 jit_solution(8073846876071861768)
XLA Ops:
  7.2 2.1 collective-permute-start
  9.3 2.3 constant_dynamic-slice_fusion.1
  12.5 2.3 constant_dynamic-slice_fusion.2
  14.9 3.5 collective-permute-done
  21.6 2.0 collective-permute-done.1
  25.8 4.2 %shard_map.67 = f32[4,2,96,512]{3,2,1,0:T(8,128)S(1)} custom-call(s32[2]{0:T(128)S(1)} %pad_add_fusion.place_ref, bf16[384,1024]{1,0:T(8,128)(2,1)S(1)} %bitcast.226, bf16[384,1024]{1,0:T(8,128)(2,1)} %bitcast.4.theirs_ref, bf16[1024,7168]{1,0:T(8,128)(2,1)} %gate_ref.9, bf16[1024,7168]{1,0:T(8,128)(2,1)} %up_ref.9, bf16[1,1,1024,512]{3,2,1,0:T(8,128)(2,1)S(1)} %bitcast.236, ...), custom_call_target="tpu_custom_call" | custom-call | tf_op jit(solution)/shard_map/pallas_call | solution.py:35
  31.1 1.7 dynamic-slice_bitcast_fusion.2
  36.9 8.8 %collective-permute-done.4 = bf16[384,512]{1,0:T(8,128)(2,1)S(1)} collective-permute-done((bf16[384,512]{1,0:T(8,128)(2,1)S(1)}, bf16[384,512]{1,0:T(8,128)(2,1)S(1)}, u32[]{:S(2)}, u32[]{:S(2)}) %collective-permute-start.4) | collective-permute-done | bytes 393248 | tf_op jit(solution)/shard_map/ppermute | solution.py:175
  45.7 8.4 %collective-permute-done.5 = bf16[384,512]{1,0:T(8,128)(2,1)S(1)} collective-permute-done((bf16[384,512]{1,0:T(8,128)(2,1)S(1)}, bf16[384,512]{1,0:T(8,128)(2,1)S(1)}, u32[]{:S(2)}, u32[]{:S(2)}) %collective-permute-start.5) | collective-permute-done | bytes 393248 | tf_op jit(solution)/shard_map/ppermute | solution.py:176
  59.0 8.3 %collective-permute-done.9 = bf16[48,3584]{1,0:T(8,128)(2,1)S(1)} collective-permute-done((bf16[48,3584]{1,0:T(8,128)(2,1)}, bf16[48,3584]{1,0:T(8,128)(2,1)S(1)}, u32[]{:S(2)}, u32[]{:S(2)}) %collective-permute-start.9) | collective-permute-done | bytes 344096 | tf_op jit(solution)/shard_map/ppermute | solution.py:172
  68.1 1.9 fusion.11
  76.5 3.9 shard_map.68
  81.5 1.7 dynamic-slice_bitcast_fusion
  84.9 1.7 fusion.16
  86.6 3.6 collective-permute-start.7
  90.2 2.1 maximum_select_fusion.2
  92.3 2.2 collective-permute-start.11
  94.5 2.2 maximum_select_fusion.3
  98.2 2.2 collective-permute-start.12
  100.4 6.7 %collective-permute-done.7 = f16[4,2,96,512]{3,2,0,1:T(8,128)(2,1)S(1)} collective-permute-done((f16[4,2,96,512]{3,2,0,1:T(8,128)(2,1)S(1)}, f16[4,2,96,512]{3,2,0,1:T(8,128)(2,1)S(1)}, u32[]{:S(2)}, u32[]{:S(2)}) %collective-permute-start.7) | collective-permute-done | bytes 786464 | tf_op jit(solution)/shard_map/ppermute | solution.py:127
  111.4 2.3 copy.77
  113.7 2.0 pad_maximum_fusion.6
  115.7 2.3 copy.78
  118.0 1.6 pad_maximum_fusion.3
  119.6 1.6 fusion.3
  127.8 6.9 %shard_map.69 = f32[4,2,192,512]{3,2,1,0:T(8,128)} custom-call(s32[2]{0:T(128)S(1)} %pad_add_fusion.1.place_ref, bf16[768,1024]{1,0:T(8,128)(2,1)S(1)} %bitcast.230, bf16[768,1024]{1,0:T(8,128)(2,1)S(1)} %bitcast.231, bf16[1024,7168]{1,0:T(8,128)(2,1)} %gate_ref.9, bf16[1024,7168]{1,0:T(8,128)(2,1)} %up_ref.9, bf16[2,2,1024,512]{3,2,1,0:T(8,128)(2,1)} %bitcast.256, ...), custom_call_target="tpu_custom_call" | custom-call | tf_op jit(solution)/shard_map/pallas_call | solution.py:35
  134.7 3.4 convert_element_type.155
  138.1 7.4 %collective-permute-start.14 = (f16[4,2,192,512]{3,2,1,0:T(8,128)(2,1)}, f16[4,2,192,512]{3,2,1,0:T(8,128)(2,1)}, u32[]{:S(2)}, u32[]{:S(2)}) collective-permute-start(f16[4,2,192,512]{3,2,1,0:T(8,128)(2,1)} %convert_element_type.155), channel_id=1, source_target_pairs={{0,4},{2,6},{12,8},{14,10},{1,5},{3,7},{13,9},{15,11},{16,20},{18,... | collective-permute-start | bytes 4718600 | tf_op jit(solution)/shard_map/ppermute | solution.py:127
  145.5 1.9 add_convert_fusion.3
  161.6 6.0 %collective-permute-done.18 = bf16[2,2,96,512]{3,2,1,0:T(8,128)(2,1)} collective-permute-done((bf16[2,2,96,512]{3,2,1,0:T(8,128)(2,1)}, bf16[2,2,96,512]{3,2,1,0:T(8,128)(2,1)}, u32[]{:S(2)}, u32[]{:S(2)}) %collective-permute-start.18) | collective-permute-done | bytes 393248 | tf_op jit(solution)/shard_map/ppermute | solution.py:127
  170.5 7.0 %shard_map.70 = f32[4,2,192,512]{3,2,1,0:T(8,128)} custom-call(s32[2]{0:T(128)S(1)} %pad_add_fusion.1.place_ref, bf16[768,1024]{1,0:T(8,128)(2,1)S(1)} %bitcast.232, bf16[768,1024]{1,0:T(8,128)(2,1)S(1)} %bitcast.233, bf16[1024,7168]{1,0:T(8,128)(2,1)} %gate_ref.9, bf16[1024,7168]{1,0:T(8,128)(2,1)} %up_ref.9, bf16[2,2,1024,512]{3,2,1,0:T(8,128)(2,1)} %bitcast.258, ...), custom_call_target="tpu_custom_call" | custom-call | tf_op jit(solution)/shard_map/pallas_call | solution.py:35
  177.5 3.6 convert_element_type.161
  185.4 7.4 %all-gather.3 = bf16[4,2,96,512]{3,2,1,0:T(8,128)(2,1)} all-gather(bf16[2,2,96,512]{3,2,1,0:T(8,128)(2,1)S(1)} %broadcast_select_fusion.9), channel_id=5, replica_groups={{0,2},{4,6},{8,10},{12,14},{1,3},{5,7},{9,11},{13,15},{16,18},{20,22},{..., dimensions={0}, use_global_device_ids=true | all-gather | bytes 1179648 | tf_op jit(solution)/shard_map/all_gather | solution.py:154
  192.8 2.5 all-gather.4
  195.3 4.7 %collective-permute-start.22 = (f16[4,2,192,512]{3,2,1,0:T(8,128)(2,1)}, f16[4,2,192,512]{3,2,1,0:T(8,128)(2,1)}, u32[]{:S(2)}, u32[]{:S(2)}) collective-permute-start(f16[4,2,192,512]{3,2,1,0:T(8,128)(2,1)} %convert_element_type.161), channel_id=1, source_target_pairs={{0,4},{2,6},{12,8},{14,10},{1,5},{3,7},{13,9},{15,11},{16,20},{18,... | collective-permute-start | bytes 4718600 | tf_op jit(solution)/shard_map/ppermute | solution.py:127
  202.9 1.6 add_multiply_fusion.4
  205.8 1.7 collective-permute-start.26
  207.5 4.6 %collective-permute-done.21 = bf16[2,2,96,512]{3,2,1,0:T(8,128)(2,1)S(1)} collective-permute-done((bf16[2,2,96,512]{3,2,1,0:T(8,128)(2,1)}, bf16[2,2,96,512]{3,2,1,0:T(8,128)(2,1)S(1)}, u32[]{:S(2)}, u32[]{:S(2)}) %collective-permute-start.21) | collective-permute-done | bytes 393248 | tf_op jit(solution)/shard_map/ppermute | solution.py:127
  217.6 3.9 shard_map.71
  223.6 3.7 all-gather.5
  227.3 2.4 all-gather.6
  229.6 5.8 %shard_map.72 = (f32[1024,3584]{1,0:T(8,128)}, f32[1024,3584]{1,0:T(8,128)}) custom-call(bf16[1024,768]{1,0:T(8,128)(2,1)S(1)} %maximum_bitcast_fusion.features_ref, bf16[2,2,2,96,512]{4,3,2,1,0:T(8,128)(2,1)S(1)} %bitcast.238, bf16[2,2,2,96,512]{4,3,2,1,0:T(8,128)(2,1)S(1)} %bitcast.239, bf16[2,2,2,96,512]{4,3,2,1,0:T(8,128)(2,1)S(1)} %bitcast.240, ...), custom_call_target="tpu_custom_call" | custom-call | tf_op jit(solution)/shard_map/pallas_call | solution.py:81
  235.5 2.3 add_convert_fusion
  244.0 2.2 add_multiply_fusion
  246.2 1.6 add_multiply_fusion.3
  249.1 13.2 %collective-permute-done.25 = bf16[2,2,192,512]{3,2,1,0:T(8,128)(2,1)S(1)} collective-permute-done((bf16[2,2,192,512]{3,2,1,0:T(8,128)(2,1)}, bf16[2,2,192,512]{3,2,1,0:T(8,128)(2,1)S(1)}, u32[]{:S(2)}, u32[]{:S(2)}) %collective-permute-start.25) | collective-permute-done | bytes 786464 | tf_op jit(solution)/shard_map/ppermute | solution.py:127
  262.3 17.0 %collective-permute-done.27 = bf16[2,2,192,512]{3,2,1,0:T(8,128)(2,1)} collective-permute-done((bf16[2,2,192,512]{3,2,1,0:T(8,128)(2,1)}, bf16[2,2,192,512]{3,2,1,0:T(8,128)(2,1)}, u32[]{:S(2)}, u32[]{:S(2)}) %collective-permute-start.27) | collective-permute-done | bytes 786464 | tf_op jit(solution)/shard_map/ppermute | solution.py:127
  284.2 3.2 collective-permute-start.28
  291.2 2.1 broadcast_select_fusion.2
  293.4 1.6 multiply_convert_fusion
  298.2 7.5 %all-gather.29.cloned.1.call-done = bf16[4,2,192,512]{3,2,1,0:T(8,128)(2,1)} async-done(((bf16[2,2,192,512]{3,2,1,0:T(8,128)(2,1)}), bf16[4,2,192,512]{3,2,1,0:T(8,128)(2,1)}) %all-gather.29.cloned.1.call-update) | async-done | bytes 1572880 | tf_op jit(solution)/shard_map/all_gather | solution.py:154
  308.5 5.8 %shard_map.73 = (f32[1024,3584]{1,0:T(8,128)}, f32[1024,3584]{1,0:T(8,128)}) custom-call(bf16[1024,768]{1,0:T(8,128)(2,1)S(1)} %maximum_bitcast_fusion.features_ref, bf16[2,2,2,192,512]{4,3,2,1,0:T(8,128)(2,1)S(1)} %bitcast.246, bf16[2,2,2,192,512]{4,3,2,1,0:T(8,128)(2,1)S(1)} %bitcast.248, ...), custom_call_target="tpu_custom_call", output_to_operand_aliasing={{0}: (3, {}), {1}: (4, {})} | custom-call | tf_op jit(solution)/shard_map/pallas_call | solution.py:81
  316.1 6.2 %collective-permute-done.24 = bf16[2,96,1536]{2,1,0:T(8,128)(2,1)} collective-permute-done((bf16[2,96,1536]{2,1,0:T(8,128)(2,1)}, bf16[2,96,1536]{2,1,0:T(8,128)(2,1)}, u32[]{:S(2)}, u32[]{:S(2)}) %collective-permute-start.24) | collective-permute-done | bytes 589856 | tf_op jit(solution)/shard_map/ppermute | solution.py:127
  329.0 15.5 %collective-permute-done.30 = bf16[2,96,256]{2,1,0:T(8,128)(2,1)S(1)} collective-permute-done((bf16[2,96,256]{2,1,0:T(8,128)(2,1)S(1)}, bf16[2,96,256]{2,1,0:T(8,128)(2,1)S(1)}, u32[]{:S(2)}, u32[]{:S(2)}) %collective-permute-start.30) | collective-permute-done | bytes 98336 | tf_op jit(solution)/shard_map/ppermute | solution.py:127
  344.6 3.4 collective-permute-start.31
  352.7 2.1 broadcast_select_fusion.1
  356.1 3.8 collective-permute-done.32
  360.0 2.1 maximum_select_fusion.5
  362.0 1.6 collective-permute-done.33
  363.7 8.4 %collective-permute-done.35 = bf16[2,2,192,256]{3,2,1,0:T(8,128)(2,1)S(1)} collective-permute-done((bf16[2,2,192,256]{3,2,1,0:T(8,128)(2,1)S(1)}, bf16[2,2,192,256]{3,2,1,0:T(8,128)(2,1)S(1)}, u32[]{:S(2)}, u32[]{:S(2)}) %collective-permute-start.35) | collective-permute-done | bytes 393248 | tf_op jit(solution)/shard_map/ppermute | solution.py:127
  372.2 3.1 all-gather.9
  375.3 2.4 all-gather.10
  380.5 5.8 %shard_map.74 = (f32[1024,3584]{1,0:T(8,128)}, f32[1024,3584]{1,0:T(8,128)}) custom-call(bf16[1024,768]{1,0:T(8,128)(2,1)S(1)} %maximum_bitcast_fusion.features_ref, bf16[2,2,2,192,512]{4,3,2,1,0:T(8,128)(2,1)S(1)} %bitcast.249, bf16[2,2,2,192,512]{4,3,2,1,0:T(8,128)(2,1)S(1)} %bitcast.247, ...), custom_call_target="tpu_custom_call", output_to_operand_aliasing={{0}: (3, {}), {1}: (4, {})} | custom-call | tf_op jit(solution)/shard_map/pallas_call | solution.py:81
  386.3 3.3 shard_map.75
  (274 shorter events, 111.3 us)
Async XLA Ops:
  7.2 119.2 %all-gather.21.cloned.1.call-start = ((), (), s32[]{:S(2)}) async-start(), calls=%async_computation | async-start | bytes 6291456 | tf_op jit(solution)/shard_map/all_gather | solution.py:154
  7.2 11.2 %collective-permute-start = (bf16[384,512]{1,0:T(8,128)(2,1)}, bf16[384,512]{1,0:T(8,128)(2,1)S(1)}, u32[]{:S(2)}, u32[]{:S(2)}) collective-permute-start(bf16[384,512]{1,0:T(8,128)(2,1)} %bitcast.279), channel_id=1, source_target_pairs={{0,16},{16,0},{1,17},{17,1},{2,18},{18,2},{3,19},{19,3},{4,20},{20... | collective-permute-start | bytes 1179656 | tf_op jit(solution)/shard_map/ppermute | solution.py:167
  11.6 6.8 %copy-start.55 = (bf16[1,384,512]{2,1,0:T(8,128)(2,1)S(1)}, bf16[1,384,512]{2,1,0:T(8,128)(2,1)}, u32[]{:S(2)}) copy-start(bf16[1,384,512]{2,1,0:T(8,128)(2,1)} %param.4) | copy-start | bytes 1179652
  11.6 12.0 %collective-permute-start.3 = (bf16[1024,512]{1,0:T(8,128)(2,1)}, bf16[1024,512]{1,0:T(8,128)(2,1)S(1)}, u32[]{:S(2)}, u32[]{:S(2)}) collective-permute-start(bf16[1024,512]{1,0:T(8,128)(2,1)} %constant_dynamic-slice_fusion.1), channel_id=1, source_target_pairs={{0,2},{2,0},{4,6},{6,4},{8,10},{10,8},{12,14},{14,12},{1,3},{3,1},... | collective-permute-start | bytes 3145736 | tf_op jit(solution)/shard_map/ppermute | solution.py:127
  14.8 8.8 %collective-permute-start.2 = (bf16[1024,512]{1,0:T(8,128)(2,1)}, bf16[1024,512]{1,0:T(8,128)(2,1)S(1)}, u32[]{:S(2)}, u32[]{:S(2)}) collective-permute-start(bf16[1024,512]{1,0:T(8,128)(2,1)} %constant_dynamic-slice_fusion.2), channel_id=1, source_target_pairs={{0,2},{2,0},{4,6},{6,4},{8,10},{10,8},{12,14},{14,12},{1,3},{3,1},... | collective-permute-start | bytes 3145736 | tf_op jit(solution)/shard_map/ppermute | solution.py:127
  20.2 9.8 %copy-start = (bf16[4,96,1024]{2,1,0:T(8,128)(2,1)}, bf16[4,96,1024]{2,1,0:T(8,128)(2,1)S(1)}, u32[]{:S(2)}) copy-start(bf16[4,96,1024]{2,1,0:T(8,128)(2,1)S(1)} %reverse_select_fusion.1) | copy-start | bytes 2359300
  20.2 3.3 collective-permute-start.1
  23.5 6.5 %copy-start.9 = (bf16[1024,512]{1,0:T(8,128)(2,1)}, bf16[1024,512]{1,0:T(8,128)(2,1)S(1)}, u32[]{:S(2)}) copy-start(bf16[1024,512]{1,0:T(8,128)(2,1)S(1)} %collective-permute-done.3) | copy-start | bytes 3145732
  34.3 134.8 %all-gather.23.cloned.1.call-start = ((), (), s32[]{:S(2)}) async-start(), calls=%async_computation.1 | async-start | bytes 6291456 | tf_op jit(solution)/shard_map/all_gather | solution.py:154
  35.3 10.4 %collective-permute-start.4 = (bf16[384,512]{1,0:T(8,128)(2,1)S(1)}, bf16[384,512]{1,0:T(8,128)(2,1)S(1)}, u32[]{:S(2)}, u32[]{:S(2)}) collective-permute-start(bf16[384,512]{1,0:T(8,128)(2,1)S(1)} %bitcast.281), channel_id=1, source_target_pairs={{0,1},{1,0},{2,3},{3,2},{4,5},{5,4},{6,7},{7,6},{8,9},{9,8},{10,11... | collective-permute-start | bytes 1179656 | tf_op jit(solution)/shard_map/ppermute | solution.py:175
  36.8 17.3 %collective-permute-start.5 = (bf16[384,512]{1,0:T(8,128)(2,1)S(1)}, bf16[384,512]{1,0:T(8,128)(2,1)S(1)}, u32[]{:S(2)}, u32[]{:S(2)}) collective-permute-start(bf16[384,512]{1,0:T(8,128)(2,1)S(1)} %copy-done.58), channel_id=1, source_target_pairs={{0,1},{1,0},{2,3},{3,2},{4,5},{5,4},{6,7},{7,6},{8,9},{9,8},{10,11... | collective-permute-start | bytes 1179656 | tf_op jit(solution)/shard_map/ppermute | solution.py:176
  36.9 19.8 %copy-start.49 = (bf16[1,48,7168]{2,1,0:T(8,128)(2,1)S(1)}, bf16[1,48,7168]{2,1,0:T(8,128)(2,1)}, u32[]{:S(2)}) copy-start(bf16[1,48,7168]{2,1,0:T(8,128)(2,1)} %param.7) | copy-start | bytes 2064388
  55.4 16.4 %copy-start.2 = (bf16[4,96,1024]{2,1,0:T(8,128)(2,1)}, bf16[4,96,1024]{2,1,0:T(8,128)(2,1)S(1)}, u32[]{:S(2)}) copy-start(bf16[4,96,1024]{2,1,0:T(8,128)(2,1)S(1)} %reverse_select_fusion) | copy-start | bytes 2359300
  55.4 15.5 %collective-permute-start.6 = (bf16[4,96,1024]{2,1,0:T(8,128)(2,1)S(1)}, bf16[4,96,1024]{2,1,0:T(8,128)(2,1)S(1)}, u32[]{:S(2)}, u32[]{:S(2)}) collective-permute-start(bf16[4,96,1024]{2,1,0:T(8,128)(2,1)S(1)} %reverse_select_fusion), channel_id=1, source_target_pairs={{0,2},{2,0},{4,6},{6,4},{8,10},{10,8},{12,14},{14,12},{1,3},{3,1},... | collective-permute-start | bytes 2359304 | tf_op jit(solution)/shard_map/ppermute | solution.py:127
  57.6 9.8 %collective-permute-start.9 = (bf16[48,3584]{1,0:T(8,128)(2,1)}, bf16[48,3584]{1,0:T(8,128)(2,1)S(1)}, u32[]{:S(2)}, u32[]{:S(2)}) collective-permute-start(bf16[48,3584]{1,0:T(8,128)(2,1)} %get-tuple-element.133), channel_id=1, source_target_pairs={{0,1},{1,0},{2,3},{3,2},{4,5},{5,4},{6,7},{7,6},{8,9},{9,8},{10,11... | collective-permute-start | bytes 1032200 | tf_op jit(solution)/shard_map/ppermute | solution.py:172
  70.0 20.2 %collective-permute-start.10 = (bf16[2,48,1792]{2,1,0:T(8,128)(2,1)}, bf16[2,48,1792]{2,1,0:T(8,128)(2,1)}, u32[]{:S(2)}, u32[]{:S(2)}) collective-permute-start(bf16[2,48,1792]{2,1,0:T(8,128)(2,1)} %get-tuple-element.132), channel_id=1, source_target_pairs={{0,2},{2,0},{4,6},{6,4},{8,10},{10,8},{12,14},{14,12},{1,3},{3,1},... | collective-permute-start | bytes 1032200 | tf_op jit(solution)/shard_map/ppermute | solution.py:127
  84.7 130.0 %all-gather.25.cloned.1.call-start = ((), (), s32[]{:S(2)}) async-start(), calls=%async_computation.2 | async-start | bytes 3145728 | tf_op jit(solution)/shard_map/all_gather | solution.py:154
  86.6 10.1 %copy-start.42 = (bf16[384,1024]{1,0:T(8,128)(2,1)S(1)}, bf16[384,1024]{1,0:T(8,128)(2,1)}, u32[]{:S(2)}) copy-start(bf16[384,1024]{1,0:T(8,128)(2,1)} %copy-done.41) | copy-start | bytes 2359300
  86.6 20.5 %collective-permute-start.7 = (f16[4,2,96,512]{3,2,0,1:T(8,128)(2,1)S(1)}, f16[4,2,96,512]{3,2,0,1:T(8,128)(2,1)S(1)}, u32[]{:S(2)}, u32[]{:S(2)}) collective-permute-start(f16[4,2,96,512]{3,2,0,1:T(8,128)(2,1)S(1)} %copy-done.48), channel_id=1, source_target_pairs={{0,4},{2,6},{12,8},{14,10},{1,5},{3,7},{13,9},{15,11},{16,20},{18,... | collective-permute-start | bytes 2359304 | tf_op jit(solution)/shard_map/ppermute | solution.py:127
  92.3 29.7 %collective-permute-start.11 = (bf16[2,96,1792]{2,1,0:T(8,128)(2,1)}, bf16[2,96,1792]{2,1,0:T(8,128)(2,1)}, u32[]{:S(2)}, u32[]{:S(2)}) collective-permute-start(bf16[2,96,1792]{2,1,0:T(8,128)(2,1)} %maximum_select_fusion.2), channel_id=1, source_target_pairs={{0,4},{2,6},{12,8},{14,10},{1,5},{3,7},{13,9},{15,11},{16,20},{18,... | collective-permute-start | bytes 2064392 | tf_op jit(solution)/shard_map/ppermute | solution.py:127
  96.9 10.2 %copy-start.1 = (bf16[4,96,1024]{2,1,0:T(8,128)(2,1)S(1)}, bf16[4,96,1024]{2,1,0:T(8,128)(2,1)}, u32[]{:S(2)}) copy-start(bf16[4,96,1024]{2,1,0:T(8,128)(2,1)} %copy-done) | copy-start | bytes 2359300
  96.9 10.3 %copy-start.4 = (bf16[4,96,1024]{2,1,0:T(8,128)(2,1)S(1)}, bf16[4,96,1024]{2,1,0:T(8,128)(2,1)}, u32[]{:S(2)}) copy-start(bf16[4,96,1024]{2,1,0:T(8,128)(2,1)} %copy-done.2) | copy-start | bytes 2359300
  98.2 47.2 %collective-permute-start.12 = (f16[4,2,96,512]{3,2,1,0:T(8,128)(2,1)}, f16[4,2,96,512]{3,2,1,0:T(8,128)(2,1)}, u32[]{:S(2)}, u32[]{:S(2)}) collective-permute-start(f16[4,2,96,512]{3,2,1,0:T(8,128)(2,1)} %convert_element_type.146), channel_id=1, source_target_pairs={{0,4},{2,6},{12,8},{14,10},{1,5},{3,7},{13,9},{15,11},{16,20},{18,... | collective-permute-start | bytes 2359304 | tf_op jit(solution)/shard_map/ppermute | solution.py:127
  108.1 11.5 %collective-permute-start.8 = (f16[2,2,96,512]{3,2,0,1:T(8,128)(2,1)}, f16[2,2,96,512]{3,2,0,1:T(8,128)(2,1)}, u32[]{:S(2)}, u32[]{:S(2)}) collective-permute-start(f16[2,2,96,512]{3,2,0,1:T(8,128)(2,1)} %fusion), channel_id=1, source_target_pairs={{4,8},{6,10},{8,4},{10,6},{5,9},{7,11},{9,5},{11,7},{20,24},{22,26... | collective-permute-start | bytes 1179656 | tf_op jit(solution)/shard_map/ppermute | solution.py:127
  123.4 26.8 %collective-permute-start.17 = (bf16[2,2,96,512]{3,2,1,0:T(8,128)(2,1)S(1)}, bf16[2,2,96,512]{3,2,1,0:T(8,128)(2,1)}, u32[]{:S(2)}, u32[]{:S(2)}) collective-permute-start(bf16[2,2,96,512]{3,2,1,0:T(8,128)(2,1)S(1)} %select_convert_fusion.4), channel_id=1, source_target_pairs={{4,8},{6,10},{8,4},{10,6},{5,9},{7,11},{9,5},{11,7},{20,24},{22,26... | collective-permute-start | bytes 1179656 | tf_op jit(solution)/shard_map/ppermute | solution.py:127
  138.1 10.7 %copy-start.43 = (bf16[384,1024]{0,1:T(8,128)(2,1)S(1)}, bf16[384,1024]{0,1:T(8,128)(2,1)}, u32[]{:S(2)}) copy-start(bf16[384,1024]{0,1:T(8,128)(2,1)} %copy.77) | copy-start | bytes 2359300
  138.1 10.7 %copy-start.44 = (bf16[384,1024]{0,1:T(8,128)(2,1)S(1)}, bf16[384,1024]{0,1:T(8,128)(2,1)}, u32[]{:S(2)}) copy-start(bf16[384,1024]{0,1:T(8,128)(2,1)} %copy.78) | copy-start | bytes 2359300
  138.1 43.0 %collective-permute-start.14 = (f16[4,2,192,512]{3,2,1,0:T(8,128)(2,1)}, f16[4,2,192,512]{3,2,1,0:T(8,128)(2,1)}, u32[]{:S(2)}, u32[]{:S(2)}) collective-permute-start(f16[4,2,192,512]{3,2,1,0:T(8,128)(2,1)} %convert_element_type.155), channel_id=1, source_target_pairs={{0,4},{2,6},{12,8},{14,10},{1,5},{3,7},{13,9},{15,11},{16,20},{18,... | collective-permute-start | bytes 4718600 | tf_op jit(solution)/shard_map/ppermute | solution.py:127
  147.3 7.5 %collective-permute-start.13 = (f16[2,2,96,512]{3,2,1,0:T(8,128)(2,1)}, f16[2,2,96,512]{3,2,1,0:T(8,128)(2,1)}, u32[]{:S(2)}, u32[]{:S(2)}) collective-permute-start(f16[2,2,96,512]{3,2,1,0:T(8,128)(2,1)} %add_convert_fusion.3), channel_id=1, source_target_pairs={{4,8},{6,10},{8,4},{10,6},{5,9},{7,11},{9,5},{11,7},{20,24},{22,26... | collective-permute-start | bytes 1179656 | tf_op jit(solution)/shard_map/ppermute | solution.py:127
  148.9 12.7 %collective-permute-start.16 = (bf16[2,2,96,512]{3,2,1,0:T(8,128)(2,1)S(1)}, bf16[2,2,96,512]{3,2,1,0:T(8,128)(2,1)}, u32[]{:S(2)}, u32[]{:S(2)}) collective-permute-start(bf16[2,2,96,512]{3,2,1,0:T(8,128)(2,1)S(1)} %select_convert_fusion.4), channel_id=1, source_target_pairs={{4,0},{6,2},{8,12},{10,14},{5,1},{7,3},{9,13},{11,15},{20,16},{22,... | collective-permute-start | bytes 1179656 | tf_op jit(solution)/shard_map/ppermute | solution.py:127
  150.2 17.4 %collective-permute-start.18 = (bf16[2,2,96,512]{3,2,1,0:T(8,128)(2,1)}, bf16[2,2,96,512]{3,2,1,0:T(8,128)(2,1)}, u32[]{:S(2)}, u32[]{:S(2)}) collective-permute-start(bf16[2,2,96,512]{3,2,1,0:T(8,128)(2,1)} %collective-permute-done.17), channel_id=1, source_target_pairs={{4,0},{6,2},{8,12},{10,14},{5,1},{7,3},{9,13},{11,15},{20,16},{22,... | collective-permute-start | bytes 1179656 | tf_op jit(solution)/shard_map/ppermute | solution.py:127
  154.8 143.4 %all-gather.27.cloned.1.call-start = ((), (), s32[]{:S(2)}) async-start(), calls=%async_computation.3 | async-start | bytes 2359296 | tf_op jit(solution)/shard_map/all_gather | solution.py:154
  156.2 11.4 %copy-start.25 = (bf16[4,2,96,1024]{3,2,0,1:T(8,128)(2,1)S(1)}, bf16[4,2,96,1024]{3,2,0,1:T(8,128)(2,1)}, u32[]{:S(2)}) copy-start(bf16[4,2,96,1024]{3,2,0,1:T(8,128)(2,1)} %pad_maximum_fusion.2) | copy-start | bytes 4718596
  158.6 9.2 %copy-start.28 = (bf16[4,2,96,1024]{3,2,0,1:T(8,128)(2,1)S(1)}, bf16[4,2,96,1024]{3,2,0,1:T(8,128)(2,1)}, u32[]{:S(2)}) copy-start(bf16[4,2,96,1024]{3,2,0,1:T(8,128)(2,1)} %copy-done.27) | copy-start | bytes 4718596
  158.6 41.5 %collective-permute-start.20 = (bf16[2,2,96,512]{3,2,1,0:T(8,128)(2,1)}, bf16[2,2,96,512]{3,2,1,0:T(8,128)(2,1)}, u32[]{:S(2)}, u32[]{:S(2)}) collective-permute-start(bf16[2,2,96,512]{3,2,1,0:T(8,128)(2,1)} %select_convert_fusion.3), channel_id=1, source_target_pairs={{4,8},{6,10},{8,4},{10,6},{5,9},{7,11},{9,5},{11,7},{20,24},{22,26... | collective-permute-start | bytes 1179656 | tf_op jit(solution)/shard_map/ppermute | solution.py:127
  160.1 47.4 %collective-permute-start.19 = (bf16[2,2,96,512]{3,2,1,0:T(8,128)(2,1)}, bf16[2,2,96,512]{3,2,1,0:T(8,128)(2,1)}, u32[]{:S(2)}, u32[]{:S(2)}) collective-permute-start(bf16[2,2,96,512]{3,2,1,0:T(8,128)(2,1)} %select_convert_fusion.3), channel_id=1, source_target_pairs={{4,0},{6,2},{8,12},{10,14},{5,1},{7,3},{9,13},{11,15},{20,16},{22,... | collective-permute-start | bytes 1179656 | tf_op jit(solution)/shard_map/ppermute | solution.py:127
  182.6 18.8 %collective-permute-start.15 = (f16[2,2,192,512]{3,2,1,0:T(8,128)(2,1)S(1)}, f16[2,2,192,512]{3,2,1,0:T(8,128)(2,1)S(1)}, u32[]{:S(2)}, u32[]{:S(2)}) collective-permute-start(f16[2,2,192,512]{3,2,1,0:T(8,128)(2,1)S(1)} %add_convert_fusion.1), channel_id=1, source_target_pairs={{4,8},{6,10},{8,4},{10,6},{5,9},{7,11},{9,5},{11,7},{20,24},{22,26... | collective-permute-start | bytes 2359304 | tf_op jit(solution)/shard_map/ppermute | solution.py:127
  195.3 7.6 %copy-start.32 = (bf16[1,2,96,1792]{3,2,1,0:T(8,128)(2,1)S(1)}, bf16[1,2,96,1792]{3,2,1,0:T(8,128)(2,1)}, u32[]{:S(2)}) copy-start(bf16[1,2,96,1792]{3,2,1,0:T(8,128)(2,1)} %maximum_select_fusion.3) | copy-start | bytes 2064388
  195.3 40.2 %collective-permute-start.22 = (f16[4,2,192,512]{3,2,1,0:T(8,128)(2,1)}, f16[4,2,192,512]{3,2,1,0:T(8,128)(2,1)}, u32[]{:S(2)}, u32[]{:S(2)}) collective-permute-start(f16[4,2,192,512]{3,2,1,0:T(8,128)(2,1)} %convert_element_type.161), channel_id=1, source_target_pairs={{0,4},{2,6},{12,8},{14,10},{1,5},{3,7},{13,9},{15,11},{16,20},{18,... | collective-permute-start | bytes 4718600 | tf_op jit(solution)/shard_map/ppermute | solution.py:127
  200.0 12.1 %collective-permute-start.21 = (bf16[2,2,96,512]{3,2,1,0:T(8,128)(2,1)}, bf16[2,2,96,512]{3,2,1,0:T(8,128)(2,1)S(1)}, u32[]{:S(2)}, u32[]{:S(2)}) collective-permute-start(bf16[2,2,96,512]{3,2,1,0:T(8,128)(2,1)} %collective-permute-done.20), channel_id=1, source_target_pairs={{4,0},{6,2},{8,12},{10,14},{5,1},{7,3},{9,13},{11,15},{20,16},{22,... | collective-permute-start | bytes 1179656 | tf_op jit(solution)/shard_map/ppermute | solution.py:127
  204.5 7.7 %copy-start.26 = (bf16[4,2,96,1024]{3,2,0,1:T(8,128)(2,1)S(1)}, bf16[4,2,96,1024]{3,2,0,1:T(8,128)(2,1)}, u32[]{:S(2)}) copy-start(bf16[4,2,96,1024]{3,2,0,1:T(8,128)(2,1)} %pad_maximum_fusion.2) | copy-start | bytes 4718596
  205.8 7.7 %copy-start.29 = (bf16[4,2,96,1024]{3,2,0,1:T(8,128)(2,1)S(1)}, bf16[4,2,96,1024]{3,2,0,1:T(8,128)(2,1)}, u32[]{:S(2)}) copy-start(bf16[4,2,96,1024]{3,2,0,1:T(8,128)(2,1)} %copy-done.27) | copy-start | bytes 4718596
  205.8 36.9 %collective-permute-start.26 = (bf16[2,2,192,512]{3,2,1,0:T(8,128)(2,1)}, bf16[2,2,192,512]{3,2,1,0:T(8,128)(2,1)}, u32[]{:S(2)}, u32[]{:S(2)}) collective-permute-start(bf16[2,2,192,512]{3,2,1,0:T(8,128)(2,1)} %select_convert_fusion.1), channel_id=1, source_target_pairs={{4,8},{6,10},{8,4},{10,6},{5,9},{7,11},{9,5},{11,7},{20,24},{22,26... | collective-permute-start | bytes 2359304 | tf_op jit(solution)/shard_map/ppermute | solution.py:127
  223.5 6.1 %copy-start.14 = (bf16[4,2,96,512]{3,2,1,0:T(8,128)(2,1)S(1)}, bf16[4,2,96,512]{3,2,1,0:T(8,128)(2,1)}, u32[]{:S(2)}) copy-start(bf16[4,2,96,512]{3,2,1,0:T(8,128)(2,1)} %all-gather.3) | copy-start | bytes 2359300
  237.8 6.2 %collective-permute-start.23 = (f16[2,2,192,512]{3,2,1,0:T(8,128)(2,1)}, f16[2,2,192,512]{3,2,1,0:T(8,128)(2,1)}, u32[]{:S(2)}, u32[]{:S(2)}) collective-permute-start(f16[2,2,192,512]{3,2,1,0:T(8,128)(2,1)} %add_convert_fusion), channel_id=1, source_target_pairs={{4,8},{6,10},{8,4},{10,6},{5,9},{7,11},{9,5},{11,7},{20,24},{22,26... | collective-permute-start | bytes 2359304 | tf_op jit(solution)/shard_map/ppermute | solution.py:127
  241.3 21.0 %collective-permute-start.25 = (bf16[2,2,192,512]{3,2,1,0:T(8,128)(2,1)}, bf16[2,2,192,512]{3,2,1,0:T(8,128)(2,1)S(1)}, u32[]{:S(2)}, u32[]{:S(2)}) collective-permute-start(bf16[2,2,192,512]{3,2,1,0:T(8,128)(2,1)} %select_convert_fusion.1), channel_id=1, source_target_pairs={{4,0},{6,2},{8,12},{10,14},{5,1},{7,3},{9,13},{11,15},{20,16},{22,... | collective-permute-start | bytes 2359304 | tf_op jit(solution)/shard_map/ppermute | solution.py:127
  242.7 36.5 %collective-permute-start.27 = (bf16[2,2,192,512]{3,2,1,0:T(8,128)(2,1)}, bf16[2,2,192,512]{3,2,1,0:T(8,128)(2,1)}, u32[]{:S(2)}, u32[]{:S(2)}) collective-permute-start(bf16[2,2,192,512]{3,2,1,0:T(8,128)(2,1)} %collective-permute-done.26), channel_id=1, source_target_pairs={{4,0},{6,2},{8,12},{10,14},{5,1},{7,3},{9,13},{11,15},{20,16},{22,... | collective-permute-start | bytes 2359304 | tf_op jit(solution)/shard_map/ppermute | solution.py:127
  280.3 25.4 %all-gather.29.cloned.1.call-start = ((), (), s32[]{:S(2)}) async-start(), calls=%async_computation.4 | async-start | bytes 2359296 | tf_op jit(solution)/shard_map/all_gather | solution.py:154
  280.3 7.1 %copy-start.36 = (f32[2,2,192,512]{3,2,1,0:T(8,128)S(1)}, f32[2,2,192,512]{3,2,1,0:T(8,128)}, u32[]{:S(2)}) copy-start(f32[2,2,192,512]{3,2,1,0:T(8,128)} %copy-done.35) | copy-start | bytes 4718596
  284.2 30.0 %collective-permute-start.28 = (f16[4,2,192,256]{3,2,1,0:T(8,128)(2,1)}, f16[4,2,192,256]{3,2,1,0:T(8,128)(2,1)}, u32[]{:S(2)}, u32[]{:S(2)}) collective-permute-start(f16[4,2,192,256]{3,2,1,0:T(8,128)(2,1)} %convert_element_type.169), channel_id=1, source_target_pairs={{0,4},{2,6},{12,8},{14,10},{1,5},{3,7},{13,9},{15,11},{16,20},{18,... | collective-permute-start | bytes 2359304 | tf_op jit(solution)/shard_map/ppermute | solution.py:127
  288.4 35.1 %collective-permute-start.37 = (bf16[2,2,192,512]{3,2,1,0:T(8,128)(2,1)}, bf16[2,2,192,512]{3,2,1,0:T(8,128)(2,1)}, u32[]{:S(2)}, u32[]{:S(2)}) collective-permute-start(bf16[2,2,192,512]{3,2,1,0:T(8,128)(2,1)} %select_convert_fusion), channel_id=1, source_target_pairs={{4,8},{6,10},{8,4},{10,6},{5,9},{7,11},{9,5},{11,7},{20,24},{22,26... | collective-permute-start | bytes 2359304 | tf_op jit(solution)/shard_map/ppermute | solution.py:127
  289.9 58.9 %collective-permute-start.36 = (bf16[2,2,192,512]{3,2,1,0:T(8,128)(2,1)}, bf16[2,2,192,512]{3,2,1,0:T(8,128)(2,1)}, u32[]{:S(2)}, u32[]{:S(2)}) collective-permute-start(bf16[2,2,192,512]{3,2,1,0:T(8,128)(2,1)} %select_convert_fusion), channel_id=1, source_target_pairs={{4,0},{6,2},{8,12},{10,14},{5,1},{7,3},{9,13},{11,15},{20,16},{22,... | collective-permute-start | bytes 2359304 | tf_op jit(solution)/shard_map/ppermute | solution.py:127
  293.4 84.3 %all-gather.33.cloned.1.call-start = ((), (), s32[]{:S(2)}) async-start(), calls=%async_computation.6 | async-start | bytes 2359296 | tf_op jit(solution)/shard_map/all_gather | solution.py:154
  296.1 26.2 %collective-permute-start.24 = (bf16[2,96,1536]{2,1,0:T(8,128)(2,1)}, bf16[2,96,1536]{2,1,0:T(8,128)(2,1)}, u32[]{:S(2)}, u32[]{:S(2)}) collective-permute-start(bf16[2,96,1536]{2,1,0:T(8,128)(2,1)} %pad_maximum_fusion.8), channel_id=1, source_target_pairs={{4,0},{6,2},{8,12},{10,14},{5,1},{7,3},{9,13},{11,15},{20,16},{22,... | collective-permute-start | bytes 1769480 | tf_op jit(solution)/shard_map/ppermute | solution.py:127
  314.3 8.1 %copy-start.45 = (bf16[1,96,1536]{2,1,0:T(8,128)(2,1)S(1)}, bf16[1,96,1536]{2,1,0:T(8,128)(2,1)}, u32[]{:S(2)}) copy-start(bf16[1,96,1536]{2,1,0:T(8,128)(2,1)} %maximum_bitcast_fusion.4) | copy-start | bytes 884740
  315.4 9.5 %collective-permute-start.29 = (f16[2,2,192,256]{3,2,1,0:T(8,128)(2,1)S(1)}, f16[2,2,192,256]{3,2,1,0:T(8,128)(2,1)S(1)}, u32[]{:S(2)}, u32[]{:S(2)}) collective-permute-start(f16[2,2,192,256]{3,2,1,0:T(8,128)(2,1)S(1)} %add_convert_fusion.2), channel_id=1, source_target_pairs={{4,8},{6,10},{8,4},{10,6},{5,9},{7,11},{9,5},{11,7},{20,24},{22,26... | collective-permute-start | bytes 1179656 | tf_op jit(solution)/shard_map/ppermute | solution.py:127
  323.5 25.3 %collective-permute-start.38 = (bf16[2,2,192,512]{3,2,1,0:T(8,128)(2,1)}, bf16[2,2,192,512]{3,2,1,0:T(8,128)(2,1)S(1)}, u32[]{:S(2)}, u32[]{:S(2)}) collective-permute-start(bf16[2,2,192,512]{3,2,1,0:T(8,128)(2,1)} %collective-permute-done.37), channel_id=1, source_target_pairs={{4,0},{6,2},{8,12},{10,14},{5,1},{7,3},{9,13},{11,15},{20,16},{22,... | collective-permute-start | bytes 2359304 | tf_op jit(solution)/shard_map/ppermute | solution.py:127
  327.3 17.1 %collective-permute-start.30 = (bf16[2,96,256]{2,1,0:T(8,128)(2,1)S(1)}, bf16[2,96,256]{2,1,0:T(8,128)(2,1)S(1)}, u32[]{:S(2)}, u32[]{:S(2)}) collective-permute-start(bf16[2,96,256]{2,1,0:T(8,128)(2,1)S(1)} %pad_maximum_fusion.14), channel_id=1, source_target_pairs={{4,0},{6,2},{8,12},{10,14},{5,1},{7,3},{9,13},{11,15},{20,16},{22,... | collective-permute-start | bytes 294920 | tf_op jit(solution)/shard_map/ppermute | solution.py:127
  344.6 5.3 %collective-permute-start.31 = (bf16[2,48,1792]{2,1,0:T(8,128)(2,1)S(1)}, bf16[2,48,1792]{2,1,0:T(8,128)(2,1)S(1)}, u32[]{:S(2)}, u32[]{:S(2)}) collective-permute-start(bf16[2,48,1792]{2,1,0:T(8,128)(2,1)S(1)} %get-tuple-element.130), channel_id=1, source_target_pairs={{0,2},{2,0},{4,6},{6,4},{8,10},{10,8},{12,14},{14,12},{1,3},{3,1},... | collective-permute-start | bytes 1032200 | tf_op jit(solution)/shard_map/ppermute | solution.py:127
  348.1 6.8 %collective-permute-start.34 = (bf16[2,2,192,256]{3,2,1,0:T(8,128)(2,1)S(1)}, bf16[2,2,192,256]{3,2,1,0:T(8,128)(2,1)S(1)}, u32[]{:S(2)}, u32[]{:S(2)}) collective-permute-start(bf16[2,2,192,256]{3,2,1,0:T(8,128)(2,1)S(1)} %select_convert_fusion.2), channel_id=1, source_target_pairs={{4,8},{6,10},{8,4},{10,6},{5,9},{7,11},{9,5},{11,7},{20,24},{22,26... | collective-permute-start | bytes 1179656 | tf_op jit(solution)/shard_map/ppermute | solution.py:127
  349.8 27.9 %all-gather.31.cloned.1.call-start = ((), (), s32[]{:S(2)}) async-start(), calls=%async_computation.5 | async-start | bytes 2359296 | tf_op jit(solution)/shard_map/all_gather | solution.py:154
  350.1 9.9 %collective-permute-start.32 = (bf16[48,3584]{1,0:T(8,128)(2,1)S(1)}, bf16[48,3584]{1,0:T(8,128)(2,1)}, u32[]{:S(2)}, u32[]{:S(2)}) collective-permute-start(bf16[48,3584]{1,0:T(8,128)(2,1)S(1)} %get-tuple-element.128), channel_id=1, source_target_pairs={{0,1},{1,0},{2,3},{3,2},{4,5},{5,4},{6,7},{7,6},{8,9},{9,8},{10,11... | collective-permute-start | bytes 1032200 | tf_op jit(solution)/shard_map/ppermute | solution.py:297
  351.4 12.3 %collective-permute-start.33 = (bf16[2,2,192,256]{3,2,1,0:T(8,128)(2,1)S(1)}, bf16[2,2,192,256]{3,2,1,0:T(8,128)(2,1)S(1)}, u32[]{:S(2)}, u32[]{:S(2)}) collective-permute-start(bf16[2,2,192,256]{3,2,1,0:T(8,128)(2,1)S(1)} %select_convert_fusion.2), channel_id=1, source_target_pairs={{4,0},{6,2},{8,12},{10,14},{5,1},{7,3},{9,13},{11,15},{20,16},{22,... | collective-permute-start | bytes 1179656 | tf_op jit(solution)/shard_map/ppermute | solution.py:127
  354.8 17.3 %collective-permute-start.35 = (bf16[2,2,192,256]{3,2,1,0:T(8,128)(2,1)S(1)}, bf16[2,2,192,256]{3,2,1,0:T(8,128)(2,1)S(1)}, u32[]{:S(2)}, u32[]{:S(2)}) collective-permute-start(bf16[2,2,192,256]{3,2,1,0:T(8,128)(2,1)S(1)} %collective-permute-done.34), channel_id=1, source_target_pairs={{4,0},{6,2},{8,12},{10,14},{5,1},{7,3},{9,13},{11,15},{20,16},{22,... | collective-permute-start | bytes 1179656 | tf_op jit(solution)/shard_map/ppermute | solution.py:127
  (42 other events, 82.6 us)
Sparse Core Ops, SparseCore 0:
  34.4 15.2 all-gather.20
  84.8 14.9 all-gather.22
  154.9 15.1 all-gather.24
  280.4 9.6 all-gather.26
  293.5 12.1 all-gather.28
  349.9 10.4 all-gather.32
  362.0 10.9 all-gather.30

commit v8 on v6

--- a/solution.py
+++ b/solution.py
@@ -11,7 +11,6 @@
 WIRE = jnp.float16
 LARGEST_TOKEN, LARGEST_WEIGHT = 6.0, 0.0625
 VMEM_LIMIT = 48 * 2**20
-NO_COST = pl.CostEstimate(flops=0, bytes_accessed=0, transcendentals=0)
 SHARES = (2, 2, 2, 1)
 
 
@@ -48,7 +47,11 @@
             out_specs=pl.BlockSpec((blocks, 2, rows, tile), lambda j, place: (0, 0, 0, j)),
         ),
         compiler_params=pltpu.CompilerParams(vmem_limit_bytes=VMEM_LIMIT),
-        cost_estimate=NO_COST,
+        cost_estimate=pl.CostEstimate(
+            flops=8 * total * depth * width,
+            bytes_accessed=8 * depth * width + 8 * total * width + 4 * total * depth,
+            transcendentals=0,
+        ),
     )(place, mine, theirs, gate_weight, up_weight, *far)
 
 
@@ -99,7 +102,11 @@
         ),
         input_output_aliases={first + i: i for i in range(len(totals))},
         compiler_params=pltpu.CompilerParams(vmem_limit_bytes=VMEM_LIMIT),
-        cost_estimate=NO_COST,
+        cost_estimate=pl.CostEstimate(
+            flops=8 * total * depth * width,
+            bytes_accessed=(16 * depth + 8 * total) * width + 2 * total * depth,
+            transcendentals=0,
+        ),
     )(place, features, *own, *other, *totals)
 
 
@@ -164,19 +171,34 @@
     def exchange_weights(k, after):
         _, start, width = pieces[k]
         first = part * half + (1 - core) * share + start
-        return [
-            send(tie(columns_of(weight, first, width), after), pairs)
-            for weight in (gate_weight, up_weight)
+        chosen = [
+            columns_of(weight, first, width) for weight in tie((gate_weight, up_weight), after)
         ]
+        return [send(value, pairs) for value in chosen]
 
     mine = tokens[0]
     over_row = lax.ppermute(mine, "row", swap)
+    cotangent = grad_hidden[0]
+    cotangent = jnp.stack(
+        [
+            columns_of(cotangent, part * half, half),
+            lax.ppermute(columns_of(cotangent, (1 - part) * half, half), "depth", swap),
+        ]
+    )
     over_depth = lax.ppermute(mine, "depth", swap)
     over_both = lax.ppermute(over_row, "depth", swap)
     far_weights = {0: exchange_weights(0, ())}
     far_weights[1] = far_weights[0]
     first_tile = ((part * half + core * share) // tile).astype(jnp.int32).reshape(1)
 
+    cotangent = by(
+        core == 0,
+        columns_of(cotangent, core * share, share),
+        send(columns_of(cotangent, (1 - core) * share, share), pairs),
+        1,
+    )
+    cotangent = jnp.stack([send(cotangent, inward), cotangent])
+
     def arrange(values):
         values = values.reshape(line, rows, depth)
         return jnp.where(at_far, values[::-1], values)
@@ -200,23 +222,8 @@
     over_depth, over_both = tie((over_depth, over_both), payload)
     features.append(by(row == 0, over_depth, over_both, 1))
     spread.append(both_cores(features[1], ()))
-    for k in range(2, last + 1):
-        far_weights[k] = exchange_weights(k, spread[1] if k < 4 else inner[0])
-
-    mine_cotangent, cotangent = tie((grad_hidden[0], grad_hidden[0]), payload)
-    cotangent = jnp.stack(
-        [
-            columns_of(mine_cotangent, part * half, half),
-            lax.ppermute(columns_of(cotangent, (1 - part) * half, half), "depth", swap),
-        ]
-    )
-    cotangent = by(
-        core == 0,
-        columns_of(cotangent, core * share, share),
-        send(columns_of(cotangent, (1 - core) * share, share), pairs),
-        1,
-    )
-    cotangent = jnp.stack([send(cotangent, inward), cotangent])
+    far_weights[2] = exchange_weights(2, payload)
+    both_rows = [jnp.stack(pair, axis=1) for pair in zip(*spread)]
 
     def activate(k, summed):
         batches, start, width = pieces[k]
@@ -225,18 +232,19 @@
         squash = jax.nn.sigmoid(gate_sum)
         product = (gate_sum * squash * up_sum).astype(jnp.bfloat16)
         given = wide(cotangent[:, batches[0] : batches[-1] + 1, :, start : start + width])
-        gate_act = given * up_sum * squash * (1.0 + gate_sum * (1.0 - squash))
-        up_act = given * gate_sum * squash
-        act = jnp.stack([gate_act, up_act], axis=1).astype(jnp.bfloat16)
+        given = given * squash
+        gate_act = given * up_sum * (1.0 + gate_sum * (1.0 - squash))
+        up_act = given * gate_sum
+        is_gate = lax.broadcasted_iota(jnp.int32, (2, 2, *given.shape[1:]), 1) == 0
+        act = jnp.where(is_gate, gate_act[:, None], up_act[:, None]).astype(jnp.bfloat16)
         return product, act.reshape(2, 2, len(batches) * rows, width)
 
     def by_side(values):
-        values = values.reshape(line, rows * depth)
+        values = values.reshape(line, rows, depth)
         values = jnp.concatenate([values[:2], values[3:], values[2:3]])
         return values.reshape(-1, depth)
 
     turned = jnp.concatenate([by_side(tie(near, inner[0])) for near, _ in spread]).T
-    place = jnp.stack([core, 1 - core]).astype(jnp.int32) * (share // tile)
 
     def outer_hidden(ks):
         def joined(batch, which):
@@ -249,50 +257,45 @@
         theirs = send(jnp.stack([joined(batch, 0) for batch in range(2)]), outward)
         return jnp.where(at_end, theirs, jnp.stack(own))
 
+    order = jnp.stack([core, 1 - core]).astype(jnp.int32) * (share // tile)
     got, act, hidden, near_out, far_out, across = {}, {}, {}, {}, {}, {}
     totals, waiting, hiddens = (), [], []
+    outer = over_centre = inner[0]
     for t in range(last + 3):
-        before = []
+        k = t
+        if k <= last:
+            if k < last:
+                tokens = spread[1] if k == 0 else both_rows
+                terms[k + 1] = multiply(k + 1, tokens, ())
+                payload = terms[k + 1].astype(WIRE)
+                inner[k + 1] = send(tie(payload, inner[k]), inward)
+            if k + 3 <= last:
+                far_weights[k + 3] = exchange_weights(k + 3, payload)
+            mine = tie(terms[k], over_centre, totals)
+            got[k] = over_centre = send(add(mine[2:], inner[k][2:]).astype(WIRE), centre)
         k = t - 1
         if 0 <= k <= last:
-            summed = jnp.stack([terms[k][0] + wide(got[k][1]), terms[k][1] + wide(got[k][0])])
-            hidden[k], act[k] = activate(k, summed)
-            across[k], near_out[k] = send(act[k], centre), send(act[k], outward)
-            before.append(act[k])
-            if k == last - 1:
-                hiddens.append(outer_hidden(range(last)))
+            hidden[k], act[k] = activate(k, add(terms[k][:2], inner[k][:2], got[k][::-1]))
+            across[k] = over_centre = send(tie(act[k], over_centre), centre)
+            near_out[k] = outer = send(tie(act[k], outer), outward)
             if k == last:
                 hiddens.append(outer_hidden([last]))
         k = t - 2
         if 0 <= k <= last:
-            near_mine, near_got, far_mine, far_got = tie(
-                (act[k], near_out[k], across[k], far_out[k]), before
-            )
             mine = [
-                jnp.where(at_end, near_got, near_mine),
-                jnp.where(at_end, far_got, far_mine),
+                jnp.where(at_end, near_out[k], act[k]),
+                jnp.where(at_end, far_out[k], across[k]),
             ]
             waiting.append((mine, [send(value, pairs) for value in mine]))
-        k = t + 1
-        if k <= last:
-            tokens = spread[1] if k == 1 else [jnp.stack(pair, axis=1) for pair in zip(*spread)]
-            terms[k] = multiply(k, tokens, before)
-            payload = terms[k].astype(WIRE)
-            inner[k] = send(payload, inward)
-            before.append(payload)
-        k = t - 2
-        if 0 <= k <= last and pieces[k][0] != (0,):
-            own, other = (sum(values, []) for values in zip(*waiting))
-            totals = gradient(place, turned, own, other, totals, half, pieces[k][1], tile)
-            waiting = []
-            before.append(totals)
-        k = t
-        if k <= last:
-            terms[k] = tie(terms[k], before) + wide(inner[k])
-            got[k] = send(terms[k][2:].astype(WIRE), centre)
+            if pieces[k][0] != (0,):
+                own, other = (sum(values, []) for values in zip(*waiting))
+                totals = gradient(order, turned, own, other, totals, half, pieces[k][1], tile)
+                waiting = []
         k = t - 1
         if 0 <= k <= last:
-            far_out[k] = send(across[k], outward)
+            far_out[k] = outer = send(tie(across[k], outer, totals), outward)
+            if k == last - 1:
+                hiddens.append(outer_hidden(range(last)))
 
     hidden = jnp.concatenate(hiddens, axis=2).reshape(2, 2, slab, share)
     mine = lax.dynamic_index_in_dim(hidden, core, 1, keepdims=False)

time: 333 us -> 353 us (1.060)
  waiting for transfers between devices: 121 us -> 165 us
  starting transfers between devices: 96.7 us -> 72 us
    ppermute x50, waiting for transfers between devices: 106 us -> 158 us  [send(): return lax.ppermute(value, 'col', route)]
    ppermute x50, starting transfers between devices: 90.2 us -> 66.6 us  [send(): return lax.ppermute(value, 'col', route)]
    add x8 -> x0, other arithmetic: 8.09 us -> none  [the longest x5 5.88 us: local(): terms[k] = tie(terms[k], before) + wide(inner[k])]
    dynamic_slice x4 -> x9, local copies, waits for them, and re-layouts: 9.49 us -> 16.4 us  [columns_of(): return lax.dynamic_slice_in_dim(array, start, width, array.ndim - 1)]
    ppermute x1, waiting for transfers between devices: 6.54 us -> 0.01 us  [local(): over_both = lax.ppermute(over_row, 'depth', swap)]
    unnamed x70 -> x42, local copies, waits for them, and re-layouts: 10.6 us -> 4.47 us
    select_n x6, other arithmetic: 4.48 us -> 8.03 us  [by(): jnp.where(first, jnp.concatenate([mine, theirs], axis=axis), jnp.concaten...]
    convert_element_type x5 -> x12, other arithmetic: 9.38 us -> 9.47 us  [the longest x4 7 us: local(): payload = terms[k + 1].astype(WIRE)]
  transfers between devices with their start and end apart: 55 -> 55, of which waited for: 17 -> 15; matrix products, arithmetic and copies ran while one was open for 17% -> 17% of each run, Pallas kernels for 13% -> 12%
where the time goes in v8:
time: 353 us; the launch traced here: 351 us
  waiting for transfers between devices  165 us (47%)
  starting transfers between devices  72 us (20%)
  Pallas kernels  46.8 us (13%)
  other arithmetic  36.4 us (10%)
  local copies, waits for them, and re-layouts  28.2 us (8%)
    ppermute x50, waiting for transfers between devices, send(): return lax.ppermute(value, 'col', route)  158 us
    ppermute x50, starting transfers between devices, send(): return lax.ppermute(value, 'col', route)  66.6 us
    pallas_call x4, Pallas kernels, gradient(): pl.pallas_call(functools.partial(gradient_kernel, len(own) // 2), out_sha...  23.5 us
    pallas_call x5, Pallas kernels, forward(): pl.pallas_call(functools.partial(forward_kernel, scale), out_shape=jax.Sh...  23.3 us
    dynamic_slice x9, local copies, waits for them, and re-layouts, columns_of(): return lax.dynamic_slice_in_dim(array, start, width, array.ndim - 1)  16.4 us
    select_n x6, other arithmetic, by(): jnp.where(first, jnp.concatenate([mine, theirs], axis=axis), jnp.concaten...  8.03 us
    ppermute x1, waiting for transfers between devices, local(): lax.ppermute(columns_of(cotangent, (1 - part) * half, half), 'depth', swap)  7.69 us
  transfers between devices with their start and end apart: 55, of which 15 were waited for; matrix products, arithmetic and copies ran while one was open for 17% of the time, Pallas kernels for 12%

profile of v8, /device:TPU:1, one launch (start us, length us, event | category | flops | bytes accessed | tf_op | source)
XLA Modules:
  0.0 350.6 jit_solution(8492377802595522256)
XLA Ops:
  0.6 2.1 collective-permute-start.6
  5.4 2.3 constant_dynamic-slice_fusion.8
  7.7 1.5 collective-permute-start.2
  9.2 2.3 constant_dynamic-slice_fusion.7
  11.5 7.7 %collective-permute-done.13 = bf16[48,3584]{1,0:T(8,128)(2,1)S(1)} collective-permute-done((bf16[48,3584]{1,0:T(8,128)(2,1)S(1)}, bf16[48,3584]{1,0:T(8,128)(2,1)S(1)}, u32[]{:S(2)}, u32[]{:S(2)}) %collective-permute-start.13) | collective-permute-done | bytes 344096 | tf_op jit(solution)/shard_map/ppermute | solution.py:185
  19.9 1.8 fusion.20
  22.9 1.4 maximum_select_fusion
  25.3 1.7 fusion.26
  27.1 1.5 collective-permute-start.7
  28.6 2.1 maximum_select_fusion.3
  30.7 2.1 maximum_select_fusion.2
  32.8 4.0 %collective-permute-start.15 = (bf16[2,96,1792]{2,1,0:T(8,128)(2,1)}, bf16[2,96,1792]{2,1,0:T(8,128)(2,1)}, u32[]{:S(2)}, u32[]{:S(2)}) collective-permute-start(bf16[2,96,1792]{2,1,0:T(8,128)(2,1)} %maximum_select_fusion.2), channel_id=1, source_target_pairs={{0,4},{2,6},{12,8},{14,10},{1,5},{3,7},{13,9},{15,11},{16,20},{18,... | collective-permute-start | bytes 2064392 | tf_op jit(solution)/shard_map/ppermute | solution.py:147
  36.8 4.4 %shard_map.67 = f32[4,2,96,512]{3,2,1,0:T(8,128)S(1)} custom-call(s32[1]{0:T(128)} %bitcast.place_ref, bf16[384,1024]{1,0:T(8,128)(2,1)S(1)} %bitcast.202, bf16[384,1024]{1,0:T(8,128)(2,1)} %bitcast.4.theirs_ref, bf16[1024,7168]{1,0:T(8,128)(2,1)} %gate_ref.9, bf16[1024,7168]{1,0:T(8,128)(2,1)} %up_ref.9, ...), custom_call_target="tpu_custom_call" | custom-call | flops 1610612736 | bytes 7340032 | tf_op jit(solution)/shard_map/pallas_call | solution.py:33
  41.2 1.6 fusion.21
  42.9 1.3 collective-permute-start.4
  44.2 1.3 maximum_select_fusion.1
  46.4 2.3 constant_dynamic-slice_fusion.6
  48.7 2.3 constant_dynamic-slice_fusion.5
  51.9 15.6 %collective-permute-done.4 = f16[4,2,96,512]{3,2,0,1:T(8,128)(2,1)S(1)} collective-permute-done((f16[4,2,96,512]{3,2,0,1:T(8,128)(2,1)S(1)}, f16[4,2,96,512]{3,2,0,1:T(8,128)(2,1)S(1)}, u32[]{:S(2)}, u32[]{:S(2)}) %collective-permute-start.4) | collective-permute-done | bytes 786464 | tf_op jit(solution)/shard_map/ppermute | solution.py:147
  67.6 1.5 pad_maximum_fusion.1
  70.9 3.4 shard_map.69
  75.5 2.3 constant_dynamic-slice_fusion.3
  78.9 5.0 %collective-permute-start.11 = (f16[4,2,96,512]{3,2,1,0:T(8,128)(2,1)}, f16[4,2,96,512]{3,2,1,0:T(8,128)(2,1)}, u32[]{:S(2)}, u32[]{:S(2)}) collective-permute-start(f16[4,2,96,512]{3,2,1,0:T(8,128)(2,1)} %convert_element_type.152), channel_id=1, source_target_pairs={{0,4},{2,6},{12,8},{14,10},{1,5},{3,7},{13,9},{15,11},{16,20},{18,... | collective-permute-start | bytes 2359304 | tf_op jit(solution)/shard_map/ppermute | solution.py:147
  84.8 2.3 copy.52
  90.2 2.3 copy.51
  92.5 1.4 constant_dynamic-slice_fusion.2
  96.7 6.3 %shard_map.68 = f32[4,2,192,512]{3,2,1,0:T(8,128)} custom-call(s32[1]{0:T(128)} %bitcast.place_ref, bf16[768,1024]{1,0:T(8,128)(2,1)S(1)} %bitcast.196, bf16[768,1024]{1,0:T(8,128)(2,1)S(1)} %bitcast.199, bf16[1024,7168]{1,0:T(8,128)(2,1)} %gate_ref.9, bf16[1024,7168]{1,0:T(8,128)(2,1)} %up_ref.9, bf16[1024,512]{1,0:T(8,128)(2,1)} %collective-permute-done.9.gate_far_ref, ...), custom_call_target="tpu_custom_call" | custom-call | flops 3221225472 | bytes 10485760 | tf_op jit(solution)/shard_map/pallas_call | solution.py:33
  103.0 2.3 convert_element_type.151
  110.9 3.0 shard_map.71
  115.0 5.0 %collective-permute-start.12 = (f16[4,2,192,512]{3,2,1,0:T(8,128)(2,1)S(1)}, f16[4,2,192,512]{3,2,1,0:T(8,128)(2,1)S(1)}, u32[]{:S(2)}, u32[]{:S(2)}) collective-permute-start(f16[4,2,192,512]{3,2,1,0:T(8,128)(2,1)S(1)} %convert_element_type.151), channel_id=1, source_target_pairs={{0,4},{2,6},{12,8},{14,10},{1,5},{3,7},{13,9},{15,11},{16,20},{18,... | collective-permute-start | bytes 4718600 | tf_op jit(solution)/shard_map/ppermute | solution.py:147
  121.2 1.3 fusion.16
  123.7 6.2 %shard_map.70 = f32[4,2,192,512]{3,2,1,0:T(8,128)} custom-call(s32[1]{0:T(128)} %bitcast.place_ref, bf16[768,1024]{1,0:T(8,128)(2,1)S(1)} %bitcast.198, bf16[768,1024]{1,0:T(8,128)(2,1)S(1)} %bitcast.201, bf16[1024,7168]{1,0:T(8,128)(2,1)} %gate_ref.9, bf16[1024,7168]{1,0:T(8,128)(2,1)} %up_ref.9, bf16[1024,512]{1,0:T(8,128)(2,1)} %collective-permute-done.19.gate_far_ref, ...), custom_call_target="tpu_custom_call" | custom-call | flops 3221225472 | bytes 10485760 | tf_op jit(solution)/shard_map/pallas_call | solution.py:33
  129.8 2.4 convert_element_type.162
  132.3 1.3 collective-permute-start.29
  133.7 19.8 %collective-permute-done.12 = f16[4,2,192,512]{3,2,1,0:T(8,128)(2,1)S(1)} collective-permute-done((f16[4,2,192,512]{3,2,1,0:T(8,128)(2,1)S(1)}, f16[4,2,192,512]{3,2,1,0:T(8,128)(2,1)S(1)}, u32[]{:S(2)}, u32[]{:S(2)}) %collective-permute-start.12) | collective-permute-done | bytes 1572896 | tf_op jit(solution)/shard_map/ppermute | solution.py:147
  153.5 4.2 %collective-permute-start.21 = (f16[4,2,192,512]{3,2,1,0:T(8,128)(2,1)S(1)}, f16[4,2,192,512]{3,2,1,0:T(8,128)(2,1)S(1)}, u32[]{:S(2)}, u32[]{:S(2)}) collective-permute-start(f16[4,2,192,512]{3,2,1,0:T(8,128)(2,1)S(1)} %convert_element_type.162), channel_id=1, source_target_pairs={{0,4},{2,6},{12,8},{14,10},{1,5},{3,7},{13,9},{15,11},{16,20},{18,... | collective-permute-start | bytes 4718600 | tf_op jit(solution)/shard_map/ppermute | solution.py:147
  158.9 1.3 collective-permute-start.30
  160.2 10.1 %collective-permute-done.30 = bf16[2,2,96,512]{3,2,1,0:T(8,128)(2,1)S(1)} collective-permute-done((bf16[2,2,96,512]{3,2,1,0:T(8,128)(2,1)S(1)}, bf16[2,2,96,512]{3,2,1,0:T(8,128)(2,1)S(1)}, u32[]{:S(2)}, u32[]{:S(2)}) %collective-permute-start.30) | collective-permute-done | bytes 393248 | tf_op jit(solution)/shard_map/ppermute | solution.py:147
  170.3 1.5 collective-permute-start.31
  171.9 2.1 collective-permute-start.33
  174.8 6.2 %collective-permute-done.31 = bf16[2,2,96,512]{3,2,1,0:T(8,128)(2,1)S(1)} collective-permute-done((bf16[2,2,96,512]{3,2,1,0:T(8,128)(2,1)S(1)}, bf16[2,2,96,512]{3,2,1,0:T(8,128)(2,1)S(1)}, u32[]{:S(2)}, u32[]{:S(2)}) %collective-permute-start.31) | collective-permute-done | bytes 393248 | tf_op jit(solution)/shard_map/ppermute | solution.py:147
  181.1 3.0 collective-permute-start.35
  184.1 6.4 %collective-permute-done.21 = f16[4,2,192,512]{3,2,1,0:T(8,128)(2,1)S(1)} collective-permute-done((f16[4,2,192,512]{3,2,1,0:T(8,128)(2,1)S(1)}, f16[4,2,192,512]{3,2,1,0:T(8,128)(2,1)S(1)}, u32[]{:S(2)}, u32[]{:S(2)}) %collective-permute-start.21) | collective-permute-done | bytes 1572896 | tf_op jit(solution)/shard_map/ppermute | solution.py:147
  192.0 1.4 collective-permute-start.32
  193.7 11.8 %collective-permute-done.32 = bf16[2,2,96,512]{3,2,1,0:T(8,128)(2,1)S(1)} collective-permute-done((bf16[2,2,96,512]{3,2,1,0:T(8,128)(2,1)S(1)}, bf16[2,2,96,512]{3,2,1,0:T(8,128)(2,1)S(1)}, u32[]{:S(2)}, u32[]{:S(2)}) %collective-permute-start.32) | collective-permute-done | bytes 393248 | tf_op jit(solution)/shard_map/ppermute | solution.py:147
  205.5 1.3 collective-permute-start.27
  206.9 2.8 collective-permute-start.36
  210.2 1.8 add_multiply_fusion
  213.9 1.3 collective-permute-start.24
  216.5 6.5 %shard_map.72 = (f32[1024,3584]{1,0:T(8,128)}, f32[1024,3584]{1,0:T(8,128)}) custom-call(s32[2]{0:T(128)S(1)} %add_multiply_fusion.3.place_ref, bf16[1024,768]{1,0:T(8,128)(2,1)S(1)} %maximum_bitcast_fusion.features_ref, bf16[2,2,96,512]{3,2,1,0:T(8,128)(2,1)S(1)} %broadcast_select_fusion.9.refs_0_, ...), custom_call_target="tpu_custom_call" | custom-call | flops 3221225472 | bytes 13107200 | tf_op jit(solution)/shard_map/pallas_call | solution.py:94
  223.9 29.2 %collective-permute-done.42 = bf16[2,2,192,512]{3,2,1,0:T(8,128)(2,1)S(1)} collective-permute-done((bf16[2,2,192,512]{3,2,1,0:T(8,128)(2,1)S(1)}, bf16[2,2,192,512]{3,2,1,0:T(8,128)(2,1)S(1)}, u32[]{:S(2)}, u32[]{:S(2)}) %collective-permute-start.42) | collective-permute-done | bytes 786464 | tf_op jit(solution)/shard_map/ppermute | solution.py:147
  256.3 17.0 %collective-permute-done.43 = bf16[2,2,192,512]{3,2,1,0:T(8,128)(2,1)S(1)} collective-permute-done((bf16[2,2,192,512]{3,2,1,0:T(8,128)(2,1)S(1)}, bf16[2,2,192,512]{3,2,1,0:T(8,128)(2,1)S(1)}, u32[]{:S(2)}, u32[]{:S(2)}) %collective-permute-start.43) | collective-permute-done | bytes 786464 | tf_op jit(solution)/shard_map/ppermute | solution.py:147
  273.3 1.7 collective-permute-start.46
  276.5 1.5 collective-permute-start.38
  279.2 6.5 %shard_map.73 = (f32[1024,3584]{1,0:T(8,128)}, f32[1024,3584]{1,0:T(8,128)}) custom-call(s32[2]{0:T(128)S(1)} %add_multiply_fusion.3.place_ref, bf16[1024,768]{1,0:T(8,128)(2,1)S(1)} %maximum_bitcast_fusion.features_ref, bf16[2,2,192,512]{3,2,1,0:T(8,128)(2,1)S(1)} %broadcast_select_fusion.3.refs_0_, ...), custom_call_target="tpu_custom_call", output_to_operand_aliasing={{0}: (6, {}), {1}: (7, {})} | custom-call | flops 3221225472 | bytes 13107200 | tf_op jit(solution)/shard_map/pallas_call | solution.py:94
  285.7 10.5 %collective-permute-done.44 = bf16[2,2,192,512]{3,2,1,0:T(8,128)(2,1)S(1)} collective-permute-done((bf16[2,2,192,512]{3,2,1,0:T(8,128)(2,1)S(1)}, bf16[2,2,192,512]{3,2,1,0:T(8,128)(2,1)S(1)}, u32[]{:S(2)}, u32[]{:S(2)}) %collective-permute-start.44) | collective-permute-done | bytes 786464 | tf_op jit(solution)/shard_map/ppermute | solution.py:147
  299.5 16.5 %collective-permute-done.47 = bf16[2,2,192,512]{3,2,1,0:T(8,128)(2,1)S(1)} collective-permute-done((bf16[2,2,192,512]{3,2,1,0:T(8,128)(2,1)S(1)}, bf16[2,2,192,512]{3,2,1,0:T(8,128)(2,1)S(1)}, u32[]{:S(2)}, u32[]{:S(2)}) %collective-permute-start.47) | collective-permute-done | bytes 786464 | tf_op jit(solution)/shard_map/ppermute | solution.py:147
  316.1 2.2 collective-permute-start.51
  319.2 1.3 collective-permute-start.48
  320.7 6.5 %shard_map.74 = (f32[1024,3584]{1,0:T(8,128)}, f32[1024,3584]{1,0:T(8,128)}) custom-call(s32[2]{0:T(128)S(1)} %add_multiply_fusion.3.place_ref, bf16[1024,768]{1,0:T(8,128)(2,1)S(1)} %maximum_bitcast_fusion.features_ref, bf16[2,2,192,512]{3,2,1,0:T(8,128)(2,1)S(1)} %broadcast_select_fusion.1.refs_0_, ...), custom_call_target="tpu_custom_call", output_to_operand_aliasing={{0}: (6, {}), {1}: (7, {})} | custom-call | flops 3221225472 | bytes 13107200 | tf_op jit(solution)/shard_map/pallas_call | solution.py:94
  327.2 4.6 %collective-permute-done.48 = bf16[2,2,192,256]{3,2,1,0:T(8,128)(2,1)S(1)} collective-permute-done((bf16[2,2,192,256]{3,2,1,0:T(8,128)(2,1)S(1)}, bf16[2,2,192,256]{3,2,1,0:T(8,128)(2,1)S(1)}, u32[]{:S(2)}, u32[]{:S(2)}) %collective-permute-start.48) | collective-permute-done | bytes 393248 | tf_op jit(solution)/shard_map/ppermute | solution.py:147
  334.7 8.8 %collective-permute-done.52 = bf16[2,2,192,256]{3,2,1,0:T(8,128)(2,1)S(1)} collective-permute-done((bf16[2,2,192,256]{3,2,1,0:T(8,128)(2,1)S(1)}, bf16[2,2,192,256]{3,2,1,0:T(8,128)(2,1)S(1)}, u32[]{:S(2)}, u32[]{:S(2)}) %collective-permute-start.52) | collective-permute-done | bytes 393248 | tf_op jit(solution)/shard_map/ppermute | solution.py:147
  343.6 1.8 collective-permute-start.54
  346.7 3.9 %shard_map.75 = (f32[1024,3584]{1,0:T(8,128)}, f32[1024,3584]{1,0:T(8,128)}) custom-call(s32[2]{0:T(128)S(1)} %add_multiply_fusion.3.place_ref, bf16[1024,768]{1,0:T(8,128)(2,1)S(1)} %maximum_bitcast_fusion.features_ref, bf16[2,2,192,256]{3,2,1,0:T(8,128)(2,1)S(1)} %broadcast_select_fusion.5.refs_0_, ...), custom_call_target="tpu_custom_call", output_to_operand_aliasing={{0}: (6, {}), {1}: (7, {})} | custom-call | flops 1610612736 | bytes 7340032 | tf_op jit(solution)/shard_map/pallas_call | solution.py:94
  (188 shorter events, 49.8 us)
Async XLA Ops:
  0.6 43.6 %collective-permute-start.6 = (bf16[384,512]{1,0:T(8,128)(2,1)}, bf16[384,512]{1,0:T(8,128)(2,1)}, u32[]{:S(2)}, u32[]{:S(2)}) collective-permute-start(bf16[384,512]{1,0:T(8,128)(2,1)} %bitcast.231), channel_id=1, source_target_pairs={{0,1},{1,0},{2,3},{3,2},{4,5},{5,4},{6,7},{7,6},{8,9},{9,8},{10,11... | collective-permute-start | bytes 1179656 | tf_op jit(solution)/shard_map/ppermute | solution.py:188
  2.8 20.2 %collective-permute-start = (bf16[384,512]{1,0:T(8,128)(2,1)}, bf16[384,512]{1,0:T(8,128)(2,1)}, u32[]{:S(2)}, u32[]{:S(2)}) collective-permute-start(bf16[384,512]{1,0:T(8,128)(2,1)} %bitcast.232), channel_id=1, source_target_pairs={{0,16},{16,0},{1,17},{17,1},{2,18},{18,2},{3,19},{19,3},{4,20},{20... | collective-permute-start | bytes 1179656 | tf_op jit(solution)/shard_map/ppermute | solution.py:180
  5.1 14.1 %collective-permute-start.13 = (bf16[48,3584]{1,0:T(8,128)(2,1)S(1)}, bf16[48,3584]{1,0:T(8,128)(2,1)S(1)}, u32[]{:S(2)}, u32[]{:S(2)}) collective-permute-start(bf16[48,3584]{1,0:T(8,128)(2,1)S(1)} %get-tuple-element.129), channel_id=1, source_target_pairs={{0,1},{1,0},{2,3},{3,2},{4,5},{5,4},{6,7},{7,6},{8,9},{9,8},{10,11... | collective-permute-start | bytes 1032200 | tf_op jit(solution)/shard_map/ppermute | solution.py:185
  7.7 15.3 %copy-start.19 = (bf16[1,384,512]{2,1,0:T(8,128)(2,1)S(1)}, bf16[1,384,512]{2,1,0:T(8,128)(2,1)}, u32[]{:S(2)}) copy-start(bf16[1,384,512]{2,1,0:T(8,128)(2,1)} %param.4) | copy-start | bytes 1179652
  7.7 29.1 %collective-permute-start.2 = (bf16[1024,512]{1,0:T(8,128)(2,1)}, bf16[1024,512]{1,0:T(8,128)(2,1)S(1)}, u32[]{:S(2)}, u32[]{:S(2)}) collective-permute-start(bf16[1024,512]{1,0:T(8,128)(2,1)} %constant_dynamic-slice_fusion.8), channel_id=1, source_target_pairs={{0,2},{2,0},{4,6},{6,4},{8,10},{10,8},{12,14},{14,12},{1,3},{3,1},... | collective-permute-start | bytes 3145736 | tf_op jit(solution)/shard_map/ppermute | solution.py:147
  11.4 25.4 %collective-permute-start.3 = (bf16[1024,512]{1,0:T(8,128)(2,1)}, bf16[1024,512]{1,0:T(8,128)(2,1)S(1)}, u32[]{:S(2)}, u32[]{:S(2)}) collective-permute-start(bf16[1024,512]{1,0:T(8,128)(2,1)} %constant_dynamic-slice_fusion.7), channel_id=1, source_target_pairs={{0,2},{2,0},{4,6},{6,4},{8,10},{10,8},{12,14},{14,12},{1,3},{3,1},... | collective-permute-start | bytes 3145736 | tf_op jit(solution)/shard_map/ppermute | solution.py:147
  21.7 5.3 %collective-permute-start.14 = (bf16[2,48,1792]{2,1,0:T(8,128)(2,1)}, bf16[2,48,1792]{2,1,0:T(8,128)(2,1)}, u32[]{:S(2)}, u32[]{:S(2)}) collective-permute-start(bf16[2,48,1792]{2,1,0:T(8,128)(2,1)} %get-tuple-element.128), channel_id=1, source_target_pairs={{0,2},{2,0},{4,6},{6,4},{8,10},{10,8},{12,14},{14,12},{1,3},{3,1},... | collective-permute-start | bytes 1032200 | tf_op jit(solution)/shard_map/ppermute | solution.py:147
  24.5 12.3 %copy-start.4 = (bf16[4,96,1024]{2,1,0:T(8,128)(2,1)}, bf16[4,96,1024]{2,1,0:T(8,128)(2,1)S(1)}, u32[]{:S(2)}) copy-start(bf16[4,96,1024]{2,1,0:T(8,128)(2,1)S(1)} %reverse_select_fusion.1) | copy-start | bytes 2359300
  24.5 8.2 %collective-permute-start.1 = (bf16[4,96,1024]{2,1,0:T(8,128)(2,1)S(1)}, bf16[4,96,1024]{2,1,0:T(8,128)(2,1)}, u32[]{:S(2)}, u32[]{:S(2)}) collective-permute-start(bf16[4,96,1024]{2,1,0:T(8,128)(2,1)S(1)} %reverse_select_fusion.1), channel_id=1, source_target_pairs={{0,2},{2,0},{4,6},{6,4},{8,10},{10,8},{12,14},{14,12},{1,3},{3,1},... | collective-permute-start | bytes 2359304 | tf_op jit(solution)/shard_map/ppermute | solution.py:147
  27.1 17.2 %collective-permute-start.7 = (bf16[384,512]{1,0:T(8,128)(2,1)}, bf16[384,512]{1,0:T(8,128)(2,1)S(1)}, u32[]{:S(2)}, u32[]{:S(2)}) collective-permute-start(bf16[384,512]{1,0:T(8,128)(2,1)} %collective-permute-done), channel_id=1, source_target_pairs={{0,1},{1,0},{2,3},{3,2},{4,5},{5,4},{6,7},{7,6},{8,9},{9,8},{10,11... | collective-permute-start | bytes 1179656 | tf_op jit(solution)/shard_map/ppermute | solution.py:189
  32.8 88.4 %collective-permute-start.15 = (bf16[2,96,1792]{2,1,0:T(8,128)(2,1)}, bf16[2,96,1792]{2,1,0:T(8,128)(2,1)}, u32[]{:S(2)}, u32[]{:S(2)}) collective-permute-start(bf16[2,96,1792]{2,1,0:T(8,128)(2,1)} %maximum_select_fusion.2), channel_id=1, source_target_pairs={{0,4},{2,6},{12,8},{14,10},{1,5},{3,7},{13,9},{15,11},{16,20},{18,... | collective-permute-start | bytes 2064392 | tf_op jit(solution)/shard_map/ppermute | solution.py:147
  36.8 4.4 %copy-start.5 = (bf16[1024,512]{1,0:T(8,128)(2,1)}, bf16[1024,512]{1,0:T(8,128)(2,1)S(1)}, u32[]{:S(2)}) copy-start(bf16[1024,512]{1,0:T(8,128)(2,1)S(1)} %collective-permute-done.2.gate_far_ref) | copy-start | bytes 3145732
  36.8 4.4 %copy-start.7 = (bf16[1024,512]{1,0:T(8,128)(2,1)}, bf16[1024,512]{1,0:T(8,128)(2,1)S(1)}, u32[]{:S(2)}) copy-start(bf16[1024,512]{1,0:T(8,128)(2,1)S(1)} %collective-permute-done.3.up_far_ref) | copy-start | bytes 3145732
  42.9 24.7 %collective-permute-start.4 = (f16[4,2,96,512]{3,2,0,1:T(8,128)(2,1)S(1)}, f16[4,2,96,512]{3,2,0,1:T(8,128)(2,1)S(1)}, u32[]{:S(2)}, u32[]{:S(2)}) collective-permute-start(f16[4,2,96,512]{3,2,0,1:T(8,128)(2,1)S(1)} %get-tuple-element.114), channel_id=1, source_target_pairs={{0,4},{2,6},{12,8},{14,10},{1,5},{3,7},{13,9},{15,11},{16,20},{18,... | collective-permute-start | bytes 2359304 | tf_op jit(solution)/shard_map/ppermute | solution.py:147
  45.8 21.9 %collective-permute-start.8 = (bf16[4,96,1024]{2,1,0:T(8,128)(2,1)S(1)}, bf16[4,96,1024]{2,1,0:T(8,128)(2,1)S(1)}, u32[]{:S(2)}, u32[]{:S(2)}) collective-permute-start(bf16[4,96,1024]{2,1,0:T(8,128)(2,1)S(1)} %reverse_select_fusion), channel_id=1, source_target_pairs={{0,2},{2,0},{4,6},{6,4},{8,10},{10,8},{12,14},{14,12},{1,3},{3,1},... | collective-permute-start | bytes 2359304 | tf_op jit(solution)/shard_map/ppermute | solution.py:147
  48.7 47.3 %collective-permute-start.9 = (bf16[1024,512]{1,0:T(8,128)(2,1)}, bf16[1024,512]{1,0:T(8,128)(2,1)}, u32[]{:S(2)}, u32[]{:S(2)}) collective-permute-start(bf16[1024,512]{1,0:T(8,128)(2,1)} %constant_dynamic-slice_fusion.6), channel_id=1, source_target_pairs={{0,2},{2,0},{4,6},{6,4},{8,10},{10,8},{12,14},{14,12},{1,3},{3,1},... | collective-permute-start | bytes 3145736 | tf_op jit(solution)/shard_map/ppermute | solution.py:147
  51.0 45.6 %collective-permute-start.10 = (bf16[1024,512]{1,0:T(8,128)(2,1)}, bf16[1024,512]{1,0:T(8,128)(2,1)}, u32[]{:S(2)}, u32[]{:S(2)}) collective-permute-start(bf16[1024,512]{1,0:T(8,128)(2,1)} %constant_dynamic-slice_fusion.5), channel_id=1, source_target_pairs={{0,2},{2,0},{4,6},{6,4},{8,10},{10,8},{12,14},{14,12},{1,3},{3,1},... | collective-permute-start | bytes 3145736 | tf_op jit(solution)/shard_map/ppermute | solution.py:147
  74.2 3.5 %copy-start = (f32[4,2,96,512]{3,2,1,0:T(8,128)}, f32[4,2,96,512]{3,2,1,0:T(8,128)S(1)}, u32[]{:S(2)}) copy-start(f32[4,2,96,512]{3,2,1,0:T(8,128)S(1)} %shard_map.69) | copy-start | bytes 4718596
  77.8 45.9 %collective-permute-start.19 = (bf16[1024,512]{1,0:T(8,128)(2,1)}, bf16[1024,512]{1,0:T(8,128)(2,1)}, u32[]{:S(2)}, u32[]{:S(2)}) collective-permute-start(bf16[1024,512]{1,0:T(8,128)(2,1)} %constant_dynamic-slice_fusion.3), channel_id=1, source_target_pairs={{0,2},{2,0},{4,6},{6,4},{8,10},{10,8},{12,14},{14,12},{1,3},{3,1},... | collective-permute-start | bytes 3145736 | tf_op jit(solution)/shard_map/ppermute | solution.py:147
  78.9 29.7 %collective-permute-start.11 = (f16[4,2,96,512]{3,2,1,0:T(8,128)(2,1)}, f16[4,2,96,512]{3,2,1,0:T(8,128)(2,1)}, u32[]{:S(2)}, u32[]{:S(2)}) collective-permute-start(f16[4,2,96,512]{3,2,1,0:T(8,128)(2,1)} %convert_element_type.152), channel_id=1, source_target_pairs={{0,4},{2,6},{12,8},{14,10},{1,5},{3,7},{13,9},{15,11},{16,20},{18,... | collective-permute-start | bytes 2359304 | tf_op jit(solution)/shard_map/ppermute | solution.py:147
  96.0 12.1 %collective-permute-start.5 = (f16[2,2,96,512]{3,2,0,1:T(8,128)(2,1)S(1)}, f16[2,2,96,512]{3,2,0,1:T(8,128)(2,1)S(1)}, u32[]{:S(2)}, u32[]{:S(2)}) collective-permute-start(f16[2,2,96,512]{3,2,0,1:T(8,128)(2,1)S(1)} %fusion.9), channel_id=1, source_target_pairs={{4,8},{6,10},{8,4},{10,6},{5,9},{7,11},{9,5},{11,7},{20,24},{22,26... | collective-permute-start | bytes 1179656 | tf_op jit(solution)/shard_map/ppermute | solution.py:147
  106.5 4.1 %collective-permute-start.25 = (bf16[1024,256]{1,0:T(8,128)(2,1)S(1)}, bf16[1024,256]{1,0:T(8,128)(2,1)S(1)}, u32[]{:S(2)}, u32[]{:S(2)}) collective-permute-start(bf16[1024,256]{1,0:T(8,128)(2,1)S(1)} %constant_dynamic-slice_fusion.1), channel_id=1, source_target_pairs={{0,2},{2,0},{4,6},{6,4},{8,10},{10,8},{12,14},{14,12},{1,3},{3,1},... | collective-permute-start | bytes 1572872 | tf_op jit(solution)/shard_map/ppermute | solution.py:147
  108.1 2.8 collective-permute-start.26
  109.7 10.3 %collective-permute-start.16 = (f16[2,2,96,512]{3,2,1,0:T(8,128)(2,1)S(1)}, f16[2,2,96,512]{3,2,1,0:T(8,128)(2,1)S(1)}, u32[]{:S(2)}, u32[]{:S(2)}) collective-permute-start(f16[2,2,96,512]{3,2,1,0:T(8,128)(2,1)S(1)} %add_convert_fusion.3), channel_id=1, source_target_pairs={{4,8},{6,10},{8,4},{10,6},{5,9},{7,11},{9,5},{11,7},{20,24},{22,26... | collective-permute-start | bytes 1179656 | tf_op jit(solution)/shard_map/ppermute | solution.py:147
  110.6 13.0 %collective-permute-start.20 = (bf16[1024,512]{1,0:T(8,128)(2,1)S(1)}, bf16[1024,512]{1,0:T(8,128)(2,1)S(1)}, u32[]{:S(2)}, u32[]{:S(2)}) collective-permute-start(bf16[1024,512]{1,0:T(8,128)(2,1)S(1)} %constant_dynamic-slice_fusion.2), channel_id=1, source_target_pairs={{0,2},{2,0},{4,6},{6,4},{8,10},{10,8},{12,14},{14,12},{1,3},{3,1},... | collective-permute-start | bytes 3145736 | tf_op jit(solution)/shard_map/ppermute | solution.py:147
  115.0 6.2 %copy-start.11 = (bf16[1,2,96,1792]{3,2,1,0:T(8,128)(2,1)S(1)}, bf16[1,2,96,1792]{3,2,1,0:T(8,128)(2,1)}, u32[]{:S(2)}) copy-start(bf16[1,2,96,1792]{3,2,1,0:T(8,128)(2,1)} %maximum_select_fusion.3) | copy-start | bytes 2064388
  115.0 38.5 %collective-permute-start.12 = (f16[4,2,192,512]{3,2,1,0:T(8,128)(2,1)S(1)}, f16[4,2,192,512]{3,2,1,0:T(8,128)(2,1)S(1)}, u32[]{:S(2)}, u32[]{:S(2)}) collective-permute-start(f16[4,2,192,512]{3,2,1,0:T(8,128)(2,1)S(1)} %convert_element_type.151), channel_id=1, source_target_pairs={{0,4},{2,6},{12,8},{14,10},{1,5},{3,7},{13,9},{15,11},{16,20},{18,... | collective-permute-start | bytes 4718600 | tf_op jit(solution)/shard_map/ppermute | solution.py:147
  122.9 10.8 %collective-permute-start.17 = (bf16[2,2,96,512]{3,2,1,0:T(8,128)(2,1)S(1)}, bf16[2,2,96,512]{3,2,1,0:T(8,128)(2,1)S(1)}, u32[]{:S(2)}, u32[]{:S(2)}) collective-permute-start(bf16[2,2,96,512]{3,2,1,0:T(8,128)(2,1)S(1)} %get-tuple-element.82), channel_id=1, source_target_pairs={{4,8},{6,10},{8,4},{10,6},{5,9},{7,11},{9,5},{11,7},{20,24},{22,26... | collective-permute-start | bytes 1179656 | tf_op jit(solution)/shard_map/ppermute | solution.py:147
  129.8 27.9 %copy-start.9 = (f32[4,2,192,512]{3,2,1,0:T(8,128)S(1)}, f32[4,2,192,512]{3,2,1,0:T(8,128)}, u32[]{:S(2)}) copy-start(f32[4,2,192,512]{3,2,1,0:T(8,128)} %shard_map.68) | copy-start | bytes 9437188
  132.3 26.6 %collective-permute-start.29 = (bf16[2,2,96,512]{3,2,1,0:T(8,128)(2,1)S(1)}, bf16[2,2,96,512]{3,2,1,0:T(8,128)(2,1)S(1)}, u32[]{:S(2)}, u32[]{:S(2)}) collective-permute-start(bf16[2,2,96,512]{3,2,1,0:T(8,128)(2,1)S(1)} %get-tuple-element.82), channel_id=1, source_target_pairs={{4,0},{6,2},{8,12},{10,14},{5,1},{7,3},{9,13},{11,15},{20,16},{22,... | collective-permute-start | bytes 1179656 | tf_op jit(solution)/shard_map/ppermute | solution.py:147
  153.5 37.0 %collective-permute-start.21 = (f16[4,2,192,512]{3,2,1,0:T(8,128)(2,1)S(1)}, f16[4,2,192,512]{3,2,1,0:T(8,128)(2,1)S(1)}, u32[]{:S(2)}, u32[]{:S(2)}) collective-permute-start(f16[4,2,192,512]{3,2,1,0:T(8,128)(2,1)S(1)} %convert_element_type.162), channel_id=1, source_target_pairs={{0,4},{2,6},{12,8},{14,10},{1,5},{3,7},{13,9},{15,11},{16,20},{18,... | collective-permute-start | bytes 4718600 | tf_op jit(solution)/shard_map/ppermute | solution.py:147
  158.0 16.0 %collective-permute-start.18 = (f16[2,2,192,512]{3,2,1,0:T(8,128)(2,1)S(1)}, f16[2,2,192,512]{3,2,1,0:T(8,128)(2,1)S(1)}, u32[]{:S(2)}, u32[]{:S(2)}) collective-permute-start(f16[2,2,192,512]{3,2,1,0:T(8,128)(2,1)S(1)} %add_convert_fusion.1), channel_id=1, source_target_pairs={{4,8},{6,10},{8,4},{10,6},{5,9},{7,11},{9,5},{11,7},{20,24},{22,26... | collective-permute-start | bytes 2359304 | tf_op jit(solution)/shard_map/ppermute | solution.py:147
  158.9 11.4 %collective-permute-start.30 = (bf16[2,2,96,512]{3,2,1,0:T(8,128)(2,1)S(1)}, bf16[2,2,96,512]{3,2,1,0:T(8,128)(2,1)S(1)}, u32[]{:S(2)}, u32[]{:S(2)}) collective-permute-start(bf16[2,2,96,512]{3,2,1,0:T(8,128)(2,1)S(1)} %collective-permute-done.17), channel_id=1, source_target_pairs={{4,0},{6,2},{8,12},{10,14},{5,1},{7,3},{9,13},{11,15},{20,16},{22,... | collective-permute-start | bytes 1179656 | tf_op jit(solution)/shard_map/ppermute | solution.py:147
  170.3 20.2 %copy-start.10 = (f32[4,2,192,512]{3,2,1,0:T(8,128)S(1)}, f32[4,2,192,512]{3,2,1,0:T(8,128)}, u32[]{:S(2)}) copy-start(f32[4,2,192,512]{3,2,1,0:T(8,128)} %shard_map.70) | copy-start | bytes 9437188
  170.3 10.7 %collective-permute-start.31 = (bf16[2,2,96,512]{3,2,1,0:T(8,128)(2,1)S(1)}, bf16[2,2,96,512]{3,2,1,0:T(8,128)(2,1)S(1)}, u32[]{:S(2)}, u32[]{:S(2)}) collective-permute-start(bf16[2,2,96,512]{3,2,1,0:T(8,128)(2,1)S(1)} %get-tuple-element.84), channel_id=1, source_target_pairs={{4,0},{6,2},{8,12},{10,14},{5,1},{7,3},{9,13},{11,15},{20,16},{22,... | collective-permute-start | bytes 1179656 | tf_op jit(solution)/shard_map/ppermute | solution.py:147
  171.9 41.2 %collective-permute-start.33 = (bf16[2,2,96,512]{3,2,1,0:T(8,128)(2,1)S(1)}, bf16[2,2,96,512]{3,2,1,0:T(8,128)(2,1)S(1)}, u32[]{:S(2)}, u32[]{:S(2)}) collective-permute-start(bf16[2,2,96,512]{3,2,1,0:T(8,128)(2,1)S(1)} %broadcast_select_fusion.9.refs_0_), channel_id=1, source_target_pairs={{0,2},{2,0},{4,6},{6,4},{8,10},{10,8},{12,14},{14,12},{1,3},{3,1},... | collective-permute-start | bytes 1179656 | tf_op jit(solution)/shard_map/ppermute | solution.py:147
  174.0 10.1 %collective-permute-start.22 = (bf16[2,2,96,512]{3,2,1,0:T(8,128)(2,1)S(1)}, bf16[2,2,96,512]{3,2,1,0:T(8,128)(2,1)S(1)}, u32[]{:S(2)}, u32[]{:S(2)}) collective-permute-start(bf16[2,2,96,512]{3,2,1,0:T(8,128)(2,1)S(1)} %get-tuple-element.84), channel_id=1, source_target_pairs={{4,8},{6,10},{8,4},{10,6},{5,9},{7,11},{9,5},{11,7},{20,24},{22,26... | collective-permute-start | bytes 1179656 | tf_op jit(solution)/shard_map/ppermute | solution.py:147
  174.7 39.1 %collective-permute-start.34 = (bf16[2,2,96,512]{3,2,1,0:T(8,128)(2,1)S(1)}, bf16[2,2,96,512]{3,2,1,0:T(8,128)(2,1)S(1)}, u32[]{:S(2)}, u32[]{:S(2)}) collective-permute-start(bf16[2,2,96,512]{3,2,1,0:T(8,128)(2,1)S(1)} %broadcast_select_fusion.8.refs_1_), channel_id=1, source_target_pairs={{0,2},{2,0},{4,6},{6,4},{8,10},{10,8},{12,14},{14,12},{1,3},{3,1},... | collective-permute-start | bytes 1179656 | tf_op jit(solution)/shard_map/ppermute | solution.py:147
  181.1 34.1 %collective-permute-start.35 = (bf16[2,2,96,512]{3,2,1,0:T(8,128)(2,1)S(1)}, bf16[2,2,96,512]{3,2,1,0:T(8,128)(2,1)S(1)}, u32[]{:S(2)}, u32[]{:S(2)}) collective-permute-start(bf16[2,2,96,512]{3,2,1,0:T(8,128)(2,1)S(1)} %broadcast_select_fusion.7.refs_2_), channel_id=1, source_target_pairs={{0,2},{2,0},{4,6},{6,4},{8,10},{10,8},{12,14},{14,12},{1,3},{3,1},... | collective-permute-start | bytes 1179656 | tf_op jit(solution)/shard_map/ppermute | solution.py:147
  190.8 16.1 %collective-permute-start.23 = (f16[2,2,192,512]{3,2,1,0:T(8,128)(2,1)S(1)}, f16[2,2,192,512]{3,2,1,0:T(8,128)(2,1)S(1)}, u32[]{:S(2)}, u32[]{:S(2)}) collective-permute-start(f16[2,2,192,512]{3,2,1,0:T(8,128)(2,1)S(1)} %add_convert_fusion), channel_id=1, source_target_pairs={{4,8},{6,10},{8,4},{10,6},{5,9},{7,11},{9,5},{11,7},{20,24},{22,26... | collective-permute-start | bytes 2359304 | tf_op jit(solution)/shard_map/ppermute | solution.py:147
  192.0 13.6 %copy-start.18 = (f16[4,2,192,256]{3,2,1,0:T(8,128)(2,1)S(1)}, f16[4,2,192,256]{3,2,1,0:T(8,128)(2,1)}, u32[]{:S(2)}) copy-start(f16[4,2,192,256]{3,2,1,0:T(8,128)(2,1)} %convert_element_type.173) | copy-start | bytes 2359300
  192.0 13.6 %collective-permute-start.32 = (bf16[2,2,96,512]{3,2,1,0:T(8,128)(2,1)S(1)}, bf16[2,2,96,512]{3,2,1,0:T(8,128)(2,1)S(1)}, u32[]{:S(2)}, u32[]{:S(2)}) collective-permute-start(bf16[2,2,96,512]{3,2,1,0:T(8,128)(2,1)S(1)} %collective-permute-done.22), channel_id=1, source_target_pairs={{4,0},{6,2},{8,12},{10,14},{5,1},{7,3},{9,13},{11,15},{20,16},{22,... | collective-permute-start | bytes 1179656 | tf_op jit(solution)/shard_map/ppermute | solution.py:147
  205.5 17.6 %collective-permute-start.27 = (f16[4,2,192,256]{3,2,1,0:T(8,128)(2,1)S(1)}, f16[4,2,192,256]{3,2,1,0:T(8,128)(2,1)S(1)}, u32[]{:S(2)}, u32[]{:S(2)}) collective-permute-start(f16[4,2,192,256]{3,2,1,0:T(8,128)(2,1)S(1)} %copy-done.18), channel_id=1, source_target_pairs={{0,4},{2,6},{12,8},{14,10},{1,5},{3,7},{13,9},{15,11},{16,20},{18,... | collective-permute-start | bytes 2359304 | tf_op jit(solution)/shard_map/ppermute | solution.py:147
  206.9 9.6 %collective-permute-start.36 = (bf16[2,2,96,512]{3,2,1,0:T(8,128)(2,1)S(1)}, bf16[2,2,96,512]{3,2,1,0:T(8,128)(2,1)S(1)}, u32[]{:S(2)}, u32[]{:S(2)}) collective-permute-start(bf16[2,2,96,512]{3,2,1,0:T(8,128)(2,1)S(1)} %broadcast_select_fusion.6.refs_3_), channel_id=1, source_target_pairs={{0,2},{2,0},{4,6},{6,4},{8,10},{10,8},{12,14},{14,12},{1,3},{3,1},... | collective-permute-start | bytes 1179656 | tf_op jit(solution)/shard_map/ppermute | solution.py:147
  213.1 10.0 %collective-permute-start.28 = (bf16[2,2,192,512]{3,2,1,0:T(8,128)(2,1)S(1)}, bf16[2,2,192,512]{3,2,1,0:T(8,128)(2,1)S(1)}, u32[]{:S(2)}, u32[]{:S(2)}) collective-permute-start(bf16[2,2,192,512]{3,2,1,0:T(8,128)(2,1)S(1)} %get-tuple-element.90), channel_id=1, source_target_pairs={{4,8},{6,10},{8,4},{10,6},{5,9},{7,11},{9,5},{11,7},{20,24},{22,26... | collective-permute-start | bytes 2359304 | tf_op jit(solution)/shard_map/ppermute | solution.py:147
  213.9 40.5 %collective-permute-start.24 = (bf16[2,96,1536]{2,1,0:T(8,128)(2,1)S(1)}, bf16[2,96,1536]{2,1,0:T(8,128)(2,1)S(1)}, u32[]{:S(2)}, u32[]{:S(2)}) collective-permute-start(bf16[2,96,1536]{2,1,0:T(8,128)(2,1)S(1)} %pad_maximum_fusion.5), channel_id=1, source_target_pairs={{4,0},{6,2},{8,12},{10,14},{5,1},{7,3},{9,13},{11,15},{20,16},{22,... | collective-permute-start | bytes 1769480 | tf_op jit(solution)/shard_map/ppermute | solution.py:147
  215.2 37.9 %collective-permute-start.42 = (bf16[2,2,192,512]{3,2,1,0:T(8,128)(2,1)S(1)}, bf16[2,2,192,512]{3,2,1,0:T(8,128)(2,1)S(1)}, u32[]{:S(2)}, u32[]{:S(2)}) collective-permute-start(bf16[2,2,192,512]{3,2,1,0:T(8,128)(2,1)S(1)} %get-tuple-element.90), channel_id=1, source_target_pairs={{4,0},{6,2},{8,12},{10,14},{5,1},{7,3},{9,13},{11,15},{20,16},{22,... | collective-permute-start | bytes 2359304 | tf_op jit(solution)/shard_map/ppermute | solution.py:147
  223.2 32.2 %collective-permute-start.37 = (f16[2,2,192,256]{3,2,1,0:T(8,128)(2,1)S(1)}, f16[2,2,192,256]{3,2,1,0:T(8,128)(2,1)S(1)}, u32[]{:S(2)}, u32[]{:S(2)}) collective-permute-start(f16[2,2,192,256]{3,2,1,0:T(8,128)(2,1)S(1)} %add_convert_fusion.2), channel_id=1, source_target_pairs={{4,8},{6,10},{8,4},{10,6},{5,9},{7,11},{9,5},{11,7},{20,24},{22,26... | collective-permute-start | bytes 1179656 | tf_op jit(solution)/shard_map/ppermute | solution.py:147
  253.1 20.2 %collective-permute-start.43 = (bf16[2,2,192,512]{3,2,1,0:T(8,128)(2,1)S(1)}, bf16[2,2,192,512]{3,2,1,0:T(8,128)(2,1)S(1)}, u32[]{:S(2)}, u32[]{:S(2)}) collective-permute-start(bf16[2,2,192,512]{3,2,1,0:T(8,128)(2,1)S(1)} %collective-permute-done.28), channel_id=1, source_target_pairs={{4,0},{6,2},{8,12},{10,14},{5,1},{7,3},{9,13},{11,15},{20,16},{22,... | collective-permute-start | bytes 2359304 | tf_op jit(solution)/shard_map/ppermute | solution.py:147
  254.6 24.6 %collective-permute-start.45 = (bf16[2,2,192,512]{3,2,1,0:T(8,128)(2,1)S(1)}, bf16[2,2,192,512]{3,2,1,0:T(8,128)(2,1)S(1)}, u32[]{:S(2)}, u32[]{:S(2)}) collective-permute-start(bf16[2,2,192,512]{3,2,1,0:T(8,128)(2,1)S(1)} %broadcast_select_fusion.3.refs_0_), channel_id=1, source_target_pairs={{0,2},{2,0},{4,6},{6,4},{8,10},{10,8},{12,14},{14,12},{1,3},{3,1},... | collective-permute-start | bytes 2359304 | tf_op jit(solution)/shard_map/ppermute | solution.py:147
  255.4 30.3 %collective-permute-start.41 = (bf16[2,2,192,512]{3,2,1,0:T(8,128)(2,1)S(1)}, bf16[2,2,192,512]{3,2,1,0:T(8,128)(2,1)S(1)}, u32[]{:S(2)}, u32[]{:S(2)}) collective-permute-start(bf16[2,2,192,512]{3,2,1,0:T(8,128)(2,1)S(1)} %get-tuple-element.92), channel_id=1, source_target_pairs={{4,8},{6,10},{8,4},{10,6},{5,9},{7,11},{9,5},{11,7},{20,24},{22,26... | collective-permute-start | bytes 2359304 | tf_op jit(solution)/shard_map/ppermute | solution.py:147
  273.3 5.8 %collective-permute-start.46 = (bf16[2,2,192,512]{3,2,1,0:T(8,128)(2,1)S(1)}, bf16[2,2,192,512]{3,2,1,0:T(8,128)(2,1)S(1)}, u32[]{:S(2)}, u32[]{:S(2)}) collective-permute-start(bf16[2,2,192,512]{3,2,1,0:T(8,128)(2,1)S(1)} %broadcast_select_fusion.2.refs_1_), channel_id=1, source_target_pairs={{0,2},{2,0},{4,6},{6,4},{8,10},{10,8},{12,14},{14,12},{1,3},{3,1},... | collective-permute-start | bytes 2359304 | tf_op jit(solution)/shard_map/ppermute | solution.py:147
  275.2 21.1 %collective-permute-start.44 = (bf16[2,2,192,512]{3,2,1,0:T(8,128)(2,1)S(1)}, bf16[2,2,192,512]{3,2,1,0:T(8,128)(2,1)S(1)}, u32[]{:S(2)}, u32[]{:S(2)}) collective-permute-start(bf16[2,2,192,512]{3,2,1,0:T(8,128)(2,1)S(1)} %get-tuple-element.92), channel_id=1, source_target_pairs={{4,0},{6,2},{8,12},{10,14},{5,1},{7,3},{9,13},{11,15},{20,16},{22,... | collective-permute-start | bytes 2359304 | tf_op jit(solution)/shard_map/ppermute | solution.py:147
  276.5 21.8 %collective-permute-start.38 = (bf16[2,96,256]{2,1,0:T(8,128)(2,1)S(1)}, bf16[2,96,256]{2,1,0:T(8,128)(2,1)S(1)}, u32[]{:S(2)}, u32[]{:S(2)}) collective-permute-start(bf16[2,96,256]{2,1,0:T(8,128)(2,1)S(1)} %pad_maximum_fusion.11), channel_id=1, source_target_pairs={{4,0},{6,2},{8,12},{10,14},{5,1},{7,3},{9,13},{11,15},{20,16},{22,... | collective-permute-start | bytes 294920 | tf_op jit(solution)/shard_map/ppermute | solution.py:147
  296.3 19.7 %collective-permute-start.47 = (bf16[2,2,192,512]{3,2,1,0:T(8,128)(2,1)S(1)}, bf16[2,2,192,512]{3,2,1,0:T(8,128)(2,1)S(1)}, u32[]{:S(2)}, u32[]{:S(2)}) collective-permute-start(bf16[2,2,192,512]{3,2,1,0:T(8,128)(2,1)S(1)} %collective-permute-done.41), channel_id=1, source_target_pairs={{4,0},{6,2},{8,12},{10,14},{5,1},{7,3},{9,13},{11,15},{20,16},{22,... | collective-permute-start | bytes 2359304 | tf_op jit(solution)/shard_map/ppermute | solution.py:147
  298.5 22.0 %collective-permute-start.39 = (bf16[2,48,1792]{2,1,0:T(8,128)(2,1)S(1)}, bf16[2,48,1792]{2,1,0:T(8,128)(2,1)S(1)}, u32[]{:S(2)}, u32[]{:S(2)}) collective-permute-start(bf16[2,48,1792]{2,1,0:T(8,128)(2,1)S(1)} %get-tuple-element.126), channel_id=1, source_target_pairs={{0,2},{2,0},{4,6},{6,4},{8,10},{10,8},{12,14},{14,12},{1,3},{3,1},... | collective-permute-start | bytes 1032200 | tf_op jit(solution)/shard_map/ppermute | solution.py:147
  299.4 21.2 %collective-permute-start.50 = (bf16[2,2,192,512]{3,2,1,0:T(8,128)(2,1)S(1)}, bf16[2,2,192,512]{3,2,1,0:T(8,128)(2,1)S(1)}, u32[]{:S(2)}, u32[]{:S(2)}) collective-permute-start(bf16[2,2,192,512]{3,2,1,0:T(8,128)(2,1)S(1)} %broadcast_select_fusion.1.refs_0_), channel_id=1, source_target_pairs={{0,2},{2,0},{4,6},{6,4},{8,10},{10,8},{12,14},{14,12},{1,3},{3,1},... | collective-permute-start | bytes 2359304 | tf_op jit(solution)/shard_map/ppermute | solution.py:147
  316.1 4.6 %collective-permute-start.51 = (bf16[2,2,192,512]{3,2,1,0:T(8,128)(2,1)S(1)}, bf16[2,2,192,512]{3,2,1,0:T(8,128)(2,1)S(1)}, u32[]{:S(2)}, u32[]{:S(2)}) collective-permute-start(bf16[2,2,192,512]{3,2,1,0:T(8,128)(2,1)S(1)} %broadcast_select_fusion.refs_1_), channel_id=1, source_target_pairs={{0,2},{2,0},{4,6},{6,4},{8,10},{10,8},{12,14},{14,12},{1,3},{3,1},... | collective-permute-start | bytes 2359304 | tf_op jit(solution)/shard_map/ppermute | solution.py:147
  318.5 8.8 %collective-permute-start.49 = (bf16[2,2,192,256]{3,2,1,0:T(8,128)(2,1)S(1)}, bf16[2,2,192,256]{3,2,1,0:T(8,128)(2,1)S(1)}, u32[]{:S(2)}, u32[]{:S(2)}) collective-permute-start(bf16[2,2,192,256]{3,2,1,0:T(8,128)(2,1)S(1)} %select_convert_fusion.2), channel_id=1, source_target_pairs={{4,8},{6,10},{8,4},{10,6},{5,9},{7,11},{9,5},{11,7},{20,24},{22,26... | collective-permute-start | bytes 1179656 | tf_op jit(solution)/shard_map/ppermute | solution.py:147
  319.2 12.6 %collective-permute-start.48 = (bf16[2,2,192,256]{3,2,1,0:T(8,128)(2,1)S(1)}, bf16[2,2,192,256]{3,2,1,0:T(8,128)(2,1)S(1)}, u32[]{:S(2)}, u32[]{:S(2)}) collective-permute-start(bf16[2,2,192,256]{3,2,1,0:T(8,128)(2,1)S(1)} %select_convert_fusion.2), channel_id=1, source_target_pairs={{4,0},{6,2},{8,12},{10,14},{5,1},{7,3},{9,13},{11,15},{20,16},{22,... | collective-permute-start | bytes 1179656 | tf_op jit(solution)/shard_map/ppermute | solution.py:147
  331.8 11.7 %collective-permute-start.52 = (bf16[2,2,192,256]{3,2,1,0:T(8,128)(2,1)S(1)}, bf16[2,2,192,256]{3,2,1,0:T(8,128)(2,1)S(1)}, u32[]{:S(2)}, u32[]{:S(2)}) collective-permute-start(bf16[2,2,192,256]{3,2,1,0:T(8,128)(2,1)S(1)} %collective-permute-done.49), channel_id=1, source_target_pairs={{4,0},{6,2},{8,12},{10,14},{5,1},{7,3},{9,13},{11,15},{20,16},{22,... | collective-permute-start | bytes 1179656 | tf_op jit(solution)/shard_map/ppermute | solution.py:147
  333.1 12.2 %collective-permute-start.40 = (bf16[48,3584]{1,0:T(8,128)(2,1)S(1)}, bf16[48,3584]{1,0:T(8,128)(2,1)S(1)}, u32[]{:S(2)}, u32[]{:S(2)}) collective-permute-start(bf16[48,3584]{1,0:T(8,128)(2,1)S(1)} %get-tuple-element.124), channel_id=1, source_target_pairs={{0,1},{1,0},{2,3},{3,2},{4,5},{5,4},{6,7},{7,6},{8,9},{9,8},{10,11... | collective-permute-start | bytes 1032200 | tf_op jit(solution)/shard_map/ppermute | solution.py:304
  333.5 12.8 %collective-permute-start.53 = (bf16[2,2,192,256]{3,2,1,0:T(8,128)(2,1)S(1)}, bf16[2,2,192,256]{3,2,1,0:T(8,128)(2,1)S(1)}, u32[]{:S(2)}, u32[]{:S(2)}) collective-permute-start(bf16[2,2,192,256]{3,2,1,0:T(8,128)(2,1)S(1)} %broadcast_select_fusion.5.refs_0_), channel_id=1, source_target_pairs={{0,2},{2,0},{4,6},{6,4},{8,10},{10,8},{12,14},{14,12},{1,3},{3,1},... | collective-permute-start | bytes 1179656 | tf_op jit(solution)/shard_map/ppermute | solution.py:147
  343.6 3.1 collective-permute-start.54
  (12 other events, 19.0 us)

commit v9 on v5

--- a/solution.py
+++ b/solution.py
@@ -11,45 +11,46 @@
 WIRE = jnp.float16
 LARGEST_TOKEN, LARGEST_WEIGHT = 6.0, 0.0625
 VMEM_LIMIT = 48 * 2**20
-NO_COST = pl.CostEstimate(flops=0, bytes_accessed=0, transcendentals=0)
+LAST_SHARES = (2, 1)
 SHARES = (4, 3)
 
 
-def forward_kernel(
-    scale, place_ref, mine_ref, theirs_ref, gate_ref, up_ref, gate_far_ref, up_far_ref, out_ref
-):
+def forward_kernel(scale, place_ref, *refs):
+    tokens, weights, out_ref = refs[: len(refs) // 3], refs[len(refs) // 3 : -1], refs[-1]
     blocks, _, rows, width = out_ref.shape
-    for which, (near, far) in enumerate(((gate_ref, gate_far_ref), (up_ref, up_far_ref))):
-        product = jnp.dot(mine_ref[...], near[...], preferred_element_type=jnp.float32)
-        product += jnp.dot(theirs_ref[...], far[...], preferred_element_type=jnp.float32)
+    for which in range(2):
+        product = sum(
+            jnp.dot(rows_ref[...], weight_ref[...], preferred_element_type=jnp.float32)
+            for rows_ref, weight_ref in zip(tokens, weights[which::2])
+        )
         out_ref[:, which] = (scale * product).reshape(blocks, rows, width)
 
 
-def forward(place, mine, theirs, gate_weight, up_weight, far, start, tile, blocks, scale):
-    total, depth = mine.shape
-    width = far[0].shape[1]
+def forward(place, tokens, weights, start, width, tile, blocks, scale):
+    total, depth = tokens[0].shape
     rows = total // blocks
-    whole = pl.BlockSpec((total, depth), lambda j, place: (0, 0))
-    weight = pl.BlockSpec((depth, tile), lambda j, place: (0, place[0] + start // tile + j))
+    far = len(tokens) - 1
+    in_specs = [pl.BlockSpec((total, depth), lambda j, place: (0, 0))] * len(tokens)
+    in_specs += [
+        pl.BlockSpec((depth, tile), lambda j, place: (0, place[0] + start // tile + j))
+    ] * 2
+    in_specs += [pl.BlockSpec((depth, tile), lambda j, place: (0, j))] * (2 * far)
     return pl.pallas_call(
         functools.partial(forward_kernel, scale),
         out_shape=jax.ShapeDtypeStruct((blocks, 2, rows, width), jnp.float32),
         grid_spec=pltpu.PrefetchScalarGridSpec(
             num_scalar_prefetch=1,
             grid=(width // tile,),
-            in_specs=[
-                whole,
-                whole,
-                weight,
-                weight,
-                pl.BlockSpec((depth, tile), lambda j, place: (0, j)),
-                pl.BlockSpec((depth, tile), lambda j, place: (0, j)),
-            ],
+            in_specs=in_specs,
             out_specs=pl.BlockSpec((blocks, 2, rows, tile), lambda j, place: (0, 0, 0, j)),
         ),
         compiler_params=pltpu.CompilerParams(vmem_limit_bytes=VMEM_LIMIT),
-        cost_estimate=NO_COST,
-    )(place, mine, theirs, gate_weight, up_weight, *far)
+        cost_estimate=pl.CostEstimate(
+            flops=4 * (far + 1) * total * depth * width,
+            bytes_accessed=(far + 1) * (4 * width + 2 * total) * depth + 8 * total * width,
+            transcendentals=0,
+        ),
+    )(place, *tokens, *weights)
 
 
 def gradient_kernel(batches, place_ref, features_ref, *refs):
@@ -87,7 +88,11 @@
         ),
         input_output_aliases={2 + len(acts) + i: i for i in range(len(totals))},
         compiler_params=pltpu.CompilerParams(vmem_limit_bytes=VMEM_LIMIT),
-        cost_estimate=NO_COST,
+        cost_estimate=pl.CostEstimate(
+            flops=4 * cores * total * depth * width,
+            bytes_accessed=cores * (8 * depth + 4 * total) * width + 2 * total * depth,
+            transcendentals=0,
+        ),
     )(place, features, *acts, *totals)
 
 
@@ -161,34 +166,42 @@
     over_row = lax.ppermute(mine, "row", swap)
     over_depth = lax.ppermute(mine, "depth", swap)
     over_both = lax.ppermute(over_row, "depth", swap)
-    far_weights = {0: exchange_weights(0, ())}
-    far_weights[1] = far_weights[0]
-    first_tile = ((part * half + core * share) // tile).astype(jnp.int32).reshape(1)
+    own_tile, other_tile = [
+        ((part * half + owner * share) // tile).astype(jnp.int32).reshape(1)
+        for owner in (core, 1 - core)
+    ]
 
     def arrange(values):
         values = values.reshape(line, rows, depth)
         return jnp.where(at_far, values[::-1], values)
 
-    def both_cores(values, after):
-        values = arrange(tie(values, after))
-        return values, send(values, pairs)
-
-    def multiply(k, tokens, after):
-        _, start, _ = pieces[k]
-        mine, theirs = (value.reshape(-1, depth) for value in tie(tokens, after))
-        weights = (gate_weight, up_weight, far_weights[k])
-        return forward(first_tile, mine, theirs, *weights, start, tile, line, scale)
-
-    features = [by(row == 0, mine, over_row, 1)]
-    spread = [both_cores(features[0], ())]
-    terms = multiply(0, spread[0], ())
-    payload = terms[3].astype(WIRE)
+    def own_features(tokens, k, after):
+        _, start, width = pieces[k]
+        tokens = tie(tokens, after).reshape(-1, depth)
+        weights = (gate_weight, up_weight)
+        common = (weights, start, width, tile, line, scale)
+        theirs = send(forward(other_tile, [tokens], *common).astype(WIRE), pairs)
+        return forward(own_tile, [tie(tokens, theirs[:0])], *common), theirs
+
+    def all_features(tokens, k, after):
+        _, start, width = pieces[k]
+        tokens = [value.reshape(-1, depth) for value in tie(tokens, after)]
+        weights = (gate_weight, up_weight, *far_weights)
+        return forward(own_tile, tokens, weights, start, width, tile, line, scale), None
+
+    def take(terms, block):
+        own, theirs = terms
+        return own[block] if theirs is None else own[block] + wide(theirs[block])
+
+    features = [arrange(by(row == 0, mine, over_row, 1))]
+    terms = own_features(features[0], 0, ())
+    payload = take(terms, 3).astype(WIRE)
     in_1 = send(payload, inward)
 
     over_depth, over_both = tie((over_depth, over_both), payload)
-    features.append(by(row == 0, over_depth, over_both, 1))
-    spread.append(both_cores(features[1], ()))
-    far_weights[2] = exchange_weights(2, spread[1])
+    features.append(arrange(by(row == 0, over_depth, over_both, 1)))
+    far_weights = exchange_weights(2, in_1)
+    far_features = [send(tie(value, in_1), pairs) for value in features]
 
     mine_cotangent, cotangent = tie((grad_hidden[0], grad_hidden[0]), in_1)
     cotangent = jnp.stack(
@@ -229,8 +242,14 @@
         )
         return blocks, send(blocks, pairs)
 
-    turned = jnp.concatenate([tie(near, in_1).reshape(-1, depth) for near, _ in spread]).T
-    turned_in_place = jnp.concatenate([tie(value, in_1) for value in features]).T
+    near_features = [tie(value, in_1) for value in features]
+    turned, turned_in_place = [
+        jnp.concatenate([value.reshape(-1, depth) for value in values]).T
+        for values in (
+            near_features,
+            [jnp.where(at_far, value[::-1], value) for value in near_features],
+        )
+    ]
 
     def finish(gathered, totals, start):
         own, other = [value for value, _ in gathered], [value for _, value in gathered]
@@ -243,39 +262,55 @@
     hidden, totals, waiting = ([], []), (), []
     act = hops = None
     for k in range(-1, last):
-        if act is not None:
+        gathering = act is not None
+        if gathering:
             side_1, centre_1 = send(act, side), send(act, centre)
         if hops is not None:
             waiting.append(merge(*hops))
             terms = tie(terms, waiting[-1][0])
-        far = add(terms[3], in_1).astype(WIRE)
-        centre_2 = send(far, centre)
-        in_2 = send(tie(terms[2], in_1).astype(WIRE), inward)
-        if act is not None:
+        centre_2 = send(add(take(terms, 3), in_1).astype(WIRE), centre)
+        in_2 = send(take(tie(terms, in_1), 2).astype(WIRE), inward)
+        arrived = ()
+        if gathering:
+            side_1, centre_1 = tie((side_1, centre_1), in_1)
             out_2, share_2 = send(centre_1, outward), send(side_1, centre)
+            arrived = (side_1, centre_1)
         following = None
         if k + 2 <= last:
-            tokens = spread[1] if k < 0 else [jnp.stack(pair, axis=1) for pair in zip(*spread)]
-            following = multiply(k + 2, tokens, (in_1, *(() if act is None else (side_1, centre_1))))
-            terms = tie(terms, following)
-        near = add(terms[2], in_2).astype(WIRE)
-        swapped = jnp.where(at_end, terms[1], add(terms[0], centre_2)).astype(WIRE)
+            if k < 0:
+                following = own_features(features[1], 1, in_1)
+            else:
+                tokens = [jnp.stack(values, axis=1) for values in (features, far_features)]
+                following = all_features(tokens, k + 2, in_1)
+        terms = tie(terms, arrived, following)
+        near = add(take(terms, 2), in_2).astype(WIRE)
+        swapped = jnp.where(at_end, take(terms, 1), add(take(terms, 0), centre_2)).astype(WIRE)
         centre_3, side_3 = send(near, centre), send(swapped, side)
         if following is not None:
-            in_1 = send(tie(following[3], near, swapped).astype(WIRE), inward)
-        if act is not None:
+            in_1 = send(take(tie(following, near, swapped), 3).astype(WIRE), inward)
+        arrived = ()
+        if gathering:
+            out_2, share_2 = tie((out_2, share_2), in_2, centre_2)
             out_3 = send(share_2, outward)
-        own = jnp.where(at_end, terms[0], terms[1])
+            arrived = (out_2, share_2)
+        terms = tie(terms, arrived)
+        own = jnp.where(at_end, take(terms, 0), take(terms, 1))
         ready = activate(k + 1, add(own, side_3, centre_3))
-        if act is not None:
+        if gathering:
             hops = tie((act, side_1, centre_1, out_2, share_2, out_3), ready)
         act, terms = ready, following
 
-    everything = lax.all_gather(tie(act, share_2), "col", axis=0).reshape(line, 2, *act.shape)
+    start, width = pieces[last][1:]
+    gathered = []
+    for begin, count in cut(width // tile, LAST_SHARES):
+        chosen = act[:, :, begin * tile : (begin + count) * tile]
+        chosen = lax.all_gather(tie(chosen, out_3), "col", axis=0)
+        gathered.append((start + begin * tile, chosen.reshape(line, 2, *chosen.shape[1:])))
     waiting.append(merge(*hops))
     totals = finish(waiting, totals, pieces[0][1])
     places = jnp.array([0, share // tile], jnp.int32)
-    totals = gradient(places, turned_in_place, [everything], totals, half, pieces[last][1], tile)
+    for start, acts in gathered:
+        totals = gradient(places, turned_in_place, [acts], totals, half, start, tile)
 
     hidden = jnp.stack([jnp.concatenate(parts, axis=1) for parts in hidden])
     hidden = hidden.reshape(2, 2, slab, share)

time: 318 us -> 285 us (0.90)
  waiting for transfers between devices: 117 us -> 95.7 us
  starting transfers between devices: 83.7 us -> 71.7 us
  local copies, waits for them, and re-layouts: 25.7 us -> 16.6 us
  other arithmetic: 27.2 us -> 35 us
    ppermute x35, waiting for transfers between devices: 101 us -> 55.3 us  [send(): return lax.ppermute(value, 'col', route)]
    all_gather x1 -> x2, waiting for transfers between devices: 0.01 us -> 23.8 us  [local(): chosen = lax.all_gather(tie(chosen, out_3), 'col', axis=0)]
    ppermute x35, starting transfers between devices: 77.3 us -> 65.4 us  [send(): return lax.ppermute(value, 'col', route)]
    convert_element_type x11 -> x14, other arithmetic: 3.15 us -> 12.7 us  [the longest x3 4.07 us: local(): jnp.where(at_end, take(terms, 1), add(take(terms, 0), centre_2))]
    dynamic_slice x5 -> x3, local copies, waits for them, and re-layouts: 11.6 us -> 5.36 us  [columns_of(): return lax.dynamic_slice_in_dim(array, start, width, array.ndim - 1)]
    optimization_barrier x4 -> x2, local copies, waits for them, and re-layouts: 5.03 us -> 0.24 us  [tie(): return lax.optimization_barrier((value, after))[0]]
    select_n x2, other arithmetic: 4.44 us -> 0.38 us  [arrange(): return jnp.where(at_far, values[::-1], values)]
    ppermute x1, waiting for transfers between devices: 6.58 us -> 3.29 us  [local(): lax.ppermute(columns_of(cotangent, (1 - part) * half, half), 'depth', swap)]
  transfers between devices with their start and end apart: 41 -> 42, of which waited for: 12 -> 15; matrix products, arithmetic and copies ran while one was open for 14% -> 15% of each run, Pallas kernels for 11% -> 15%
where the time goes in v9:
time: 285 us; the launch traced here: 283 us
  waiting for transfers between devices  95.7 us (34%)
  starting transfers between devices  71.7 us (25%)
  Pallas kernels  49.6 us (17%)
  other arithmetic  35 us (12%)
  local copies, waits for them, and re-layouts  16.6 us (6%)
  between operations  14.9 us (5%)
    ppermute x35, starting transfers between devices, send(): return lax.ppermute(value, 'col', route)  65.4 us
    ppermute x35, waiting for transfers between devices, send(): return lax.ppermute(value, 'col', route)  55.3 us
    pallas_call x5, Pallas kernels, forward(): pl.pallas_call(functools.partial(forward_kernel, scale), out_shape=jax.Sh...  26 us
    all_gather x2, waiting for transfers between devices, local(): chosen = lax.all_gather(tie(chosen, out_3), 'col', axis=0)  23.8 us
    pallas_call x4, Pallas kernels, gradient(): pl.pallas_call(functools.partial(gradient_kernel, len(acts)), out_shape=(...  23.6 us
    ppermute x1, waiting for transfers between devices, local(): over_row = lax.ppermute(mine, 'row', swap)  9.05 us
    unnamed x68, local copies, waits for them, and re-layouts  6.09 us
  transfers between devices with their start and end apart: 42, of which 15 were waited for; matrix products, arithmetic and copies ran while one was open for 15% of the time, Pallas kernels for 15%

profile of v9, /device:TPU:1, one launch (start us, length us, event | category | flops | bytes accessed | tf_op | source)
XLA Modules:
  0.0 283.5 jit_solution(13994016993485357547)
XLA Ops:
  7.2 2.1 collective-permute-start
  9.3 9.1 %collective-permute-done = bf16[384,512]{1,0:T(8,128)(2,1)S(1)} collective-permute-done((bf16[384,512]{1,0:T(8,128)(2,1)}, bf16[384,512]{1,0:T(8,128)(2,1)S(1)}, u32[]{:S(2)}, u32[]{:S(2)}) %collective-permute-start) | collective-permute-done | bytes 393248 | tf_op jit(solution)/shard_map/ppermute | solution.py:166
  18.4 1.4 maximum_select_fusion
  19.9 4.4 %shard_map.77 = f32[4,2,96,1024]{3,2,1,0:T(8,128)S(1)} custom-call(s32[1]{0:T(128)} %bitcast.5.place_ref, bf16[384,1024]{1,0:T(8,128)(2,1)S(1)} %bitcast.181, bf16[1024,7168]{1,0:T(8,128)(2,1)} %refs_2_.9, bf16[1024,7168]{1,0:T(8,128)(2,1)} %refs_3_.1), custom_call_target="tpu_custom_call" | custom-call | flops 1610612736 | bytes 8126464 | tf_op jit(solution)/shard_map/pallas_call | solution.py:38
  24.4 1.5 convert_element_type.191
  27.1 1.5 collective-permute-start.2
  28.6 2.7 constant_dynamic-slice_fusion.2
  31.3 2.7 constant_dynamic-slice_fusion.1
  34.1 4.4 %shard_map.76 = f32[4,2,96,1024]{3,2,1,0:T(8,128)S(1)} custom-call(s32[1]{0:T(128)} %bitcast.place_ref, bf16[384,1024]{1,0:T(8,128)(2,1)S(1)} %bitcast.182, bf16[1024,7168]{1,0:T(8,128)(2,1)} %refs_2_.9, bf16[1024,7168]{1,0:T(8,128)(2,1)} %refs_3_.1), custom_call_target="tpu_custom_call" | custom-call | flops 1610612736 | bytes 8126464 | tf_op jit(solution)/shard_map/pallas_call | solution.py:38
  39.7 3.4 %collective-permute-start.4 = (f16[2,96,1024]{2,1,0:T(8,128)(2,1)S(1)}, f16[2,96,1024]{2,1,0:T(8,128)(2,1)S(1)}, u32[]{:S(2)}, u32[]{:S(2)}) collective-permute-start(f16[2,96,1024]{2,1,0:T(8,128)(2,1)S(1)} %fusion.27), channel_id=1, source_target_pairs={{0,4},{2,6},{12,8},{14,10},{1,5},{3,7},{13,9},{15,11},{16,20},{18,... | collective-permute-start | bytes 1179656 | tf_op jit(solution)/shard_map/ppermute | solution.py:133
  43.2 3.1 %collective-permute-done.3 = bf16[384,512]{1,0:T(8,128)(2,1)S(1)} collective-permute-done((bf16[384,512]{1,0:T(8,128)(2,1)S(1)}, bf16[384,512]{1,0:T(8,128)(2,1)S(1)}, u32[]{:S(2)}, u32[]{:S(2)}) %collective-permute-start.3) | collective-permute-done | bytes 393248 | tf_op jit(solution)/shard_map/ppermute | solution.py:168
  46.8 1.3 pad_maximum_fusion
  48.3 2.8 collective-permute-done.4
  51.1 1.4 collective-permute-start.11
  52.5 4.4 %shard_map.79 = f32[4,2,96,1024]{3,2,1,0:T(8,128)S(1)} custom-call(s32[1]{0:T(128)} %bitcast.5.place_ref, bf16[384,1024]{1,0:T(8,128)(2,1)S(1)} %bitcast.184, bf16[1024,7168]{1,0:T(8,128)(2,1)} %refs_2_.9, bf16[1024,7168]{1,0:T(8,128)(2,1)} %refs_3_.1), custom_call_target="tpu_custom_call" | custom-call | flops 1610612736 | bytes 8126464 | tf_op jit(solution)/shard_map/pallas_call | solution.py:38
  57.0 1.3 collective-permute-start.15
  58.3 2.0 add_convert_fusion.3
  60.2 1.4 collective-permute-start.6
  61.7 1.5 convert_element_type.194
  63.4 3.3 %collective-permute-done.15 = bf16[48,3584]{1,0:T(8,128)(2,1)S(1)} collective-permute-done((bf16[48,3584]{1,0:T(8,128)(2,1)S(1)}, bf16[48,3584]{1,0:T(8,128)(2,1)S(1)}, u32[]{:S(2)}, u32[]{:S(2)}) %collective-permute-start.15) | collective-permute-done | bytes 344096 | tf_op jit(solution)/shard_map/ppermute | solution.py:210
  68.8 4.1 %collective-permute-start.8 = (f16[2,96,1024]{2,1,0:T(8,128)(2,1)S(1)}, f16[2,96,1024]{2,1,0:T(8,128)(2,1)S(1)}, u32[]{:S(2)}, u32[]{:S(2)}) collective-permute-start(f16[2,96,1024]{2,1,0:T(8,128)(2,1)S(1)} %fusion.39), channel_id=1, source_target_pairs={{0,4},{2,6},{12,8},{14,10},{1,5},{3,7},{13,9},{15,11},{16,20},{18,... | collective-permute-start | bytes 1179656 | tf_op jit(solution)/shard_map/ppermute | solution.py:133
  72.9 4.4 %shard_map.78 = f32[4,2,96,1024]{3,2,1,0:T(8,128)S(1)} custom-call(s32[1]{0:T(128)} %bitcast.place_ref, bf16[384,1024]{1,0:T(8,128)(2,1)S(1)} %bitcast.185, bf16[1024,7168]{1,0:T(8,128)(2,1)} %refs_2_.9, bf16[1024,7168]{1,0:T(8,128)(2,1)} %refs_3_.1), custom_call_target="tpu_custom_call" | custom-call | flops 1610612736 | bytes 8126464 | tf_op jit(solution)/shard_map/pallas_call | solution.py:38
  79.1 2.3 collective-permute-done.8
  81.4 2.0 fusion.17
  83.4 2.3 collective-permute-start.7
  86.6 1.3 pad_maximum_fusion.1
  88.0 4.3 %collective-permute-start.12 = (f16[2,96,1024]{2,1,0:T(8,128)(2,1)S(1)}, f16[2,96,1024]{2,1,0:T(8,128)(2,1)S(1)}, u32[]{:S(2)}, u32[]{:S(2)}) collective-permute-start(f16[2,96,1024]{2,1,0:T(8,128)(2,1)S(1)} %fusion.40), channel_id=1, source_target_pairs={{0,4},{2,6},{12,8},{14,10},{1,5},{3,7},{13,9},{15,11},{16,20},{18,... | collective-permute-start | bytes 1179656 | tf_op jit(solution)/shard_map/ppermute | solution.py:133
  92.3 2.1 collective-permute-done.7
  94.4 1.6 fusion.19
  97.1 5.7 %collective-permute-start.17 = (bf16[2,96,1024]{2,1,0:T(8,128)(2,1)S(1)}, bf16[2,96,1024]{2,1,0:T(8,128)(2,1)S(1)}, u32[]{:S(2)}, u32[]{:S(2)}) collective-permute-start(bf16[2,96,1024]{2,1,0:T(8,128)(2,1)S(1)} %pad_maximum_fusion.5), channel_id=1, source_target_pairs={{0,4},{2,6},{12,8},{14,10},{4,0},{6,2},{8,12},{10,14},{1,5},{3,7},... | collective-permute-start | bytes 1179656 | tf_op jit(solution)/shard_map/ppermute | solution.py:133
  103.8 1.4 collective-permute-start.22
  105.5 5.6 %collective-permute-start.21 = (f16[2,96,1024]{2,1,0:T(8,128)(2,1)S(1)}, f16[2,96,1024]{2,1,0:T(8,128)(2,1)}, u32[]{:S(2)}, u32[]{:S(2)}) collective-permute-start(f16[2,96,1024]{2,1,0:T(8,128)(2,1)S(1)} %fusion.41), channel_id=1, source_target_pairs={{0,4},{2,6},{12,8},{14,10},{1,5},{3,7},{13,9},{15,11},{16,20},{18,... | collective-permute-start | bytes 1179656 | tf_op jit(solution)/shard_map/ppermute | solution.py:133
  112.3 8.2 %shard_map.80 = f32[4,2,192,768]{3,2,1,0:T(8,128)} custom-call(s32[1]{0:T(128)} %bitcast.place_ref, bf16[768,1024]{1,0:T(8,128)(2,1)S(1)} %bitcast.187, bf16[768,1024]{1,0:T(8,128)(2,1)S(1)} %bitcast.188, bf16[1024,7168]{1,0:T(8,128)(2,1)} %refs_2_.9, bf16[1024,7168]{1,0:T(8,128)(2,1)} %refs_3_.1, bf16[1024,768]{1,0:T(8,128)(2,1)S(1)} %collective-permute-done.13.refs_4_, ...), custom_call_target="tpu_custom_call" | custom-call | flops 4831838208 | bytes 14155776 | tf_op jit(solution)/shard_map/pallas_call | solution.py:38
  121.4 1.6 collective-permute-start.19
  123.0 1.7 fusion.12
  124.7 2.2 collective-permute-start.24
  127.6 3.4 %collective-permute-start.28 = (f16[2,192,768]{2,1,0:T(8,128)(2,1)S(1)}, f16[2,192,768]{2,1,0:T(8,128)(2,1)S(1)}, u32[]{:S(2)}, u32[]{:S(2)}) collective-permute-start(f16[2,192,768]{2,1,0:T(8,128)(2,1)S(1)} %fusion.25), channel_id=1, source_target_pairs={{0,4},{2,6},{12,8},{14,10},{1,5},{3,7},{13,9},{15,11},{16,20},{18,... | collective-permute-start | bytes 1769480 | tf_op jit(solution)/shard_map/ppermute | solution.py:133
  131.1 1.5 collective-permute-start.23
  132.5 7.0 %collective-permute-done.24 = f16[2,96,1024]{2,1,0:T(8,128)(2,1)S(1)} collective-permute-done((f16[2,96,1024]{2,1,0:T(8,128)(2,1)S(1)}, f16[2,96,1024]{2,1,0:T(8,128)(2,1)S(1)}, u32[]{:S(2)}, u32[]{:S(2)}) %collective-permute-start.24) | collective-permute-done | bytes 393248 | tf_op jit(solution)/shard_map/ppermute | solution.py:133
  140.9 7.0 %collective-permute-done.23 = bf16[2,96,1024]{2,1,0:T(8,128)(2,1)S(1)} collective-permute-done((bf16[2,96,1024]{2,1,0:T(8,128)(2,1)S(1)}, bf16[2,96,1024]{2,1,0:T(8,128)(2,1)S(1)}, u32[]{:S(2)}, u32[]{:S(2)}) %collective-permute-start.23) | collective-permute-done | bytes 393248 | tf_op jit(solution)/shard_map/ppermute | solution.py:133
  148.1 1.9 fusion.46
  151.0 3.0 %collective-permute-start.31 = (f16[2,192,768]{2,1,0:T(8,128)(2,1)S(1)}, f16[2,192,768]{2,1,0:T(8,128)(2,1)S(1)}, u32[]{:S(2)}, u32[]{:S(2)}) collective-permute-start(f16[2,192,768]{2,1,0:T(8,128)(2,1)S(1)} %fusion.26), channel_id=1, source_target_pairs={{0,4},{2,6},{12,8},{14,10},{1,5},{3,7},{13,9},{15,11},{16,20},{18,... | collective-permute-start | bytes 1769480 | tf_op jit(solution)/shard_map/ppermute | solution.py:133
  154.7 1.5 collective-permute-start.26
  156.2 14.9 %collective-permute-done.26 = bf16[2,96,1024]{2,1,0:T(8,128)(2,1)S(1)} collective-permute-done((bf16[2,96,1024]{2,1,0:T(8,128)(2,1)S(1)}, bf16[2,96,1024]{2,1,0:T(8,128)(2,1)S(1)}, u32[]{:S(2)}, u32[]{:S(2)}) %collective-permute-start.26) | collective-permute-done | bytes 393248 | tf_op jit(solution)/shard_map/ppermute | solution.py:133
  171.6 2.3 collective-permute-start.33
  174.5 1.4 collective-permute-start.30
  176.0 1.3 collective-permute-start.29
  177.4 12.8 %collective-permute-done.29 = bf16[2,96,1024]{2,1,0:T(8,128)(2,1)S(1)} collective-permute-done((bf16[2,96,1024]{2,1,0:T(8,128)(2,1)S(1)}, bf16[2,96,1024]{2,1,0:T(8,128)(2,1)S(1)}, u32[]{:S(2)}, u32[]{:S(2)}) %collective-permute-start.29) | collective-permute-done | bytes 393248 | tf_op jit(solution)/shard_map/ppermute | solution.py:133
  190.1 1.3 collective-permute-start.37
  191.8 1.3 fusion.24
  193.9 6.2 %collective-permute-done.37 = bf16[2,96,1024]{2,1,0:T(8,128)(2,1)} collective-permute-done((bf16[2,96,1024]{2,1,0:T(8,128)(2,1)}, bf16[2,96,1024]{2,1,0:T(8,128)(2,1)}, u32[]{:S(2)}, u32[]{:S(2)}) %collective-permute-start.37) | collective-permute-done | bytes 393248 | tf_op jit(solution)/shard_map/ppermute | solution.py:133
  205.4 1.3 maximum_bitcast_fusion.features_ref
  206.7 7.6 %collective-permute-start.38 = (bf16[4,2,96,1024]{3,2,1,0:T(8,128)(2,1)}, bf16[4,2,96,1024]{3,2,1,0:T(8,128)(2,1)}, u32[]{:S(2)}, u32[]{:S(2)}) collective-permute-start(bf16[4,2,96,1024]{3,2,1,0:T(8,128)(2,1)} %get-tuple-element.134), channel_id=1, source_target_pairs={{0,2},{2,0},{4,6},{6,4},{8,10},{10,8},{12,14},{14,12},{1,3},{3,1},... | collective-permute-start | bytes 4718600 | tf_op jit(solution)/shard_map/ppermute | solution.py:133
  216.9 1.9 fusion.45
  219.8 1.3 maximum_select_fusion.3
  221.2 1.3 collective-permute-start.36
  223.8 5.9 %shard_map.81 = (f32[1024,3584]{1,0:T(8,128)}, f32[1024,3584]{1,0:T(8,128)}) custom-call(s32[1]{0:T(128)} %bitcast.77.place_ref, bf16[1024,768]{1,0:T(8,128)(2,1)S(1)} %maximum_bitcast_fusion.1.features_ref, bf16[4,1,2,96,1024]{4,3,2,1,0:T(8,128)(2,1)S(1)} %copy-done.4, bf16[4,1,2,96,1024]{4,3,2,1,0:T(8,128)(2,1)S(1)} %copy-done.5), custom_call_target="tpu_custom_call" | custom-call | flops 3221225472 | bytes 13107200 | tf_op jit(solution)/shard_map/pallas_call | solution.py:80
  231.8 7.3 %shard_map.82 = (f32[1024,3584]{1,0:T(8,128)}, f32[1024,3584]{1,0:T(8,128)}) custom-call(s32[1]{0:T(128)} %bitcast.67.place_ref, bf16[1024,768]{1,0:T(8,128)(2,1)S(1)} %maximum_bitcast_fusion.1.features_ref, bf16[4,1,2,96,1024]{4,3,2,1,0:T(8,128)(2,1)} %bitcast.71.refs_0_, ...), custom_call_target="tpu_custom_call", output_to_operand_aliasing={{0}: (4, {}), {1}: (5, {})} | custom-call | flops 3221225472 | bytes 13107200 | tf_op jit(solution)/shard_map/pallas_call | solution.py:80
  239.2 6.5 %all-gather.7.cloned.1.call-done = bf16[16,192,512]{2,1,0:T(8,128)(2,1)} async-done(((bf16[2,192,512]{2,1,0:T(8,128)(2,1)}), bf16[16,192,512]{2,1,0:T(8,128)(2,1)}) %all-gather.7.cloned.1.call-update) | async-done | bytes 3145744 | tf_op jit(solution)/shard_map/all_gather | solution.py:307
  245.6 1.9 copy-done.2
  247.5 6.3 %shard_map.83 = (f32[1024,3584]{1,0:T(8,128)}, f32[1024,3584]{1,0:T(8,128)}) custom-call(s32[2]{0:T(128)S(1)} %iota_multiply_fusion.place_ref, bf16[1024,768]{1,0:T(8,128)(2,1)S(1)} %maximum_bitcast_fusion.features_ref, bf16[4,2,2,192,512]{4,3,2,1,0:T(8,128)(2,1)S(1)} %bitcast.189, ...), custom_call_target="tpu_custom_call", output_to_operand_aliasing={{0}: (3, {}), {1}: (4, {})} | custom-call | flops 3221225472 | bytes 13107200 | tf_op jit(solution)/shard_map/pallas_call | solution.py:80
  253.9 17.4 %all-gather.5.cloned.1.call-done = bf16[16,192,256]{2,1,0:T(8,128)(2,1)} async-done(((bf16[2,192,256]{2,1,0:T(8,128)(2,1)}), bf16[16,192,256]{2,1,0:T(8,128)(2,1)}) %all-gather.5.cloned.1.call-update) | async-done | bytes 1572880 | tf_op jit(solution)/shard_map/all_gather | solution.py:307
  271.2 1.4 copy-done.3
  272.6 4.0 %shard_map.84 = (f32[1024,3584]{1,0:T(8,128)}, f32[1024,3584]{1,0:T(8,128)}) custom-call(s32[2]{0:T(128)S(1)} %iota_multiply_fusion.place_ref, bf16[1024,768]{1,0:T(8,128)(2,1)S(1)} %maximum_bitcast_fusion.features_ref, bf16[4,2,2,192,256]{4,3,2,1,0:T(8,128)(2,1)S(1)} %bitcast.190, ...), custom_call_target="tpu_custom_call", output_to_operand_aliasing={{0}: (3, {}), {1}: (4, {})} | custom-call | flops 1610612736 | bytes 7340032 | tf_op jit(solution)/shard_map/pallas_call | solution.py:80
  (165 shorter events, 31.3 us)
Async XLA Ops:
  7.2 49.8 %copy-start = (bf16[1,48,7168]{2,1,0:T(8,128)(2,1)S(1)}, bf16[1,48,7168]{2,1,0:T(8,128)(2,1)}, u32[]{:S(2)}) copy-start(bf16[1,48,7168]{2,1,0:T(8,128)(2,1)} %param.8) | copy-start | bytes 2064388
  7.2 238.5 %all-gather.7.cloned.1.call-start = ((), (), s32[]{:S(2)}) async-start(), calls=%async_computation.1 | async-start | bytes 3538944 | tf_op jit(solution)/shard_map/all_gather | solution.py:307
  7.2 11.2 %collective-permute-start = (bf16[384,512]{1,0:T(8,128)(2,1)}, bf16[384,512]{1,0:T(8,128)(2,1)S(1)}, u32[]{:S(2)}, u32[]{:S(2)}) collective-permute-start(bf16[384,512]{1,0:T(8,128)(2,1)} %bitcast.201), channel_id=1, source_target_pairs={{0,16},{16,0},{1,17},{17,1},{2,18},{18,2},{3,19},{19,3},{4,20},{20... | collective-permute-start | bytes 1179656 | tf_op jit(solution)/shard_map/ppermute | solution.py:166
  24.4 2.7 copy-start.27
  25.9 12.7 %collective-permute-start.1 = (f16[4,2,96,1024]{3,2,1,0:T(8,128)(2,1)}, f16[4,2,96,1024]{3,2,1,0:T(8,128)(2,1)}, u32[]{:S(2)}, u32[]{:S(2)}) collective-permute-start(f16[4,2,96,1024]{3,2,1,0:T(8,128)(2,1)} %convert_element_type.191), channel_id=1, source_target_pairs={{0,2},{2,0},{4,6},{6,4},{8,10},{10,8},{12,14},{14,12},{1,3},{3,1},... | collective-permute-start | bytes 4718600 | tf_op jit(solution)/shard_map/ppermute | solution.py:133
  27.1 16.1 %collective-permute-start.2 = (bf16[384,512]{1,0:T(8,128)(2,1)S(1)}, bf16[384,512]{1,0:T(8,128)(2,1)S(1)}, u32[]{:S(2)}, u32[]{:S(2)}) collective-permute-start(bf16[384,512]{1,0:T(8,128)(2,1)S(1)} %bitcast.203), channel_id=1, source_target_pairs={{0,1},{1,0},{2,3},{3,2},{4,5},{5,4},{6,7},{7,6},{8,9},{9,8},{10,11... | collective-permute-start | bytes 1179656 | tf_op jit(solution)/shard_map/ppermute | solution.py:167
  33.9 12.4 %collective-permute-start.3 = (bf16[384,512]{1,0:T(8,128)(2,1)S(1)}, bf16[384,512]{1,0:T(8,128)(2,1)S(1)}, u32[]{:S(2)}, u32[]{:S(2)}) collective-permute-start(bf16[384,512]{1,0:T(8,128)(2,1)S(1)} %collective-permute-done), channel_id=1, source_target_pairs={{0,1},{1,0},{2,3},{3,2},{4,5},{5,4},{6,7},{7,6},{8,9},{9,8},{10,11... | collective-permute-start | bytes 1179656 | tf_op jit(solution)/shard_map/ppermute | solution.py:168
  39.7 11.3 %collective-permute-start.4 = (f16[2,96,1024]{2,1,0:T(8,128)(2,1)S(1)}, f16[2,96,1024]{2,1,0:T(8,128)(2,1)S(1)}, u32[]{:S(2)}, u32[]{:S(2)}) collective-permute-start(f16[2,96,1024]{2,1,0:T(8,128)(2,1)S(1)} %fusion.27), channel_id=1, source_target_pairs={{0,4},{2,6},{12,8},{14,10},{1,5},{3,7},{13,9},{15,11},{16,20},{18,... | collective-permute-start | bytes 1179656 | tf_op jit(solution)/shard_map/ppermute | solution.py:133
  51.1 34.6 %collective-permute-start.11 = (bf16[4,96,1024]{2,1,0:T(8,128)(2,1)S(1)}, bf16[4,96,1024]{2,1,0:T(8,128)(2,1)S(1)}, u32[]{:S(2)}, u32[]{:S(2)}) collective-permute-start(bf16[4,96,1024]{2,1,0:T(8,128)(2,1)S(1)} %reverse_select_fusion.2), channel_id=1, source_target_pairs={{0,2},{2,0},{4,6},{6,4},{8,10},{10,8},{12,14},{14,12},{1,3},{3,1},... | collective-permute-start | bytes 2359304 | tf_op jit(solution)/shard_map/ppermute | solution.py:133
  57.0 9.8 %collective-permute-start.15 = (bf16[48,3584]{1,0:T(8,128)(2,1)S(1)}, bf16[48,3584]{1,0:T(8,128)(2,1)S(1)}, u32[]{:S(2)}, u32[]{:S(2)}) collective-permute-start(bf16[48,3584]{1,0:T(8,128)(2,1)S(1)} %constant_dynamic-slice_fusion), channel_id=1, source_target_pairs={{0,1},{1,0},{2,3},{3,2},{4,5},{5,4},{6,7},{7,6},{8,9},{9,8},{10,11... | collective-permute-start | bytes 1032200 | tf_op jit(solution)/shard_map/ppermute | solution.py:210
  60.2 18.0 %collective-permute-start.6 = (f16[2,96,1024]{2,1,0:T(8,128)(2,1)}, f16[2,96,1024]{2,1,0:T(8,128)(2,1)}, u32[]{:S(2)}, u32[]{:S(2)}) collective-permute-start(f16[2,96,1024]{2,1,0:T(8,128)(2,1)} %add_convert_fusion.3), channel_id=1, source_target_pairs={{4,8},{6,10},{8,4},{10,6},{5,9},{7,11},{9,5},{11,7},{20,24},{22,26... | collective-permute-start | bytes 1179656 | tf_op jit(solution)/shard_map/ppermute | solution.py:133
  63.1 14.8 %collective-permute-start.5 = (f16[4,2,96,1024]{3,2,1,0:T(8,128)(2,1)}, f16[4,2,96,1024]{3,2,1,0:T(8,128)(2,1)S(1)}, u32[]{:S(2)}, u32[]{:S(2)}) collective-permute-start(f16[4,2,96,1024]{3,2,1,0:T(8,128)(2,1)} %convert_element_type.194), channel_id=1, source_target_pairs={{0,2},{2,0},{4,6},{6,4},{8,10},{10,8},{12,14},{14,12},{1,3},{3,1},... | collective-permute-start | bytes 4718600 | tf_op jit(solution)/shard_map/ppermute | solution.py:133
  66.8 10.6 %collective-permute-start.16 = (bf16[2,48,1792]{2,1,0:T(8,128)(2,1)S(1)}, bf16[2,48,1792]{2,1,0:T(8,128)(2,1)S(1)}, u32[]{:S(2)}, u32[]{:S(2)}) collective-permute-start(bf16[2,48,1792]{2,1,0:T(8,128)(2,1)S(1)} %get-tuple-element.156), channel_id=1, source_target_pairs={{0,2},{2,0},{4,6},{6,4},{8,10},{10,8},{12,14},{14,12},{1,3},{3,1},... | collective-permute-start | bytes 1032200 | tf_op jit(solution)/shard_map/ppermute | solution.py:133
  68.8 12.6 %collective-permute-start.8 = (f16[2,96,1024]{2,1,0:T(8,128)(2,1)S(1)}, f16[2,96,1024]{2,1,0:T(8,128)(2,1)S(1)}, u32[]{:S(2)}, u32[]{:S(2)}) collective-permute-start(f16[2,96,1024]{2,1,0:T(8,128)(2,1)S(1)} %fusion.39), channel_id=1, source_target_pairs={{0,4},{2,6},{12,8},{14,10},{1,5},{3,7},{13,9},{15,11},{16,20},{18,... | collective-permute-start | bytes 1179656 | tf_op jit(solution)/shard_map/ppermute | solution.py:133
  77.4 8.9 %collective-permute-start.10 = (bf16[4,96,1024]{2,1,0:T(8,128)(2,1)S(1)}, bf16[4,96,1024]{2,1,0:T(8,128)(2,1)S(1)}, u32[]{:S(2)}, u32[]{:S(2)}) collective-permute-start(bf16[4,96,1024]{2,1,0:T(8,128)(2,1)S(1)} %reverse_select_fusion.3), channel_id=1, source_target_pairs={{0,2},{2,0},{4,6},{6,4},{8,10},{10,8},{12,14},{14,12},{1,3},{3,1},... | collective-permute-start | bytes 2359304 | tf_op jit(solution)/shard_map/ppermute | solution.py:133
  77.9 9.9 %copy-start.8 = (f16[4,2,96,1024]{3,2,1,0:T(8,128)(2,1)}, f16[4,2,96,1024]{3,2,1,0:T(8,128)(2,1)S(1)}, u32[]{:S(2)}) copy-start(f16[4,2,96,1024]{3,2,1,0:T(8,128)(2,1)S(1)} %collective-permute-done.5) | copy-start | bytes 4718596
  77.9 27.6 %collective-permute-start.13 = (bf16[1024,768]{1,0:T(8,128)(2,1)}, bf16[1024,768]{1,0:T(8,128)(2,1)S(1)}, u32[]{:S(2)}, u32[]{:S(2)}) collective-permute-start(bf16[1024,768]{1,0:T(8,128)(2,1)} %constant_dynamic-slice_fusion.2), channel_id=1, source_target_pairs={{0,2},{2,0},{4,6},{6,4},{8,10},{10,8},{12,14},{14,12},{1,3},{3,1},... | collective-permute-start | bytes 4718600 | tf_op jit(solution)/shard_map/ppermute | solution.py:133
  78.8 32.4 %collective-permute-start.14 = (bf16[1024,768]{1,0:T(8,128)(2,1)S(1)}, bf16[1024,768]{1,0:T(8,128)(2,1)S(1)}, u32[]{:S(2)}, u32[]{:S(2)}) collective-permute-start(bf16[1024,768]{1,0:T(8,128)(2,1)S(1)} %copy-done.19), channel_id=1, source_target_pairs={{0,2},{2,0},{4,6},{6,4},{8,10},{10,8},{12,14},{14,12},{1,3},{3,1},... | collective-permute-start | bytes 4718600 | tf_op jit(solution)/shard_map/ppermute | solution.py:133
  83.4 11.0 %collective-permute-start.7 = (f16[2,96,1024]{2,1,0:T(8,128)(2,1)S(1)}, f16[2,96,1024]{2,1,0:T(8,128)(2,1)S(1)}, u32[]{:S(2)}, u32[]{:S(2)}) collective-permute-start(f16[2,96,1024]{2,1,0:T(8,128)(2,1)S(1)} %get-tuple-element.129), channel_id=1, source_target_pairs={{0,4},{2,6},{12,8},{14,10},{4,0},{6,2},{8,12},{10,14},{1,5},{3,7},... | collective-permute-start | bytes 1179656 | tf_op jit(solution)/shard_map/ppermute | solution.py:133
  85.7 8.7 %collective-permute-start.9 = (f16[2,96,1024]{2,1,0:T(8,128)(2,1)S(1)}, f16[2,96,1024]{2,1,0:T(8,128)(2,1)S(1)}, u32[]{:S(2)}, u32[]{:S(2)}) collective-permute-start(f16[2,96,1024]{2,1,0:T(8,128)(2,1)S(1)} %get-tuple-element.130), channel_id=1, source_target_pairs={{4,8},{6,10},{8,4},{10,6},{5,9},{7,11},{9,5},{11,7},{20,24},{22,26... | collective-permute-start | bytes 1179656 | tf_op jit(solution)/shard_map/ppermute | solution.py:133
  88.0 14.8 %collective-permute-start.12 = (f16[2,96,1024]{2,1,0:T(8,128)(2,1)S(1)}, f16[2,96,1024]{2,1,0:T(8,128)(2,1)S(1)}, u32[]{:S(2)}, u32[]{:S(2)}) collective-permute-start(f16[2,96,1024]{2,1,0:T(8,128)(2,1)S(1)} %fusion.40), channel_id=1, source_target_pairs={{0,4},{2,6},{12,8},{14,10},{1,5},{3,7},{13,9},{15,11},{16,20},{18,... | collective-permute-start | bytes 1179656 | tf_op jit(solution)/shard_map/ppermute | solution.py:133
  95.9 6.8 %copy-start.7 = (bf16[4,2,96,1024]{3,2,0,1:T(8,128)(2,1)S(1)}, bf16[4,2,96,1024]{3,2,0,1:T(8,128)(2,1)}, u32[]{:S(2)}) copy-start(bf16[4,2,96,1024]{3,2,0,1:T(8,128)(2,1)} %pad_maximum_fusion) | copy-start | bytes 4718596
  96.3 6.6 %copy-start.9 = (f16[4,2,96,1024]{3,2,1,0:T(8,128)(2,1)S(1)}, f16[4,2,96,1024]{3,2,1,0:T(8,128)(2,1)}, u32[]{:S(2)}) copy-start(f16[4,2,96,1024]{3,2,1,0:T(8,128)(2,1)} %copy-done.8) | copy-start | bytes 4718596
  96.3 24.2 %collective-permute-start.18 = (bf16[2,96,1024]{2,1,0:T(8,128)(2,1)S(1)}, bf16[2,96,1024]{2,1,0:T(8,128)(2,1)S(1)}, u32[]{:S(2)}, u32[]{:S(2)}) collective-permute-start(bf16[2,96,1024]{2,1,0:T(8,128)(2,1)S(1)} %pad_maximum_fusion.5), channel_id=1, source_target_pairs={{4,8},{6,10},{8,4},{10,6},{5,9},{7,11},{9,5},{11,7},{20,24},{22,26... | collective-permute-start | bytes 1179656 | tf_op jit(solution)/shard_map/ppermute | solution.py:133
  97.1 23.4 %collective-permute-start.17 = (bf16[2,96,1024]{2,1,0:T(8,128)(2,1)S(1)}, bf16[2,96,1024]{2,1,0:T(8,128)(2,1)S(1)}, u32[]{:S(2)}, u32[]{:S(2)}) collective-permute-start(bf16[2,96,1024]{2,1,0:T(8,128)(2,1)S(1)} %pad_maximum_fusion.5), channel_id=1, source_target_pairs={{0,4},{2,6},{12,8},{14,10},{4,0},{6,2},{8,12},{10,14},{1,5},{3,7},... | collective-permute-start | bytes 1179656 | tf_op jit(solution)/shard_map/ppermute | solution.py:133
  103.8 19.1 %collective-permute-start.22 = (f16[2,96,1024]{2,1,0:T(8,128)(2,1)}, f16[2,96,1024]{2,1,0:T(8,128)(2,1)}, u32[]{:S(2)}, u32[]{:S(2)}) collective-permute-start(f16[2,96,1024]{2,1,0:T(8,128)(2,1)} %fusion.8), channel_id=1, source_target_pairs={{4,8},{6,10},{8,4},{10,6},{5,9},{7,11},{9,5},{11,7},{20,24},{22,26... | collective-permute-start | bytes 1179656 | tf_op jit(solution)/shard_map/ppermute | solution.py:133
  105.5 17.4 %collective-permute-start.21 = (f16[2,96,1024]{2,1,0:T(8,128)(2,1)S(1)}, f16[2,96,1024]{2,1,0:T(8,128)(2,1)}, u32[]{:S(2)}, u32[]{:S(2)}) collective-permute-start(f16[2,96,1024]{2,1,0:T(8,128)(2,1)S(1)} %fusion.41), channel_id=1, source_target_pairs={{0,4},{2,6},{12,8},{14,10},{1,5},{3,7},{13,9},{15,11},{16,20},{18,... | collective-permute-start | bytes 1179656 | tf_op jit(solution)/shard_map/ppermute | solution.py:133
  112.3 10.6 %copy-start.10 = (f16[4,2,96,1024]{3,2,1,0:T(8,128)(2,1)S(1)}, f16[4,2,96,1024]{3,2,1,0:T(8,128)(2,1)}, u32[]{:S(2)}) copy-start(f16[4,2,96,1024]{3,2,1,0:T(8,128)(2,1)} %copy-done.8) | copy-start | bytes 4718596
  120.5 7.0 %copy-start.6 = (f32[4,2,192,768]{3,2,1,0:T(8,128)S(1)}, f32[4,2,192,768]{3,2,1,0:T(8,128)}, u32[]{:S(2)}) copy-start(f32[4,2,192,768]{3,2,1,0:T(8,128)} %shard_map.80) | copy-start | bytes 14155780
  120.5 4.2 %copy-start.32 = (bf16[2,96,1024]{2,1,0:T(8,128)(2,1)}, bf16[2,96,1024]{2,1,0:T(8,128)(2,1)S(1)}, u32[]{:S(2)}) copy-start(bf16[2,96,1024]{2,1,0:T(8,128)(2,1)S(1)} %collective-permute-done.18) | copy-start | bytes 1179652
  120.5 4.2 %copy-start.30 = (bf16[2,96,1024]{2,1,0:T(8,128)(2,1)}, bf16[2,96,1024]{2,1,0:T(8,128)(2,1)S(1)}, u32[]{:S(2)}) copy-start(bf16[2,96,1024]{2,1,0:T(8,128)(2,1)S(1)} %collective-permute-done.17) | copy-start | bytes 1179652
  120.5 10.4 %collective-permute-start.20 = (bf16[2,96,1024]{2,1,0:T(8,128)(2,1)S(1)}, bf16[2,96,1024]{2,1,0:T(8,128)(2,1)S(1)}, u32[]{:S(2)}, u32[]{:S(2)}) collective-permute-start(bf16[2,96,1024]{2,1,0:T(8,128)(2,1)S(1)} %collective-permute-done.17), channel_id=1, source_target_pairs={{4,8},{6,10},{8,4},{10,6},{5,9},{7,11},{9,5},{11,7},{20,24},{22,26... | collective-permute-start | bytes 1179656 | tf_op jit(solution)/shard_map/ppermute | solution.py:133
  121.4 9.7 %collective-permute-start.19 = (bf16[2,96,1024]{2,1,0:T(8,128)(2,1)S(1)}, bf16[2,96,1024]{2,1,0:T(8,128)(2,1)S(1)}, u32[]{:S(2)}, u32[]{:S(2)}) collective-permute-start(bf16[2,96,1024]{2,1,0:T(8,128)(2,1)S(1)} %collective-permute-done.18), channel_id=1, source_target_pairs={{4,0},{6,2},{8,12},{10,14},{5,1},{7,3},{9,13},{11,15},{20,16},{22,... | collective-permute-start | bytes 1179656 | tf_op jit(solution)/shard_map/ppermute | solution.py:133
  124.7 14.8 %collective-permute-start.24 = (f16[2,96,1024]{2,1,0:T(8,128)(2,1)S(1)}, f16[2,96,1024]{2,1,0:T(8,128)(2,1)S(1)}, u32[]{:S(2)}, u32[]{:S(2)}) collective-permute-start(f16[2,96,1024]{2,1,0:T(8,128)(2,1)S(1)} %get-tuple-element.127), channel_id=1, source_target_pairs={{0,4},{2,6},{12,8},{14,10},{4,0},{6,2},{8,12},{10,14},{1,5},{3,7},... | collective-permute-start | bytes 1179656 | tf_op jit(solution)/shard_map/ppermute | solution.py:133
  126.9 12.6 %collective-permute-start.25 = (f16[2,96,1024]{2,1,0:T(8,128)(2,1)S(1)}, f16[2,96,1024]{2,1,0:T(8,128)(2,1)S(1)}, u32[]{:S(2)}, u32[]{:S(2)}) collective-permute-start(f16[2,96,1024]{2,1,0:T(8,128)(2,1)S(1)} %get-tuple-element.128), channel_id=1, source_target_pairs={{4,8},{6,10},{8,4},{10,6},{5,9},{7,11},{9,5},{11,7},{20,24},{22,26... | collective-permute-start | bytes 1179656 | tf_op jit(solution)/shard_map/ppermute | solution.py:133
  127.6 22.4 %collective-permute-start.28 = (f16[2,192,768]{2,1,0:T(8,128)(2,1)S(1)}, f16[2,192,768]{2,1,0:T(8,128)(2,1)S(1)}, u32[]{:S(2)}, u32[]{:S(2)}) collective-permute-start(f16[2,192,768]{2,1,0:T(8,128)(2,1)S(1)} %fusion.25), channel_id=1, source_target_pairs={{0,4},{2,6},{12,8},{14,10},{1,5},{3,7},{13,9},{15,11},{16,20},{18,... | collective-permute-start | bytes 1769480 | tf_op jit(solution)/shard_map/ppermute | solution.py:133
  131.1 16.9 %collective-permute-start.23 = (bf16[2,96,1024]{2,1,0:T(8,128)(2,1)S(1)}, bf16[2,96,1024]{2,1,0:T(8,128)(2,1)S(1)}, u32[]{:S(2)}, u32[]{:S(2)}) collective-permute-start(bf16[2,96,1024]{2,1,0:T(8,128)(2,1)S(1)} %collective-permute-done.20), channel_id=1, source_target_pairs={{4,0},{6,2},{8,12},{10,14},{5,1},{7,3},{9,13},{11,15},{20,16},{22,... | collective-permute-start | bytes 1179656 | tf_op jit(solution)/shard_map/ppermute | solution.py:133
  139.9 8.0 %copy-start.33 = (bf16[2,96,1024]{2,1,0:T(8,128)(2,1)S(1)}, bf16[2,96,1024]{2,1,0:T(8,128)(2,1)}, u32[]{:S(2)}) copy-start(bf16[2,96,1024]{2,1,0:T(8,128)(2,1)} %copy-done.32) | copy-start | bytes 1179652
  140.8 7.2 %copy-start.31 = (bf16[2,96,1024]{2,1,0:T(8,128)(2,1)S(1)}, bf16[2,96,1024]{2,1,0:T(8,128)(2,1)}, u32[]{:S(2)}) copy-start(bf16[2,96,1024]{2,1,0:T(8,128)(2,1)} %copy-done.30) | copy-start | bytes 1179652
  140.9 13.8 %copy-start.17 = (bf16[2,96,1024]{2,1,0:T(8,128)(2,1)}, bf16[2,96,1024]{2,1,0:T(8,128)(2,1)S(1)}, u32[]{:S(2)}) copy-start(bf16[2,96,1024]{2,1,0:T(8,128)(2,1)S(1)} %pad_maximum_fusion.6) | copy-start | bytes 1179652
  150.3 20.9 %collective-permute-start.32 = (f16[2,192,768]{2,1,0:T(8,128)(2,1)S(1)}, f16[2,192,768]{2,1,0:T(8,128)(2,1)S(1)}, u32[]{:S(2)}, u32[]{:S(2)}) collective-permute-start(f16[2,192,768]{2,1,0:T(8,128)(2,1)S(1)} %fusion.5), channel_id=1, source_target_pairs={{4,8},{6,10},{8,4},{10,6},{5,9},{7,11},{9,5},{11,7},{20,24},{22,26... | collective-permute-start | bytes 1769480 | tf_op jit(solution)/shard_map/ppermute | solution.py:133
  151.0 20.2 %collective-permute-start.31 = (f16[2,192,768]{2,1,0:T(8,128)(2,1)S(1)}, f16[2,192,768]{2,1,0:T(8,128)(2,1)S(1)}, u32[]{:S(2)}, u32[]{:S(2)}) collective-permute-start(f16[2,192,768]{2,1,0:T(8,128)(2,1)S(1)} %fusion.26), channel_id=1, source_target_pairs={{0,4},{2,6},{12,8},{14,10},{1,5},{3,7},{13,9},{15,11},{16,20},{18,... | collective-permute-start | bytes 1769480 | tf_op jit(solution)/shard_map/ppermute | solution.py:133
  154.0 2.2 collective-permute-start.27
  154.7 16.5 %collective-permute-start.26 = (bf16[2,96,1024]{2,1,0:T(8,128)(2,1)S(1)}, bf16[2,96,1024]{2,1,0:T(8,128)(2,1)S(1)}, u32[]{:S(2)}, u32[]{:S(2)}) collective-permute-start(bf16[2,96,1024]{2,1,0:T(8,128)(2,1)S(1)} %pad_maximum_fusion.6), channel_id=1, source_target_pairs={{0,4},{2,6},{12,8},{14,10},{4,0},{6,2},{8,12},{10,14},{1,5},{3,7},... | collective-permute-start | bytes 1179656 | tf_op jit(solution)/shard_map/ppermute | solution.py:133
  156.2 19.8 %copy-start.23 = (bf16[2,96,1024]{2,1,0:T(8,128)(2,1)}, bf16[2,96,1024]{2,1,0:T(8,128)(2,1)S(1)}, u32[]{:S(2)}) copy-start(bf16[2,96,1024]{2,1,0:T(8,128)(2,1)S(1)} %collective-permute-done.27) | copy-start | bytes 1179652
  171.2 3.4 %copy-start.28 = (bf16[2,96,1024]{2,1,0:T(8,128)(2,1)}, bf16[2,96,1024]{2,1,0:T(8,128)(2,1)S(1)}, u32[]{:S(2)}) copy-start(bf16[2,96,1024]{2,1,0:T(8,128)(2,1)S(1)} %collective-permute-done.26) | copy-start | bytes 1179652
  171.6 19.8 %collective-permute-start.33 = (f16[2,192,768]{2,1,0:T(8,128)(2,1)S(1)}, f16[2,192,768]{2,1,0:T(8,128)(2,1)S(1)}, u32[]{:S(2)}, u32[]{:S(2)}) collective-permute-start(f16[2,192,768]{2,1,0:T(8,128)(2,1)S(1)} %get-tuple-element.125), channel_id=1, source_target_pairs={{0,4},{2,6},{12,8},{14,10},{4,0},{6,2},{8,12},{10,14},{1,5},{3,7},... | collective-permute-start | bytes 1769480 | tf_op jit(solution)/shard_map/ppermute | solution.py:133
  173.8 17.6 %collective-permute-start.34 = (f16[2,192,768]{2,1,0:T(8,128)(2,1)S(1)}, f16[2,192,768]{2,1,0:T(8,128)(2,1)S(1)}, u32[]{:S(2)}, u32[]{:S(2)}) collective-permute-start(f16[2,192,768]{2,1,0:T(8,128)(2,1)S(1)} %get-tuple-element.126), channel_id=1, source_target_pairs={{4,8},{6,10},{8,4},{10,6},{5,9},{7,11},{9,5},{11,7},{20,24},{22,26... | collective-permute-start | bytes 1769480 | tf_op jit(solution)/shard_map/ppermute | solution.py:133
  174.5 2.8 collective-permute-start.30
  176.0 14.1 %collective-permute-start.29 = (bf16[2,96,1024]{2,1,0:T(8,128)(2,1)S(1)}, bf16[2,96,1024]{2,1,0:T(8,128)(2,1)S(1)}, u32[]{:S(2)}, u32[]{:S(2)}) collective-permute-start(bf16[2,96,1024]{2,1,0:T(8,128)(2,1)S(1)} %collective-permute-done.27), channel_id=1, source_target_pairs={{4,0},{6,2},{8,12},{10,14},{5,1},{7,3},{9,13},{11,15},{20,16},{22,... | collective-permute-start | bytes 1179656 | tf_op jit(solution)/shard_map/ppermute | solution.py:133
  190.1 10.1 %collective-permute-start.37 = (bf16[2,96,1024]{2,1,0:T(8,128)(2,1)}, bf16[2,96,1024]{2,1,0:T(8,128)(2,1)}, u32[]{:S(2)}, u32[]{:S(2)}) collective-permute-start(bf16[2,96,1024]{2,1,0:T(8,128)(2,1)} %collective-permute-done.30), channel_id=1, source_target_pairs={{4,0},{6,2},{8,12},{10,14},{5,1},{7,3},{9,13},{11,15},{20,16},{22,... | collective-permute-start | bytes 1179656 | tf_op jit(solution)/shard_map/ppermute | solution.py:133
  193.1 7.2 %copy-start.13 = (bf16[1,192,768]{2,1,0:T(8,128)(2,1)}, bf16[1,192,768]{2,1,0:T(8,128)(2,1)S(1)}, u32[]{:S(2)}) copy-start(bf16[1,192,768]{2,1,0:T(8,128)(2,1)S(1)} %get-tuple-element.136) | copy-start | bytes 884740
  200.2 71.0 %all-gather.5.cloned.1.call-start = ((), (), s32[]{:S(2)}) async-start(), calls=%async_computation | async-start | bytes 1769472 | tf_op jit(solution)/shard_map/all_gather | solution.py:307
  205.4 8.9 %copy-start.24 = (bf16[2,96,1024]{2,1,0:T(8,128)(2,1)S(1)}, bf16[2,96,1024]{2,1,0:T(8,128)(2,1)}, u32[]{:S(2)}) copy-start(bf16[2,96,1024]{2,1,0:T(8,128)(2,1)} %copy-done.23) | copy-start | bytes 1179652
  205.4 8.9 %copy-start.26 = (bf16[2,96,1024]{2,1,0:T(8,128)(2,1)S(1)}, bf16[2,96,1024]{2,1,0:T(8,128)(2,1)}, u32[]{:S(2)}) copy-start(bf16[2,96,1024]{2,1,0:T(8,128)(2,1)} %copy-done.25) | copy-start | bytes 1179652
  206.7 8.7 %copy-start.15 = (f32[1,192,768]{2,1,0:T(8,128)S(1)}, f32[1,192,768]{2,1,0:T(8,128)}, u32[]{:S(2)}) copy-start(f32[1,192,768]{2,1,0:T(8,128)} %get-tuple-element.137) | copy-start | bytes 1769476
  206.7 8.7 %copy-start.16 = (f32[1,192,768]{2,1,0:T(8,128)S(1)}, f32[1,192,768]{2,1,0:T(8,128)}, u32[]{:S(2)}) copy-start(f32[1,192,768]{2,1,0:T(8,128)} %get-tuple-element.138) | copy-start | bytes 1769476
  206.7 25.1 %collective-permute-start.38 = (bf16[4,2,96,1024]{3,2,1,0:T(8,128)(2,1)}, bf16[4,2,96,1024]{3,2,1,0:T(8,128)(2,1)}, u32[]{:S(2)}, u32[]{:S(2)}) collective-permute-start(bf16[4,2,96,1024]{3,2,1,0:T(8,128)(2,1)} %get-tuple-element.134), channel_id=1, source_target_pairs={{0,2},{2,0},{4,6},{6,4},{8,10},{10,8},{12,14},{14,12},{1,3},{3,1},... | collective-permute-start | bytes 4718600 | tf_op jit(solution)/shard_map/ppermute | solution.py:133
  216.5 3.3 %collective-permute-start.35 = (bf16[2,48,1792]{2,1,0:T(8,128)(2,1)S(1)}, bf16[2,48,1792]{2,1,0:T(8,128)(2,1)}, u32[]{:S(2)}, u32[]{:S(2)}) collective-permute-start(bf16[2,48,1792]{2,1,0:T(8,128)(2,1)S(1)} %get-tuple-element.152), channel_id=1, source_target_pairs={{0,2},{2,0},{4,6},{6,4},{8,10},{10,8},{12,14},{14,12},{1,3},{3,1},... | collective-permute-start | bytes 1032200 | tf_op jit(solution)/shard_map/ppermute | solution.py:133
  218.8 13.1 %collective-permute-start.39 = (bf16[4,2,96,1024]{3,2,1,0:T(8,128)(2,1)}, bf16[4,2,96,1024]{3,2,1,0:T(8,128)(2,1)}, u32[]{:S(2)}, u32[]{:S(2)}) collective-permute-start(bf16[4,2,96,1024]{3,2,1,0:T(8,128)(2,1)} %get-tuple-element.132), channel_id=1, source_target_pairs={{0,2},{2,0},{4,6},{6,4},{8,10},{10,8},{12,14},{14,12},{1,3},{3,1},... | collective-permute-start | bytes 4718600 | tf_op jit(solution)/shard_map/ppermute | solution.py:133
  219.8 2.7 copy-start.11
  221.2 2.6 copy-start.4
  221.2 9.6 %collective-permute-start.36 = (bf16[48,3584]{1,0:T(8,128)(2,1)S(1)}, bf16[48,3584]{1,0:T(8,128)(2,1)S(1)}, u32[]{:S(2)}, u32[]{:S(2)}) collective-permute-start(bf16[48,3584]{1,0:T(8,128)(2,1)S(1)} %get-tuple-element.150), channel_id=1, source_target_pairs={{0,1},{1,0},{2,3},{3,2},{4,5},{5,4},{6,7},{7,6},{8,9},{9,8},{10,11... | collective-permute-start | bytes 1032200 | tf_op jit(solution)/shard_map/ppermute | solution.py:320
  272.6 4.0 %copy-start.1 = (bf16[1,48,7168]{2,1,0:T(8,128)(2,1)S(1)}, bf16[1,48,7168]{2,1,0:T(8,128)(2,1)}, u32[]{:S(2)}) copy-start(bf16[1,48,7168]{2,1,0:T(8,128)(2,1)} %param.8) | copy-start | bytes 2064388
  (12 other events, 17.8 us)
Sparse Core Ops, SparseCore 0:
  200.3 45.2 all-gather.6
  247.3 23.9 all-gather.4

commit v10 on v9

--- a/solution.py
+++ b/solution.py
@@ -11,8 +11,8 @@
 WIRE = jnp.float16
 LARGEST_TOKEN, LARGEST_WEIGHT = 6.0, 0.0625
 VMEM_LIMIT = 48 * 2**20
-LAST_SHARES = (2, 1)
-SHARES = (4, 3)
+NO_COST = pl.CostEstimate(flops=0, bytes_accessed=0, transcendentals=0)
+SHARES = (5, 2)
 
 
 def forward_kernel(scale, place_ref, *refs):
@@ -20,7 +20,11 @@
     blocks, _, rows, width = out_ref.shape
     for which in range(2):
         product = sum(
-            jnp.dot(rows_ref[...], weight_ref[...], preferred_element_type=jnp.float32)
+            jnp.dot(
+                rows_ref[...],
+                weight_ref[...].reshape(weight_ref.shape[-2:]),
+                preferred_element_type=jnp.float32,
+            )
             for rows_ref, weight_ref in zip(tokens, weights[which::2])
         )
         out_ref[:, which] = (scale * product).reshape(blocks, rows, width)
@@ -34,7 +38,10 @@
     in_specs += [
         pl.BlockSpec((depth, tile), lambda j, place: (0, place[0] + start // tile + j))
     ] * 2
-    in_specs += [pl.BlockSpec((depth, tile), lambda j, place: (0, j))] * (2 * far)
+    in_specs += [
+        pl.BlockSpec((1, depth, tile), lambda j, place, which=which: (which, 0, j))
+        for which in range(2 * far)
+    ]
     return pl.pallas_call(
         functools.partial(forward_kernel, scale),
         out_shape=jax.ShapeDtypeStruct((blocks, 2, rows, width), jnp.float32),
@@ -45,11 +52,7 @@
             out_specs=pl.BlockSpec((blocks, 2, rows, tile), lambda j, place: (0, 0, 0, j)),
         ),
         compiler_params=pltpu.CompilerParams(vmem_limit_bytes=VMEM_LIMIT),
-        cost_estimate=pl.CostEstimate(
-            flops=4 * (far + 1) * total * depth * width,
-            bytes_accessed=(far + 1) * (4 * width + 2 * total) * depth + 8 * total * width,
-            transcendentals=0,
-        ),
+        cost_estimate=NO_COST,
     )(place, *tokens, *weights)
 
 
@@ -88,11 +91,7 @@
         ),
         input_output_aliases={2 + len(acts) + i: i for i in range(len(totals))},
         compiler_params=pltpu.CompilerParams(vmem_limit_bytes=VMEM_LIMIT),
-        cost_estimate=pl.CostEstimate(
-            flops=4 * cores * total * depth * width,
-            bytes_accessed=cores * (8 * depth + 4 * total) * width + 2 * total * depth,
-            transcendentals=0,
-        ),
+        cost_estimate=NO_COST,
     )(place, features, *acts, *totals)
 
 
@@ -157,10 +156,10 @@
     def exchange_weights(k, after):
         _, start, width = pieces[k]
         first = part * half + (1 - core) * share + start
-        return [
-            send(tie(columns_of(weight, first, width), after), pairs)
-            for weight in (gate_weight, up_weight)
+        chosen = [
+            columns_of(weight, first, width) for weight in tie((gate_weight, up_weight), after)
         ]
+        return send(jnp.stack(chosen), pairs)
 
     mine = tokens[0]
     over_row = lax.ppermute(mine, "row", swap)
@@ -178,15 +177,18 @@
     def own_features(tokens, k, after):
         _, start, width = pieces[k]
         tokens = tie(tokens, after).reshape(-1, depth)
-        weights = (gate_weight, up_weight)
-        common = (weights, start, width, tile, line, scale)
-        theirs = send(forward(other_tile, [tokens], *common).astype(WIRE), pairs)
-        return forward(own_tile, [tie(tokens, theirs[:0])], *common), theirs
+        common = ((gate_weight, up_weight), start, width, tile, line, scale)
+        payload = forward(other_tile, [tokens], *common).astype(WIRE)
+
+        def own(after):
+            return forward(own_tile, [tie(tokens, payload, after)], *common)
+
+        return payload, own
 
     def all_features(tokens, k, after):
         _, start, width = pieces[k]
         tokens = [value.reshape(-1, depth) for value in tie(tokens, after)]
-        weights = (gate_weight, up_weight, *far_weights)
+        weights = (gate_weight, up_weight, far_weights, far_weights)
         return forward(own_tile, tokens, weights, start, width, tile, line, scale), None
 
     def take(terms, block):
@@ -194,28 +196,15 @@
         return own[block] if theirs is None else own[block] + wide(theirs[block])
 
     features = [arrange(by(row == 0, mine, over_row, 1))]
-    terms = own_features(features[0], 0, ())
+    theirs, own = own_features(features[0], 0, ())
+    terms = (own((over_depth, over_both)), send(theirs, pairs))
     payload = take(terms, 3).astype(WIRE)
     in_1 = send(payload, inward)
 
     over_depth, over_both = tie((over_depth, over_both), payload)
     features.append(arrange(by(row == 0, over_depth, over_both, 1)))
-    far_weights = exchange_weights(2, in_1)
-    far_features = [send(tie(value, in_1), pairs) for value in features]
-
-    mine_cotangent, cotangent = tie((grad_hidden[0], grad_hidden[0]), in_1)
-    cotangent = jnp.stack(
-        [
-            columns_of(mine_cotangent, part * half, half),
-            lax.ppermute(columns_of(cotangent, (1 - part) * half, half), "depth", swap),
-        ]
-    )
-    cotangent = by(
-        core == 0,
-        columns_of(cotangent, core * share, share),
-        send(columns_of(cotangent, (1 - core) * share, share), pairs),
-        1,
-    )
+    theirs, own = own_features(features[1], 1, ())
+    terms = tie(terms, theirs)
 
     def activate(k, summed):
         batches, start, width = pieces[k]
@@ -242,75 +231,89 @@
         )
         return blocks, send(blocks, pairs)
 
-    near_features = [tie(value, in_1) for value in features]
-    turned, turned_in_place = [
-        jnp.concatenate([value.reshape(-1, depth) for value in values]).T
-        for values in (
-            near_features,
-            [jnp.where(at_far, value[::-1], value) for value in near_features],
-        )
-    ]
-
-    def finish(gathered, totals, start):
-        own, other = [value for value, _ in gathered], [value for _, value in gathered]
-        for values, owner in ((own, core), (other, 1 - core)):
-            where = (owner * (share // tile)).astype(jnp.int32).reshape(1)
-            values = [value[:, None] for value in values]
-            totals = gradient(where, turned, values, totals, half, start, tile)
-        return totals
-
-    hidden, totals, waiting = ([], []), (), []
+    turned = jnp.concatenate([tie(value, in_1).reshape(-1, depth) for value in features]).T
+
+    def add_gradients(acts, owner, totals, start):
+        where = (owner * (share // tile)).astype(jnp.int32).reshape(1)
+        acts = [value[:, None] for value in acts]
+        return gradient(where, turned, acts, totals, half, start, tile)
+
+    hidden, totals, merged, products = ([], []), (), [], {}
     act = hops = None
-    for k in range(-1, last):
-        gathering = act is not None
+    for k in range(-1, last + 1):
+        adding, gathering = k < last, act is not None
         if gathering:
             side_1, centre_1 = send(act, side), send(act, centre)
         if hops is not None:
-            waiting.append(merge(*hops))
-            terms = tie(terms, waiting[-1][0])
-        centre_2 = send(add(take(terms, 3), in_1).astype(WIRE), centre)
-        in_2 = send(take(tie(terms, in_1), 2).astype(WIRE), inward)
-        arrived = ()
+            merged.append(merge(*hops))
+            if adding:
+                terms = tie(terms, merged[-1][0])
+            elif last > 1:
+                side_1, centre_1 = tie((side_1, centre_1), merged[-1][0])
+        before = ()
+        if adding:
+            far, near = add(take(terms, 3), in_1).astype(WIRE), take(tie(terms, in_1), 2)
+            near = near.astype(WIRE)
+            centre_2, in_2 = send(far, centre), send(near, inward)
+            before = (in_1,)
         if gathering:
-            side_1, centre_1 = tie((side_1, centre_1), in_1)
+            side_1, centre_1 = tie((side_1, centre_1), before)
             out_2, share_2 = send(centre_1, outward), send(side_1, centre)
-            arrived = (side_1, centre_1)
-        following = None
-        if k + 2 <= last:
-            if k < 0:
-                following = own_features(features[1], 1, in_1)
-            else:
-                tokens = [jnp.stack(values, axis=1) for values in (features, far_features)]
-                following = all_features(tokens, k + 2, in_1)
-        terms = tie(terms, arrived, following)
-        near = add(take(terms, 2), in_2).astype(WIRE)
-        swapped = jnp.where(at_end, take(terms, 1), add(take(terms, 0), centre_2)).astype(WIRE)
-        centre_3, side_3 = send(near, centre), send(swapped, side)
-        if following is not None:
-            in_1 = send(take(tie(following, near, swapped), 3).astype(WIRE), inward)
-        arrived = ()
+        if k < 0:
+            products[1] = (own((far, near)), send(theirs, pairs))
+            cotangent = tie(grad_hidden[0], far, near)
+            theirs = lax.ppermute(columns_of(cotangent, (1 - part) * half, half), "depth", swap)
+            cotangent = jnp.stack([columns_of(cotangent, part * half, half), theirs])
+            terms = tie(terms, products[1][0], theirs)
+        if k == 0:
+            products[2] = all_features(tokens, 2, (side_1, centre_1))
+            terms = tie(terms, products[2])
+        if not adding:
+            own_acts, other_acts = zip(*merged)
+            totals = add_gradients(own_acts, core, (), pieces[0][1])
+            share_2 = tie(share_2, totals)
+        before = ()
+        if adding:
+            if gathering:
+                terms = tie(terms, side_1, centre_1)
+            near = add(take(terms, 2), in_2).astype(WIRE)
+            swapped = jnp.where(at_end, take(terms, 1), add(take(terms, 0), centre_2))
+            swapped = swapped.astype(WIRE)
+            centre_3, side_3 = send(near, centre), send(swapped, side)
+            if k + 2 <= last:
+                payload = take(tie(products[k + 2], near, swapped), 3).astype(WIRE)
+                in_1 = send(payload, inward)
+            before = (in_2, centre_2)
+        if k < 0:
+            cotangent = tie(cotangent, near, swapped)
+            cotangent = by(
+                core == 0,
+                columns_of(cotangent, core * share, share),
+                send(columns_of(cotangent, (1 - core) * share, share), pairs),
+                1,
+            )
+            far_weights = exchange_weights(2, (near, swapped))
+            tokens = jnp.stack(tie(features, near, swapped), axis=1)
+            tokens = (tokens, send(tokens, pairs))
+            terms = tie(terms, turned)
         if gathering:
-            out_2, share_2 = tie((out_2, share_2), in_2, centre_2)
+            out_2, share_2 = tie((out_2, share_2), before)
             out_3 = send(share_2, outward)
-            arrived = (out_2, share_2)
-        terms = tie(terms, arrived)
-        own = jnp.where(at_end, take(terms, 0), take(terms, 1))
-        ready = activate(k + 1, add(own, side_3, centre_3))
-        if gathering:
-            hops = tie((act, side_1, centre_1, out_2, share_2, out_3), ready)
-        act, terms = ready, following
-
-    start, width = pieces[last][1:]
-    gathered = []
-    for begin, count in cut(width // tile, LAST_SHARES):
-        chosen = act[:, :, begin * tile : (begin + count) * tile]
-        chosen = lax.all_gather(tie(chosen, out_3), "col", axis=0)
-        gathered.append((start + begin * tile, chosen.reshape(line, 2, *chosen.shape[1:])))
-    waiting.append(merge(*hops))
-    totals = finish(waiting, totals, pieces[0][1])
-    places = jnp.array([0, share // tile], jnp.int32)
-    for start, acts in gathered:
-        totals = gradient(places, turned_in_place, [acts], totals, half, start, tile)
+        if not adding:
+            totals = add_gradients(other_acts, 1 - core, totals, pieces[0][1])
+            out_3 = tie(out_3, totals)
+        if adding:
+            if gathering:
+                terms = tie(terms, out_2, share_2)
+            own = jnp.where(at_end, take(terms, 0), take(terms, 1))
+            ready = activate(k + 1, add(own, side_3, centre_3))
+            if gathering:
+                hops = tie((act, side_1, centre_1, out_2, share_2, out_3), ready)
+            act, terms = ready, products.get(k + 2)
+        else:
+            own_acts, other_acts = merge(act, side_1, centre_1, out_2, share_2, out_3)
+    totals = add_gradients([own_acts], core, totals, pieces[last][1])
+    totals = add_gradients([other_acts], 1 - core, totals, pieces[last][1])
 
     hidden = jnp.stack([jnp.concatenate(parts, axis=1) for parts in hidden])
     hidden = hidden.reshape(2, 2, slab, share)

time: 285 us -> 276 us (0.968)
  waiting for transfers between devices: 95.7 us -> 67.8 us
  starting transfers between devices: 71.7 us -> 91.2 us
  between operations: 14.9 us -> 1.38 us
  other arithmetic: 35 us -> 44.5 us
    ppermute x35 -> x39, waiting for transfers between devices: 55.3 us -> 31.2 us  [send(): return lax.ppermute(value, 'col', route)]
    all_gather x2 -> x0, waiting for transfers between devices: 23.8 us -> none  [local(): chosen = lax.all_gather(tie(chosen, out_3), 'col', axis=0)]
    ppermute x35 -> x39, starting transfers between devices: 65.4 us -> 86.1 us  [send(): return lax.ppermute(value, 'col', route)]
    ppermute x1, waiting for transfers between devices: 0.01 us -> 9.28 us  [local(): over_depth = lax.ppermute(mine, 'depth', swap)]
    ppermute x1, waiting for transfers between devices: 1.08 us -> 9.78 us  [local(): hidden = by(part == 0, hidden[0], lax.ppermute(hidden[1], 'depth', swap), 1)]
    convert_element_type x13, other arithmetic: 11.6 us -> 18.6 us  [the longest x3 6.31 us: local(): swapped = swapped.astype(WIRE)]
    dynamic_slice x3 -> x1, local copies, waits for them, and re-layouts: 5.36 us -> 0.05 us  [columns_of(): return lax.dynamic_slice_in_dim(array, start, width, array.ndim - 1)]
    ppermute x1, waiting for transfers between devices: 3.14 us -> 8.43 us  [local(): over_both = lax.ppermute(over_row, 'depth', swap)]
  transfers between devices with their start and end apart: 42 -> 44, of which waited for: 15 -> 14; matrix products, arithmetic and copies ran while one was open for 15% -> 16% of each run, Pallas kernels for 15% -> 15%
where the time goes in v10:
time: 276 us; the launch traced here: 273 us
  starting transfers between devices  91.2 us (33%)
  waiting for transfers between devices  67.8 us (25%)
  Pallas kernels  52.3 us (19%)
  other arithmetic  44.5 us (16%)
  local copies, waits for them, and re-layouts  16 us (6%)
    ppermute x39, starting transfers between devices, send(): return lax.ppermute(value, 'col', route)  86.1 us
    ppermute x39, waiting for transfers between devices, send(): return lax.ppermute(value, 'col', route)  31.2 us
    pallas_call x5, Pallas kernels, forward(): pl.pallas_call(functools.partial(forward_kernel, scale), out_shape=jax.Sh...  28.4 us
    pallas_call x4, Pallas kernels, gradient(): pl.pallas_call(functools.partial(gradient_kernel, len(acts)), out_shape=(...  23.9 us
    ppermute x1, waiting for transfers between devices, local(): hidden = by(part == 0, hidden[0], lax.ppermute(hidden[1], 'depth', swap), 1)  9.78 us
    ppermute x1, waiting for transfers between devices, local(): over_depth = lax.ppermute(mine, 'depth', swap)  9.28 us
    ppermute x1, waiting for transfers between devices, local(): over_row = lax.ppermute(mine, 'row', swap)  9.05 us
    ppermute x1, waiting for transfers between devices, local(): over_both = lax.ppermute(over_row, 'depth', swap)  8.43 us
  transfers between devices with their start and end apart: 44, of which 14 were waited for; matrix products, arithmetic and copies ran while one was open for 16% of the time, Pallas kernels for 15%

profile of v10, /device:TPU:1, one launch (start us, length us, event | category | flops | bytes accessed | tf_op | source)
XLA Modules:
  0.0 273.2 jit_solution(9632779330231918130)
XLA Ops:
  0.6 2.1 collective-permute-start
  2.7 9.1 %collective-permute-done = bf16[384,512]{1,0:T(8,128)(2,1)S(1)} collective-permute-done((bf16[384,512]{1,0:T(8,128)(2,1)}, bf16[384,512]{1,0:T(8,128)(2,1)S(1)}, u32[]{:S(2)}, u32[]{:S(2)}) %collective-permute-start) | collective-permute-done | bytes 393248 | tf_op jit(solution)/shard_map/ppermute | solution.py:165
  11.8 1.4 maximum_select_fusion
  13.3 5.6 %shard_map.67 = f32[4,2,96,1280]{3,2,1,0:T(8,128)S(1)} custom-call(s32[1]{0:T(128)} %bitcast.5.place_ref, bf16[384,1024]{1,0:T(8,128)(2,1)S(1)} %bitcast.187, bf16[1024,7168]{1,0:T(8,128)(2,1)} %refs_2_.9, bf16[1024,7168]{1,0:T(8,128)(2,1)} %refs_3_.1), custom_call_target="tpu_custom_call" | custom-call | tf_op jit(solution)/shard_map/pallas_call | solution.py:45
  18.9 1.5 convert_element_type.197
  21.7 1.5 collective-permute-start.1
  23.2 9.3 %collective-permute-done.1 = bf16[384,512]{1,0:T(8,128)(2,1)S(1)} collective-permute-done((bf16[384,512]{1,0:T(8,128)(2,1)S(1)}, bf16[384,512]{1,0:T(8,128)(2,1)S(1)}, u32[]{:S(2)}, u32[]{:S(2)}) %collective-permute-start.1) | collective-permute-done | bytes 393248 | tf_op jit(solution)/shard_map/ppermute | solution.py:166
  32.5 8.4 %collective-permute-done.2 = bf16[384,512]{1,0:T(8,128)(2,1)S(1)} collective-permute-done((bf16[384,512]{1,0:T(8,128)(2,1)S(1)}, bf16[384,512]{1,0:T(8,128)(2,1)S(1)}, u32[]{:S(2)}, u32[]{:S(2)}) %collective-permute-start.2) | collective-permute-done | bytes 393248 | tf_op jit(solution)/shard_map/ppermute | solution.py:167
  40.9 5.5 %shard_map.68 = f32[4,2,96,1280]{3,2,1,0:T(8,128)S(1)} custom-call(s32[1]{0:T(128)} %bitcast.place_ref, bf16[384,1024]{1,0:T(8,128)(2,1)S(1)} %bitcast.188, bf16[1024,7168]{1,0:T(8,128)(2,1)} %refs_2_.9, bf16[1024,7168]{1,0:T(8,128)(2,1)} %refs_3_.1), custom_call_target="tpu_custom_call" | custom-call | tf_op jit(solution)/shard_map/pallas_call | solution.py:45
  46.5 1.9 copy-done
  48.4 1.9 fusion.34
  50.3 3.4 %collective-permute-start.4 = (f16[2,96,1280]{2,1,0:T(8,128)(2,1)}, f16[2,96,1280]{2,1,0:T(8,128)(2,1)S(1)}, u32[]{:S(2)}, u32[]{:S(2)}) collective-permute-start(f16[2,96,1280]{2,1,0:T(8,128)(2,1)} %fusion.34), channel_id=1, source_target_pairs={{0,4},{2,6},{12,8},{14,10},{1,5},{3,7},{13,9},{15,11},{16,20},{18,... | collective-permute-start | bytes 1474568 | tf_op jit(solution)/shard_map/ppermute | solution.py:132
  54.2 5.6 %shard_map.69 = f32[4,2,96,1280]{3,2,1,0:T(8,128)S(1)} custom-call(s32[1]{0:T(128)} %bitcast.5.place_ref, bf16[384,1024]{1,0:T(8,128)(2,1)S(1)} %bitcast.191, bf16[1024,7168]{1,0:T(8,128)(2,1)} %refs_2_.9, bf16[1024,7168]{1,0:T(8,128)(2,1)} %refs_3_.1), custom_call_target="tpu_custom_call" | custom-call | tf_op jit(solution)/shard_map/pallas_call | solution.py:45
  59.7 1.5 convert_element_type.201
  61.3 2.5 collective-permute-done.4
  63.8 2.0 fusion.31
  65.7 2.0 fusion.14
  69.8 2.0 collective-permute-start.14
  71.8 1.4 collective-permute-start.6
  73.2 6.6 %collective-permute-start.8 = (f16[2,96,1280]{2,1,0:T(8,128)(2,1)}, f16[2,96,1280]{2,1,0:T(8,128)(2,1)}, u32[]{:S(2)}, u32[]{:S(2)}) collective-permute-start(f16[2,96,1280]{2,1,0:T(8,128)(2,1)} %fusion.31), channel_id=1, source_target_pairs={{0,4},{2,6},{12,8},{14,10},{1,5},{3,7},{13,9},{15,11},{16,20},{18,... | collective-permute-start | bytes 1474568 | tf_op jit(solution)/shard_map/ppermute | solution.py:132
  82.2 1.5 maximum_bitcast_fusion.features_ref
  83.7 5.7 %shard_map.70 = f32[4,2,96,1280]{3,2,1,0:T(8,128)S(1)} custom-call(s32[1]{0:T(128)} %bitcast.place_ref, bf16[384,1024]{1,0:T(8,128)(2,1)S(1)} %bitcast.193, bf16[1024,7168]{1,0:T(8,128)(2,1)} %refs_2_.9, bf16[1024,7168]{1,0:T(8,128)(2,1)} %refs_3_.1), custom_call_target="tpu_custom_call" | custom-call | tf_op jit(solution)/shard_map/pallas_call | solution.py:45
  90.5 2.1 fusion.11
  92.6 1.4 collective-permute-start.7
  94.7 1.4 collective-permute-start.11
  97.7 1.3 dynamic-slice_bitcast_fusion
  100.0 4.8 %collective-permute-done.7 = f16[2,96,1280]{2,1,0:T(8,128)(2,1)S(1)} collective-permute-done((f16[2,96,1280]{2,1,0:T(8,128)(2,1)S(1)}, f16[2,96,1280]{2,1,0:T(8,128)(2,1)S(1)}, u32[]{:S(2)}, u32[]{:S(2)}) %collective-permute-start.7) | collective-permute-done | bytes 491552 | tf_op jit(solution)/shard_map/ppermute | solution.py:132
  104.8 1.6 fusion.13
  107.6 4.9 %collective-permute-start.15 = (f16[2,96,1280]{2,1,0:T(8,128)(2,1)S(1)}, f16[2,96,1280]{2,1,0:T(8,128)(2,1)S(1)}, u32[]{:S(2)}, u32[]{:S(2)}) collective-permute-start(f16[2,96,1280]{2,1,0:T(8,128)(2,1)S(1)} %fusion.32), channel_id=1, source_target_pairs={{0,4},{2,6},{12,8},{14,10},{1,5},{3,7},{13,9},{15,11},{16,20},{18,... | collective-permute-start | bytes 1474568 | tf_op jit(solution)/shard_map/ppermute | solution.py:132
  115.1 6.0 %collective-permute-done.15 = f16[2,96,1280]{2,1,0:T(8,128)(2,1)S(1)} collective-permute-done((f16[2,96,1280]{2,1,0:T(8,128)(2,1)S(1)}, f16[2,96,1280]{2,1,0:T(8,128)(2,1)S(1)}, u32[]{:S(2)}, u32[]{:S(2)}) %collective-permute-start.15) | collective-permute-done | bytes 491552 | tf_op jit(solution)/shard_map/ppermute | solution.py:132
  124.1 5.5 %collective-permute-start.19 = (f16[2,96,1280]{2,1,0:T(8,128)(2,1)S(1)}, f16[2,96,1280]{2,1,0:T(8,128)(2,1)S(1)}, u32[]{:S(2)}, u32[]{:S(2)}) collective-permute-start(f16[2,96,1280]{2,1,0:T(8,128)(2,1)S(1)} %fusion.33), channel_id=1, source_target_pairs={{0,4},{2,6},{12,8},{14,10},{1,5},{3,7},{13,9},{15,11},{16,20},{18,... | collective-permute-start | bytes 1474568 | tf_op jit(solution)/shard_map/ppermute | solution.py:132
  129.7 1.9 collective-permute-done.12
  133.9 1.3 copy-done.3
  135.2 1.6 copy-done.4
  136.8 6.0 %shard_map.71 = f32[4,2,192,512]{3,2,1,0:T(8,128)} custom-call(s32[1]{0:T(128)} %bitcast.place_ref, bf16[768,1024]{1,0:T(8,128)(2,1)S(1)} %bitcast.195, bf16[768,1024]{1,0:T(8,128)(2,1)S(1)} %bitcast.196, bf16[1024,7168]{1,0:T(8,128)(2,1)} %refs_2_.9, bf16[1024,7168]{1,0:T(8,128)(2,1)} %refs_3_.1, bf16[2,1024,512]{2,1,0:T(8,128)(2,1)S(1)} %copy-done.4, ...), custom_call_target="tpu_custom_call" | custom-call | tf_op jit(solution)/shard_map/pallas_call | solution.py:45
  142.8 2.0 fusion.6
  144.8 3.7 %collective-permute-start.22 = (f16[2,96,1280]{2,1,0:T(8,128)(2,1)S(1)}, f16[2,96,1280]{2,1,0:T(8,128)(2,1)S(1)}, u32[]{:S(2)}, u32[]{:S(2)}) collective-permute-start(f16[2,96,1280]{2,1,0:T(8,128)(2,1)S(1)} %get-tuple-element.149), channel_id=1, source_target_pairs={{0,4},{2,6},{12,8},{14,10},{4,0},{6,2},{8,12},{10,14},{1,5},{3,7},... | collective-permute-start | bytes 1474568 | tf_op jit(solution)/shard_map/ppermute | solution.py:132
  150.6 4.7 %collective-permute-start.26 = (f16[2,192,512]{2,1,0:T(8,128)(2,1)S(1)}, f16[2,192,512]{2,1,0:T(8,128)(2,1)S(1)}, u32[]{:S(2)}, u32[]{:S(2)}) collective-permute-start(f16[2,192,512]{2,1,0:T(8,128)(2,1)S(1)} %fusion.40), channel_id=1, source_target_pairs={{0,4},{2,6},{12,8},{14,10},{1,5},{3,7},{13,9},{15,11},{16,20},{18,... | collective-permute-start | bytes 1179656 | tf_op jit(solution)/shard_map/ppermute | solution.py:132
  155.3 1.5 fusion.8
  158.6 1.5 collective-permute-start.25
  160.1 4.9 %collective-permute-start.24 = (bf16[2,96,1280]{2,1,0:T(8,128)(2,1)}, bf16[2,96,1280]{2,1,0:T(8,128)(2,1)}, u32[]{:S(2)}, u32[]{:S(2)}) collective-permute-start(bf16[2,96,1280]{2,1,0:T(8,128)(2,1)} %pad_maximum_fusion.7), channel_id=1, source_target_pairs={{0,4},{2,6},{12,8},{14,10},{4,0},{6,2},{8,12},{10,14},{1,5},{3,7},... | collective-permute-start | bytes 1474568 | tf_op jit(solution)/shard_map/ppermute | solution.py:132
  165.2 1.6 fusion.44
  168.5 1.4 collective-permute-start.30
  170.0 3.7 %collective-permute-start.29 = (f16[2,192,512]{2,1,0:T(8,128)(2,1)}, f16[2,192,512]{2,1,0:T(8,128)(2,1)}, u32[]{:S(2)}, u32[]{:S(2)}) collective-permute-start(f16[2,192,512]{2,1,0:T(8,128)(2,1)} %fusion.41), channel_id=1, source_target_pairs={{0,4},{2,6},{12,8},{14,10},{1,5},{3,7},{13,9},{15,11},{16,20},{18,... | collective-permute-start | bytes 1179656 | tf_op jit(solution)/shard_map/ppermute | solution.py:132
  173.7 2.9 %collective-permute-done.24 = bf16[2,96,1280]{2,1,0:T(8,128)(2,1)} collective-permute-done((bf16[2,96,1280]{2,1,0:T(8,128)(2,1)}, bf16[2,96,1280]{2,1,0:T(8,128)(2,1)}, u32[]{:S(2)}, u32[]{:S(2)}) %collective-permute-start.24) | collective-permute-done | bytes 491552 | tf_op jit(solution)/shard_map/ppermute | solution.py:132
  178.6 2.6 collective-permute-done.29
  181.2 2.2 fusion.17
  183.4 2.3 collective-permute-start.31
  188.2 13.6 %collective-permute-start.41 = (bf16[4,2,96,1280]{3,2,1,0:T(8,128)(2,1)}, bf16[4,2,96,1280]{3,2,1,0:T(8,128)(2,1)}, u32[]{:S(2)}, u32[]{:S(2)}) collective-permute-start(bf16[4,2,96,1280]{3,2,1,0:T(8,128)(2,1)} %get-tuple-element.158), channel_id=1, source_target_pairs={{0,2},{2,0},{4,6},{6,4},{8,10},{10,8},{12,14},{14,12},{1,3},{3,1},... | collective-permute-start | bytes 5898248 | tf_op jit(solution)/shard_map/ppermute | solution.py:132
  204.4 1.4 collective-permute-start.36
  205.9 3.3 %collective-permute-start.35 = (bf16[2,192,512]{2,1,0:T(8,128)(2,1)}, bf16[2,192,512]{2,1,0:T(8,128)(2,1)}, u32[]{:S(2)}, u32[]{:S(2)}) collective-permute-start(bf16[2,192,512]{2,1,0:T(8,128)(2,1)} %pad_maximum_fusion.8), channel_id=1, source_target_pairs={{0,4},{2,6},{12,8},{14,10},{4,0},{6,2},{8,12},{10,14},{1,5},{3,7},... | collective-permute-start | bytes 1179656 | tf_op jit(solution)/shard_map/ppermute | solution.py:132
  209.3 7.1 %collective-permute-done.37 = bf16[2,96,1280]{2,1,0:T(8,128)(2,1)S(1)} collective-permute-done((bf16[2,96,1280]{2,1,0:T(8,128)(2,1)S(1)}, bf16[2,96,1280]{2,1,0:T(8,128)(2,1)S(1)}, u32[]{:S(2)}, u32[]{:S(2)}) %collective-permute-start.37) | collective-permute-done | bytes 491552 | tf_op jit(solution)/shard_map/ppermute | solution.py:132
  217.8 2.2 fusion.43
  222.3 2.6 collective-permute-done.35
  227.0 1.5 maximum_select_fusion.3
  228.5 1.5 copy-done.5
  230.0 7.0 %shard_map.72 = (f32[1024,3584]{1,0:T(8,128)}, f32[1024,3584]{1,0:T(8,128)}) custom-call(s32[1]{0:T(128)} %bitcast.73.place_ref, bf16[1024,768]{1,0:T(8,128)(2,1)S(1)} %maximum_bitcast_fusion.features_ref, bf16[4,1,2,96,1280]{4,3,2,1,0:T(8,128)(2,1)S(1)} %get-tuple-element.157.refs_0_, bf16[4,1,2,96,1280]{4,3,2,1,0:T(8,128)(2,1)S(1)} %copy-done.5), custom_call_target="tpu_custom_call" | custom-call | tf_op jit(solution)/shard_map/pallas_call | solution.py:83
  240.0 9.0 %shard_map.73 = (f32[1024,3584]{1,0:T(8,128)}, f32[1024,3584]{1,0:T(8,128)}) custom-call(s32[1]{0:T(128)} %bitcast.62.place_ref, bf16[1024,768]{1,0:T(8,128)(2,1)S(1)} %maximum_bitcast_fusion.features_ref, bf16[4,1,2,96,1280]{4,3,2,1,0:T(8,128)(2,1)} %bitcast.80.refs_0_, ...), custom_call_target="tpu_custom_call", output_to_operand_aliasing={{0}: (4, {}), {1}: (5, {})} | custom-call | tf_op jit(solution)/shard_map/pallas_call | solution.py:83
  249.0 1.4 fusion.42
  250.5 2.0 collective-permute-start.43
  253.4 9.8 %collective-permute-done.34 = bf16[48,3584]{1,0:T(8,128)(2,1)} collective-permute-done((bf16[48,3584]{1,0:T(8,128)(2,1)}, bf16[48,3584]{1,0:T(8,128)(2,1)}, u32[]{:S(2)}, u32[]{:S(2)}) %collective-permute-start.34) | collective-permute-done | bytes 344096 | tf_op jit(solution)/shard_map/ppermute | solution.py:323
  263.2 2.1 maximum_select_fusion.4
  265.3 3.4 %shard_map.74 = (f32[1024,3584]{1,0:T(8,128)}, f32[1024,3584]{1,0:T(8,128)}) custom-call(s32[1]{0:T(128)} %bitcast.73.place_ref, bf16[1024,768]{1,0:T(8,128)(2,1)S(1)} %maximum_bitcast_fusion.features_ref, bf16[4,1,2,192,512]{4,3,2,1,0:T(8,128)(2,1)S(1)} %get-tuple-element.159.refs_0_, ...), custom_call_target="tpu_custom_call", output_to_operand_aliasing={{0}: (3, {}), {1}: (4, {})} | custom-call | tf_op jit(solution)/shard_map/pallas_call | solution.py:83
  268.7 4.4 %shard_map.75 = (f32[1024,3584]{1,0:T(8,128)}, f32[1024,3584]{1,0:T(8,128)}) custom-call(s32[1]{0:T(128)} %bitcast.62.place_ref, bf16[1024,768]{1,0:T(8,128)(2,1)S(1)} %maximum_bitcast_fusion.features_ref, bf16[4,1,2,192,512]{4,3,2,1,0:T(8,128)(2,1)} %bitcast.83.refs_0_, ...), custom_call_target="tpu_custom_call", output_to_operand_aliasing={{0}: (3, {}), {1}: (4, {})} | custom-call | tf_op jit(solution)/shard_map/pallas_call | solution.py:83
  (131 shorter events, 42.1 us)
Async XLA Ops:
  0.6 11.2 %collective-permute-start = (bf16[384,512]{1,0:T(8,128)(2,1)}, bf16[384,512]{1,0:T(8,128)(2,1)S(1)}, u32[]{:S(2)}, u32[]{:S(2)}) collective-permute-start(bf16[384,512]{1,0:T(8,128)(2,1)} %bitcast.202), channel_id=1, source_target_pairs={{0,16},{16,0},{1,17},{17,1},{2,18},{18,2},{3,19},{19,3},{4,20},{20... | collective-permute-start | bytes 1179656 | tf_op jit(solution)/shard_map/ppermute | solution.py:165
  18.9 2.7 %copy-start.17 = (bf16[1,384,512]{2,1,0:T(8,128)(2,1)S(1)}, bf16[1,384,512]{2,1,0:T(8,128)(2,1)}, u32[]{:S(2)}) copy-start(bf16[1,384,512]{2,1,0:T(8,128)(2,1)} %param.4) | copy-start | bytes 1179652
  20.4 26.0 %collective-permute-start.3 = (f16[4,2,96,1280]{3,2,1,0:T(8,128)(2,1)}, f16[4,2,96,1280]{3,2,1,0:T(8,128)(2,1)}, u32[]{:S(2)}, u32[]{:S(2)}) collective-permute-start(f16[4,2,96,1280]{3,2,1,0:T(8,128)(2,1)} %convert_element_type.197), channel_id=1, source_target_pairs={{0,2},{2,0},{4,6},{6,4},{8,10},{10,8},{12,14},{14,12},{1,3},{3,1},... | collective-permute-start | bytes 5898248 | tf_op jit(solution)/shard_map/ppermute | solution.py:132
  21.7 10.8 %collective-permute-start.1 = (bf16[384,512]{1,0:T(8,128)(2,1)S(1)}, bf16[384,512]{1,0:T(8,128)(2,1)S(1)}, u32[]{:S(2)}, u32[]{:S(2)}) collective-permute-start(bf16[384,512]{1,0:T(8,128)(2,1)S(1)} %bitcast.204), channel_id=1, source_target_pairs={{0,1},{1,0},{2,3},{3,2},{4,5},{5,4},{6,7},{7,6},{8,9},{9,8},{10,11... | collective-permute-start | bytes 1179656 | tf_op jit(solution)/shard_map/ppermute | solution.py:166
  23.2 17.7 %collective-permute-start.2 = (bf16[384,512]{1,0:T(8,128)(2,1)S(1)}, bf16[384,512]{1,0:T(8,128)(2,1)S(1)}, u32[]{:S(2)}, u32[]{:S(2)}) collective-permute-start(bf16[384,512]{1,0:T(8,128)(2,1)S(1)} %collective-permute-done), channel_id=1, source_target_pairs={{0,1},{1,0},{2,3},{3,2},{4,5},{5,4},{6,7},{7,6},{8,9},{9,8},{10,11... | collective-permute-start | bytes 1179656 | tf_op jit(solution)/shard_map/ppermute | solution.py:167
  46.5 1.9 copy-start
  50.3 13.5 %collective-permute-start.4 = (f16[2,96,1280]{2,1,0:T(8,128)(2,1)}, f16[2,96,1280]{2,1,0:T(8,128)(2,1)S(1)}, u32[]{:S(2)}, u32[]{:S(2)}) collective-permute-start(f16[2,96,1280]{2,1,0:T(8,128)(2,1)} %fusion.34), channel_id=1, source_target_pairs={{0,4},{2,6},{12,8},{14,10},{1,5},{3,7},{13,9},{15,11},{16,20},{18,... | collective-permute-start | bytes 1474568 | tf_op jit(solution)/shard_map/ppermute | solution.py:132
  59.7 4.0 %copy-start.1 = (f32[4,2,96,1280]{3,2,1,0:T(8,128)S(1)}, f32[4,2,96,1280]{3,2,1,0:T(8,128)}, u32[]{:S(2)}) copy-start(f32[4,2,96,1280]{3,2,1,0:T(8,128)} %copy-done) | copy-start | bytes 11796484
  61.2 6.5 %copy-start.16 = (bf16[1,48,7168]{2,1,0:T(8,128)(2,1)S(1)}, bf16[1,48,7168]{2,1,0:T(8,128)(2,1)}, u32[]{:S(2)}) copy-start(bf16[1,48,7168]{2,1,0:T(8,128)(2,1)} %param.7) | copy-start | bytes 2064388
  68.6 20.8 %collective-permute-start.5 = (bf16[48,3584]{1,0:T(8,128)(2,1)}, bf16[48,3584]{1,0:T(8,128)(2,1)}, u32[]{:S(2)}, u32[]{:S(2)}) collective-permute-start(bf16[48,3584]{1,0:T(8,128)(2,1)} %get-tuple-element.186), channel_id=1, source_target_pairs={{0,1},{1,0},{2,3},{3,2},{4,5},{5,4},{6,7},{7,6},{8,9},{9,8},{10,11... | collective-permute-start | bytes 1032200 | tf_op jit(solution)/shard_map/ppermute | solution.py:265
  69.8 36.6 %collective-permute-start.14 = (f16[4,2,96,1280]{3,2,1,0:T(8,128)(2,1)}, f16[4,2,96,1280]{3,2,1,0:T(8,128)(2,1)}, u32[]{:S(2)}, u32[]{:S(2)}) collective-permute-start(f16[4,2,96,1280]{3,2,1,0:T(8,128)(2,1)} %convert_element_type.201), channel_id=1, source_target_pairs={{0,2},{2,0},{4,6},{6,4},{8,10},{10,8},{12,14},{14,12},{1,3},{3,1},... | collective-permute-start | bytes 5898248 | tf_op jit(solution)/shard_map/ppermute | solution.py:132
  71.8 18.7 %collective-permute-start.6 = (f16[2,96,1280]{2,1,0:T(8,128)(2,1)}, f16[2,96,1280]{2,1,0:T(8,128)(2,1)}, u32[]{:S(2)}, u32[]{:S(2)}) collective-permute-start(f16[2,96,1280]{2,1,0:T(8,128)(2,1)} %fusion.14), channel_id=1, source_target_pairs={{4,8},{6,10},{8,4},{10,6},{5,9},{7,11},{9,5},{11,7},{20,24},{22,26... | collective-permute-start | bytes 1474568 | tf_op jit(solution)/shard_map/ppermute | solution.py:132
  73.2 17.3 %collective-permute-start.8 = (f16[2,96,1280]{2,1,0:T(8,128)(2,1)}, f16[2,96,1280]{2,1,0:T(8,128)(2,1)}, u32[]{:S(2)}, u32[]{:S(2)}) collective-permute-start(f16[2,96,1280]{2,1,0:T(8,128)(2,1)} %fusion.31), channel_id=1, source_target_pairs={{0,4},{2,6},{12,8},{14,10},{1,5},{3,7},{13,9},{15,11},{16,20},{18,... | collective-permute-start | bytes 1474568 | tf_op jit(solution)/shard_map/ppermute | solution.py:132
  83.7 6.8 %copy-start.2 = (f32[4,2,96,1280]{3,2,1,0:T(8,128)S(1)}, f32[4,2,96,1280]{3,2,1,0:T(8,128)}, u32[]{:S(2)}) copy-start(f32[4,2,96,1280]{3,2,1,0:T(8,128)} %copy-done) | copy-start | bytes 11796484
  92.6 12.1 %collective-permute-start.7 = (f16[2,96,1280]{2,1,0:T(8,128)(2,1)S(1)}, f16[2,96,1280]{2,1,0:T(8,128)(2,1)S(1)}, u32[]{:S(2)}, u32[]{:S(2)}) collective-permute-start(f16[2,96,1280]{2,1,0:T(8,128)(2,1)S(1)} %get-tuple-element.151), channel_id=1, source_target_pairs={{0,4},{2,6},{12,8},{14,10},{4,0},{6,2},{8,12},{10,14},{1,5},{3,7},... | collective-permute-start | bytes 1474568 | tf_op jit(solution)/shard_map/ppermute | solution.py:132
  94.0 10.8 %collective-permute-start.9 = (f16[2,96,1280]{2,1,0:T(8,128)(2,1)S(1)}, f16[2,96,1280]{2,1,0:T(8,128)(2,1)S(1)}, u32[]{:S(2)}, u32[]{:S(2)}) collective-permute-start(f16[2,96,1280]{2,1,0:T(8,128)(2,1)S(1)} %get-tuple-element.152), channel_id=1, source_target_pairs={{4,8},{6,10},{8,4},{10,6},{5,9},{7,11},{9,5},{11,7},{20,24},{22,26... | collective-permute-start | bytes 1474568 | tf_op jit(solution)/shard_map/ppermute | solution.py:132
  94.7 4.5 %collective-permute-start.11 = (bf16[2,48,1792]{2,1,0:T(8,128)(2,1)S(1)}, bf16[2,48,1792]{2,1,0:T(8,128)(2,1)S(1)}, u32[]{:S(2)}, u32[]{:S(2)}) collective-permute-start(bf16[2,48,1792]{2,1,0:T(8,128)(2,1)S(1)} %get-tuple-element.184), channel_id=1, source_target_pairs={{0,2},{2,0},{4,6},{6,4},{8,10},{10,8},{12,14},{14,12},{1,3},{3,1},... | collective-permute-start | bytes 1032200 | tf_op jit(solution)/shard_map/ppermute | solution.py:132
  96.3 36.0 %collective-permute-start.10 = (bf16[4,2,96,1024]{3,2,0,1:T(8,128)(2,1)S(1)}, bf16[4,2,96,1024]{3,2,0,1:T(8,128)(2,1)S(1)}, u32[]{:S(2)}, u32[]{:S(2)}) collective-permute-start(bf16[4,2,96,1024]{3,2,0,1:T(8,128)(2,1)S(1)} %pad_maximum_fusion.3), channel_id=1, source_target_pairs={{0,2},{2,0},{4,6},{6,4},{8,10},{10,8},{12,14},{14,12},{1,3},{3,1},... | collective-permute-start | bytes 4718600 | tf_op jit(solution)/shard_map/ppermute | solution.py:132
  99.2 34.7 %collective-permute-start.16 = (bf16[2,1024,512]{2,1,0:T(8,128)(2,1)S(1)}, bf16[2,1024,512]{2,1,0:T(8,128)(2,1)S(1)}, u32[]{:S(2)}, u32[]{:S(2)}) collective-permute-start(bf16[2,1024,512]{2,1,0:T(8,128)(2,1)S(1)} %pad_maximum_fusion), channel_id=1, source_target_pairs={{0,2},{2,0},{4,6},{6,4},{8,10},{10,8},{12,14},{14,12},{1,3},{3,1},... | collective-permute-start | bytes 6291464 | tf_op jit(solution)/shard_map/ppermute | solution.py:132
  99.9 12.6 %copy-start.12 = (bf16[96,1792]{1,0:T(8,128)(2,1)}, bf16[96,1792]{1,0:T(8,128)(2,1)S(1)}, u32[]{:S(2)}) copy-start(bf16[96,1792]{1,0:T(8,128)(2,1)S(1)} %get-tuple-element.182) | copy-start | bytes 1032196
  100.0 56.9 %copy-start.13 = (bf16[96,1792]{1,0:T(8,128)(2,1)}, bf16[96,1792]{1,0:T(8,128)(2,1)S(1)}, u32[]{:S(2)}) copy-start(bf16[96,1792]{1,0:T(8,128)(2,1)S(1)} %get-tuple-element.181) | copy-start | bytes 1032196
  107.6 13.5 %collective-permute-start.15 = (f16[2,96,1280]{2,1,0:T(8,128)(2,1)S(1)}, f16[2,96,1280]{2,1,0:T(8,128)(2,1)S(1)}, u32[]{:S(2)}, u32[]{:S(2)}) collective-permute-start(f16[2,96,1280]{2,1,0:T(8,128)(2,1)S(1)} %fusion.32), channel_id=1, source_target_pairs={{0,4},{2,6},{12,8},{14,10},{1,5},{3,7},{13,9},{15,11},{16,20},{18,... | collective-permute-start | bytes 1474568 | tf_op jit(solution)/shard_map/ppermute | solution.py:132
  113.6 10.6 %collective-permute-start.13 = (bf16[2,96,1280]{2,1,0:T(8,128)(2,1)S(1)}, bf16[2,96,1280]{2,1,0:T(8,128)(2,1)S(1)}, u32[]{:S(2)}, u32[]{:S(2)}) collective-permute-start(bf16[2,96,1280]{2,1,0:T(8,128)(2,1)S(1)} %pad_maximum_fusion.6), channel_id=1, source_target_pairs={{4,8},{6,10},{8,4},{10,6},{5,9},{7,11},{9,5},{11,7},{20,24},{22,26... | collective-permute-start | bytes 1474568 | tf_op jit(solution)/shard_map/ppermute | solution.py:132
  114.3 17.4 %collective-permute-start.12 = (bf16[2,96,1280]{2,1,0:T(8,128)(2,1)S(1)}, bf16[2,96,1280]{2,1,0:T(8,128)(2,1)S(1)}, u32[]{:S(2)}, u32[]{:S(2)}) collective-permute-start(bf16[2,96,1280]{2,1,0:T(8,128)(2,1)S(1)} %pad_maximum_fusion.6), channel_id=1, source_target_pairs={{0,4},{2,6},{12,8},{14,10},{4,0},{6,2},{8,12},{10,14},{1,5},{3,7},... | collective-permute-start | bytes 1474568 | tf_op jit(solution)/shard_map/ppermute | solution.py:132
  122.3 20.5 %collective-permute-start.20 = (f16[2,96,1280]{2,1,0:T(8,128)(2,1)S(1)}, f16[2,96,1280]{2,1,0:T(8,128)(2,1)S(1)}, u32[]{:S(2)}, u32[]{:S(2)}) collective-permute-start(f16[2,96,1280]{2,1,0:T(8,128)(2,1)S(1)} %fusion.2), channel_id=1, source_target_pairs={{4,8},{6,10},{8,4},{10,6},{5,9},{7,11},{9,5},{11,7},{20,24},{22,26... | collective-permute-start | bytes 1474568 | tf_op jit(solution)/shard_map/ppermute | solution.py:132
  124.1 18.6 %collective-permute-start.19 = (f16[2,96,1280]{2,1,0:T(8,128)(2,1)S(1)}, f16[2,96,1280]{2,1,0:T(8,128)(2,1)S(1)}, u32[]{:S(2)}, u32[]{:S(2)}) collective-permute-start(f16[2,96,1280]{2,1,0:T(8,128)(2,1)S(1)} %fusion.33), channel_id=1, source_target_pairs={{0,4},{2,6},{12,8},{14,10},{1,5},{3,7},{13,9},{15,11},{16,20},{18,... | collective-permute-start | bytes 1474568 | tf_op jit(solution)/shard_map/ppermute | solution.py:132
  131.6 17.6 %collective-permute-start.18 = (bf16[2,96,1280]{2,1,0:T(8,128)(2,1)S(1)}, bf16[2,96,1280]{2,1,0:T(8,128)(2,1)S(1)}, u32[]{:S(2)}, u32[]{:S(2)}) collective-permute-start(bf16[2,96,1280]{2,1,0:T(8,128)(2,1)S(1)} %collective-permute-done.12), channel_id=1, source_target_pairs={{4,8},{6,10},{8,4},{10,6},{5,9},{7,11},{9,5},{11,7},{20,24},{22,26... | collective-permute-start | bytes 1474568 | tf_op jit(solution)/shard_map/ppermute | solution.py:132
  132.3 16.9 %collective-permute-start.17 = (bf16[2,96,1280]{2,1,0:T(8,128)(2,1)S(1)}, bf16[2,96,1280]{2,1,0:T(8,128)(2,1)S(1)}, u32[]{:S(2)}, u32[]{:S(2)}) collective-permute-start(bf16[2,96,1280]{2,1,0:T(8,128)(2,1)S(1)} %collective-permute-done.13), channel_id=1, source_target_pairs={{4,0},{6,2},{8,12},{10,14},{5,1},{7,3},{9,13},{11,15},{20,16},{22,... | collective-permute-start | bytes 1474568 | tf_op jit(solution)/shard_map/ppermute | solution.py:132
  133.9 1.3 copy-start.3
  135.2 1.6 copy-start.4
  142.8 7.8 %copy-start.6 = (f32[4,2,192,512]{3,2,1,0:T(8,128)S(1)}, f32[4,2,192,512]{3,2,1,0:T(8,128)}, u32[]{:S(2)}) copy-start(f32[4,2,192,512]{3,2,1,0:T(8,128)} %shard_map.71) | copy-start | bytes 9437188
  144.8 10.4 %collective-permute-start.22 = (f16[2,96,1280]{2,1,0:T(8,128)(2,1)S(1)}, f16[2,96,1280]{2,1,0:T(8,128)(2,1)S(1)}, u32[]{:S(2)}, u32[]{:S(2)}) collective-permute-start(f16[2,96,1280]{2,1,0:T(8,128)(2,1)S(1)} %get-tuple-element.149), channel_id=1, source_target_pairs={{0,4},{2,6},{12,8},{14,10},{4,0},{6,2},{8,12},{10,14},{1,5},{3,7},... | collective-permute-start | bytes 1474568 | tf_op jit(solution)/shard_map/ppermute | solution.py:132
  148.5 6.8 %collective-permute-start.23 = (f16[2,96,1280]{2,1,0:T(8,128)(2,1)S(1)}, f16[2,96,1280]{2,1,0:T(8,128)(2,1)S(1)}, u32[]{:S(2)}, u32[]{:S(2)}) collective-permute-start(f16[2,96,1280]{2,1,0:T(8,128)(2,1)S(1)} %get-tuple-element.150), channel_id=1, source_target_pairs={{4,8},{6,10},{8,4},{10,6},{5,9},{7,11},{9,5},{11,7},{20,24},{22,26... | collective-permute-start | bytes 1474568 | tf_op jit(solution)/shard_map/ppermute | solution.py:132
  149.2 15.8 %collective-permute-start.21 = (bf16[2,96,1280]{2,1,0:T(8,128)(2,1)S(1)}, bf16[2,96,1280]{2,1,0:T(8,128)(2,1)S(1)}, u32[]{:S(2)}, u32[]{:S(2)}) collective-permute-start(bf16[2,96,1280]{2,1,0:T(8,128)(2,1)S(1)} %collective-permute-done.18), channel_id=1, source_target_pairs={{4,0},{6,2},{8,12},{10,14},{5,1},{7,3},{9,13},{11,15},{20,16},{22,... | collective-permute-start | bytes 1474568 | tf_op jit(solution)/shard_map/ppermute | solution.py:132
  150.6 16.3 %collective-permute-start.26 = (f16[2,192,512]{2,1,0:T(8,128)(2,1)S(1)}, f16[2,192,512]{2,1,0:T(8,128)(2,1)S(1)}, u32[]{:S(2)}, u32[]{:S(2)}) collective-permute-start(f16[2,192,512]{2,1,0:T(8,128)(2,1)S(1)} %fusion.40), channel_id=1, source_target_pairs={{0,4},{2,6},{12,8},{14,10},{1,5},{3,7},{13,9},{15,11},{16,20},{18,... | collective-permute-start | bytes 1179656 | tf_op jit(solution)/shard_map/ppermute | solution.py:132
  158.6 15.1 %collective-permute-start.25 = (bf16[2,96,1280]{2,1,0:T(8,128)(2,1)}, bf16[2,96,1280]{2,1,0:T(8,128)(2,1)}, u32[]{:S(2)}, u32[]{:S(2)}) collective-permute-start(bf16[2,96,1280]{2,1,0:T(8,128)(2,1)} %pad_maximum_fusion.7), channel_id=1, source_target_pairs={{4,8},{6,10},{8,4},{10,6},{5,9},{7,11},{9,5},{11,7},{20,24},{22,26... | collective-permute-start | bytes 1474568 | tf_op jit(solution)/shard_map/ppermute | solution.py:132
  160.1 16.5 %collective-permute-start.24 = (bf16[2,96,1280]{2,1,0:T(8,128)(2,1)}, bf16[2,96,1280]{2,1,0:T(8,128)(2,1)}, u32[]{:S(2)}, u32[]{:S(2)}) collective-permute-start(bf16[2,96,1280]{2,1,0:T(8,128)(2,1)} %pad_maximum_fusion.7), channel_id=1, source_target_pairs={{0,4},{2,6},{12,8},{14,10},{4,0},{6,2},{8,12},{10,14},{1,5},{3,7},... | collective-permute-start | bytes 1474568 | tf_op jit(solution)/shard_map/ppermute | solution.py:132
  168.5 10.0 %collective-permute-start.30 = (f16[2,192,512]{2,1,0:T(8,128)(2,1)}, f16[2,192,512]{2,1,0:T(8,128)(2,1)}, u32[]{:S(2)}, u32[]{:S(2)}) collective-permute-start(f16[2,192,512]{2,1,0:T(8,128)(2,1)} %fusion.20), channel_id=1, source_target_pairs={{4,8},{6,10},{8,4},{10,6},{5,9},{7,11},{9,5},{11,7},{20,24},{22,26... | collective-permute-start | bytes 1179656 | tf_op jit(solution)/shard_map/ppermute | solution.py:132
  170.0 11.3 %collective-permute-start.29 = (f16[2,192,512]{2,1,0:T(8,128)(2,1)}, f16[2,192,512]{2,1,0:T(8,128)(2,1)}, u32[]{:S(2)}, u32[]{:S(2)}) collective-permute-start(f16[2,192,512]{2,1,0:T(8,128)(2,1)} %fusion.41), channel_id=1, source_target_pairs={{0,4},{2,6},{12,8},{14,10},{1,5},{3,7},{13,9},{15,11},{16,20},{18,... | collective-permute-start | bytes 1179656 | tf_op jit(solution)/shard_map/ppermute | solution.py:132
  173.7 29.4 %copy-start.7 = (f32[4,2,192,512]{3,2,1,0:T(8,128)S(1)}, f32[4,2,192,512]{3,2,1,0:T(8,128)}, u32[]{:S(2)}) copy-start(f32[4,2,192,512]{3,2,1,0:T(8,128)} %shard_map.71) | copy-start | bytes 9437188
  176.6 25.1 %collective-permute-start.28 = (bf16[2,96,1280]{2,1,0:T(8,128)(2,1)}, bf16[2,96,1280]{2,1,0:T(8,128)(2,1)S(1)}, u32[]{:S(2)}, u32[]{:S(2)}) collective-permute-start(bf16[2,96,1280]{2,1,0:T(8,128)(2,1)} %collective-permute-done.24), channel_id=1, source_target_pairs={{4,8},{6,10},{8,4},{10,6},{5,9},{7,11},{9,5},{11,7},{20,24},{22,26... | collective-permute-start | bytes 1474568 | tf_op jit(solution)/shard_map/ppermute | solution.py:132
  177.3 24.4 %collective-permute-start.27 = (bf16[2,96,1280]{2,1,0:T(8,128)(2,1)}, bf16[2,96,1280]{2,1,0:T(8,128)(2,1)S(1)}, u32[]{:S(2)}, u32[]{:S(2)}) collective-permute-start(bf16[2,96,1280]{2,1,0:T(8,128)(2,1)} %collective-permute-done.25), channel_id=1, source_target_pairs={{4,0},{6,2},{8,12},{10,14},{5,1},{7,3},{9,13},{11,15},{20,16},{22,... | collective-permute-start | bytes 1474568 | tf_op jit(solution)/shard_map/ppermute | solution.py:132
  183.4 19.6 %collective-permute-start.31 = (f16[2,192,512]{2,1,0:T(8,128)(2,1)S(1)}, f16[2,192,512]{2,1,0:T(8,128)(2,1)S(1)}, u32[]{:S(2)}, u32[]{:S(2)}) collective-permute-start(f16[2,192,512]{2,1,0:T(8,128)(2,1)S(1)} %get-tuple-element.153), channel_id=1, source_target_pairs={{0,4},{2,6},{12,8},{14,10},{4,0},{6,2},{8,12},{10,14},{1,5},{3,7},... | collective-permute-start | bytes 1179656 | tf_op jit(solution)/shard_map/ppermute | solution.py:132
  185.7 17.4 %collective-permute-start.32 = (f16[2,192,512]{2,1,0:T(8,128)(2,1)S(1)}, f16[2,192,512]{2,1,0:T(8,128)(2,1)S(1)}, u32[]{:S(2)}, u32[]{:S(2)}) collective-permute-start(f16[2,192,512]{2,1,0:T(8,128)(2,1)S(1)} %get-tuple-element.154), channel_id=1, source_target_pairs={{4,8},{6,10},{8,4},{10,6},{5,9},{7,11},{9,5},{11,7},{20,24},{22,26... | collective-permute-start | bytes 1179656 | tf_op jit(solution)/shard_map/ppermute | solution.py:132
  188.2 51.8 %collective-permute-start.41 = (bf16[4,2,96,1280]{3,2,1,0:T(8,128)(2,1)}, bf16[4,2,96,1280]{3,2,1,0:T(8,128)(2,1)}, u32[]{:S(2)}, u32[]{:S(2)}) collective-permute-start(bf16[4,2,96,1280]{3,2,1,0:T(8,128)(2,1)} %get-tuple-element.158), channel_id=1, source_target_pairs={{0,2},{2,0},{4,6},{6,4},{8,10},{10,8},{12,14},{14,12},{1,3},{3,1},... | collective-permute-start | bytes 5898248 | tf_op jit(solution)/shard_map/ppermute | solution.py:132
  201.7 14.7 %collective-permute-start.37 = (bf16[2,96,1280]{2,1,0:T(8,128)(2,1)S(1)}, bf16[2,96,1280]{2,1,0:T(8,128)(2,1)S(1)}, u32[]{:S(2)}, u32[]{:S(2)}) collective-permute-start(bf16[2,96,1280]{2,1,0:T(8,128)(2,1)S(1)} %collective-permute-done.28), channel_id=1, source_target_pairs={{4,0},{6,2},{8,12},{10,14},{5,1},{7,3},{9,13},{11,15},{20,16},{22,... | collective-permute-start | bytes 1474568 | tf_op jit(solution)/shard_map/ppermute | solution.py:132
  203.6 5.7 %copy-start.8 = (bf16[1,192,512]{2,1,0:T(8,128)(2,1)}, bf16[1,192,512]{2,1,0:T(8,128)(2,1)S(1)}, u32[]{:S(2)}) copy-start(bf16[1,192,512]{2,1,0:T(8,128)(2,1)S(1)} %get-tuple-element.167) | copy-start | bytes 589828
  203.6 5.7 %copy-start.10 = (bf16[1,192,512]{2,1,0:T(8,128)(2,1)}, bf16[1,192,512]{2,1,0:T(8,128)(2,1)S(1)}, u32[]{:S(2)}) copy-start(bf16[1,192,512]{2,1,0:T(8,128)(2,1)S(1)} %get-tuple-element.168) | copy-start | bytes 589828
  204.4 17.9 %collective-permute-start.36 = (bf16[2,192,512]{2,1,0:T(8,128)(2,1)}, bf16[2,192,512]{2,1,0:T(8,128)(2,1)}, u32[]{:S(2)}, u32[]{:S(2)}) collective-permute-start(bf16[2,192,512]{2,1,0:T(8,128)(2,1)} %pad_maximum_fusion.8), channel_id=1, source_target_pairs={{4,8},{6,10},{8,4},{10,6},{5,9},{7,11},{9,5},{11,7},{20,24},{22,26... | collective-permute-start | bytes 1179656 | tf_op jit(solution)/shard_map/ppermute | solution.py:132
  205.9 19.1 %collective-permute-start.35 = (bf16[2,192,512]{2,1,0:T(8,128)(2,1)}, bf16[2,192,512]{2,1,0:T(8,128)(2,1)}, u32[]{:S(2)}, u32[]{:S(2)}) collective-permute-start(bf16[2,192,512]{2,1,0:T(8,128)(2,1)} %pad_maximum_fusion.8), channel_id=1, source_target_pairs={{0,4},{2,6},{12,8},{14,10},{4,0},{6,2},{8,12},{10,14},{1,5},{3,7},... | collective-permute-start | bytes 1179656 | tf_op jit(solution)/shard_map/ppermute | solution.py:132
  217.8 3.5 %copy-start.14 = (bf16[1,96,1280]{2,1,0:T(8,128)(2,1)S(1)}, bf16[1,96,1280]{2,1,0:T(8,128)(2,1)}, u32[]{:S(2)}) copy-start(bf16[1,96,1280]{2,1,0:T(8,128)(2,1)} %get-tuple-element.169) | copy-start | bytes 737284
  217.8 3.5 %copy-start.15 = (bf16[1,96,1280]{2,1,0:T(8,128)(2,1)S(1)}, bf16[1,96,1280]{2,1,0:T(8,128)(2,1)}, u32[]{:S(2)}) copy-start(bf16[1,96,1280]{2,1,0:T(8,128)(2,1)} %get-tuple-element.170) | copy-start | bytes 737284
  220.1 19.9 %collective-permute-start.42 = (bf16[4,2,96,1280]{3,2,1,0:T(8,128)(2,1)}, bf16[4,2,96,1280]{3,2,1,0:T(8,128)(2,1)}, u32[]{:S(2)}, u32[]{:S(2)}) collective-permute-start(bf16[4,2,96,1280]{3,2,1,0:T(8,128)(2,1)} %get-tuple-element.156), channel_id=1, source_target_pairs={{0,2},{2,0},{4,6},{6,4},{8,10},{10,8},{12,14},{14,12},{1,3},{3,1},... | collective-permute-start | bytes 5898248 | tf_op jit(solution)/shard_map/ppermute | solution.py:132
  222.3 4.6 %collective-permute-start.33 = (bf16[2,48,1792]{2,1,0:T(8,128)(2,1)}, bf16[2,48,1792]{2,1,0:T(8,128)(2,1)}, u32[]{:S(2)}, u32[]{:S(2)}) collective-permute-start(bf16[2,48,1792]{2,1,0:T(8,128)(2,1)} %get-tuple-element.180), channel_id=1, source_target_pairs={{0,2},{2,0},{4,6},{6,4},{8,10},{10,8},{12,14},{14,12},{1,3},{3,1},... | collective-permute-start | bytes 1032200 | tf_op jit(solution)/shard_map/ppermute | solution.py:132
  225.0 12.1 %collective-permute-start.39 = (bf16[2,192,512]{2,1,0:T(8,128)(2,1)}, bf16[2,192,512]{2,1,0:T(8,128)(2,1)S(1)}, u32[]{:S(2)}, u32[]{:S(2)}) collective-permute-start(bf16[2,192,512]{2,1,0:T(8,128)(2,1)} %collective-permute-done.35), channel_id=1, source_target_pairs={{4,8},{6,10},{8,4},{10,6},{5,9},{7,11},{9,5},{11,7},{20,24},{22,26... | collective-permute-start | bytes 1179656 | tf_op jit(solution)/shard_map/ppermute | solution.py:132
  225.6 11.9 %collective-permute-start.38 = (bf16[2,192,512]{2,1,0:T(8,128)(2,1)}, bf16[2,192,512]{2,1,0:T(8,128)(2,1)S(1)}, u32[]{:S(2)}, u32[]{:S(2)}) collective-permute-start(bf16[2,192,512]{2,1,0:T(8,128)(2,1)} %collective-permute-done.36), channel_id=1, source_target_pairs={{4,0},{6,2},{8,12},{10,14},{5,1},{7,3},{9,13},{11,15},{20,16},{22,... | collective-permute-start | bytes 1179656 | tf_op jit(solution)/shard_map/ppermute | solution.py:132
  228.5 1.5 copy-start.5
  230.0 8.8 %copy-start.9 = (bf16[1,192,512]{2,1,0:T(8,128)(2,1)S(1)}, bf16[1,192,512]{2,1,0:T(8,128)(2,1)}, u32[]{:S(2)}) copy-start(bf16[1,192,512]{2,1,0:T(8,128)(2,1)} %copy-done.8) | copy-start | bytes 589828
  230.0 8.8 %copy-start.11 = (bf16[1,192,512]{2,1,0:T(8,128)(2,1)S(1)}, bf16[1,192,512]{2,1,0:T(8,128)(2,1)}, u32[]{:S(2)}) copy-start(bf16[1,192,512]{2,1,0:T(8,128)(2,1)} %copy-done.10) | copy-start | bytes 589828
  237.6 11.4 %collective-permute-start.40 = (bf16[2,192,512]{2,1,0:T(8,128)(2,1)S(1)}, bf16[2,192,512]{2,1,0:T(8,128)(2,1)S(1)}, u32[]{:S(2)}, u32[]{:S(2)}) collective-permute-start(bf16[2,192,512]{2,1,0:T(8,128)(2,1)S(1)} %collective-permute-done.39), channel_id=1, source_target_pairs={{4,0},{6,2},{8,12},{10,14},{5,1},{7,3},{9,13},{11,15},{20,16},{22,... | collective-permute-start | bytes 1179656 | tf_op jit(solution)/shard_map/ppermute | solution.py:132
  250.5 18.3 %collective-permute-start.43 = (bf16[4,2,192,512]{3,2,1,0:T(8,128)(2,1)}, bf16[4,2,192,512]{3,2,1,0:T(8,128)(2,1)}, u32[]{:S(2)}, u32[]{:S(2)}) collective-permute-start(bf16[4,2,192,512]{3,2,1,0:T(8,128)(2,1)} %get-tuple-element.160), channel_id=1, source_target_pairs={{0,2},{2,0},{4,6},{6,4},{8,10},{10,8},{12,14},{14,12},{1,3},{3,1},... | collective-permute-start | bytes 4718600 | tf_op jit(solution)/shard_map/ppermute | solution.py:132
  253.2 10.0 %collective-permute-start.34 = (bf16[48,3584]{1,0:T(8,128)(2,1)}, bf16[48,3584]{1,0:T(8,128)(2,1)}, u32[]{:S(2)}, u32[]{:S(2)}) collective-permute-start(bf16[48,3584]{1,0:T(8,128)(2,1)} %get-tuple-element.178), channel_id=1, source_target_pairs={{0,1},{1,0},{2,3},{3,2},{4,5},{5,4},{6,7},{7,6},{8,9},{9,8},{10,11... | collective-permute-start | bytes 1032200 | tf_op jit(solution)/shard_map/ppermute | solution.py:323

commit v11 on v10

--- a/solution.py
+++ b/solution.py
@@ -195,9 +195,10 @@
         own, theirs = terms
         return own[block] if theirs is None else own[block] + wide(theirs[block])
 
+    over_row = tie(over_row, over_depth)
     features = [arrange(by(row == 0, mine, over_row, 1))]
     theirs, own = own_features(features[0], 0, ())
-    terms = (own((over_depth, over_both)), send(theirs, pairs))
+    terms = (own(()), send(theirs, pairs))
     payload = take(terms, 3).astype(WIRE)
     in_1 = send(payload, inward)
 
@@ -269,9 +270,16 @@
             products[2] = all_features(tokens, 2, (side_1, centre_1))
             terms = tie(terms, products[2])
         if not adding:
+            hidden = jnp.stack([jnp.concatenate(parts, axis=1) for parts in hidden])
+            hidden = hidden.reshape(2, 2, slab, share)
+            mine = lax.dynamic_index_in_dim(hidden, core, 1, keepdims=False)
+            theirs = lax.dynamic_index_in_dim(hidden, 1 - core, 1, keepdims=False)
+            theirs = send(theirs, pairs)
             own_acts, other_acts = zip(*merged)
             totals = add_gradients(own_acts, core, (), pieces[0][1])
-            share_2 = tie(share_2, totals)
+            share_2 = tie(share_2, totals, theirs)
+            hidden = by(core == 0, mine, theirs, 2)
+            theirs = lax.ppermute(tie(hidden[1], side_1), "depth", swap)
         before = ()
         if adding:
             if gathering:
@@ -301,7 +309,8 @@
             out_3 = send(share_2, outward)
         if not adding:
             totals = add_gradients(other_acts, 1 - core, totals, pieces[0][1])
-            out_3 = tie(out_3, totals)
+            out_3 = tie(out_3, totals, theirs)
+            hidden = by(part == 0, hidden[0], theirs, 1)
         if adding:
             if gathering:
                 terms = tie(terms, out_2, share_2)
@@ -315,12 +324,6 @@
     totals = add_gradients([own_acts], core, totals, pieces[last][1])
     totals = add_gradients([other_acts], 1 - core, totals, pieces[last][1])
 
-    hidden = jnp.stack([jnp.concatenate(parts, axis=1) for parts in hidden])
-    hidden = hidden.reshape(2, 2, slab, share)
-    mine = lax.dynamic_index_in_dim(hidden, core, 1, keepdims=False)
-    theirs = lax.dynamic_index_in_dim(hidden, 1 - core, 1, keepdims=False)
-    hidden = by(core == 0, mine, send(theirs, pairs), 2)
-    hidden = by(part == 0, hidden[0], lax.ppermute(hidden[1], "depth", swap), 1)
     return (hidden[None], *totals)
 
 

time: 276 us -> 256 us (0.928)
  waiting for transfers between devices: 67.8 us -> 49.9 us
    ppermute x1, waiting for transfers between devices: 9.78 us -> 0.01 us  [local(): theirs = lax.ppermute(tie(hidden[1], side_1), 'depth', swap)]
    ppermute x1, waiting for transfers between devices: 9.28 us -> 0.82 us  [local(): over_depth = lax.ppermute(mine, 'depth', swap)]
    ppermute x39, waiting for transfers between devices: 31.2 us -> 37.5 us  [send(): return lax.ppermute(value, 'col', route)]
    ppermute x1, waiting for transfers between devices: 8.43 us -> 3.74 us  [local(): over_both = lax.ppermute(over_row, 'depth', swap)]
    unnamed x36 -> x38, local copies, waits for them, and re-layouts: 6.41 us -> 5.52 us
  transfers between devices with their start and end apart: 44 -> 44, of which waited for: 14 -> 11; matrix products, arithmetic and copies ran while one was open for 16% -> 17% of each run, Pallas kernels for 15% -> 17%
where the time goes in v11:
time: 256 us; the launch traced here: 254 us
  starting transfers between devices  91.5 us (36%)
  Pallas kernels  52.3 us (20%)
  waiting for transfers between devices  49.9 us (19%)
  other arithmetic  44.1 us (17%)
  local copies, waits for them, and re-layouts  15.1 us (6%)
    ppermute x39, starting transfers between devices, send(): return lax.ppermute(value, 'col', route)  85.3 us
    ppermute x39, waiting for transfers between devices, send(): return lax.ppermute(value, 'col', route)  37.5 us
    pallas_call x5, Pallas kernels, forward(): pl.pallas_call(functools.partial(forward_kernel, scale), out_shape=jax.Sh...  28.4 us
    pallas_call x4, Pallas kernels, gradient(): pl.pallas_call(functools.partial(gradient_kernel, len(acts)), out_shape=(...  23.9 us
    ppermute x1, waiting for transfers between devices, local(): over_row = lax.ppermute(mine, 'row', swap)  7.81 us
    convert_element_type x3, other arithmetic, local(): swapped = swapped.astype(WIRE)  6.2 us
    unnamed x38, local copies, waits for them, and re-layouts  5.52 us
    broadcast_in_dim x3, other arithmetic, add_gradients(): acts = [value[:, None] for value in acts]  5.23 us
  transfers between devices with their start and end apart: 44, of which 11 were waited for; matrix products, arithmetic and copies ran while one was open for 17% of the time, Pallas kernels for 17%

profile of v11, /device:TPU:1, one launch (start us, length us, event | category | flops | bytes accessed | tf_op | source)
XLA Modules:
  0.0 254.2 jit_solution(9835050335086937927)
XLA Ops:
  0.6 2.1 collective-permute-start
  4.0 7.8 %collective-permute-done = bf16[384,512]{1,0:T(8,128)(2,1)S(1)} collective-permute-done((bf16[384,512]{1,0:T(8,128)(2,1)}, bf16[384,512]{1,0:T(8,128)(2,1)S(1)}, u32[]{:S(2)}, u32[]{:S(2)}) %collective-permute-start) | collective-permute-done | bytes 393248 | tf_op jit(solution)/shard_map/ppermute | solution.py:165
  12.6 1.3 maximum_select_fusion
  14.2 5.6 %shard_map.67 = f32[4,2,96,1280]{3,2,1,0:T(8,128)S(1)} custom-call(s32[1]{0:T(128)} %bitcast.5.place_ref, bf16[384,1024]{1,0:T(8,128)(2,1)S(1)} %bitcast.187, bf16[1024,7168]{1,0:T(8,128)(2,1)} %refs_2_.9, bf16[1024,7168]{1,0:T(8,128)(2,1)} %refs_3_.1), custom_call_target="tpu_custom_call" | custom-call | tf_op jit(solution)/shard_map/pallas_call | solution.py:45
  19.7 1.5 convert_element_type.197
  21.2 1.9 collective-permute-start.2
  23.1 5.5 %shard_map.68 = f32[4,2,96,1280]{3,2,1,0:T(8,128)S(1)} custom-call(s32[1]{0:T(128)} %bitcast.place_ref, bf16[384,1024]{1,0:T(8,128)(2,1)S(1)} %bitcast.188, bf16[1024,7168]{1,0:T(8,128)(2,1)} %refs_2_.9, bf16[1024,7168]{1,0:T(8,128)(2,1)} %refs_3_.1), custom_call_target="tpu_custom_call" | custom-call | tf_op jit(solution)/shard_map/pallas_call | solution.py:45
  28.7 1.3 collective-permute-start.3
  30.6 1.9 fusion.34
  32.5 3.2 %collective-permute-start.4 = (f16[2,96,1280]{2,1,0:T(8,128)(2,1)}, f16[2,96,1280]{2,1,0:T(8,128)(2,1)S(1)}, u32[]{:S(2)}, u32[]{:S(2)}) collective-permute-start(f16[2,96,1280]{2,1,0:T(8,128)(2,1)} %fusion.34), channel_id=1, source_target_pairs={{0,4},{2,6},{12,8},{14,10},{1,5},{3,7},{13,9},{15,11},{16,20},{18,... | collective-permute-start | bytes 1474568 | tf_op jit(solution)/shard_map/ppermute | solution.py:132
  35.8 3.7 %collective-permute-done.3 = bf16[384,512]{1,0:T(8,128)(2,1)S(1)} collective-permute-done((bf16[384,512]{1,0:T(8,128)(2,1)S(1)}, bf16[384,512]{1,0:T(8,128)(2,1)S(1)}, u32[]{:S(2)}, u32[]{:S(2)}) %collective-permute-start.3) | collective-permute-done | bytes 393248 | tf_op jit(solution)/shard_map/ppermute | solution.py:167
  39.9 5.6 %shard_map.69 = f32[4,2,96,1280]{3,2,1,0:T(8,128)S(1)} custom-call(s32[1]{0:T(128)} %bitcast.5.place_ref, bf16[384,1024]{1,0:T(8,128)(2,1)S(1)} %bitcast.191, bf16[1024,7168]{1,0:T(8,128)(2,1)} %refs_2_.9, bf16[1024,7168]{1,0:T(8,128)(2,1)} %refs_3_.1), custom_call_target="tpu_custom_call" | custom-call | tf_op jit(solution)/shard_map/pallas_call | solution.py:45
  45.5 1.5 convert_element_type.201
  47.0 1.3 copy-done.1
  48.3 2.0 fusion.31
  50.3 2.0 fusion.14
  55.5 4.0 %collective-permute-start.8 = (f16[2,96,1280]{2,1,0:T(8,128)(2,1)}, f16[2,96,1280]{2,1,0:T(8,128)(2,1)}, u32[]{:S(2)}, u32[]{:S(2)}) collective-permute-start(f16[2,96,1280]{2,1,0:T(8,128)(2,1)} %fusion.31), channel_id=1, source_target_pairs={{0,4},{2,6},{12,8},{14,10},{1,5},{3,7},{13,9},{15,11},{16,20},{18,... | collective-permute-start | bytes 1474568 | tf_op jit(solution)/shard_map/ppermute | solution.py:132
  59.4 1.4 collective-permute-start.6
  63.2 1.5 maximum_bitcast_fusion.features_ref
  64.7 5.7 %shard_map.70 = f32[4,2,96,1280]{3,2,1,0:T(8,128)S(1)} custom-call(s32[1]{0:T(128)} %bitcast.place_ref, bf16[384,1024]{1,0:T(8,128)(2,1)S(1)} %bitcast.193, bf16[1024,7168]{1,0:T(8,128)(2,1)} %refs_2_.9, bf16[1024,7168]{1,0:T(8,128)(2,1)} %refs_3_.1), custom_call_target="tpu_custom_call" | custom-call | tf_op jit(solution)/shard_map/pallas_call | solution.py:45
  71.6 2.1 fusion.11
  73.6 1.6 collective-permute-start.7
  77.1 1.3 dynamic-slice_bitcast_fusion.1
  78.4 1.3 dynamic-slice_bitcast_fusion
  80.9 5.1 %collective-permute-done.7 = f16[2,96,1280]{2,1,0:T(8,128)(2,1)S(1)} collective-permute-done((f16[2,96,1280]{2,1,0:T(8,128)(2,1)S(1)}, f16[2,96,1280]{2,1,0:T(8,128)(2,1)S(1)}, u32[]{:S(2)}, u32[]{:S(2)}) %collective-permute-start.7) | collective-permute-done | bytes 491552 | tf_op jit(solution)/shard_map/ppermute | solution.py:132
  86.1 1.5 fusion.13
  88.8 5.0 %collective-permute-start.15 = (f16[2,96,1280]{2,1,0:T(8,128)(2,1)S(1)}, f16[2,96,1280]{2,1,0:T(8,128)(2,1)S(1)}, u32[]{:S(2)}, u32[]{:S(2)}) collective-permute-start(f16[2,96,1280]{2,1,0:T(8,128)(2,1)S(1)} %fusion.32), channel_id=1, source_target_pairs={{0,4},{2,6},{12,8},{14,10},{1,5},{3,7},{13,9},{15,11},{16,20},{18,... | collective-permute-start | bytes 1474568 | tf_op jit(solution)/shard_map/ppermute | solution.py:132
  95.6 7.0 %collective-permute-done.15 = f16[2,96,1280]{2,1,0:T(8,128)(2,1)S(1)} collective-permute-done((f16[2,96,1280]{2,1,0:T(8,128)(2,1)S(1)}, f16[2,96,1280]{2,1,0:T(8,128)(2,1)S(1)}, u32[]{:S(2)}, u32[]{:S(2)}) %collective-permute-start.15) | collective-permute-done | bytes 491552 | tf_op jit(solution)/shard_map/ppermute | solution.py:132
  102.5 1.9 fusion.33
  104.5 4.1 %collective-permute-start.19 = (f16[2,96,1280]{2,1,0:T(8,128)(2,1)}, f16[2,96,1280]{2,1,0:T(8,128)(2,1)S(1)}, u32[]{:S(2)}, u32[]{:S(2)}) collective-permute-start(f16[2,96,1280]{2,1,0:T(8,128)(2,1)} %fusion.33), channel_id=1, source_target_pairs={{0,4},{2,6},{12,8},{14,10},{1,5},{3,7},{13,9},{15,11},{16,20},{18,... | collective-permute-start | bytes 1474568 | tf_op jit(solution)/shard_map/ppermute | solution.py:132
  109.8 3.3 %collective-permute-done.12 = bf16[2,96,1280]{2,1,0:T(8,128)(2,1)S(1)} collective-permute-done((bf16[2,96,1280]{2,1,0:T(8,128)(2,1)S(1)}, bf16[2,96,1280]{2,1,0:T(8,128)(2,1)S(1)}, u32[]{:S(2)}, u32[]{:S(2)}) %collective-permute-start.12) | collective-permute-done | bytes 491552 | tf_op jit(solution)/shard_map/ppermute | solution.py:132
  115.1 1.5 collective-permute-start.18
  116.8 1.3 copy-done.3
  118.1 1.6 copy-done.4
  119.7 6.0 %shard_map.71 = f32[4,2,192,512]{3,2,1,0:T(8,128)} custom-call(s32[1]{0:T(128)} %bitcast.place_ref, bf16[768,1024]{1,0:T(8,128)(2,1)S(1)} %bitcast.195, bf16[768,1024]{1,0:T(8,128)(2,1)S(1)} %bitcast.196, bf16[1024,7168]{1,0:T(8,128)(2,1)} %refs_2_.9, bf16[1024,7168]{1,0:T(8,128)(2,1)} %refs_3_.1, bf16[2,1024,512]{2,1,0:T(8,128)(2,1)S(1)} %copy-done.4, ...), custom_call_target="tpu_custom_call" | custom-call | tf_op jit(solution)/shard_map/pallas_call | solution.py:45
  125.7 1.9 fusion.6
  127.6 5.4 %collective-permute-start.22 = (f16[2,96,1280]{2,1,0:T(8,128)(2,1)S(1)}, f16[2,96,1280]{2,1,0:T(8,128)(2,1)S(1)}, u32[]{:S(2)}, u32[]{:S(2)}) collective-permute-start(f16[2,96,1280]{2,1,0:T(8,128)(2,1)S(1)} %get-tuple-element.153), channel_id=1, source_target_pairs={{0,4},{2,6},{12,8},{14,10},{4,0},{6,2},{8,12},{10,14},{1,5},{3,7},... | collective-permute-start | bytes 1474568 | tf_op jit(solution)/shard_map/ppermute | solution.py:132
  135.2 4.7 %collective-permute-start.26 = (f16[2,192,512]{2,1,0:T(8,128)(2,1)S(1)}, f16[2,192,512]{2,1,0:T(8,128)(2,1)S(1)}, u32[]{:S(2)}, u32[]{:S(2)}) collective-permute-start(f16[2,192,512]{2,1,0:T(8,128)(2,1)S(1)} %fusion.40), channel_id=1, source_target_pairs={{0,4},{2,6},{12,8},{14,10},{1,5},{3,7},{13,9},{15,11},{16,20},{18,... | collective-permute-start | bytes 1179656 | tf_op jit(solution)/shard_map/ppermute | solution.py:132
  139.9 1.6 fusion.8
  143.3 8.4 %collective-permute-start.24 = (bf16[2,96,1280]{2,1,0:T(8,128)(2,1)}, bf16[2,96,1280]{2,1,0:T(8,128)(2,1)}, u32[]{:S(2)}, u32[]{:S(2)}) collective-permute-start(bf16[2,96,1280]{2,1,0:T(8,128)(2,1)} %pad_maximum_fusion.7), channel_id=1, source_target_pairs={{0,4},{2,6},{12,8},{14,10},{4,0},{6,2},{8,12},{10,14},{1,5},{3,7},... | collective-permute-start | bytes 1474568 | tf_op jit(solution)/shard_map/ppermute | solution.py:132
  151.7 1.4 collective-permute-start.25
  153.4 1.6 fusion.44
  155.8 5.4 %collective-permute-start.29 = (f16[2,192,512]{2,1,0:T(8,128)(2,1)}, f16[2,192,512]{2,1,0:T(8,128)(2,1)}, u32[]{:S(2)}, u32[]{:S(2)}) collective-permute-start(f16[2,192,512]{2,1,0:T(8,128)(2,1)} %fusion.41), channel_id=1, source_target_pairs={{0,4},{2,6},{12,8},{14,10},{1,5},{3,7},{13,9},{15,11},{16,20},{18,... | collective-permute-start | bytes 1179656 | tf_op jit(solution)/shard_map/ppermute | solution.py:132
  162.1 1.4 collective-permute-start.30
  163.9 1.4 collective-permute-start.27
  166.0 3.8 %collective-permute-done.29 = f16[2,192,512]{2,1,0:T(8,128)(2,1)} collective-permute-done((f16[2,192,512]{2,1,0:T(8,128)(2,1)}, f16[2,192,512]{2,1,0:T(8,128)(2,1)}, u32[]{:S(2)}, u32[]{:S(2)}) %collective-permute-start.29) | collective-permute-done | bytes 393248 | tf_op jit(solution)/shard_map/ppermute | solution.py:132
  169.8 2.2 fusion.17
  171.9 2.6 %collective-permute-start.31 = (f16[2,192,512]{2,1,0:T(8,128)(2,1)S(1)}, f16[2,192,512]{2,1,0:T(8,128)(2,1)S(1)}, u32[]{:S(2)}, u32[]{:S(2)}) collective-permute-start(f16[2,192,512]{2,1,0:T(8,128)(2,1)S(1)} %get-tuple-element.157), channel_id=1, source_target_pairs={{0,4},{2,6},{12,8},{14,10},{4,0},{6,2},{8,12},{10,14},{1,5},{3,7},... | collective-permute-start | bytes 1179656 | tf_op jit(solution)/shard_map/ppermute | solution.py:132
  177.0 7.2 %collective-permute-start.41 = (bf16[4,2,96,1280]{3,2,1,0:T(8,128)(2,1)}, bf16[4,2,96,1280]{3,2,1,0:T(8,128)(2,1)}, u32[]{:S(2)}, u32[]{:S(2)}) collective-permute-start(bf16[4,2,96,1280]{3,2,1,0:T(8,128)(2,1)} %get-tuple-element.162), channel_id=1, source_target_pairs={{0,2},{2,0},{4,6},{6,4},{8,10},{10,8},{12,14},{14,12},{1,3},{3,1},... | collective-permute-start | bytes 5898248 | tf_op jit(solution)/shard_map/ppermute | solution.py:132
  187.9 2.6 %collective-permute-start.33 = (bf16[2,48,1792]{2,1,0:T(8,128)(2,1)}, bf16[2,48,1792]{2,1,0:T(8,128)(2,1)}, u32[]{:S(2)}, u32[]{:S(2)}) collective-permute-start(bf16[2,48,1792]{2,1,0:T(8,128)(2,1)} %get-tuple-element.184), channel_id=1, source_target_pairs={{0,2},{2,0},{4,6},{6,4},{8,10},{10,8},{12,14},{14,12},{1,3},{3,1},... | collective-permute-start | bytes 1032200 | tf_op jit(solution)/shard_map/ppermute | solution.py:132
  191.3 4.7 %collective-permute-done.36 = bf16[2,96,1280]{2,1,0:T(8,128)(2,1)S(1)} collective-permute-done((bf16[2,96,1280]{2,1,0:T(8,128)(2,1)S(1)}, bf16[2,96,1280]{2,1,0:T(8,128)(2,1)S(1)}, u32[]{:S(2)}, u32[]{:S(2)}) %collective-permute-start.36) | collective-permute-done | bytes 491552 | tf_op jit(solution)/shard_map/ppermute | solution.py:132
  197.3 2.2 fusion.43
  199.6 3.9 %collective-permute-start.42 = (bf16[4,2,96,1280]{3,2,1,0:T(8,128)(2,1)}, bf16[4,2,96,1280]{3,2,1,0:T(8,128)(2,1)}, u32[]{:S(2)}, u32[]{:S(2)}) collective-permute-start(bf16[4,2,96,1280]{3,2,1,0:T(8,128)(2,1)} %get-tuple-element.160), channel_id=1, source_target_pairs={{0,2},{2,0},{4,6},{6,4},{8,10},{10,8},{12,14},{14,12},{1,3},{3,1},... | collective-permute-start | bytes 5898248 | tf_op jit(solution)/shard_map/ppermute | solution.py:132
  204.6 1.5 maximum_select_fusion.3
  206.0 8.4 %collective-permute-done.34 = bf16[2,192,512]{2,1,0:T(8,128)(2,1)S(1)} collective-permute-done((bf16[2,192,512]{2,1,0:T(8,128)(2,1)}, bf16[2,192,512]{2,1,0:T(8,128)(2,1)S(1)}, u32[]{:S(2)}, u32[]{:S(2)}) %collective-permute-start.34) | collective-permute-done | bytes 393248 | tf_op jit(solution)/shard_map/ppermute | solution.py:132
  215.1 1.3 collective-permute-start.38
  217.4 7.0 %shard_map.72 = (f32[1024,3584]{1,0:T(8,128)}, f32[1024,3584]{1,0:T(8,128)}) custom-call(s32[1]{0:T(128)} %bitcast.73.place_ref, bf16[1024,768]{1,0:T(8,128)(2,1)S(1)} %maximum_bitcast_fusion.features_ref, bf16[4,1,2,96,1280]{4,3,2,1,0:T(8,128)(2,1)S(1)} %get-tuple-element.161.refs_0_, bf16[4,1,2,96,1280]{4,3,2,1,0:T(8,128)(2,1)S(1)} %copy-done.5), custom_call_target="tpu_custom_call" | custom-call | tf_op jit(solution)/shard_map/pallas_call | solution.py:83
  224.5 4.9 %collective-permute-done.38 = bf16[2,192,512]{2,1,0:T(8,128)(2,1)S(1)} collective-permute-done((bf16[2,192,512]{2,1,0:T(8,128)(2,1)S(1)}, bf16[2,192,512]{2,1,0:T(8,128)(2,1)S(1)}, u32[]{:S(2)}, u32[]{:S(2)}) %collective-permute-start.38) | collective-permute-done | bytes 393248 | tf_op jit(solution)/shard_map/ppermute | solution.py:132
  230.8 9.0 %shard_map.73 = (f32[1024,3584]{1,0:T(8,128)}, f32[1024,3584]{1,0:T(8,128)}) custom-call(s32[1]{0:T(128)} %bitcast.70.place_ref, bf16[1024,768]{1,0:T(8,128)(2,1)S(1)} %maximum_bitcast_fusion.features_ref, bf16[4,1,2,96,1280]{4,3,2,1,0:T(8,128)(2,1)} %bitcast.80.refs_0_, ...), custom_call_target="tpu_custom_call", output_to_operand_aliasing={{0}: (4, {}), {1}: (5, {})} | custom-call | tf_op jit(solution)/shard_map/pallas_call | solution.py:83
  239.8 1.4 fusion.42
  241.3 2.9 %collective-permute-start.43 = (bf16[4,2,192,512]{3,2,1,0:T(8,128)(2,1)}, bf16[4,2,192,512]{3,2,1,0:T(8,128)(2,1)}, u32[]{:S(2)}, u32[]{:S(2)}) collective-permute-start(bf16[4,2,192,512]{3,2,1,0:T(8,128)(2,1)} %get-tuple-element.164), channel_id=1, source_target_pairs={{0,2},{2,0},{4,6},{6,4},{8,10},{10,8},{12,14},{14,12},{1,3},{3,1},... | collective-permute-start | bytes 4718600 | tf_op jit(solution)/shard_map/ppermute | solution.py:132
  244.2 2.1 maximum_select_fusion.4
  246.3 3.4 %shard_map.74 = (f32[1024,3584]{1,0:T(8,128)}, f32[1024,3584]{1,0:T(8,128)}) custom-call(s32[1]{0:T(128)} %bitcast.73.place_ref, bf16[1024,768]{1,0:T(8,128)(2,1)S(1)} %maximum_bitcast_fusion.features_ref, bf16[4,1,2,192,512]{4,3,2,1,0:T(8,128)(2,1)S(1)} %get-tuple-element.163.refs_0_, ...), custom_call_target="tpu_custom_call", output_to_operand_aliasing={{0}: (3, {}), {1}: (4, {})} | custom-call | tf_op jit(solution)/shard_map/pallas_call | solution.py:83
  249.7 4.4 %shard_map.75 = (f32[1024,3584]{1,0:T(8,128)}, f32[1024,3584]{1,0:T(8,128)}) custom-call(s32[1]{0:T(128)} %bitcast.70.place_ref, bf16[1024,768]{1,0:T(8,128)(2,1)S(1)} %maximum_bitcast_fusion.features_ref, bf16[4,1,2,192,512]{4,3,2,1,0:T(8,128)(2,1)} %bitcast.83.refs_0_, ...), custom_call_target="tpu_custom_call", output_to_operand_aliasing={{0}: (3, {}), {1}: (4, {})} | custom-call | tf_op jit(solution)/shard_map/pallas_call | solution.py:83
  (133 shorter events, 38.5 us)
Async XLA Ops:
  0.6 11.2 %collective-permute-start = (bf16[384,512]{1,0:T(8,128)(2,1)}, bf16[384,512]{1,0:T(8,128)(2,1)S(1)}, u32[]{:S(2)}, u32[]{:S(2)}) collective-permute-start(bf16[384,512]{1,0:T(8,128)(2,1)} %bitcast.202), channel_id=1, source_target_pairs={{0,16},{16,0},{1,17},{17,1},{2,18},{18,2},{3,19},{19,3},{4,20},{20... | collective-permute-start | bytes 1179656 | tf_op jit(solution)/shard_map/ppermute | solution.py:165
  2.7 9.9 %collective-permute-start.1 = (bf16[384,512]{1,0:T(8,128)(2,1)}, bf16[384,512]{1,0:T(8,128)(2,1)S(1)}, u32[]{:S(2)}, u32[]{:S(2)}) collective-permute-start(bf16[384,512]{1,0:T(8,128)(2,1)} %bitcast.203), channel_id=1, source_target_pairs={{0,1},{1,0},{2,3},{3,2},{4,5},{5,4},{6,7},{7,6},{8,9},{9,8},{10,11... | collective-permute-start | bytes 1179656 | tf_op jit(solution)/shard_map/ppermute | solution.py:166
  21.2 8.7 %collective-permute-start.2 = (f16[4,2,96,1280]{3,2,1,0:T(8,128)(2,1)}, f16[4,2,96,1280]{3,2,1,0:T(8,128)(2,1)}, u32[]{:S(2)}, u32[]{:S(2)}) collective-permute-start(f16[4,2,96,1280]{3,2,1,0:T(8,128)(2,1)} %convert_element_type.197), channel_id=1, source_target_pairs={{0,2},{2,0},{4,6},{6,4},{8,10},{10,8},{12,14},{14,12},{1,3},{3,1},... | collective-permute-start | bytes 5898248 | tf_op jit(solution)/shard_map/ppermute | solution.py:132
  28.7 1.9 copy-start
  28.7 10.8 %collective-permute-start.3 = (bf16[384,512]{1,0:T(8,128)(2,1)S(1)}, bf16[384,512]{1,0:T(8,128)(2,1)S(1)}, u32[]{:S(2)}, u32[]{:S(2)}) collective-permute-start(bf16[384,512]{1,0:T(8,128)(2,1)S(1)} %collective-permute-done), channel_id=1, source_target_pairs={{0,1},{1,0},{2,3},{3,2},{4,5},{5,4},{6,7},{7,6},{8,9},{9,8},{10,11... | collective-permute-start | bytes 1179656 | tf_op jit(solution)/shard_map/ppermute | solution.py:167
  32.5 14.5 %collective-permute-start.4 = (f16[2,96,1280]{2,1,0:T(8,128)(2,1)}, f16[2,96,1280]{2,1,0:T(8,128)(2,1)S(1)}, u32[]{:S(2)}, u32[]{:S(2)}) collective-permute-start(f16[2,96,1280]{2,1,0:T(8,128)(2,1)} %fusion.34), channel_id=1, source_target_pairs={{0,4},{2,6},{12,8},{14,10},{1,5},{3,7},{13,9},{15,11},{16,20},{18,... | collective-permute-start | bytes 1474568 | tf_op jit(solution)/shard_map/ppermute | solution.py:132
  45.5 2.8 %copy-start.1 = (f32[4,2,96,1280]{3,2,1,0:T(8,128)S(1)}, f32[4,2,96,1280]{3,2,1,0:T(8,128)}, u32[]{:S(2)}) copy-start(f32[4,2,96,1280]{3,2,1,0:T(8,128)} %copy-done) | copy-start | bytes 11796484
  47.0 5.3 %copy-start.17 = (bf16[1,48,7168]{2,1,0:T(8,128)(2,1)S(1)}, bf16[1,48,7168]{2,1,0:T(8,128)(2,1)}, u32[]{:S(2)}) copy-start(bf16[1,48,7168]{2,1,0:T(8,128)(2,1)} %param.7) | copy-start | bytes 2064388
  53.1 17.3 %collective-permute-start.5 = (bf16[48,3584]{1,0:T(8,128)(2,1)}, bf16[48,3584]{1,0:T(8,128)(2,1)}, u32[]{:S(2)}, u32[]{:S(2)}) collective-permute-start(bf16[48,3584]{1,0:T(8,128)(2,1)} %get-tuple-element.190), channel_id=1, source_target_pairs={{0,1},{1,0},{2,3},{3,2},{4,5},{5,4},{6,7},{7,6},{8,9},{9,8},{10,11... | collective-permute-start | bytes 1032200 | tf_op jit(solution)/shard_map/ppermute | solution.py:266
  54.4 33.2 %collective-permute-start.14 = (f16[4,2,96,1280]{3,2,1,0:T(8,128)(2,1)}, f16[4,2,96,1280]{3,2,1,0:T(8,128)(2,1)}, u32[]{:S(2)}, u32[]{:S(2)}) collective-permute-start(f16[4,2,96,1280]{3,2,1,0:T(8,128)(2,1)} %convert_element_type.201), channel_id=1, source_target_pairs={{0,2},{2,0},{4,6},{6,4},{8,10},{10,8},{12,14},{14,12},{1,3},{3,1},... | collective-permute-start | bytes 5898248 | tf_op jit(solution)/shard_map/ppermute | solution.py:132
  55.5 16.1 %collective-permute-start.8 = (f16[2,96,1280]{2,1,0:T(8,128)(2,1)}, f16[2,96,1280]{2,1,0:T(8,128)(2,1)}, u32[]{:S(2)}, u32[]{:S(2)}) collective-permute-start(f16[2,96,1280]{2,1,0:T(8,128)(2,1)} %fusion.31), channel_id=1, source_target_pairs={{0,4},{2,6},{12,8},{14,10},{1,5},{3,7},{13,9},{15,11},{16,20},{18,... | collective-permute-start | bytes 1474568 | tf_op jit(solution)/shard_map/ppermute | solution.py:132
  59.4 12.1 %collective-permute-start.6 = (f16[2,96,1280]{2,1,0:T(8,128)(2,1)}, f16[2,96,1280]{2,1,0:T(8,128)(2,1)}, u32[]{:S(2)}, u32[]{:S(2)}) collective-permute-start(f16[2,96,1280]{2,1,0:T(8,128)(2,1)} %fusion.14), channel_id=1, source_target_pairs={{4,8},{6,10},{8,4},{10,6},{5,9},{7,11},{9,5},{11,7},{20,24},{22,26... | collective-permute-start | bytes 1474568 | tf_op jit(solution)/shard_map/ppermute | solution.py:132
  64.7 6.8 %copy-start.2 = (f32[4,2,96,1280]{3,2,1,0:T(8,128)S(1)}, f32[4,2,96,1280]{3,2,1,0:T(8,128)}, u32[]{:S(2)}) copy-start(f32[4,2,96,1280]{3,2,1,0:T(8,128)} %copy-done) | copy-start | bytes 11796484
  73.6 12.4 %collective-permute-start.7 = (f16[2,96,1280]{2,1,0:T(8,128)(2,1)S(1)}, f16[2,96,1280]{2,1,0:T(8,128)(2,1)S(1)}, u32[]{:S(2)}, u32[]{:S(2)}) collective-permute-start(f16[2,96,1280]{2,1,0:T(8,128)(2,1)S(1)} %get-tuple-element.155), channel_id=1, source_target_pairs={{0,4},{2,6},{12,8},{14,10},{4,0},{6,2},{8,12},{10,14},{1,5},{3,7},... | collective-permute-start | bytes 1474568 | tf_op jit(solution)/shard_map/ppermute | solution.py:132
  75.2 10.8 %collective-permute-start.9 = (f16[2,96,1280]{2,1,0:T(8,128)(2,1)S(1)}, f16[2,96,1280]{2,1,0:T(8,128)(2,1)S(1)}, u32[]{:S(2)}, u32[]{:S(2)}) collective-permute-start(f16[2,96,1280]{2,1,0:T(8,128)(2,1)S(1)} %get-tuple-element.156), channel_id=1, source_target_pairs={{4,8},{6,10},{8,4},{10,6},{5,9},{7,11},{9,5},{11,7},{20,24},{22,26... | collective-permute-start | bytes 1474568 | tf_op jit(solution)/shard_map/ppermute | solution.py:132
  76.0 4.2 %collective-permute-start.11 = (bf16[2,48,1792]{2,1,0:T(8,128)(2,1)S(1)}, bf16[2,48,1792]{2,1,0:T(8,128)(2,1)S(1)}, u32[]{:S(2)}, u32[]{:S(2)}) collective-permute-start(bf16[2,48,1792]{2,1,0:T(8,128)(2,1)S(1)} %get-tuple-element.188), channel_id=1, source_target_pairs={{0,2},{2,0},{4,6},{6,4},{8,10},{10,8},{12,14},{14,12},{1,3},{3,1},... | collective-permute-start | bytes 1032200 | tf_op jit(solution)/shard_map/ppermute | solution.py:132
  79.9 36.9 %collective-permute-start.16 = (bf16[2,1024,512]{2,1,0:T(8,128)(2,1)S(1)}, bf16[2,1024,512]{2,1,0:T(8,128)(2,1)S(1)}, u32[]{:S(2)}, u32[]{:S(2)}) collective-permute-start(bf16[2,1024,512]{2,1,0:T(8,128)(2,1)S(1)} %pad_maximum_fusion), channel_id=1, source_target_pairs={{0,2},{2,0},{4,6},{6,4},{8,10},{10,8},{12,14},{14,12},{1,3},{3,1},... | collective-permute-start | bytes 6291464 | tf_op jit(solution)/shard_map/ppermute | solution.py:132
  80.2 34.9 %collective-permute-start.10 = (bf16[4,2,96,1024]{3,2,0,1:T(8,128)(2,1)S(1)}, bf16[4,2,96,1024]{3,2,0,1:T(8,128)(2,1)S(1)}, u32[]{:S(2)}, u32[]{:S(2)}) collective-permute-start(bf16[4,2,96,1024]{3,2,0,1:T(8,128)(2,1)S(1)} %pad_maximum_fusion.3), channel_id=1, source_target_pairs={{0,2},{2,0},{4,6},{6,4},{8,10},{10,8},{12,14},{14,12},{1,3},{3,1},... | collective-permute-start | bytes 4718600 | tf_op jit(solution)/shard_map/ppermute | solution.py:132
  80.9 12.9 %copy-start.12 = (bf16[96,1792]{1,0:T(8,128)(2,1)}, bf16[96,1792]{1,0:T(8,128)(2,1)S(1)}, u32[]{:S(2)}) copy-start(bf16[96,1792]{1,0:T(8,128)(2,1)S(1)} %get-tuple-element.186) | copy-start | bytes 1032196
  80.9 60.6 %copy-start.13 = (bf16[96,1792]{1,0:T(8,128)(2,1)}, bf16[96,1792]{1,0:T(8,128)(2,1)S(1)}, u32[]{:S(2)}) copy-start(bf16[96,1792]{1,0:T(8,128)(2,1)S(1)} %get-tuple-element.185) | copy-start | bytes 1032196
  88.8 13.8 %collective-permute-start.15 = (f16[2,96,1280]{2,1,0:T(8,128)(2,1)S(1)}, f16[2,96,1280]{2,1,0:T(8,128)(2,1)S(1)}, u32[]{:S(2)}, u32[]{:S(2)}) collective-permute-start(f16[2,96,1280]{2,1,0:T(8,128)(2,1)S(1)} %fusion.32), channel_id=1, source_target_pairs={{0,4},{2,6},{12,8},{14,10},{1,5},{3,7},{13,9},{15,11},{16,20},{18,... | collective-permute-start | bytes 1474568 | tf_op jit(solution)/shard_map/ppermute | solution.py:132
  94.8 18.3 %collective-permute-start.12 = (bf16[2,96,1280]{2,1,0:T(8,128)(2,1)S(1)}, bf16[2,96,1280]{2,1,0:T(8,128)(2,1)S(1)}, u32[]{:S(2)}, u32[]{:S(2)}) collective-permute-start(bf16[2,96,1280]{2,1,0:T(8,128)(2,1)S(1)} %pad_maximum_fusion.6), channel_id=1, source_target_pairs={{0,4},{2,6},{12,8},{14,10},{4,0},{6,2},{8,12},{10,14},{1,5},{3,7},... | collective-permute-start | bytes 1474568 | tf_op jit(solution)/shard_map/ppermute | solution.py:132
  94.9 18.9 %collective-permute-start.13 = (bf16[2,96,1280]{2,1,0:T(8,128)(2,1)S(1)}, bf16[2,96,1280]{2,1,0:T(8,128)(2,1)S(1)}, u32[]{:S(2)}, u32[]{:S(2)}) collective-permute-start(bf16[2,96,1280]{2,1,0:T(8,128)(2,1)S(1)} %pad_maximum_fusion.6), channel_id=1, source_target_pairs={{4,8},{6,10},{8,4},{10,6},{5,9},{7,11},{9,5},{11,7},{20,24},{22,26... | collective-permute-start | bytes 1474568 | tf_op jit(solution)/shard_map/ppermute | solution.py:132
  104.5 21.2 %collective-permute-start.19 = (f16[2,96,1280]{2,1,0:T(8,128)(2,1)}, f16[2,96,1280]{2,1,0:T(8,128)(2,1)S(1)}, u32[]{:S(2)}, u32[]{:S(2)}) collective-permute-start(f16[2,96,1280]{2,1,0:T(8,128)(2,1)} %fusion.33), channel_id=1, source_target_pairs={{0,4},{2,6},{12,8},{14,10},{1,5},{3,7},{13,9},{15,11},{16,20},{18,... | collective-permute-start | bytes 1474568 | tf_op jit(solution)/shard_map/ppermute | solution.py:132
  113.1 12.6 %collective-permute-start.20 = (f16[2,96,1280]{2,1,0:T(8,128)(2,1)S(1)}, f16[2,96,1280]{2,1,0:T(8,128)(2,1)S(1)}, u32[]{:S(2)}, u32[]{:S(2)}) collective-permute-start(f16[2,96,1280]{2,1,0:T(8,128)(2,1)S(1)} %fusion.2), channel_id=1, source_target_pairs={{4,8},{6,10},{8,4},{10,6},{5,9},{7,11},{9,5},{11,7},{20,24},{22,26... | collective-permute-start | bytes 1474568 | tf_op jit(solution)/shard_map/ppermute | solution.py:132
  113.8 20.0 %collective-permute-start.17 = (bf16[2,96,1280]{2,1,0:T(8,128)(2,1)S(1)}, bf16[2,96,1280]{2,1,0:T(8,128)(2,1)S(1)}, u32[]{:S(2)}, u32[]{:S(2)}) collective-permute-start(bf16[2,96,1280]{2,1,0:T(8,128)(2,1)S(1)} %collective-permute-done.13), channel_id=1, source_target_pairs={{4,0},{6,2},{8,12},{10,14},{5,1},{7,3},{9,13},{11,15},{20,16},{22,... | collective-permute-start | bytes 1474568 | tf_op jit(solution)/shard_map/ppermute | solution.py:132
  115.1 18.7 %collective-permute-start.18 = (bf16[2,96,1280]{2,1,0:T(8,128)(2,1)S(1)}, bf16[2,96,1280]{2,1,0:T(8,128)(2,1)}, u32[]{:S(2)}, u32[]{:S(2)}) collective-permute-start(bf16[2,96,1280]{2,1,0:T(8,128)(2,1)S(1)} %collective-permute-done.12), channel_id=1, source_target_pairs={{4,8},{6,10},{8,4},{10,6},{5,9},{7,11},{9,5},{11,7},{20,24},{22,26... | collective-permute-start | bytes 1474568 | tf_op jit(solution)/shard_map/ppermute | solution.py:132
  116.8 1.3 copy-start.3
  118.1 1.6 copy-start.4
  125.7 9.4 %copy-start.6 = (f32[4,2,192,512]{3,2,1,0:T(8,128)S(1)}, f32[4,2,192,512]{3,2,1,0:T(8,128)}, u32[]{:S(2)}) copy-start(f32[4,2,192,512]{3,2,1,0:T(8,128)} %shard_map.71) | copy-start | bytes 9437188
  127.6 12.2 %collective-permute-start.22 = (f16[2,96,1280]{2,1,0:T(8,128)(2,1)S(1)}, f16[2,96,1280]{2,1,0:T(8,128)(2,1)S(1)}, u32[]{:S(2)}, u32[]{:S(2)}) collective-permute-start(f16[2,96,1280]{2,1,0:T(8,128)(2,1)S(1)} %get-tuple-element.153), channel_id=1, source_target_pairs={{0,4},{2,6},{12,8},{14,10},{4,0},{6,2},{8,12},{10,14},{1,5},{3,7},... | collective-permute-start | bytes 1474568 | tf_op jit(solution)/shard_map/ppermute | solution.py:132
  133.1 6.8 %collective-permute-start.23 = (f16[2,96,1280]{2,1,0:T(8,128)(2,1)S(1)}, f16[2,96,1280]{2,1,0:T(8,128)(2,1)S(1)}, u32[]{:S(2)}, u32[]{:S(2)}) collective-permute-start(f16[2,96,1280]{2,1,0:T(8,128)(2,1)S(1)} %get-tuple-element.154), channel_id=1, source_target_pairs={{4,8},{6,10},{8,4},{10,6},{5,9},{7,11},{9,5},{11,7},{20,24},{22,26... | collective-permute-start | bytes 1474568 | tf_op jit(solution)/shard_map/ppermute | solution.py:132
  133.8 19.4 %collective-permute-start.21 = (bf16[2,96,1280]{2,1,0:T(8,128)(2,1)}, bf16[2,96,1280]{2,1,0:T(8,128)(2,1)S(1)}, u32[]{:S(2)}, u32[]{:S(2)}) collective-permute-start(bf16[2,96,1280]{2,1,0:T(8,128)(2,1)} %collective-permute-done.18), channel_id=1, source_target_pairs={{4,0},{6,2},{8,12},{10,14},{5,1},{7,3},{9,13},{11,15},{20,16},{22,... | collective-permute-start | bytes 1474568 | tf_op jit(solution)/shard_map/ppermute | solution.py:132
  135.2 19.8 %collective-permute-start.26 = (f16[2,192,512]{2,1,0:T(8,128)(2,1)S(1)}, f16[2,192,512]{2,1,0:T(8,128)(2,1)S(1)}, u32[]{:S(2)}, u32[]{:S(2)}) collective-permute-start(f16[2,192,512]{2,1,0:T(8,128)(2,1)S(1)} %fusion.40), channel_id=1, source_target_pairs={{0,4},{2,6},{12,8},{14,10},{1,5},{3,7},{13,9},{15,11},{16,20},{18,... | collective-permute-start | bytes 1179656 | tf_op jit(solution)/shard_map/ppermute | solution.py:132
  143.3 20.6 %collective-permute-start.24 = (bf16[2,96,1280]{2,1,0:T(8,128)(2,1)}, bf16[2,96,1280]{2,1,0:T(8,128)(2,1)}, u32[]{:S(2)}, u32[]{:S(2)}) collective-permute-start(bf16[2,96,1280]{2,1,0:T(8,128)(2,1)} %pad_maximum_fusion.7), channel_id=1, source_target_pairs={{0,4},{2,6},{12,8},{14,10},{4,0},{6,2},{8,12},{10,14},{1,5},{3,7},... | collective-permute-start | bytes 1474568 | tf_op jit(solution)/shard_map/ppermute | solution.py:132
  151.7 12.2 %collective-permute-start.25 = (bf16[2,96,1280]{2,1,0:T(8,128)(2,1)}, bf16[2,96,1280]{2,1,0:T(8,128)(2,1)}, u32[]{:S(2)}, u32[]{:S(2)}) collective-permute-start(bf16[2,96,1280]{2,1,0:T(8,128)(2,1)} %pad_maximum_fusion.7), channel_id=1, source_target_pairs={{4,8},{6,10},{8,4},{10,6},{5,9},{7,11},{9,5},{11,7},{20,24},{22,26... | collective-permute-start | bytes 1474568 | tf_op jit(solution)/shard_map/ppermute | solution.py:132
  155.8 14.0 %collective-permute-start.29 = (f16[2,192,512]{2,1,0:T(8,128)(2,1)}, f16[2,192,512]{2,1,0:T(8,128)(2,1)}, u32[]{:S(2)}, u32[]{:S(2)}) collective-permute-start(f16[2,192,512]{2,1,0:T(8,128)(2,1)} %fusion.41), channel_id=1, source_target_pairs={{0,4},{2,6},{12,8},{14,10},{1,5},{3,7},{13,9},{15,11},{16,20},{18,... | collective-permute-start | bytes 1179656 | tf_op jit(solution)/shard_map/ppermute | solution.py:132
  162.1 7.7 %collective-permute-start.30 = (f16[2,192,512]{2,1,0:T(8,128)(2,1)}, f16[2,192,512]{2,1,0:T(8,128)(2,1)}, u32[]{:S(2)}, u32[]{:S(2)}) collective-permute-start(f16[2,192,512]{2,1,0:T(8,128)(2,1)} %fusion.20), channel_id=1, source_target_pairs={{4,8},{6,10},{8,4},{10,6},{5,9},{7,11},{9,5},{11,7},{20,24},{22,26... | collective-permute-start | bytes 1179656 | tf_op jit(solution)/shard_map/ppermute | solution.py:132
  163.5 22.1 %copy-start.7 = (f32[4,2,192,512]{3,2,1,0:T(8,128)S(1)}, f32[4,2,192,512]{3,2,1,0:T(8,128)}, u32[]{:S(2)}) copy-start(f32[4,2,192,512]{3,2,1,0:T(8,128)} %shard_map.71) | copy-start | bytes 9437188
  163.9 20.4 %collective-permute-start.27 = (bf16[2,96,1280]{2,1,0:T(8,128)(2,1)}, bf16[2,96,1280]{2,1,0:T(8,128)(2,1)S(1)}, u32[]{:S(2)}, u32[]{:S(2)}) collective-permute-start(bf16[2,96,1280]{2,1,0:T(8,128)(2,1)} %collective-permute-done.25), channel_id=1, source_target_pairs={{4,0},{6,2},{8,12},{10,14},{5,1},{7,3},{9,13},{11,15},{20,16},{22,... | collective-permute-start | bytes 1474568 | tf_op jit(solution)/shard_map/ppermute | solution.py:132
  165.3 19.0 %collective-permute-start.28 = (bf16[2,96,1280]{2,1,0:T(8,128)(2,1)}, bf16[2,96,1280]{2,1,0:T(8,128)(2,1)S(1)}, u32[]{:S(2)}, u32[]{:S(2)}) collective-permute-start(bf16[2,96,1280]{2,1,0:T(8,128)(2,1)} %collective-permute-done.24), channel_id=1, source_target_pairs={{4,8},{6,10},{8,4},{10,6},{5,9},{7,11},{9,5},{11,7},{20,24},{22,26... | collective-permute-start | bytes 1474568 | tf_op jit(solution)/shard_map/ppermute | solution.py:132
  171.9 13.6 %collective-permute-start.31 = (f16[2,192,512]{2,1,0:T(8,128)(2,1)S(1)}, f16[2,192,512]{2,1,0:T(8,128)(2,1)S(1)}, u32[]{:S(2)}, u32[]{:S(2)}) collective-permute-start(f16[2,192,512]{2,1,0:T(8,128)(2,1)S(1)} %get-tuple-element.157), channel_id=1, source_target_pairs={{0,4},{2,6},{12,8},{14,10},{4,0},{6,2},{8,12},{10,14},{1,5},{3,7},... | collective-permute-start | bytes 1179656 | tf_op jit(solution)/shard_map/ppermute | solution.py:132
  174.5 11.0 %collective-permute-start.32 = (f16[2,192,512]{2,1,0:T(8,128)(2,1)S(1)}, f16[2,192,512]{2,1,0:T(8,128)(2,1)S(1)}, u32[]{:S(2)}, u32[]{:S(2)}) collective-permute-start(f16[2,192,512]{2,1,0:T(8,128)(2,1)S(1)} %get-tuple-element.158), channel_id=1, source_target_pairs={{4,8},{6,10},{8,4},{10,6},{5,9},{7,11},{9,5},{11,7},{20,24},{22,26... | collective-permute-start | bytes 1179656 | tf_op jit(solution)/shard_map/ppermute | solution.py:132
  177.0 53.7 %collective-permute-start.41 = (bf16[4,2,96,1280]{3,2,1,0:T(8,128)(2,1)}, bf16[4,2,96,1280]{3,2,1,0:T(8,128)(2,1)}, u32[]{:S(2)}, u32[]{:S(2)}) collective-permute-start(bf16[4,2,96,1280]{3,2,1,0:T(8,128)(2,1)} %get-tuple-element.162), channel_id=1, source_target_pairs={{0,2},{2,0},{4,6},{6,4},{8,10},{10,8},{12,14},{14,12},{1,3},{3,1},... | collective-permute-start | bytes 5898248 | tf_op jit(solution)/shard_map/ppermute | solution.py:132
  184.3 11.6 %collective-permute-start.36 = (bf16[2,96,1280]{2,1,0:T(8,128)(2,1)S(1)}, bf16[2,96,1280]{2,1,0:T(8,128)(2,1)S(1)}, u32[]{:S(2)}, u32[]{:S(2)}) collective-permute-start(bf16[2,96,1280]{2,1,0:T(8,128)(2,1)S(1)} %collective-permute-done.28), channel_id=1, source_target_pairs={{4,0},{6,2},{8,12},{10,14},{5,1},{7,3},{9,13},{11,15},{20,16},{22,... | collective-permute-start | bytes 1474568 | tf_op jit(solution)/shard_map/ppermute | solution.py:132
  185.9 0.9 copy-start.15
  185.9 1.1 copy-start.16
  186.2 4.3 %copy-start.8 = (bf16[1,192,512]{2,1,0:T(8,128)(2,1)}, bf16[1,192,512]{2,1,0:T(8,128)(2,1)S(1)}, u32[]{:S(2)}) copy-start(bf16[1,192,512]{2,1,0:T(8,128)(2,1)S(1)} %get-tuple-element.171) | copy-start | bytes 589828
  186.2 4.3 %copy-start.10 = (bf16[1,192,512]{2,1,0:T(8,128)(2,1)}, bf16[1,192,512]{2,1,0:T(8,128)(2,1)S(1)}, u32[]{:S(2)}) copy-start(bf16[1,192,512]{2,1,0:T(8,128)(2,1)S(1)} %get-tuple-element.172) | copy-start | bytes 589828
  187.9 16.7 %collective-permute-start.33 = (bf16[2,48,1792]{2,1,0:T(8,128)(2,1)}, bf16[2,48,1792]{2,1,0:T(8,128)(2,1)}, u32[]{:S(2)}, u32[]{:S(2)}) collective-permute-start(bf16[2,48,1792]{2,1,0:T(8,128)(2,1)} %get-tuple-element.184), channel_id=1, source_target_pairs={{0,2},{2,0},{4,6},{6,4},{8,10},{10,8},{12,14},{14,12},{1,3},{3,1},... | collective-permute-start | bytes 1032200 | tf_op jit(solution)/shard_map/ppermute | solution.py:132
  199.6 31.2 %collective-permute-start.42 = (bf16[4,2,96,1280]{3,2,1,0:T(8,128)(2,1)}, bf16[4,2,96,1280]{3,2,1,0:T(8,128)(2,1)}, u32[]{:S(2)}, u32[]{:S(2)}) collective-permute-start(bf16[4,2,96,1280]{3,2,1,0:T(8,128)(2,1)} %get-tuple-element.160), channel_id=1, source_target_pairs={{0,2},{2,0},{4,6},{6,4},{8,10},{10,8},{12,14},{14,12},{1,3},{3,1},... | collective-permute-start | bytes 5898248 | tf_op jit(solution)/shard_map/ppermute | solution.py:132
  203.5 14.0 %copy-start.5 = (bf16[4,1,2,96,1280]{4,3,2,1,0:T(8,128)(2,1)S(1)}, bf16[4,1,2,96,1280]{4,3,2,1,0:T(8,128)(2,1)}, u32[]{:S(2)}) copy-start(bf16[4,1,2,96,1280]{4,3,2,1,0:T(8,128)(2,1)} %get-tuple-element.159.refs_1_) | copy-start | bytes 5898244
  203.5 11.0 %collective-permute-start.34 = (bf16[2,192,512]{2,1,0:T(8,128)(2,1)}, bf16[2,192,512]{2,1,0:T(8,128)(2,1)S(1)}, u32[]{:S(2)}, u32[]{:S(2)}) collective-permute-start(bf16[2,192,512]{2,1,0:T(8,128)(2,1)} %pad_maximum_fusion.8), channel_id=1, source_target_pairs={{0,4},{2,6},{12,8},{14,10},{4,0},{6,2},{8,12},{10,14},{1,5},{3,7},... | collective-permute-start | bytes 1179656 | tf_op jit(solution)/shard_map/ppermute | solution.py:132
  203.7 10.7 %collective-permute-start.35 = (bf16[2,192,512]{2,1,0:T(8,128)(2,1)}, bf16[2,192,512]{2,1,0:T(8,128)(2,1)S(1)}, u32[]{:S(2)}, u32[]{:S(2)}) collective-permute-start(bf16[2,192,512]{2,1,0:T(8,128)(2,1)} %pad_maximum_fusion.8), channel_id=1, source_target_pairs={{4,8},{6,10},{8,4},{10,6},{5,9},{7,11},{9,5},{11,7},{20,24},{22,26... | collective-permute-start | bytes 1179656 | tf_op jit(solution)/shard_map/ppermute | solution.py:132
  214.4 10.0 %collective-permute-start.39 = (bf16[2,192,512]{2,1,0:T(8,128)(2,1)S(1)}, bf16[2,192,512]{2,1,0:T(8,128)(2,1)S(1)}, u32[]{:S(2)}, u32[]{:S(2)}) collective-permute-start(bf16[2,192,512]{2,1,0:T(8,128)(2,1)S(1)} %collective-permute-done.34), channel_id=1, source_target_pairs={{4,8},{6,10},{8,4},{10,6},{5,9},{7,11},{9,5},{11,7},{20,24},{22,26... | collective-permute-start | bytes 1179656 | tf_op jit(solution)/shard_map/ppermute | solution.py:132
  215.1 14.2 %collective-permute-start.38 = (bf16[2,192,512]{2,1,0:T(8,128)(2,1)S(1)}, bf16[2,192,512]{2,1,0:T(8,128)(2,1)S(1)}, u32[]{:S(2)}, u32[]{:S(2)}) collective-permute-start(bf16[2,192,512]{2,1,0:T(8,128)(2,1)S(1)} %collective-permute-done.35), channel_id=1, source_target_pairs={{4,0},{6,2},{8,12},{10,14},{5,1},{7,3},{9,13},{11,15},{20,16},{22,... | collective-permute-start | bytes 1179656 | tf_op jit(solution)/shard_map/ppermute | solution.py:132
  217.2 22.6 %collective-permute-start.37 = (bf16[48,3584]{1,0:T(8,128)(2,1)S(1)}, bf16[48,3584]{1,0:T(8,128)(2,1)S(1)}, u32[]{:S(2)}, u32[]{:S(2)}) collective-permute-start(bf16[48,3584]{1,0:T(8,128)(2,1)S(1)} %get-tuple-element.139), channel_id=1, source_target_pairs={{0,1},{1,0},{2,3},{3,2},{4,5},{5,4},{6,7},{7,6},{8,9},{9,8},{10,11... | collective-permute-start | bytes 1032200 | tf_op jit(solution)/shard_map/ppermute | solution.py:282
  217.4 13.2 %copy-start.9 = (bf16[1,192,512]{2,1,0:T(8,128)(2,1)S(1)}, bf16[1,192,512]{2,1,0:T(8,128)(2,1)}, u32[]{:S(2)}) copy-start(bf16[1,192,512]{2,1,0:T(8,128)(2,1)} %copy-done.8) | copy-start | bytes 589828
  217.4 13.2 %copy-start.11 = (bf16[1,192,512]{2,1,0:T(8,128)(2,1)S(1)}, bf16[1,192,512]{2,1,0:T(8,128)(2,1)}, u32[]{:S(2)}) copy-start(bf16[1,192,512]{2,1,0:T(8,128)(2,1)} %copy-done.10) | copy-start | bytes 589828
  229.3 10.5 %collective-permute-start.40 = (bf16[2,192,512]{2,1,0:T(8,128)(2,1)S(1)}, bf16[2,192,512]{2,1,0:T(8,128)(2,1)S(1)}, u32[]{:S(2)}, u32[]{:S(2)}) collective-permute-start(bf16[2,192,512]{2,1,0:T(8,128)(2,1)S(1)} %collective-permute-done.39), channel_id=1, source_target_pairs={{4,0},{6,2},{8,12},{10,14},{5,1},{7,3},{9,13},{11,15},{20,16},{22,... | collective-permute-start | bytes 1179656 | tf_op jit(solution)/shard_map/ppermute | solution.py:132
  239.8 1.5 copy-start.18
  239.8 4.4 %copy-start.14 = (bf16[1,48,3584]{2,1,0:T(8,128)(2,1)S(1)}, bf16[1,48,3584]{2,1,0:T(8,128)(2,1)}, u32[]{:S(2)}) copy-start(bf16[1,48,3584]{2,1,0:T(8,128)(2,1)} %get-tuple-element.181) | copy-start | bytes 1032196
  241.3 8.5 %collective-permute-start.43 = (bf16[4,2,192,512]{3,2,1,0:T(8,128)(2,1)}, bf16[4,2,192,512]{3,2,1,0:T(8,128)(2,1)}, u32[]{:S(2)}, u32[]{:S(2)}) collective-permute-start(bf16[4,2,192,512]{3,2,1,0:T(8,128)(2,1)} %get-tuple-element.164), channel_id=1, source_target_pairs={{0,2},{2,0},{4,6},{6,4},{8,10},{10,8},{12,14},{14,12},{1,3},{3,1},... | collective-permute-start | bytes 4718600 | tf_op jit(solution)/shard_map/ppermute | solution.py:132

commit v12 on v11

--- a/solution.py
+++ b/solution.py
@@ -174,11 +174,11 @@
         values = values.reshape(line, rows, depth)
         return jnp.where(at_far, values[::-1], values)
 
-    def own_features(tokens, k, after):
+    def own_features(tokens, k, after, wire):
         _, start, width = pieces[k]
         tokens = tie(tokens, after).reshape(-1, depth)
         common = ((gate_weight, up_weight), start, width, tile, line, scale)
-        payload = forward(other_tile, [tokens], *common).astype(WIRE)
+        payload = forward(other_tile, [tokens], *common).astype(wire)
 
         def own(after):
             return forward(own_tile, [tie(tokens, payload, after)], *common)
@@ -197,14 +197,21 @@
 
     over_row = tie(over_row, over_depth)
     features = [arrange(by(row == 0, mine, over_row, 1))]
-    theirs, own = own_features(features[0], 0, ())
-    terms = (own(()), send(theirs, pairs))
+    theirs, own = own_features(features[0], 0, (), WIRE)
+    cotangent = tie(grad_hidden[0], features[0])
+    cotangent = jnp.stack(
+        [
+            columns_of(cotangent, part * half, half),
+            lax.ppermute(columns_of(cotangent, (1 - part) * half, half), "depth", swap),
+        ]
+    )
+    terms = tie((own(()), send(theirs, pairs)), cotangent)
     payload = take(terms, 3).astype(WIRE)
     in_1 = send(payload, inward)
 
     over_depth, over_both = tie((over_depth, over_both), payload)
     features.append(arrange(by(row == 0, over_depth, over_both, 1)))
-    theirs, own = own_features(features[1], 1, ())
+    theirs, own = own_features(features[1], 1, (), WIRE)
     terms = tie(terms, theirs)
 
     def activate(k, summed):
@@ -232,8 +239,6 @@
         )
         return blocks, send(blocks, pairs)
 
-    turned = jnp.concatenate([tie(value, in_1).reshape(-1, depth) for value in features]).T
-
     def add_gradients(acts, owner, totals, start):
         where = (owner * (share // tile)).astype(jnp.int32).reshape(1)
         acts = [value[:, None] for value in acts]
@@ -245,42 +250,37 @@
         adding, gathering = k < last, act is not None
         if gathering:
             side_1, centre_1 = send(act, side), send(act, centre)
-        if hops is not None:
-            merged.append(merge(*hops))
-            if adding:
+        if adding:
+            if hops is not None:
+                merged.append(merge(*hops))
                 terms = tie(terms, merged[-1][0])
-            elif last > 1:
-                side_1, centre_1 = tie((side_1, centre_1), merged[-1][0])
-        before = ()
-        if adding:
+            if k == 0:
+                products[2] = all_features(tokens, 2, act)
+                terms = tie(terms, products[2])
             far, near = add(take(terms, 3), in_1).astype(WIRE), take(tie(terms, in_1), 2)
             near = near.astype(WIRE)
             centre_2, in_2 = send(far, centre), send(near, inward)
             before = (in_1,)
+        else:
+            hidden = jnp.stack([jnp.concatenate(parts, axis=1) for parts in hidden])
+            hidden = hidden.reshape(2, 2, slab, share)
+            mine = lax.dynamic_index_in_dim(hidden, core, 1, keepdims=False)
+            theirs = lax.dynamic_index_in_dim(hidden, 1 - core, 1, keepdims=False)
+            theirs = send(theirs, pairs)
+            before = (theirs,)
         if gathering:
             side_1, centre_1 = tie((side_1, centre_1), before)
             out_2, share_2 = send(centre_1, outward), send(side_1, centre)
         if k < 0:
             products[1] = (own((far, near)), send(theirs, pairs))
-            cotangent = tie(grad_hidden[0], far, near)
-            theirs = lax.ppermute(columns_of(cotangent, (1 - part) * half, half), "depth", swap)
-            cotangent = jnp.stack([columns_of(cotangent, part * half, half), theirs])
-            terms = tie(terms, products[1][0], theirs)
-        if k == 0:
-            products[2] = all_features(tokens, 2, (side_1, centre_1))
-            terms = tie(terms, products[2])
+            terms = tie(terms, products[1])
         if not adding:
-            hidden = jnp.stack([jnp.concatenate(parts, axis=1) for parts in hidden])
-            hidden = hidden.reshape(2, 2, slab, share)
-            mine = lax.dynamic_index_in_dim(hidden, core, 1, keepdims=False)
-            theirs = lax.dynamic_index_in_dim(hidden, 1 - core, 1, keepdims=False)
-            theirs = send(theirs, pairs)
+            merged.append(merge(*tie(hops, side_1, centre_1)))
             own_acts, other_acts = zip(*merged)
             totals = add_gradients(own_acts, core, (), pieces[0][1])
-            share_2 = tie(share_2, totals, theirs)
+            share_2 = tie(share_2, totals)
             hidden = by(core == 0, mine, theirs, 2)
             theirs = lax.ppermute(tie(hidden[1], side_1), "depth", swap)
-        before = ()
         if adding:
             if gathering:
                 terms = tie(terms, side_1, centre_1)
@@ -303,23 +303,25 @@
             far_weights = exchange_weights(2, (near, swapped))
             tokens = jnp.stack(tie(features, near, swapped), axis=1)
             tokens = (tokens, send(tokens, pairs))
+        if k == 0:
+            turned = [value.reshape(-1, depth) for value in tie(features, near, swapped)]
+            turned = jnp.concatenate(turned).T
             terms = tie(terms, turned)
         if gathering:
             out_2, share_2 = tie((out_2, share_2), before)
             out_3 = send(share_2, outward)
-        if not adding:
-            totals = add_gradients(other_acts, 1 - core, totals, pieces[0][1])
-            out_3 = tie(out_3, totals, theirs)
-            hidden = by(part == 0, hidden[0], theirs, 1)
         if adding:
             if gathering:
                 terms = tie(terms, out_2, share_2)
-            own = jnp.where(at_end, take(terms, 0), take(terms, 1))
-            ready = activate(k + 1, add(own, side_3, centre_3))
+            own_sum = jnp.where(at_end, take(terms, 0), take(terms, 1))
+            ready = activate(k + 1, add(own_sum, side_3, centre_3))
             if gathering:
                 hops = tie((act, side_1, centre_1, out_2, share_2, out_3), ready)
             act, terms = ready, products.get(k + 2)
         else:
+            totals = add_gradients(other_acts, 1 - core, totals, pieces[0][1])
+            hidden = by(part == 0, hidden[0], theirs, 1)
+            out_3 = tie(out_3, totals, hidden)
             own_acts, other_acts = merge(act, side_1, centre_1, out_2, share_2, out_3)
     totals = add_gradients([own_acts], core, totals, pieces[last][1])
     totals = add_gradients([other_acts], 1 - core, totals, pieces[last][1])

time: 256 us -> 252 us (0.984)
  other arithmetic: 44.1 us -> 38.6 us
  starting transfers between devices: 91.5 us -> 86.6 us
  waiting for transfers between devices: 49.9 us -> 54.8 us
    ppermute x1, waiting for transfers between devices: 0.01 us -> 9.78 us  [local(): theirs = lax.ppermute(tie(hidden[1], side_1), 'depth', swap)]
    ppermute x39, waiting for transfers between devices: 37.5 us -> 30.5 us  [send(): return lax.ppermute(value, 'col', route)]
    ppermute x1, waiting for transfers between devices: 0.82 us -> 7.84 us  [local(): over_depth = lax.ppermute(mine, 'depth', swap)]
    ppermute x1, waiting for transfers between devices: 7.81 us -> 0.82 us  [local(): over_row = lax.ppermute(mine, 'row', swap)]
    ppermute x39, starting transfers between devices: 85.3 us -> 81.5 us  [send(): return lax.ppermute(value, 'col', route)]
    another operation x8 -> x9, other arithmetic: 1.76 us -> 5.16 us  [merge(): jnp.stack([jnp.where(at_end, act, side_1), jnp.where(at_end, side_1, act)...]
    convert_element_type x3, other arithmetic: 4.72 us -> 1.8 us  [local(): near = near.astype(WIRE)]
    ppermute x1, waiting for transfers between devices: 0.01 us -> 2.84 us  [local(): lax.ppermute(columns_of(cotangent, (1 - part) * half, half), 'depth', swap)]
  transfers between devices with their start and end apart: 44 -> 44, of which waited for: 11 -> 16; matrix products, arithmetic and copies ran while one was open for 17% -> 17% of each run, Pallas kernels for 17% -> 17%
where the time goes in v12:
time: 252 us; the launch traced here: 250 us
  starting transfers between devices  86.6 us (34%)
  waiting for transfers between devices  54.8 us (22%)
  Pallas kernels  52.7 us (21%)
  other arithmetic  38.6 us (15%)
  local copies, waits for them, and re-layouts  15.8 us (6%)
    ppermute x39, starting transfers between devices, send(): return lax.ppermute(value, 'col', route)  81.5 us
    ppermute x39, waiting for transfers between devices, send(): return lax.ppermute(value, 'col', route)  30.5 us
    pallas_call x5, Pallas kernels, forward(): pl.pallas_call(functools.partial(forward_kernel, scale), out_shape=jax.Sh...  28.8 us
    pallas_call x4, Pallas kernels, gradient(): pl.pallas_call(functools.partial(gradient_kernel, len(acts)), out_shape=(...  23.9 us
    ppermute x1, waiting for transfers between devices, local(): theirs = lax.ppermute(tie(hidden[1], side_1), 'depth', swap)  9.78 us
    ppermute x1, waiting for transfers between devices, local(): over_depth = lax.ppermute(mine, 'depth', swap)  7.84 us
    select_n x5, other arithmetic, by(): jnp.where(first, jnp.concatenate([mine, theirs], axis=axis), jnp.concaten...  5.3 us
    convert_element_type x3, other arithmetic, local(): swapped = swapped.astype(WIRE)  5.21 us
  transfers between devices with their start and end apart: 44, of which 16 were waited for; matrix products, arithmetic and copies ran while one was open for 17% of the time, Pallas kernels for 17%

profile of v12, /device:TPU:1, one launch (start us, length us, event | category | flops | bytes accessed | tf_op | source)
XLA Modules:
  0.0 249.9 jit_solution(8023400272170960453)
XLA Ops:
  0.6 2.1 collective-permute-start.1
  4.0 7.8 %collective-permute-done.1 = bf16[384,512]{1,0:T(8,128)(2,1)S(1)} collective-permute-done((bf16[384,512]{1,0:T(8,128)(2,1)}, bf16[384,512]{1,0:T(8,128)(2,1)S(1)}, u32[]{:S(2)}, u32[]{:S(2)}) %collective-permute-start.1) | collective-permute-done | bytes 393248 | tf_op jit(solution)/shard_map/ppermute | solution.py:166
  13.4 1.3 maximum_select_fusion
  14.9 5.6 %shard_map.67 = f32[4,2,96,1280]{3,2,1,0:T(8,128)S(1)} custom-call(s32[1]{0:T(128)} %bitcast.5.place_ref, bf16[384,1024]{1,0:T(8,128)(2,1)S(1)} %bitcast.187, bf16[1024,7168]{1,0:T(8,128)(2,1)} %refs_2_.9, bf16[1024,7168]{1,0:T(8,128)(2,1)} %refs_3_.1), custom_call_target="tpu_custom_call" | custom-call | tf_op jit(solution)/shard_map/pallas_call | solution.py:45
  20.5 1.5 convert_element_type.191
  22.0 1.9 collective-permute-start.2
  23.9 1.8 dynamic-slice_bitcast_fusion.4
  25.8 5.6 %shard_map.68 = f32[4,2,96,1280]{3,2,1,0:T(8,128)S(1)} custom-call(s32[1]{0:T(128)} %bitcast.place_ref, bf16[384,1024]{1,0:T(8,128)(2,1)S(1)} %bitcast.188, bf16[1024,7168]{1,0:T(8,128)(2,1)} %refs_2_.9, bf16[1024,7168]{1,0:T(8,128)(2,1)} %refs_3_.1), custom_call_target="tpu_custom_call" | custom-call | tf_op jit(solution)/shard_map/pallas_call | solution.py:45
  31.4 1.5 collective-permute-start.4
  32.9 2.8 %collective-permute-done.3 = bf16[48,3584]{1,0:T(8,128)(2,1)} collective-permute-done((bf16[48,3584]{1,0:T(8,128)(2,1)}, bf16[48,3584]{1,0:T(8,128)(2,1)}, u32[]{:S(2)}, u32[]{:S(2)}) %collective-permute-start.3) | collective-permute-done | bytes 344096 | tf_op jit(solution)/shard_map/ppermute | solution.py:205
  35.7 1.9 pad_maximum_fusion.5
  37.8 3.2 %collective-permute-start.5 = (f16[2,96,1280]{2,1,0:T(8,128)(2,1)S(1)}, f16[2,96,1280]{2,1,0:T(8,128)(2,1)S(1)}, u32[]{:S(2)}, u32[]{:S(2)}) collective-permute-start(f16[2,96,1280]{2,1,0:T(8,128)(2,1)S(1)} %fusion.28), channel_id=1, source_target_pairs={{0,4},{2,6},{12,8},{14,10},{1,5},{3,7},{13,9},{15,11},{16,20},{18,... | collective-permute-start | bytes 1474568 | tf_op jit(solution)/shard_map/ppermute | solution.py:132
  41.0 3.1 %collective-permute-done.4 = bf16[384,512]{1,0:T(8,128)(2,1)S(1)} collective-permute-done((bf16[384,512]{1,0:T(8,128)(2,1)S(1)}, bf16[384,512]{1,0:T(8,128)(2,1)S(1)}, u32[]{:S(2)}, u32[]{:S(2)}) %collective-permute-start.4) | collective-permute-done | bytes 393248 | tf_op jit(solution)/shard_map/ppermute | solution.py:167
  44.5 5.6 %shard_map.69 = f32[4,2,96,1280]{3,2,1,0:T(8,128)S(1)} custom-call(s32[1]{0:T(128)} %bitcast.5.place_ref, bf16[384,1024]{1,0:T(8,128)(2,1)S(1)} %bitcast.191, bf16[1024,7168]{1,0:T(8,128)(2,1)} %refs_2_.9, bf16[1024,7168]{1,0:T(8,128)(2,1)} %refs_3_.1), custom_call_target="tpu_custom_call" | custom-call | tf_op jit(solution)/shard_map/pallas_call | solution.py:45
  50.1 1.5 convert_element_type.195
  53.4 1.5 collective-permute-start.7
  55.7 5.8 %collective-permute-start.9 = (f16[2,96,1280]{2,1,0:T(8,128)(2,1)}, f16[2,96,1280]{2,1,0:T(8,128)(2,1)}, u32[]{:S(2)}, u32[]{:S(2)}) collective-permute-start(f16[2,96,1280]{2,1,0:T(8,128)(2,1)} %fusion.29), channel_id=1, source_target_pairs={{0,4},{2,6},{12,8},{14,10},{1,5},{3,7},{13,9},{15,11},{16,20},{18,... | collective-permute-start | bytes 1474568 | tf_op jit(solution)/shard_map/ppermute | solution.py:132
  61.5 6.1 %shard_map.70 = f32[4,2,96,1280]{3,2,1,0:T(8,128)S(1)} custom-call(s32[1]{0:T(128)} %bitcast.place_ref, bf16[384,1024]{1,0:T(8,128)(2,1)S(1)} %bitcast.192, bf16[1024,7168]{1,0:T(8,128)(2,1)} %refs_2_.9, bf16[1024,7168]{1,0:T(8,128)(2,1)} %refs_3_.1), custom_call_target="tpu_custom_call" | custom-call | tf_op jit(solution)/shard_map/pallas_call | solution.py:45
  67.6 2.7 %collective-permute-done.9 = f16[2,96,1280]{2,1,0:T(8,128)(2,1)} collective-permute-done((f16[2,96,1280]{2,1,0:T(8,128)(2,1)}, f16[2,96,1280]{2,1,0:T(8,128)(2,1)}, u32[]{:S(2)}, u32[]{:S(2)}) %collective-permute-start.9) | collective-permute-done | bytes 491552 | tf_op jit(solution)/shard_map/ppermute | solution.py:132
  70.3 1.6 fusion.10
  71.9 2.3 collective-permute-start.8
  75.0 2.4 collective-permute-start.12
  78.3 4.1 %collective-permute-start.16 = (f16[2,96,1280]{2,1,0:T(8,128)(2,1)}, f16[2,96,1280]{2,1,0:T(8,128)(2,1)}, u32[]{:S(2)}, u32[]{:S(2)}) collective-permute-start(f16[2,96,1280]{2,1,0:T(8,128)(2,1)} %fusion.30), channel_id=1, source_target_pairs={{0,4},{2,6},{12,8},{14,10},{1,5},{3,7},{13,9},{15,11},{16,20},{18,... | collective-permute-start | bytes 1474568 | tf_op jit(solution)/shard_map/ppermute | solution.py:132
  82.4 1.3 dynamic-slice_bitcast_fusion.1
  83.7 1.3 dynamic-slice_bitcast_fusion
  91.9 6.0 %shard_map.71 = f32[4,2,192,512]{3,2,1,0:T(8,128)} custom-call(s32[1]{0:T(128)} %bitcast.place_ref, bf16[768,1024]{1,0:T(8,128)(2,1)S(1)} %bitcast.195, bf16[768,1024]{1,0:T(8,128)(2,1)S(1)} %bitcast.196, bf16[1024,7168]{1,0:T(8,128)(2,1)} %refs_2_.9, bf16[1024,7168]{1,0:T(8,128)(2,1)} %refs_3_.1, ...), custom_call_target="tpu_custom_call" | custom-call | tf_op jit(solution)/shard_map/pallas_call | solution.py:45
  100.0 3.7 %collective-permute-start.19 = (f16[2,96,1280]{2,1,0:T(8,128)(2,1)S(1)}, f16[2,96,1280]{2,1,0:T(8,128)(2,1)S(1)}, u32[]{:S(2)}, u32[]{:S(2)}) collective-permute-start(f16[2,96,1280]{2,1,0:T(8,128)(2,1)S(1)} %fusion.31), channel_id=1, source_target_pairs={{0,4},{2,6},{12,8},{14,10},{1,5},{3,7},{13,9},{15,11},{16,20},{18,... | collective-permute-start | bytes 1474568 | tf_op jit(solution)/shard_map/ppermute | solution.py:132
  103.7 1.5 collective-permute-start.18
  106.5 8.2 %collective-permute-done.19 = f16[2,96,1280]{2,1,0:T(8,128)(2,1)S(1)} collective-permute-done((f16[2,96,1280]{2,1,0:T(8,128)(2,1)S(1)}, f16[2,96,1280]{2,1,0:T(8,128)(2,1)S(1)}, u32[]{:S(2)}, u32[]{:S(2)}) %collective-permute-start.19) | collective-permute-done | bytes 491552 | tf_op jit(solution)/shard_map/ppermute | solution.py:132
  114.7 1.4 fusion.3
  116.1 2.2 collective-permute-start.22
  118.3 1.4 collective-permute-start.23
  124.2 1.6 maximum_bitcast_fusion.features_ref
  127.1 5.1 %collective-permute-start.26 = (f16[2,192,512]{2,1,0:T(8,128)(2,1)S(1)}, f16[2,192,512]{2,1,0:T(8,128)(2,1)S(1)}, u32[]{:S(2)}, u32[]{:S(2)}) collective-permute-start(f16[2,192,512]{2,1,0:T(8,128)(2,1)S(1)} %fusion.37), channel_id=1, source_target_pairs={{0,4},{2,6},{12,8},{14,10},{1,5},{3,7},{13,9},{15,11},{16,20},{18,... | collective-permute-start | bytes 1179656 | tf_op jit(solution)/shard_map/ppermute | solution.py:132
  132.2 1.6 fusion.1
  135.7 1.5 collective-permute-start.25
  137.1 2.2 collective-permute-start.24
  139.3 1.7 collective-permute-done.21
  142.3 1.6 fusion.41
  146.6 1.4 collective-permute-start.30
  148.0 2.5 collective-permute-start.29
  153.0 3.9 %collective-permute-done.29 = f16[2,192,512]{2,1,0:T(8,128)(2,1)} collective-permute-done((f16[2,192,512]{2,1,0:T(8,128)(2,1)}, f16[2,192,512]{2,1,0:T(8,128)(2,1)}, u32[]{:S(2)}, u32[]{:S(2)}) %collective-permute-start.29) | collective-permute-done | bytes 393248 | tf_op jit(solution)/shard_map/ppermute | solution.py:132
  156.9 2.2 fusion.14
  159.1 2.3 collective-permute-start.31
  163.9 1.3 collective-permute-start.39
  165.2 6.1 %collective-permute-done.31 = f16[2,192,512]{2,1,0:T(8,128)(2,1)S(1)} collective-permute-done((f16[2,192,512]{2,1,0:T(8,128)(2,1)S(1)}, f16[2,192,512]{2,1,0:T(8,128)(2,1)S(1)}, u32[]{:S(2)}, u32[]{:S(2)}) %collective-permute-start.31) | collective-permute-done | bytes 393248 | tf_op jit(solution)/shard_map/ppermute | solution.py:132
  172.6 7.4 %collective-permute-start.34 = (bf16[2,192,512]{2,1,0:T(8,128)(2,1)S(1)}, bf16[2,192,512]{2,1,0:T(8,128)(2,1)S(1)}, u32[]{:S(2)}, u32[]{:S(2)}) collective-permute-start(bf16[2,192,512]{2,1,0:T(8,128)(2,1)S(1)} %pad_maximum_fusion.8), channel_id=1, source_target_pairs={{0,4},{2,6},{12,8},{14,10},{4,0},{6,2},{8,12},{10,14},{1,5},{3,7},... | collective-permute-start | bytes 1179656 | tf_op jit(solution)/shard_map/ppermute | solution.py:132
  181.0 5.9 %collective-permute-start.33 = (bf16[2,48,1792]{2,1,0:T(8,128)(2,1)S(1)}, bf16[2,48,1792]{2,1,0:T(8,128)(2,1)S(1)}, u32[]{:S(2)}, u32[]{:S(2)}) collective-permute-start(bf16[2,48,1792]{2,1,0:T(8,128)(2,1)S(1)} %get-tuple-element.196), channel_id=1, source_target_pairs={{0,2},{2,0},{4,6},{6,4},{8,10},{10,8},{12,14},{14,12},{1,3},{3,1},... | collective-permute-start | bytes 1032200 | tf_op jit(solution)/shard_map/ppermute | solution.py:132
  186.9 1.7 collective-permute-done.33
  188.6 1.6 collective-permute-done.34
  190.2 1.4 select_bitcast_fusion.3
  191.8 2.2 pad_maximum_fusion.2
  194.1 6.4 %collective-permute-start.42 = (bf16[4,2,96,1280]{3,2,1,0:T(8,128)(2,1)}, bf16[4,2,96,1280]{3,2,1,0:T(8,128)(2,1)}, u32[]{:S(2)}, u32[]{:S(2)}) collective-permute-start(bf16[4,2,96,1280]{3,2,1,0:T(8,128)(2,1)} %get-tuple-element.171), channel_id=1, source_target_pairs={{0,2},{2,0},{4,6},{6,4},{8,10},{10,8},{12,14},{14,12},{1,3},{3,1},... | collective-permute-start | bytes 5898248 | tf_op jit(solution)/shard_map/ppermute | solution.py:132
  202.4 1.5 maximum_select_fusion.3
  204.0 1.5 copy-done.4
  205.6 7.1 %shard_map.72 = (f32[1024,3584]{1,0:T(8,128)}, f32[1024,3584]{1,0:T(8,128)}) custom-call(s32[1]{0:T(128)} %bitcast.68.place_ref, bf16[1024,768]{1,0:T(8,128)(2,1)S(1)} %maximum_bitcast_fusion.features_ref, bf16[4,1,2,96,1280]{4,3,2,1,0:T(8,128)(2,1)S(1)} %get-tuple-element.173.refs_0_, bf16[4,1,2,96,1280]{4,3,2,1,0:T(8,128)(2,1)S(1)} %copy-done.4), custom_call_target="tpu_custom_call" | custom-call | tf_op jit(solution)/shard_map/pallas_call | solution.py:83
  214.8 9.0 %shard_map.73 = (f32[1024,3584]{1,0:T(8,128)}, f32[1024,3584]{1,0:T(8,128)}) custom-call(s32[1]{0:T(128)} %bitcast.65.place_ref, bf16[1024,768]{1,0:T(8,128)(2,1)S(1)} %maximum_bitcast_fusion.features_ref, bf16[4,1,2,96,1280]{4,3,2,1,0:T(8,128)(2,1)} %bitcast.79.refs_0_, ...), custom_call_target="tpu_custom_call", output_to_operand_aliasing={{0}: (4, {}), {1}: (5, {})} | custom-call | tf_op jit(solution)/shard_map/pallas_call | solution.py:83
  223.8 2.3 collective-permute-done.40
  226.1 1.4 fusion.39
  227.5 1.7 collective-permute-start.43
  230.2 9.8 %collective-permute-done.36 = bf16[48,3584]{1,0:T(8,128)(2,1)} collective-permute-done((bf16[48,3584]{1,0:T(8,128)(2,1)}, bf16[48,3584]{1,0:T(8,128)(2,1)}, u32[]{:S(2)}, u32[]{:S(2)}) %collective-permute-start.36) | collective-permute-done | bytes 344096 | tf_op jit(solution)/shard_map/ppermute | solution.py:283
  240.0 2.1 maximum_select_fusion.4
  242.0 3.4 %shard_map.74 = (f32[1024,3584]{1,0:T(8,128)}, f32[1024,3584]{1,0:T(8,128)}) custom-call(s32[1]{0:T(128)} %bitcast.68.place_ref, bf16[1024,768]{1,0:T(8,128)(2,1)S(1)} %maximum_bitcast_fusion.features_ref, bf16[4,1,2,192,512]{4,3,2,1,0:T(8,128)(2,1)S(1)} %get-tuple-element.175.refs_0_, ...), custom_call_target="tpu_custom_call", output_to_operand_aliasing={{0}: (3, {}), {1}: (4, {})} | custom-call | tf_op jit(solution)/shard_map/pallas_call | solution.py:83
  245.5 4.4 %shard_map.75 = (f32[1024,3584]{1,0:T(8,128)}, f32[1024,3584]{1,0:T(8,128)}) custom-call(s32[1]{0:T(128)} %bitcast.65.place_ref, bf16[1024,768]{1,0:T(8,128)(2,1)S(1)} %maximum_bitcast_fusion.features_ref, bf16[4,1,2,192,512]{4,3,2,1,0:T(8,128)(2,1)} %bitcast.82.refs_0_, ...), custom_call_target="tpu_custom_call", output_to_operand_aliasing={{0}: (3, {}), {1}: (4, {})} | custom-call | tf_op jit(solution)/shard_map/pallas_call | solution.py:83
  (163 shorter events, 42.0 us)
Async XLA Ops:
  0.6 11.2 %collective-permute-start.1 = (bf16[384,512]{1,0:T(8,128)(2,1)}, bf16[384,512]{1,0:T(8,128)(2,1)S(1)}, u32[]{:S(2)}, u32[]{:S(2)}) collective-permute-start(bf16[384,512]{1,0:T(8,128)(2,1)} %bitcast.202), channel_id=1, source_target_pairs={{0,1},{1,0},{2,3},{3,2},{4,5},{5,4},{6,7},{7,6},{8,9},{9,8},{10,11... | collective-permute-start | bytes 1179656 | tf_op jit(solution)/shard_map/ppermute | solution.py:166
  2.8 9.9 %collective-permute-start = (bf16[384,512]{1,0:T(8,128)(2,1)}, bf16[384,512]{1,0:T(8,128)(2,1)S(1)}, u32[]{:S(2)}, u32[]{:S(2)}) collective-permute-start(bf16[384,512]{1,0:T(8,128)(2,1)} %bitcast.203), channel_id=1, source_target_pairs={{0,16},{16,0},{1,17},{17,1},{2,18},{18,2},{3,19},{19,3},{4,20},{20... | collective-permute-start | bytes 1179656 | tf_op jit(solution)/shard_map/ppermute | solution.py:165
  22.0 15.6 %collective-permute-start.2 = (f16[4,2,96,1280]{3,2,1,0:T(8,128)(2,1)}, f16[4,2,96,1280]{3,2,1,0:T(8,128)(2,1)S(1)}, u32[]{:S(2)}, u32[]{:S(2)}) collective-permute-start(f16[4,2,96,1280]{3,2,1,0:T(8,128)(2,1)} %convert_element_type.191), channel_id=1, source_target_pairs={{0,2},{2,0},{4,6},{6,4},{8,10},{10,8},{12,14},{14,12},{1,3},{3,1},... | collective-permute-start | bytes 5898248 | tf_op jit(solution)/shard_map/ppermute | solution.py:132
  25.7 10.0 %collective-permute-start.3 = (bf16[48,3584]{1,0:T(8,128)(2,1)}, bf16[48,3584]{1,0:T(8,128)(2,1)}, u32[]{:S(2)}, u32[]{:S(2)}) collective-permute-start(bf16[48,3584]{1,0:T(8,128)(2,1)} %get-tuple-element.202), channel_id=1, source_target_pairs={{0,1},{1,0},{2,3},{3,2},{4,5},{5,4},{6,7},{7,6},{8,9},{9,8},{10,11... | collective-permute-start | bytes 1032200 | tf_op jit(solution)/shard_map/ppermute | solution.py:205
  31.4 23.4 %copy-start.2 = (f32[4,2,96,1280]{3,2,1,0:T(8,128)}, f32[4,2,96,1280]{3,2,1,0:T(8,128)S(1)}, u32[]{:S(2)}) copy-start(f32[4,2,96,1280]{3,2,1,0:T(8,128)S(1)} %shard_map.68) | copy-start | bytes 11796484
  31.4 12.6 %collective-permute-start.4 = (bf16[384,512]{1,0:T(8,128)(2,1)S(1)}, bf16[384,512]{1,0:T(8,128)(2,1)S(1)}, u32[]{:S(2)}, u32[]{:S(2)}) collective-permute-start(bf16[384,512]{1,0:T(8,128)(2,1)S(1)} %copy-done.28), channel_id=1, source_target_pairs={{0,1},{1,0},{2,3},{3,2},{4,5},{5,4},{6,7},{7,6},{8,9},{9,8},{10,11... | collective-permute-start | bytes 1179656 | tf_op jit(solution)/shard_map/ppermute | solution.py:167
  37.8 14.6 %collective-permute-start.5 = (f16[2,96,1280]{2,1,0:T(8,128)(2,1)S(1)}, f16[2,96,1280]{2,1,0:T(8,128)(2,1)S(1)}, u32[]{:S(2)}, u32[]{:S(2)}) collective-permute-start(f16[2,96,1280]{2,1,0:T(8,128)(2,1)S(1)} %fusion.28), channel_id=1, source_target_pairs={{0,4},{2,6},{12,8},{14,10},{1,5},{3,7},{13,9},{15,11},{16,20},{18,... | collective-permute-start | bytes 1474568 | tf_op jit(solution)/shard_map/ppermute | solution.py:132
  51.6 16.0 %collective-permute-start.6 = (f16[4,2,96,1280]{3,2,1,0:T(8,128)(2,1)}, f16[4,2,96,1280]{3,2,1,0:T(8,128)(2,1)S(1)}, u32[]{:S(2)}, u32[]{:S(2)}) collective-permute-start(f16[4,2,96,1280]{3,2,1,0:T(8,128)(2,1)} %convert_element_type.195), channel_id=1, source_target_pairs={{0,2},{2,0},{4,6},{6,4},{8,10},{10,8},{12,14},{14,12},{1,3},{3,1},... | collective-permute-start | bytes 5898248 | tf_op jit(solution)/shard_map/ppermute | solution.py:132
  53.4 14.3 %collective-permute-start.7 = (f16[2,96,1280]{2,1,0:T(8,128)(2,1)}, f16[2,96,1280]{2,1,0:T(8,128)(2,1)}, u32[]{:S(2)}, u32[]{:S(2)}) collective-permute-start(f16[2,96,1280]{2,1,0:T(8,128)(2,1)} %fusion.11), channel_id=1, source_target_pairs={{4,8},{6,10},{8,4},{10,6},{5,9},{7,11},{9,5},{11,7},{20,24},{22,26... | collective-permute-start | bytes 1474568 | tf_op jit(solution)/shard_map/ppermute | solution.py:132
  55.7 14.6 %collective-permute-start.9 = (f16[2,96,1280]{2,1,0:T(8,128)(2,1)}, f16[2,96,1280]{2,1,0:T(8,128)(2,1)}, u32[]{:S(2)}, u32[]{:S(2)}) collective-permute-start(f16[2,96,1280]{2,1,0:T(8,128)(2,1)} %fusion.29), channel_id=1, source_target_pairs={{0,4},{2,6},{12,8},{14,10},{1,5},{3,7},{13,9},{15,11},{16,20},{18,... | collective-permute-start | bytes 1474568 | tf_op jit(solution)/shard_map/ppermute | solution.py:132
  61.5 8.8 %copy-start.3 = (f32[4,2,96,1280]{3,2,1,0:T(8,128)S(1)}, f32[4,2,96,1280]{3,2,1,0:T(8,128)}, u32[]{:S(2)}) copy-start(f32[4,2,96,1280]{3,2,1,0:T(8,128)} %copy-done.2) | copy-start | bytes 11796484
  61.5 8.8 %copy-start.9 = (f16[4,2,96,1280]{3,2,1,0:T(8,128)(2,1)S(1)}, f16[4,2,96,1280]{3,2,1,0:T(8,128)(2,1)}, u32[]{:S(2)}) copy-start(f16[4,2,96,1280]{3,2,1,0:T(8,128)(2,1)} %copy-done.7) | copy-start | bytes 5898244
  67.6 47.2 %copy-start = (f32[4,2,96,1280]{3,2,1,0:T(8,128)}, f32[4,2,96,1280]{3,2,1,0:T(8,128)S(1)}, u32[]{:S(2)}) copy-start(f32[4,2,96,1280]{3,2,1,0:T(8,128)S(1)} %shard_map.70) | copy-start | bytes 11796484
  67.6 7.3 %copy-start.10 = (bf16[2,48,3584]{2,1,0:T(8,128)(2,1)S(1)}, bf16[2,48,3584]{2,1,0:T(8,128)(2,1)}, u32[]{:S(2)}) copy-start(bf16[2,48,3584]{2,1,0:T(8,128)(2,1)} %pad_maximum_fusion.5) | copy-start | bytes 2064388
  71.9 15.0 %collective-permute-start.8 = (f16[2,96,1280]{2,1,0:T(8,128)(2,1)S(1)}, f16[2,96,1280]{2,1,0:T(8,128)(2,1)S(1)}, u32[]{:S(2)}, u32[]{:S(2)}) collective-permute-start(f16[2,96,1280]{2,1,0:T(8,128)(2,1)S(1)} %get-tuple-element.167), channel_id=1, source_target_pairs={{0,4},{2,6},{12,8},{14,10},{4,0},{6,2},{8,12},{10,14},{1,5},{3,7},... | collective-permute-start | bytes 1474568 | tf_op jit(solution)/shard_map/ppermute | solution.py:132
  74.2 12.7 %collective-permute-start.10 = (f16[2,96,1280]{2,1,0:T(8,128)(2,1)S(1)}, f16[2,96,1280]{2,1,0:T(8,128)(2,1)S(1)}, u32[]{:S(2)}, u32[]{:S(2)}) collective-permute-start(f16[2,96,1280]{2,1,0:T(8,128)(2,1)S(1)} %get-tuple-element.168), channel_id=1, source_target_pairs={{4,8},{6,10},{8,4},{10,6},{5,9},{7,11},{9,5},{11,7},{20,24},{22,26... | collective-permute-start | bytes 1474568 | tf_op jit(solution)/shard_map/ppermute | solution.py:132
  75.0 10.7 %collective-permute-start.12 = (bf16[2,48,1792]{2,1,0:T(8,128)(2,1)S(1)}, bf16[2,48,1792]{2,1,0:T(8,128)(2,1)S(1)}, u32[]{:S(2)}, u32[]{:S(2)}) collective-permute-start(bf16[2,48,1792]{2,1,0:T(8,128)(2,1)S(1)} %get-tuple-element.200), channel_id=1, source_target_pairs={{0,2},{2,0},{4,6},{6,4},{8,10},{10,8},{12,14},{14,12},{1,3},{3,1},... | collective-permute-start | bytes 1032200 | tf_op jit(solution)/shard_map/ppermute | solution.py:132
  78.3 19.6 %collective-permute-start.16 = (f16[2,96,1280]{2,1,0:T(8,128)(2,1)}, f16[2,96,1280]{2,1,0:T(8,128)(2,1)}, u32[]{:S(2)}, u32[]{:S(2)}) collective-permute-start(f16[2,96,1280]{2,1,0:T(8,128)(2,1)} %fusion.30), channel_id=1, source_target_pairs={{0,4},{2,6},{12,8},{14,10},{1,5},{3,7},{13,9},{15,11},{16,20},{18,... | collective-permute-start | bytes 1474568 | tf_op jit(solution)/shard_map/ppermute | solution.py:132
  85.2 6.7 %collective-permute-start.13 = (bf16[2,1024,512]{2,1,0:T(8,128)(2,1)S(1)}, bf16[2,1024,512]{2,1,0:T(8,128)(2,1)S(1)}, u32[]{:S(2)}, u32[]{:S(2)}) collective-permute-start(bf16[2,1024,512]{2,1,0:T(8,128)(2,1)S(1)} %pad_maximum_fusion), channel_id=1, source_target_pairs={{0,2},{2,0},{4,6},{6,4},{8,10},{10,8},{12,14},{14,12},{1,3},{3,1},... | collective-permute-start | bytes 6291464 | tf_op jit(solution)/shard_map/ppermute | solution.py:132
  85.7 6.0 %collective-permute-start.11 = (bf16[4,2,96,1024]{3,2,0,1:T(8,128)(2,1)S(1)}, bf16[4,2,96,1024]{3,2,0,1:T(8,128)(2,1)S(1)}, u32[]{:S(2)}, u32[]{:S(2)}) collective-permute-start(bf16[4,2,96,1024]{3,2,0,1:T(8,128)(2,1)S(1)} %pad_maximum_fusion.3), channel_id=1, source_target_pairs={{0,2},{2,0},{4,6},{6,4},{8,10},{10,8},{12,14},{14,12},{1,3},{3,1},... | collective-permute-start | bytes 4718600 | tf_op jit(solution)/shard_map/ppermute | solution.py:132
  88.7 15.0 %collective-permute-start.15 = (bf16[2,96,1280]{2,1,0:T(8,128)(2,1)S(1)}, bf16[2,96,1280]{2,1,0:T(8,128)(2,1)S(1)}, u32[]{:S(2)}, u32[]{:S(2)}) collective-permute-start(bf16[2,96,1280]{2,1,0:T(8,128)(2,1)S(1)} %pad_maximum_fusion.6), channel_id=1, source_target_pairs={{4,8},{6,10},{8,4},{10,6},{5,9},{7,11},{9,5},{11,7},{20,24},{22,26... | collective-permute-start | bytes 1474568 | tf_op jit(solution)/shard_map/ppermute | solution.py:132
  89.4 14.3 %collective-permute-start.14 = (bf16[2,96,1280]{2,1,0:T(8,128)(2,1)S(1)}, bf16[2,96,1280]{2,1,0:T(8,128)(2,1)S(1)}, u32[]{:S(2)}, u32[]{:S(2)}) collective-permute-start(bf16[2,96,1280]{2,1,0:T(8,128)(2,1)S(1)} %pad_maximum_fusion.6), channel_id=1, source_target_pairs={{0,4},{2,6},{12,8},{14,10},{4,0},{6,2},{8,12},{10,14},{1,5},{3,7},... | collective-permute-start | bytes 1474568 | tf_op jit(solution)/shard_map/ppermute | solution.py:132
  99.1 7.3 %collective-permute-start.20 = (f16[2,96,1280]{2,1,0:T(8,128)(2,1)S(1)}, f16[2,96,1280]{2,1,0:T(8,128)(2,1)S(1)}, u32[]{:S(2)}, u32[]{:S(2)}) collective-permute-start(f16[2,96,1280]{2,1,0:T(8,128)(2,1)S(1)} %fusion.5), channel_id=1, source_target_pairs={{4,8},{6,10},{8,4},{10,6},{5,9},{7,11},{9,5},{11,7},{20,24},{22,26... | collective-permute-start | bytes 1474568 | tf_op jit(solution)/shard_map/ppermute | solution.py:132
  100.0 14.8 %collective-permute-start.19 = (f16[2,96,1280]{2,1,0:T(8,128)(2,1)S(1)}, f16[2,96,1280]{2,1,0:T(8,128)(2,1)S(1)}, u32[]{:S(2)}, u32[]{:S(2)}) collective-permute-start(f16[2,96,1280]{2,1,0:T(8,128)(2,1)S(1)} %fusion.31), channel_id=1, source_target_pairs={{0,4},{2,6},{12,8},{14,10},{1,5},{3,7},{13,9},{15,11},{16,20},{18,... | collective-permute-start | bytes 1474568 | tf_op jit(solution)/shard_map/ppermute | solution.py:132
  103.7 12.4 %copy-start.23 = (bf16[2,96,1280]{2,1,0:T(8,128)(2,1)}, bf16[2,96,1280]{2,1,0:T(8,128)(2,1)S(1)}, u32[]{:S(2)}) copy-start(bf16[2,96,1280]{2,1,0:T(8,128)(2,1)S(1)} %collective-permute-done.15) | copy-start | bytes 1474564
  103.7 12.4 %copy-start.21 = (bf16[2,96,1280]{2,1,0:T(8,128)(2,1)}, bf16[2,96,1280]{2,1,0:T(8,128)(2,1)S(1)}, u32[]{:S(2)}) copy-start(bf16[2,96,1280]{2,1,0:T(8,128)(2,1)S(1)} %collective-permute-done.14) | copy-start | bytes 1474564
  103.7 16.1 %collective-permute-start.18 = (bf16[2,96,1280]{2,1,0:T(8,128)(2,1)S(1)}, bf16[2,96,1280]{2,1,0:T(8,128)(2,1)}, u32[]{:S(2)}, u32[]{:S(2)}) collective-permute-start(bf16[2,96,1280]{2,1,0:T(8,128)(2,1)S(1)} %collective-permute-done.14), channel_id=1, source_target_pairs={{4,8},{6,10},{8,4},{10,6},{5,9},{7,11},{9,5},{11,7},{20,24},{22,26... | collective-permute-start | bytes 1474568 | tf_op jit(solution)/shard_map/ppermute | solution.py:132
  105.2 14.6 %collective-permute-start.17 = (bf16[2,96,1280]{2,1,0:T(8,128)(2,1)S(1)}, bf16[2,96,1280]{2,1,0:T(8,128)(2,1)S(1)}, u32[]{:S(2)}, u32[]{:S(2)}) collective-permute-start(bf16[2,96,1280]{2,1,0:T(8,128)(2,1)S(1)} %collective-permute-done.15), channel_id=1, source_target_pairs={{4,0},{6,2},{8,12},{10,14},{5,1},{7,3},{9,13},{11,15},{20,16},{22,... | collective-permute-start | bytes 1474568 | tf_op jit(solution)/shard_map/ppermute | solution.py:132
  116.1 16.0 %collective-permute-start.22 = (f16[2,96,1280]{2,1,0:T(8,128)(2,1)}, f16[2,96,1280]{2,1,0:T(8,128)(2,1)}, u32[]{:S(2)}, u32[]{:S(2)}) collective-permute-start(f16[2,96,1280]{2,1,0:T(8,128)(2,1)} %get-tuple-element.165), channel_id=1, source_target_pairs={{0,4},{2,6},{12,8},{14,10},{4,0},{6,2},{8,12},{10,14},{1,5},{3,7},... | collective-permute-start | bytes 1474568 | tf_op jit(solution)/shard_map/ppermute | solution.py:132
  118.3 13.8 %collective-permute-start.23 = (f16[2,96,1280]{2,1,0:T(8,128)(2,1)}, f16[2,96,1280]{2,1,0:T(8,128)(2,1)}, u32[]{:S(2)}, u32[]{:S(2)}) collective-permute-start(f16[2,96,1280]{2,1,0:T(8,128)(2,1)} %get-tuple-element.166), channel_id=1, source_target_pairs={{4,8},{6,10},{8,4},{10,6},{5,9},{7,11},{9,5},{11,7},{20,24},{22,26... | collective-permute-start | bytes 1474568 | tf_op jit(solution)/shard_map/ppermute | solution.py:132
  120.6 20.5 %collective-permute-start.21 = (bf16[2,96,1280]{2,1,0:T(8,128)(2,1)}, bf16[2,96,1280]{2,1,0:T(8,128)(2,1)}, u32[]{:S(2)}, u32[]{:S(2)}) collective-permute-start(bf16[2,96,1280]{2,1,0:T(8,128)(2,1)} %collective-permute-done.18), channel_id=1, source_target_pairs={{4,0},{6,2},{8,12},{10,14},{5,1},{7,3},{9,13},{11,15},{20,16},{22,... | collective-permute-start | bytes 1474568 | tf_op jit(solution)/shard_map/ppermute | solution.py:132
  124.2 8.0 %copy-start.1 = (f32[4,2,96,1280]{3,2,1,0:T(8,128)S(1)}, f32[4,2,96,1280]{3,2,1,0:T(8,128)}, u32[]{:S(2)}) copy-start(f32[4,2,96,1280]{3,2,1,0:T(8,128)} %copy-done) | copy-start | bytes 11796484
  127.0 6.8 %copy-start.18 = (bf16[96,1792]{1,0:T(8,128)(2,1)S(1)}, bf16[96,1792]{1,0:T(8,128)(2,1)}, u32[]{:S(2)}) copy-start(bf16[96,1792]{1,0:T(8,128)(2,1)} %get-tuple-element.197) | copy-start | bytes 1032196
  127.1 16.8 %collective-permute-start.26 = (f16[2,192,512]{2,1,0:T(8,128)(2,1)S(1)}, f16[2,192,512]{2,1,0:T(8,128)(2,1)S(1)}, u32[]{:S(2)}, u32[]{:S(2)}) collective-permute-start(f16[2,192,512]{2,1,0:T(8,128)(2,1)S(1)} %fusion.37), channel_id=1, source_target_pairs={{0,4},{2,6},{12,8},{14,10},{1,5},{3,7},{13,9},{15,11},{16,20},{18,... | collective-permute-start | bytes 1179656 | tf_op jit(solution)/shard_map/ppermute | solution.py:132
  133.8 7.2 %copy-start.12 = (bf16[2,96,1280]{2,1,0:T(8,128)(2,1)S(1)}, bf16[2,96,1280]{2,1,0:T(8,128)(2,1)}, u32[]{:S(2)}) copy-start(bf16[2,96,1280]{2,1,0:T(8,128)(2,1)} %copy-done.11) | copy-start | bytes 1474564
  133.9 7.2 %copy-start.22 = (bf16[2,96,1280]{2,1,0:T(8,128)(2,1)S(1)}, bf16[2,96,1280]{2,1,0:T(8,128)(2,1)}, u32[]{:S(2)}) copy-start(bf16[2,96,1280]{2,1,0:T(8,128)(2,1)} %copy-done.21) | copy-start | bytes 1474564
  135.7 14.8 %collective-permute-start.25 = (bf16[2,96,1280]{2,1,0:T(8,128)(2,1)}, bf16[2,96,1280]{2,1,0:T(8,128)(2,1)}, u32[]{:S(2)}, u32[]{:S(2)}) collective-permute-start(bf16[2,96,1280]{2,1,0:T(8,128)(2,1)} %pad_maximum_fusion.7), channel_id=1, source_target_pairs={{4,8},{6,10},{8,4},{10,6},{5,9},{7,11},{9,5},{11,7},{20,24},{22,26... | collective-permute-start | bytes 1474568 | tf_op jit(solution)/shard_map/ppermute | solution.py:132
  137.1 13.8 %collective-permute-start.24 = (bf16[2,96,1280]{2,1,0:T(8,128)(2,1)}, bf16[2,96,1280]{2,1,0:T(8,128)(2,1)}, u32[]{:S(2)}, u32[]{:S(2)}) collective-permute-start(bf16[2,96,1280]{2,1,0:T(8,128)(2,1)} %pad_maximum_fusion.7), channel_id=1, source_target_pairs={{0,4},{2,6},{12,8},{14,10},{4,0},{6,2},{8,12},{10,14},{1,5},{3,7},... | collective-permute-start | bytes 1474568 | tf_op jit(solution)/shard_map/ppermute | solution.py:132
  146.6 6.5 %collective-permute-start.30 = (f16[2,192,512]{2,1,0:T(8,128)(2,1)}, f16[2,192,512]{2,1,0:T(8,128)(2,1)}, u32[]{:S(2)}, u32[]{:S(2)}) collective-permute-start(f16[2,192,512]{2,1,0:T(8,128)(2,1)} %fusion.17), channel_id=1, source_target_pairs={{4,8},{6,10},{8,4},{10,6},{5,9},{7,11},{9,5},{11,7},{20,24},{22,26... | collective-permute-start | bytes 1179656 | tf_op jit(solution)/shard_map/ppermute | solution.py:132
  148.0 8.9 %collective-permute-start.29 = (f16[2,192,512]{2,1,0:T(8,128)(2,1)}, f16[2,192,512]{2,1,0:T(8,128)(2,1)}, u32[]{:S(2)}, u32[]{:S(2)}) collective-permute-start(f16[2,192,512]{2,1,0:T(8,128)(2,1)} %fusion.38), channel_id=1, source_target_pairs={{0,4},{2,6},{12,8},{14,10},{1,5},{3,7},{13,9},{15,11},{16,20},{18,... | collective-permute-start | bytes 1179656 | tf_op jit(solution)/shard_map/ppermute | solution.py:132
  150.4 20.8 %copy-start.6 = (f32[4,2,192,512]{3,2,1,0:T(8,128)S(1)}, f32[4,2,192,512]{3,2,1,0:T(8,128)}, u32[]{:S(2)}) copy-start(f32[4,2,192,512]{3,2,1,0:T(8,128)} %shard_map.71) | copy-start | bytes 9437188
  150.9 13.0 %collective-permute-start.28 = (bf16[2,96,1280]{2,1,0:T(8,128)(2,1)}, bf16[2,96,1280]{2,1,0:T(8,128)(2,1)S(1)}, u32[]{:S(2)}, u32[]{:S(2)}) collective-permute-start(bf16[2,96,1280]{2,1,0:T(8,128)(2,1)} %collective-permute-done.24), channel_id=1, source_target_pairs={{4,8},{6,10},{8,4},{10,6},{5,9},{7,11},{9,5},{11,7},{20,24},{22,26... | collective-permute-start | bytes 1474568 | tf_op jit(solution)/shard_map/ppermute | solution.py:132
  151.7 12.1 %collective-permute-start.27 = (bf16[2,96,1280]{2,1,0:T(8,128)(2,1)}, bf16[2,96,1280]{2,1,0:T(8,128)(2,1)S(1)}, u32[]{:S(2)}, u32[]{:S(2)}) collective-permute-start(bf16[2,96,1280]{2,1,0:T(8,128)(2,1)} %collective-permute-done.25), channel_id=1, source_target_pairs={{4,0},{6,2},{8,12},{10,14},{5,1},{7,3},{9,13},{11,15},{20,16},{22,... | collective-permute-start | bytes 1474568 | tf_op jit(solution)/shard_map/ppermute | solution.py:132
  159.1 12.2 %collective-permute-start.31 = (f16[2,192,512]{2,1,0:T(8,128)(2,1)S(1)}, f16[2,192,512]{2,1,0:T(8,128)(2,1)S(1)}, u32[]{:S(2)}, u32[]{:S(2)}) collective-permute-start(f16[2,192,512]{2,1,0:T(8,128)(2,1)S(1)} %get-tuple-element.169), channel_id=1, source_target_pairs={{0,4},{2,6},{12,8},{14,10},{4,0},{6,2},{8,12},{10,14},{1,5},{3,7},... | collective-permute-start | bytes 1179656 | tf_op jit(solution)/shard_map/ppermute | solution.py:132
  161.3 9.9 %collective-permute-start.32 = (f16[2,192,512]{2,1,0:T(8,128)(2,1)S(1)}, f16[2,192,512]{2,1,0:T(8,128)(2,1)S(1)}, u32[]{:S(2)}, u32[]{:S(2)}) collective-permute-start(f16[2,192,512]{2,1,0:T(8,128)(2,1)S(1)} %get-tuple-element.170), channel_id=1, source_target_pairs={{4,8},{6,10},{8,4},{10,6},{5,9},{7,11},{9,5},{11,7},{20,24},{22,26... | collective-permute-start | bytes 1179656 | tf_op jit(solution)/shard_map/ppermute | solution.py:132
  163.9 26.3 %collective-permute-start.39 = (bf16[2,96,1280]{2,1,0:T(8,128)(2,1)S(1)}, bf16[2,96,1280]{2,1,0:T(8,128)(2,1)S(1)}, u32[]{:S(2)}, u32[]{:S(2)}) collective-permute-start(bf16[2,96,1280]{2,1,0:T(8,128)(2,1)S(1)} %collective-permute-done.28), channel_id=1, source_target_pairs={{4,0},{6,2},{8,12},{10,14},{5,1},{7,3},{9,13},{11,15},{20,16},{22,... | collective-permute-start | bytes 1474568 | tf_op jit(solution)/shard_map/ppermute | solution.py:132
  171.5 8.6 %copy-start.19 = (bf16[1,96,1280]{2,1,0:T(8,128)(2,1)S(1)}, bf16[1,96,1280]{2,1,0:T(8,128)(2,1)}, u32[]{:S(2)}) copy-start(bf16[1,96,1280]{2,1,0:T(8,128)(2,1)} %get-tuple-element.185) | copy-start | bytes 737284
  171.5 8.6 %copy-start.20 = (bf16[1,96,1280]{2,1,0:T(8,128)(2,1)S(1)}, bf16[1,96,1280]{2,1,0:T(8,128)(2,1)}, u32[]{:S(2)}) copy-start(bf16[1,96,1280]{2,1,0:T(8,128)(2,1)} %get-tuple-element.186) | copy-start | bytes 737284
  171.8 8.3 %copy-start.13 = (bf16[1,192,512]{2,1,0:T(8,128)(2,1)}, bf16[1,192,512]{2,1,0:T(8,128)(2,1)S(1)}, u32[]{:S(2)}) copy-start(bf16[1,192,512]{2,1,0:T(8,128)(2,1)S(1)} %get-tuple-element.183) | copy-start | bytes 589828
  171.8 8.3 %copy-start.15 = (bf16[1,192,512]{2,1,0:T(8,128)(2,1)}, bf16[1,192,512]{2,1,0:T(8,128)(2,1)S(1)}, u32[]{:S(2)}) copy-start(bf16[1,192,512]{2,1,0:T(8,128)(2,1)S(1)} %get-tuple-element.184) | copy-start | bytes 589828
  171.9 16.7 %collective-permute-start.35 = (bf16[2,192,512]{2,1,0:T(8,128)(2,1)S(1)}, bf16[2,192,512]{2,1,0:T(8,128)(2,1)S(1)}, u32[]{:S(2)}, u32[]{:S(2)}) collective-permute-start(bf16[2,192,512]{2,1,0:T(8,128)(2,1)S(1)} %pad_maximum_fusion.8), channel_id=1, source_target_pairs={{4,8},{6,10},{8,4},{10,6},{5,9},{7,11},{9,5},{11,7},{20,24},{22,26... | collective-permute-start | bytes 1179656 | tf_op jit(solution)/shard_map/ppermute | solution.py:132
  172.6 17.7 %collective-permute-start.34 = (bf16[2,192,512]{2,1,0:T(8,128)(2,1)S(1)}, bf16[2,192,512]{2,1,0:T(8,128)(2,1)S(1)}, u32[]{:S(2)}, u32[]{:S(2)}) collective-permute-start(bf16[2,192,512]{2,1,0:T(8,128)(2,1)S(1)} %pad_maximum_fusion.8), channel_id=1, source_target_pairs={{0,4},{2,6},{12,8},{14,10},{4,0},{6,2},{8,12},{10,14},{1,5},{3,7},... | collective-permute-start | bytes 1179656 | tf_op jit(solution)/shard_map/ppermute | solution.py:132
  181.0 7.6 %collective-permute-start.33 = (bf16[2,48,1792]{2,1,0:T(8,128)(2,1)S(1)}, bf16[2,48,1792]{2,1,0:T(8,128)(2,1)S(1)}, u32[]{:S(2)}, u32[]{:S(2)}) collective-permute-start(bf16[2,48,1792]{2,1,0:T(8,128)(2,1)S(1)} %get-tuple-element.196), channel_id=1, source_target_pairs={{0,2},{2,0},{4,6},{6,4},{8,10},{10,8},{12,14},{14,12},{1,3},{3,1},... | collective-permute-start | bytes 1032200 | tf_op jit(solution)/shard_map/ppermute | solution.py:132
  186.9 27.9 %collective-permute-start.41 = (bf16[4,2,96,1280]{3,2,1,0:T(8,128)(2,1)}, bf16[4,2,96,1280]{3,2,1,0:T(8,128)(2,1)}, u32[]{:S(2)}, u32[]{:S(2)}) collective-permute-start(bf16[4,2,96,1280]{3,2,1,0:T(8,128)(2,1)} %get-tuple-element.174), channel_id=1, source_target_pairs={{0,2},{2,0},{4,6},{6,4},{8,10},{10,8},{12,14},{14,12},{1,3},{3,1},... | collective-permute-start | bytes 5898248 | tf_op jit(solution)/shard_map/ppermute | solution.py:132
  194.1 20.7 %collective-permute-start.42 = (bf16[4,2,96,1280]{3,2,1,0:T(8,128)(2,1)}, bf16[4,2,96,1280]{3,2,1,0:T(8,128)(2,1)}, u32[]{:S(2)}, u32[]{:S(2)}) collective-permute-start(bf16[4,2,96,1280]{3,2,1,0:T(8,128)(2,1)} %get-tuple-element.171), channel_id=1, source_target_pairs={{0,2},{2,0},{4,6},{6,4},{8,10},{10,8},{12,14},{14,12},{1,3},{3,1},... | collective-permute-start | bytes 5898248 | tf_op jit(solution)/shard_map/ppermute | solution.py:132
  200.5 12.8 %collective-permute-start.37 = (bf16[2,192,512]{2,1,0:T(8,128)(2,1)}, bf16[2,192,512]{2,1,0:T(8,128)(2,1)S(1)}, u32[]{:S(2)}, u32[]{:S(2)}) collective-permute-start(bf16[2,192,512]{2,1,0:T(8,128)(2,1)} %copy-done.29), channel_id=1, source_target_pairs={{4,0},{6,2},{8,12},{10,14},{5,1},{7,3},{9,13},{11,15},{20,16},{22,... | collective-permute-start | bytes 1179656 | tf_op jit(solution)/shard_map/ppermute | solution.py:132
  201.8 10.9 %collective-permute-start.38 = (bf16[2,192,512]{2,1,0:T(8,128)(2,1)}, bf16[2,192,512]{2,1,0:T(8,128)(2,1)S(1)}, u32[]{:S(2)}, u32[]{:S(2)}) collective-permute-start(bf16[2,192,512]{2,1,0:T(8,128)(2,1)} %copy-done.31), channel_id=1, source_target_pairs={{4,8},{6,10},{8,4},{10,6},{5,9},{7,11},{9,5},{11,7},{20,24},{22,26... | collective-permute-start | bytes 1179656 | tf_op jit(solution)/shard_map/ppermute | solution.py:132
  205.5 9.1 %copy-start.14 = (bf16[1,192,512]{2,1,0:T(8,128)(2,1)S(1)}, bf16[1,192,512]{2,1,0:T(8,128)(2,1)}, u32[]{:S(2)}) copy-start(bf16[1,192,512]{2,1,0:T(8,128)(2,1)} %copy-done.13) | copy-start | bytes 589828
  205.5 9.1 %copy-start.16 = (bf16[1,192,512]{2,1,0:T(8,128)(2,1)S(1)}, bf16[1,192,512]{2,1,0:T(8,128)(2,1)}, u32[]{:S(2)}) copy-start(bf16[1,192,512]{2,1,0:T(8,128)(2,1)} %copy-done.15) | copy-start | bytes 589828
  205.5 9.1 %copy-start.32 = (bf16[2,192,512]{2,1,0:T(8,128)(2,1)S(1)}, bf16[2,192,512]{2,1,0:T(8,128)(2,1)}, u32[]{:S(2)}) copy-start(bf16[2,192,512]{2,1,0:T(8,128)(2,1)} %copy-done.31) | copy-start | bytes 1179652
  205.6 9.1 %copy-start.30 = (bf16[2,192,512]{2,1,0:T(8,128)(2,1)S(1)}, bf16[2,192,512]{2,1,0:T(8,128)(2,1)}, u32[]{:S(2)}) copy-start(bf16[2,192,512]{2,1,0:T(8,128)(2,1)} %copy-done.29) | copy-start | bytes 1179652
  213.3 12.7 %collective-permute-start.40 = (bf16[2,192,512]{2,1,0:T(8,128)(2,1)S(1)}, bf16[2,192,512]{2,1,0:T(8,128)(2,1)S(1)}, u32[]{:S(2)}, u32[]{:S(2)}) collective-permute-start(bf16[2,192,512]{2,1,0:T(8,128)(2,1)S(1)} %collective-permute-done.38), channel_id=1, source_target_pairs={{4,0},{6,2},{8,12},{10,14},{5,1},{7,3},{9,13},{11,15},{20,16},{22,... | collective-permute-start | bytes 1179656 | tf_op jit(solution)/shard_map/ppermute | solution.py:132
  227.5 18.0 %collective-permute-start.43 = (bf16[4,2,192,512]{3,2,1,0:T(8,128)(2,1)}, bf16[4,2,192,512]{3,2,1,0:T(8,128)(2,1)}, u32[]{:S(2)}, u32[]{:S(2)}) collective-permute-start(bf16[4,2,192,512]{3,2,1,0:T(8,128)(2,1)} %get-tuple-element.176), channel_id=1, source_target_pairs={{0,2},{2,0},{4,6},{6,4},{8,10},{10,8},{12,14},{14,12},{1,3},{3,1},... | collective-permute-start | bytes 4718600 | tf_op jit(solution)/shard_map/ppermute | solution.py:132
  230.0 10.0 %collective-permute-start.36 = (bf16[48,3584]{1,0:T(8,128)(2,1)}, bf16[48,3584]{1,0:T(8,128)(2,1)}, u32[]{:S(2)}, u32[]{:S(2)}) collective-permute-start(bf16[48,3584]{1,0:T(8,128)(2,1)} %get-tuple-element.139), channel_id=1, source_target_pairs={{0,1},{1,0},{2,3},{3,2},{4,5},{5,4},{6,7},{7,6},{8,9},{9,8},{10,11... | collective-permute-start | bytes 1032200 | tf_op jit(solution)/shard_map/ppermute | solution.py:283
  (14 other events, 44.6 us)

commit v13 on v12

--- a/solution.py
+++ b/solution.py
@@ -91,8 +91,38 @@
         ),
         input_output_aliases={2 + len(acts) + i: i for i in range(len(totals))},
         compiler_params=pltpu.CompilerParams(vmem_limit_bytes=VMEM_LIMIT),
+        cost_estimate=pl.CostEstimate(
+            flops=4 * cores * total * depth * width,
+            bytes_accessed=cores * (8 * depth + 4 * total) * width + 2 * total * depth,
+            transcendentals=0,
+        ),
+    )(place, features, *acts, *totals)
+
+
+def gather_kernel(at_end_ref, act, side_1, centre_1, out_2, share_2, out_3, out_ref):
+    def fill(*blocks):
+        for block, block_ref in enumerate(blocks):
+            out_ref[block] = block_ref[...]
+
+    pl.when(at_end_ref[0] == 1)(functools.partial(fill, act, side_1, out_2, out_3))
+    pl.when(at_end_ref[0] == 0)(functools.partial(fill, side_1, act, centre_1, share_2))
+
+
+def gather_blocks(at_end, *hops):
+    _, rows, width = hops[0].shape
+    spec = pl.BlockSpec((1, rows, width), lambda i, at_end: (i, 0, 0))
+    return pl.pallas_call(
+        gather_kernel,
+        out_shape=jax.ShapeDtypeStruct((4, 2, rows, width), hops[0].dtype),
+        grid_spec=pltpu.PrefetchScalarGridSpec(
+            num_scalar_prefetch=1,
+            grid=(2,),
+            in_specs=[spec] * len(hops),
+            out_specs=pl.BlockSpec((4, 1, rows, width), lambda i, at_end: (0, i, 0, 0)),
+        ),
+        compiler_params=pltpu.CompilerParams(vmem_limit_bytes=VMEM_LIMIT),
         cost_estimate=NO_COST,
-    )(place, features, *acts, *totals)
+    )(at_end, *hops)
 
 
 def tie(value, *after):
@@ -195,17 +225,15 @@
         own, theirs = terms
         return own[block] if theirs is None else own[block] + wide(theirs[block])
 
-    over_row = tie(over_row, over_depth)
+    cotangent = grad_hidden[0]
+    cotangent = (
+        columns_of(cotangent, part * half, half),
+        lax.ppermute(columns_of(cotangent, (1 - part) * half, half), "depth", swap),
+    )
+    over_row = tie(over_row, over_depth, cotangent)
     features = [arrange(by(row == 0, mine, over_row, 1))]
     theirs, own = own_features(features[0], 0, (), WIRE)
-    cotangent = tie(grad_hidden[0], features[0])
-    cotangent = jnp.stack(
-        [
-            columns_of(cotangent, part * half, half),
-            lax.ppermute(columns_of(cotangent, (1 - part) * half, half), "depth", swap),
-        ]
-    )
-    terms = tie((own(()), send(theirs, pairs)), cotangent)
+    terms = (own(()), send(theirs, pairs))
     payload = take(terms, 3).astype(WIRE)
     in_1 = send(payload, inward)
 
@@ -228,15 +256,8 @@
         act = jnp.stack([gate_act, up_act]).astype(jnp.bfloat16)
         return act.reshape(2, len(batches) * rows, width)
 
-    def merge(act, side_1, centre_1, out_2, share_2, out_3):
-        blocks = jnp.stack(
-            [
-                jnp.where(at_end, act, side_1),
-                jnp.where(at_end, side_1, act),
-                jnp.where(at_end, out_2, centre_1),
-                jnp.where(at_end, out_3, share_2),
-            ]
-        )
+    def merge(*hops):
+        blocks = gather_blocks(at_end.astype(jnp.int32).reshape(1), *hops)
         return blocks, send(blocks, pairs)
 
     def add_gradients(acts, owner, totals, start):
@@ -267,7 +288,8 @@
             mine = lax.dynamic_index_in_dim(hidden, core, 1, keepdims=False)
             theirs = lax.dynamic_index_in_dim(hidden, 1 - core, 1, keepdims=False)
             theirs = send(theirs, pairs)
-            before = (theirs,)
+            merged.append(merge(*tie(hops, theirs)))
+            before = (theirs, merged[-1][0])
         if gathering:
             side_1, centre_1 = tie((side_1, centre_1), before)
             out_2, share_2 = send(centre_1, outward), send(side_1, centre)
@@ -275,12 +297,13 @@
             products[1] = (own((far, near)), send(theirs, pairs))
             terms = tie(terms, products[1])
         if not adding:
-            merged.append(merge(*tie(hops, side_1, centre_1)))
             own_acts, other_acts = zip(*merged)
             totals = add_gradients(own_acts, core, (), pieces[0][1])
             share_2 = tie(share_2, totals)
-            hidden = by(core == 0, mine, theirs, 2)
-            theirs = lax.ppermute(tie(hidden[1], side_1), "depth", swap)
+            hidden = by(core == 0, *tie((mine, theirs), side_1, centre_1), 2)
+            theirs = lax.ppermute(hidden[1], "depth", swap)
+            hidden = by(part == 0, hidden[0], theirs, 1)
+            other_acts = tie(other_acts, theirs)
         if adding:
             if gathering:
                 terms = tie(terms, side_1, centre_1)
@@ -293,7 +316,7 @@
                 in_1 = send(payload, inward)
             before = (in_2, centre_2)
         if k < 0:
-            cotangent = tie(cotangent, near, swapped)
+            cotangent = jnp.stack(tie(cotangent, near, swapped))
             cotangent = by(
                 core == 0,
                 columns_of(cotangent, core * share, share),
@@ -320,8 +343,7 @@
             act, terms = ready, products.get(k + 2)
         else:
             totals = add_gradients(other_acts, 1 - core, totals, pieces[0][1])
-            hidden = by(part == 0, hidden[0], theirs, 1)
-            out_3 = tie(out_3, totals, hidden)
+            out_3 = tie(out_3, totals)
             own_acts, other_acts = merge(act, side_1, centre_1, out_2, share_2, out_3)
     totals = add_gradients([own_acts], core, totals, pieces[last][1])
     totals = add_gradients([other_acts], 1 - core, totals, pieces[last][1])

time: 252 us -> 244 us (0.968)
  other arithmetic: 38.6 us -> 26.9 us
  Pallas kernels: 52.7 us -> 58.6 us
  starting transfers between devices: 86.6 us -> 82.1 us
  waiting for transfers between devices: 54.8 us -> 57.4 us
    ppermute x1, waiting for transfers between devices: 2.84 us -> 13.1 us  [local(): lax.ppermute(columns_of(cotangent, (1 - part) * half, half), 'depth', swap)]
    ppermute x1, waiting for transfers between devices: 9.78 us -> 0.01 us  [local(): theirs = lax.ppermute(hidden[1], 'depth', swap)]
    ppermute x39, waiting for transfers between devices: 30.5 us -> 38.4 us  [send(): return lax.ppermute(value, 'col', route)]
    ppermute x1, waiting for transfers between devices: 7.84 us -> 0.01 us  [local(): over_depth = lax.ppermute(mine, 'depth', swap)]
    another operation x13 -> x4, other arithmetic: 9.23 us -> 2.24 us  [the longest x9 5.16 us: merge(): jnp.stack([jnp.where(at_end, act, side_1), jnp.where(at_end, side_1, act)...]
    ppermute x39, starting transfers between devices: 81.5 us -> 75.7 us  [send(): return lax.ppermute(value, 'col', route)]
    pallas_call x0 -> x3, Pallas kernels: none -> 4.77 us  [gather_blocks(): pl.pallas_call(gather_kernel, out_shape=jax.ShapeDtypeStruct((4, 2, rows,...]
    broadcast_in_dim x2 -> x0, other arithmetic: 2.99 us -> none  [add_gradients(): acts = [value[:, None] for value in acts]]
  transfers between devices with their start and end apart: 44 -> 44, of which waited for: 16 -> 12; matrix products, arithmetic and copies ran while one was open for 17% -> 13% of each run, Pallas kernels for 17% -> 19%
where the time goes in v13:
time: 244 us; the launch traced here: 242 us
  starting transfers between devices  82.1 us (34%)
  Pallas kernels  58.6 us (24%)
  waiting for transfers between devices  57.4 us (24%)
  other arithmetic  26.9 us (11%)
  local copies, waits for them, and re-layouts  15.6 us (6%)
    ppermute x39, starting transfers between devices, send(): return lax.ppermute(value, 'col', route)  75.7 us
    ppermute x39, waiting for transfers between devices, send(): return lax.ppermute(value, 'col', route)  38.4 us
    pallas_call x5, Pallas kernels, forward(): pl.pallas_call(functools.partial(forward_kernel, scale), out_shape=jax.Sh...  28.9 us
    pallas_call x4, Pallas kernels, gradient(): pl.pallas_call(functools.partial(gradient_kernel, len(acts)), out_shape=(...  24.9 us
    ppermute x1, waiting for transfers between devices, local(): lax.ppermute(columns_of(cotangent, (1 - part) * half, half), 'depth', swap)  13.1 us
    unnamed x68, local copies, waits for them, and re-layouts  5.98 us
    ppermute x1, waiting for transfers between devices, local(): over_both = lax.ppermute(over_row, 'depth', swap)  5.92 us
    select_n x5, other arithmetic, by(): jnp.where(first, jnp.concatenate([mine, theirs], axis=axis), jnp.concaten...  5.23 us
  transfers between devices with their start and end apart: 44, of which 12 were waited for; matrix products, arithmetic and copies ran while one was open for 13% of the time, Pallas kernels for 19%

profile of v13, /device:TPU:1, one launch (start us, length us, event | category | flops | bytes accessed | tf_op | source)
XLA Modules:
  0.0 241.9 jit_solution(11089547282993352357)
XLA Ops:
  0.6 2.1 collective-permute-start.1
  4.0 1.9 dynamic-slice_bitcast_fusion.4
  6.1 13.1 %collective-permute-done.2 = bf16[48,3584]{1,0:T(8,128)(2,1)S(1)} collective-permute-done((bf16[48,3584]{1,0:T(8,128)(2,1)S(1)}, bf16[48,3584]{1,0:T(8,128)(2,1)S(1)}, u32[]{:S(2)}, u32[]{:S(2)}) %collective-permute-start.2) | collective-permute-done | bytes 344096 | tf_op jit(solution)/shard_map/ppermute | solution.py:231
  19.9 1.3 maximum_select_fusion
  21.5 5.6 %shard_map.67 = f32[4,2,96,1280]{3,2,1,0:T(8,128)S(1)} custom-call(s32[1]{0:T(128)} %bitcast.7.place_ref, bf16[384,1024]{1,0:T(8,128)(2,1)S(1)} %bitcast.155, bf16[1024,7168]{1,0:T(8,128)(2,1)} %refs_2_.9, bf16[1024,7168]{1,0:T(8,128)(2,1)} %refs_3_.1), custom_call_target="tpu_custom_call" | custom-call | tf_op jit(solution)/shard_map/pallas_call | solution.py:45
  27.1 1.5 convert_element_type.194
  29.8 5.5 %shard_map.68 = f32[4,2,96,1280]{3,2,1,0:T(8,128)S(1)} custom-call(s32[1]{0:T(128)} %bitcast.place_ref, bf16[384,1024]{1,0:T(8,128)(2,1)S(1)} %bitcast.156, bf16[1024,7168]{1,0:T(8,128)(2,1)} %refs_2_.9, bf16[1024,7168]{1,0:T(8,128)(2,1)} %refs_3_.1), custom_call_target="tpu_custom_call" | custom-call | tf_op jit(solution)/shard_map/pallas_call | solution.py:45
  35.4 1.5 collective-permute-start.4
  37.0 3.2 %collective-permute-start.5 = (f16[2,96,1280]{2,1,0:T(8,128)(2,1)S(1)}, f16[2,96,1280]{2,1,0:T(8,128)(2,1)S(1)}, u32[]{:S(2)}, u32[]{:S(2)}) collective-permute-start(f16[2,96,1280]{2,1,0:T(8,128)(2,1)S(1)} %fusion.32), channel_id=1, source_target_pairs={{0,4},{2,6},{12,8},{14,10},{1,5},{3,7},{13,9},{15,11},{16,20},{18,... | collective-permute-start | bytes 1474568 | tf_op jit(solution)/shard_map/ppermute | solution.py:162
  40.2 5.9 %collective-permute-done.4 = bf16[384,512]{1,0:T(8,128)(2,1)S(1)} collective-permute-done((bf16[384,512]{1,0:T(8,128)(2,1)S(1)}, bf16[384,512]{1,0:T(8,128)(2,1)S(1)}, u32[]{:S(2)}, u32[]{:S(2)}) %collective-permute-start.4) | collective-permute-done | bytes 393248 | tf_op jit(solution)/shard_map/ppermute | solution.py:197
  46.6 5.6 %shard_map.69 = f32[4,2,96,1280]{3,2,1,0:T(8,128)S(1)} custom-call(s32[1]{0:T(128)} %bitcast.7.place_ref, bf16[384,1024]{1,0:T(8,128)(2,1)S(1)} %bitcast.159, bf16[1024,7168]{1,0:T(8,128)(2,1)} %refs_2_.9, bf16[1024,7168]{1,0:T(8,128)(2,1)} %refs_3_.1), custom_call_target="tpu_custom_call" | custom-call | tf_op jit(solution)/shard_map/pallas_call | solution.py:45
  52.2 1.5 convert_element_type.198
  55.4 1.5 collective-permute-start.7
  57.8 5.9 %collective-permute-start.9 = (f16[2,96,1280]{2,1,0:T(8,128)(2,1)}, f16[2,96,1280]{2,1,0:T(8,128)(2,1)}, u32[]{:S(2)}, u32[]{:S(2)}) collective-permute-start(f16[2,96,1280]{2,1,0:T(8,128)(2,1)} %fusion.29), channel_id=1, source_target_pairs={{0,4},{2,6},{12,8},{14,10},{1,5},{3,7},{13,9},{15,11},{16,20},{18,... | collective-permute-start | bytes 1474568 | tf_op jit(solution)/shard_map/ppermute | solution.py:162
  63.8 6.1 %shard_map.70 = f32[4,2,96,1280]{3,2,1,0:T(8,128)S(1)} custom-call(s32[1]{0:T(128)} %bitcast.place_ref, bf16[384,1024]{1,0:T(8,128)(2,1)S(1)} %bitcast.160, bf16[1024,7168]{1,0:T(8,128)(2,1)} %refs_2_.9, bf16[1024,7168]{1,0:T(8,128)(2,1)} %refs_3_.1), custom_call_target="tpu_custom_call" | custom-call | tf_op jit(solution)/shard_map/pallas_call | solution.py:45
  69.9 2.8 %collective-permute-done.9 = f16[2,96,1280]{2,1,0:T(8,128)(2,1)} collective-permute-done((f16[2,96,1280]{2,1,0:T(8,128)(2,1)}, f16[2,96,1280]{2,1,0:T(8,128)(2,1)}, u32[]{:S(2)}, u32[]{:S(2)}) %collective-permute-start.9) | collective-permute-done | bytes 491552 | tf_op jit(solution)/shard_map/ppermute | solution.py:162
  72.8 1.6 fusion.11
  74.4 2.3 collective-permute-start.8
  77.4 2.3 collective-permute-start.12
  80.6 3.3 %collective-permute-start.16 = (f16[2,96,1280]{2,1,0:T(8,128)(2,1)}, f16[2,96,1280]{2,1,0:T(8,128)(2,1)S(1)}, u32[]{:S(2)}, u32[]{:S(2)}) collective-permute-start(f16[2,96,1280]{2,1,0:T(8,128)(2,1)} %fusion.30), channel_id=1, source_target_pairs={{0,4},{2,6},{12,8},{14,10},{1,5},{3,7},{13,9},{15,11},{16,20},{18,... | collective-permute-start | bytes 1474568 | tf_op jit(solution)/shard_map/ppermute | solution.py:162
  84.0 1.7 dynamic-slice_bitcast_fusion
  90.1 2.9 %collective-permute-start.14 = (bf16[2,96,1280]{2,1,0:T(8,128)(2,1)S(1)}, bf16[2,96,1280]{2,1,0:T(8,128)(2,1)S(1)}, u32[]{:S(2)}, u32[]{:S(2)}) collective-permute-start(bf16[2,96,1280]{2,1,0:T(8,128)(2,1)S(1)} %pad_maximum_fusion.2.act), channel_id=1, source_target_pairs={{0,4},{2,6},{12,8},{14,10},{4,0},{6,2},{8,12},{10,14},{1,5},{3,7},... | collective-permute-start | bytes 1474568 | tf_op jit(solution)/shard_map/ppermute | solution.py:162
  93.2 6.1 %shard_map.71 = f32[4,2,192,512]{3,2,1,0:T(8,128)} custom-call(s32[1]{0:T(128)} %bitcast.place_ref, bf16[768,1024]{1,0:T(8,128)(2,1)S(1)} %bitcast.164, bf16[768,1024]{1,0:T(8,128)(2,1)S(1)} %bitcast.165, bf16[1024,7168]{1,0:T(8,128)(2,1)} %refs_2_.9, bf16[1024,7168]{1,0:T(8,128)(2,1)} %refs_3_.1, ...), custom_call_target="tpu_custom_call" | custom-call | tf_op jit(solution)/shard_map/pallas_call | solution.py:45
  100.4 4.5 %collective-permute-start.19 = (f16[2,96,1280]{2,1,0:T(8,128)(2,1)S(1)}, f16[2,96,1280]{2,1,0:T(8,128)(2,1)S(1)}, u32[]{:S(2)}, u32[]{:S(2)}) collective-permute-start(f16[2,96,1280]{2,1,0:T(8,128)(2,1)S(1)} %fusion.31), channel_id=1, source_target_pairs={{0,4},{2,6},{12,8},{14,10},{1,5},{3,7},{13,9},{15,11},{16,20},{18,... | collective-permute-start | bytes 1474568 | tf_op jit(solution)/shard_map/ppermute | solution.py:162
  104.9 1.4 collective-permute-done.14.side_1
  107.0 1.3 collective-permute-start.17
  108.3 8.5 %collective-permute-done.19 = f16[2,96,1280]{2,1,0:T(8,128)(2,1)S(1)} collective-permute-done((f16[2,96,1280]{2,1,0:T(8,128)(2,1)S(1)}, f16[2,96,1280]{2,1,0:T(8,128)(2,1)S(1)}, u32[]{:S(2)}, u32[]{:S(2)}) %collective-permute-start.19) | collective-permute-done | bytes 491552 | tf_op jit(solution)/shard_map/ppermute | solution.py:162
  116.8 1.4 fusion.4
  118.2 2.2 collective-permute-start.22
  120.4 1.4 collective-permute-start.23
  121.9 1.3 collective-permute-start.21
  125.5 1.6 maximum_bitcast_fusion.features_ref
  128.4 4.6 %collective-permute-start.26 = (f16[2,192,512]{2,1,0:T(8,128)(2,1)S(1)}, f16[2,192,512]{2,1,0:T(8,128)(2,1)S(1)}, u32[]{:S(2)}, u32[]{:S(2)}) collective-permute-start(f16[2,192,512]{2,1,0:T(8,128)(2,1)S(1)} %fusion.38), channel_id=1, source_target_pairs={{0,4},{2,6},{12,8},{14,10},{1,5},{3,7},{13,9},{15,11},{16,20},{18,... | collective-permute-start | bytes 1179656 | tf_op jit(solution)/shard_map/ppermute | solution.py:162
  133.1 1.9 fusion.2
  136.1 1.4 collective-permute-start.25
  137.5 3.6 %collective-permute-start.24 = (bf16[2,96,1280]{2,1,0:T(8,128)(2,1)S(1)}, bf16[2,96,1280]{2,1,0:T(8,128)(2,1)}, u32[]{:S(2)}, u32[]{:S(2)}) collective-permute-start(bf16[2,96,1280]{2,1,0:T(8,128)(2,1)S(1)} %pad_maximum_fusion.3.act), channel_id=1, source_target_pairs={{0,4},{2,6},{12,8},{14,10},{4,0},{6,2},{8,12},{10,14},{1,5},{3,7},... | collective-permute-start | bytes 1474568 | tf_op jit(solution)/shard_map/ppermute | solution.py:162
  141.1 1.9 collective-permute-done.21.out_3
  145.2 1.6 copy-done.20
  147.6 3.2 %collective-permute-start.29 = (f16[2,192,512]{2,1,0:T(8,128)(2,1)S(1)}, f16[2,192,512]{2,1,0:T(8,128)(2,1)S(1)}, u32[]{:S(2)}, u32[]{:S(2)}) collective-permute-start(f16[2,192,512]{2,1,0:T(8,128)(2,1)S(1)} %fusion.39), channel_id=1, source_target_pairs={{0,4},{2,6},{12,8},{14,10},{1,5},{3,7},{13,9},{15,11},{16,20},{18,... | collective-permute-start | bytes 1179656 | tf_op jit(solution)/shard_map/ppermute | solution.py:162
  150.8 2.8 %collective-permute-done.24.side_1 = bf16[2,96,1280]{2,1,0:T(8,128)(2,1)} collective-permute-done((bf16[2,96,1280]{2,1,0:T(8,128)(2,1)S(1)}, bf16[2,96,1280]{2,1,0:T(8,128)(2,1)}, u32[]{:S(2)}, u32[]{:S(2)}) %collective-permute-start.24) | collective-permute-done | bytes 491552 | tf_op jit(solution)/shard_map/ppermute | solution.py:162
  153.7 1.4 collective-permute-start.28
  155.1 1.3 collective-permute-start.27
  156.4 1.3 collective-permute-done.29
  159.0 2.3 collective-permute-start.31
  161.2 1.4 collective-permute-start.32
  163.7 3.2 %collective-permute-done.27.out_2 = bf16[2,96,1280]{2,1,0:T(8,128)(2,1)} collective-permute-done((bf16[2,96,1280]{2,1,0:T(8,128)(2,1)}, bf16[2,96,1280]{2,1,0:T(8,128)(2,1)}, u32[]{:S(2)}, u32[]{:S(2)}) %collective-permute-start.27) | collective-permute-done | bytes 491552 | tf_op jit(solution)/shard_map/ppermute | solution.py:162
  166.9 1.3 collective-permute-start.36
  168.2 7.1 %collective-permute-done.31 = f16[2,192,512]{2,1,0:T(8,128)(2,1)} collective-permute-done((f16[2,192,512]{2,1,0:T(8,128)(2,1)}, f16[2,192,512]{2,1,0:T(8,128)(2,1)}, u32[]{:S(2)}, u32[]{:S(2)}) %collective-permute-start.31) | collective-permute-done | bytes 393248 | tf_op jit(solution)/shard_map/ppermute | solution.py:162
  175.3 1.9 fusion.17
  179.1 8.9 %collective-permute-start.33 = (bf16[2,48,1792]{2,1,0:T(8,128)(2,1)S(1)}, bf16[2,48,1792]{2,1,0:T(8,128)(2,1)}, u32[]{:S(2)}, u32[]{:S(2)}) collective-permute-start(bf16[2,48,1792]{2,1,0:T(8,128)(2,1)S(1)} %get-tuple-element.185), channel_id=1, source_target_pairs={{0,2},{2,0},{4,6},{6,4},{8,10},{10,8},{12,14},{14,12},{1,3},{3,1},... | collective-permute-start | bytes 1032200 | tf_op jit(solution)/shard_map/ppermute | solution.py:162
  188.7 1.4 collective-permute-start.35
  190.8 2.7 %shard_map.73 = bf16[4,2,96,1280]{3,2,1,0:T(8,128)(2,1)} custom-call(s32[1]{0:T(128)} %bitcast.29.at_end_ref, bf16[2,96,1280]{2,1,0:T(8,128)(2,1)S(1)} %copy-done.5, bf16[2,96,1280]{2,1,0:T(8,128)(2,1)} %collective-permute-done.24.side_1, bf16[2,96,1280]{2,1,0:T(8,128)(2,1)} %collective-permute-done.25.centre_1, ...), custom_call_target="tpu_custom_call" | custom-call | tf_op jit(solution)/shard_map/pallas_call | solution.py:114
  193.6 7.6 %collective-permute-done.34.side_1 = bf16[2,192,512]{2,1,0:T(8,128)(2,1)} collective-permute-done((bf16[2,192,512]{2,1,0:T(8,128)(2,1)}, bf16[2,192,512]{2,1,0:T(8,128)(2,1)}, u32[]{:S(2)}, u32[]{:S(2)}) %collective-permute-start.34) | collective-permute-done | bytes 393248 | tf_op jit(solution)/shard_map/ppermute | solution.py:162
  201.2 1.5 collective-permute-start.39
  202.7 1.3 collective-permute-start.38
  203.9 1.5 maximum_select_fusion.3
  207.6 8.0 %shard_map.74 = (f32[1024,3584]{1,0:T(8,128)}, f32[1024,3584]{1,0:T(8,128)}) custom-call(s32[1]{0:T(128)} %bitcast.64.place_ref, bf16[1024,768]{1,0:T(8,128)(2,1)S(1)} %maximum_bitcast_fusion.features_ref, bf16[4,1,2,96,1280]{4,3,2,1,0:T(8,128)(2,1)S(1)} %bitcast.166, bf16[4,1,2,96,1280]{4,3,2,1,0:T(8,128)(2,1)} %bitcast.66.refs_1_), custom_call_target="tpu_custom_call" | custom-call | flops 4026531840 | bytes 15990784 | tf_op jit(solution)/shard_map/pallas_call | solution.py:83
  217.7 9.0 %shard_map.75 = (f32[1024,3584]{1,0:T(8,128)}, f32[1024,3584]{1,0:T(8,128)}) custom-call(s32[1]{0:T(128)} %bitcast.63.place_ref, bf16[1024,768]{1,0:T(8,128)(2,1)S(1)} %maximum_bitcast_fusion.features_ref, bf16[4,1,2,96,1280]{4,3,2,1,0:T(8,128)(2,1)} %bitcast.67.refs_0_, ...), custom_call_target="tpu_custom_call", output_to_operand_aliasing={{0}: (4, {}), {1}: (5, {})} | custom-call | flops 4026531840 | bytes 15990784 | tf_op jit(solution)/shard_map/pallas_call | solution.py:83
  226.7 1.4 collective-permute-done.40.out_3
  228.1 1.8 shard_map.76
  229.9 2.1 collective-permute-start.43
  232.0 2.1 maximum_select_fusion.4
  234.1 3.4 %shard_map.77 = (f32[1024,3584]{1,0:T(8,128)}, f32[1024,3584]{1,0:T(8,128)}) custom-call(s32[1]{0:T(128)} %bitcast.64.place_ref, bf16[1024,768]{1,0:T(8,128)(2,1)S(1)} %maximum_bitcast_fusion.features_ref, bf16[4,1,2,192,512]{4,3,2,1,0:T(8,128)(2,1)S(1)} %bitcast.163, ...), custom_call_target="tpu_custom_call", output_to_operand_aliasing={{0}: (3, {}), {1}: (4, {})} | custom-call | flops 1610612736 | bytes 7340032 | tf_op jit(solution)/shard_map/pallas_call | solution.py:83
  237.5 4.4 %shard_map.78 = (f32[1024,3584]{1,0:T(8,128)}, f32[1024,3584]{1,0:T(8,128)}) custom-call(s32[1]{0:T(128)} %bitcast.63.place_ref, bf16[1024,768]{1,0:T(8,128)(2,1)S(1)} %maximum_bitcast_fusion.features_ref, bf16[4,1,2,192,512]{4,3,2,1,0:T(8,128)(2,1)} %bitcast.69.refs_0_, ...), custom_call_target="tpu_custom_call", output_to_operand_aliasing={{0}: (3, {}), {1}: (4, {})} | custom-call | flops 1610612736 | bytes 7340032 | tf_op jit(solution)/shard_map/pallas_call | solution.py:83
  (152 shorter events, 32.1 us)
Async XLA Ops:
  0.6 18.6 %collective-permute-start.1 = (bf16[384,512]{1,0:T(8,128)(2,1)}, bf16[384,512]{1,0:T(8,128)(2,1)S(1)}, u32[]{:S(2)}, u32[]{:S(2)}) collective-permute-start(bf16[384,512]{1,0:T(8,128)(2,1)} %bitcast.172), channel_id=1, source_target_pairs={{0,1},{1,0},{2,3},{3,2},{4,5},{5,4},{6,7},{7,6},{8,9},{9,8},{10,11... | collective-permute-start | bytes 1179656 | tf_op jit(solution)/shard_map/ppermute | solution.py:196
  2.8 16.4 %collective-permute-start = (bf16[384,512]{1,0:T(8,128)(2,1)}, bf16[384,512]{1,0:T(8,128)(2,1)S(1)}, u32[]{:S(2)}, u32[]{:S(2)}) collective-permute-start(bf16[384,512]{1,0:T(8,128)(2,1)} %bitcast.173), channel_id=1, source_target_pairs={{0,16},{16,0},{1,17},{17,1},{2,18},{18,2},{3,19},{19,3},{4,20},{20... | collective-permute-start | bytes 1179656 | tf_op jit(solution)/shard_map/ppermute | solution.py:195
  5.8 13.3 %collective-permute-start.2 = (bf16[48,3584]{1,0:T(8,128)(2,1)S(1)}, bf16[48,3584]{1,0:T(8,128)(2,1)S(1)}, u32[]{:S(2)}, u32[]{:S(2)}) collective-permute-start(bf16[48,3584]{1,0:T(8,128)(2,1)S(1)} %get-tuple-element.191), channel_id=1, source_target_pairs={{0,1},{1,0},{2,3},{3,2},{4,5},{5,4},{6,7},{7,6},{8,9},{9,8},{10,11... | collective-permute-start | bytes 1032200 | tf_op jit(solution)/shard_map/ppermute | solution.py:231
  28.6 8.3 %collective-permute-start.3 = (f16[4,2,96,1280]{3,2,1,0:T(8,128)(2,1)}, f16[4,2,96,1280]{3,2,1,0:T(8,128)(2,1)S(1)}, u32[]{:S(2)}, u32[]{:S(2)}) collective-permute-start(f16[4,2,96,1280]{3,2,1,0:T(8,128)(2,1)} %convert_element_type.194), channel_id=1, source_target_pairs={{0,2},{2,0},{4,6},{6,4},{8,10},{10,8},{12,14},{14,12},{1,3},{3,1},... | collective-permute-start | bytes 5898248 | tf_op jit(solution)/shard_map/ppermute | solution.py:162
  35.3 21.6 %copy-start.2 = (f32[4,2,96,1280]{3,2,1,0:T(8,128)}, f32[4,2,96,1280]{3,2,1,0:T(8,128)S(1)}, u32[]{:S(2)}) copy-start(f32[4,2,96,1280]{3,2,1,0:T(8,128)S(1)} %shard_map.68) | copy-start | bytes 11796484
  35.4 10.8 %collective-permute-start.4 = (bf16[384,512]{1,0:T(8,128)(2,1)S(1)}, bf16[384,512]{1,0:T(8,128)(2,1)S(1)}, u32[]{:S(2)}, u32[]{:S(2)}) collective-permute-start(bf16[384,512]{1,0:T(8,128)(2,1)S(1)} %collective-permute-done), channel_id=1, source_target_pairs={{0,1},{1,0},{2,3},{3,2},{4,5},{5,4},{6,7},{7,6},{8,9},{9,8},{10,11... | collective-permute-start | bytes 1179656 | tf_op jit(solution)/shard_map/ppermute | solution.py:197
  36.9 9.3 %copy-start.23 = (f16[4,2,96,1280]{3,2,1,0:T(8,128)(2,1)}, f16[4,2,96,1280]{3,2,1,0:T(8,128)(2,1)S(1)}, u32[]{:S(2)}) copy-start(f16[4,2,96,1280]{3,2,1,0:T(8,128)(2,1)S(1)} %collective-permute-done.3) | copy-start | bytes 5898244
  37.0 17.5 %collective-permute-start.5 = (f16[2,96,1280]{2,1,0:T(8,128)(2,1)S(1)}, f16[2,96,1280]{2,1,0:T(8,128)(2,1)S(1)}, u32[]{:S(2)}, u32[]{:S(2)}) collective-permute-start(f16[2,96,1280]{2,1,0:T(8,128)(2,1)S(1)} %fusion.32), channel_id=1, source_target_pairs={{0,4},{2,6},{12,8},{14,10},{1,5},{3,7},{13,9},{15,11},{16,20},{18,... | collective-permute-start | bytes 1474568 | tf_op jit(solution)/shard_map/ppermute | solution.py:162
  53.7 16.2 %collective-permute-start.6 = (f16[4,2,96,1280]{3,2,1,0:T(8,128)(2,1)}, f16[4,2,96,1280]{3,2,1,0:T(8,128)(2,1)S(1)}, u32[]{:S(2)}, u32[]{:S(2)}) collective-permute-start(f16[4,2,96,1280]{3,2,1,0:T(8,128)(2,1)} %convert_element_type.198), channel_id=1, source_target_pairs={{0,2},{2,0},{4,6},{6,4},{8,10},{10,8},{12,14},{14,12},{1,3},{3,1},... | collective-permute-start | bytes 5898248 | tf_op jit(solution)/shard_map/ppermute | solution.py:162
  55.4 14.5 %collective-permute-start.7 = (f16[2,96,1280]{2,1,0:T(8,128)(2,1)}, f16[2,96,1280]{2,1,0:T(8,128)(2,1)}, u32[]{:S(2)}, u32[]{:S(2)}) collective-permute-start(f16[2,96,1280]{2,1,0:T(8,128)(2,1)} %fusion.12), channel_id=1, source_target_pairs={{4,8},{6,10},{8,4},{10,6},{5,9},{7,11},{9,5},{11,7},{20,24},{22,26... | collective-permute-start | bytes 1474568 | tf_op jit(solution)/shard_map/ppermute | solution.py:162
  57.8 14.9 %collective-permute-start.9 = (f16[2,96,1280]{2,1,0:T(8,128)(2,1)}, f16[2,96,1280]{2,1,0:T(8,128)(2,1)}, u32[]{:S(2)}, u32[]{:S(2)}) collective-permute-start(f16[2,96,1280]{2,1,0:T(8,128)(2,1)} %fusion.29), channel_id=1, source_target_pairs={{0,4},{2,6},{12,8},{14,10},{1,5},{3,7},{13,9},{15,11},{16,20},{18,... | collective-permute-start | bytes 1474568 | tf_op jit(solution)/shard_map/ppermute | solution.py:162
  63.8 9.0 %copy-start.3 = (f32[4,2,96,1280]{3,2,1,0:T(8,128)S(1)}, f32[4,2,96,1280]{3,2,1,0:T(8,128)}, u32[]{:S(2)}) copy-start(f32[4,2,96,1280]{3,2,1,0:T(8,128)} %copy-done.2) | copy-start | bytes 11796484
  63.8 9.0 %copy-start.25 = (f16[4,2,96,1280]{3,2,1,0:T(8,128)(2,1)S(1)}, f16[4,2,96,1280]{3,2,1,0:T(8,128)(2,1)}, u32[]{:S(2)}) copy-start(f16[4,2,96,1280]{3,2,1,0:T(8,128)(2,1)} %copy-done.23) | copy-start | bytes 5898244
  69.9 47.0 %copy-start = (f32[4,2,96,1280]{3,2,1,0:T(8,128)}, f32[4,2,96,1280]{3,2,1,0:T(8,128)S(1)}, u32[]{:S(2)}) copy-start(f32[4,2,96,1280]{3,2,1,0:T(8,128)S(1)} %shard_map.70) | copy-start | bytes 11796484
  69.9 7.5 %copy-start.26 = (bf16[48,3584]{1,0:T(8,128)(2,1)S(1)}, bf16[48,3584]{1,0:T(8,128)(2,1)}, u32[]{:S(2)}) copy-start(bf16[48,3584]{1,0:T(8,128)(2,1)} %get-tuple-element.98) | copy-start | bytes 1032196
  69.9 7.5 %copy-start.33 = (bf16[48,3584]{1,0:T(8,128)(2,1)S(1)}, bf16[48,3584]{1,0:T(8,128)(2,1)}, u32[]{:S(2)}) copy-start(bf16[48,3584]{1,0:T(8,128)(2,1)} %copy-done.32) | copy-start | bytes 1032196
  69.9 9.8 %copy-start.21 = (f16[4,2,96,1280]{3,2,1,0:T(8,128)(2,1)}, f16[4,2,96,1280]{3,2,1,0:T(8,128)(2,1)S(1)}, u32[]{:S(2)}) copy-start(f16[4,2,96,1280]{3,2,1,0:T(8,128)(2,1)S(1)} %collective-permute-done.6) | copy-start | bytes 5898244
  74.4 13.2 %collective-permute-start.8 = (f16[2,96,1280]{2,1,0:T(8,128)(2,1)S(1)}, f16[2,96,1280]{2,1,0:T(8,128)(2,1)S(1)}, u32[]{:S(2)}, u32[]{:S(2)}) collective-permute-start(f16[2,96,1280]{2,1,0:T(8,128)(2,1)S(1)} %get-tuple-element.169), channel_id=1, source_target_pairs={{0,4},{2,6},{12,8},{14,10},{4,0},{6,2},{8,12},{10,14},{1,5},{3,7},... | collective-permute-start | bytes 1474568 | tf_op jit(solution)/shard_map/ppermute | solution.py:162
  76.7 10.9 %collective-permute-start.10 = (f16[2,96,1280]{2,1,0:T(8,128)(2,1)S(1)}, f16[2,96,1280]{2,1,0:T(8,128)(2,1)S(1)}, u32[]{:S(2)}, u32[]{:S(2)}) collective-permute-start(f16[2,96,1280]{2,1,0:T(8,128)(2,1)S(1)} %get-tuple-element.170), channel_id=1, source_target_pairs={{4,8},{6,10},{8,4},{10,6},{5,9},{7,11},{9,5},{11,7},{20,24},{22,26... | collective-permute-start | bytes 1474568 | tf_op jit(solution)/shard_map/ppermute | solution.py:162
  77.4 9.0 %collective-permute-start.12 = (bf16[2,48,1792]{2,1,0:T(8,128)(2,1)S(1)}, bf16[2,48,1792]{2,1,0:T(8,128)(2,1)S(1)}, u32[]{:S(2)}, u32[]{:S(2)}) collective-permute-start(bf16[2,48,1792]{2,1,0:T(8,128)(2,1)S(1)} %get-tuple-element.190), channel_id=1, source_target_pairs={{0,2},{2,0},{4,6},{6,4},{8,10},{10,8},{12,14},{14,12},{1,3},{3,1},... | collective-permute-start | bytes 1032200 | tf_op jit(solution)/shard_map/ppermute | solution.py:162
  80.6 18.7 %collective-permute-start.16 = (f16[2,96,1280]{2,1,0:T(8,128)(2,1)}, f16[2,96,1280]{2,1,0:T(8,128)(2,1)S(1)}, u32[]{:S(2)}, u32[]{:S(2)}) collective-permute-start(f16[2,96,1280]{2,1,0:T(8,128)(2,1)} %fusion.30), channel_id=1, source_target_pairs={{0,4},{2,6},{12,8},{14,10},{1,5},{3,7},{13,9},{15,11},{16,20},{18,... | collective-permute-start | bytes 1474568 | tf_op jit(solution)/shard_map/ppermute | solution.py:162
  85.9 7.3 %collective-permute-start.13 = (bf16[2,1024,512]{2,1,0:T(8,128)(2,1)S(1)}, bf16[2,1024,512]{2,1,0:T(8,128)(2,1)S(1)}, u32[]{:S(2)}, u32[]{:S(2)}) collective-permute-start(bf16[2,1024,512]{2,1,0:T(8,128)(2,1)S(1)} %pad_maximum_fusion), channel_id=1, source_target_pairs={{0,2},{2,0},{4,6},{6,4},{8,10},{10,8},{12,14},{14,12},{1,3},{3,1},... | collective-permute-start | bytes 6291464 | tf_op jit(solution)/shard_map/ppermute | solution.py:162
  86.4 6.5 %collective-permute-start.11 = (bf16[4,2,96,1024]{3,2,0,1:T(8,128)(2,1)S(1)}, bf16[4,2,96,1024]{3,2,0,1:T(8,128)(2,1)S(1)}, u32[]{:S(2)}, u32[]{:S(2)}) collective-permute-start(bf16[4,2,96,1024]{3,2,0,1:T(8,128)(2,1)S(1)} %pad_maximum_fusion.1), channel_id=1, source_target_pairs={{0,2},{2,0},{4,6},{6,4},{8,10},{10,8},{12,14},{14,12},{1,3},{3,1},... | collective-permute-start | bytes 4718600 | tf_op jit(solution)/shard_map/ppermute | solution.py:162
  89.4 15.5 %collective-permute-start.15 = (bf16[2,96,1280]{2,1,0:T(8,128)(2,1)S(1)}, bf16[2,96,1280]{2,1,0:T(8,128)(2,1)S(1)}, u32[]{:S(2)}, u32[]{:S(2)}) collective-permute-start(bf16[2,96,1280]{2,1,0:T(8,128)(2,1)S(1)} %pad_maximum_fusion.2.act), channel_id=1, source_target_pairs={{4,8},{6,10},{8,4},{10,6},{5,9},{7,11},{9,5},{11,7},{20,24},{22,26... | collective-permute-start | bytes 1474568 | tf_op jit(solution)/shard_map/ppermute | solution.py:162
  90.1 16.2 %collective-permute-start.14 = (bf16[2,96,1280]{2,1,0:T(8,128)(2,1)S(1)}, bf16[2,96,1280]{2,1,0:T(8,128)(2,1)S(1)}, u32[]{:S(2)}, u32[]{:S(2)}) collective-permute-start(bf16[2,96,1280]{2,1,0:T(8,128)(2,1)S(1)} %pad_maximum_fusion.2.act), channel_id=1, source_target_pairs={{0,4},{2,6},{12,8},{14,10},{4,0},{6,2},{8,12},{10,14},{1,5},{3,7},... | collective-permute-start | bytes 1474568 | tf_op jit(solution)/shard_map/ppermute | solution.py:162
  99.5 8.8 %collective-permute-start.20 = (f16[2,96,1280]{2,1,0:T(8,128)(2,1)S(1)}, f16[2,96,1280]{2,1,0:T(8,128)(2,1)S(1)}, u32[]{:S(2)}, u32[]{:S(2)}) collective-permute-start(f16[2,96,1280]{2,1,0:T(8,128)(2,1)S(1)} %fusion.6), channel_id=1, source_target_pairs={{4,8},{6,10},{8,4},{10,6},{5,9},{7,11},{9,5},{11,7},{20,24},{22,26... | collective-permute-start | bytes 1474568 | tf_op jit(solution)/shard_map/ppermute | solution.py:162
  100.4 16.5 %collective-permute-start.19 = (f16[2,96,1280]{2,1,0:T(8,128)(2,1)S(1)}, f16[2,96,1280]{2,1,0:T(8,128)(2,1)S(1)}, u32[]{:S(2)}, u32[]{:S(2)}) collective-permute-start(f16[2,96,1280]{2,1,0:T(8,128)(2,1)S(1)} %fusion.31), channel_id=1, source_target_pairs={{0,4},{2,6},{12,8},{14,10},{1,5},{3,7},{13,9},{15,11},{16,20},{18,... | collective-permute-start | bytes 1474568 | tf_op jit(solution)/shard_map/ppermute | solution.py:162
  104.8 13.4 %copy-start.8 = (bf16[2,96,1280]{2,1,0:T(8,128)(2,1)}, bf16[2,96,1280]{2,1,0:T(8,128)(2,1)S(1)}, u32[]{:S(2)}) copy-start(bf16[2,96,1280]{2,1,0:T(8,128)(2,1)S(1)} %collective-permute-done.15.centre_1) | copy-start | bytes 1474564
  106.3 11.9 %copy-start.10 = (bf16[2,96,1280]{2,1,0:T(8,128)(2,1)}, bf16[2,96,1280]{2,1,0:T(8,128)(2,1)S(1)}, u32[]{:S(2)}) copy-start(bf16[2,96,1280]{2,1,0:T(8,128)(2,1)S(1)} %collective-permute-done.14.side_1) | copy-start | bytes 1474564
  106.3 15.6 %collective-permute-start.18 = (bf16[2,96,1280]{2,1,0:T(8,128)(2,1)S(1)}, bf16[2,96,1280]{2,1,0:T(8,128)(2,1)S(1)}, u32[]{:S(2)}, u32[]{:S(2)}) collective-permute-start(bf16[2,96,1280]{2,1,0:T(8,128)(2,1)S(1)} %collective-permute-done.14.side_1), channel_id=1, source_target_pairs={{4,8},{6,10},{8,4},{10,6},{5,9},{7,11},{9,5},{11,7},{20,24},{22,26... | collective-permute-start | bytes 1474568 | tf_op jit(solution)/shard_map/ppermute | solution.py:162
  107.0 14.9 %collective-permute-start.17 = (bf16[2,96,1280]{2,1,0:T(8,128)(2,1)S(1)}, bf16[2,96,1280]{2,1,0:T(8,128)(2,1)S(1)}, u32[]{:S(2)}, u32[]{:S(2)}) collective-permute-start(bf16[2,96,1280]{2,1,0:T(8,128)(2,1)S(1)} %collective-permute-done.15.centre_1), channel_id=1, source_target_pairs={{4,0},{6,2},{8,12},{10,14},{5,1},{7,3},{9,13},{11,15},{20,16},{22,... | collective-permute-start | bytes 1474568 | tf_op jit(solution)/shard_map/ppermute | solution.py:162
  118.2 14.8 %collective-permute-start.22 = (f16[2,96,1280]{2,1,0:T(8,128)(2,1)}, f16[2,96,1280]{2,1,0:T(8,128)(2,1)}, u32[]{:S(2)}, u32[]{:S(2)}) collective-permute-start(f16[2,96,1280]{2,1,0:T(8,128)(2,1)} %get-tuple-element.167), channel_id=1, source_target_pairs={{0,4},{2,6},{12,8},{14,10},{4,0},{6,2},{8,12},{10,14},{1,5},{3,7},... | collective-permute-start | bytes 1474568 | tf_op jit(solution)/shard_map/ppermute | solution.py:162
  120.4 12.6 %collective-permute-start.23 = (f16[2,96,1280]{2,1,0:T(8,128)(2,1)}, f16[2,96,1280]{2,1,0:T(8,128)(2,1)}, u32[]{:S(2)}, u32[]{:S(2)}) collective-permute-start(f16[2,96,1280]{2,1,0:T(8,128)(2,1)} %get-tuple-element.168), channel_id=1, source_target_pairs={{4,8},{6,10},{8,4},{10,6},{5,9},{7,11},{9,5},{11,7},{20,24},{22,26... | collective-permute-start | bytes 1474568 | tf_op jit(solution)/shard_map/ppermute | solution.py:162
  121.9 21.1 %collective-permute-start.21 = (bf16[2,96,1280]{2,1,0:T(8,128)(2,1)S(1)}, bf16[2,96,1280]{2,1,0:T(8,128)(2,1)S(1)}, u32[]{:S(2)}, u32[]{:S(2)}) collective-permute-start(bf16[2,96,1280]{2,1,0:T(8,128)(2,1)S(1)} %collective-permute-done.18.share_2), channel_id=1, source_target_pairs={{4,0},{6,2},{8,12},{10,14},{5,1},{7,3},{9,13},{11,15},{20,16},{22,... | collective-permute-start | bytes 1474568 | tf_op jit(solution)/shard_map/ppermute | solution.py:162
  125.5 7.5 %copy-start.1 = (f32[4,2,96,1280]{3,2,1,0:T(8,128)S(1)}, f32[4,2,96,1280]{3,2,1,0:T(8,128)}, u32[]{:S(2)}) copy-start(f32[4,2,96,1280]{3,2,1,0:T(8,128)} %copy-done) | copy-start | bytes 11796484
  128.4 6.7 %copy-start.27 = (bf16[96,1792]{1,0:T(8,128)(2,1)S(1)}, bf16[96,1792]{1,0:T(8,128)(2,1)}, u32[]{:S(2)}) copy-start(bf16[96,1792]{1,0:T(8,128)(2,1)} %get-tuple-element.187) | copy-start | bytes 1032196
  128.4 16.8 %collective-permute-start.26 = (f16[2,192,512]{2,1,0:T(8,128)(2,1)S(1)}, f16[2,192,512]{2,1,0:T(8,128)(2,1)S(1)}, u32[]{:S(2)}, u32[]{:S(2)}) collective-permute-start(f16[2,192,512]{2,1,0:T(8,128)(2,1)S(1)} %fusion.38), channel_id=1, source_target_pairs={{0,4},{2,6},{12,8},{14,10},{1,5},{3,7},{13,9},{15,11},{16,20},{18,... | collective-permute-start | bytes 1179656 | tf_op jit(solution)/shard_map/ppermute | solution.py:162
  135.0 8.8 %copy-start.7 = (bf16[2,96,1280]{2,1,0:T(8,128)(2,1)S(1)}, bf16[2,96,1280]{2,1,0:T(8,128)(2,1)}, u32[]{:S(2)}) copy-start(bf16[2,96,1280]{2,1,0:T(8,128)(2,1)} %copy-done.6) | copy-start | bytes 1474564
  135.0 8.8 %copy-start.9 = (bf16[2,96,1280]{2,1,0:T(8,128)(2,1)S(1)}, bf16[2,96,1280]{2,1,0:T(8,128)(2,1)}, u32[]{:S(2)}) copy-start(bf16[2,96,1280]{2,1,0:T(8,128)(2,1)} %copy-done.8) | copy-start | bytes 1474564
  135.0 8.8 %copy-start.11 = (bf16[2,96,1280]{2,1,0:T(8,128)(2,1)S(1)}, bf16[2,96,1280]{2,1,0:T(8,128)(2,1)}, u32[]{:S(2)}) copy-start(bf16[2,96,1280]{2,1,0:T(8,128)(2,1)} %copy-done.10) | copy-start | bytes 1474564
  135.0 8.8 %copy-start.13 = (bf16[2,96,1280]{2,1,0:T(8,128)(2,1)S(1)}, bf16[2,96,1280]{2,1,0:T(8,128)(2,1)}, u32[]{:S(2)}) copy-start(bf16[2,96,1280]{2,1,0:T(8,128)(2,1)} %copy-done.12) | copy-start | bytes 1474564
  135.0 8.8 %copy-start.15 = (bf16[2,96,1280]{2,1,0:T(8,128)(2,1)S(1)}, bf16[2,96,1280]{2,1,0:T(8,128)(2,1)}, u32[]{:S(2)}) copy-start(bf16[2,96,1280]{2,1,0:T(8,128)(2,1)} %copy-done.14) | copy-start | bytes 1474564
  136.1 9.1 %copy-start.4 = (bf16[2,96,1280]{2,1,0:T(8,128)(2,1)}, bf16[2,96,1280]{2,1,0:T(8,128)(2,1)S(1)}, u32[]{:S(2)}) copy-start(bf16[2,96,1280]{2,1,0:T(8,128)(2,1)S(1)} %pad_maximum_fusion.3.act) | copy-start | bytes 1474564
  136.1 14.7 %collective-permute-start.25 = (bf16[2,96,1280]{2,1,0:T(8,128)(2,1)S(1)}, bf16[2,96,1280]{2,1,0:T(8,128)(2,1)}, u32[]{:S(2)}, u32[]{:S(2)}) collective-permute-start(bf16[2,96,1280]{2,1,0:T(8,128)(2,1)S(1)} %pad_maximum_fusion.3.act), channel_id=1, source_target_pairs={{4,8},{6,10},{8,4},{10,6},{5,9},{7,11},{9,5},{11,7},{20,24},{22,26... | collective-permute-start | bytes 1474568 | tf_op jit(solution)/shard_map/ppermute | solution.py:162
  137.5 16.1 %collective-permute-start.24 = (bf16[2,96,1280]{2,1,0:T(8,128)(2,1)S(1)}, bf16[2,96,1280]{2,1,0:T(8,128)(2,1)}, u32[]{:S(2)}, u32[]{:S(2)}) collective-permute-start(bf16[2,96,1280]{2,1,0:T(8,128)(2,1)S(1)} %pad_maximum_fusion.3.act), channel_id=1, source_target_pairs={{0,4},{2,6},{12,8},{14,10},{4,0},{6,2},{8,12},{10,14},{1,5},{3,7},... | collective-permute-start | bytes 1474568 | tf_op jit(solution)/shard_map/ppermute | solution.py:162
  146.9 9.5 %collective-permute-start.30 = (f16[2,192,512]{2,1,0:T(8,128)(2,1)S(1)}, f16[2,192,512]{2,1,0:T(8,128)(2,1)S(1)}, u32[]{:S(2)}, u32[]{:S(2)}) collective-permute-start(f16[2,192,512]{2,1,0:T(8,128)(2,1)S(1)} %fusion.18), channel_id=1, source_target_pairs={{4,8},{6,10},{8,4},{10,6},{5,9},{7,11},{9,5},{11,7},{20,24},{22,26... | collective-permute-start | bytes 1179656 | tf_op jit(solution)/shard_map/ppermute | solution.py:162
  147.6 10.1 %collective-permute-start.29 = (f16[2,192,512]{2,1,0:T(8,128)(2,1)S(1)}, f16[2,192,512]{2,1,0:T(8,128)(2,1)S(1)}, u32[]{:S(2)}, u32[]{:S(2)}) collective-permute-start(f16[2,192,512]{2,1,0:T(8,128)(2,1)S(1)} %fusion.39), channel_id=1, source_target_pairs={{0,4},{2,6},{12,8},{14,10},{1,5},{3,7},{13,9},{15,11},{16,20},{18,... | collective-permute-start | bytes 1179656 | tf_op jit(solution)/shard_map/ppermute | solution.py:162
  153.7 10.0 %collective-permute-start.28 = (bf16[2,96,1280]{2,1,0:T(8,128)(2,1)}, bf16[2,96,1280]{2,1,0:T(8,128)(2,1)}, u32[]{:S(2)}, u32[]{:S(2)}) collective-permute-start(bf16[2,96,1280]{2,1,0:T(8,128)(2,1)} %collective-permute-done.24.side_1), channel_id=1, source_target_pairs={{4,8},{6,10},{8,4},{10,6},{5,9},{7,11},{9,5},{11,7},{20,24},{22,26... | collective-permute-start | bytes 1474568 | tf_op jit(solution)/shard_map/ppermute | solution.py:162
  155.1 11.8 %collective-permute-start.27 = (bf16[2,96,1280]{2,1,0:T(8,128)(2,1)}, bf16[2,96,1280]{2,1,0:T(8,128)(2,1)}, u32[]{:S(2)}, u32[]{:S(2)}) collective-permute-start(bf16[2,96,1280]{2,1,0:T(8,128)(2,1)} %collective-permute-done.25.centre_1), channel_id=1, source_target_pairs={{4,0},{6,2},{8,12},{10,14},{5,1},{7,3},{9,13},{11,15},{20,16},{22,... | collective-permute-start | bytes 1474568 | tf_op jit(solution)/shard_map/ppermute | solution.py:162
  159.0 16.4 %collective-permute-start.31 = (f16[2,192,512]{2,1,0:T(8,128)(2,1)}, f16[2,192,512]{2,1,0:T(8,128)(2,1)}, u32[]{:S(2)}, u32[]{:S(2)}) collective-permute-start(f16[2,192,512]{2,1,0:T(8,128)(2,1)} %get-tuple-element.171), channel_id=1, source_target_pairs={{0,4},{2,6},{12,8},{14,10},{4,0},{6,2},{8,12},{10,14},{1,5},{3,7},... | collective-permute-start | bytes 1179656 | tf_op jit(solution)/shard_map/ppermute | solution.py:162
  161.2 14.1 %collective-permute-start.32 = (f16[2,192,512]{2,1,0:T(8,128)(2,1)}, f16[2,192,512]{2,1,0:T(8,128)(2,1)}, u32[]{:S(2)}, u32[]{:S(2)}) collective-permute-start(f16[2,192,512]{2,1,0:T(8,128)(2,1)} %get-tuple-element.172), channel_id=1, source_target_pairs={{4,8},{6,10},{8,4},{10,6},{5,9},{7,11},{9,5},{11,7},{20,24},{22,26... | collective-permute-start | bytes 1179656 | tf_op jit(solution)/shard_map/ppermute | solution.py:162
  166.9 23.9 %collective-permute-start.36 = (bf16[2,96,1280]{2,1,0:T(8,128)(2,1)}, bf16[2,96,1280]{2,1,0:T(8,128)(2,1)S(1)}, u32[]{:S(2)}, u32[]{:S(2)}) collective-permute-start(bf16[2,96,1280]{2,1,0:T(8,128)(2,1)} %collective-permute-done.28.share_2), channel_id=1, source_target_pairs={{4,0},{6,2},{8,12},{10,14},{5,1},{7,3},{9,13},{11,15},{20,16},{22,... | collective-permute-start | bytes 1474568 | tf_op jit(solution)/shard_map/ppermute | solution.py:162
  177.6 13.3 %copy-start.5 = (bf16[2,96,1280]{2,1,0:T(8,128)(2,1)S(1)}, bf16[2,96,1280]{2,1,0:T(8,128)(2,1)}, u32[]{:S(2)}) copy-start(bf16[2,96,1280]{2,1,0:T(8,128)(2,1)} %copy-done.4) | copy-start | bytes 1474564
  179.1 11.8 %collective-permute-start.33 = (bf16[2,48,1792]{2,1,0:T(8,128)(2,1)S(1)}, bf16[2,48,1792]{2,1,0:T(8,128)(2,1)}, u32[]{:S(2)}, u32[]{:S(2)}) collective-permute-start(bf16[2,48,1792]{2,1,0:T(8,128)(2,1)S(1)} %get-tuple-element.185), channel_id=1, source_target_pairs={{0,2},{2,0},{4,6},{6,4},{8,10},{10,8},{12,14},{14,12},{1,3},{3,1},... | collective-permute-start | bytes 1032200 | tf_op jit(solution)/shard_map/ppermute | solution.py:162
  188.7 4.8 %collective-permute-start.35 = (bf16[2,192,512]{2,1,0:T(8,128)(2,1)}, bf16[2,192,512]{2,1,0:T(8,128)(2,1)}, u32[]{:S(2)}, u32[]{:S(2)}) collective-permute-start(bf16[2,192,512]{2,1,0:T(8,128)(2,1)} %pad_maximum_fusion.4.act), channel_id=1, source_target_pairs={{4,8},{6,10},{8,4},{10,6},{5,9},{7,11},{9,5},{11,7},{20,24},{22,26... | collective-permute-start | bytes 1179656 | tf_op jit(solution)/shard_map/ppermute | solution.py:162
  190.1 11.1 %collective-permute-start.34 = (bf16[2,192,512]{2,1,0:T(8,128)(2,1)}, bf16[2,192,512]{2,1,0:T(8,128)(2,1)}, u32[]{:S(2)}, u32[]{:S(2)}) collective-permute-start(bf16[2,192,512]{2,1,0:T(8,128)(2,1)} %pad_maximum_fusion.4.act), channel_id=1, source_target_pairs={{0,4},{2,6},{12,8},{14,10},{4,0},{6,2},{8,12},{10,14},{1,5},{3,7},... | collective-permute-start | bytes 1179656 | tf_op jit(solution)/shard_map/ppermute | solution.py:162
  190.3 27.4 %collective-permute-start.41 = (bf16[4,2,96,1280]{3,2,1,0:T(8,128)(2,1)S(1)}, bf16[4,2,96,1280]{3,2,1,0:T(8,128)(2,1)}, u32[]{:S(2)}, u32[]{:S(2)}) collective-permute-start(bf16[4,2,96,1280]{3,2,1,0:T(8,128)(2,1)S(1)} %shard_map.72), channel_id=1, source_target_pairs={{0,2},{2,0},{4,6},{6,4},{8,10},{10,8},{12,14},{14,12},{1,3},{3,1},... | collective-permute-start | bytes 5898248 | tf_op jit(solution)/shard_map/ppermute | solution.py:162
  193.5 24.1 %collective-permute-start.42 = (bf16[4,2,96,1280]{3,2,1,0:T(8,128)(2,1)}, bf16[4,2,96,1280]{3,2,1,0:T(8,128)(2,1)}, u32[]{:S(2)}, u32[]{:S(2)}) collective-permute-start(bf16[4,2,96,1280]{3,2,1,0:T(8,128)(2,1)} %shard_map.73), channel_id=1, source_target_pairs={{0,2},{2,0},{4,6},{6,4},{8,10},{10,8},{12,14},{14,12},{1,3},{3,1},... | collective-permute-start | bytes 5898248 | tf_op jit(solution)/shard_map/ppermute | solution.py:162
  201.2 14.4 %collective-permute-start.39 = (bf16[2,192,512]{2,1,0:T(8,128)(2,1)}, bf16[2,192,512]{2,1,0:T(8,128)(2,1)}, u32[]{:S(2)}, u32[]{:S(2)}) collective-permute-start(bf16[2,192,512]{2,1,0:T(8,128)(2,1)} %collective-permute-done.34.side_1), channel_id=1, source_target_pairs={{4,8},{6,10},{8,4},{10,6},{5,9},{7,11},{9,5},{11,7},{20,24},{22,26... | collective-permute-start | bytes 1179656 | tf_op jit(solution)/shard_map/ppermute | solution.py:162
  202.7 12.9 %collective-permute-start.38 = (bf16[2,192,512]{2,1,0:T(8,128)(2,1)}, bf16[2,192,512]{2,1,0:T(8,128)(2,1)S(1)}, u32[]{:S(2)}, u32[]{:S(2)}) collective-permute-start(bf16[2,192,512]{2,1,0:T(8,128)(2,1)} %collective-permute-done.35.centre_1), channel_id=1, source_target_pairs={{4,0},{6,2},{8,12},{10,14},{5,1},{7,3},{9,13},{11,15},{20,16},{22,... | collective-permute-start | bytes 1179656 | tf_op jit(solution)/shard_map/ppermute | solution.py:162
  206.3 11.3 %collective-permute-start.37 = (bf16[48,3584]{1,0:T(8,128)(2,1)}, bf16[48,3584]{1,0:T(8,128)(2,1)}, u32[]{:S(2)}, u32[]{:S(2)}) collective-permute-start(bf16[48,3584]{1,0:T(8,128)(2,1)} %get-tuple-element.184), channel_id=1, source_target_pairs={{0,1},{1,0},{2,3},{3,2},{4,5},{5,4},{6,7},{7,6},{8,9},{9,8},{10,11... | collective-permute-start | bytes 1032200 | tf_op jit(solution)/shard_map/ppermute | solution.py:304
  216.4 11.8 %collective-permute-start.40 = (bf16[2,192,512]{2,1,0:T(8,128)(2,1)}, bf16[2,192,512]{2,1,0:T(8,128)(2,1)}, u32[]{:S(2)}, u32[]{:S(2)}) collective-permute-start(bf16[2,192,512]{2,1,0:T(8,128)(2,1)} %collective-permute-done.39.share_2), channel_id=1, source_target_pairs={{4,0},{6,2},{8,12},{10,14},{5,1},{7,3},{9,13},{11,15},{20,16},{22,... | collective-permute-start | bytes 1179656 | tf_op jit(solution)/shard_map/ppermute | solution.py:162
  217.7 10.4 %copy-start.19 = (bf16[2,192,512]{2,1,0:T(8,128)(2,1)S(1)}, bf16[2,192,512]{2,1,0:T(8,128)(2,1)}, u32[]{:S(2)}) copy-start(bf16[2,192,512]{2,1,0:T(8,128)(2,1)} %copy-done.18) | copy-start | bytes 1179652
  229.9 7.6 %collective-permute-start.43 = (bf16[4,2,192,512]{3,2,1,0:T(8,128)(2,1)S(1)}, bf16[4,2,192,512]{3,2,1,0:T(8,128)(2,1)}, u32[]{:S(2)}, u32[]{:S(2)}) collective-permute-start(bf16[4,2,192,512]{3,2,1,0:T(8,128)(2,1)S(1)} %shard_map.76), channel_id=1, source_target_pairs={{0,2},{2,0},{4,6},{6,4},{8,10},{10,8},{12,14},{14,12},{1,3},{3,1},... | collective-permute-start | bytes 4718600 | tf_op jit(solution)/shard_map/ppermute | solution.py:162
  (14 other events, 34.7 us)

commit v14 on v13

--- a/solution.py
+++ b/solution.py
@@ -12,47 +12,59 @@
 LARGEST_TOKEN, LARGEST_WEIGHT = 6.0, 0.0625
 VMEM_LIMIT = 48 * 2**20
 NO_COST = pl.CostEstimate(flops=0, bytes_accessed=0, transcendentals=0)
+LONG = pl.CostEstimate(flops=6 * 10**9, bytes_accessed=0, transcendentals=0)
 SHARES = (5, 2)
 
 
-def forward_kernel(scale, place_ref, *refs):
-    tokens, weights, out_ref = refs[: len(refs) // 3], refs[len(refs) // 3 : -1], refs[-1]
-    blocks, _, rows, width = out_ref.shape
-    for which in range(2):
-        product = sum(
-            jnp.dot(
-                rows_ref[...],
-                weight_ref[...].reshape(weight_ref.shape[-2:]),
-                preferred_element_type=jnp.float32,
+def forward_kernel(scale, start, cores, place_ref, *refs):
+    tokens, weights = refs[:cores], refs[cores : cores + 2 * cores]
+    out_ref, held, arrived = refs[3 * cores :]
+    tiles, _, tile = held.shape[1:]
+    blocks, _, rows, _ = out_ref.shape
+
+    def copy(j, which):
+        first = start + j * tile
+        if which < 2:
+            columns = pl.ds(pl.multiple_of(place_ref[0] * tile + first, tile), tile)
+            source = weights[which].at[:, columns]
+        else:
+            source = weights[which].at[which - 2, :, pl.ds(j * tile, tile)]
+        return pltpu.make_async_copy(source, held.at[which, j], arrived.at[which, j])
+
+    for j in range(tiles):
+        for which in range(2 * cores):
+            copy(j, which).start()
+    for j in range(tiles):
+        for which in range(2 * cores):
+            copy(j, which).wait()
+        for which in range(2):
+            product = sum(
+                jnp.dot(
+                    tokens[i][...], held[which + 2 * i, j], preferred_element_type=jnp.float32
+                )
+                for i in range(cores)
             )
-            for rows_ref, weight_ref in zip(tokens, weights[which::2])
-        )
-        out_ref[:, which] = (scale * product).reshape(blocks, rows, width)
-
-
-def forward(place, tokens, weights, start, width, tile, blocks, scale):
+            product = (scale * product).reshape(blocks, rows, tile)
+            out_ref[:, which, :, j * tile : (j + 1) * tile] = product
+
+
+def forward(place, tokens, weights, start, width, tile, blocks, scale, cost=NO_COST):
     total, depth = tokens[0].shape
-    rows = total // blocks
-    far = len(tokens) - 1
-    in_specs = [pl.BlockSpec((total, depth), lambda j, place: (0, 0))] * len(tokens)
-    in_specs += [
-        pl.BlockSpec((depth, tile), lambda j, place: (0, place[0] + start // tile + j))
-    ] * 2
-    in_specs += [
-        pl.BlockSpec((1, depth, tile), lambda j, place, which=which: (which, 0, j))
-        for which in range(2 * far)
-    ]
+    cores = len(tokens)
+    shape = (blocks, 2, total // blocks, width)
     return pl.pallas_call(
-        functools.partial(forward_kernel, scale),
-        out_shape=jax.ShapeDtypeStruct((blocks, 2, rows, width), jnp.float32),
-        grid_spec=pltpu.PrefetchScalarGridSpec(
-            num_scalar_prefetch=1,
-            grid=(width // tile,),
-            in_specs=in_specs,
-            out_specs=pl.BlockSpec((blocks, 2, rows, tile), lambda j, place: (0, 0, 0, j)),
-        ),
+        functools.partial(forward_kernel, scale, start, cores),
+        out_shape=jax.ShapeDtypeStruct(shape, jnp.float32),
+        in_specs=[pl.BlockSpec(memory_space=pltpu.SMEM)]
+        + [pl.BlockSpec(memory_space=pltpu.VMEM)] * cores
+        + [pl.BlockSpec(memory_space=pl.ANY)] * (2 * cores),
+        out_specs=pl.BlockSpec(memory_space=pltpu.VMEM),
+        scratch_shapes=[
+            pltpu.VMEM((2 * cores, width // tile, depth, tile), jnp.bfloat16),
+            pltpu.SemaphoreType.DMA((2 * cores, width // tile)),
+        ],
         compiler_params=pltpu.CompilerParams(vmem_limit_bytes=VMEM_LIMIT),
-        cost_estimate=NO_COST,
+        cost_estimate=cost,
     )(place, *tokens, *weights)
 
 
@@ -210,8 +222,8 @@
         common = ((gate_weight, up_weight), start, width, tile, line, scale)
         payload = forward(other_tile, [tokens], *common).astype(wire)
 
-        def own(after):
-            return forward(own_tile, [tie(tokens, payload, after)], *common)
+        def own(after, cost=NO_COST):
+            return forward(own_tile, [tie(tokens, payload, after)], *common, cost)
 
         return payload, own
 
@@ -225,12 +237,7 @@
         own, theirs = terms
         return own[block] if theirs is None else own[block] + wide(theirs[block])
 
-    cotangent = grad_hidden[0]
-    cotangent = (
-        columns_of(cotangent, part * half, half),
-        lax.ppermute(columns_of(cotangent, (1 - part) * half, half), "depth", swap),
-    )
-    over_row = tie(over_row, over_depth, cotangent)
+    over_row = tie(over_row, over_depth)
     features = [arrange(by(row == 0, mine, over_row, 1))]
     theirs, own = own_features(features[0], 0, (), WIRE)
     terms = (own(()), send(theirs, pairs))
@@ -294,8 +301,13 @@
             side_1, centre_1 = tie((side_1, centre_1), before)
             out_2, share_2 = send(centre_1, outward), send(side_1, centre)
         if k < 0:
-            products[1] = (own((far, near)), send(theirs, pairs))
-            terms = tie(terms, products[1])
+            products[1] = (own((far, near), LONG), send(theirs, pairs))
+            cotangent = tie(grad_hidden[0], far, near)
+            cotangent = (
+                columns_of(cotangent, part * half, half),
+                lax.ppermute(columns_of(cotangent, (1 - part) * half, half), "depth", swap),
+            )
+            terms = tie(terms, products[1], cotangent[1])
         if not adding:
             own_acts, other_acts = zip(*merged)
             totals = add_gradients(own_acts, core, (), pieces[0][1])

time: 244 us -> 234 us (0.959)
  waiting for transfers between devices: 57.4 us -> 50.7 us
  Pallas kernels: 58.6 us -> 53.1 us
  other arithmetic: 26.9 us -> 30.3 us
    ppermute x1, waiting for transfers between devices: 13.1 us -> 4 us  [local(): lax.ppermute(columns_of(cotangent, (1 - part) * half, half), 'depth', swap)]
    ppermute x1, waiting for transfers between devices: 0.01 us -> 7.84 us  [local(): over_depth = lax.ppermute(mine, 'depth', swap)]
    pallas_call x5, Pallas kernels: 28.9 us -> 23.4 us  [forward(): pl.pallas_call(functools.partial(forward_kernel, scale, start, cores), ou...]
    ppermute x39, waiting for transfers between devices: 38.4 us -> 33.9 us  [send(): return lax.ppermute(value, 'col', route)]
    unnamed x68 -> x58, local copies, waits for them, and re-layouts: 5.98 us -> 7.99 us
  transfers between devices with their start and end apart: 44 -> 44, of which waited for: 12 -> 12; matrix products, arithmetic and copies ran while one was open for 13% -> 14% of each run, Pallas kernels for 19% -> 18%
where the time goes in v14:
time: 234 us; the launch traced here: 233 us
  starting transfers between devices  80.9 us (35%)
  Pallas kernels  53.1 us (23%)
  waiting for transfers between devices  50.7 us (22%)
  other arithmetic  30.3 us (13%)
  local copies, waits for them, and re-layouts  16.5 us (7%)
    ppermute x39, starting transfers between devices, send(): return lax.ppermute(value, 'col', route)  76.9 us
    ppermute x39, waiting for transfers between devices, send(): return lax.ppermute(value, 'col', route)  33.9 us
    pallas_call x4, Pallas kernels, gradient(): pl.pallas_call(functools.partial(gradient_kernel, len(acts)), out_shape=(...  24.9 us
    pallas_call x5, Pallas kernels, forward(): pl.pallas_call(functools.partial(forward_kernel, scale, start, cores), ou...  23.4 us
    unnamed x58, local copies, waits for them, and re-layouts  7.99 us
    ppermute x1, waiting for transfers between devices, local(): over_depth = lax.ppermute(mine, 'depth', swap)  7.84 us
    select_n x5, other arithmetic, by(): jnp.where(first, jnp.concatenate([mine, theirs], axis=axis), jnp.concaten...  6.35 us
    convert_element_type x3, other arithmetic, local(): swapped = swapped.astype(WIRE)  4.97 us
  transfers between devices with their start and end apart: 44, of which 12 were waited for; matrix products, arithmetic and copies ran while one was open for 14% of the time, Pallas kernels for 18%

profile of v14, /device:TPU:1, one launch (start us, length us, event | category | flops | bytes accessed | tf_op | source)
XLA Modules:
  0.0 232.8 jit_solution(2559196215452864049)
XLA Ops:
  0.6 2.1 collective-permute-start.1
  4.0 7.8 %collective-permute-done.1 = bf16[384,512]{1,0:T(8,128)(2,1)S(1)} collective-permute-done((bf16[384,512]{1,0:T(8,128)(2,1)}, bf16[384,512]{1,0:T(8,128)(2,1)S(1)}, u32[]{:S(2)}, u32[]{:S(2)}) %collective-permute-start.1) | collective-permute-done | bytes 393248 | tf_op jit(solution)/shard_map/ppermute | solution.py:208
  12.6 1.3 maximum_select_fusion
  14.2 4.2 %shard_map.67 = f32[4,2,96,1280]{3,2,1,0:T(8,128)S(1)} custom-call(s32[1]{0:T(128)} %bitcast.5.place_ref, bf16[384,1024]{1,0:T(8,128)(2,1)S(1)} %bitcast.152, bf16[1024,7168]{1,0:T(8,128)(2,1)} %refs_2_.9, bf16[1024,7168]{1,0:T(8,128)(2,1)} %refs_3_.1), custom_call_target="tpu_custom_call" | custom-call | tf_op jit(solution)/shard_map/pallas_call | solution.py:55
  18.4 1.5 convert_element_type.194
  19.9 1.9 collective-permute-start.2
  21.8 4.2 %shard_map.68 = f32[4,2,96,1280]{3,2,1,0:T(8,128)S(1)} custom-call(s32[1]{0:T(128)} %bitcast.place_ref, bf16[384,1024]{1,0:T(8,128)(2,1)S(1)} %bitcast.153, bf16[1024,7168]{1,0:T(8,128)(2,1)} %refs_2_.9, bf16[1024,7168]{1,0:T(8,128)(2,1)} %refs_3_.1), custom_call_target="tpu_custom_call" | custom-call | tf_op jit(solution)/shard_map/pallas_call | solution.py:55
  26.1 1.8 copy-done.2
  28.8 4.0 %collective-permute-start.4 = (f16[2,96,1280]{2,1,0:T(8,128)(2,1)}, f16[2,96,1280]{2,1,0:T(8,128)(2,1)}, u32[]{:S(2)}, u32[]{:S(2)}) collective-permute-start(f16[2,96,1280]{2,1,0:T(8,128)(2,1)} %fusion.32), channel_id=1, source_target_pairs={{0,4},{2,6},{12,8},{14,10},{1,5},{3,7},{13,9},{15,11},{16,20},{18,... | collective-permute-start | bytes 1474568 | tf_op jit(solution)/shard_map/ppermute | solution.py:174
  32.7 4.1 %collective-permute-done.3 = bf16[384,512]{1,0:T(8,128)(2,1)} collective-permute-done((bf16[384,512]{1,0:T(8,128)(2,1)S(1)}, bf16[384,512]{1,0:T(8,128)(2,1)}, u32[]{:S(2)}, u32[]{:S(2)}) %collective-permute-start.3) | collective-permute-done | bytes 393248 | tf_op jit(solution)/shard_map/ppermute | solution.py:209
  36.9 1.3 maximum_select_fusion.1
  38.4 4.2 %shard_map.69 = f32[4,2,96,1280]{3,2,1,0:T(8,128)S(1)} custom-call(s32[1]{0:T(128)} %bitcast.5.place_ref, bf16[384,1024]{1,0:T(8,128)(2,1)S(1)} %bitcast.156, bf16[1024,7168]{1,0:T(8,128)(2,1)} %refs_2_.9, bf16[1024,7168]{1,0:T(8,128)(2,1)} %refs_3_.1), custom_call_target="tpu_custom_call" | custom-call | tf_op jit(solution)/shard_map/pallas_call | solution.py:55
  44.7 2.0 fusion.12
  46.7 1.4 collective-permute-start.7
  49.0 5.7 %collective-permute-start.9 = (f16[2,96,1280]{2,1,0:T(8,128)(2,1)}, f16[2,96,1280]{2,1,0:T(8,128)(2,1)}, u32[]{:S(2)}, u32[]{:S(2)}) collective-permute-start(f16[2,96,1280]{2,1,0:T(8,128)(2,1)} %fusion.29), channel_id=1, source_target_pairs={{0,4},{2,6},{12,8},{14,10},{1,5},{3,7},{13,9},{15,11},{16,20},{18,... | collective-permute-start | bytes 1474568 | tf_op jit(solution)/shard_map/ppermute | solution.py:174
  55.8 4.2 %shard_map.70 = f32[4,2,96,1280]{3,2,1,0:T(8,128)S(1)} custom-call(s32[1]{0:T(128)} %bitcast.place_ref, bf16[384,1024]{1,0:T(8,128)(2,1)S(1)} %bitcast.157, bf16[1024,7168]{1,0:T(8,128)(2,1)} %refs_2_.9, bf16[1024,7168]{1,0:T(8,128)(2,1)} %refs_3_.1), custom_call_target="tpu_custom_call" | custom-call | flops 6000000000 | tf_op jit(solution)/shard_map/pallas_call | solution.py:55
  60.0 4.0 %collective-permute-done.6 = bf16[48,3584]{1,0:T(8,128)(2,1)S(1)} collective-permute-done((bf16[48,3584]{1,0:T(8,128)(2,1)}, bf16[48,3584]{1,0:T(8,128)(2,1)S(1)}, u32[]{:S(2)}, u32[]{:S(2)}) %collective-permute-start.6) | collective-permute-done | bytes 344096 | tf_op jit(solution)/shard_map/ppermute | solution.py:308
  64.0 2.3 %fusion.11 = (f16[2,96,1280]{2,1,0:T(8,128)(2,1)S(1)}, f16[2,96,1280]{2,1,0:T(8,128)(2,1)S(1)}) fusion(f16[2,96,1280]{2,1,0:T(8,128)(2,1)} %collective-permute-done.7, f32[4,2,96,1280]{3,2,1,0:T(8,128)S(1)} %copy-done.3, pred[]{:T(512)S(6)} %or.3, f16[4,2,96,1280]{3,2,1,0:T(8,128)(2,1)S(1)} %collective-permute-done.2, ...), kind=kLoop, calls=%fused_computation.26 | loop fusion | flops 3194880 | bytes 6389761 | tf_op jit(solution)/shard_map/convert_element_type | solution.py:324
  66.4 1.3 collective-permute-start.8
  68.4 2.3 %collective-permute-start.12 = (bf16[2,48,1792]{2,1,0:T(8,128)(2,1)S(1)}, bf16[2,48,1792]{2,1,0:T(8,128)(2,1)S(1)}, u32[]{:S(2)}, u32[]{:S(2)}) collective-permute-start(bf16[2,48,1792]{2,1,0:T(8,128)(2,1)S(1)} %get-tuple-element.192), channel_id=1, source_target_pairs={{0,2},{2,0},{4,6},{6,4},{8,10},{10,8},{12,14},{14,12},{1,3},{3,1},... | collective-permute-start | bytes 1032200 | tf_op jit(solution)/shard_map/ppermute | solution.py:174
  71.7 4.9 %collective-permute-start.16 = (f16[2,96,1280]{2,1,0:T(8,128)(2,1)}, f16[2,96,1280]{2,1,0:T(8,128)(2,1)}, u32[]{:S(2)}, u32[]{:S(2)}) collective-permute-start(f16[2,96,1280]{2,1,0:T(8,128)(2,1)} %fusion.30), channel_id=1, source_target_pairs={{0,4},{2,6},{12,8},{14,10},{1,5},{3,7},{13,9},{15,11},{16,20},{18,... | collective-permute-start | bytes 1474568 | tf_op jit(solution)/shard_map/ppermute | solution.py:174
  76.5 1.7 dynamic-slice_bitcast_fusion
  82.6 1.4 collective-permute-start.14
  85.2 6.7 %shard_map.71 = f32[4,2,192,512]{3,2,1,0:T(8,128)} custom-call(s32[1]{0:T(128)} %bitcast.place_ref, bf16[768,1024]{1,0:T(8,128)(2,1)S(1)} %bitcast.161, bf16[768,1024]{1,0:T(8,128)(2,1)S(1)} %bitcast.162, bf16[1024,7168]{1,0:T(8,128)(2,1)} %refs_2_.9, bf16[1024,7168]{1,0:T(8,128)(2,1)} %refs_3_.1, ...), custom_call_target="tpu_custom_call" | custom-call | tf_op jit(solution)/shard_map/pallas_call | solution.py:55
  93.9 3.7 %collective-permute-start.19 = (f16[2,96,1280]{2,1,0:T(8,128)(2,1)S(1)}, f16[2,96,1280]{2,1,0:T(8,128)(2,1)S(1)}, u32[]{:S(2)}, u32[]{:S(2)}) collective-permute-start(f16[2,96,1280]{2,1,0:T(8,128)(2,1)S(1)} %fusion.31), channel_id=1, source_target_pairs={{0,4},{2,6},{12,8},{14,10},{1,5},{3,7},{13,9},{15,11},{16,20},{18,... | collective-permute-start | bytes 1474568 | tf_op jit(solution)/shard_map/ppermute | solution.py:174
  98.4 1.3 collective-permute-start.17
  99.7 8.3 %collective-permute-done.19 = f16[2,96,1280]{2,1,0:T(8,128)(2,1)S(1)} collective-permute-done((f16[2,96,1280]{2,1,0:T(8,128)(2,1)S(1)}, f16[2,96,1280]{2,1,0:T(8,128)(2,1)S(1)}, u32[]{:S(2)}, u32[]{:S(2)}) %collective-permute-start.19) | collective-permute-done | bytes 491552 | tf_op jit(solution)/shard_map/ppermute | solution.py:174
  108.0 1.4 fusion.4
  109.4 2.2 collective-permute-start.22
  111.6 1.4 collective-permute-start.23
  113.0 1.3 collective-permute-start.21
  116.7 1.6 maximum_bitcast_fusion.features_ref
  119.5 4.2 %collective-permute-start.26 = (f16[2,192,512]{2,1,0:T(8,128)(2,1)S(1)}, f16[2,192,512]{2,1,0:T(8,128)(2,1)S(1)}, u32[]{:S(2)}, u32[]{:S(2)}) collective-permute-start(f16[2,192,512]{2,1,0:T(8,128)(2,1)S(1)} %fusion.38), channel_id=1, source_target_pairs={{0,4},{2,6},{12,8},{14,10},{1,5},{3,7},{13,9},{15,11},{16,20},{18,... | collective-permute-start | bytes 1179656 | tf_op jit(solution)/shard_map/ppermute | solution.py:174
  123.7 1.9 fusion.2
  126.8 1.4 collective-permute-start.25
  128.2 4.1 %collective-permute-start.24 = (bf16[2,96,1280]{2,1,0:T(8,128)(2,1)S(1)}, bf16[2,96,1280]{2,1,0:T(8,128)(2,1)}, u32[]{:S(2)}, u32[]{:S(2)}) collective-permute-start(bf16[2,96,1280]{2,1,0:T(8,128)(2,1)S(1)} %pad_maximum_fusion.3.act), channel_id=1, source_target_pairs={{0,4},{2,6},{12,8},{14,10},{4,0},{6,2},{8,12},{10,14},{1,5},{3,7},... | collective-permute-start | bytes 1474568 | tf_op jit(solution)/shard_map/ppermute | solution.py:174
  132.3 1.8 collective-permute-done.21.out_3
  136.3 1.6 copy-done.20
  138.8 2.6 %collective-permute-start.29 = (f16[2,192,512]{2,1,0:T(8,128)(2,1)S(1)}, f16[2,192,512]{2,1,0:T(8,128)(2,1)S(1)}, u32[]{:S(2)}, u32[]{:S(2)}) collective-permute-start(f16[2,192,512]{2,1,0:T(8,128)(2,1)S(1)} %fusion.39), channel_id=1, source_target_pairs={{0,4},{2,6},{12,8},{14,10},{1,5},{3,7},{13,9},{15,11},{16,20},{18,... | collective-permute-start | bytes 1179656 | tf_op jit(solution)/shard_map/ppermute | solution.py:174
  141.4 3.4 %collective-permute-done.24.side_1 = bf16[2,96,1280]{2,1,0:T(8,128)(2,1)} collective-permute-done((bf16[2,96,1280]{2,1,0:T(8,128)(2,1)S(1)}, bf16[2,96,1280]{2,1,0:T(8,128)(2,1)}, u32[]{:S(2)}, u32[]{:S(2)}) %collective-permute-start.24) | collective-permute-done | bytes 491552 | tf_op jit(solution)/shard_map/ppermute | solution.py:174
  144.8 1.4 collective-permute-start.28
  146.2 1.3 collective-permute-start.27
  147.5 4.3 %collective-permute-done.29 = f16[2,192,512]{2,1,0:T(8,128)(2,1)S(1)} collective-permute-done((f16[2,192,512]{2,1,0:T(8,128)(2,1)S(1)}, f16[2,192,512]{2,1,0:T(8,128)(2,1)S(1)}, u32[]{:S(2)}, u32[]{:S(2)}) %collective-permute-start.29) | collective-permute-done | bytes 393248 | tf_op jit(solution)/shard_map/ppermute | solution.py:174
  151.9 1.2 fusion.15
  153.1 2.2 collective-permute-start.31
  155.3 1.4 collective-permute-start.32
  157.7 1.3 collective-permute-start.36
  159.0 6.9 %collective-permute-done.31 = f16[2,192,512]{2,1,0:T(8,128)(2,1)} collective-permute-done((f16[2,192,512]{2,1,0:T(8,128)(2,1)}, f16[2,192,512]{2,1,0:T(8,128)(2,1)}, u32[]{:S(2)}, u32[]{:S(2)}) %collective-permute-start.31) | collective-permute-done | bytes 393248 | tf_op jit(solution)/shard_map/ppermute | solution.py:174
  165.9 1.9 fusion.17
  169.7 10.0 %collective-permute-start.33 = (bf16[2,48,1792]{2,1,0:T(8,128)(2,1)S(1)}, bf16[2,48,1792]{2,1,0:T(8,128)(2,1)}, u32[]{:S(2)}, u32[]{:S(2)}) collective-permute-start(bf16[2,48,1792]{2,1,0:T(8,128)(2,1)S(1)} %get-tuple-element.187), channel_id=1, source_target_pairs={{0,2},{2,0},{4,6},{6,4},{8,10},{10,8},{12,14},{14,12},{1,3},{3,1},... | collective-permute-start | bytes 1032200 | tf_op jit(solution)/shard_map/ppermute | solution.py:174
  180.4 1.4 collective-permute-start.35
  182.9 2.7 %shard_map.73 = bf16[4,2,96,1280]{3,2,1,0:T(8,128)(2,1)} custom-call(s32[1]{0:T(128)} %bitcast.28.at_end_ref, bf16[2,96,1280]{2,1,0:T(8,128)(2,1)S(1)} %copy-done.5, bf16[2,96,1280]{2,1,0:T(8,128)(2,1)} %collective-permute-done.24.side_1, bf16[2,96,1280]{2,1,0:T(8,128)(2,1)} %collective-permute-done.25.centre_1, ...), custom_call_target="tpu_custom_call" | custom-call | tf_op jit(solution)/shard_map/pallas_call | solution.py:126
  185.6 7.3 %collective-permute-done.34.side_1 = bf16[2,192,512]{2,1,0:T(8,128)(2,1)} collective-permute-done((bf16[2,192,512]{2,1,0:T(8,128)(2,1)}, bf16[2,192,512]{2,1,0:T(8,128)(2,1)}, u32[]{:S(2)}, u32[]{:S(2)}) %collective-permute-start.34) | collective-permute-done | bytes 393248 | tf_op jit(solution)/shard_map/ppermute | solution.py:174
  192.9 1.5 collective-permute-start.39
  194.4 1.5 collective-permute-start.38
  195.9 1.5 maximum_select_fusion.3
  198.5 8.0 %shard_map.74 = (f32[1024,3584]{1,0:T(8,128)}, f32[1024,3584]{1,0:T(8,128)}) custom-call(s32[1]{0:T(128)} %bitcast.63.place_ref, bf16[1024,768]{1,0:T(8,128)(2,1)S(1)} %maximum_bitcast_fusion.features_ref, bf16[4,1,2,96,1280]{4,3,2,1,0:T(8,128)(2,1)S(1)} %bitcast.163, bf16[4,1,2,96,1280]{4,3,2,1,0:T(8,128)(2,1)} %bitcast.65.refs_1_), custom_call_target="tpu_custom_call" | custom-call | flops 4026531840 | bytes 15990784 | tf_op jit(solution)/shard_map/pallas_call | solution.py:95
  207.3 1.3 collective-permute-start.40
  208.6 9.0 %shard_map.75 = (f32[1024,3584]{1,0:T(8,128)}, f32[1024,3584]{1,0:T(8,128)}) custom-call(s32[1]{0:T(128)} %bitcast.62.place_ref, bf16[1024,768]{1,0:T(8,128)(2,1)S(1)} %maximum_bitcast_fusion.features_ref, bf16[4,1,2,96,1280]{4,3,2,1,0:T(8,128)(2,1)} %bitcast.66.refs_0_, ...), custom_call_target="tpu_custom_call", output_to_operand_aliasing={{0}: (4, {}), {1}: (5, {})} | custom-call | flops 4026531840 | bytes 15990784 | tf_op jit(solution)/shard_map/pallas_call | solution.py:95
  218.6 1.8 shard_map.76
  220.4 2.5 %collective-permute-start.43 = (bf16[4,2,192,512]{3,2,1,0:T(8,128)(2,1)S(1)}, bf16[4,2,192,512]{3,2,1,0:T(8,128)(2,1)}, u32[]{:S(2)}, u32[]{:S(2)}) collective-permute-start(bf16[4,2,192,512]{3,2,1,0:T(8,128)(2,1)S(1)} %shard_map.76), channel_id=1, source_target_pairs={{0,2},{2,0},{4,6},{6,4},{8,10},{10,8},{12,14},{14,12},{1,3},{3,1},... | collective-permute-start | bytes 4718600 | tf_op jit(solution)/shard_map/ppermute | solution.py:174
  222.8 2.1 maximum_select_fusion.4
  224.9 3.4 %shard_map.77 = (f32[1024,3584]{1,0:T(8,128)}, f32[1024,3584]{1,0:T(8,128)}) custom-call(s32[1]{0:T(128)} %bitcast.63.place_ref, bf16[1024,768]{1,0:T(8,128)(2,1)S(1)} %maximum_bitcast_fusion.features_ref, bf16[4,1,2,192,512]{4,3,2,1,0:T(8,128)(2,1)S(1)} %bitcast.160, ...), custom_call_target="tpu_custom_call", output_to_operand_aliasing={{0}: (3, {}), {1}: (4, {})} | custom-call | flops 1610612736 | bytes 7340032 | tf_op jit(solution)/shard_map/pallas_call | solution.py:95
  228.4 4.4 %shard_map.78 = (f32[1024,3584]{1,0:T(8,128)}, f32[1024,3584]{1,0:T(8,128)}) custom-call(s32[1]{0:T(128)} %bitcast.62.place_ref, bf16[1024,768]{1,0:T(8,128)(2,1)S(1)} %maximum_bitcast_fusion.features_ref, bf16[4,1,2,192,512]{4,3,2,1,0:T(8,128)(2,1)} %bitcast.68.refs_0_, ...), custom_call_target="tpu_custom_call", output_to_operand_aliasing={{0}: (3, {}), {1}: (4, {})} | custom-call | flops 1610612736 | bytes 7340032 | tf_op jit(solution)/shard_map/pallas_call | solution.py:95
  (142 shorter events, 32.6 us)
Async XLA Ops:
  0.6 11.2 %collective-permute-start.1 = (bf16[384,512]{1,0:T(8,128)(2,1)}, bf16[384,512]{1,0:T(8,128)(2,1)S(1)}, u32[]{:S(2)}, u32[]{:S(2)}) collective-permute-start(bf16[384,512]{1,0:T(8,128)(2,1)} %bitcast.170), channel_id=1, source_target_pairs={{0,1},{1,0},{2,3},{3,2},{4,5},{5,4},{6,7},{7,6},{8,9},{9,8},{10,11... | collective-permute-start | bytes 1179656 | tf_op jit(solution)/shard_map/ppermute | solution.py:208
  2.8 9.9 %collective-permute-start = (bf16[384,512]{1,0:T(8,128)(2,1)}, bf16[384,512]{1,0:T(8,128)(2,1)S(1)}, u32[]{:S(2)}, u32[]{:S(2)}) collective-permute-start(bf16[384,512]{1,0:T(8,128)(2,1)} %bitcast.171), channel_id=1, source_target_pairs={{0,16},{16,0},{1,17},{17,1},{2,18},{18,2},{3,19},{19,3},{4,20},{20... | collective-permute-start | bytes 1179656 | tf_op jit(solution)/shard_map/ppermute | solution.py:207
  19.9 6.2 %collective-permute-start.2 = (f16[4,2,96,1280]{3,2,1,0:T(8,128)(2,1)}, f16[4,2,96,1280]{3,2,1,0:T(8,128)(2,1)S(1)}, u32[]{:S(2)}, u32[]{:S(2)}) collective-permute-start(f16[4,2,96,1280]{3,2,1,0:T(8,128)(2,1)} %convert_element_type.194), channel_id=1, source_target_pairs={{0,2},{2,0},{4,6},{6,4},{8,10},{10,8},{12,14},{14,12},{1,3},{3,1},... | collective-permute-start | bytes 5898248 | tf_op jit(solution)/shard_map/ppermute | solution.py:174
  25.9 10.9 %collective-permute-start.3 = (bf16[384,512]{1,0:T(8,128)(2,1)S(1)}, bf16[384,512]{1,0:T(8,128)(2,1)}, u32[]{:S(2)}, u32[]{:S(2)}) collective-permute-start(bf16[384,512]{1,0:T(8,128)(2,1)S(1)} %collective-permute-done), channel_id=1, source_target_pairs={{0,1},{1,0},{2,3},{3,2},{4,5},{5,4},{6,7},{7,6},{8,9},{9,8},{10,11... | collective-permute-start | bytes 1179656 | tf_op jit(solution)/shard_map/ppermute | solution.py:209
  28.8 15.0 %collective-permute-start.4 = (f16[2,96,1280]{2,1,0:T(8,128)(2,1)}, f16[2,96,1280]{2,1,0:T(8,128)(2,1)}, u32[]{:S(2)}, u32[]{:S(2)}) collective-permute-start(f16[2,96,1280]{2,1,0:T(8,128)(2,1)} %fusion.32), channel_id=1, source_target_pairs={{0,4},{2,6},{12,8},{14,10},{1,5},{3,7},{13,9},{15,11},{16,20},{18,... | collective-permute-start | bytes 1474568 | tf_op jit(solution)/shard_map/ppermute | solution.py:174
  42.8 11.9 %copy-start.28 = (bf16[1,48,7168]{2,1,0:T(8,128)(2,1)S(1)}, bf16[1,48,7168]{2,1,0:T(8,128)(2,1)}, u32[]{:S(2)}) copy-start(bf16[1,48,7168]{2,1,0:T(8,128)(2,1)} %param.7) | copy-start | bytes 2064388
  42.9 21.1 %collective-permute-start.5 = (f16[4,2,96,1280]{3,2,1,0:T(8,128)(2,1)S(1)}, f16[4,2,96,1280]{3,2,1,0:T(8,128)(2,1)S(1)}, u32[]{:S(2)}, u32[]{:S(2)}) collective-permute-start(f16[4,2,96,1280]{3,2,1,0:T(8,128)(2,1)S(1)} %convert_element_type.198), channel_id=1, source_target_pairs={{0,2},{2,0},{4,6},{6,4},{8,10},{10,8},{12,14},{14,12},{1,3},{3,1},... | collective-permute-start | bytes 5898248 | tf_op jit(solution)/shard_map/ppermute | solution.py:174
  46.7 17.3 %collective-permute-start.7 = (f16[2,96,1280]{2,1,0:T(8,128)(2,1)}, f16[2,96,1280]{2,1,0:T(8,128)(2,1)}, u32[]{:S(2)}, u32[]{:S(2)}) collective-permute-start(f16[2,96,1280]{2,1,0:T(8,128)(2,1)} %fusion.12), channel_id=1, source_target_pairs={{4,8},{6,10},{8,4},{10,6},{5,9},{7,11},{9,5},{11,7},{20,24},{22,26... | collective-permute-start | bytes 1474568 | tf_op jit(solution)/shard_map/ppermute | solution.py:174
  49.0 15.0 %collective-permute-start.9 = (f16[2,96,1280]{2,1,0:T(8,128)(2,1)}, f16[2,96,1280]{2,1,0:T(8,128)(2,1)}, u32[]{:S(2)}, u32[]{:S(2)}) collective-permute-start(f16[2,96,1280]{2,1,0:T(8,128)(2,1)} %fusion.29), channel_id=1, source_target_pairs={{0,4},{2,6},{12,8},{14,10},{1,5},{3,7},{13,9},{15,11},{16,20},{18,... | collective-permute-start | bytes 1474568 | tf_op jit(solution)/shard_map/ppermute | solution.py:174
  55.6 8.4 %collective-permute-start.6 = (bf16[48,3584]{1,0:T(8,128)(2,1)}, bf16[48,3584]{1,0:T(8,128)(2,1)S(1)}, u32[]{:S(2)}, u32[]{:S(2)}) collective-permute-start(bf16[48,3584]{1,0:T(8,128)(2,1)} %get-tuple-element.194), channel_id=1, source_target_pairs={{0,1},{1,0},{2,3},{3,2},{4,5},{5,4},{6,7},{7,6},{8,9},{9,8},{10,11... | collective-permute-start | bytes 1032200 | tf_op jit(solution)/shard_map/ppermute | solution.py:308
  60.0 48.0 %copy-start = (f32[4,2,96,1280]{3,2,1,0:T(8,128)}, f32[4,2,96,1280]{3,2,1,0:T(8,128)S(1)}, u32[]{:S(2)}) copy-start(f32[4,2,96,1280]{3,2,1,0:T(8,128)S(1)} %shard_map.70) | copy-start | bytes 11796484
  64.0 6.7 %copy-start.21 = (f16[4,2,96,1280]{3,2,1,0:T(8,128)(2,1)}, f16[4,2,96,1280]{3,2,1,0:T(8,128)(2,1)S(1)}, u32[]{:S(2)}) copy-start(f16[4,2,96,1280]{3,2,1,0:T(8,128)(2,1)S(1)} %collective-permute-done.5) | copy-start | bytes 5898244
  66.4 13.8 %collective-permute-start.8 = (f16[2,96,1280]{2,1,0:T(8,128)(2,1)S(1)}, f16[2,96,1280]{2,1,0:T(8,128)(2,1)S(1)}, u32[]{:S(2)}, u32[]{:S(2)}) collective-permute-start(f16[2,96,1280]{2,1,0:T(8,128)(2,1)S(1)} %get-tuple-element.171), channel_id=1, source_target_pairs={{0,4},{2,6},{12,8},{14,10},{4,0},{6,2},{8,12},{10,14},{1,5},{3,7},... | collective-permute-start | bytes 1474568 | tf_op jit(solution)/shard_map/ppermute | solution.py:174
  67.6 12.5 %collective-permute-start.10 = (f16[2,96,1280]{2,1,0:T(8,128)(2,1)S(1)}, f16[2,96,1280]{2,1,0:T(8,128)(2,1)S(1)}, u32[]{:S(2)}, u32[]{:S(2)}) collective-permute-start(f16[2,96,1280]{2,1,0:T(8,128)(2,1)S(1)} %get-tuple-element.172), channel_id=1, source_target_pairs={{4,8},{6,10},{8,4},{10,6},{5,9},{7,11},{9,5},{11,7},{20,24},{22,26... | collective-permute-start | bytes 1474568 | tf_op jit(solution)/shard_map/ppermute | solution.py:174
  68.4 10.6 %collective-permute-start.12 = (bf16[2,48,1792]{2,1,0:T(8,128)(2,1)S(1)}, bf16[2,48,1792]{2,1,0:T(8,128)(2,1)S(1)}, u32[]{:S(2)}, u32[]{:S(2)}) collective-permute-start(bf16[2,48,1792]{2,1,0:T(8,128)(2,1)S(1)} %get-tuple-element.192), channel_id=1, source_target_pairs={{0,2},{2,0},{4,6},{6,4},{8,10},{10,8},{12,14},{14,12},{1,3},{3,1},... | collective-permute-start | bytes 1032200 | tf_op jit(solution)/shard_map/ppermute | solution.py:174
  71.7 20.2 %collective-permute-start.16 = (f16[2,96,1280]{2,1,0:T(8,128)(2,1)}, f16[2,96,1280]{2,1,0:T(8,128)(2,1)}, u32[]{:S(2)}, u32[]{:S(2)}) collective-permute-start(f16[2,96,1280]{2,1,0:T(8,128)(2,1)} %fusion.30), channel_id=1, source_target_pairs={{0,4},{2,6},{12,8},{14,10},{1,5},{3,7},{13,9},{15,11},{16,20},{18,... | collective-permute-start | bytes 1474568 | tf_op jit(solution)/shard_map/ppermute | solution.py:174
  78.4 6.7 %collective-permute-start.13 = (bf16[2,1024,512]{2,1,0:T(8,128)(2,1)S(1)}, bf16[2,1024,512]{2,1,0:T(8,128)(2,1)S(1)}, u32[]{:S(2)}, u32[]{:S(2)}) collective-permute-start(bf16[2,1024,512]{2,1,0:T(8,128)(2,1)S(1)} %pad_maximum_fusion), channel_id=1, source_target_pairs={{0,2},{2,0},{4,6},{6,4},{8,10},{10,8},{12,14},{14,12},{1,3},{3,1},... | collective-permute-start | bytes 6291464 | tf_op jit(solution)/shard_map/ppermute | solution.py:174
  79.0 5.9 %collective-permute-start.11 = (bf16[4,2,96,1024]{3,2,0,1:T(8,128)(2,1)S(1)}, bf16[4,2,96,1024]{3,2,0,1:T(8,128)(2,1)S(1)}, u32[]{:S(2)}, u32[]{:S(2)}) collective-permute-start(bf16[4,2,96,1024]{3,2,0,1:T(8,128)(2,1)S(1)} %pad_maximum_fusion.1), channel_id=1, source_target_pairs={{0,2},{2,0},{4,6},{6,4},{8,10},{10,8},{12,14},{14,12},{1,3},{3,1},... | collective-permute-start | bytes 4718600 | tf_op jit(solution)/shard_map/ppermute | solution.py:174
  81.9 3.3 %copy-start.6 = (bf16[2,96,1280]{2,1,0:T(8,128)(2,1)}, bf16[2,96,1280]{2,1,0:T(8,128)(2,1)S(1)}, u32[]{:S(2)}) copy-start(bf16[2,96,1280]{2,1,0:T(8,128)(2,1)S(1)} %pad_maximum_fusion.2.act) | copy-start | bytes 1474564
  81.9 15.7 %collective-permute-start.15 = (bf16[2,96,1280]{2,1,0:T(8,128)(2,1)S(1)}, bf16[2,96,1280]{2,1,0:T(8,128)(2,1)S(1)}, u32[]{:S(2)}, u32[]{:S(2)}) collective-permute-start(bf16[2,96,1280]{2,1,0:T(8,128)(2,1)S(1)} %pad_maximum_fusion.2.act), channel_id=1, source_target_pairs={{4,8},{6,10},{8,4},{10,6},{5,9},{7,11},{9,5},{11,7},{20,24},{22,26... | collective-permute-start | bytes 1474568 | tf_op jit(solution)/shard_map/ppermute | solution.py:174
  82.6 15.0 %collective-permute-start.14 = (bf16[2,96,1280]{2,1,0:T(8,128)(2,1)S(1)}, bf16[2,96,1280]{2,1,0:T(8,128)(2,1)S(1)}, u32[]{:S(2)}, u32[]{:S(2)}) collective-permute-start(bf16[2,96,1280]{2,1,0:T(8,128)(2,1)S(1)} %pad_maximum_fusion.2.act), channel_id=1, source_target_pairs={{0,4},{2,6},{12,8},{14,10},{4,0},{6,2},{8,12},{10,14},{1,5},{3,7},... | collective-permute-start | bytes 1474568 | tf_op jit(solution)/shard_map/ppermute | solution.py:174
  85.2 6.7 %copy-start.22 = (f16[4,2,96,1280]{3,2,1,0:T(8,128)(2,1)S(1)}, f16[4,2,96,1280]{3,2,1,0:T(8,128)(2,1)}, u32[]{:S(2)}) copy-start(f16[4,2,96,1280]{3,2,1,0:T(8,128)(2,1)} %copy-done.21) | copy-start | bytes 5898244
  93.1 6.6 %collective-permute-start.20 = (f16[2,96,1280]{2,1,0:T(8,128)(2,1)S(1)}, f16[2,96,1280]{2,1,0:T(8,128)(2,1)S(1)}, u32[]{:S(2)}, u32[]{:S(2)}) collective-permute-start(f16[2,96,1280]{2,1,0:T(8,128)(2,1)S(1)} %fusion.6), channel_id=1, source_target_pairs={{4,8},{6,10},{8,4},{10,6},{5,9},{7,11},{9,5},{11,7},{20,24},{22,26... | collective-permute-start | bytes 1474568 | tf_op jit(solution)/shard_map/ppermute | solution.py:174
  93.9 14.0 %collective-permute-start.19 = (f16[2,96,1280]{2,1,0:T(8,128)(2,1)S(1)}, f16[2,96,1280]{2,1,0:T(8,128)(2,1)S(1)}, u32[]{:S(2)}, u32[]{:S(2)}) collective-permute-start(f16[2,96,1280]{2,1,0:T(8,128)(2,1)S(1)} %fusion.31), channel_id=1, source_target_pairs={{0,4},{2,6},{12,8},{14,10},{1,5},{3,7},{13,9},{15,11},{16,20},{18,... | collective-permute-start | bytes 1474568 | tf_op jit(solution)/shard_map/ppermute | solution.py:174
  97.6 11.7 %copy-start.8 = (bf16[2,96,1280]{2,1,0:T(8,128)(2,1)}, bf16[2,96,1280]{2,1,0:T(8,128)(2,1)S(1)}, u32[]{:S(2)}) copy-start(bf16[2,96,1280]{2,1,0:T(8,128)(2,1)S(1)} %collective-permute-done.15.centre_1) | copy-start | bytes 1474564
  97.7 11.7 %copy-start.10 = (bf16[2,96,1280]{2,1,0:T(8,128)(2,1)}, bf16[2,96,1280]{2,1,0:T(8,128)(2,1)S(1)}, u32[]{:S(2)}) copy-start(bf16[2,96,1280]{2,1,0:T(8,128)(2,1)S(1)} %collective-permute-done.14.side_1) | copy-start | bytes 1474564
  97.7 15.3 %collective-permute-start.18 = (bf16[2,96,1280]{2,1,0:T(8,128)(2,1)S(1)}, bf16[2,96,1280]{2,1,0:T(8,128)(2,1)S(1)}, u32[]{:S(2)}, u32[]{:S(2)}) collective-permute-start(bf16[2,96,1280]{2,1,0:T(8,128)(2,1)S(1)} %collective-permute-done.14.side_1), channel_id=1, source_target_pairs={{4,8},{6,10},{8,4},{10,6},{5,9},{7,11},{9,5},{11,7},{20,24},{22,26... | collective-permute-start | bytes 1474568 | tf_op jit(solution)/shard_map/ppermute | solution.py:174
  98.4 14.6 %collective-permute-start.17 = (bf16[2,96,1280]{2,1,0:T(8,128)(2,1)S(1)}, bf16[2,96,1280]{2,1,0:T(8,128)(2,1)S(1)}, u32[]{:S(2)}, u32[]{:S(2)}) collective-permute-start(bf16[2,96,1280]{2,1,0:T(8,128)(2,1)S(1)} %collective-permute-done.15.centre_1), channel_id=1, source_target_pairs={{4,0},{6,2},{8,12},{10,14},{5,1},{7,3},{9,13},{11,15},{20,16},{22,... | collective-permute-start | bytes 1474568 | tf_op jit(solution)/shard_map/ppermute | solution.py:174
  109.4 14.4 %collective-permute-start.22 = (f16[2,96,1280]{2,1,0:T(8,128)(2,1)}, f16[2,96,1280]{2,1,0:T(8,128)(2,1)}, u32[]{:S(2)}, u32[]{:S(2)}) collective-permute-start(f16[2,96,1280]{2,1,0:T(8,128)(2,1)} %get-tuple-element.169), channel_id=1, source_target_pairs={{0,4},{2,6},{12,8},{14,10},{4,0},{6,2},{8,12},{10,14},{1,5},{3,7},... | collective-permute-start | bytes 1474568 | tf_op jit(solution)/shard_map/ppermute | solution.py:174
  111.6 12.2 %collective-permute-start.23 = (f16[2,96,1280]{2,1,0:T(8,128)(2,1)}, f16[2,96,1280]{2,1,0:T(8,128)(2,1)}, u32[]{:S(2)}, u32[]{:S(2)}) collective-permute-start(f16[2,96,1280]{2,1,0:T(8,128)(2,1)} %get-tuple-element.170), channel_id=1, source_target_pairs={{4,8},{6,10},{8,4},{10,6},{5,9},{7,11},{9,5},{11,7},{20,24},{22,26... | collective-permute-start | bytes 1474568 | tf_op jit(solution)/shard_map/ppermute | solution.py:174
  113.0 5.3 %copy-start.12 = (bf16[2,96,1280]{2,1,0:T(8,128)(2,1)}, bf16[2,96,1280]{2,1,0:T(8,128)(2,1)S(1)}, u32[]{:S(2)}) copy-start(bf16[2,96,1280]{2,1,0:T(8,128)(2,1)S(1)} %collective-permute-done.18.share_2) | copy-start | bytes 1474564
  113.0 5.3 %copy-start.14 = (bf16[2,96,1280]{2,1,0:T(8,128)(2,1)}, bf16[2,96,1280]{2,1,0:T(8,128)(2,1)S(1)}, u32[]{:S(2)}) copy-start(bf16[2,96,1280]{2,1,0:T(8,128)(2,1)S(1)} %collective-permute-done.17.out_2) | copy-start | bytes 1474564
  113.0 21.1 %collective-permute-start.21 = (bf16[2,96,1280]{2,1,0:T(8,128)(2,1)S(1)}, bf16[2,96,1280]{2,1,0:T(8,128)(2,1)S(1)}, u32[]{:S(2)}, u32[]{:S(2)}) collective-permute-start(bf16[2,96,1280]{2,1,0:T(8,128)(2,1)S(1)} %collective-permute-done.18.share_2), channel_id=1, source_target_pairs={{4,0},{6,2},{8,12},{10,14},{5,1},{7,3},{9,13},{11,15},{20,16},{22,... | collective-permute-start | bytes 1474568 | tf_op jit(solution)/shard_map/ppermute | solution.py:174
  116.6 7.1 %copy-start.1 = (f32[4,2,96,1280]{3,2,1,0:T(8,128)S(1)}, f32[4,2,96,1280]{3,2,1,0:T(8,128)}, u32[]{:S(2)}) copy-start(f32[4,2,96,1280]{3,2,1,0:T(8,128)} %copy-done) | copy-start | bytes 11796484
  119.5 6.2 %copy-start.23 = (bf16[96,1792]{1,0:T(8,128)(2,1)S(1)}, bf16[96,1792]{1,0:T(8,128)(2,1)}, u32[]{:S(2)}) copy-start(bf16[96,1792]{1,0:T(8,128)(2,1)} %get-tuple-element.189) | copy-start | bytes 1032196
  119.5 16.8 %collective-permute-start.26 = (f16[2,192,512]{2,1,0:T(8,128)(2,1)S(1)}, f16[2,192,512]{2,1,0:T(8,128)(2,1)S(1)}, u32[]{:S(2)}, u32[]{:S(2)}) collective-permute-start(f16[2,192,512]{2,1,0:T(8,128)(2,1)S(1)} %fusion.38), channel_id=1, source_target_pairs={{0,4},{2,6},{12,8},{14,10},{1,5},{3,7},{13,9},{15,11},{16,20},{18,... | collective-permute-start | bytes 1179656 | tf_op jit(solution)/shard_map/ppermute | solution.py:174
  125.7 9.2 %copy-start.7 = (bf16[2,96,1280]{2,1,0:T(8,128)(2,1)S(1)}, bf16[2,96,1280]{2,1,0:T(8,128)(2,1)}, u32[]{:S(2)}) copy-start(bf16[2,96,1280]{2,1,0:T(8,128)(2,1)} %copy-done.6) | copy-start | bytes 1474564
  125.7 9.2 %copy-start.9 = (bf16[2,96,1280]{2,1,0:T(8,128)(2,1)S(1)}, bf16[2,96,1280]{2,1,0:T(8,128)(2,1)}, u32[]{:S(2)}) copy-start(bf16[2,96,1280]{2,1,0:T(8,128)(2,1)} %copy-done.8) | copy-start | bytes 1474564
  125.7 9.2 %copy-start.11 = (bf16[2,96,1280]{2,1,0:T(8,128)(2,1)S(1)}, bf16[2,96,1280]{2,1,0:T(8,128)(2,1)}, u32[]{:S(2)}) copy-start(bf16[2,96,1280]{2,1,0:T(8,128)(2,1)} %copy-done.10) | copy-start | bytes 1474564
  125.7 9.2 %copy-start.13 = (bf16[2,96,1280]{2,1,0:T(8,128)(2,1)S(1)}, bf16[2,96,1280]{2,1,0:T(8,128)(2,1)}, u32[]{:S(2)}) copy-start(bf16[2,96,1280]{2,1,0:T(8,128)(2,1)} %copy-done.12) | copy-start | bytes 1474564
  125.7 9.2 %copy-start.15 = (bf16[2,96,1280]{2,1,0:T(8,128)(2,1)S(1)}, bf16[2,96,1280]{2,1,0:T(8,128)(2,1)}, u32[]{:S(2)}) copy-start(bf16[2,96,1280]{2,1,0:T(8,128)(2,1)} %copy-done.14) | copy-start | bytes 1474564
  126.8 9.5 %copy-start.4 = (bf16[2,96,1280]{2,1,0:T(8,128)(2,1)}, bf16[2,96,1280]{2,1,0:T(8,128)(2,1)S(1)}, u32[]{:S(2)}) copy-start(bf16[2,96,1280]{2,1,0:T(8,128)(2,1)S(1)} %pad_maximum_fusion.3.act) | copy-start | bytes 1474564
  126.8 14.6 %collective-permute-start.25 = (bf16[2,96,1280]{2,1,0:T(8,128)(2,1)S(1)}, bf16[2,96,1280]{2,1,0:T(8,128)(2,1)}, u32[]{:S(2)}, u32[]{:S(2)}) collective-permute-start(bf16[2,96,1280]{2,1,0:T(8,128)(2,1)S(1)} %pad_maximum_fusion.3.act), channel_id=1, source_target_pairs={{4,8},{6,10},{8,4},{10,6},{5,9},{7,11},{9,5},{11,7},{20,24},{22,26... | collective-permute-start | bytes 1474568 | tf_op jit(solution)/shard_map/ppermute | solution.py:174
  128.2 16.5 %collective-permute-start.24 = (bf16[2,96,1280]{2,1,0:T(8,128)(2,1)S(1)}, bf16[2,96,1280]{2,1,0:T(8,128)(2,1)}, u32[]{:S(2)}, u32[]{:S(2)}) collective-permute-start(bf16[2,96,1280]{2,1,0:T(8,128)(2,1)S(1)} %pad_maximum_fusion.3.act), channel_id=1, source_target_pairs={{0,4},{2,6},{12,8},{14,10},{4,0},{6,2},{8,12},{10,14},{1,5},{3,7},... | collective-permute-start | bytes 1474568 | tf_op jit(solution)/shard_map/ppermute | solution.py:174
  138.1 9.5 %collective-permute-start.30 = (f16[2,192,512]{2,1,0:T(8,128)(2,1)S(1)}, f16[2,192,512]{2,1,0:T(8,128)(2,1)S(1)}, u32[]{:S(2)}, u32[]{:S(2)}) collective-permute-start(f16[2,192,512]{2,1,0:T(8,128)(2,1)S(1)} %fusion.18), channel_id=1, source_target_pairs={{4,8},{6,10},{8,4},{10,6},{5,9},{7,11},{9,5},{11,7},{20,24},{22,26... | collective-permute-start | bytes 1179656 | tf_op jit(solution)/shard_map/ppermute | solution.py:174
  138.8 13.1 %collective-permute-start.29 = (f16[2,192,512]{2,1,0:T(8,128)(2,1)S(1)}, f16[2,192,512]{2,1,0:T(8,128)(2,1)S(1)}, u32[]{:S(2)}, u32[]{:S(2)}) collective-permute-start(f16[2,192,512]{2,1,0:T(8,128)(2,1)S(1)} %fusion.39), channel_id=1, source_target_pairs={{0,4},{2,6},{12,8},{14,10},{1,5},{3,7},{13,9},{15,11},{16,20},{18,... | collective-permute-start | bytes 1179656 | tf_op jit(solution)/shard_map/ppermute | solution.py:174
  144.8 12.9 %collective-permute-start.28 = (bf16[2,96,1280]{2,1,0:T(8,128)(2,1)}, bf16[2,96,1280]{2,1,0:T(8,128)(2,1)}, u32[]{:S(2)}, u32[]{:S(2)}) collective-permute-start(bf16[2,96,1280]{2,1,0:T(8,128)(2,1)} %collective-permute-done.24.side_1), channel_id=1, source_target_pairs={{4,8},{6,10},{8,4},{10,6},{5,9},{7,11},{9,5},{11,7},{20,24},{22,26... | collective-permute-start | bytes 1474568 | tf_op jit(solution)/shard_map/ppermute | solution.py:174
  146.2 11.5 %collective-permute-start.27 = (bf16[2,96,1280]{2,1,0:T(8,128)(2,1)}, bf16[2,96,1280]{2,1,0:T(8,128)(2,1)}, u32[]{:S(2)}, u32[]{:S(2)}) collective-permute-start(bf16[2,96,1280]{2,1,0:T(8,128)(2,1)} %collective-permute-done.25.centre_1), channel_id=1, source_target_pairs={{4,0},{6,2},{8,12},{10,14},{5,1},{7,3},{9,13},{11,15},{20,16},{22,... | collective-permute-start | bytes 1474568 | tf_op jit(solution)/shard_map/ppermute | solution.py:174
  153.1 12.8 %collective-permute-start.31 = (f16[2,192,512]{2,1,0:T(8,128)(2,1)}, f16[2,192,512]{2,1,0:T(8,128)(2,1)}, u32[]{:S(2)}, u32[]{:S(2)}) collective-permute-start(f16[2,192,512]{2,1,0:T(8,128)(2,1)} %get-tuple-element.173), channel_id=1, source_target_pairs={{0,4},{2,6},{12,8},{14,10},{4,0},{6,2},{8,12},{10,14},{1,5},{3,7},... | collective-permute-start | bytes 1179656 | tf_op jit(solution)/shard_map/ppermute | solution.py:174
  155.3 10.6 %collective-permute-start.32 = (f16[2,192,512]{2,1,0:T(8,128)(2,1)}, f16[2,192,512]{2,1,0:T(8,128)(2,1)}, u32[]{:S(2)}, u32[]{:S(2)}) collective-permute-start(f16[2,192,512]{2,1,0:T(8,128)(2,1)} %get-tuple-element.174), channel_id=1, source_target_pairs={{4,8},{6,10},{8,4},{10,6},{5,9},{7,11},{9,5},{11,7},{20,24},{22,26... | collective-permute-start | bytes 1179656 | tf_op jit(solution)/shard_map/ppermute | solution.py:174
  157.7 25.2 %collective-permute-start.36 = (bf16[2,96,1280]{2,1,0:T(8,128)(2,1)}, bf16[2,96,1280]{2,1,0:T(8,128)(2,1)S(1)}, u32[]{:S(2)}, u32[]{:S(2)}) collective-permute-start(bf16[2,96,1280]{2,1,0:T(8,128)(2,1)} %collective-permute-done.28.share_2), channel_id=1, source_target_pairs={{4,0},{6,2},{8,12},{10,14},{5,1},{7,3},{9,13},{11,15},{20,16},{22,... | collective-permute-start | bytes 1474568 | tf_op jit(solution)/shard_map/ppermute | solution.py:174
  168.2 14.8 %copy-start.5 = (bf16[2,96,1280]{2,1,0:T(8,128)(2,1)S(1)}, bf16[2,96,1280]{2,1,0:T(8,128)(2,1)}, u32[]{:S(2)}) copy-start(bf16[2,96,1280]{2,1,0:T(8,128)(2,1)} %copy-done.4) | copy-start | bytes 1474564
  169.7 13.2 %collective-permute-start.33 = (bf16[2,48,1792]{2,1,0:T(8,128)(2,1)S(1)}, bf16[2,48,1792]{2,1,0:T(8,128)(2,1)}, u32[]{:S(2)}, u32[]{:S(2)}) collective-permute-start(bf16[2,48,1792]{2,1,0:T(8,128)(2,1)S(1)} %get-tuple-element.187), channel_id=1, source_target_pairs={{0,2},{2,0},{4,6},{6,4},{8,10},{10,8},{12,14},{14,12},{1,3},{3,1},... | collective-permute-start | bytes 1032200 | tf_op jit(solution)/shard_map/ppermute | solution.py:174
  180.4 5.2 %collective-permute-start.35 = (bf16[2,192,512]{2,1,0:T(8,128)(2,1)}, bf16[2,192,512]{2,1,0:T(8,128)(2,1)}, u32[]{:S(2)}, u32[]{:S(2)}) collective-permute-start(bf16[2,192,512]{2,1,0:T(8,128)(2,1)} %pad_maximum_fusion.4.act), channel_id=1, source_target_pairs={{4,8},{6,10},{8,4},{10,6},{5,9},{7,11},{9,5},{11,7},{20,24},{22,26... | collective-permute-start | bytes 1179656 | tf_op jit(solution)/shard_map/ppermute | solution.py:174
  181.8 11.1 %collective-permute-start.34 = (bf16[2,192,512]{2,1,0:T(8,128)(2,1)}, bf16[2,192,512]{2,1,0:T(8,128)(2,1)}, u32[]{:S(2)}, u32[]{:S(2)}) collective-permute-start(bf16[2,192,512]{2,1,0:T(8,128)(2,1)} %pad_maximum_fusion.4.act), channel_id=1, source_target_pairs={{0,4},{2,6},{12,8},{14,10},{4,0},{6,2},{8,12},{10,14},{1,5},{3,7},... | collective-permute-start | bytes 1179656 | tf_op jit(solution)/shard_map/ppermute | solution.py:174
  182.4 26.2 %collective-permute-start.41 = (bf16[4,2,96,1280]{3,2,1,0:T(8,128)(2,1)S(1)}, bf16[4,2,96,1280]{3,2,1,0:T(8,128)(2,1)}, u32[]{:S(2)}, u32[]{:S(2)}) collective-permute-start(bf16[4,2,96,1280]{3,2,1,0:T(8,128)(2,1)S(1)} %shard_map.72), channel_id=1, source_target_pairs={{0,2},{2,0},{4,6},{6,4},{8,10},{10,8},{12,14},{14,12},{1,3},{3,1},... | collective-permute-start | bytes 5898248 | tf_op jit(solution)/shard_map/ppermute | solution.py:174
  185.6 22.9 %collective-permute-start.42 = (bf16[4,2,96,1280]{3,2,1,0:T(8,128)(2,1)}, bf16[4,2,96,1280]{3,2,1,0:T(8,128)(2,1)}, u32[]{:S(2)}, u32[]{:S(2)}) collective-permute-start(bf16[4,2,96,1280]{3,2,1,0:T(8,128)(2,1)} %shard_map.73), channel_id=1, source_target_pairs={{0,2},{2,0},{4,6},{6,4},{8,10},{10,8},{12,14},{14,12},{1,3},{3,1},... | collective-permute-start | bytes 5898248 | tf_op jit(solution)/shard_map/ppermute | solution.py:174
  192.9 13.6 %collective-permute-start.39 = (bf16[2,192,512]{2,1,0:T(8,128)(2,1)}, bf16[2,192,512]{2,1,0:T(8,128)(2,1)}, u32[]{:S(2)}, u32[]{:S(2)}) collective-permute-start(bf16[2,192,512]{2,1,0:T(8,128)(2,1)} %collective-permute-done.34.side_1), channel_id=1, source_target_pairs={{4,8},{6,10},{8,4},{10,6},{5,9},{7,11},{9,5},{11,7},{20,24},{22,26... | collective-permute-start | bytes 1179656 | tf_op jit(solution)/shard_map/ppermute | solution.py:174
  194.4 12.1 %collective-permute-start.38 = (bf16[2,192,512]{2,1,0:T(8,128)(2,1)}, bf16[2,192,512]{2,1,0:T(8,128)(2,1)S(1)}, u32[]{:S(2)}, u32[]{:S(2)}) collective-permute-start(bf16[2,192,512]{2,1,0:T(8,128)(2,1)} %collective-permute-done.35.centre_1), channel_id=1, source_target_pairs={{4,0},{6,2},{8,12},{10,14},{5,1},{7,3},{9,13},{11,15},{20,16},{22,... | collective-permute-start | bytes 1179656 | tf_op jit(solution)/shard_map/ppermute | solution.py:174
  198.2 10.3 %collective-permute-start.37 = (bf16[48,3584]{1,0:T(8,128)(2,1)}, bf16[48,3584]{1,0:T(8,128)(2,1)}, u32[]{:S(2)}, u32[]{:S(2)}) collective-permute-start(bf16[48,3584]{1,0:T(8,128)(2,1)} %get-tuple-element.186), channel_id=1, source_target_pairs={{0,1},{1,0},{2,3},{3,2},{4,5},{5,4},{6,7},{7,6},{8,9},{9,8},{10,11... | collective-permute-start | bytes 1032200 | tf_op jit(solution)/shard_map/ppermute | solution.py:316
  207.3 11.3 %collective-permute-start.40 = (bf16[2,192,512]{2,1,0:T(8,128)(2,1)}, bf16[2,192,512]{2,1,0:T(8,128)(2,1)}, u32[]{:S(2)}, u32[]{:S(2)}) collective-permute-start(bf16[2,192,512]{2,1,0:T(8,128)(2,1)} %collective-permute-done.39.share_2), channel_id=1, source_target_pairs={{4,0},{6,2},{8,12},{10,14},{5,1},{7,3},{9,13},{11,15},{20,16},{22,... | collective-permute-start | bytes 1179656 | tf_op jit(solution)/shard_map/ppermute | solution.py:174
  208.6 10.0 %copy-start.19 = (bf16[2,192,512]{2,1,0:T(8,128)(2,1)S(1)}, bf16[2,192,512]{2,1,0:T(8,128)(2,1)}, u32[]{:S(2)}) copy-start(bf16[2,192,512]{2,1,0:T(8,128)(2,1)} %copy-done.18) | copy-start | bytes 1179652
  218.6 4.3 %copy-start.25 = (bf16[1,48,3584]{2,1,0:T(8,128)(2,1)S(1)}, bf16[1,48,3584]{2,1,0:T(8,128)(2,1)}, u32[]{:S(2)}) copy-start(bf16[1,48,3584]{2,1,0:T(8,128)(2,1)} %get-tuple-element.185) | copy-start | bytes 1032196
  220.4 8.0 %collective-permute-start.43 = (bf16[4,2,192,512]{3,2,1,0:T(8,128)(2,1)S(1)}, bf16[4,2,192,512]{3,2,1,0:T(8,128)(2,1)}, u32[]{:S(2)}, u32[]{:S(2)}) collective-permute-start(bf16[4,2,192,512]{3,2,1,0:T(8,128)(2,1)S(1)} %shard_map.76), channel_id=1, source_target_pairs={{0,2},{2,0},{4,6},{6,4},{8,10},{10,8},{12,14},{14,12},{1,3},{3,1},... | collective-permute-start | bytes 4718600 | tf_op jit(solution)/shard_map/ppermute | solution.py:174
  (9 other events, 11.3 us)

commit v15 on v14

--- a/solution.py
+++ b/solution.py
@@ -20,6 +20,7 @@
     tokens, weights = refs[:cores], refs[cores : cores + 2 * cores]
     out_ref, held, arrived = refs[3 * cores :]
     tiles, _, tile = held.shape[1:]
+    tile //= 2
     blocks, _, rows, _ = out_ref.shape
 
     def copy(j, which):
@@ -29,7 +30,9 @@
             source = weights[which].at[:, columns]
         else:
             source = weights[which].at[which - 2, :, pl.ds(j * tile, tile)]
-        return pltpu.make_async_copy(source, held.at[which, j], arrived.at[which, j])
+        place = pl.ds(which % 2 * tile, tile)
+        held_here = held.at[which // 2, j, :, place]
+        return pltpu.make_async_copy(source, held_here, arrived.at[which, j])
 
     for j in range(tiles):
         for which in range(2 * cores):
@@ -37,15 +40,13 @@
     for j in range(tiles):
         for which in range(2 * cores):
             copy(j, which).wait()
+        product = scale * sum(
+            jnp.dot(tokens[i][...], held[i, j], preferred_element_type=jnp.float32)
+            for i in range(cores)
+        )
         for which in range(2):
-            product = sum(
-                jnp.dot(
-                    tokens[i][...], held[which + 2 * i, j], preferred_element_type=jnp.float32
-                )
-                for i in range(cores)
-            )
-            product = (scale * product).reshape(blocks, rows, tile)
-            out_ref[:, which, :, j * tile : (j + 1) * tile] = product
+            half = product[:, which * tile : (which + 1) * tile].reshape(blocks, rows, tile)
+            out_ref[:, which, :, j * tile : (j + 1) * tile] = half
 
 
 def forward(place, tokens, weights, start, width, tile, blocks, scale, cost=NO_COST):
@@ -60,7 +61,7 @@
         + [pl.BlockSpec(memory_space=pl.ANY)] * (2 * cores),
         out_specs=pl.BlockSpec(memory_space=pltpu.VMEM),
         scratch_shapes=[
-            pltpu.VMEM((2 * cores, width // tile, depth, tile), jnp.bfloat16),
+            pltpu.VMEM((cores, width // tile, depth, 2 * tile), jnp.bfloat16),
             pltpu.SemaphoreType.DMA((2 * cores, width // tile)),
         ],
         compiler_params=pltpu.CompilerParams(vmem_limit_bytes=VMEM_LIMIT),
@@ -70,7 +71,8 @@
 
 def gradient_kernel(batches, place_ref, features_ref, *refs):
     acts, outs = refs[:batches], refs[-2:]
-    for which, out_ref in enumerate(outs):
+    halves = []
+    for which in range(2):
         parts = []
         for act_ref in acts:
             blocks, _, _, rows, width = act_ref.shape
@@ -78,9 +80,12 @@
             for i in range(2 // batches):
                 part = act_ref[:, 0, which, i * rows : (i + 1) * rows]
                 parts.append(part.reshape(blocks * rows, width))
-        out_ref[...] = jnp.dot(
-            features_ref[...], jnp.concatenate(parts), preferred_element_type=jnp.float32
-        )
+        halves.append(jnp.concatenate(parts))
+    both = jnp.dot(
+        features_ref[...], jnp.concatenate(halves, axis=1), preferred_element_type=jnp.float32
+    )
+    for which, out_ref in enumerate(outs):
+        out_ref[...] = both[:, which * width : (which + 1) * width]
 
 
 def gradient(place, features, acts, totals, columns, start, tile):
@@ -355,7 +360,7 @@
             act, terms = ready, products.get(k + 2)
         else:
             totals = add_gradients(other_acts, 1 - core, totals, pieces[0][1])
-            out_3 = tie(out_3, totals)
+            out_3, hidden = lax.optimization_barrier((tie(out_3, totals), hidden))
             own_acts, other_acts = merge(act, side_1, centre_1, out_2, share_2, out_3)
     totals = add_gradients([own_acts], core, totals, pieces[last][1])
     totals = add_gradients([other_acts], 1 - core, totals, pieces[last][1])

time: 234 us -> 224 us (0.957)
  Pallas kernels: 53.1 us -> 48 us
  waiting for transfers between devices: 50.7 us -> 45.9 us
  starting transfers between devices: 80.9 us -> 83.6 us
    ppermute x39, waiting for transfers between devices: 33.9 us -> 29.1 us  [send(): return lax.ppermute(value, 'col', route)]
    pallas_call x4, Pallas kernels: 24.9 us -> 20.9 us  [gradient(): pl.pallas_call(functools.partial(gradient_kernel, len(acts)), out_shape=(...]
    ppermute x39, starting transfers between devices: 76.9 us -> 79.5 us  [send(): return lax.ppermute(value, 'col', route)]
    unnamed x58 -> x54, local copies, waits for them, and re-layouts: 7.99 us -> 7.61 us
  transfers between devices with their start and end apart: 44 -> 44, of which waited for: 12 -> 14; matrix products, arithmetic and copies ran while one was open for 14% -> 14% of each run, Pallas kernels for 18% -> 17%
where the time goes in v15:
time: 224 us; the launch traced here: 223 us
  starting transfers between devices  83.6 us (37%)
  Pallas kernels  48 us (21%)
  waiting for transfers between devices  45.9 us (20%)
  other arithmetic  29 us (13%)
  local copies, waits for them, and re-layouts  15.4 us (7%)
    ppermute x39, starting transfers between devices, send(): return lax.ppermute(value, 'col', route)  79.5 us
    ppermute x39, waiting for transfers between devices, send(): return lax.ppermute(value, 'col', route)  29.1 us
    pallas_call x5, Pallas kernels, forward(): pl.pallas_call(functools.partial(forward_kernel, scale, start, cores), ou...  23.3 us
    pallas_call x4, Pallas kernels, gradient(): pl.pallas_call(functools.partial(gradient_kernel, len(acts)), out_shape=(...  20.9 us
    ppermute x1, waiting for transfers between devices, local(): over_depth = lax.ppermute(mine, 'depth', swap)  7.84 us
    unnamed x54, local copies, waits for them, and re-layouts  7.61 us
    select_n x5, other arithmetic, by(): jnp.where(first, jnp.concatenate([mine, theirs], axis=axis), jnp.concaten...  5.04 us
    convert_element_type x3, other arithmetic, local(): swapped = swapped.astype(WIRE)  4.97 us
  transfers between devices with their start and end apart: 44, of which 14 were waited for; matrix products, arithmetic and copies ran while one was open for 14% of the time, Pallas kernels for 17%

profile of v15, /device:TPU:1, one launch (start us, length us, event | category | flops | bytes accessed | tf_op | source)
XLA Modules:
  0.0 223.2 jit_solution(15144090095103308265)
XLA Ops:
  0.6 2.1 collective-permute-start.1
  2.8 1.2 collective-permute-start
  4.0 7.8 %collective-permute-done.1 = bf16[384,512]{1,0:T(8,128)(2,1)S(1)} collective-permute-done((bf16[384,512]{1,0:T(8,128)(2,1)}, bf16[384,512]{1,0:T(8,128)(2,1)S(1)}, u32[]{:S(2)}, u32[]{:S(2)}) %collective-permute-start.1) | collective-permute-done | bytes 393248 | tf_op jit(solution)/shard_map/ppermute | solution.py:213
  12.6 1.3 maximum_select_fusion
  14.2 4.2 %shard_map.67 = f32[4,2,96,1280]{3,2,1,0:T(8,128)S(1)} custom-call(s32[1]{0:T(128)} %bitcast.6.place_ref, bf16[384,1024]{1,0:T(8,128)(2,1)S(1)} %bitcast.154, bf16[1024,7168]{1,0:T(8,128)(2,1)} %refs_2_.9, bf16[1024,7168]{1,0:T(8,128)(2,1)} %refs_3_.1), custom_call_target="tpu_custom_call" | custom-call | tf_op jit(solution)/shard_map/pallas_call | solution.py:56
  18.4 1.5 convert_element_type.194
  19.9 1.9 collective-permute-start.2
  21.7 4.2 %shard_map.68 = f32[4,2,96,1280]{3,2,1,0:T(8,128)S(1)} custom-call(s32[1]{0:T(128)} %bitcast.1.place_ref, bf16[384,1024]{1,0:T(8,128)(2,1)S(1)} %bitcast.155, bf16[1024,7168]{1,0:T(8,128)(2,1)} %refs_2_.9, bf16[1024,7168]{1,0:T(8,128)(2,1)} %refs_3_.1), custom_call_target="tpu_custom_call" | custom-call | tf_op jit(solution)/shard_map/pallas_call | solution.py:56
  26.1 1.8 copy-done.2
  28.7 4.0 %collective-permute-start.4 = (f16[2,96,1280]{2,1,0:T(8,128)(2,1)}, f16[2,96,1280]{2,1,0:T(8,128)(2,1)}, u32[]{:S(2)}, u32[]{:S(2)}) collective-permute-start(f16[2,96,1280]{2,1,0:T(8,128)(2,1)} %fusion.33), channel_id=1, source_target_pairs={{0,4},{2,6},{12,8},{14,10},{1,5},{3,7},{13,9},{15,11},{16,20},{18,... | collective-permute-start | bytes 1474568 | tf_op jit(solution)/shard_map/ppermute | solution.py:179
  32.7 4.1 %collective-permute-done.3 = bf16[384,512]{1,0:T(8,128)(2,1)} collective-permute-done((bf16[384,512]{1,0:T(8,128)(2,1)S(1)}, bf16[384,512]{1,0:T(8,128)(2,1)}, u32[]{:S(2)}, u32[]{:S(2)}) %collective-permute-start.3) | collective-permute-done | bytes 393248 | tf_op jit(solution)/shard_map/ppermute | solution.py:214
  36.8 1.3 maximum_select_fusion.1
  38.4 4.2 %shard_map.69 = f32[4,2,96,1280]{3,2,1,0:T(8,128)S(1)} custom-call(s32[1]{0:T(128)} %bitcast.6.place_ref, bf16[384,1024]{1,0:T(8,128)(2,1)S(1)} %bitcast.158, bf16[1024,7168]{1,0:T(8,128)(2,1)} %refs_2_.9, bf16[1024,7168]{1,0:T(8,128)(2,1)} %refs_3_.1), custom_call_target="tpu_custom_call" | custom-call | tf_op jit(solution)/shard_map/pallas_call | solution.py:56
  44.7 2.0 fusion.13
  46.7 1.5 collective-permute-start.8
  49.0 5.7 %collective-permute-start.7 = (f16[2,96,1280]{2,1,0:T(8,128)(2,1)}, f16[2,96,1280]{2,1,0:T(8,128)(2,1)}, u32[]{:S(2)}, u32[]{:S(2)}) collective-permute-start(f16[2,96,1280]{2,1,0:T(8,128)(2,1)} %fusion.30), channel_id=1, source_target_pairs={{0,4},{2,6},{12,8},{14,10},{1,5},{3,7},{13,9},{15,11},{16,20},{18,... | collective-permute-start | bytes 1474568 | tf_op jit(solution)/shard_map/ppermute | solution.py:179
  55.8 4.2 %shard_map.70 = f32[4,2,96,1280]{3,2,1,0:T(8,128)S(1)} custom-call(s32[1]{0:T(128)} %bitcast.1.place_ref, bf16[384,1024]{1,0:T(8,128)(2,1)S(1)} %bitcast.159, bf16[1024,7168]{1,0:T(8,128)(2,1)} %refs_2_.9, bf16[1024,7168]{1,0:T(8,128)(2,1)} %refs_3_.1), custom_call_target="tpu_custom_call" | custom-call | flops 6000000000 | tf_op jit(solution)/shard_map/pallas_call | solution.py:56
  59.9 4.0 %collective-permute-done.5 = bf16[48,3584]{1,0:T(8,128)(2,1)S(1)} collective-permute-done((bf16[48,3584]{1,0:T(8,128)(2,1)}, bf16[48,3584]{1,0:T(8,128)(2,1)S(1)}, u32[]{:S(2)}, u32[]{:S(2)}) %collective-permute-start.5) | collective-permute-done | bytes 344096 | tf_op jit(solution)/shard_map/ppermute | solution.py:313
  64.0 2.3 %fusion.8 = (f16[2,96,1280]{2,1,0:T(8,128)(2,1)S(1)}, f16[2,96,1280]{2,1,0:T(8,128)(2,1)S(1)}) fusion(f16[2,96,1280]{2,1,0:T(8,128)(2,1)} %collective-permute-done.8, f32[4,2,96,1280]{3,2,1,0:T(8,128)S(1)} %copy-done.3, pred[]{:T(512)S(6)} %or.3, f16[4,2,96,1280]{3,2,1,0:T(8,128)(2,1)S(1)} %collective-permute-done.2, ...), kind=kLoop, calls=%fused_computation.22 | loop fusion | flops 3194880 | bytes 6389761 | tf_op jit(solution)/shard_map/convert_element_type | solution.py:329
  66.3 1.3 collective-permute-start.11
  68.4 2.3 %collective-permute-start.9 = (bf16[2,48,1792]{2,1,0:T(8,128)(2,1)S(1)}, bf16[2,48,1792]{2,1,0:T(8,128)(2,1)S(1)}, u32[]{:S(2)}, u32[]{:S(2)}) collective-permute-start(bf16[2,48,1792]{2,1,0:T(8,128)(2,1)S(1)} %get-tuple-element.196), channel_id=1, source_target_pairs={{0,2},{2,0},{4,6},{6,4},{8,10},{10,8},{12,14},{14,12},{1,3},{3,1},... | collective-permute-start | bytes 1032200 | tf_op jit(solution)/shard_map/ppermute | solution.py:179
  71.6 4.9 %collective-permute-start.16 = (f16[2,96,1280]{2,1,0:T(8,128)(2,1)}, f16[2,96,1280]{2,1,0:T(8,128)(2,1)}, u32[]{:S(2)}, u32[]{:S(2)}) collective-permute-start(f16[2,96,1280]{2,1,0:T(8,128)(2,1)} %fusion.31), channel_id=1, source_target_pairs={{0,4},{2,6},{12,8},{14,10},{1,5},{3,7},{13,9},{15,11},{16,20},{18,... | collective-permute-start | bytes 1474568 | tf_op jit(solution)/shard_map/ppermute | solution.py:179
  76.5 1.7 dynamic-slice_bitcast_fusion
  85.2 6.7 %shard_map.71 = f32[4,2,192,512]{3,2,1,0:T(8,128)} custom-call(s32[1]{0:T(128)} %bitcast.1.place_ref, bf16[768,1024]{1,0:T(8,128)(2,1)S(1)} %bitcast.163, bf16[768,1024]{1,0:T(8,128)(2,1)S(1)} %bitcast.164, bf16[1024,7168]{1,0:T(8,128)(2,1)} %refs_2_.9, bf16[1024,7168]{1,0:T(8,128)(2,1)} %refs_3_.1, ...), custom_call_target="tpu_custom_call" | custom-call | tf_op jit(solution)/shard_map/pallas_call | solution.py:56
  93.9 3.9 %collective-permute-start.19 = (f16[2,96,1280]{2,1,0:T(8,128)(2,1)S(1)}, f16[2,96,1280]{2,1,0:T(8,128)(2,1)S(1)}, u32[]{:S(2)}, u32[]{:S(2)}) collective-permute-start(f16[2,96,1280]{2,1,0:T(8,128)(2,1)S(1)} %fusion.32), channel_id=1, source_target_pairs={{0,4},{2,6},{12,8},{14,10},{1,5},{3,7},{13,9},{15,11},{16,20},{18,... | collective-permute-start | bytes 1474568 | tf_op jit(solution)/shard_map/ppermute | solution.py:179
  98.6 1.3 collective-permute-start.17
  99.9 7.9 %collective-permute-done.19 = f16[2,96,1280]{2,1,0:T(8,128)(2,1)S(1)} collective-permute-done((f16[2,96,1280]{2,1,0:T(8,128)(2,1)S(1)}, f16[2,96,1280]{2,1,0:T(8,128)(2,1)S(1)}, u32[]{:S(2)}, u32[]{:S(2)}) %collective-permute-start.19) | collective-permute-done | bytes 491552 | tf_op jit(solution)/shard_map/ppermute | solution.py:179
  107.8 1.4 fusion.4
  109.2 2.2 collective-permute-start.22
  111.4 1.4 collective-permute-start.23
  113.0 1.3 collective-permute-start.21
  116.7 1.6 maximum_bitcast_fusion.features_ref
  119.5 4.2 %collective-permute-start.26 = (f16[2,192,512]{2,1,0:T(8,128)(2,1)S(1)}, f16[2,192,512]{2,1,0:T(8,128)(2,1)S(1)}, u32[]{:S(2)}, u32[]{:S(2)}) collective-permute-start(f16[2,192,512]{2,1,0:T(8,128)(2,1)S(1)} %fusion.39), channel_id=1, source_target_pairs={{0,4},{2,6},{12,8},{14,10},{1,5},{3,7},{13,9},{15,11},{16,20},{18,... | collective-permute-start | bytes 1179656 | tf_op jit(solution)/shard_map/ppermute | solution.py:179
  123.7 1.9 fusion.2
  126.8 1.5 collective-permute-start.25
  128.3 3.9 %collective-permute-start.24 = (bf16[2,96,1280]{2,1,0:T(8,128)(2,1)S(1)}, bf16[2,96,1280]{2,1,0:T(8,128)(2,1)}, u32[]{:S(2)}, u32[]{:S(2)}) collective-permute-start(bf16[2,96,1280]{2,1,0:T(8,128)(2,1)S(1)} %pad_maximum_fusion.3.act), channel_id=1, source_target_pairs={{0,4},{2,6},{12,8},{14,10},{4,0},{6,2},{8,12},{10,14},{1,5},{3,7},... | collective-permute-start | bytes 1474568 | tf_op jit(solution)/shard_map/ppermute | solution.py:179
  132.1 1.9 collective-permute-done.21.out_3
  136.2 1.6 copy-done.18
  138.7 2.5 %collective-permute-start.29 = (f16[2,192,512]{2,1,0:T(8,128)(2,1)S(1)}, f16[2,192,512]{2,1,0:T(8,128)(2,1)S(1)}, u32[]{:S(2)}, u32[]{:S(2)}) collective-permute-start(f16[2,192,512]{2,1,0:T(8,128)(2,1)S(1)} %fusion.40), channel_id=1, source_target_pairs={{0,4},{2,6},{12,8},{14,10},{1,5},{3,7},{13,9},{15,11},{16,20},{18,... | collective-permute-start | bytes 1179656 | tf_op jit(solution)/shard_map/ppermute | solution.py:179
  141.2 3.5 %collective-permute-done.24.side_1 = bf16[2,96,1280]{2,1,0:T(8,128)(2,1)} collective-permute-done((bf16[2,96,1280]{2,1,0:T(8,128)(2,1)S(1)}, bf16[2,96,1280]{2,1,0:T(8,128)(2,1)}, u32[]{:S(2)}, u32[]{:S(2)}) %collective-permute-start.24) | collective-permute-done | bytes 491552 | tf_op jit(solution)/shard_map/ppermute | solution.py:179
  144.7 1.5 collective-permute-start.28
  146.2 1.3 collective-permute-start.27
  147.5 4.2 %collective-permute-done.29 = f16[2,192,512]{2,1,0:T(8,128)(2,1)S(1)} collective-permute-done((f16[2,192,512]{2,1,0:T(8,128)(2,1)S(1)}, f16[2,192,512]{2,1,0:T(8,128)(2,1)S(1)}, u32[]{:S(2)}, u32[]{:S(2)}) %collective-permute-start.29) | collective-permute-done | bytes 393248 | tf_op jit(solution)/shard_map/ppermute | solution.py:179
  151.6 1.2 fusion.16
  152.9 2.2 collective-permute-start.31
  155.1 1.4 collective-permute-start.32
  157.5 1.3 collective-permute-start.36
  158.8 5.3 %collective-permute-done.31 = f16[2,192,512]{2,1,0:T(8,128)(2,1)} collective-permute-done((f16[2,192,512]{2,1,0:T(8,128)(2,1)}, f16[2,192,512]{2,1,0:T(8,128)(2,1)}, u32[]{:S(2)}, u32[]{:S(2)}) %collective-permute-start.31) | collective-permute-done | bytes 393248 | tf_op jit(solution)/shard_map/ppermute | solution.py:179
  164.1 1.9 fusion.18
  167.0 1.4 collective-permute-start.34
  168.4 5.9 %collective-permute-start.33 = (bf16[2,192,512]{2,1,0:T(8,128)(2,1)}, bf16[2,192,512]{2,1,0:T(8,128)(2,1)}, u32[]{:S(2)}, u32[]{:S(2)}) collective-permute-start(bf16[2,192,512]{2,1,0:T(8,128)(2,1)} %pad_maximum_fusion.4.act), channel_id=1, source_target_pairs={{0,4},{2,6},{12,8},{14,10},{4,0},{6,2},{8,12},{10,14},{1,5},{3,7},... | collective-permute-start | bytes 1179656 | tf_op jit(solution)/shard_map/ppermute | solution.py:179
  175.4 7.3 %collective-permute-start.35 = (bf16[2,48,1792]{2,1,0:T(8,128)(2,1)}, bf16[2,48,1792]{2,1,0:T(8,128)(2,1)}, u32[]{:S(2)}, u32[]{:S(2)}) collective-permute-start(bf16[2,48,1792]{2,1,0:T(8,128)(2,1)} %get-tuple-element.192), channel_id=1, source_target_pairs={{0,2},{2,0},{4,6},{6,4},{8,10},{10,8},{12,14},{14,12},{1,3},{3,1},... | collective-permute-start | bytes 1032200 | tf_op jit(solution)/shard_map/ppermute | solution.py:179
  182.8 2.1 collective-permute-done.35
  185.9 2.0 shard_map.73
  188.7 1.3 collective-permute-start.37
  190.7 1.2 maximum_select_fusion.3
  192.3 7.0 %shard_map.74 = (f32[1024,3584]{1,0:T(8,128)}, f32[1024,3584]{1,0:T(8,128)}) custom-call(s32[1]{0:T(128)} %bitcast.59.place_ref, bf16[1024,768]{1,0:T(8,128)(2,1)S(1)} %maximum_bitcast_fusion.features_ref, bf16[4,1,2,96,1280]{4,3,2,1,0:T(8,128)(2,1)S(1)} %bitcast.165, bf16[4,1,2,96,1280]{4,3,2,1,0:T(8,128)(2,1)S(1)} %bitcast.167), custom_call_target="tpu_custom_call" | custom-call | flops 4026531840 | bytes 15990784 | tf_op jit(solution)/shard_map/pallas_call | solution.py:100
  200.3 1.5 collective-permute-start.39
  202.8 7.0 %shard_map.75 = (f32[1024,3584]{1,0:T(8,128)}, f32[1024,3584]{1,0:T(8,128)}) custom-call(s32[1]{0:T(128)} %bitcast.62.place_ref, bf16[1024,768]{1,0:T(8,128)(2,1)S(1)} %maximum_bitcast_fusion.features_ref, bf16[4,1,2,96,1280]{4,3,2,1,0:T(8,128)(2,1)S(1)} %bitcast.166, ...), custom_call_target="tpu_custom_call", output_to_operand_aliasing={{0}: (4, {}), {1}: (5, {})} | custom-call | flops 4026531840 | bytes 15990784 | tf_op jit(solution)/shard_map/pallas_call | solution.py:100
  209.8 2.0 collective-permute-done.39.out_3
  211.9 1.5 shard_map.76
  213.3 3.0 %collective-permute-start.43 = (bf16[4,2,192,512]{3,2,1,0:T(8,128)(2,1)S(1)}, bf16[4,2,192,512]{3,2,1,0:T(8,128)(2,1)S(1)}, u32[]{:S(2)}, u32[]{:S(2)}) collective-permute-start(bf16[4,2,192,512]{3,2,1,0:T(8,128)(2,1)S(1)} %shard_map.76), channel_id=1, source_target_pairs={{0,2},{2,0},{4,6},{6,4},{8,10},{10,8},{12,14},{14,12},{1,3},{3,1},... | collective-permute-start | bytes 4718600 | tf_op jit(solution)/shard_map/ppermute | solution.py:179
  216.3 3.4 %shard_map.77 = (f32[1024,3584]{1,0:T(8,128)}, f32[1024,3584]{1,0:T(8,128)}) custom-call(s32[1]{0:T(128)} %bitcast.59.place_ref, bf16[1024,768]{1,0:T(8,128)(2,1)S(1)} %maximum_bitcast_fusion.features_ref, bf16[4,1,2,192,512]{4,3,2,1,0:T(8,128)(2,1)S(1)} %bitcast.162, ...), custom_call_target="tpu_custom_call", output_to_operand_aliasing={{0}: (3, {}), {1}: (4, {})} | custom-call | flops 1610612736 | bytes 7340032 | tf_op jit(solution)/shard_map/pallas_call | solution.py:100
  219.8 3.4 %shard_map.78 = (f32[1024,3584]{1,0:T(8,128)}, f32[1024,3584]{1,0:T(8,128)}) custom-call(s32[1]{0:T(128)} %bitcast.62.place_ref, bf16[1024,768]{1,0:T(8,128)(2,1)S(1)} %maximum_bitcast_fusion.features_ref, bf16[4,1,2,192,512]{4,3,2,1,0:T(8,128)(2,1)S(1)} %bitcast.169, ...), custom_call_target="tpu_custom_call", output_to_operand_aliasing={{0}: (3, {}), {1}: (4, {})} | custom-call | flops 1610612736 | bytes 7340032 | tf_op jit(solution)/shard_map/pallas_call | solution.py:100
  (138 shorter events, 33.3 us)
Async XLA Ops:
  0.6 11.2 %collective-permute-start.1 = (bf16[384,512]{1,0:T(8,128)(2,1)}, bf16[384,512]{1,0:T(8,128)(2,1)S(1)}, u32[]{:S(2)}, u32[]{:S(2)}) collective-permute-start(bf16[384,512]{1,0:T(8,128)(2,1)} %bitcast.177), channel_id=1, source_target_pairs={{0,1},{1,0},{2,3},{3,2},{4,5},{5,4},{6,7},{7,6},{8,9},{9,8},{10,11... | collective-permute-start | bytes 1179656 | tf_op jit(solution)/shard_map/ppermute | solution.py:213
  2.8 9.9 %collective-permute-start = (bf16[384,512]{1,0:T(8,128)(2,1)}, bf16[384,512]{1,0:T(8,128)(2,1)S(1)}, u32[]{:S(2)}, u32[]{:S(2)}) collective-permute-start(bf16[384,512]{1,0:T(8,128)(2,1)} %bitcast.178), channel_id=1, source_target_pairs={{0,16},{16,0},{1,17},{17,1},{2,18},{18,2},{3,19},{19,3},{4,20},{20... | collective-permute-start | bytes 1179656 | tf_op jit(solution)/shard_map/ppermute | solution.py:212
  19.9 6.2 %collective-permute-start.2 = (f16[4,2,96,1280]{3,2,1,0:T(8,128)(2,1)}, f16[4,2,96,1280]{3,2,1,0:T(8,128)(2,1)S(1)}, u32[]{:S(2)}, u32[]{:S(2)}) collective-permute-start(f16[4,2,96,1280]{3,2,1,0:T(8,128)(2,1)} %convert_element_type.194), channel_id=1, source_target_pairs={{0,2},{2,0},{4,6},{6,4},{8,10},{10,8},{12,14},{14,12},{1,3},{3,1},... | collective-permute-start | bytes 5898248 | tf_op jit(solution)/shard_map/ppermute | solution.py:179
  25.9 10.9 %collective-permute-start.3 = (bf16[384,512]{1,0:T(8,128)(2,1)S(1)}, bf16[384,512]{1,0:T(8,128)(2,1)}, u32[]{:S(2)}, u32[]{:S(2)}) collective-permute-start(bf16[384,512]{1,0:T(8,128)(2,1)S(1)} %collective-permute-done), channel_id=1, source_target_pairs={{0,1},{1,0},{2,3},{3,2},{4,5},{5,4},{6,7},{7,6},{8,9},{9,8},{10,11... | collective-permute-start | bytes 1179656 | tf_op jit(solution)/shard_map/ppermute | solution.py:214
  28.7 14.9 %collective-permute-start.4 = (f16[2,96,1280]{2,1,0:T(8,128)(2,1)}, f16[2,96,1280]{2,1,0:T(8,128)(2,1)}, u32[]{:S(2)}, u32[]{:S(2)}) collective-permute-start(f16[2,96,1280]{2,1,0:T(8,128)(2,1)} %fusion.33), channel_id=1, source_target_pairs={{0,4},{2,6},{12,8},{14,10},{1,5},{3,7},{13,9},{15,11},{16,20},{18,... | collective-permute-start | bytes 1474568 | tf_op jit(solution)/shard_map/ppermute | solution.py:179
  42.8 11.9 %copy-start.26 = (bf16[1,48,7168]{2,1,0:T(8,128)(2,1)S(1)}, bf16[1,48,7168]{2,1,0:T(8,128)(2,1)}, u32[]{:S(2)}) copy-start(bf16[1,48,7168]{2,1,0:T(8,128)(2,1)} %param.7) | copy-start | bytes 2064388
  42.8 21.1 %collective-permute-start.6 = (f16[4,2,96,1280]{3,2,1,0:T(8,128)(2,1)S(1)}, f16[4,2,96,1280]{3,2,1,0:T(8,128)(2,1)S(1)}, u32[]{:S(2)}, u32[]{:S(2)}) collective-permute-start(f16[4,2,96,1280]{3,2,1,0:T(8,128)(2,1)S(1)} %convert_element_type.198), channel_id=1, source_target_pairs={{0,2},{2,0},{4,6},{6,4},{8,10},{10,8},{12,14},{14,12},{1,3},{3,1},... | collective-permute-start | bytes 5898248 | tf_op jit(solution)/shard_map/ppermute | solution.py:179
  46.7 17.3 %collective-permute-start.8 = (f16[2,96,1280]{2,1,0:T(8,128)(2,1)}, f16[2,96,1280]{2,1,0:T(8,128)(2,1)}, u32[]{:S(2)}, u32[]{:S(2)}) collective-permute-start(f16[2,96,1280]{2,1,0:T(8,128)(2,1)} %fusion.13), channel_id=1, source_target_pairs={{4,8},{6,10},{8,4},{10,6},{5,9},{7,11},{9,5},{11,7},{20,24},{22,26... | collective-permute-start | bytes 1474568 | tf_op jit(solution)/shard_map/ppermute | solution.py:179
  49.0 14.9 %collective-permute-start.7 = (f16[2,96,1280]{2,1,0:T(8,128)(2,1)}, f16[2,96,1280]{2,1,0:T(8,128)(2,1)}, u32[]{:S(2)}, u32[]{:S(2)}) collective-permute-start(f16[2,96,1280]{2,1,0:T(8,128)(2,1)} %fusion.30), channel_id=1, source_target_pairs={{0,4},{2,6},{12,8},{14,10},{1,5},{3,7},{13,9},{15,11},{16,20},{18,... | collective-permute-start | bytes 1474568 | tf_op jit(solution)/shard_map/ppermute | solution.py:179
  55.5 8.4 %collective-permute-start.5 = (bf16[48,3584]{1,0:T(8,128)(2,1)}, bf16[48,3584]{1,0:T(8,128)(2,1)S(1)}, u32[]{:S(2)}, u32[]{:S(2)}) collective-permute-start(bf16[48,3584]{1,0:T(8,128)(2,1)} %get-tuple-element.197), channel_id=1, source_target_pairs={{0,1},{1,0},{2,3},{3,2},{4,5},{5,4},{6,7},{7,6},{8,9},{9,8},{10,11... | collective-permute-start | bytes 1032200 | tf_op jit(solution)/shard_map/ppermute | solution.py:313
  59.9 47.8 %copy-start = (f32[4,2,96,1280]{3,2,1,0:T(8,128)}, f32[4,2,96,1280]{3,2,1,0:T(8,128)S(1)}, u32[]{:S(2)}) copy-start(f32[4,2,96,1280]{3,2,1,0:T(8,128)S(1)} %shard_map.70) | copy-start | bytes 11796484
  64.0 6.7 %copy-start.19 = (f16[4,2,96,1280]{3,2,1,0:T(8,128)(2,1)}, f16[4,2,96,1280]{3,2,1,0:T(8,128)(2,1)S(1)}, u32[]{:S(2)}) copy-start(f16[4,2,96,1280]{3,2,1,0:T(8,128)(2,1)S(1)} %collective-permute-done.6) | copy-start | bytes 5898244
  66.3 13.8 %collective-permute-start.11 = (f16[2,96,1280]{2,1,0:T(8,128)(2,1)S(1)}, f16[2,96,1280]{2,1,0:T(8,128)(2,1)S(1)}, u32[]{:S(2)}, u32[]{:S(2)}) collective-permute-start(f16[2,96,1280]{2,1,0:T(8,128)(2,1)S(1)} %get-tuple-element.175), channel_id=1, source_target_pairs={{0,4},{2,6},{12,8},{14,10},{4,0},{6,2},{8,12},{10,14},{1,5},{3,7},... | collective-permute-start | bytes 1474568 | tf_op jit(solution)/shard_map/ppermute | solution.py:179
  67.6 12.5 %collective-permute-start.12 = (f16[2,96,1280]{2,1,0:T(8,128)(2,1)S(1)}, f16[2,96,1280]{2,1,0:T(8,128)(2,1)S(1)}, u32[]{:S(2)}, u32[]{:S(2)}) collective-permute-start(f16[2,96,1280]{2,1,0:T(8,128)(2,1)S(1)} %get-tuple-element.176), channel_id=1, source_target_pairs={{4,8},{6,10},{8,4},{10,6},{5,9},{7,11},{9,5},{11,7},{20,24},{22,26... | collective-permute-start | bytes 1474568 | tf_op jit(solution)/shard_map/ppermute | solution.py:179
  68.4 10.6 %collective-permute-start.9 = (bf16[2,48,1792]{2,1,0:T(8,128)(2,1)S(1)}, bf16[2,48,1792]{2,1,0:T(8,128)(2,1)S(1)}, u32[]{:S(2)}, u32[]{:S(2)}) collective-permute-start(bf16[2,48,1792]{2,1,0:T(8,128)(2,1)S(1)} %get-tuple-element.196), channel_id=1, source_target_pairs={{0,2},{2,0},{4,6},{6,4},{8,10},{10,8},{12,14},{14,12},{1,3},{3,1},... | collective-permute-start | bytes 1032200 | tf_op jit(solution)/shard_map/ppermute | solution.py:179
  71.6 20.2 %collective-permute-start.16 = (f16[2,96,1280]{2,1,0:T(8,128)(2,1)}, f16[2,96,1280]{2,1,0:T(8,128)(2,1)}, u32[]{:S(2)}, u32[]{:S(2)}) collective-permute-start(f16[2,96,1280]{2,1,0:T(8,128)(2,1)} %fusion.31), channel_id=1, source_target_pairs={{0,4},{2,6},{12,8},{14,10},{1,5},{3,7},{13,9},{15,11},{16,20},{18,... | collective-permute-start | bytes 1474568 | tf_op jit(solution)/shard_map/ppermute | solution.py:179
  78.4 6.7 %collective-permute-start.13 = (bf16[2,1024,512]{2,1,0:T(8,128)(2,1)S(1)}, bf16[2,1024,512]{2,1,0:T(8,128)(2,1)S(1)}, u32[]{:S(2)}, u32[]{:S(2)}) collective-permute-start(bf16[2,1024,512]{2,1,0:T(8,128)(2,1)S(1)} %pad_maximum_fusion), channel_id=1, source_target_pairs={{0,2},{2,0},{4,6},{6,4},{8,10},{10,8},{12,14},{14,12},{1,3},{3,1},... | collective-permute-start | bytes 6291464 | tf_op jit(solution)/shard_map/ppermute | solution.py:179
  78.9 5.9 %collective-permute-start.10 = (bf16[4,2,96,1024]{3,2,0,1:T(8,128)(2,1)S(1)}, bf16[4,2,96,1024]{3,2,0,1:T(8,128)(2,1)S(1)}, u32[]{:S(2)}, u32[]{:S(2)}) collective-permute-start(bf16[4,2,96,1024]{3,2,0,1:T(8,128)(2,1)S(1)} %pad_maximum_fusion.1), channel_id=1, source_target_pairs={{0,2},{2,0},{4,6},{6,4},{8,10},{10,8},{12,14},{14,12},{1,3},{3,1},... | collective-permute-start | bytes 4718600 | tf_op jit(solution)/shard_map/ppermute | solution.py:179
  81.9 3.2 %copy-start.6 = (bf16[2,96,1280]{2,1,0:T(8,128)(2,1)}, bf16[2,96,1280]{2,1,0:T(8,128)(2,1)S(1)}, u32[]{:S(2)}) copy-start(bf16[2,96,1280]{2,1,0:T(8,128)(2,1)S(1)} %pad_maximum_fusion.2.act) | copy-start | bytes 1474564
  81.9 15.9 %collective-permute-start.15 = (bf16[2,96,1280]{2,1,0:T(8,128)(2,1)S(1)}, bf16[2,96,1280]{2,1,0:T(8,128)(2,1)S(1)}, u32[]{:S(2)}, u32[]{:S(2)}) collective-permute-start(bf16[2,96,1280]{2,1,0:T(8,128)(2,1)S(1)} %pad_maximum_fusion.2.act), channel_id=1, source_target_pairs={{4,8},{6,10},{8,4},{10,6},{5,9},{7,11},{9,5},{11,7},{20,24},{22,26... | collective-permute-start | bytes 1474568 | tf_op jit(solution)/shard_map/ppermute | solution.py:179
  82.8 15.0 %collective-permute-start.14 = (bf16[2,96,1280]{2,1,0:T(8,128)(2,1)S(1)}, bf16[2,96,1280]{2,1,0:T(8,128)(2,1)S(1)}, u32[]{:S(2)}, u32[]{:S(2)}) collective-permute-start(bf16[2,96,1280]{2,1,0:T(8,128)(2,1)S(1)} %pad_maximum_fusion.2.act), channel_id=1, source_target_pairs={{0,4},{2,6},{12,8},{14,10},{4,0},{6,2},{8,12},{10,14},{1,5},{3,7},... | collective-permute-start | bytes 1474568 | tf_op jit(solution)/shard_map/ppermute | solution.py:179
  85.2 6.7 %copy-start.20 = (f16[4,2,96,1280]{3,2,1,0:T(8,128)(2,1)S(1)}, f16[4,2,96,1280]{3,2,1,0:T(8,128)(2,1)}, u32[]{:S(2)}) copy-start(f16[4,2,96,1280]{3,2,1,0:T(8,128)(2,1)} %copy-done.19) | copy-start | bytes 5898244
  93.1 6.8 %collective-permute-start.20 = (f16[2,96,1280]{2,1,0:T(8,128)(2,1)S(1)}, f16[2,96,1280]{2,1,0:T(8,128)(2,1)S(1)}, u32[]{:S(2)}, u32[]{:S(2)}) collective-permute-start(f16[2,96,1280]{2,1,0:T(8,128)(2,1)S(1)} %fusion.6), channel_id=1, source_target_pairs={{4,8},{6,10},{8,4},{10,6},{5,9},{7,11},{9,5},{11,7},{20,24},{22,26... | collective-permute-start | bytes 1474568 | tf_op jit(solution)/shard_map/ppermute | solution.py:179
  93.9 13.9 %collective-permute-start.19 = (f16[2,96,1280]{2,1,0:T(8,128)(2,1)S(1)}, f16[2,96,1280]{2,1,0:T(8,128)(2,1)S(1)}, u32[]{:S(2)}, u32[]{:S(2)}) collective-permute-start(f16[2,96,1280]{2,1,0:T(8,128)(2,1)S(1)} %fusion.32), channel_id=1, source_target_pairs={{0,4},{2,6},{12,8},{14,10},{1,5},{3,7},{13,9},{15,11},{16,20},{18,... | collective-permute-start | bytes 1474568 | tf_op jit(solution)/shard_map/ppermute | solution.py:179
  97.8 11.3 %copy-start.8 = (bf16[2,96,1280]{2,1,0:T(8,128)(2,1)}, bf16[2,96,1280]{2,1,0:T(8,128)(2,1)S(1)}, u32[]{:S(2)}) copy-start(bf16[2,96,1280]{2,1,0:T(8,128)(2,1)S(1)} %collective-permute-done.15.centre_1) | copy-start | bytes 1474564
  97.8 11.3 %copy-start.10 = (bf16[2,96,1280]{2,1,0:T(8,128)(2,1)}, bf16[2,96,1280]{2,1,0:T(8,128)(2,1)S(1)}, u32[]{:S(2)}) copy-start(bf16[2,96,1280]{2,1,0:T(8,128)(2,1)S(1)} %collective-permute-done.14.side_1) | copy-start | bytes 1474564
  97.9 14.9 %collective-permute-start.18 = (bf16[2,96,1280]{2,1,0:T(8,128)(2,1)S(1)}, bf16[2,96,1280]{2,1,0:T(8,128)(2,1)S(1)}, u32[]{:S(2)}, u32[]{:S(2)}) collective-permute-start(bf16[2,96,1280]{2,1,0:T(8,128)(2,1)S(1)} %collective-permute-done.14.side_1), channel_id=1, source_target_pairs={{4,8},{6,10},{8,4},{10,6},{5,9},{7,11},{9,5},{11,7},{20,24},{22,26... | collective-permute-start | bytes 1474568 | tf_op jit(solution)/shard_map/ppermute | solution.py:179
  98.6 14.5 %collective-permute-start.17 = (bf16[2,96,1280]{2,1,0:T(8,128)(2,1)S(1)}, bf16[2,96,1280]{2,1,0:T(8,128)(2,1)S(1)}, u32[]{:S(2)}, u32[]{:S(2)}) collective-permute-start(bf16[2,96,1280]{2,1,0:T(8,128)(2,1)S(1)} %collective-permute-done.15.centre_1), channel_id=1, source_target_pairs={{4,0},{6,2},{8,12},{10,14},{5,1},{7,3},{9,13},{11,15},{20,16},{22,... | collective-permute-start | bytes 1474568 | tf_op jit(solution)/shard_map/ppermute | solution.py:179
  109.2 14.5 %collective-permute-start.22 = (f16[2,96,1280]{2,1,0:T(8,128)(2,1)}, f16[2,96,1280]{2,1,0:T(8,128)(2,1)}, u32[]{:S(2)}, u32[]{:S(2)}) collective-permute-start(f16[2,96,1280]{2,1,0:T(8,128)(2,1)} %get-tuple-element.173), channel_id=1, source_target_pairs={{0,4},{2,6},{12,8},{14,10},{4,0},{6,2},{8,12},{10,14},{1,5},{3,7},... | collective-permute-start | bytes 1474568 | tf_op jit(solution)/shard_map/ppermute | solution.py:179
  111.4 12.3 %collective-permute-start.23 = (f16[2,96,1280]{2,1,0:T(8,128)(2,1)}, f16[2,96,1280]{2,1,0:T(8,128)(2,1)}, u32[]{:S(2)}, u32[]{:S(2)}) collective-permute-start(f16[2,96,1280]{2,1,0:T(8,128)(2,1)} %get-tuple-element.174), channel_id=1, source_target_pairs={{4,8},{6,10},{8,4},{10,6},{5,9},{7,11},{9,5},{11,7},{20,24},{22,26... | collective-permute-start | bytes 1474568 | tf_op jit(solution)/shard_map/ppermute | solution.py:179
  112.8 5.5 %copy-start.12 = (bf16[2,96,1280]{2,1,0:T(8,128)(2,1)}, bf16[2,96,1280]{2,1,0:T(8,128)(2,1)S(1)}, u32[]{:S(2)}) copy-start(bf16[2,96,1280]{2,1,0:T(8,128)(2,1)S(1)} %collective-permute-done.18.share_2) | copy-start | bytes 1474564
  113.0 5.3 %copy-start.14 = (bf16[2,96,1280]{2,1,0:T(8,128)(2,1)}, bf16[2,96,1280]{2,1,0:T(8,128)(2,1)S(1)}, u32[]{:S(2)}) copy-start(bf16[2,96,1280]{2,1,0:T(8,128)(2,1)S(1)} %collective-permute-done.17.out_2) | copy-start | bytes 1474564
  113.0 21.1 %collective-permute-start.21 = (bf16[2,96,1280]{2,1,0:T(8,128)(2,1)S(1)}, bf16[2,96,1280]{2,1,0:T(8,128)(2,1)S(1)}, u32[]{:S(2)}, u32[]{:S(2)}) collective-permute-start(bf16[2,96,1280]{2,1,0:T(8,128)(2,1)S(1)} %collective-permute-done.18.share_2), channel_id=1, source_target_pairs={{4,0},{6,2},{8,12},{10,14},{5,1},{7,3},{9,13},{11,15},{20,16},{22,... | collective-permute-start | bytes 1474568 | tf_op jit(solution)/shard_map/ppermute | solution.py:179
  116.6 7.1 %copy-start.1 = (f32[4,2,96,1280]{3,2,1,0:T(8,128)S(1)}, f32[4,2,96,1280]{3,2,1,0:T(8,128)}, u32[]{:S(2)}) copy-start(f32[4,2,96,1280]{3,2,1,0:T(8,128)} %copy-done) | copy-start | bytes 11796484
  119.5 6.2 %copy-start.22 = (bf16[96,1792]{1,0:T(8,128)(2,1)S(1)}, bf16[96,1792]{1,0:T(8,128)(2,1)}, u32[]{:S(2)}) copy-start(bf16[96,1792]{1,0:T(8,128)(2,1)} %get-tuple-element.194) | copy-start | bytes 1032196
  119.5 16.7 %collective-permute-start.26 = (f16[2,192,512]{2,1,0:T(8,128)(2,1)S(1)}, f16[2,192,512]{2,1,0:T(8,128)(2,1)S(1)}, u32[]{:S(2)}, u32[]{:S(2)}) collective-permute-start(f16[2,192,512]{2,1,0:T(8,128)(2,1)S(1)} %fusion.39), channel_id=1, source_target_pairs={{0,4},{2,6},{12,8},{14,10},{1,5},{3,7},{13,9},{15,11},{16,20},{18,... | collective-permute-start | bytes 1179656 | tf_op jit(solution)/shard_map/ppermute | solution.py:179
  125.7 9.2 %copy-start.7 = (bf16[2,96,1280]{2,1,0:T(8,128)(2,1)S(1)}, bf16[2,96,1280]{2,1,0:T(8,128)(2,1)}, u32[]{:S(2)}) copy-start(bf16[2,96,1280]{2,1,0:T(8,128)(2,1)} %copy-done.6) | copy-start | bytes 1474564
  125.7 9.2 %copy-start.9 = (bf16[2,96,1280]{2,1,0:T(8,128)(2,1)S(1)}, bf16[2,96,1280]{2,1,0:T(8,128)(2,1)}, u32[]{:S(2)}) copy-start(bf16[2,96,1280]{2,1,0:T(8,128)(2,1)} %copy-done.8) | copy-start | bytes 1474564
  125.7 9.2 %copy-start.11 = (bf16[2,96,1280]{2,1,0:T(8,128)(2,1)S(1)}, bf16[2,96,1280]{2,1,0:T(8,128)(2,1)}, u32[]{:S(2)}) copy-start(bf16[2,96,1280]{2,1,0:T(8,128)(2,1)} %copy-done.10) | copy-start | bytes 1474564
  125.7 9.2 %copy-start.13 = (bf16[2,96,1280]{2,1,0:T(8,128)(2,1)S(1)}, bf16[2,96,1280]{2,1,0:T(8,128)(2,1)}, u32[]{:S(2)}) copy-start(bf16[2,96,1280]{2,1,0:T(8,128)(2,1)} %copy-done.12) | copy-start | bytes 1474564
  125.7 9.2 %copy-start.15 = (bf16[2,96,1280]{2,1,0:T(8,128)(2,1)S(1)}, bf16[2,96,1280]{2,1,0:T(8,128)(2,1)}, u32[]{:S(2)}) copy-start(bf16[2,96,1280]{2,1,0:T(8,128)(2,1)} %copy-done.14) | copy-start | bytes 1474564
  126.8 9.5 %copy-start.4 = (bf16[2,96,1280]{2,1,0:T(8,128)(2,1)}, bf16[2,96,1280]{2,1,0:T(8,128)(2,1)S(1)}, u32[]{:S(2)}) copy-start(bf16[2,96,1280]{2,1,0:T(8,128)(2,1)S(1)} %pad_maximum_fusion.3.act) | copy-start | bytes 1474564
  126.8 14.4 %collective-permute-start.25 = (bf16[2,96,1280]{2,1,0:T(8,128)(2,1)S(1)}, bf16[2,96,1280]{2,1,0:T(8,128)(2,1)}, u32[]{:S(2)}, u32[]{:S(2)}) collective-permute-start(bf16[2,96,1280]{2,1,0:T(8,128)(2,1)S(1)} %pad_maximum_fusion.3.act), channel_id=1, source_target_pairs={{4,8},{6,10},{8,4},{10,6},{5,9},{7,11},{9,5},{11,7},{20,24},{22,26... | collective-permute-start | bytes 1474568 | tf_op jit(solution)/shard_map/ppermute | solution.py:179
  128.3 16.5 %collective-permute-start.24 = (bf16[2,96,1280]{2,1,0:T(8,128)(2,1)S(1)}, bf16[2,96,1280]{2,1,0:T(8,128)(2,1)}, u32[]{:S(2)}, u32[]{:S(2)}) collective-permute-start(bf16[2,96,1280]{2,1,0:T(8,128)(2,1)S(1)} %pad_maximum_fusion.3.act), channel_id=1, source_target_pairs={{0,4},{2,6},{12,8},{14,10},{4,0},{6,2},{8,12},{10,14},{1,5},{3,7},... | collective-permute-start | bytes 1474568 | tf_op jit(solution)/shard_map/ppermute | solution.py:179
  138.0 9.5 %collective-permute-start.30 = (f16[2,192,512]{2,1,0:T(8,128)(2,1)S(1)}, f16[2,192,512]{2,1,0:T(8,128)(2,1)S(1)}, u32[]{:S(2)}, u32[]{:S(2)}) collective-permute-start(f16[2,192,512]{2,1,0:T(8,128)(2,1)S(1)} %fusion.19), channel_id=1, source_target_pairs={{4,8},{6,10},{8,4},{10,6},{5,9},{7,11},{9,5},{11,7},{20,24},{22,26... | collective-permute-start | bytes 1179656 | tf_op jit(solution)/shard_map/ppermute | solution.py:179
  138.7 13.0 %collective-permute-start.29 = (f16[2,192,512]{2,1,0:T(8,128)(2,1)S(1)}, f16[2,192,512]{2,1,0:T(8,128)(2,1)S(1)}, u32[]{:S(2)}, u32[]{:S(2)}) collective-permute-start(f16[2,192,512]{2,1,0:T(8,128)(2,1)S(1)} %fusion.40), channel_id=1, source_target_pairs={{0,4},{2,6},{12,8},{14,10},{1,5},{3,7},{13,9},{15,11},{16,20},{18,... | collective-permute-start | bytes 1179656 | tf_op jit(solution)/shard_map/ppermute | solution.py:179
  144.7 12.8 %collective-permute-start.28 = (bf16[2,96,1280]{2,1,0:T(8,128)(2,1)}, bf16[2,96,1280]{2,1,0:T(8,128)(2,1)}, u32[]{:S(2)}, u32[]{:S(2)}) collective-permute-start(bf16[2,96,1280]{2,1,0:T(8,128)(2,1)} %collective-permute-done.24.side_1), channel_id=1, source_target_pairs={{4,8},{6,10},{8,4},{10,6},{5,9},{7,11},{9,5},{11,7},{20,24},{22,26... | collective-permute-start | bytes 1474568 | tf_op jit(solution)/shard_map/ppermute | solution.py:179
  146.2 11.3 %collective-permute-start.27 = (bf16[2,96,1280]{2,1,0:T(8,128)(2,1)}, bf16[2,96,1280]{2,1,0:T(8,128)(2,1)}, u32[]{:S(2)}, u32[]{:S(2)}) collective-permute-start(bf16[2,96,1280]{2,1,0:T(8,128)(2,1)} %collective-permute-done.25.centre_1), channel_id=1, source_target_pairs={{4,0},{6,2},{8,12},{10,14},{5,1},{7,3},{9,13},{11,15},{20,16},{22,... | collective-permute-start | bytes 1474568 | tf_op jit(solution)/shard_map/ppermute | solution.py:179
  152.9 11.2 %collective-permute-start.31 = (f16[2,192,512]{2,1,0:T(8,128)(2,1)}, f16[2,192,512]{2,1,0:T(8,128)(2,1)}, u32[]{:S(2)}, u32[]{:S(2)}) collective-permute-start(f16[2,192,512]{2,1,0:T(8,128)(2,1)} %get-tuple-element.177), channel_id=1, source_target_pairs={{0,4},{2,6},{12,8},{14,10},{4,0},{6,2},{8,12},{10,14},{1,5},{3,7},... | collective-permute-start | bytes 1179656 | tf_op jit(solution)/shard_map/ppermute | solution.py:179
  155.1 9.0 %collective-permute-start.32 = (f16[2,192,512]{2,1,0:T(8,128)(2,1)}, f16[2,192,512]{2,1,0:T(8,128)(2,1)}, u32[]{:S(2)}, u32[]{:S(2)}) collective-permute-start(f16[2,192,512]{2,1,0:T(8,128)(2,1)} %get-tuple-element.178), channel_id=1, source_target_pairs={{4,8},{6,10},{8,4},{10,6},{5,9},{7,11},{9,5},{11,7},{20,24},{22,26... | collective-permute-start | bytes 1179656 | tf_op jit(solution)/shard_map/ppermute | solution.py:179
  157.5 25.3 %collective-permute-start.36 = (bf16[2,96,1280]{2,1,0:T(8,128)(2,1)}, bf16[2,96,1280]{2,1,0:T(8,128)(2,1)}, u32[]{:S(2)}, u32[]{:S(2)}) collective-permute-start(bf16[2,96,1280]{2,1,0:T(8,128)(2,1)} %collective-permute-done.28.share_2), channel_id=1, source_target_pairs={{4,0},{6,2},{8,12},{10,14},{5,1},{7,3},{9,13},{11,15},{20,16},{22,... | collective-permute-start | bytes 1474568 | tf_op jit(solution)/shard_map/ppermute | solution.py:179
  165.9 8.5 %copy-start.24 = (bf16[1,96,1280]{2,1,0:T(8,128)(2,1)S(1)}, bf16[1,96,1280]{2,1,0:T(8,128)(2,1)}, u32[]{:S(2)}) copy-start(bf16[1,96,1280]{2,1,0:T(8,128)(2,1)} %get-tuple-element.183) | copy-start | bytes 737284
  166.0 8.5 %copy-start.25 = (bf16[1,96,1280]{2,1,0:T(8,128)(2,1)S(1)}, bf16[1,96,1280]{2,1,0:T(8,128)(2,1)}, u32[]{:S(2)}) copy-start(bf16[1,96,1280]{2,1,0:T(8,128)(2,1)} %get-tuple-element.184) | copy-start | bytes 737284
  167.0 21.7 %collective-permute-start.34 = (bf16[2,192,512]{2,1,0:T(8,128)(2,1)}, bf16[2,192,512]{2,1,0:T(8,128)(2,1)}, u32[]{:S(2)}, u32[]{:S(2)}) collective-permute-start(bf16[2,192,512]{2,1,0:T(8,128)(2,1)} %pad_maximum_fusion.4.act), channel_id=1, source_target_pairs={{4,8},{6,10},{8,4},{10,6},{5,9},{7,11},{9,5},{11,7},{20,24},{22,26... | collective-permute-start | bytes 1179656 | tf_op jit(solution)/shard_map/ppermute | solution.py:179
  168.4 20.3 %collective-permute-start.33 = (bf16[2,192,512]{2,1,0:T(8,128)(2,1)}, bf16[2,192,512]{2,1,0:T(8,128)(2,1)}, u32[]{:S(2)}, u32[]{:S(2)}) collective-permute-start(bf16[2,192,512]{2,1,0:T(8,128)(2,1)} %pad_maximum_fusion.4.act), channel_id=1, source_target_pairs={{0,4},{2,6},{12,8},{14,10},{4,0},{6,2},{8,12},{10,14},{1,5},{3,7},... | collective-permute-start | bytes 1179656 | tf_op jit(solution)/shard_map/ppermute | solution.py:179
  175.4 9.4 %collective-permute-start.35 = (bf16[2,48,1792]{2,1,0:T(8,128)(2,1)}, bf16[2,48,1792]{2,1,0:T(8,128)(2,1)}, u32[]{:S(2)}, u32[]{:S(2)}) collective-permute-start(bf16[2,48,1792]{2,1,0:T(8,128)(2,1)} %get-tuple-element.192), channel_id=1, source_target_pairs={{0,2},{2,0},{4,6},{6,4},{8,10},{10,8},{12,14},{14,12},{1,3},{3,1},... | collective-permute-start | bytes 1032200 | tf_op jit(solution)/shard_map/ppermute | solution.py:179
  182.8 20.0 %collective-permute-start.40 = (bf16[4,2,96,1280]{3,2,1,0:T(8,128)(2,1)S(1)}, bf16[4,2,96,1280]{3,2,1,0:T(8,128)(2,1)S(1)}, u32[]{:S(2)}, u32[]{:S(2)}) collective-permute-start(bf16[4,2,96,1280]{3,2,1,0:T(8,128)(2,1)S(1)} %shard_map.72), channel_id=1, source_target_pairs={{0,2},{2,0},{4,6},{6,4},{8,10},{10,8},{12,14},{14,12},{1,3},{3,1},... | collective-permute-start | bytes 5898248 | tf_op jit(solution)/shard_map/ppermute | solution.py:179
  185.9 4.8 %copy-start.23 = (bf16[2,48,1792]{2,1,0:T(8,128)(2,1)S(1)}, bf16[2,48,1792]{2,1,0:T(8,128)(2,1)}, u32[]{:S(2)}) copy-start(bf16[2,48,1792]{2,1,0:T(8,128)(2,1)} %get-tuple-element.159) | copy-start | bytes 1032196
  187.9 14.9 %collective-permute-start.41 = (bf16[4,2,96,1280]{3,2,1,0:T(8,128)(2,1)S(1)}, bf16[4,2,96,1280]{3,2,1,0:T(8,128)(2,1)S(1)}, u32[]{:S(2)}, u32[]{:S(2)}) collective-permute-start(bf16[4,2,96,1280]{3,2,1,0:T(8,128)(2,1)S(1)} %shard_map.73), channel_id=1, source_target_pairs={{0,2},{2,0},{4,6},{6,4},{8,10},{10,8},{12,14},{14,12},{1,3},{3,1},... | collective-permute-start | bytes 5898248 | tf_op jit(solution)/shard_map/ppermute | solution.py:179
  188.7 11.6 %collective-permute-start.37 = (bf16[2,192,512]{2,1,0:T(8,128)(2,1)}, bf16[2,192,512]{2,1,0:T(8,128)(2,1)S(1)}, u32[]{:S(2)}, u32[]{:S(2)}) collective-permute-start(bf16[2,192,512]{2,1,0:T(8,128)(2,1)} %collective-permute-done.34.centre_1), channel_id=1, source_target_pairs={{4,0},{6,2},{8,12},{10,14},{5,1},{7,3},{9,13},{11,15},{20,16},{22,... | collective-permute-start | bytes 1179656 | tf_op jit(solution)/shard_map/ppermute | solution.py:179
  190.0 9.3 %collective-permute-start.38 = (bf16[2,192,512]{2,1,0:T(8,128)(2,1)}, bf16[2,192,512]{2,1,0:T(8,128)(2,1)S(1)}, u32[]{:S(2)}, u32[]{:S(2)}) collective-permute-start(bf16[2,192,512]{2,1,0:T(8,128)(2,1)} %collective-permute-done.33.side_1), channel_id=1, source_target_pairs={{4,8},{6,10},{8,4},{10,6},{5,9},{7,11},{9,5},{11,7},{20,24},{22,26... | collective-permute-start | bytes 1179656 | tf_op jit(solution)/shard_map/ppermute | solution.py:179
  192.0 9.8 %collective-permute-start.42 = (bf16[48,3584]{1,0:T(8,128)(2,1)S(1)}, bf16[48,3584]{1,0:T(8,128)(2,1)S(1)}, u32[]{:S(2)}, u32[]{:S(2)}) collective-permute-start(bf16[48,3584]{1,0:T(8,128)(2,1)S(1)} %get-tuple-element.190), channel_id=1, source_target_pairs={{0,1},{1,0},{2,3},{3,2},{4,5},{5,4},{6,7},{7,6},{8,9},{9,8},{10,11... | collective-permute-start | bytes 1032200 | tf_op jit(solution)/shard_map/ppermute | solution.py:321
  200.3 11.6 %collective-permute-start.39 = (bf16[2,192,512]{2,1,0:T(8,128)(2,1)S(1)}, bf16[2,192,512]{2,1,0:T(8,128)(2,1)S(1)}, u32[]{:S(2)}, u32[]{:S(2)}) collective-permute-start(bf16[2,192,512]{2,1,0:T(8,128)(2,1)S(1)} %collective-permute-done.38.share_2), channel_id=1, source_target_pairs={{4,0},{6,2},{8,12},{10,14},{5,1},{7,3},{9,13},{11,15},{20,16},{22,... | collective-permute-start | bytes 1179656 | tf_op jit(solution)/shard_map/ppermute | solution.py:179
  213.3 6.4 %collective-permute-start.43 = (bf16[4,2,192,512]{3,2,1,0:T(8,128)(2,1)S(1)}, bf16[4,2,192,512]{3,2,1,0:T(8,128)(2,1)S(1)}, u32[]{:S(2)}, u32[]{:S(2)}) collective-permute-start(bf16[4,2,192,512]{3,2,1,0:T(8,128)(2,1)S(1)} %shard_map.76), channel_id=1, source_target_pairs={{0,2},{2,0},{4,6},{6,4},{8,10},{10,8},{12,14},{14,12},{1,3},{3,1},... | collective-permute-start | bytes 4718600 | tf_op jit(solution)/shard_map/ppermute | solution.py:179
  (7 other events, 9.5 us)

commit v16 on v15

--- a/solution.py
+++ b/solution.py
@@ -16,7 +16,7 @@
 SHARES = (5, 2)
 
 
-def forward_kernel(scale, start, cores, place_ref, *refs):
+def forward_kernel(scale, start, unit, cores, place_ref, *refs):
     tokens, weights = refs[:cores], refs[cores : cores + 2 * cores]
     out_ref, held, arrived = refs[3 * cores :]
     tiles, _, tile = held.shape[1:]
@@ -26,7 +26,7 @@
     def copy(j, which):
         first = start + j * tile
         if which < 2:
-            columns = pl.ds(pl.multiple_of(place_ref[0] * tile + first, tile), tile)
+            columns = pl.ds(pl.multiple_of(place_ref[0] * unit + first, 128), tile)
             source = weights[which].at[:, columns]
         else:
             source = weights[which].at[which - 2, :, pl.ds(j * tile, tile)]
@@ -53,16 +53,17 @@
     total, depth = tokens[0].shape
     cores = len(tokens)
     shape = (blocks, 2, total // blocks, width)
+    steps = 2 if width % 256 == 0 else 1
     return pl.pallas_call(
-        functools.partial(forward_kernel, scale, start, cores),
+        functools.partial(forward_kernel, scale, start, tile, cores),
         out_shape=jax.ShapeDtypeStruct(shape, jnp.float32),
         in_specs=[pl.BlockSpec(memory_space=pltpu.SMEM)]
         + [pl.BlockSpec(memory_space=pltpu.VMEM)] * cores
         + [pl.BlockSpec(memory_space=pl.ANY)] * (2 * cores),
         out_specs=pl.BlockSpec(memory_space=pltpu.VMEM),
         scratch_shapes=[
-            pltpu.VMEM((cores, width // tile, depth, 2 * tile), jnp.bfloat16),
-            pltpu.SemaphoreType.DMA((2 * cores, width // tile)),
+            pltpu.VMEM((cores, steps, depth, 2 * (width // steps)), jnp.bfloat16),
+            pltpu.SemaphoreType.DMA((2 * cores, steps)),
         ],
         compiler_params=pltpu.CompilerParams(vmem_limit_bytes=VMEM_LIMIT),
         cost_estimate=cost,
@@ -245,7 +246,7 @@
     over_row = tie(over_row, over_depth)
     features = [arrange(by(row == 0, mine, over_row, 1))]
     theirs, own = own_features(features[0], 0, (), WIRE)
-    terms = (own(()), send(theirs, pairs))
+    terms = (own((), LONG), send(theirs, pairs))
     payload = take(terms, 3).astype(WIRE)
     in_1 = send(payload, inward)
 

time: 224 us -> 225 us (level)
    ppermute x39, waiting for transfers between devices: 29.1 us -> 33.3 us  [send(): return lax.ppermute(value, 'col', route)]
    ppermute x1, waiting for transfers between devices: 4.13 us -> 0.01 us  [local(): over_both = lax.ppermute(over_row, 'depth', swap)]
  transfers between devices with their start and end apart: 44 -> 44, of which waited for: 14 -> 14; matrix products, arithmetic and copies ran while one was open for 14% -> 14% of each run, Pallas kernels for 17% -> 18%
where the time goes in v16:
time: 225 us; the launch traced here: 224 us
  starting transfers between devices  85.5 us (38%)
  Pallas kernels  49.4 us (22%)
  waiting for transfers between devices  44.3 us (20%)
  other arithmetic  29 us (13%)
  local copies, waits for them, and re-layouts  14.5 us (6%)
    ppermute x39, starting transfers between devices, send(): return lax.ppermute(value, 'col', route)  79.5 us
    ppermute x39, waiting for transfers between devices, send(): return lax.ppermute(value, 'col', route)  33.3 us
    pallas_call x5, Pallas kernels, forward(): pl.pallas_call(functools.partial(forward_kernel, scale, start, tile, core...  24.8 us
    pallas_call x4, Pallas kernels, gradient(): pl.pallas_call(functools.partial(gradient_kernel, len(acts)), out_shape=(...  20.9 us
    ppermute x1, waiting for transfers between devices, local(): over_depth = lax.ppermute(mine, 'depth', swap)  7.84 us
    unnamed x54, local copies, waits for them, and re-layouts  6.75 us
    select_n x5, other arithmetic, by(): jnp.where(first, jnp.concatenate([mine, theirs], axis=axis), jnp.concaten...  5.04 us
    convert_element_type x3, other arithmetic, local(): swapped = swapped.astype(WIRE)  4.97 us
  transfers between devices with their start and end apart: 44, of which 14 were waited for; matrix products, arithmetic and copies ran while one was open for 14% of the time, Pallas kernels for 18%

profile of v16, /device:TPU:1, one launch (start us, length us, event | category | flops | bytes accessed | tf_op | source)
XLA Modules:
  0.0 224.1 jit_solution(14264249018571194983)
XLA Ops:
  0.6 2.1 collective-permute-start.1
  4.0 7.8 %collective-permute-done.1 = bf16[384,512]{1,0:T(8,128)(2,1)S(1)} collective-permute-done((bf16[384,512]{1,0:T(8,128)(2,1)}, bf16[384,512]{1,0:T(8,128)(2,1)S(1)}, u32[]{:S(2)}, u32[]{:S(2)}) %collective-permute-start.1) | collective-permute-done | bytes 393248 | tf_op jit(solution)/shard_map/ppermute | solution.py:214
  12.6 1.3 maximum_select_fusion
  14.2 4.5 %shard_map.67 = f32[4,2,96,1280]{3,2,1,0:T(8,128)S(1)} custom-call(s32[1]{0:T(128)} %bitcast.6.place_ref, bf16[384,1024]{1,0:T(8,128)(2,1)S(1)} %bitcast.154, bf16[1024,7168]{1,0:T(8,128)(2,1)} %refs_2_.9, bf16[1024,7168]{1,0:T(8,128)(2,1)} %refs_3_.1), custom_call_target="tpu_custom_call" | custom-call | tf_op jit(solution)/shard_map/pallas_call | solution.py:57
  18.7 1.5 convert_element_type.194
  20.2 1.9 collective-permute-start.2
  22.2 4.5 %shard_map.68 = f32[4,2,96,1280]{3,2,1,0:T(8,128)S(1)} custom-call(s32[1]{0:T(128)} %bitcast.1.place_ref, bf16[384,1024]{1,0:T(8,128)(2,1)S(1)} %bitcast.155, bf16[1024,7168]{1,0:T(8,128)(2,1)} %refs_2_.9, bf16[1024,7168]{1,0:T(8,128)(2,1)} %refs_3_.1), custom_call_target="tpu_custom_call" | custom-call | flops 6000000000 | tf_op jit(solution)/shard_map/pallas_call | solution.py:57
  26.7 1.9 copy-done.2
  29.5 4.1 %collective-permute-start.4 = (f16[2,96,1280]{2,1,0:T(8,128)(2,1)}, f16[2,96,1280]{2,1,0:T(8,128)(2,1)}, u32[]{:S(2)}, u32[]{:S(2)}) collective-permute-start(f16[2,96,1280]{2,1,0:T(8,128)(2,1)} %fusion.33), channel_id=1, source_target_pairs={{0,4},{2,6},{12,8},{14,10},{1,5},{3,7},{13,9},{15,11},{16,20},{18,... | collective-permute-start | bytes 1474568 | tf_op jit(solution)/shard_map/ppermute | solution.py:180
  33.6 1.3 maximum_select_fusion.1
  35.2 4.5 %shard_map.69 = f32[4,2,96,1280]{3,2,1,0:T(8,128)S(1)} custom-call(s32[1]{0:T(128)} %bitcast.6.place_ref, bf16[384,1024]{1,0:T(8,128)(2,1)S(1)} %bitcast.158, bf16[1024,7168]{1,0:T(8,128)(2,1)} %refs_2_.9, bf16[1024,7168]{1,0:T(8,128)(2,1)} %refs_3_.1), custom_call_target="tpu_custom_call" | custom-call | tf_op jit(solution)/shard_map/pallas_call | solution.py:57
  40.6 2.9 %collective-permute-done.4 = f16[2,96,1280]{2,1,0:T(8,128)(2,1)} collective-permute-done((f16[2,96,1280]{2,1,0:T(8,128)(2,1)}, f16[2,96,1280]{2,1,0:T(8,128)(2,1)}, u32[]{:S(2)}, u32[]{:S(2)}) %collective-permute-start.4) | collective-permute-done | bytes 491552 | tf_op jit(solution)/shard_map/ppermute | solution.py:180
  43.5 2.0 fusion.13
  45.5 1.5 collective-permute-start.8
  47.8 6.6 %collective-permute-start.7 = (f16[2,96,1280]{2,1,0:T(8,128)(2,1)}, f16[2,96,1280]{2,1,0:T(8,128)(2,1)}, u32[]{:S(2)}, u32[]{:S(2)}) collective-permute-start(f16[2,96,1280]{2,1,0:T(8,128)(2,1)} %fusion.30), channel_id=1, source_target_pairs={{0,4},{2,6},{12,8},{14,10},{1,5},{3,7},{13,9},{15,11},{16,20},{18,... | collective-permute-start | bytes 1474568 | tf_op jit(solution)/shard_map/ppermute | solution.py:180
  55.2 1.2 collective-permute-start.5
  56.5 4.5 %shard_map.70 = f32[4,2,96,1280]{3,2,1,0:T(8,128)S(1)} custom-call(s32[1]{0:T(128)} %bitcast.1.place_ref, bf16[384,1024]{1,0:T(8,128)(2,1)S(1)} %bitcast.159, bf16[1024,7168]{1,0:T(8,128)(2,1)} %refs_2_.9, bf16[1024,7168]{1,0:T(8,128)(2,1)} %refs_3_.1), custom_call_target="tpu_custom_call" | custom-call | flops 6000000000 | tf_op jit(solution)/shard_map/pallas_call | solution.py:57
  61.0 2.3 %collective-permute-done.5 = bf16[48,3584]{1,0:T(8,128)(2,1)S(1)} collective-permute-done((bf16[48,3584]{1,0:T(8,128)(2,1)}, bf16[48,3584]{1,0:T(8,128)(2,1)S(1)}, u32[]{:S(2)}, u32[]{:S(2)}) %collective-permute-start.5) | collective-permute-done | bytes 344096 | tf_op jit(solution)/shard_map/ppermute | solution.py:314
  63.4 2.3 %fusion.8 = (f16[2,96,1280]{2,1,0:T(8,128)(2,1)S(1)}, f16[2,96,1280]{2,1,0:T(8,128)(2,1)S(1)}) fusion(f16[2,96,1280]{2,1,0:T(8,128)(2,1)} %collective-permute-done.8, f32[4,2,96,1280]{3,2,1,0:T(8,128)S(1)} %copy-done.3, pred[]{:T(512)S(6)} %or.3, f16[4,2,96,1280]{3,2,1,0:T(8,128)(2,1)S(1)} %collective-permute-done.2, ...), kind=kLoop, calls=%fused_computation.22 | loop fusion | flops 3194880 | bytes 6389761 | tf_op jit(solution)/shard_map/convert_element_type | solution.py:330
  65.7 1.3 collective-permute-start.11
  67.8 2.6 %collective-permute-start.9 = (bf16[2,48,1792]{2,1,0:T(8,128)(2,1)S(1)}, bf16[2,48,1792]{2,1,0:T(8,128)(2,1)S(1)}, u32[]{:S(2)}, u32[]{:S(2)}) collective-permute-start(bf16[2,48,1792]{2,1,0:T(8,128)(2,1)S(1)} %get-tuple-element.196), channel_id=1, source_target_pairs={{0,2},{2,0},{4,6},{6,4},{8,10},{10,8},{12,14},{14,12},{1,3},{3,1},... | collective-permute-start | bytes 1032200 | tf_op jit(solution)/shard_map/ppermute | solution.py:180
  71.3 5.1 %collective-permute-start.16 = (f16[2,96,1280]{2,1,0:T(8,128)(2,1)}, f16[2,96,1280]{2,1,0:T(8,128)(2,1)}, u32[]{:S(2)}, u32[]{:S(2)}) collective-permute-start(f16[2,96,1280]{2,1,0:T(8,128)(2,1)} %fusion.31), channel_id=1, source_target_pairs={{0,4},{2,6},{12,8},{14,10},{1,5},{3,7},{13,9},{15,11},{16,20},{18,... | collective-permute-start | bytes 1474568 | tf_op jit(solution)/shard_map/ppermute | solution.py:180
  76.4 1.7 dynamic-slice_bitcast_fusion
  85.1 6.7 %shard_map.71 = f32[4,2,192,512]{3,2,1,0:T(8,128)} custom-call(s32[1]{0:T(128)} %bitcast.1.place_ref, bf16[768,1024]{1,0:T(8,128)(2,1)S(1)} %bitcast.163, bf16[768,1024]{1,0:T(8,128)(2,1)S(1)} %bitcast.164, bf16[1024,7168]{1,0:T(8,128)(2,1)} %refs_2_.9, bf16[1024,7168]{1,0:T(8,128)(2,1)} %refs_3_.1, ...), custom_call_target="tpu_custom_call" | custom-call | tf_op jit(solution)/shard_map/pallas_call | solution.py:57
  93.8 3.7 %collective-permute-start.19 = (f16[2,96,1280]{2,1,0:T(8,128)(2,1)S(1)}, f16[2,96,1280]{2,1,0:T(8,128)(2,1)S(1)}, u32[]{:S(2)}, u32[]{:S(2)}) collective-permute-start(f16[2,96,1280]{2,1,0:T(8,128)(2,1)S(1)} %fusion.32), channel_id=1, source_target_pairs={{0,4},{2,6},{12,8},{14,10},{1,5},{3,7},{13,9},{15,11},{16,20},{18,... | collective-permute-start | bytes 1474568 | tf_op jit(solution)/shard_map/ppermute | solution.py:180
  98.3 1.3 collective-permute-start.17
  99.6 7.8 %collective-permute-done.19 = f16[2,96,1280]{2,1,0:T(8,128)(2,1)S(1)} collective-permute-done((f16[2,96,1280]{2,1,0:T(8,128)(2,1)S(1)}, f16[2,96,1280]{2,1,0:T(8,128)(2,1)S(1)}, u32[]{:S(2)}, u32[]{:S(2)}) %collective-permute-start.19) | collective-permute-done | bytes 491552 | tf_op jit(solution)/shard_map/ppermute | solution.py:180
  107.4 1.4 fusion.4
  108.8 2.2 collective-permute-start.22
  111.0 1.4 collective-permute-start.23
  113.4 1.3 collective-permute-start.21
  117.0 1.6 maximum_bitcast_fusion.features_ref
  119.9 4.2 %collective-permute-start.26 = (f16[2,192,512]{2,1,0:T(8,128)(2,1)S(1)}, f16[2,192,512]{2,1,0:T(8,128)(2,1)S(1)}, u32[]{:S(2)}, u32[]{:S(2)}) collective-permute-start(f16[2,192,512]{2,1,0:T(8,128)(2,1)S(1)} %fusion.39), channel_id=1, source_target_pairs={{0,4},{2,6},{12,8},{14,10},{1,5},{3,7},{13,9},{15,11},{16,20},{18,... | collective-permute-start | bytes 1179656 | tf_op jit(solution)/shard_map/ppermute | solution.py:180
  124.1 1.9 fusion.2
  127.1 1.5 collective-permute-start.25
  128.6 3.2 %collective-permute-start.24 = (bf16[2,96,1280]{2,1,0:T(8,128)(2,1)S(1)}, bf16[2,96,1280]{2,1,0:T(8,128)(2,1)}, u32[]{:S(2)}, u32[]{:S(2)}) collective-permute-start(bf16[2,96,1280]{2,1,0:T(8,128)(2,1)S(1)} %pad_maximum_fusion.3.act), channel_id=1, source_target_pairs={{0,4},{2,6},{12,8},{14,10},{4,0},{6,2},{8,12},{10,14},{1,5},{3,7},... | collective-permute-start | bytes 1474568 | tf_op jit(solution)/shard_map/ppermute | solution.py:180
  131.8 2.7 %collective-permute-done.21.out_3 = bf16[2,96,1280]{2,1,0:T(8,128)(2,1)S(1)} collective-permute-done((bf16[2,96,1280]{2,1,0:T(8,128)(2,1)S(1)}, bf16[2,96,1280]{2,1,0:T(8,128)(2,1)S(1)}, u32[]{:S(2)}, u32[]{:S(2)}) %collective-permute-start.21) | collective-permute-done | bytes 491552 | tf_op jit(solution)/shard_map/ppermute | solution.py:180
  136.6 1.6 copy-done.18
  139.0 2.4 %collective-permute-start.29 = (f16[2,192,512]{2,1,0:T(8,128)(2,1)S(1)}, f16[2,192,512]{2,1,0:T(8,128)(2,1)S(1)}, u32[]{:S(2)}, u32[]{:S(2)}) collective-permute-start(f16[2,192,512]{2,1,0:T(8,128)(2,1)S(1)} %fusion.40), channel_id=1, source_target_pairs={{0,4},{2,6},{12,8},{14,10},{1,5},{3,7},{13,9},{15,11},{16,20},{18,... | collective-permute-start | bytes 1179656 | tf_op jit(solution)/shard_map/ppermute | solution.py:180
  141.5 3.6 %collective-permute-done.24.side_1 = bf16[2,96,1280]{2,1,0:T(8,128)(2,1)} collective-permute-done((bf16[2,96,1280]{2,1,0:T(8,128)(2,1)S(1)}, bf16[2,96,1280]{2,1,0:T(8,128)(2,1)}, u32[]{:S(2)}, u32[]{:S(2)}) %collective-permute-start.24) | collective-permute-done | bytes 491552 | tf_op jit(solution)/shard_map/ppermute | solution.py:180
  145.1 1.5 collective-permute-start.28
  146.5 1.3 collective-permute-start.27
  147.8 2.5 %collective-permute-done.29 = f16[2,192,512]{2,1,0:T(8,128)(2,1)S(1)} collective-permute-done((f16[2,192,512]{2,1,0:T(8,128)(2,1)S(1)}, f16[2,192,512]{2,1,0:T(8,128)(2,1)S(1)}, u32[]{:S(2)}, u32[]{:S(2)}) %collective-permute-start.29) | collective-permute-done | bytes 393248 | tf_op jit(solution)/shard_map/ppermute | solution.py:180
  151.6 2.2 collective-permute-start.31
  153.8 1.4 collective-permute-start.32
  156.4 1.3 collective-permute-start.36
  157.7 6.2 %collective-permute-done.31 = f16[2,192,512]{2,1,0:T(8,128)(2,1)} collective-permute-done((f16[2,192,512]{2,1,0:T(8,128)(2,1)}, f16[2,192,512]{2,1,0:T(8,128)(2,1)}, u32[]{:S(2)}, u32[]{:S(2)}) %collective-permute-start.31) | collective-permute-done | bytes 393248 | tf_op jit(solution)/shard_map/ppermute | solution.py:180
  163.9 1.9 fusion.18
  166.8 1.4 collective-permute-start.34
  168.3 6.0 %collective-permute-start.33 = (bf16[2,192,512]{2,1,0:T(8,128)(2,1)}, bf16[2,192,512]{2,1,0:T(8,128)(2,1)}, u32[]{:S(2)}, u32[]{:S(2)}) collective-permute-start(bf16[2,192,512]{2,1,0:T(8,128)(2,1)} %pad_maximum_fusion.4.act), channel_id=1, source_target_pairs={{0,4},{2,6},{12,8},{14,10},{4,0},{6,2},{8,12},{10,14},{1,5},{3,7},... | collective-permute-start | bytes 1179656 | tf_op jit(solution)/shard_map/ppermute | solution.py:180
  175.3 7.3 %collective-permute-start.35 = (bf16[2,48,1792]{2,1,0:T(8,128)(2,1)}, bf16[2,48,1792]{2,1,0:T(8,128)(2,1)}, u32[]{:S(2)}, u32[]{:S(2)}) collective-permute-start(bf16[2,48,1792]{2,1,0:T(8,128)(2,1)} %get-tuple-element.192), channel_id=1, source_target_pairs={{0,2},{2,0},{4,6},{6,4},{8,10},{10,8},{12,14},{14,12},{1,3},{3,1},... | collective-permute-start | bytes 1032200 | tf_op jit(solution)/shard_map/ppermute | solution.py:180
  182.7 2.1 collective-permute-done.35
  185.8 2.0 shard_map.73
  188.6 1.3 collective-permute-start.37
  190.6 1.2 maximum_select_fusion.3
  191.9 1.3 collective-permute-start.42
  193.2 7.0 %shard_map.74 = (f32[1024,3584]{1,0:T(8,128)}, f32[1024,3584]{1,0:T(8,128)}) custom-call(s32[1]{0:T(128)} %bitcast.59.place_ref, bf16[1024,768]{1,0:T(8,128)(2,1)S(1)} %maximum_bitcast_fusion.features_ref, bf16[4,1,2,96,1280]{4,3,2,1,0:T(8,128)(2,1)S(1)} %bitcast.165, bf16[4,1,2,96,1280]{4,3,2,1,0:T(8,128)(2,1)S(1)} %bitcast.167), custom_call_target="tpu_custom_call" | custom-call | flops 4026531840 | bytes 15990784 | tf_op jit(solution)/shard_map/pallas_call | solution.py:101
  200.2 1.5 collective-permute-start.39
  202.8 7.0 %shard_map.75 = (f32[1024,3584]{1,0:T(8,128)}, f32[1024,3584]{1,0:T(8,128)}) custom-call(s32[1]{0:T(128)} %bitcast.62.place_ref, bf16[1024,768]{1,0:T(8,128)(2,1)S(1)} %maximum_bitcast_fusion.features_ref, bf16[4,1,2,96,1280]{4,3,2,1,0:T(8,128)(2,1)S(1)} %bitcast.166, ...), custom_call_target="tpu_custom_call", output_to_operand_aliasing={{0}: (4, {}), {1}: (5, {})} | custom-call | flops 4026531840 | bytes 15990784 | tf_op jit(solution)/shard_map/pallas_call | solution.py:101
  209.8 3.3 %collective-permute-done.39.out_3 = bf16[2,192,512]{2,1,0:T(8,128)(2,1)S(1)} collective-permute-done((bf16[2,192,512]{2,1,0:T(8,128)(2,1)S(1)}, bf16[2,192,512]{2,1,0:T(8,128)(2,1)S(1)}, u32[]{:S(2)}, u32[]{:S(2)}) %collective-permute-start.39) | collective-permute-done | bytes 393248 | tf_op jit(solution)/shard_map/ppermute | solution.py:180
  213.1 1.5 shard_map.76
  214.6 2.7 %collective-permute-start.43 = (bf16[4,2,192,512]{3,2,1,0:T(8,128)(2,1)S(1)}, bf16[4,2,192,512]{3,2,1,0:T(8,128)(2,1)S(1)}, u32[]{:S(2)}, u32[]{:S(2)}) collective-permute-start(bf16[4,2,192,512]{3,2,1,0:T(8,128)(2,1)S(1)} %shard_map.76), channel_id=1, source_target_pairs={{0,2},{2,0},{4,6},{6,4},{8,10},{10,8},{12,14},{14,12},{1,3},{3,1},... | collective-permute-start | bytes 4718600 | tf_op jit(solution)/shard_map/ppermute | solution.py:180
  217.3 3.4 %shard_map.77 = (f32[1024,3584]{1,0:T(8,128)}, f32[1024,3584]{1,0:T(8,128)}) custom-call(s32[1]{0:T(128)} %bitcast.59.place_ref, bf16[1024,768]{1,0:T(8,128)(2,1)S(1)} %maximum_bitcast_fusion.features_ref, bf16[4,1,2,192,512]{4,3,2,1,0:T(8,128)(2,1)S(1)} %bitcast.162, ...), custom_call_target="tpu_custom_call", output_to_operand_aliasing={{0}: (3, {}), {1}: (4, {})} | custom-call | flops 1610612736 | bytes 7340032 | tf_op jit(solution)/shard_map/pallas_call | solution.py:101
  220.7 3.4 %shard_map.78 = (f32[1024,3584]{1,0:T(8,128)}, f32[1024,3584]{1,0:T(8,128)}) custom-call(s32[1]{0:T(128)} %bitcast.62.place_ref, bf16[1024,768]{1,0:T(8,128)(2,1)S(1)} %maximum_bitcast_fusion.features_ref, bf16[4,1,2,192,512]{4,3,2,1,0:T(8,128)(2,1)S(1)} %bitcast.169, ...), custom_call_target="tpu_custom_call", output_to_operand_aliasing={{0}: (3, {}), {1}: (4, {})} | custom-call | flops 1610612736 | bytes 7340032 | tf_op jit(solution)/shard_map/pallas_call | solution.py:101
  (138 shorter events, 33.9 us)
Async XLA Ops:
  0.6 11.2 %collective-permute-start.1 = (bf16[384,512]{1,0:T(8,128)(2,1)}, bf16[384,512]{1,0:T(8,128)(2,1)S(1)}, u32[]{:S(2)}, u32[]{:S(2)}) collective-permute-start(bf16[384,512]{1,0:T(8,128)(2,1)} %bitcast.177), channel_id=1, source_target_pairs={{0,1},{1,0},{2,3},{3,2},{4,5},{5,4},{6,7},{7,6},{8,9},{9,8},{10,11... | collective-permute-start | bytes 1179656 | tf_op jit(solution)/shard_map/ppermute | solution.py:214
  2.8 9.9 %collective-permute-start = (bf16[384,512]{1,0:T(8,128)(2,1)}, bf16[384,512]{1,0:T(8,128)(2,1)S(1)}, u32[]{:S(2)}, u32[]{:S(2)}) collective-permute-start(bf16[384,512]{1,0:T(8,128)(2,1)} %bitcast.178), channel_id=1, source_target_pairs={{0,16},{16,0},{1,17},{17,1},{2,18},{18,2},{3,19},{19,3},{4,20},{20... | collective-permute-start | bytes 1179656 | tf_op jit(solution)/shard_map/ppermute | solution.py:213
  20.2 6.5 %collective-permute-start.2 = (f16[4,2,96,1280]{3,2,1,0:T(8,128)(2,1)}, f16[4,2,96,1280]{3,2,1,0:T(8,128)(2,1)S(1)}, u32[]{:S(2)}, u32[]{:S(2)}) collective-permute-start(f16[4,2,96,1280]{3,2,1,0:T(8,128)(2,1)} %convert_element_type.194), channel_id=1, source_target_pairs={{0,2},{2,0},{4,6},{6,4},{8,10},{10,8},{12,14},{14,12},{1,3},{3,1},... | collective-permute-start | bytes 5898248 | tf_op jit(solution)/shard_map/ppermute | solution.py:180
  22.1 11.6 %collective-permute-start.3 = (bf16[384,512]{1,0:T(8,128)(2,1)S(1)}, bf16[384,512]{1,0:T(8,128)(2,1)}, u32[]{:S(2)}, u32[]{:S(2)}) collective-permute-start(bf16[384,512]{1,0:T(8,128)(2,1)S(1)} %collective-permute-done), channel_id=1, source_target_pairs={{0,1},{1,0},{2,3},{3,2},{4,5},{5,4},{6,7},{7,6},{8,9},{9,8},{10,11... | collective-permute-start | bytes 1179656 | tf_op jit(solution)/shard_map/ppermute | solution.py:215
  29.5 14.0 %collective-permute-start.4 = (f16[2,96,1280]{2,1,0:T(8,128)(2,1)}, f16[2,96,1280]{2,1,0:T(8,128)(2,1)}, u32[]{:S(2)}, u32[]{:S(2)}) collective-permute-start(f16[2,96,1280]{2,1,0:T(8,128)(2,1)} %fusion.33), channel_id=1, source_target_pairs={{0,4},{2,6},{12,8},{14,10},{1,5},{3,7},{13,9},{15,11},{16,20},{18,... | collective-permute-start | bytes 1474568 | tf_op jit(solution)/shard_map/ppermute | solution.py:180
  39.7 3.8 %copy-start.3 = (f32[4,2,96,1280]{3,2,1,0:T(8,128)S(1)}, f32[4,2,96,1280]{3,2,1,0:T(8,128)}, u32[]{:S(2)}) copy-start(f32[4,2,96,1280]{3,2,1,0:T(8,128)} %copy-done.2) | copy-start | bytes 11796484
  40.0 14.5 %copy-start.26 = (bf16[1,48,7168]{2,1,0:T(8,128)(2,1)S(1)}, bf16[1,48,7168]{2,1,0:T(8,128)(2,1)}, u32[]{:S(2)}) copy-start(bf16[1,48,7168]{2,1,0:T(8,128)(2,1)} %param.7) | copy-start | bytes 2064388
  40.0 23.4 %collective-permute-start.6 = (f16[4,2,96,1280]{3,2,1,0:T(8,128)(2,1)S(1)}, f16[4,2,96,1280]{3,2,1,0:T(8,128)(2,1)S(1)}, u32[]{:S(2)}, u32[]{:S(2)}) collective-permute-start(f16[4,2,96,1280]{3,2,1,0:T(8,128)(2,1)S(1)} %convert_element_type.198), channel_id=1, source_target_pairs={{0,2},{2,0},{4,6},{6,4},{8,10},{10,8},{12,14},{14,12},{1,3},{3,1},... | collective-permute-start | bytes 5898248 | tf_op jit(solution)/shard_map/ppermute | solution.py:180
  45.5 17.9 %collective-permute-start.8 = (f16[2,96,1280]{2,1,0:T(8,128)(2,1)}, f16[2,96,1280]{2,1,0:T(8,128)(2,1)}, u32[]{:S(2)}, u32[]{:S(2)}) collective-permute-start(f16[2,96,1280]{2,1,0:T(8,128)(2,1)} %fusion.13), channel_id=1, source_target_pairs={{4,8},{6,10},{8,4},{10,6},{5,9},{7,11},{9,5},{11,7},{20,24},{22,26... | collective-permute-start | bytes 1474568 | tf_op jit(solution)/shard_map/ppermute | solution.py:180
  47.8 15.5 %collective-permute-start.7 = (f16[2,96,1280]{2,1,0:T(8,128)(2,1)}, f16[2,96,1280]{2,1,0:T(8,128)(2,1)}, u32[]{:S(2)}, u32[]{:S(2)}) collective-permute-start(f16[2,96,1280]{2,1,0:T(8,128)(2,1)} %fusion.30), channel_id=1, source_target_pairs={{0,4},{2,6},{12,8},{14,10},{1,5},{3,7},{13,9},{15,11},{16,20},{18,... | collective-permute-start | bytes 1474568 | tf_op jit(solution)/shard_map/ppermute | solution.py:180
  55.2 8.1 %collective-permute-start.5 = (bf16[48,3584]{1,0:T(8,128)(2,1)}, bf16[48,3584]{1,0:T(8,128)(2,1)S(1)}, u32[]{:S(2)}, u32[]{:S(2)}) collective-permute-start(bf16[48,3584]{1,0:T(8,128)(2,1)} %get-tuple-element.197), channel_id=1, source_target_pairs={{0,1},{1,0},{2,3},{3,2},{4,5},{5,4},{6,7},{7,6},{8,9},{9,8},{10,11... | collective-permute-start | bytes 1032200 | tf_op jit(solution)/shard_map/ppermute | solution.py:314
  61.0 46.4 %copy-start = (f32[4,2,96,1280]{3,2,1,0:T(8,128)}, f32[4,2,96,1280]{3,2,1,0:T(8,128)S(1)}, u32[]{:S(2)}) copy-start(f32[4,2,96,1280]{3,2,1,0:T(8,128)S(1)} %shard_map.70) | copy-start | bytes 11796484
  63.4 7.1 %copy-start.19 = (f16[4,2,96,1280]{3,2,1,0:T(8,128)(2,1)}, f16[4,2,96,1280]{3,2,1,0:T(8,128)(2,1)S(1)}, u32[]{:S(2)}) copy-start(f16[4,2,96,1280]{3,2,1,0:T(8,128)(2,1)S(1)} %collective-permute-done.6) | copy-start | bytes 5898244
  65.7 14.3 %collective-permute-start.11 = (f16[2,96,1280]{2,1,0:T(8,128)(2,1)S(1)}, f16[2,96,1280]{2,1,0:T(8,128)(2,1)S(1)}, u32[]{:S(2)}, u32[]{:S(2)}) collective-permute-start(f16[2,96,1280]{2,1,0:T(8,128)(2,1)S(1)} %get-tuple-element.175), channel_id=1, source_target_pairs={{0,4},{2,6},{12,8},{14,10},{4,0},{6,2},{8,12},{10,14},{1,5},{3,7},... | collective-permute-start | bytes 1474568 | tf_op jit(solution)/shard_map/ppermute | solution.py:180
  67.0 13.0 %collective-permute-start.12 = (f16[2,96,1280]{2,1,0:T(8,128)(2,1)S(1)}, f16[2,96,1280]{2,1,0:T(8,128)(2,1)S(1)}, u32[]{:S(2)}, u32[]{:S(2)}) collective-permute-start(f16[2,96,1280]{2,1,0:T(8,128)(2,1)S(1)} %get-tuple-element.176), channel_id=1, source_target_pairs={{4,8},{6,10},{8,4},{10,6},{5,9},{7,11},{9,5},{11,7},{20,24},{22,26... | collective-permute-start | bytes 1474568 | tf_op jit(solution)/shard_map/ppermute | solution.py:180
  67.8 11.1 %collective-permute-start.9 = (bf16[2,48,1792]{2,1,0:T(8,128)(2,1)S(1)}, bf16[2,48,1792]{2,1,0:T(8,128)(2,1)S(1)}, u32[]{:S(2)}, u32[]{:S(2)}) collective-permute-start(bf16[2,48,1792]{2,1,0:T(8,128)(2,1)S(1)} %get-tuple-element.196), channel_id=1, source_target_pairs={{0,2},{2,0},{4,6},{6,4},{8,10},{10,8},{12,14},{14,12},{1,3},{3,1},... | collective-permute-start | bytes 1032200 | tf_op jit(solution)/shard_map/ppermute | solution.py:180
  71.3 20.4 %collective-permute-start.16 = (f16[2,96,1280]{2,1,0:T(8,128)(2,1)}, f16[2,96,1280]{2,1,0:T(8,128)(2,1)}, u32[]{:S(2)}, u32[]{:S(2)}) collective-permute-start(f16[2,96,1280]{2,1,0:T(8,128)(2,1)} %fusion.31), channel_id=1, source_target_pairs={{0,4},{2,6},{12,8},{14,10},{1,5},{3,7},{13,9},{15,11},{16,20},{18,... | collective-permute-start | bytes 1474568 | tf_op jit(solution)/shard_map/ppermute | solution.py:180
  78.3 6.7 %collective-permute-start.13 = (bf16[2,1024,512]{2,1,0:T(8,128)(2,1)S(1)}, bf16[2,1024,512]{2,1,0:T(8,128)(2,1)S(1)}, u32[]{:S(2)}, u32[]{:S(2)}) collective-permute-start(bf16[2,1024,512]{2,1,0:T(8,128)(2,1)S(1)} %pad_maximum_fusion), channel_id=1, source_target_pairs={{0,2},{2,0},{4,6},{6,4},{8,10},{10,8},{12,14},{14,12},{1,3},{3,1},... | collective-permute-start | bytes 6291464 | tf_op jit(solution)/shard_map/ppermute | solution.py:180
  78.8 5.9 %collective-permute-start.10 = (bf16[4,2,96,1024]{3,2,0,1:T(8,128)(2,1)S(1)}, bf16[4,2,96,1024]{3,2,0,1:T(8,128)(2,1)S(1)}, u32[]{:S(2)}, u32[]{:S(2)}) collective-permute-start(bf16[4,2,96,1024]{3,2,0,1:T(8,128)(2,1)S(1)} %pad_maximum_fusion.1), channel_id=1, source_target_pairs={{0,2},{2,0},{4,6},{6,4},{8,10},{10,8},{12,14},{14,12},{1,3},{3,1},... | collective-permute-start | bytes 4718600 | tf_op jit(solution)/shard_map/ppermute | solution.py:180
  81.8 15.7 %collective-permute-start.15 = (bf16[2,96,1280]{2,1,0:T(8,128)(2,1)S(1)}, bf16[2,96,1280]{2,1,0:T(8,128)(2,1)S(1)}, u32[]{:S(2)}, u32[]{:S(2)}) collective-permute-start(bf16[2,96,1280]{2,1,0:T(8,128)(2,1)S(1)} %pad_maximum_fusion.2.act), channel_id=1, source_target_pairs={{4,8},{6,10},{8,4},{10,6},{5,9},{7,11},{9,5},{11,7},{20,24},{22,26... | collective-permute-start | bytes 1474568 | tf_op jit(solution)/shard_map/ppermute | solution.py:180
  82.5 15.0 %collective-permute-start.14 = (bf16[2,96,1280]{2,1,0:T(8,128)(2,1)S(1)}, bf16[2,96,1280]{2,1,0:T(8,128)(2,1)S(1)}, u32[]{:S(2)}, u32[]{:S(2)}) collective-permute-start(bf16[2,96,1280]{2,1,0:T(8,128)(2,1)S(1)} %pad_maximum_fusion.2.act), channel_id=1, source_target_pairs={{0,4},{2,6},{12,8},{14,10},{4,0},{6,2},{8,12},{10,14},{1,5},{3,7},... | collective-permute-start | bytes 1474568 | tf_op jit(solution)/shard_map/ppermute | solution.py:180
  85.0 6.7 %copy-start.20 = (f16[4,2,96,1280]{3,2,1,0:T(8,128)(2,1)S(1)}, f16[4,2,96,1280]{3,2,1,0:T(8,128)(2,1)}, u32[]{:S(2)}) copy-start(f16[4,2,96,1280]{3,2,1,0:T(8,128)(2,1)} %copy-done.19) | copy-start | bytes 5898244
  93.0 6.6 %collective-permute-start.20 = (f16[2,96,1280]{2,1,0:T(8,128)(2,1)S(1)}, f16[2,96,1280]{2,1,0:T(8,128)(2,1)S(1)}, u32[]{:S(2)}, u32[]{:S(2)}) collective-permute-start(f16[2,96,1280]{2,1,0:T(8,128)(2,1)S(1)} %fusion.6), channel_id=1, source_target_pairs={{4,8},{6,10},{8,4},{10,6},{5,9},{7,11},{9,5},{11,7},{20,24},{22,26... | collective-permute-start | bytes 1474568 | tf_op jit(solution)/shard_map/ppermute | solution.py:180
  93.8 13.6 %collective-permute-start.19 = (f16[2,96,1280]{2,1,0:T(8,128)(2,1)S(1)}, f16[2,96,1280]{2,1,0:T(8,128)(2,1)S(1)}, u32[]{:S(2)}, u32[]{:S(2)}) collective-permute-start(f16[2,96,1280]{2,1,0:T(8,128)(2,1)S(1)} %fusion.32), channel_id=1, source_target_pairs={{0,4},{2,6},{12,8},{14,10},{1,5},{3,7},{13,9},{15,11},{16,20},{18,... | collective-permute-start | bytes 1474568 | tf_op jit(solution)/shard_map/ppermute | solution.py:180
  97.5 11.2 %copy-start.8 = (bf16[2,96,1280]{2,1,0:T(8,128)(2,1)}, bf16[2,96,1280]{2,1,0:T(8,128)(2,1)S(1)}, u32[]{:S(2)}) copy-start(bf16[2,96,1280]{2,1,0:T(8,128)(2,1)S(1)} %collective-permute-done.15.centre_1) | copy-start | bytes 1474564
  97.6 11.2 %copy-start.10 = (bf16[2,96,1280]{2,1,0:T(8,128)(2,1)}, bf16[2,96,1280]{2,1,0:T(8,128)(2,1)S(1)}, u32[]{:S(2)}) copy-start(bf16[2,96,1280]{2,1,0:T(8,128)(2,1)S(1)} %collective-permute-done.14.side_1) | copy-start | bytes 1474564
  97.6 14.9 %collective-permute-start.18 = (bf16[2,96,1280]{2,1,0:T(8,128)(2,1)S(1)}, bf16[2,96,1280]{2,1,0:T(8,128)(2,1)S(1)}, u32[]{:S(2)}, u32[]{:S(2)}) collective-permute-start(bf16[2,96,1280]{2,1,0:T(8,128)(2,1)S(1)} %collective-permute-done.14.side_1), channel_id=1, source_target_pairs={{4,8},{6,10},{8,4},{10,6},{5,9},{7,11},{9,5},{11,7},{20,24},{22,26... | collective-permute-start | bytes 1474568 | tf_op jit(solution)/shard_map/ppermute | solution.py:180
  98.3 15.1 %collective-permute-start.17 = (bf16[2,96,1280]{2,1,0:T(8,128)(2,1)S(1)}, bf16[2,96,1280]{2,1,0:T(8,128)(2,1)S(1)}, u32[]{:S(2)}, u32[]{:S(2)}) collective-permute-start(bf16[2,96,1280]{2,1,0:T(8,128)(2,1)S(1)} %collective-permute-done.15.centre_1), channel_id=1, source_target_pairs={{4,0},{6,2},{8,12},{10,14},{5,1},{7,3},{9,13},{11,15},{20,16},{22,... | collective-permute-start | bytes 1474568 | tf_op jit(solution)/shard_map/ppermute | solution.py:180
  108.8 15.3 %collective-permute-start.22 = (f16[2,96,1280]{2,1,0:T(8,128)(2,1)}, f16[2,96,1280]{2,1,0:T(8,128)(2,1)}, u32[]{:S(2)}, u32[]{:S(2)}) collective-permute-start(f16[2,96,1280]{2,1,0:T(8,128)(2,1)} %get-tuple-element.173), channel_id=1, source_target_pairs={{0,4},{2,6},{12,8},{14,10},{4,0},{6,2},{8,12},{10,14},{1,5},{3,7},... | collective-permute-start | bytes 1474568 | tf_op jit(solution)/shard_map/ppermute | solution.py:180
  111.0 13.1 %collective-permute-start.23 = (f16[2,96,1280]{2,1,0:T(8,128)(2,1)}, f16[2,96,1280]{2,1,0:T(8,128)(2,1)}, u32[]{:S(2)}, u32[]{:S(2)}) collective-permute-start(f16[2,96,1280]{2,1,0:T(8,128)(2,1)} %get-tuple-element.174), channel_id=1, source_target_pairs={{4,8},{6,10},{8,4},{10,6},{5,9},{7,11},{9,5},{11,7},{20,24},{22,26... | collective-permute-start | bytes 1474568 | tf_op jit(solution)/shard_map/ppermute | solution.py:180
  112.4 6.2 %copy-start.12 = (bf16[2,96,1280]{2,1,0:T(8,128)(2,1)}, bf16[2,96,1280]{2,1,0:T(8,128)(2,1)S(1)}, u32[]{:S(2)}) copy-start(bf16[2,96,1280]{2,1,0:T(8,128)(2,1)S(1)} %collective-permute-done.18.share_2) | copy-start | bytes 1474564
  113.4 5.3 %copy-start.14 = (bf16[2,96,1280]{2,1,0:T(8,128)(2,1)}, bf16[2,96,1280]{2,1,0:T(8,128)(2,1)S(1)}, u32[]{:S(2)}) copy-start(bf16[2,96,1280]{2,1,0:T(8,128)(2,1)S(1)} %collective-permute-done.17.out_2) | copy-start | bytes 1474564
  113.4 21.1 %collective-permute-start.21 = (bf16[2,96,1280]{2,1,0:T(8,128)(2,1)S(1)}, bf16[2,96,1280]{2,1,0:T(8,128)(2,1)S(1)}, u32[]{:S(2)}, u32[]{:S(2)}) collective-permute-start(bf16[2,96,1280]{2,1,0:T(8,128)(2,1)S(1)} %collective-permute-done.18.share_2), channel_id=1, source_target_pairs={{4,0},{6,2},{8,12},{10,14},{5,1},{7,3},{9,13},{11,15},{20,16},{22,... | collective-permute-start | bytes 1474568 | tf_op jit(solution)/shard_map/ppermute | solution.py:180
  117.0 7.1 %copy-start.1 = (f32[4,2,96,1280]{3,2,1,0:T(8,128)S(1)}, f32[4,2,96,1280]{3,2,1,0:T(8,128)}, u32[]{:S(2)}) copy-start(f32[4,2,96,1280]{3,2,1,0:T(8,128)} %copy-done) | copy-start | bytes 11796484
  119.9 6.2 %copy-start.22 = (bf16[96,1792]{1,0:T(8,128)(2,1)S(1)}, bf16[96,1792]{1,0:T(8,128)(2,1)}, u32[]{:S(2)}) copy-start(bf16[96,1792]{1,0:T(8,128)(2,1)} %get-tuple-element.194) | copy-start | bytes 1032196
  119.9 16.7 %collective-permute-start.26 = (f16[2,192,512]{2,1,0:T(8,128)(2,1)S(1)}, f16[2,192,512]{2,1,0:T(8,128)(2,1)S(1)}, u32[]{:S(2)}, u32[]{:S(2)}) collective-permute-start(f16[2,192,512]{2,1,0:T(8,128)(2,1)S(1)} %fusion.39), channel_id=1, source_target_pairs={{0,4},{2,6},{12,8},{14,10},{1,5},{3,7},{13,9},{15,11},{16,20},{18,... | collective-permute-start | bytes 1179656 | tf_op jit(solution)/shard_map/ppermute | solution.py:180
  126.0 9.2 %copy-start.7 = (bf16[2,96,1280]{2,1,0:T(8,128)(2,1)S(1)}, bf16[2,96,1280]{2,1,0:T(8,128)(2,1)}, u32[]{:S(2)}) copy-start(bf16[2,96,1280]{2,1,0:T(8,128)(2,1)} %copy-done.6) | copy-start | bytes 1474564
  126.0 9.2 %copy-start.9 = (bf16[2,96,1280]{2,1,0:T(8,128)(2,1)S(1)}, bf16[2,96,1280]{2,1,0:T(8,128)(2,1)}, u32[]{:S(2)}) copy-start(bf16[2,96,1280]{2,1,0:T(8,128)(2,1)} %copy-done.8) | copy-start | bytes 1474564
  126.0 9.2 %copy-start.11 = (bf16[2,96,1280]{2,1,0:T(8,128)(2,1)S(1)}, bf16[2,96,1280]{2,1,0:T(8,128)(2,1)}, u32[]{:S(2)}) copy-start(bf16[2,96,1280]{2,1,0:T(8,128)(2,1)} %copy-done.10) | copy-start | bytes 1474564
  126.1 9.2 %copy-start.13 = (bf16[2,96,1280]{2,1,0:T(8,128)(2,1)S(1)}, bf16[2,96,1280]{2,1,0:T(8,128)(2,1)}, u32[]{:S(2)}) copy-start(bf16[2,96,1280]{2,1,0:T(8,128)(2,1)} %copy-done.12) | copy-start | bytes 1474564
  126.1 9.2 %copy-start.15 = (bf16[2,96,1280]{2,1,0:T(8,128)(2,1)S(1)}, bf16[2,96,1280]{2,1,0:T(8,128)(2,1)}, u32[]{:S(2)}) copy-start(bf16[2,96,1280]{2,1,0:T(8,128)(2,1)} %copy-done.14) | copy-start | bytes 1474564
  127.1 9.5 %copy-start.4 = (bf16[2,96,1280]{2,1,0:T(8,128)(2,1)}, bf16[2,96,1280]{2,1,0:T(8,128)(2,1)S(1)}, u32[]{:S(2)}) copy-start(bf16[2,96,1280]{2,1,0:T(8,128)(2,1)S(1)} %pad_maximum_fusion.3.act) | copy-start | bytes 1474564
  127.1 14.4 %collective-permute-start.25 = (bf16[2,96,1280]{2,1,0:T(8,128)(2,1)S(1)}, bf16[2,96,1280]{2,1,0:T(8,128)(2,1)}, u32[]{:S(2)}, u32[]{:S(2)}) collective-permute-start(bf16[2,96,1280]{2,1,0:T(8,128)(2,1)S(1)} %pad_maximum_fusion.3.act), channel_id=1, source_target_pairs={{4,8},{6,10},{8,4},{10,6},{5,9},{7,11},{9,5},{11,7},{20,24},{22,26... | collective-permute-start | bytes 1474568 | tf_op jit(solution)/shard_map/ppermute | solution.py:180
  128.6 16.5 %collective-permute-start.24 = (bf16[2,96,1280]{2,1,0:T(8,128)(2,1)S(1)}, bf16[2,96,1280]{2,1,0:T(8,128)(2,1)}, u32[]{:S(2)}, u32[]{:S(2)}) collective-permute-start(bf16[2,96,1280]{2,1,0:T(8,128)(2,1)S(1)} %pad_maximum_fusion.3.act), channel_id=1, source_target_pairs={{0,4},{2,6},{12,8},{14,10},{4,0},{6,2},{8,12},{10,14},{1,5},{3,7},... | collective-permute-start | bytes 1474568 | tf_op jit(solution)/shard_map/ppermute | solution.py:180
  138.3 9.5 %collective-permute-start.30 = (f16[2,192,512]{2,1,0:T(8,128)(2,1)S(1)}, f16[2,192,512]{2,1,0:T(8,128)(2,1)S(1)}, u32[]{:S(2)}, u32[]{:S(2)}) collective-permute-start(f16[2,192,512]{2,1,0:T(8,128)(2,1)S(1)} %fusion.19), channel_id=1, source_target_pairs={{4,8},{6,10},{8,4},{10,6},{5,9},{7,11},{9,5},{11,7},{20,24},{22,26... | collective-permute-start | bytes 1179656 | tf_op jit(solution)/shard_map/ppermute | solution.py:180
  139.0 11.3 %collective-permute-start.29 = (f16[2,192,512]{2,1,0:T(8,128)(2,1)S(1)}, f16[2,192,512]{2,1,0:T(8,128)(2,1)S(1)}, u32[]{:S(2)}, u32[]{:S(2)}) collective-permute-start(f16[2,192,512]{2,1,0:T(8,128)(2,1)S(1)} %fusion.40), channel_id=1, source_target_pairs={{0,4},{2,6},{12,8},{14,10},{1,5},{3,7},{13,9},{15,11},{16,20},{18,... | collective-permute-start | bytes 1179656 | tf_op jit(solution)/shard_map/ppermute | solution.py:180
  145.1 11.1 %collective-permute-start.28 = (bf16[2,96,1280]{2,1,0:T(8,128)(2,1)}, bf16[2,96,1280]{2,1,0:T(8,128)(2,1)}, u32[]{:S(2)}, u32[]{:S(2)}) collective-permute-start(bf16[2,96,1280]{2,1,0:T(8,128)(2,1)} %collective-permute-done.24.side_1), channel_id=1, source_target_pairs={{4,8},{6,10},{8,4},{10,6},{5,9},{7,11},{9,5},{11,7},{20,24},{22,26... | collective-permute-start | bytes 1474568 | tf_op jit(solution)/shard_map/ppermute | solution.py:180
  146.5 9.9 %collective-permute-start.27 = (bf16[2,96,1280]{2,1,0:T(8,128)(2,1)}, bf16[2,96,1280]{2,1,0:T(8,128)(2,1)}, u32[]{:S(2)}, u32[]{:S(2)}) collective-permute-start(bf16[2,96,1280]{2,1,0:T(8,128)(2,1)} %collective-permute-done.25.centre_1), channel_id=1, source_target_pairs={{4,0},{6,2},{8,12},{10,14},{5,1},{7,3},{9,13},{11,15},{20,16},{22,... | collective-permute-start | bytes 1474568 | tf_op jit(solution)/shard_map/ppermute | solution.py:180
  151.6 12.3 %collective-permute-start.31 = (f16[2,192,512]{2,1,0:T(8,128)(2,1)}, f16[2,192,512]{2,1,0:T(8,128)(2,1)}, u32[]{:S(2)}, u32[]{:S(2)}) collective-permute-start(f16[2,192,512]{2,1,0:T(8,128)(2,1)} %get-tuple-element.177), channel_id=1, source_target_pairs={{0,4},{2,6},{12,8},{14,10},{4,0},{6,2},{8,12},{10,14},{1,5},{3,7},... | collective-permute-start | bytes 1179656 | tf_op jit(solution)/shard_map/ppermute | solution.py:180
  153.8 10.1 %collective-permute-start.32 = (f16[2,192,512]{2,1,0:T(8,128)(2,1)}, f16[2,192,512]{2,1,0:T(8,128)(2,1)}, u32[]{:S(2)}, u32[]{:S(2)}) collective-permute-start(f16[2,192,512]{2,1,0:T(8,128)(2,1)} %get-tuple-element.178), channel_id=1, source_target_pairs={{4,8},{6,10},{8,4},{10,6},{5,9},{7,11},{9,5},{11,7},{20,24},{22,26... | collective-permute-start | bytes 1179656 | tf_op jit(solution)/shard_map/ppermute | solution.py:180
  156.4 26.3 %collective-permute-start.36 = (bf16[2,96,1280]{2,1,0:T(8,128)(2,1)}, bf16[2,96,1280]{2,1,0:T(8,128)(2,1)}, u32[]{:S(2)}, u32[]{:S(2)}) collective-permute-start(bf16[2,96,1280]{2,1,0:T(8,128)(2,1)} %collective-permute-done.28.share_2), channel_id=1, source_target_pairs={{4,0},{6,2},{8,12},{10,14},{5,1},{7,3},{9,13},{11,15},{20,16},{22,... | collective-permute-start | bytes 1474568 | tf_op jit(solution)/shard_map/ppermute | solution.py:180
  165.8 8.6 %copy-start.24 = (bf16[1,96,1280]{2,1,0:T(8,128)(2,1)S(1)}, bf16[1,96,1280]{2,1,0:T(8,128)(2,1)}, u32[]{:S(2)}) copy-start(bf16[1,96,1280]{2,1,0:T(8,128)(2,1)} %get-tuple-element.183) | copy-start | bytes 737284
  165.8 8.6 %copy-start.25 = (bf16[1,96,1280]{2,1,0:T(8,128)(2,1)S(1)}, bf16[1,96,1280]{2,1,0:T(8,128)(2,1)}, u32[]{:S(2)}) copy-start(bf16[1,96,1280]{2,1,0:T(8,128)(2,1)} %get-tuple-element.184) | copy-start | bytes 737284
  166.8 21.8 %collective-permute-start.34 = (bf16[2,192,512]{2,1,0:T(8,128)(2,1)}, bf16[2,192,512]{2,1,0:T(8,128)(2,1)}, u32[]{:S(2)}, u32[]{:S(2)}) collective-permute-start(bf16[2,192,512]{2,1,0:T(8,128)(2,1)} %pad_maximum_fusion.4.act), channel_id=1, source_target_pairs={{4,8},{6,10},{8,4},{10,6},{5,9},{7,11},{9,5},{11,7},{20,24},{22,26... | collective-permute-start | bytes 1179656 | tf_op jit(solution)/shard_map/ppermute | solution.py:180
  168.3 20.4 %collective-permute-start.33 = (bf16[2,192,512]{2,1,0:T(8,128)(2,1)}, bf16[2,192,512]{2,1,0:T(8,128)(2,1)}, u32[]{:S(2)}, u32[]{:S(2)}) collective-permute-start(bf16[2,192,512]{2,1,0:T(8,128)(2,1)} %pad_maximum_fusion.4.act), channel_id=1, source_target_pairs={{0,4},{2,6},{12,8},{14,10},{4,0},{6,2},{8,12},{10,14},{1,5},{3,7},... | collective-permute-start | bytes 1179656 | tf_op jit(solution)/shard_map/ppermute | solution.py:180
  175.3 9.4 %collective-permute-start.35 = (bf16[2,48,1792]{2,1,0:T(8,128)(2,1)}, bf16[2,48,1792]{2,1,0:T(8,128)(2,1)}, u32[]{:S(2)}, u32[]{:S(2)}) collective-permute-start(bf16[2,48,1792]{2,1,0:T(8,128)(2,1)} %get-tuple-element.192), channel_id=1, source_target_pairs={{0,2},{2,0},{4,6},{6,4},{8,10},{10,8},{12,14},{14,12},{1,3},{3,1},... | collective-permute-start | bytes 1032200 | tf_op jit(solution)/shard_map/ppermute | solution.py:180
  182.7 20.1 %collective-permute-start.40 = (bf16[4,2,96,1280]{3,2,1,0:T(8,128)(2,1)S(1)}, bf16[4,2,96,1280]{3,2,1,0:T(8,128)(2,1)S(1)}, u32[]{:S(2)}, u32[]{:S(2)}) collective-permute-start(bf16[4,2,96,1280]{3,2,1,0:T(8,128)(2,1)S(1)} %shard_map.72), channel_id=1, source_target_pairs={{0,2},{2,0},{4,6},{6,4},{8,10},{10,8},{12,14},{14,12},{1,3},{3,1},... | collective-permute-start | bytes 5898248 | tf_op jit(solution)/shard_map/ppermute | solution.py:180
  185.8 4.8 %copy-start.23 = (bf16[2,48,1792]{2,1,0:T(8,128)(2,1)S(1)}, bf16[2,48,1792]{2,1,0:T(8,128)(2,1)}, u32[]{:S(2)}) copy-start(bf16[2,48,1792]{2,1,0:T(8,128)(2,1)} %get-tuple-element.159) | copy-start | bytes 1032196
  187.8 15.0 %collective-permute-start.41 = (bf16[4,2,96,1280]{3,2,1,0:T(8,128)(2,1)S(1)}, bf16[4,2,96,1280]{3,2,1,0:T(8,128)(2,1)S(1)}, u32[]{:S(2)}, u32[]{:S(2)}) collective-permute-start(bf16[4,2,96,1280]{3,2,1,0:T(8,128)(2,1)S(1)} %shard_map.73), channel_id=1, source_target_pairs={{0,2},{2,0},{4,6},{6,4},{8,10},{10,8},{12,14},{14,12},{1,3},{3,1},... | collective-permute-start | bytes 5898248 | tf_op jit(solution)/shard_map/ppermute | solution.py:180
  188.6 11.6 %collective-permute-start.37 = (bf16[2,192,512]{2,1,0:T(8,128)(2,1)}, bf16[2,192,512]{2,1,0:T(8,128)(2,1)S(1)}, u32[]{:S(2)}, u32[]{:S(2)}) collective-permute-start(bf16[2,192,512]{2,1,0:T(8,128)(2,1)} %collective-permute-done.34.centre_1), channel_id=1, source_target_pairs={{4,0},{6,2},{8,12},{10,14},{5,1},{7,3},{9,13},{11,15},{20,16},{22,... | collective-permute-start | bytes 1179656 | tf_op jit(solution)/shard_map/ppermute | solution.py:180
  189.9 10.3 %collective-permute-start.38 = (bf16[2,192,512]{2,1,0:T(8,128)(2,1)}, bf16[2,192,512]{2,1,0:T(8,128)(2,1)S(1)}, u32[]{:S(2)}, u32[]{:S(2)}) collective-permute-start(bf16[2,192,512]{2,1,0:T(8,128)(2,1)} %collective-permute-done.33.side_1), channel_id=1, source_target_pairs={{4,8},{6,10},{8,4},{10,6},{5,9},{7,11},{9,5},{11,7},{20,24},{22,26... | collective-permute-start | bytes 1179656 | tf_op jit(solution)/shard_map/ppermute | solution.py:180
  191.9 9.9 %collective-permute-start.42 = (bf16[48,3584]{1,0:T(8,128)(2,1)S(1)}, bf16[48,3584]{1,0:T(8,128)(2,1)S(1)}, u32[]{:S(2)}, u32[]{:S(2)}) collective-permute-start(bf16[48,3584]{1,0:T(8,128)(2,1)S(1)} %get-tuple-element.190), channel_id=1, source_target_pairs={{0,1},{1,0},{2,3},{3,2},{4,5},{5,4},{6,7},{7,6},{8,9},{9,8},{10,11... | collective-permute-start | bytes 1032200 | tf_op jit(solution)/shard_map/ppermute | solution.py:322
  200.2 12.8 %collective-permute-start.39 = (bf16[2,192,512]{2,1,0:T(8,128)(2,1)S(1)}, bf16[2,192,512]{2,1,0:T(8,128)(2,1)S(1)}, u32[]{:S(2)}, u32[]{:S(2)}) collective-permute-start(bf16[2,192,512]{2,1,0:T(8,128)(2,1)S(1)} %collective-permute-done.38.share_2), channel_id=1, source_target_pairs={{4,0},{6,2},{8,12},{10,14},{5,1},{7,3},{9,13},{11,15},{20,16},{22,... | collective-permute-start | bytes 1179656 | tf_op jit(solution)/shard_map/ppermute | solution.py:180
  214.6 6.1 %collective-permute-start.43 = (bf16[4,2,192,512]{3,2,1,0:T(8,128)(2,1)S(1)}, bf16[4,2,192,512]{3,2,1,0:T(8,128)(2,1)S(1)}, u32[]{:S(2)}, u32[]{:S(2)}) collective-permute-start(bf16[4,2,192,512]{3,2,1,0:T(8,128)(2,1)S(1)} %shard_map.76), channel_id=1, source_target_pairs={{0,2},{2,0},{4,6},{6,4},{8,10},{10,8},{12,14},{14,12},{1,3},{3,1},... | collective-permute-start | bytes 4718600 | tf_op jit(solution)/shard_map/ppermute | solution.py:180
  (7 other events, 10.6 us)

commit v17 on v15

--- a/solution.py
+++ b/solution.py
@@ -10,7 +10,7 @@
 
 WIRE = jnp.float16
 LARGEST_TOKEN, LARGEST_WEIGHT = 6.0, 0.0625
-VMEM_LIMIT = 48 * 2**20
+VMEM_LIMIT = 20 * 2**20
 NO_COST = pl.CostEstimate(flops=0, bytes_accessed=0, transcendentals=0)
 LONG = pl.CostEstimate(flops=6 * 10**9, bytes_accessed=0, transcendentals=0)
 SHARES = (5, 2)
@@ -245,7 +245,7 @@
     over_row = tie(over_row, over_depth)
     features = [arrange(by(row == 0, mine, over_row, 1))]
     theirs, own = own_features(features[0], 0, (), WIRE)
-    terms = (own(()), send(theirs, pairs))
+    terms = (own((), LONG), send(theirs, pairs))
     payload = take(terms, 3).astype(WIRE)
     in_1 = send(payload, inward)
 
@@ -290,8 +290,8 @@
             if k == 0:
                 products[2] = all_features(tokens, 2, act)
                 terms = tie(terms, products[2])
-            far, near = add(take(terms, 3), in_1).astype(WIRE), take(tie(terms, in_1), 2)
-            near = near.astype(WIRE)
+            near = take(tie(terms, in_1) if gathering else terms, 2).astype(WIRE)
+            far = add(take(tie(terms, near), 3), in_1).astype(WIRE)
             centre_2, in_2 = send(far, centre), send(near, inward)
             before = (in_1,)
         else:

time: 224 us -> 237 us (1.058)
  local copies, waits for them, and re-layouts: 15.4 us -> 33.8 us
  waiting for transfers between devices: 45.9 us -> 39.4 us
  starting transfers between devices: 83.6 us -> 89.3 us
  other arithmetic: 29 us -> 26.1 us
    unnamed x54 -> x66, local copies, waits for them, and re-layouts: 7.61 us -> 24.8 us
    ppermute x1, waiting for transfers between devices: 4.13 us -> 0.01 us  [local(): over_both = lax.ppermute(over_row, 'depth', swap)]
    ppermute x39, starting transfers between devices: 79.5 us -> 83.5 us  [send(): return lax.ppermute(value, 'col', route)]
    pallas_call x5, Pallas kernels: 23.3 us -> 19.7 us  [forward(): pl.pallas_call(functools.partial(forward_kernel, scale, start, cores), ou...]
    convert_element_type x2, other arithmetic: 1.73 us -> 5.26 us  [own_features(): payload = forward(other_tile, [tokens], *common).astype(wire)]
    convert_element_type x6, other arithmetic: 4.38 us -> 0.88 us  [the longest x3 0.59 us: local(): far = add(take(tie(terms, near), 3), in_1).astype(WIRE)]
    ppermute x39, waiting for transfers between devices: 29.1 us -> 25.7 us  [send(): return lax.ppermute(value, 'col', route)]
  transfers between devices with their start and end apart: 44 -> 44, of which waited for: 14 -> 12; matrix products, arithmetic and copies ran while one was open for 14% -> 13% of each run, Pallas kernels for 17% -> 16%
where the time goes in v17:
time: 237 us; the launch traced here: 236 us
  starting transfers between devices  89.3 us (38%)
  Pallas kernels  45.7 us (19%)
  waiting for transfers between devices  39.4 us (17%)
  local copies, waits for them, and re-layouts  33.8 us (14%)
  other arithmetic  26.1 us (11%)
    ppermute x39, starting transfers between devices, send(): return lax.ppermute(value, 'col', route)  83.5 us
    ppermute x39, waiting for transfers between devices, send(): return lax.ppermute(value, 'col', route)  25.7 us
    unnamed x66, local copies, waits for them, and re-layouts  24.8 us
    pallas_call x4, Pallas kernels, gradient(): pl.pallas_call(functools.partial(gradient_kernel, len(acts)), out_shape=(...  20.9 us
    pallas_call x5, Pallas kernels, forward(): pl.pallas_call(functools.partial(forward_kernel, scale, start, cores), ou...  19.7 us
    ppermute x1, waiting for transfers between devices, local(): over_depth = lax.ppermute(mine, 'depth', swap)  7.94 us
    convert_element_type x2, other arithmetic, own_features(): payload = forward(other_tile, [tokens], *common).astype(wire)  5.26 us
    pallas_call x3, Pallas kernels, gather_blocks(): pl.pallas_call(gather_kernel, out_shape=jax.ShapeDtypeStruct((4, 2, rows,...  5.05 us
  transfers between devices with their start and end apart: 44, of which 12 were waited for; matrix products, arithmetic and copies ran while one was open for 13% of the time, Pallas kernels for 16%

profile of v17, /device:TPU:1, one launch (start us, length us, event | category | flops | bytes accessed | tf_op | source)
XLA Modules:
  0.0 235.8 jit_solution(4031878704749448738)
XLA Ops:
  0.6 2.1 collective-permute-start.1
  4.0 7.9 %collective-permute-done.1 = bf16[384,512]{1,0:T(8,128)(2,1)S(1)} collective-permute-done((bf16[384,512]{1,0:T(8,128)(2,1)}, bf16[384,512]{1,0:T(8,128)(2,1)S(1)}, u32[]{:S(2)}, u32[]{:S(2)}) %collective-permute-start.1) | collective-permute-done | bytes 393248 | tf_op jit(solution)/shard_map/ppermute | solution.py:213
  12.7 1.6 maximum_select_fusion
  14.6 5.4 %copy-done = bf16[1024,7168]{1,0:T(8,128)(2,1)S(1)} copy-done((bf16[1024,7168]{1,0:T(8,128)(2,1)S(1)}, bf16[1024,7168]{1,0:T(8,128)(2,1)}, u32[]{:S(2)}) %copy-start) | copy-done | bytes 14680088
  20.1 5.2 %copy-done.2 = bf16[1024,7168]{1,0:T(8,128)(2,1)S(1)} copy-done((bf16[1024,7168]{1,0:T(8,128)(2,1)S(1)}, bf16[1024,7168]{1,0:T(8,128)(2,1)}, u32[]{:S(2)}) %copy-start.2) | copy-done | bytes 14680088
  25.2 3.7 %shard_map.67 = f32[4,2,96,1280]{3,2,1,0:T(8,128)S(1)} custom-call(s32[1]{0:T(128)} %bitcast.6.place_ref, bf16[384,1024]{1,0:T(8,128)(2,1)S(1)} %bitcast.156, bf16[1024,7168]{1,0:T(8,128)(2,1)S(1)} %copy-done, bf16[1024,7168]{1,0:T(8,128)(2,1)S(1)} %copy-done.2), custom_call_target="tpu_custom_call" | custom-call | tf_op jit(solution)/shard_map/pallas_call | solution.py:56
  28.9 1.5 convert_element_type.194
  30.4 1.9 collective-permute-start.2
  32.9 5.2 %copy-done.1 = bf16[1024,7168]{1,0:T(8,128)(2,1)S(1)} copy-done((bf16[1024,7168]{1,0:T(8,128)(2,1)S(1)}, bf16[1024,7168]{1,0:T(8,128)(2,1)}, u32[]{:S(2)}) %copy-start.1) | copy-done | bytes 14680088
  38.1 5.2 %copy-done.3 = bf16[1024,7168]{1,0:T(8,128)(2,1)S(1)} copy-done((bf16[1024,7168]{1,0:T(8,128)(2,1)S(1)}, bf16[1024,7168]{1,0:T(8,128)(2,1)}, u32[]{:S(2)}) %copy-start.3) | copy-done | bytes 14680088
  43.3 3.7 %shard_map.68 = f32[4,2,96,1280]{3,2,1,0:T(8,128)S(1)} custom-call(s32[1]{0:T(128)} %bitcast.1.place_ref, bf16[384,1024]{1,0:T(8,128)(2,1)S(1)} %bitcast.157, bf16[1024,7168]{1,0:T(8,128)(2,1)S(1)} %copy-done.1, bf16[1024,7168]{1,0:T(8,128)(2,1)S(1)} %copy-done.3), custom_call_target="tpu_custom_call" | custom-call | flops 6000000000 | tf_op jit(solution)/shard_map/pallas_call | solution.py:56
  47.9 3.2 %collective-permute-start.4 = (f16[2,96,1280]{2,1,0:T(8,128)(2,1)}, f16[2,96,1280]{2,1,0:T(8,128)(2,1)S(1)}, u32[]{:S(2)}, u32[]{:S(2)}) collective-permute-start(f16[2,96,1280]{2,1,0:T(8,128)(2,1)} %fusion.33), channel_id=1, source_target_pairs={{0,4},{2,6},{12,8},{14,10},{1,5},{3,7},{13,9},{15,11},{16,20},{18,... | collective-permute-start | bytes 1474568 | tf_op jit(solution)/shard_map/ppermute | solution.py:179
  51.7 3.7 %shard_map.69 = f32[4,2,96,1280]{3,2,1,0:T(8,128)S(1)} custom-call(s32[1]{0:T(128)} %bitcast.6.place_ref, bf16[384,1024]{1,0:T(8,128)(2,1)S(1)} %bitcast.160, bf16[1024,7168]{1,0:T(8,128)(2,1)S(1)} %copy-done.1, bf16[1024,7168]{1,0:T(8,128)(2,1)S(1)} %copy-done.3), custom_call_target="tpu_custom_call" | custom-call | tf_op jit(solution)/shard_map/pallas_call | solution.py:56
  55.4 1.9 copy-done.9
  57.3 3.8 %convert_element_type.198 = f16[4,2,96,1280]{3,2,1,0:T(8,128)(2,1)} convert(f32[4,2,96,1280]{3,2,1,0:T(8,128)} %copy-done.9) | non-fusion elementwise | flops 983040 | bytes 5898240 | tf_op jit(solution)/shard_map/convert_element_type | solution.py:228
  61.7 1.3 collective-permute-start.7
  65.1 3.7 %shard_map.70 = f32[4,2,96,1280]{3,2,1,0:T(8,128)S(1)} custom-call(s32[1]{0:T(128)} %bitcast.1.place_ref, bf16[384,1024]{1,0:T(8,128)(2,1)S(1)} %bitcast.161, bf16[1024,7168]{1,0:T(8,128)(2,1)S(1)} %copy-done.1, bf16[1024,7168]{1,0:T(8,128)(2,1)S(1)} %copy-done.3), custom_call_target="tpu_custom_call" | custom-call | flops 6000000000 | tf_op jit(solution)/shard_map/pallas_call | solution.py:56
  68.9 4.9 %collective-permute-done.5 = bf16[48,3584]{1,0:T(8,128)(2,1)S(1)} collective-permute-done((bf16[48,3584]{1,0:T(8,128)(2,1)S(1)}, bf16[48,3584]{1,0:T(8,128)(2,1)S(1)}, u32[]{:S(2)}, u32[]{:S(2)}) %collective-permute-start.5) | collective-permute-done | bytes 344096 | tf_op jit(solution)/shard_map/ppermute | solution.py:313
  74.6 2.1 fusion.8
  76.7 3.0 %collective-permute-start.11 = (f16[2,96,1280]{2,1,0:T(8,128)(2,1)S(1)}, f16[2,96,1280]{2,1,0:T(8,128)(2,1)S(1)}, u32[]{:S(2)}, u32[]{:S(2)}) collective-permute-start(f16[2,96,1280]{2,1,0:T(8,128)(2,1)S(1)} %get-tuple-element.181), channel_id=1, source_target_pairs={{0,4},{2,6},{12,8},{14,10},{4,0},{6,2},{8,12},{10,14},{1,5},{3,7},... | collective-permute-start | bytes 1474568 | tf_op jit(solution)/shard_map/ppermute | solution.py:179
  80.5 2.4 %collective-permute-start.9 = (bf16[2,48,1792]{2,1,0:T(8,128)(2,1)S(1)}, bf16[2,48,1792]{2,1,0:T(8,128)(2,1)S(1)}, u32[]{:S(2)}, u32[]{:S(2)}) collective-permute-start(bf16[2,48,1792]{2,1,0:T(8,128)(2,1)S(1)} %get-tuple-element.202), channel_id=1, source_target_pairs={{0,2},{2,0},{4,6},{6,4},{8,10},{10,8},{12,14},{14,12},{1,3},{3,1},... | collective-permute-start | bytes 1032200 | tf_op jit(solution)/shard_map/ppermute | solution.py:179
  83.0 4.5 %collective-permute-start.16 = (f16[2,96,1280]{2,1,0:T(8,128)(2,1)S(1)}, f16[2,96,1280]{2,1,0:T(8,128)(2,1)S(1)}, u32[]{:S(2)}, u32[]{:S(2)}) collective-permute-start(f16[2,96,1280]{2,1,0:T(8,128)(2,1)S(1)} %fusion.31), channel_id=1, source_target_pairs={{0,4},{2,6},{12,8},{14,10},{1,5},{3,7},{13,9},{15,11},{16,20},{18,... | collective-permute-start | bytes 1474568 | tf_op jit(solution)/shard_map/ppermute | solution.py:179
  87.5 1.4 dynamic-slice_bitcast_fusion
  93.3 1.6 collective-permute-start.15
  94.9 2.2 collective-permute-start.14
  97.6 4.9 %shard_map.71 = f32[4,2,192,512]{3,2,1,0:T(8,128)S(1)} custom-call(s32[1]{0:T(128)} %bitcast.1.place_ref, bf16[768,1024]{1,0:T(8,128)(2,1)S(1)} %bitcast.165, bf16[768,1024]{1,0:T(8,128)(2,1)S(1)} %bitcast.166, bf16[1024,7168]{1,0:T(8,128)(2,1)S(1)} %bitcast.155, bf16[1024,7168]{1,0:T(8,128)(2,1)} %refs_3_.1, ...), custom_call_target="tpu_custom_call" | custom-call | tf_op jit(solution)/shard_map/pallas_call | solution.py:56
  103.6 3.3 %collective-permute-start.19 = (f16[2,96,1280]{2,1,0:T(8,128)(2,1)S(1)}, f16[2,96,1280]{2,1,0:T(8,128)(2,1)S(1)}, u32[]{:S(2)}, u32[]{:S(2)}) collective-permute-start(f16[2,96,1280]{2,1,0:T(8,128)(2,1)S(1)} %fusion.32), channel_id=1, source_target_pairs={{0,4},{2,6},{12,8},{14,10},{1,5},{3,7},{13,9},{15,11},{16,20},{18,... | collective-permute-start | bytes 1474568 | tf_op jit(solution)/shard_map/ppermute | solution.py:179
  106.9 2.4 %collective-permute-done.14.side_1 = bf16[2,96,1280]{2,1,0:T(8,128)(2,1)} collective-permute-done((bf16[2,96,1280]{2,1,0:T(8,128)(2,1)S(1)}, bf16[2,96,1280]{2,1,0:T(8,128)(2,1)}, u32[]{:S(2)}, u32[]{:S(2)}) %collective-permute-start.14) | collective-permute-done | bytes 491552 | tf_op jit(solution)/shard_map/ppermute | solution.py:179
  109.3 1.4 collective-permute-start.18
  112.0 7.8 %collective-permute-done.19 = f16[2,96,1280]{2,1,0:T(8,128)(2,1)S(1)} collective-permute-done((f16[2,96,1280]{2,1,0:T(8,128)(2,1)S(1)}, f16[2,96,1280]{2,1,0:T(8,128)(2,1)S(1)}, u32[]{:S(2)}, u32[]{:S(2)}) %collective-permute-start.19) | collective-permute-done | bytes 491552 | tf_op jit(solution)/shard_map/ppermute | solution.py:179
  119.8 1.4 fusion.4
  121.2 2.2 collective-permute-start.22
  123.4 1.5 collective-permute-start.23
  124.9 1.3 collective-permute-start.21
  126.2 2.3 copy.27
  128.5 2.3 copy.28
  130.8 2.8 %maximum_bitcast_fusion.features_ref = bf16[1024,768]{1,0:T(8,128)(2,1)} fusion(bf16[384,1024]{0,1:T(8,128)(2,1)} %copy.28, bf16[384,1024]{0,1:T(8,128)(2,1)} %copy.27), kind=kLoop, calls=%fused_computation.2 | loop fusion | flops 3145728 | bytes 3145728 | tf_op jit(solution)/shard_map/transpose | solution.py:348
  133.6 5.2 %collective-permute-start.26 = (f16[2,192,512]{2,1,0:T(8,128)(2,1)S(1)}, f16[2,192,512]{2,1,0:T(8,128)(2,1)S(1)}, u32[]{:S(2)}, u32[]{:S(2)}) collective-permute-start(f16[2,192,512]{2,1,0:T(8,128)(2,1)S(1)} %fusion.39), channel_id=1, source_target_pairs={{0,4},{2,6},{12,8},{14,10},{1,5},{3,7},{13,9},{15,11},{16,20},{18,... | collective-permute-start | bytes 1179656 | tf_op jit(solution)/shard_map/ppermute | solution.py:179
  138.9 1.9 fusion.2
  142.0 1.5 collective-permute-start.25
  143.4 1.8 collective-permute-start.24
  146.1 1.9 shard_map.72
  149.0 3.7 %collective-permute-start.29 = (f16[2,192,512]{2,1,0:T(8,128)(2,1)S(1)}, f16[2,192,512]{2,1,0:T(8,128)(2,1)S(1)}, u32[]{:S(2)}, u32[]{:S(2)}) collective-permute-start(f16[2,192,512]{2,1,0:T(8,128)(2,1)S(1)} %fusion.40), channel_id=1, source_target_pairs={{0,4},{2,6},{12,8},{14,10},{1,5},{3,7},{13,9},{15,11},{16,20},{18,... | collective-permute-start | bytes 1179656 | tf_op jit(solution)/shard_map/ppermute | solution.py:179
  152.7 2.5 %collective-permute-done.24.side_1 = bf16[2,96,1280]{2,1,0:T(8,128)(2,1)} collective-permute-done((bf16[2,96,1280]{2,1,0:T(8,128)(2,1)S(1)}, bf16[2,96,1280]{2,1,0:T(8,128)(2,1)}, u32[]{:S(2)}, u32[]{:S(2)}) %collective-permute-start.24) | collective-permute-done | bytes 491552 | tf_op jit(solution)/shard_map/ppermute | solution.py:179
  155.2 1.5 collective-permute-start.28
  156.7 1.5 collective-permute-start.27
  158.2 4.2 %collective-permute-done.29 = f16[2,192,512]{2,1,0:T(8,128)(2,1)S(1)} collective-permute-done((f16[2,192,512]{2,1,0:T(8,128)(2,1)S(1)}, f16[2,192,512]{2,1,0:T(8,128)(2,1)S(1)}, u32[]{:S(2)}, u32[]{:S(2)}) %collective-permute-start.29) | collective-permute-done | bytes 393248 | tf_op jit(solution)/shard_map/ppermute | solution.py:179
  162.4 1.3 fusion.16
  163.7 2.3 collective-permute-start.31
  166.1 1.4 collective-permute-start.32
  168.4 1.3 collective-permute-start.36
  169.7 3.5 %collective-permute-done.31 = f16[2,192,512]{2,1,0:T(8,128)(2,1)} collective-permute-done((f16[2,192,512]{2,1,0:T(8,128)(2,1)}, f16[2,192,512]{2,1,0:T(8,128)(2,1)}, u32[]{:S(2)}, u32[]{:S(2)}) %collective-permute-start.31) | collective-permute-done | bytes 393248 | tf_op jit(solution)/shard_map/ppermute | solution.py:179
  173.2 1.4 fusion.18
  175.6 8.5 %collective-permute-start.33 = (bf16[2,192,512]{2,1,0:T(8,128)(2,1)S(1)}, bf16[2,192,512]{2,1,0:T(8,128)(2,1)}, u32[]{:S(2)}, u32[]{:S(2)}) collective-permute-start(bf16[2,192,512]{2,1,0:T(8,128)(2,1)S(1)} %pad_maximum_fusion.4.act), channel_id=1, source_target_pairs={{0,4},{2,6},{12,8},{14,10},{4,0},{6,2},{8,12},{10,14},{1,5},{3,7},... | collective-permute-start | bytes 1179656 | tf_op jit(solution)/shard_map/ppermute | solution.py:179
  185.2 11.7 %collective-permute-start.35 = (bf16[2,48,1792]{2,1,0:T(8,128)(2,1)}, bf16[2,48,1792]{2,1,0:T(8,128)(2,1)}, u32[]{:S(2)}, u32[]{:S(2)}) collective-permute-start(bf16[2,48,1792]{2,1,0:T(8,128)(2,1)} %get-tuple-element.198), channel_id=1, source_target_pairs={{0,2},{2,0},{4,6},{6,4},{8,10},{10,8},{12,14},{14,12},{1,3},{3,1},... | collective-permute-start | bytes 1032200 | tf_op jit(solution)/shard_map/ppermute | solution.py:179
  198.6 1.9 shard_map.73
  201.0 1.4 collective-permute-start.37
  205.3 7.0 %shard_map.74 = (f32[1024,3584]{1,0:T(8,128)}, f32[1024,3584]{1,0:T(8,128)}) custom-call(s32[1]{0:T(128)} %bitcast.59.place_ref, bf16[1024,768]{1,0:T(8,128)(2,1)S(1)} %copy-done.6, bf16[4,1,2,96,1280]{4,3,2,1,0:T(8,128)(2,1)S(1)} %bitcast.167, bf16[4,1,2,96,1280]{4,3,2,1,0:T(8,128)(2,1)S(1)} %bitcast.169), custom_call_target="tpu_custom_call" | custom-call | flops 4026531840 | bytes 15990784 | tf_op jit(solution)/shard_map/pallas_call | solution.py:100
  213.1 1.3 collective-permute-start.39
  215.4 7.0 %shard_map.75 = (f32[1024,3584]{1,0:T(8,128)}, f32[1024,3584]{1,0:T(8,128)}) custom-call(s32[1]{0:T(128)} %bitcast.62.place_ref, bf16[1024,768]{1,0:T(8,128)(2,1)S(1)} %copy-done.6, bf16[4,1,2,96,1280]{4,3,2,1,0:T(8,128)(2,1)S(1)} %bitcast.168, bf16[4,1,2,96,1280]{4,3,2,1,0:T(8,128)(2,1)S(1)} %bitcast.170, ...), custom_call_target="tpu_custom_call", output_to_operand_aliasing={{0}: (4, {}), {1}: (5, {})} | custom-call | flops 4026531840 | bytes 15990784 | tf_op jit(solution)/shard_map/pallas_call | solution.py:100
  222.4 2.7 %collective-permute-done.39.out_3 = bf16[2,192,512]{2,1,0:T(8,128)(2,1)S(1)} collective-permute-done((bf16[2,192,512]{2,1,0:T(8,128)(2,1)S(1)}, bf16[2,192,512]{2,1,0:T(8,128)(2,1)S(1)}, u32[]{:S(2)}, u32[]{:S(2)}) %collective-permute-start.39) | collective-permute-done | bytes 393248 | tf_op jit(solution)/shard_map/ppermute | solution.py:179
  226.3 2.6 %collective-permute-start.43 = (bf16[4,2,192,512]{3,2,1,0:T(8,128)(2,1)S(1)}, bf16[4,2,192,512]{3,2,1,0:T(8,128)(2,1)S(1)}, u32[]{:S(2)}, u32[]{:S(2)}) collective-permute-start(bf16[4,2,192,512]{3,2,1,0:T(8,128)(2,1)S(1)} %shard_map.76), channel_id=1, source_target_pairs={{0,2},{2,0},{4,6},{6,4},{8,10},{10,8},{12,14},{14,12},{1,3},{3,1},... | collective-permute-start | bytes 4718600 | tf_op jit(solution)/shard_map/ppermute | solution.py:179
  229.0 3.4 %shard_map.77 = (f32[1024,3584]{1,0:T(8,128)}, f32[1024,3584]{1,0:T(8,128)}) custom-call(s32[1]{0:T(128)} %bitcast.59.place_ref, bf16[1024,768]{1,0:T(8,128)(2,1)S(1)} %copy-done.6, bf16[4,1,2,192,512]{4,3,2,1,0:T(8,128)(2,1)S(1)} %bitcast.164, f32[1024,3584]{1,0:T(8,128)} %get-tuple-element.169.refs_1_, ...), custom_call_target="tpu_custom_call", output_to_operand_aliasing={{0}: (3, {}), {1}: (4, {})} | custom-call | flops 1610612736 | bytes 7340032 | tf_op jit(solution)/shard_map/pallas_call | solution.py:100
  232.4 3.4 %shard_map.78 = (f32[1024,3584]{1,0:T(8,128)}, f32[1024,3584]{1,0:T(8,128)}) custom-call(s32[1]{0:T(128)} %bitcast.62.place_ref, bf16[1024,768]{1,0:T(8,128)(2,1)S(1)} %copy-done.6, bf16[4,1,2,192,512]{4,3,2,1,0:T(8,128)(2,1)S(1)} %bitcast.171, f32[1024,3584]{1,0:T(8,128)} %get-tuple-element.175.refs_1_, ...), custom_call_target="tpu_custom_call", output_to_operand_aliasing={{0}: (3, {}), {1}: (4, {})} | custom-call | flops 1610612736 | bytes 7340032 | tf_op jit(solution)/shard_map/pallas_call | solution.py:100
  (151 shorter events, 29.5 us)
Async XLA Ops:
  0.6 11.3 %collective-permute-start.1 = (bf16[384,512]{1,0:T(8,128)(2,1)}, bf16[384,512]{1,0:T(8,128)(2,1)S(1)}, u32[]{:S(2)}, u32[]{:S(2)}) collective-permute-start(bf16[384,512]{1,0:T(8,128)(2,1)} %bitcast.179), channel_id=1, source_target_pairs={{0,1},{1,0},{2,3},{3,2},{4,5},{5,4},{6,7},{7,6},{8,9},{9,8},{10,11... | collective-permute-start | bytes 1179656 | tf_op jit(solution)/shard_map/ppermute | solution.py:213
  2.8 10.0 %collective-permute-start = (bf16[384,512]{1,0:T(8,128)(2,1)}, bf16[384,512]{1,0:T(8,128)(2,1)}, u32[]{:S(2)}, u32[]{:S(2)}) collective-permute-start(bf16[384,512]{1,0:T(8,128)(2,1)} %bitcast.180), channel_id=1, source_target_pairs={{0,16},{16,0},{1,17},{17,1},{2,18},{18,2},{3,19},{19,3},{4,20},{20... | collective-permute-start | bytes 1179656 | tf_op jit(solution)/shard_map/ppermute | solution.py:212
  14.6 75.1 %copy-start.7 = (bf16[4,96,1024]{2,1,0:T(8,128)(2,1)}, bf16[4,96,1024]{2,1,0:T(8,128)(2,1)S(1)}, u32[]{:S(2)}) copy-start(bf16[4,96,1024]{2,1,0:T(8,128)(2,1)S(1)} %reverse_select_fusion.1) | copy-start | bytes 2359300
  14.6 5.5 %copy-start = (bf16[1024,7168]{1,0:T(8,128)(2,1)S(1)}, bf16[1024,7168]{1,0:T(8,128)(2,1)}, u32[]{:S(2)}) copy-start(bf16[1024,7168]{1,0:T(8,128)(2,1)} %refs_2_.9) | copy-start | bytes 44040196
  20.1 5.2 %copy-start.2 = (bf16[1024,7168]{1,0:T(8,128)(2,1)S(1)}, bf16[1024,7168]{1,0:T(8,128)(2,1)}, u32[]{:S(2)}) copy-start(bf16[1024,7168]{1,0:T(8,128)(2,1)} %refs_3_.1) | copy-start | bytes 44040196
  30.4 16.6 %collective-permute-start.2 = (f16[4,2,96,1280]{3,2,1,0:T(8,128)(2,1)}, f16[4,2,96,1280]{3,2,1,0:T(8,128)(2,1)S(1)}, u32[]{:S(2)}, u32[]{:S(2)}) collective-permute-start(f16[4,2,96,1280]{3,2,1,0:T(8,128)(2,1)} %convert_element_type.194), channel_id=1, source_target_pairs={{0,2},{2,0},{4,6},{6,4},{8,10},{10,8},{12,14},{14,12},{1,3},{3,1},... | collective-permute-start | bytes 5898248 | tf_op jit(solution)/shard_map/ppermute | solution.py:179
  32.3 18.9 %collective-permute-start.3 = (bf16[384,512]{1,0:T(8,128)(2,1)}, bf16[384,512]{1,0:T(8,128)(2,1)S(1)}, u32[]{:S(2)}, u32[]{:S(2)}) collective-permute-start(bf16[384,512]{1,0:T(8,128)(2,1)} %collective-permute-done), channel_id=1, source_target_pairs={{0,1},{1,0},{2,3},{3,2},{4,5},{5,4},{6,7},{7,6},{8,9},{9,8},{10,11... | collective-permute-start | bytes 1179656 | tf_op jit(solution)/shard_map/ppermute | solution.py:214
  47.9 15.1 %collective-permute-start.4 = (f16[2,96,1280]{2,1,0:T(8,128)(2,1)}, f16[2,96,1280]{2,1,0:T(8,128)(2,1)S(1)}, u32[]{:S(2)}, u32[]{:S(2)}) collective-permute-start(f16[2,96,1280]{2,1,0:T(8,128)(2,1)} %fusion.33), channel_id=1, source_target_pairs={{0,4},{2,6},{12,8},{14,10},{1,5},{3,7},{13,9},{15,11},{16,20},{18,... | collective-permute-start | bytes 1474568 | tf_op jit(solution)/shard_map/ppermute | solution.py:179
  51.6 38.0 %copy-start.8 = (bf16[4,96,1024]{2,1,0:T(8,128)(2,1)}, bf16[4,96,1024]{2,1,0:T(8,128)(2,1)S(1)}, u32[]{:S(2)}) copy-start(bf16[4,96,1024]{2,1,0:T(8,128)(2,1)S(1)} %reverse_select_fusion) | copy-start | bytes 2359300
  61.1 12.7 %collective-permute-start.6 = (f16[4,2,96,1280]{3,2,1,0:T(8,128)(2,1)}, f16[4,2,96,1280]{3,2,1,0:T(8,128)(2,1)S(1)}, u32[]{:S(2)}, u32[]{:S(2)}) collective-permute-start(f16[4,2,96,1280]{3,2,1,0:T(8,128)(2,1)} %convert_element_type.198), channel_id=1, source_target_pairs={{0,2},{2,0},{4,6},{6,4},{8,10},{10,8},{12,14},{14,12},{1,3},{3,1},... | collective-permute-start | bytes 5898248 | tf_op jit(solution)/shard_map/ppermute | solution.py:179
  61.7 12.0 %collective-permute-start.7 = (f16[2,96,1280]{2,1,0:T(8,128)(2,1)S(1)}, f16[2,96,1280]{2,1,0:T(8,128)(2,1)S(1)}, u32[]{:S(2)}, u32[]{:S(2)}) collective-permute-start(f16[2,96,1280]{2,1,0:T(8,128)(2,1)S(1)} %fusion.30), channel_id=1, source_target_pairs={{0,4},{2,6},{12,8},{14,10},{1,5},{3,7},{13,9},{15,11},{16,20},{18,... | collective-permute-start | bytes 1474568 | tf_op jit(solution)/shard_map/ppermute | solution.py:179
  63.3 11.3 %collective-permute-start.8 = (f16[2,96,1280]{2,1,0:T(8,128)(2,1)S(1)}, f16[2,96,1280]{2,1,0:T(8,128)(2,1)S(1)}, u32[]{:S(2)}, u32[]{:S(2)}) collective-permute-start(f16[2,96,1280]{2,1,0:T(8,128)(2,1)S(1)} %fusion.13), channel_id=1, source_target_pairs={{4,8},{6,10},{8,4},{10,6},{5,9},{7,11},{9,5},{11,7},{20,24},{22,26... | collective-permute-start | bytes 1474568 | tf_op jit(solution)/shard_map/ppermute | solution.py:179
  64.3 9.5 %collective-permute-start.5 = (bf16[48,3584]{1,0:T(8,128)(2,1)S(1)}, bf16[48,3584]{1,0:T(8,128)(2,1)S(1)}, u32[]{:S(2)}, u32[]{:S(2)}) collective-permute-start(bf16[48,3584]{1,0:T(8,128)(2,1)S(1)} %get-tuple-element.203), channel_id=1, source_target_pairs={{0,1},{1,0},{2,3},{3,2},{4,5},{5,4},{6,7},{7,6},{8,9},{9,8},{10,11... | collective-permute-start | bytes 1032200 | tf_op jit(solution)/shard_map/ppermute | solution.py:313
  68.9 51.0 %copy-start.4 = (f32[4,2,96,1280]{3,2,1,0:T(8,128)}, f32[4,2,96,1280]{3,2,1,0:T(8,128)S(1)}, u32[]{:S(2)}) copy-start(f32[4,2,96,1280]{3,2,1,0:T(8,128)S(1)} %shard_map.70) | copy-start | bytes 11796484
  73.8 9.1 %copy-start.16 = (f16[4,2,96,1280]{3,2,1,0:T(8,128)(2,1)}, f16[4,2,96,1280]{3,2,1,0:T(8,128)(2,1)S(1)}, u32[]{:S(2)}) copy-start(f16[4,2,96,1280]{3,2,1,0:T(8,128)(2,1)S(1)} %collective-permute-done.6) | copy-start | bytes 5898244
  76.7 14.2 %collective-permute-start.11 = (f16[2,96,1280]{2,1,0:T(8,128)(2,1)S(1)}, f16[2,96,1280]{2,1,0:T(8,128)(2,1)S(1)}, u32[]{:S(2)}, u32[]{:S(2)}) collective-permute-start(f16[2,96,1280]{2,1,0:T(8,128)(2,1)S(1)} %get-tuple-element.181), channel_id=1, source_target_pairs={{0,4},{2,6},{12,8},{14,10},{4,0},{6,2},{8,12},{10,14},{1,5},{3,7},... | collective-permute-start | bytes 1474568 | tf_op jit(solution)/shard_map/ppermute | solution.py:179
  79.7 11.2 %collective-permute-start.12 = (f16[2,96,1280]{2,1,0:T(8,128)(2,1)S(1)}, f16[2,96,1280]{2,1,0:T(8,128)(2,1)S(1)}, u32[]{:S(2)}, u32[]{:S(2)}) collective-permute-start(f16[2,96,1280]{2,1,0:T(8,128)(2,1)S(1)} %get-tuple-element.182), channel_id=1, source_target_pairs={{4,8},{6,10},{8,4},{10,6},{5,9},{7,11},{9,5},{11,7},{20,24},{22,26... | collective-permute-start | bytes 1474568 | tf_op jit(solution)/shard_map/ppermute | solution.py:179
  80.4 17.1 %slice-start = ((s8[14680064]{0:T(1024)(128)(4,1)}), s8[2097152]{0:T(1024)(128)(4,1)S(1)}, s32[]{:S(2)}) async-start(s8[14680064]{0:T(1024)(128)(4,1)} %bitcast.154), calls=%async_computation | async-start | bytes 4194304
  80.5 9.4 %collective-permute-start.9 = (bf16[2,48,1792]{2,1,0:T(8,128)(2,1)S(1)}, bf16[2,48,1792]{2,1,0:T(8,128)(2,1)S(1)}, u32[]{:S(2)}, u32[]{:S(2)}) collective-permute-start(bf16[2,48,1792]{2,1,0:T(8,128)(2,1)S(1)} %get-tuple-element.202), channel_id=1, source_target_pairs={{0,2},{2,0},{4,6},{6,4},{8,10},{10,8},{12,14},{14,12},{1,3},{3,1},... | collective-permute-start | bytes 1032200 | tf_op jit(solution)/shard_map/ppermute | solution.py:179
  83.0 19.5 %collective-permute-start.16 = (f16[2,96,1280]{2,1,0:T(8,128)(2,1)S(1)}, f16[2,96,1280]{2,1,0:T(8,128)(2,1)S(1)}, u32[]{:S(2)}, u32[]{:S(2)}) collective-permute-start(f16[2,96,1280]{2,1,0:T(8,128)(2,1)S(1)} %fusion.31), channel_id=1, source_target_pairs={{0,4},{2,6},{12,8},{14,10},{1,5},{3,7},{13,9},{15,11},{16,20},{18,... | collective-permute-start | bytes 1474568 | tf_op jit(solution)/shard_map/ppermute | solution.py:179
  89.0 8.6 %slice-start.1 = ((s8[14680064]{0:T(1024)(128)(4,1)}), s8[4194304]{0:T(1024)(128)(4,1)S(1)}, s32[]{:S(2)}) async-start(s8[14680064]{0:T(1024)(128)(4,1)} %bitcast.154), calls=%async_computation.1 | async-start | bytes 8388608
  89.2 8.3 %collective-permute-start.13 = (bf16[2,1024,512]{2,1,0:T(8,128)(2,1)S(1)}, bf16[2,1024,512]{2,1,0:T(8,128)(2,1)S(1)}, u32[]{:S(2)}, u32[]{:S(2)}) collective-permute-start(bf16[2,1024,512]{2,1,0:T(8,128)(2,1)S(1)} %pad_maximum_fusion), channel_id=1, source_target_pairs={{0,2},{2,0},{4,6},{6,4},{8,10},{10,8},{12,14},{14,12},{1,3},{3,1},... | collective-permute-start | bytes 6291464 | tf_op jit(solution)/shard_map/ppermute | solution.py:179
  89.9 7.3 %collective-permute-start.10 = (bf16[4,2,96,1024]{3,2,0,1:T(8,128)(2,1)S(1)}, bf16[4,2,96,1024]{3,2,0,1:T(8,128)(2,1)S(1)}, u32[]{:S(2)}, u32[]{:S(2)}) collective-permute-start(bf16[4,2,96,1024]{3,2,0,1:T(8,128)(2,1)S(1)} %pad_maximum_fusion.1), channel_id=1, source_target_pairs={{0,2},{2,0},{4,6},{6,4},{8,10},{10,8},{12,14},{14,12},{1,3},{3,1},... | collective-permute-start | bytes 4718600 | tf_op jit(solution)/shard_map/ppermute | solution.py:179
  90.0 7.5 %slice-start.2 = ((s8[14680064]{0:T(1024)(128)(4,1)}), s8[4194304]{0:T(1024)(128)(4,1)S(1)}, s32[]{:S(2)}) async-start(s8[14680064]{0:T(1024)(128)(4,1)} %bitcast.154), calls=%async_computation.2 | async-start | bytes 8388608
  92.3 5.2 %slice-start.3 = ((s8[14680064]{0:T(1024)(128)(4,1)}), s8[4194304]{0:T(1024)(128)(4,1)S(1)}, s32[]{:S(2)}) async-start(s8[14680064]{0:T(1024)(128)(4,1)} %bitcast.154), calls=%async_computation.3 | async-start | bytes 8388608
  93.3 13.6 %collective-permute-start.15 = (bf16[2,96,1280]{2,1,0:T(8,128)(2,1)S(1)}, bf16[2,96,1280]{2,1,0:T(8,128)(2,1)}, u32[]{:S(2)}, u32[]{:S(2)}) collective-permute-start(bf16[2,96,1280]{2,1,0:T(8,128)(2,1)S(1)} %pad_maximum_fusion.2.act), channel_id=1, source_target_pairs={{4,8},{6,10},{8,4},{10,6},{5,9},{7,11},{9,5},{11,7},{20,24},{22,26... | collective-permute-start | bytes 1474568 | tf_op jit(solution)/shard_map/ppermute | solution.py:179
  94.9 14.4 %collective-permute-start.14 = (bf16[2,96,1280]{2,1,0:T(8,128)(2,1)S(1)}, bf16[2,96,1280]{2,1,0:T(8,128)(2,1)}, u32[]{:S(2)}, u32[]{:S(2)}) collective-permute-start(bf16[2,96,1280]{2,1,0:T(8,128)(2,1)S(1)} %pad_maximum_fusion.2.act), channel_id=1, source_target_pairs={{0,4},{2,6},{12,8},{14,10},{4,0},{6,2},{8,12},{10,14},{1,5},{3,7},... | collective-permute-start | bytes 1474568 | tf_op jit(solution)/shard_map/ppermute | solution.py:179
  102.9 9.2 %collective-permute-start.20 = (f16[2,96,1280]{2,1,0:T(8,128)(2,1)S(1)}, f16[2,96,1280]{2,1,0:T(8,128)(2,1)S(1)}, u32[]{:S(2)}, u32[]{:S(2)}) collective-permute-start(f16[2,96,1280]{2,1,0:T(8,128)(2,1)S(1)} %fusion.6), channel_id=1, source_target_pairs={{4,8},{6,10},{8,4},{10,6},{5,9},{7,11},{9,5},{11,7},{20,24},{22,26... | collective-permute-start | bytes 1474568 | tf_op jit(solution)/shard_map/ppermute | solution.py:179
  103.6 16.3 %collective-permute-start.19 = (f16[2,96,1280]{2,1,0:T(8,128)(2,1)S(1)}, f16[2,96,1280]{2,1,0:T(8,128)(2,1)S(1)}, u32[]{:S(2)}, u32[]{:S(2)}) collective-permute-start(f16[2,96,1280]{2,1,0:T(8,128)(2,1)S(1)} %fusion.32), channel_id=1, source_target_pairs={{0,4},{2,6},{12,8},{14,10},{1,5},{3,7},{13,9},{15,11},{16,20},{18,... | collective-permute-start | bytes 1474568 | tf_op jit(solution)/shard_map/ppermute | solution.py:179
  109.3 15.6 %collective-permute-start.18 = (bf16[2,96,1280]{2,1,0:T(8,128)(2,1)}, bf16[2,96,1280]{2,1,0:T(8,128)(2,1)}, u32[]{:S(2)}, u32[]{:S(2)}) collective-permute-start(bf16[2,96,1280]{2,1,0:T(8,128)(2,1)} %collective-permute-done.14.side_1), channel_id=1, source_target_pairs={{4,8},{6,10},{8,4},{10,6},{5,9},{7,11},{9,5},{11,7},{20,24},{22,26... | collective-permute-start | bytes 1474568 | tf_op jit(solution)/shard_map/ppermute | solution.py:179
  110.7 14.2 %collective-permute-start.17 = (bf16[2,96,1280]{2,1,0:T(8,128)(2,1)}, bf16[2,96,1280]{2,1,0:T(8,128)(2,1)}, u32[]{:S(2)}, u32[]{:S(2)}) collective-permute-start(bf16[2,96,1280]{2,1,0:T(8,128)(2,1)} %collective-permute-done.15.centre_1), channel_id=1, source_target_pairs={{4,0},{6,2},{8,12},{10,14},{5,1},{7,3},{9,13},{11,15},{20,16},{22,... | collective-permute-start | bytes 1474568 | tf_op jit(solution)/shard_map/ppermute | solution.py:179
  121.2 17.7 %collective-permute-start.22 = (f16[2,96,1280]{2,1,0:T(8,128)(2,1)}, f16[2,96,1280]{2,1,0:T(8,128)(2,1)}, u32[]{:S(2)}, u32[]{:S(2)}) collective-permute-start(f16[2,96,1280]{2,1,0:T(8,128)(2,1)} %get-tuple-element.179), channel_id=1, source_target_pairs={{0,4},{2,6},{12,8},{14,10},{4,0},{6,2},{8,12},{10,14},{1,5},{3,7},... | collective-permute-start | bytes 1474568 | tf_op jit(solution)/shard_map/ppermute | solution.py:179
  123.4 15.5 %collective-permute-start.23 = (f16[2,96,1280]{2,1,0:T(8,128)(2,1)}, f16[2,96,1280]{2,1,0:T(8,128)(2,1)}, u32[]{:S(2)}, u32[]{:S(2)}) collective-permute-start(f16[2,96,1280]{2,1,0:T(8,128)(2,1)} %get-tuple-element.180), channel_id=1, source_target_pairs={{4,8},{6,10},{8,4},{10,6},{5,9},{7,11},{9,5},{11,7},{20,24},{22,26... | collective-permute-start | bytes 1474568 | tf_op jit(solution)/shard_map/ppermute | solution.py:179
  124.9 21.2 %collective-permute-start.21 = (bf16[2,96,1280]{2,1,0:T(8,128)(2,1)}, bf16[2,96,1280]{2,1,0:T(8,128)(2,1)}, u32[]{:S(2)}, u32[]{:S(2)}) collective-permute-start(bf16[2,96,1280]{2,1,0:T(8,128)(2,1)} %collective-permute-done.18.share_2), channel_id=1, source_target_pairs={{4,0},{6,2},{8,12},{10,14},{5,1},{7,3},{9,13},{11,15},{20,16},{22,... | collective-permute-start | bytes 1474568 | tf_op jit(solution)/shard_map/ppermute | solution.py:179
  130.8 8.1 %copy-start.5 = (f32[4,2,96,1280]{3,2,1,0:T(8,128)S(1)}, f32[4,2,96,1280]{3,2,1,0:T(8,128)}, u32[]{:S(2)}) copy-start(f32[4,2,96,1280]{3,2,1,0:T(8,128)} %copy-done.4) | copy-start | bytes 11796484
  133.6 7.2 %copy-start.21 = (bf16[96,1792]{1,0:T(8,128)(2,1)S(1)}, bf16[96,1792]{1,0:T(8,128)(2,1)}, u32[]{:S(2)}) copy-start(bf16[96,1792]{1,0:T(8,128)(2,1)} %get-tuple-element.200) | copy-start | bytes 1032196
  133.6 14.4 %collective-permute-start.26 = (f16[2,192,512]{2,1,0:T(8,128)(2,1)S(1)}, f16[2,192,512]{2,1,0:T(8,128)(2,1)S(1)}, u32[]{:S(2)}, u32[]{:S(2)}) collective-permute-start(f16[2,192,512]{2,1,0:T(8,128)(2,1)S(1)} %fusion.39), channel_id=1, source_target_pairs={{0,4},{2,6},{12,8},{14,10},{1,5},{3,7},{13,9},{15,11},{16,20},{18,... | collective-permute-start | bytes 1179656 | tf_op jit(solution)/shard_map/ppermute | solution.py:179
  140.9 5.2 %copy-start.15 = (bf16[2,96,1280]{2,1,0:T(8,128)(2,1)S(1)}, bf16[2,96,1280]{2,1,0:T(8,128)(2,1)}, u32[]{:S(2)}) copy-start(bf16[2,96,1280]{2,1,0:T(8,128)(2,1)} %copy-done.14) | copy-start | bytes 1474564
  141.9 6.1 %copy-start.12 = (bf16[2,96,1280]{2,1,0:T(8,128)(2,1)}, bf16[2,96,1280]{2,1,0:T(8,128)(2,1)S(1)}, u32[]{:S(2)}) copy-start(bf16[2,96,1280]{2,1,0:T(8,128)(2,1)S(1)} %pad_maximum_fusion.3.act) | copy-start | bytes 1474564
  142.0 10.7 %collective-permute-start.25 = (bf16[2,96,1280]{2,1,0:T(8,128)(2,1)S(1)}, bf16[2,96,1280]{2,1,0:T(8,128)(2,1)}, u32[]{:S(2)}, u32[]{:S(2)}) collective-permute-start(bf16[2,96,1280]{2,1,0:T(8,128)(2,1)S(1)} %pad_maximum_fusion.3.act), channel_id=1, source_target_pairs={{4,8},{6,10},{8,4},{10,6},{5,9},{7,11},{9,5},{11,7},{20,24},{22,26... | collective-permute-start | bytes 1474568 | tf_op jit(solution)/shard_map/ppermute | solution.py:179
  143.4 11.8 %collective-permute-start.24 = (bf16[2,96,1280]{2,1,0:T(8,128)(2,1)S(1)}, bf16[2,96,1280]{2,1,0:T(8,128)(2,1)}, u32[]{:S(2)}, u32[]{:S(2)}) collective-permute-start(bf16[2,96,1280]{2,1,0:T(8,128)(2,1)S(1)} %pad_maximum_fusion.3.act), channel_id=1, source_target_pairs={{0,4},{2,6},{12,8},{14,10},{4,0},{6,2},{8,12},{10,14},{1,5},{3,7},... | collective-permute-start | bytes 1474568 | tf_op jit(solution)/shard_map/ppermute | solution.py:179
  148.0 15.7 %copy-start.10 = (bf16[4,2,96,1280]{3,2,1,0:T(8,128)(2,1)}, bf16[4,2,96,1280]{3,2,1,0:T(8,128)(2,1)S(1)}, u32[]{:S(2)}) copy-start(bf16[4,2,96,1280]{3,2,1,0:T(8,128)(2,1)S(1)} %shard_map.72) | copy-start | bytes 5898244
  148.3 9.9 %collective-permute-start.30 = (f16[2,192,512]{2,1,0:T(8,128)(2,1)S(1)}, f16[2,192,512]{2,1,0:T(8,128)(2,1)S(1)}, u32[]{:S(2)}, u32[]{:S(2)}) collective-permute-start(f16[2,192,512]{2,1,0:T(8,128)(2,1)S(1)} %fusion.19), channel_id=1, source_target_pairs={{4,8},{6,10},{8,4},{10,6},{5,9},{7,11},{9,5},{11,7},{20,24},{22,26... | collective-permute-start | bytes 1179656 | tf_op jit(solution)/shard_map/ppermute | solution.py:179
  149.0 13.5 %collective-permute-start.29 = (f16[2,192,512]{2,1,0:T(8,128)(2,1)S(1)}, f16[2,192,512]{2,1,0:T(8,128)(2,1)S(1)}, u32[]{:S(2)}, u32[]{:S(2)}) collective-permute-start(f16[2,192,512]{2,1,0:T(8,128)(2,1)S(1)} %fusion.40), channel_id=1, source_target_pairs={{0,4},{2,6},{12,8},{14,10},{1,5},{3,7},{13,9},{15,11},{16,20},{18,... | collective-permute-start | bytes 1179656 | tf_op jit(solution)/shard_map/ppermute | solution.py:179
  155.2 13.2 %collective-permute-start.28 = (bf16[2,96,1280]{2,1,0:T(8,128)(2,1)}, bf16[2,96,1280]{2,1,0:T(8,128)(2,1)}, u32[]{:S(2)}, u32[]{:S(2)}) collective-permute-start(bf16[2,96,1280]{2,1,0:T(8,128)(2,1)} %collective-permute-done.24.side_1), channel_id=1, source_target_pairs={{4,8},{6,10},{8,4},{10,6},{5,9},{7,11},{9,5},{11,7},{20,24},{22,26... | collective-permute-start | bytes 1474568 | tf_op jit(solution)/shard_map/ppermute | solution.py:179
  156.7 11.7 %collective-permute-start.27 = (bf16[2,96,1280]{2,1,0:T(8,128)(2,1)}, bf16[2,96,1280]{2,1,0:T(8,128)(2,1)}, u32[]{:S(2)}, u32[]{:S(2)}) collective-permute-start(bf16[2,96,1280]{2,1,0:T(8,128)(2,1)} %collective-permute-done.25.centre_1), channel_id=1, source_target_pairs={{4,0},{6,2},{8,12},{10,14},{5,1},{7,3},{9,13},{11,15},{20,16},{22,... | collective-permute-start | bytes 1474568 | tf_op jit(solution)/shard_map/ppermute | solution.py:179
  163.7 9.5 %collective-permute-start.31 = (f16[2,192,512]{2,1,0:T(8,128)(2,1)}, f16[2,192,512]{2,1,0:T(8,128)(2,1)}, u32[]{:S(2)}, u32[]{:S(2)}) collective-permute-start(f16[2,192,512]{2,1,0:T(8,128)(2,1)} %get-tuple-element.183), channel_id=1, source_target_pairs={{0,4},{2,6},{12,8},{14,10},{4,0},{6,2},{8,12},{10,14},{1,5},{3,7},... | collective-permute-start | bytes 1179656 | tf_op jit(solution)/shard_map/ppermute | solution.py:179
  166.1 7.2 %collective-permute-start.32 = (f16[2,192,512]{2,1,0:T(8,128)(2,1)}, f16[2,192,512]{2,1,0:T(8,128)(2,1)}, u32[]{:S(2)}, u32[]{:S(2)}) collective-permute-start(f16[2,192,512]{2,1,0:T(8,128)(2,1)} %get-tuple-element.184), channel_id=1, source_target_pairs={{4,8},{6,10},{8,4},{10,6},{5,9},{7,11},{9,5},{11,7},{20,24},{22,26... | collective-permute-start | bytes 1179656 | tf_op jit(solution)/shard_map/ppermute | solution.py:179
  168.4 29.2 %collective-permute-start.36 = (bf16[2,96,1280]{2,1,0:T(8,128)(2,1)}, bf16[2,96,1280]{2,1,0:T(8,128)(2,1)}, u32[]{:S(2)}, u32[]{:S(2)}) collective-permute-start(bf16[2,96,1280]{2,1,0:T(8,128)(2,1)} %collective-permute-done.28.share_2), channel_id=1, source_target_pairs={{4,0},{6,2},{8,12},{10,14},{5,1},{7,3},{9,13},{11,15},{20,16},{22,... | collective-permute-start | bytes 1474568 | tf_op jit(solution)/shard_map/ppermute | solution.py:179
  174.6 9.7 %copy-start.23 = (bf16[1,96,1280]{2,1,0:T(8,128)(2,1)S(1)}, bf16[1,96,1280]{2,1,0:T(8,128)(2,1)}, u32[]{:S(2)}) copy-start(bf16[1,96,1280]{2,1,0:T(8,128)(2,1)} %get-tuple-element.189) | copy-start | bytes 737284
  174.6 9.7 %copy-start.24 = (bf16[1,96,1280]{2,1,0:T(8,128)(2,1)S(1)}, bf16[1,96,1280]{2,1,0:T(8,128)(2,1)}, u32[]{:S(2)}) copy-start(bf16[1,96,1280]{2,1,0:T(8,128)(2,1)} %get-tuple-element.190) | copy-start | bytes 737284
  174.9 26.1 %collective-permute-start.34 = (bf16[2,192,512]{2,1,0:T(8,128)(2,1)S(1)}, bf16[2,192,512]{2,1,0:T(8,128)(2,1)S(1)}, u32[]{:S(2)}, u32[]{:S(2)}) collective-permute-start(bf16[2,192,512]{2,1,0:T(8,128)(2,1)S(1)} %pad_maximum_fusion.4.act), channel_id=1, source_target_pairs={{4,8},{6,10},{8,4},{10,6},{5,9},{7,11},{9,5},{11,7},{20,24},{22,26... | collective-permute-start | bytes 1179656 | tf_op jit(solution)/shard_map/ppermute | solution.py:179
  175.6 25.4 %collective-permute-start.33 = (bf16[2,192,512]{2,1,0:T(8,128)(2,1)S(1)}, bf16[2,192,512]{2,1,0:T(8,128)(2,1)}, u32[]{:S(2)}, u32[]{:S(2)}) collective-permute-start(bf16[2,192,512]{2,1,0:T(8,128)(2,1)S(1)} %pad_maximum_fusion.4.act), channel_id=1, source_target_pairs={{0,4},{2,6},{12,8},{14,10},{4,0},{6,2},{8,12},{10,14},{1,5},{3,7},... | collective-permute-start | bytes 1179656 | tf_op jit(solution)/shard_map/ppermute | solution.py:179
  184.1 12.9 %copy-start.11 = (bf16[4,2,96,1280]{3,2,1,0:T(8,128)(2,1)S(1)}, bf16[4,2,96,1280]{3,2,1,0:T(8,128)(2,1)}, u32[]{:S(2)}) copy-start(bf16[4,2,96,1280]{3,2,1,0:T(8,128)(2,1)} %copy-done.10) | copy-start | bytes 5898244
  184.1 14.5 %copy-start.13 = (bf16[2,96,1280]{2,1,0:T(8,128)(2,1)S(1)}, bf16[2,96,1280]{2,1,0:T(8,128)(2,1)}, u32[]{:S(2)}) copy-start(bf16[2,96,1280]{2,1,0:T(8,128)(2,1)} %copy-done.12) | copy-start | bytes 1474564
  185.2 13.3 %collective-permute-start.35 = (bf16[2,48,1792]{2,1,0:T(8,128)(2,1)}, bf16[2,48,1792]{2,1,0:T(8,128)(2,1)}, u32[]{:S(2)}, u32[]{:S(2)}) collective-permute-start(bf16[2,48,1792]{2,1,0:T(8,128)(2,1)} %get-tuple-element.198), channel_id=1, source_target_pairs={{0,2},{2,0},{4,6},{6,4},{8,10},{10,8},{12,14},{14,12},{1,3},{3,1},... | collective-permute-start | bytes 1032200 | tf_op jit(solution)/shard_map/ppermute | solution.py:179
  197.0 6.1 %copy-start.22 = (bf16[2,48,1792]{2,1,0:T(8,128)(2,1)S(1)}, bf16[2,48,1792]{2,1,0:T(8,128)(2,1)}, u32[]{:S(2)}) copy-start(bf16[2,48,1792]{2,1,0:T(8,128)(2,1)} %get-tuple-element.165) | copy-start | bytes 1032196
  197.0 18.4 %collective-permute-start.40 = (bf16[4,2,96,1280]{3,2,1,0:T(8,128)(2,1)S(1)}, bf16[4,2,96,1280]{3,2,1,0:T(8,128)(2,1)S(1)}, u32[]{:S(2)}, u32[]{:S(2)}) collective-permute-start(bf16[4,2,96,1280]{3,2,1,0:T(8,128)(2,1)S(1)} %copy-done.11), channel_id=1, source_target_pairs={{0,2},{2,0},{4,6},{6,4},{8,10},{10,8},{12,14},{14,12},{1,3},{3,1},... | collective-permute-start | bytes 5898248 | tf_op jit(solution)/shard_map/ppermute | solution.py:179
  200.5 14.9 %collective-permute-start.41 = (bf16[4,2,96,1280]{3,2,1,0:T(8,128)(2,1)S(1)}, bf16[4,2,96,1280]{3,2,1,0:T(8,128)(2,1)S(1)}, u32[]{:S(2)}, u32[]{:S(2)}) collective-permute-start(bf16[4,2,96,1280]{3,2,1,0:T(8,128)(2,1)S(1)} %shard_map.73), channel_id=1, source_target_pairs={{0,2},{2,0},{4,6},{6,4},{8,10},{10,8},{12,14},{14,12},{1,3},{3,1},... | collective-permute-start | bytes 5898248 | tf_op jit(solution)/shard_map/ppermute | solution.py:179
  201.0 12.1 %collective-permute-start.37 = (bf16[2,192,512]{2,1,0:T(8,128)(2,1)S(1)}, bf16[2,192,512]{2,1,0:T(8,128)(2,1)S(1)}, u32[]{:S(2)}, u32[]{:S(2)}) collective-permute-start(bf16[2,192,512]{2,1,0:T(8,128)(2,1)S(1)} %collective-permute-done.34.centre_1), channel_id=1, source_target_pairs={{4,0},{6,2},{8,12},{10,14},{5,1},{7,3},{9,13},{11,15},{20,16},{22,... | collective-permute-start | bytes 1179656 | tf_op jit(solution)/shard_map/ppermute | solution.py:179
  202.4 9.9 %collective-permute-start.38 = (bf16[2,192,512]{2,1,0:T(8,128)(2,1)}, bf16[2,192,512]{2,1,0:T(8,128)(2,1)S(1)}, u32[]{:S(2)}, u32[]{:S(2)}) collective-permute-start(bf16[2,192,512]{2,1,0:T(8,128)(2,1)} %collective-permute-done.33.side_1), channel_id=1, source_target_pairs={{4,8},{6,10},{8,4},{10,6},{5,9},{7,11},{9,5},{11,7},{20,24},{22,26... | collective-permute-start | bytes 1179656 | tf_op jit(solution)/shard_map/ppermute | solution.py:179
  204.4 10.0 %collective-permute-start.42 = (bf16[48,3584]{1,0:T(8,128)(2,1)S(1)}, bf16[48,3584]{1,0:T(8,128)(2,1)S(1)}, u32[]{:S(2)}, u32[]{:S(2)}) collective-permute-start(bf16[48,3584]{1,0:T(8,128)(2,1)S(1)} %get-tuple-element.196), channel_id=1, source_target_pairs={{0,1},{1,0},{2,3},{3,2},{4,5},{5,4},{6,7},{7,6},{8,9},{9,8},{10,11... | collective-permute-start | bytes 1032200 | tf_op jit(solution)/shard_map/ppermute | solution.py:321
  213.1 12.1 %collective-permute-start.39 = (bf16[2,192,512]{2,1,0:T(8,128)(2,1)S(1)}, bf16[2,192,512]{2,1,0:T(8,128)(2,1)S(1)}, u32[]{:S(2)}, u32[]{:S(2)}) collective-permute-start(bf16[2,192,512]{2,1,0:T(8,128)(2,1)S(1)} %collective-permute-done.38.share_2), channel_id=1, source_target_pairs={{4,0},{6,2},{8,12},{10,14},{5,1},{7,3},{9,13},{11,15},{20,16},{22,... | collective-permute-start | bytes 1179656 | tf_op jit(solution)/shard_map/ppermute | solution.py:179
  226.3 6.1 %collective-permute-start.43 = (bf16[4,2,192,512]{3,2,1,0:T(8,128)(2,1)S(1)}, bf16[4,2,192,512]{3,2,1,0:T(8,128)(2,1)S(1)}, u32[]{:S(2)}, u32[]{:S(2)}) collective-permute-start(bf16[4,2,192,512]{3,2,1,0:T(8,128)(2,1)S(1)} %shard_map.76), channel_id=1, source_target_pairs={{0,2},{2,0},{4,6},{6,4},{8,10},{10,8},{12,14},{14,12},{1,3},{3,1},... | collective-permute-start | bytes 4718600 | tf_op jit(solution)/shard_map/ppermute | solution.py:179
  (13 other events, 46.1 us)

commit v18 on v17

--- a/solution.py
+++ b/solution.py
@@ -11,6 +11,7 @@
 WIRE = jnp.float16
 LARGEST_TOKEN, LARGEST_WEIGHT = 6.0, 0.0625
 VMEM_LIMIT = 20 * 2**20
+FORWARD_VMEM_LIMIT = 48 * 2**20
 NO_COST = pl.CostEstimate(flops=0, bytes_accessed=0, transcendentals=0)
 LONG = pl.CostEstimate(flops=6 * 10**9, bytes_accessed=0, transcendentals=0)
 SHARES = (5, 2)
@@ -64,7 +65,7 @@
             pltpu.VMEM((cores, width // tile, depth, 2 * tile), jnp.bfloat16),
             pltpu.SemaphoreType.DMA((2 * cores, width // tile)),
         ],
-        compiler_params=pltpu.CompilerParams(vmem_limit_bytes=VMEM_LIMIT),
+        compiler_params=pltpu.CompilerParams(vmem_limit_bytes=FORWARD_VMEM_LIMIT),
         cost_estimate=cost,
     )(place, *tokens, *weights)
 

time: 237 us -> 220 us (0.928)
  local copies, waits for them, and re-layouts: 33.8 us -> 15.5 us
  waiting for transfers between devices: 39.4 us -> 35.9 us
    unnamed x66 -> x54, local copies, waits for them, and re-layouts: 24.8 us -> 7.74 us
    ppermute x39, waiting for transfers between devices: 25.7 us -> 20.6 us  [send(): return lax.ppermute(value, 'col', route)]
    pallas_call x5, Pallas kernels: 19.7 us -> 23.3 us  [forward(): pl.pallas_call(functools.partial(forward_kernel, scale, start, cores), ou...]
    convert_element_type x2, other arithmetic: 5.26 us -> 1.73 us  [own_features(): payload = forward(other_tile, [tokens], *common).astype(wire)]
    ppermute x39, starting transfers between devices: 83.5 us -> 86.5 us  [send(): return lax.ppermute(value, 'col', route)]
    convert_element_type x3, other arithmetic: 0.59 us -> 3.32 us  [local(): far = add(take(tie(terms, near), 3), in_1).astype(WIRE)]
  transfers between devices with their start and end apart: 44 -> 44, of which waited for: 12 -> 11; matrix products, arithmetic and copies ran while one was open for 13% -> 14% of each run, Pallas kernels for 16% -> 18%
where the time goes in v18:
time: 220 us; the launch traced here: 219 us
  starting transfers between devices  90.2 us (41%)
  Pallas kernels  48 us (22%)
  waiting for transfers between devices  35.9 us (16%)
  other arithmetic  27.9 us (13%)
  local copies, waits for them, and re-layouts  15.5 us (7%)
    ppermute x39, starting transfers between devices, send(): return lax.ppermute(value, 'col', route)  86.5 us
    pallas_call x5, Pallas kernels, forward(): pl.pallas_call(functools.partial(forward_kernel, scale, start, cores), ou...  23.3 us
    pallas_call x4, Pallas kernels, gradient(): pl.pallas_call(functools.partial(gradient_kernel, len(acts)), out_shape=(...  20.9 us
    ppermute x39, waiting for transfers between devices, send(): return lax.ppermute(value, 'col', route)  20.6 us
    ppermute x1, waiting for transfers between devices, local(): over_depth = lax.ppermute(mine, 'depth', swap)  7.84 us
    unnamed x54, local copies, waits for them, and re-layouts  7.74 us
    ppermute x1, waiting for transfers between devices, local(): lax.ppermute(columns_of(cotangent, (1 - part) * half, half), 'depth', swap)  5.16 us
    convert_element_type x3, other arithmetic, local(): swapped = swapped.astype(WIRE)  5.03 us
  transfers between devices with their start and end apart: 44, of which 11 were waited for; matrix products, arithmetic and copies ran while one was open for 14% of the time, Pallas kernels for 18%

profile of v18, /device:TPU:1, one launch (start us, length us, event | category | flops | bytes accessed | tf_op | source)
XLA Modules:
  0.0 218.9 jit_solution(2157674349502497360)
XLA Ops:
  0.6 2.1 collective-permute-start.1
  2.8 1.2 collective-permute-start
  4.0 7.8 %collective-permute-done.1 = bf16[384,512]{1,0:T(8,128)(2,1)S(1)} collective-permute-done((bf16[384,512]{1,0:T(8,128)(2,1)}, bf16[384,512]{1,0:T(8,128)(2,1)S(1)}, u32[]{:S(2)}, u32[]{:S(2)}) %collective-permute-start.1) | collective-permute-done | bytes 393248 | tf_op jit(solution)/shard_map/ppermute | solution.py:214
  12.6 1.3 maximum_select_fusion
  14.2 4.2 %shard_map.67 = f32[4,2,96,1280]{3,2,1,0:T(8,128)S(1)} custom-call(s32[1]{0:T(128)} %bitcast.6.place_ref, bf16[384,1024]{1,0:T(8,128)(2,1)S(1)} %bitcast.154, bf16[1024,7168]{1,0:T(8,128)(2,1)} %refs_2_.9, bf16[1024,7168]{1,0:T(8,128)(2,1)} %refs_3_.1), custom_call_target="tpu_custom_call" | custom-call | tf_op jit(solution)/shard_map/pallas_call | solution.py:57
  18.4 1.5 convert_element_type.194
  19.9 1.9 collective-permute-start.2
  21.8 4.2 %shard_map.68 = f32[4,2,96,1280]{3,2,1,0:T(8,128)S(1)} custom-call(s32[1]{0:T(128)} %bitcast.1.place_ref, bf16[384,1024]{1,0:T(8,128)(2,1)S(1)} %bitcast.155, bf16[1024,7168]{1,0:T(8,128)(2,1)} %refs_2_.9, bf16[1024,7168]{1,0:T(8,128)(2,1)} %refs_3_.1), custom_call_target="tpu_custom_call" | custom-call | flops 6000000000 | tf_op jit(solution)/shard_map/pallas_call | solution.py:57
  26.9 4.1 %collective-permute-start.4 = (f16[2,96,1280]{2,1,0:T(8,128)(2,1)}, f16[2,96,1280]{2,1,0:T(8,128)(2,1)}, u32[]{:S(2)}, u32[]{:S(2)}) collective-permute-start(f16[2,96,1280]{2,1,0:T(8,128)(2,1)} %fusion.33), channel_id=1, source_target_pairs={{0,4},{2,6},{12,8},{14,10},{1,5},{3,7},{13,9},{15,11},{16,20},{18,... | collective-permute-start | bytes 1474568 | tf_op jit(solution)/shard_map/ppermute | solution.py:180
  31.0 1.5 collective-permute-done.3
  32.9 4.2 %shard_map.69 = f32[4,2,96,1280]{3,2,1,0:T(8,128)S(1)} custom-call(s32[1]{0:T(128)} %bitcast.6.place_ref, bf16[384,1024]{1,0:T(8,128)(2,1)S(1)} %bitcast.158, bf16[1024,7168]{1,0:T(8,128)(2,1)} %refs_2_.9, bf16[1024,7168]{1,0:T(8,128)(2,1)} %refs_3_.1), custom_call_target="tpu_custom_call" | custom-call | tf_op jit(solution)/shard_map/pallas_call | solution.py:57
  39.1 4.0 %collective-permute-start.7 = (f16[2,96,1280]{2,1,0:T(8,128)(2,1)}, f16[2,96,1280]{2,1,0:T(8,128)(2,1)}, u32[]{:S(2)}, u32[]{:S(2)}) collective-permute-start(f16[2,96,1280]{2,1,0:T(8,128)(2,1)} %fusion.30), channel_id=1, source_target_pairs={{0,4},{2,6},{12,8},{14,10},{1,5},{3,7},{13,9},{15,11},{16,20},{18,... | collective-permute-start | bytes 1474568 | tf_op jit(solution)/shard_map/ppermute | solution.py:180
  43.1 2.0 fusion.13
  45.1 1.4 collective-permute-start.8
  47.5 4.2 %shard_map.70 = f32[4,2,96,1280]{3,2,1,0:T(8,128)S(1)} custom-call(s32[1]{0:T(128)} %bitcast.1.place_ref, bf16[384,1024]{1,0:T(8,128)(2,1)S(1)} %bitcast.159, bf16[1024,7168]{1,0:T(8,128)(2,1)} %refs_2_.9, bf16[1024,7168]{1,0:T(8,128)(2,1)} %refs_3_.1), custom_call_target="tpu_custom_call" | custom-call | flops 6000000000 | tf_op jit(solution)/shard_map/pallas_call | solution.py:57
  51.7 5.2 %collective-permute-done.5 = bf16[48,3584]{1,0:T(8,128)(2,1)S(1)} collective-permute-done((bf16[48,3584]{1,0:T(8,128)(2,1)}, bf16[48,3584]{1,0:T(8,128)(2,1)S(1)}, u32[]{:S(2)}, u32[]{:S(2)}) %collective-permute-start.5) | collective-permute-done | bytes 344096 | tf_op jit(solution)/shard_map/ppermute | solution.py:314
  56.9 2.3 %fusion.8 = (f16[2,96,1280]{2,1,0:T(8,128)(2,1)S(1)}, f16[2,96,1280]{2,1,0:T(8,128)(2,1)S(1)}) fusion(f16[2,96,1280]{2,1,0:T(8,128)(2,1)} %collective-permute-done.8, f32[4,2,96,1280]{3,2,1,0:T(8,128)S(1)} %shard_map.68, pred[]{:T(512)S(6)} %or.3, f16[4,2,96,1280]{3,2,1,0:T(8,128)(2,1)S(1)} %collective-permute-done.2, ...), kind=kLoop, calls=%fused_computation.22 | loop fusion | flops 3194880 | bytes 6389761 | tf_op jit(solution)/shard_map/convert_element_type | solution.py:330
  59.2 1.3 collective-permute-start.11
  61.3 2.4 %collective-permute-start.9 = (bf16[2,48,1792]{2,1,0:T(8,128)(2,1)S(1)}, bf16[2,48,1792]{2,1,0:T(8,128)(2,1)S(1)}, u32[]{:S(2)}, u32[]{:S(2)}) collective-permute-start(bf16[2,48,1792]{2,1,0:T(8,128)(2,1)S(1)} %get-tuple-element.202), channel_id=1, source_target_pairs={{0,2},{2,0},{4,6},{6,4},{8,10},{10,8},{12,14},{14,12},{1,3},{3,1},... | collective-permute-start | bytes 1032200 | tf_op jit(solution)/shard_map/ppermute | solution.py:180
  64.6 5.2 %collective-permute-start.16 = (f16[2,96,1280]{2,1,0:T(8,128)(2,1)}, f16[2,96,1280]{2,1,0:T(8,128)(2,1)}, u32[]{:S(2)}, u32[]{:S(2)}) collective-permute-start(f16[2,96,1280]{2,1,0:T(8,128)(2,1)} %fusion.31), channel_id=1, source_target_pairs={{0,4},{2,6},{12,8},{14,10},{1,5},{3,7},{13,9},{15,11},{16,20},{18,... | collective-permute-start | bytes 1474568 | tf_op jit(solution)/shard_map/ppermute | solution.py:180
  69.9 1.7 dynamic-slice_bitcast_fusion
  76.2 2.2 %collective-permute-start.14 = (bf16[2,96,1280]{2,1,0:T(8,128)(2,1)S(1)}, bf16[2,96,1280]{2,1,0:T(8,128)(2,1)S(1)}, u32[]{:S(2)}, u32[]{:S(2)}) collective-permute-start(bf16[2,96,1280]{2,1,0:T(8,128)(2,1)S(1)} %pad_maximum_fusion.2.act), channel_id=1, source_target_pairs={{0,4},{2,6},{12,8},{14,10},{4,0},{6,2},{8,12},{10,14},{1,5},{3,7},... | collective-permute-start | bytes 1474568 | tf_op jit(solution)/shard_map/ppermute | solution.py:180
  78.6 1.3 copy-done.2
  80.0 1.6 copy-done.3
  81.5 6.7 %shard_map.71 = f32[4,2,192,512]{3,2,1,0:T(8,128)} custom-call(s32[1]{0:T(128)} %bitcast.1.place_ref, bf16[768,1024]{1,0:T(8,128)(2,1)S(1)} %bitcast.163, bf16[768,1024]{1,0:T(8,128)(2,1)S(1)} %bitcast.164, bf16[1024,7168]{1,0:T(8,128)(2,1)} %refs_2_.9, bf16[1024,7168]{1,0:T(8,128)(2,1)} %refs_3_.1, bf16[2,1024,512]{2,1,0:T(8,128)(2,1)S(1)} %copy-done.3, ...), custom_call_target="tpu_custom_call" | custom-call | tf_op jit(solution)/shard_map/pallas_call | solution.py:57
  90.3 3.3 %collective-permute-start.19 = (f16[2,96,1280]{2,1,0:T(8,128)(2,1)S(1)}, f16[2,96,1280]{2,1,0:T(8,128)(2,1)S(1)}, u32[]{:S(2)}, u32[]{:S(2)}) collective-permute-start(f16[2,96,1280]{2,1,0:T(8,128)(2,1)S(1)} %fusion.32), channel_id=1, source_target_pairs={{0,4},{2,6},{12,8},{14,10},{1,5},{3,7},{13,9},{15,11},{16,20},{18,... | collective-permute-start | bytes 1474568 | tf_op jit(solution)/shard_map/ppermute | solution.py:180
  94.4 1.3 collective-permute-start.17
  95.7 5.0 %collective-permute-done.19 = f16[2,96,1280]{2,1,0:T(8,128)(2,1)S(1)} collective-permute-done((f16[2,96,1280]{2,1,0:T(8,128)(2,1)S(1)}, f16[2,96,1280]{2,1,0:T(8,128)(2,1)S(1)}, u32[]{:S(2)}, u32[]{:S(2)}) %collective-permute-start.19) | collective-permute-done | bytes 491552 | tf_op jit(solution)/shard_map/ppermute | solution.py:180
  100.7 1.4 fusion.4
  102.1 2.2 %collective-permute-start.22 = (f16[2,96,1280]{2,1,0:T(8,128)(2,1)}, f16[2,96,1280]{2,1,0:T(8,128)(2,1)}, u32[]{:S(2)}, u32[]{:S(2)}) collective-permute-start(f16[2,96,1280]{2,1,0:T(8,128)(2,1)} %get-tuple-element.179), channel_id=1, source_target_pairs={{0,4},{2,6},{12,8},{14,10},{4,0},{6,2},{8,12},{10,14},{1,5},{3,7},... | collective-permute-start | bytes 1474568 | tf_op jit(solution)/shard_map/ppermute | solution.py:180
  104.3 1.4 collective-permute-start.23
  105.7 1.3 collective-permute-start.21
  109.4 1.6 maximum_bitcast_fusion.features_ref
  112.3 7.5 %collective-permute-start.26 = (f16[2,192,512]{2,1,0:T(8,128)(2,1)S(1)}, f16[2,192,512]{2,1,0:T(8,128)(2,1)S(1)}, u32[]{:S(2)}, u32[]{:S(2)}) collective-permute-start(f16[2,192,512]{2,1,0:T(8,128)(2,1)S(1)} %fusion.39), channel_id=1, source_target_pairs={{0,4},{2,6},{12,8},{14,10},{1,5},{3,7},{13,9},{15,11},{16,20},{18,... | collective-permute-start | bytes 1179656 | tf_op jit(solution)/shard_map/ppermute | solution.py:180
  119.8 1.9 fusion.2
  122.9 1.5 collective-permute-start.25
  124.4 3.1 %collective-permute-start.24 = (bf16[2,96,1280]{2,1,0:T(8,128)(2,1)S(1)}, bf16[2,96,1280]{2,1,0:T(8,128)(2,1)}, u32[]{:S(2)}, u32[]{:S(2)}) collective-permute-start(bf16[2,96,1280]{2,1,0:T(8,128)(2,1)S(1)} %pad_maximum_fusion.3.act), channel_id=1, source_target_pairs={{0,4},{2,6},{12,8},{14,10},{4,0},{6,2},{8,12},{10,14},{1,5},{3,7},... | collective-permute-start | bytes 1474568 | tf_op jit(solution)/shard_map/ppermute | solution.py:180
  129.6 1.6 copy-done.18
  132.1 4.0 %collective-permute-start.29 = (f16[2,192,512]{2,1,0:T(8,128)(2,1)S(1)}, f16[2,192,512]{2,1,0:T(8,128)(2,1)S(1)}, u32[]{:S(2)}, u32[]{:S(2)}) collective-permute-start(f16[2,192,512]{2,1,0:T(8,128)(2,1)S(1)} %fusion.40), channel_id=1, source_target_pairs={{0,4},{2,6},{12,8},{14,10},{1,5},{3,7},{13,9},{15,11},{16,20},{18,... | collective-permute-start | bytes 1179656 | tf_op jit(solution)/shard_map/ppermute | solution.py:180
  137.1 1.5 collective-permute-start.28
  138.6 1.3 collective-permute-start.27
  139.9 5.7 %collective-permute-done.29 = f16[2,192,512]{2,1,0:T(8,128)(2,1)S(1)} collective-permute-done((f16[2,192,512]{2,1,0:T(8,128)(2,1)S(1)}, f16[2,192,512]{2,1,0:T(8,128)(2,1)S(1)}, u32[]{:S(2)}, u32[]{:S(2)}) %collective-permute-start.29) | collective-permute-done | bytes 393248 | tf_op jit(solution)/shard_map/ppermute | solution.py:180
  145.5 1.3 fusion.16
  146.8 2.3 %collective-permute-start.31 = (f16[2,192,512]{2,1,0:T(8,128)(2,1)}, f16[2,192,512]{2,1,0:T(8,128)(2,1)}, u32[]{:S(2)}, u32[]{:S(2)}) collective-permute-start(f16[2,192,512]{2,1,0:T(8,128)(2,1)} %get-tuple-element.183), channel_id=1, source_target_pairs={{0,4},{2,6},{12,8},{14,10},{4,0},{6,2},{8,12},{10,14},{1,5},{3,7},... | collective-permute-start | bytes 1179656 | tf_op jit(solution)/shard_map/ppermute | solution.py:180
  149.1 1.4 collective-permute-start.32
  151.6 1.3 collective-permute-start.36
  152.9 2.6 %collective-permute-done.31 = f16[2,192,512]{2,1,0:T(8,128)(2,1)} collective-permute-done((f16[2,192,512]{2,1,0:T(8,128)(2,1)}, f16[2,192,512]{2,1,0:T(8,128)(2,1)}, u32[]{:S(2)}, u32[]{:S(2)}) %collective-permute-start.31) | collective-permute-done | bytes 393248 | tf_op jit(solution)/shard_map/ppermute | solution.py:180
  155.5 1.8 fusion.18
  158.4 1.4 collective-permute-start.34
  159.8 9.6 %collective-permute-start.33 = (bf16[2,192,512]{2,1,0:T(8,128)(2,1)}, bf16[2,192,512]{2,1,0:T(8,128)(2,1)}, u32[]{:S(2)}, u32[]{:S(2)}) collective-permute-start(bf16[2,192,512]{2,1,0:T(8,128)(2,1)} %pad_maximum_fusion.4.act), channel_id=1, source_target_pairs={{0,4},{2,6},{12,8},{14,10},{4,0},{6,2},{8,12},{10,14},{1,5},{3,7},... | collective-permute-start | bytes 1179656 | tf_op jit(solution)/shard_map/ppermute | solution.py:180
  170.5 7.9 %collective-permute-start.35 = (bf16[2,48,1792]{2,1,0:T(8,128)(2,1)}, bf16[2,48,1792]{2,1,0:T(8,128)(2,1)}, u32[]{:S(2)}, u32[]{:S(2)}) collective-permute-start(bf16[2,48,1792]{2,1,0:T(8,128)(2,1)} %get-tuple-element.198), channel_id=1, source_target_pairs={{0,2},{2,0},{4,6},{6,4},{8,10},{10,8},{12,14},{14,12},{1,3},{3,1},... | collective-permute-start | bytes 1032200 | tf_op jit(solution)/shard_map/ppermute | solution.py:180
  178.4 2.1 collective-permute-done.35
  181.5 2.0 shard_map.73
  183.9 1.3 collective-permute-start.37
  185.9 1.2 maximum_select_fusion.3
  187.4 7.0 %shard_map.74 = (f32[1024,3584]{1,0:T(8,128)}, f32[1024,3584]{1,0:T(8,128)}) custom-call(s32[1]{0:T(128)} %bitcast.59.place_ref, bf16[1024,768]{1,0:T(8,128)(2,1)S(1)} %maximum_bitcast_fusion.features_ref, bf16[4,1,2,96,1280]{4,3,2,1,0:T(8,128)(2,1)S(1)} %bitcast.165, bf16[4,1,2,96,1280]{4,3,2,1,0:T(8,128)(2,1)S(1)} %bitcast.167), custom_call_target="tpu_custom_call" | custom-call | flops 4026531840 | bytes 15990784 | tf_op jit(solution)/shard_map/pallas_call | solution.py:101
  194.4 1.7 collective-permute-done.37.out_2
  196.1 1.5 collective-permute-start.39
  198.6 7.0 %shard_map.75 = (f32[1024,3584]{1,0:T(8,128)}, f32[1024,3584]{1,0:T(8,128)}) custom-call(s32[1]{0:T(128)} %bitcast.62.place_ref, bf16[1024,768]{1,0:T(8,128)(2,1)S(1)} %maximum_bitcast_fusion.features_ref, bf16[4,1,2,96,1280]{4,3,2,1,0:T(8,128)(2,1)S(1)} %bitcast.166, ...), custom_call_target="tpu_custom_call", output_to_operand_aliasing={{0}: (4, {}), {1}: (5, {})} | custom-call | flops 4026531840 | bytes 15990784 | tf_op jit(solution)/shard_map/pallas_call | solution.py:101
  205.7 2.4 %collective-permute-done.39.out_3 = bf16[2,192,512]{2,1,0:T(8,128)(2,1)S(1)} collective-permute-done((bf16[2,192,512]{2,1,0:T(8,128)(2,1)S(1)}, bf16[2,192,512]{2,1,0:T(8,128)(2,1)S(1)}, u32[]{:S(2)}, u32[]{:S(2)}) %collective-permute-start.39) | collective-permute-done | bytes 393248 | tf_op jit(solution)/shard_map/ppermute | solution.py:180
  208.1 1.5 shard_map.76
  209.6 2.5 %collective-permute-start.43 = (bf16[4,2,192,512]{3,2,1,0:T(8,128)(2,1)S(1)}, bf16[4,2,192,512]{3,2,1,0:T(8,128)(2,1)S(1)}, u32[]{:S(2)}, u32[]{:S(2)}) collective-permute-start(bf16[4,2,192,512]{3,2,1,0:T(8,128)(2,1)S(1)} %shard_map.76), channel_id=1, source_target_pairs={{0,2},{2,0},{4,6},{6,4},{8,10},{10,8},{12,14},{14,12},{1,3},{3,1},... | collective-permute-start | bytes 4718600 | tf_op jit(solution)/shard_map/ppermute | solution.py:180
  212.1 3.4 %shard_map.77 = (f32[1024,3584]{1,0:T(8,128)}, f32[1024,3584]{1,0:T(8,128)}) custom-call(s32[1]{0:T(128)} %bitcast.59.place_ref, bf16[1024,768]{1,0:T(8,128)(2,1)S(1)} %maximum_bitcast_fusion.features_ref, bf16[4,1,2,192,512]{4,3,2,1,0:T(8,128)(2,1)S(1)} %bitcast.162, ...), custom_call_target="tpu_custom_call", output_to_operand_aliasing={{0}: (3, {}), {1}: (4, {})} | custom-call | flops 1610612736 | bytes 7340032 | tf_op jit(solution)/shard_map/pallas_call | solution.py:101
  215.5 3.4 %shard_map.78 = (f32[1024,3584]{1,0:T(8,128)}, f32[1024,3584]{1,0:T(8,128)}) custom-call(s32[1]{0:T(128)} %bitcast.62.place_ref, bf16[1024,768]{1,0:T(8,128)(2,1)S(1)} %maximum_bitcast_fusion.features_ref, bf16[4,1,2,192,512]{4,3,2,1,0:T(8,128)(2,1)S(1)} %bitcast.169, ...), custom_call_target="tpu_custom_call", output_to_operand_aliasing={{0}: (3, {}), {1}: (4, {})} | custom-call | flops 1610612736 | bytes 7340032 | tf_op jit(solution)/shard_map/pallas_call | solution.py:101
  (138 shorter events, 29.7 us)
Async XLA Ops:
  0.6 11.2 %collective-permute-start.1 = (bf16[384,512]{1,0:T(8,128)(2,1)}, bf16[384,512]{1,0:T(8,128)(2,1)S(1)}, u32[]{:S(2)}, u32[]{:S(2)}) collective-permute-start(bf16[384,512]{1,0:T(8,128)(2,1)} %bitcast.177), channel_id=1, source_target_pairs={{0,1},{1,0},{2,3},{3,2},{4,5},{5,4},{6,7},{7,6},{8,9},{9,8},{10,11... | collective-permute-start | bytes 1179656 | tf_op jit(solution)/shard_map/ppermute | solution.py:214
  2.8 9.9 %collective-permute-start = (bf16[384,512]{1,0:T(8,128)(2,1)}, bf16[384,512]{1,0:T(8,128)(2,1)S(1)}, u32[]{:S(2)}, u32[]{:S(2)}) collective-permute-start(bf16[384,512]{1,0:T(8,128)(2,1)} %bitcast.178), channel_id=1, source_target_pairs={{0,16},{16,0},{1,17},{17,1},{2,18},{18,2},{3,19},{19,3},{4,20},{20... | collective-permute-start | bytes 1179656 | tf_op jit(solution)/shard_map/ppermute | solution.py:213
  19.9 6.1 %collective-permute-start.2 = (f16[4,2,96,1280]{3,2,1,0:T(8,128)(2,1)}, f16[4,2,96,1280]{3,2,1,0:T(8,128)(2,1)S(1)}, u32[]{:S(2)}, u32[]{:S(2)}) collective-permute-start(f16[4,2,96,1280]{3,2,1,0:T(8,128)(2,1)} %convert_element_type.194), channel_id=1, source_target_pairs={{0,2},{2,0},{4,6},{6,4},{8,10},{10,8},{12,14},{14,12},{1,3},{3,1},... | collective-permute-start | bytes 5898248 | tf_op jit(solution)/shard_map/ppermute | solution.py:180
  21.7 10.7 %collective-permute-start.3 = (bf16[384,512]{1,0:T(8,128)(2,1)S(1)}, bf16[384,512]{1,0:T(8,128)(2,1)S(1)}, u32[]{:S(2)}, u32[]{:S(2)}) collective-permute-start(bf16[384,512]{1,0:T(8,128)(2,1)S(1)} %collective-permute-done), channel_id=1, source_target_pairs={{0,1},{1,0},{2,3},{3,2},{4,5},{5,4},{6,7},{7,6},{8,9},{9,8},{10,11... | collective-permute-start | bytes 1179656 | tf_op jit(solution)/shard_map/ppermute | solution.py:215
  26.9 16.2 %collective-permute-start.4 = (f16[2,96,1280]{2,1,0:T(8,128)(2,1)}, f16[2,96,1280]{2,1,0:T(8,128)(2,1)}, u32[]{:S(2)}, u32[]{:S(2)}) collective-permute-start(f16[2,96,1280]{2,1,0:T(8,128)(2,1)} %fusion.33), channel_id=1, source_target_pairs={{0,4},{2,6},{12,8},{14,10},{1,5},{3,7},{13,9},{15,11},{16,20},{18,... | collective-permute-start | bytes 1474568 | tf_op jit(solution)/shard_map/ppermute | solution.py:180
  37.3 9.2 %copy-start.26 = (bf16[1,48,7168]{2,1,0:T(8,128)(2,1)S(1)}, bf16[1,48,7168]{2,1,0:T(8,128)(2,1)}, u32[]{:S(2)}) copy-start(bf16[1,48,7168]{2,1,0:T(8,128)(2,1)} %param.7) | copy-start | bytes 2064388
  37.3 19.5 %collective-permute-start.6 = (f16[4,2,96,1280]{3,2,1,0:T(8,128)(2,1)S(1)}, f16[4,2,96,1280]{3,2,1,0:T(8,128)(2,1)S(1)}, u32[]{:S(2)}, u32[]{:S(2)}) collective-permute-start(f16[4,2,96,1280]{3,2,1,0:T(8,128)(2,1)S(1)} %convert_element_type.198), channel_id=1, source_target_pairs={{0,2},{2,0},{4,6},{6,4},{8,10},{10,8},{12,14},{14,12},{1,3},{3,1},... | collective-permute-start | bytes 5898248 | tf_op jit(solution)/shard_map/ppermute | solution.py:180
  39.1 17.8 %collective-permute-start.7 = (f16[2,96,1280]{2,1,0:T(8,128)(2,1)}, f16[2,96,1280]{2,1,0:T(8,128)(2,1)}, u32[]{:S(2)}, u32[]{:S(2)}) collective-permute-start(f16[2,96,1280]{2,1,0:T(8,128)(2,1)} %fusion.30), channel_id=1, source_target_pairs={{0,4},{2,6},{12,8},{14,10},{1,5},{3,7},{13,9},{15,11},{16,20},{18,... | collective-permute-start | bytes 1474568 | tf_op jit(solution)/shard_map/ppermute | solution.py:180
  45.1 11.8 %collective-permute-start.8 = (f16[2,96,1280]{2,1,0:T(8,128)(2,1)}, f16[2,96,1280]{2,1,0:T(8,128)(2,1)}, u32[]{:S(2)}, u32[]{:S(2)}) collective-permute-start(f16[2,96,1280]{2,1,0:T(8,128)(2,1)} %fusion.13), channel_id=1, source_target_pairs={{4,8},{6,10},{8,4},{10,6},{5,9},{7,11},{9,5},{11,7},{20,24},{22,26... | collective-permute-start | bytes 1474568 | tf_op jit(solution)/shard_map/ppermute | solution.py:180
  47.3 9.6 %collective-permute-start.5 = (bf16[48,3584]{1,0:T(8,128)(2,1)}, bf16[48,3584]{1,0:T(8,128)(2,1)S(1)}, u32[]{:S(2)}, u32[]{:S(2)}) collective-permute-start(bf16[48,3584]{1,0:T(8,128)(2,1)} %get-tuple-element.203), channel_id=1, source_target_pairs={{0,1},{1,0},{2,3},{3,2},{4,5},{5,4},{6,7},{7,6},{8,9},{9,8},{10,11... | collective-permute-start | bytes 1032200 | tf_op jit(solution)/shard_map/ppermute | solution.py:314
  51.7 49.0 %copy-start = (f32[4,2,96,1280]{3,2,1,0:T(8,128)}, f32[4,2,96,1280]{3,2,1,0:T(8,128)S(1)}, u32[]{:S(2)}) copy-start(f32[4,2,96,1280]{3,2,1,0:T(8,128)S(1)} %shard_map.70) | copy-start | bytes 11796484
  56.9 6.8 %copy-start.19 = (f16[4,2,96,1280]{3,2,1,0:T(8,128)(2,1)}, f16[4,2,96,1280]{3,2,1,0:T(8,128)(2,1)S(1)}, u32[]{:S(2)}) copy-start(f16[4,2,96,1280]{3,2,1,0:T(8,128)(2,1)S(1)} %collective-permute-done.6) | copy-start | bytes 5898244
  59.2 14.3 %collective-permute-start.11 = (f16[2,96,1280]{2,1,0:T(8,128)(2,1)S(1)}, f16[2,96,1280]{2,1,0:T(8,128)(2,1)S(1)}, u32[]{:S(2)}, u32[]{:S(2)}) collective-permute-start(f16[2,96,1280]{2,1,0:T(8,128)(2,1)S(1)} %get-tuple-element.181), channel_id=1, source_target_pairs={{0,4},{2,6},{12,8},{14,10},{4,0},{6,2},{8,12},{10,14},{1,5},{3,7},... | collective-permute-start | bytes 1474568 | tf_op jit(solution)/shard_map/ppermute | solution.py:180
  60.6 12.9 %collective-permute-start.12 = (f16[2,96,1280]{2,1,0:T(8,128)(2,1)S(1)}, f16[2,96,1280]{2,1,0:T(8,128)(2,1)S(1)}, u32[]{:S(2)}, u32[]{:S(2)}) collective-permute-start(f16[2,96,1280]{2,1,0:T(8,128)(2,1)S(1)} %get-tuple-element.182), channel_id=1, source_target_pairs={{4,8},{6,10},{8,4},{10,6},{5,9},{7,11},{9,5},{11,7},{20,24},{22,26... | collective-permute-start | bytes 1474568 | tf_op jit(solution)/shard_map/ppermute | solution.py:180
  61.3 11.0 %collective-permute-start.9 = (bf16[2,48,1792]{2,1,0:T(8,128)(2,1)S(1)}, bf16[2,48,1792]{2,1,0:T(8,128)(2,1)S(1)}, u32[]{:S(2)}, u32[]{:S(2)}) collective-permute-start(bf16[2,48,1792]{2,1,0:T(8,128)(2,1)S(1)} %get-tuple-element.202), channel_id=1, source_target_pairs={{0,2},{2,0},{4,6},{6,4},{8,10},{10,8},{12,14},{14,12},{1,3},{3,1},... | collective-permute-start | bytes 1032200 | tf_op jit(solution)/shard_map/ppermute | solution.py:180
  64.6 23.6 %collective-permute-start.16 = (f16[2,96,1280]{2,1,0:T(8,128)(2,1)}, f16[2,96,1280]{2,1,0:T(8,128)(2,1)}, u32[]{:S(2)}, u32[]{:S(2)}) collective-permute-start(f16[2,96,1280]{2,1,0:T(8,128)(2,1)} %fusion.31), channel_id=1, source_target_pairs={{0,4},{2,6},{12,8},{14,10},{1,5},{3,7},{13,9},{15,11},{16,20},{18,... | collective-permute-start | bytes 1474568 | tf_op jit(solution)/shard_map/ppermute | solution.py:180
  71.8 6.9 %collective-permute-start.13 = (bf16[2,1024,512]{2,1,0:T(8,128)(2,1)S(1)}, bf16[2,1024,512]{2,1,0:T(8,128)(2,1)S(1)}, u32[]{:S(2)}, u32[]{:S(2)}) collective-permute-start(bf16[2,1024,512]{2,1,0:T(8,128)(2,1)S(1)} %pad_maximum_fusion), channel_id=1, source_target_pairs={{0,2},{2,0},{4,6},{6,4},{8,10},{10,8},{12,14},{14,12},{1,3},{3,1},... | collective-permute-start | bytes 6291464 | tf_op jit(solution)/shard_map/ppermute | solution.py:180
  72.3 6.1 %collective-permute-start.10 = (bf16[4,2,96,1024]{3,2,0,1:T(8,128)(2,1)S(1)}, bf16[4,2,96,1024]{3,2,0,1:T(8,128)(2,1)S(1)}, u32[]{:S(2)}, u32[]{:S(2)}) collective-permute-start(bf16[4,2,96,1024]{3,2,0,1:T(8,128)(2,1)S(1)} %pad_maximum_fusion.1), channel_id=1, source_target_pairs={{0,2},{2,0},{4,6},{6,4},{8,10},{10,8},{12,14},{14,12},{1,3},{3,1},... | collective-permute-start | bytes 4718600 | tf_op jit(solution)/shard_map/ppermute | solution.py:180
  75.3 3.4 %copy-start.6 = (bf16[2,96,1280]{2,1,0:T(8,128)(2,1)}, bf16[2,96,1280]{2,1,0:T(8,128)(2,1)S(1)}, u32[]{:S(2)}) copy-start(bf16[2,96,1280]{2,1,0:T(8,128)(2,1)S(1)} %pad_maximum_fusion.2.act) | copy-start | bytes 1474564
  75.3 18.4 %collective-permute-start.15 = (bf16[2,96,1280]{2,1,0:T(8,128)(2,1)S(1)}, bf16[2,96,1280]{2,1,0:T(8,128)(2,1)S(1)}, u32[]{:S(2)}, u32[]{:S(2)}) collective-permute-start(bf16[2,96,1280]{2,1,0:T(8,128)(2,1)S(1)} %pad_maximum_fusion.2.act), channel_id=1, source_target_pairs={{4,8},{6,10},{8,4},{10,6},{5,9},{7,11},{9,5},{11,7},{20,24},{22,26... | collective-permute-start | bytes 1474568 | tf_op jit(solution)/shard_map/ppermute | solution.py:180
  76.2 17.5 %collective-permute-start.14 = (bf16[2,96,1280]{2,1,0:T(8,128)(2,1)S(1)}, bf16[2,96,1280]{2,1,0:T(8,128)(2,1)S(1)}, u32[]{:S(2)}, u32[]{:S(2)}) collective-permute-start(bf16[2,96,1280]{2,1,0:T(8,128)(2,1)S(1)} %pad_maximum_fusion.2.act), channel_id=1, source_target_pairs={{0,4},{2,6},{12,8},{14,10},{4,0},{6,2},{8,12},{10,14},{1,5},{3,7},... | collective-permute-start | bytes 1474568 | tf_op jit(solution)/shard_map/ppermute | solution.py:180
  81.5 6.7 %copy-start.20 = (f16[4,2,96,1280]{3,2,1,0:T(8,128)(2,1)S(1)}, f16[4,2,96,1280]{3,2,1,0:T(8,128)(2,1)}, u32[]{:S(2)}) copy-start(f16[4,2,96,1280]{3,2,1,0:T(8,128)(2,1)} %copy-done.19) | copy-start | bytes 5898244
  89.6 6.1 %collective-permute-start.20 = (f16[2,96,1280]{2,1,0:T(8,128)(2,1)S(1)}, f16[2,96,1280]{2,1,0:T(8,128)(2,1)S(1)}, u32[]{:S(2)}, u32[]{:S(2)}) collective-permute-start(f16[2,96,1280]{2,1,0:T(8,128)(2,1)S(1)} %fusion.6), channel_id=1, source_target_pairs={{4,8},{6,10},{8,4},{10,6},{5,9},{7,11},{9,5},{11,7},{20,24},{22,26... | collective-permute-start | bytes 1474568 | tf_op jit(solution)/shard_map/ppermute | solution.py:180
  90.3 10.4 %collective-permute-start.19 = (f16[2,96,1280]{2,1,0:T(8,128)(2,1)S(1)}, f16[2,96,1280]{2,1,0:T(8,128)(2,1)S(1)}, u32[]{:S(2)}, u32[]{:S(2)}) collective-permute-start(f16[2,96,1280]{2,1,0:T(8,128)(2,1)S(1)} %fusion.32), channel_id=1, source_target_pairs={{0,4},{2,6},{12,8},{14,10},{1,5},{3,7},{13,9},{15,11},{16,20},{18,... | collective-permute-start | bytes 1474568 | tf_op jit(solution)/shard_map/ppermute | solution.py:180
  93.6 8.5 %copy-start.8 = (bf16[2,96,1280]{2,1,0:T(8,128)(2,1)}, bf16[2,96,1280]{2,1,0:T(8,128)(2,1)S(1)}, u32[]{:S(2)}) copy-start(bf16[2,96,1280]{2,1,0:T(8,128)(2,1)S(1)} %collective-permute-done.15.centre_1) | copy-start | bytes 1474564
  93.7 8.4 %copy-start.10 = (bf16[2,96,1280]{2,1,0:T(8,128)(2,1)}, bf16[2,96,1280]{2,1,0:T(8,128)(2,1)S(1)}, u32[]{:S(2)}) copy-start(bf16[2,96,1280]{2,1,0:T(8,128)(2,1)S(1)} %collective-permute-done.14.side_1) | copy-start | bytes 1474564
  93.7 12.1 %collective-permute-start.18 = (bf16[2,96,1280]{2,1,0:T(8,128)(2,1)S(1)}, bf16[2,96,1280]{2,1,0:T(8,128)(2,1)S(1)}, u32[]{:S(2)}, u32[]{:S(2)}) collective-permute-start(bf16[2,96,1280]{2,1,0:T(8,128)(2,1)S(1)} %collective-permute-done.14.side_1), channel_id=1, source_target_pairs={{4,8},{6,10},{8,4},{10,6},{5,9},{7,11},{9,5},{11,7},{20,24},{22,26... | collective-permute-start | bytes 1474568 | tf_op jit(solution)/shard_map/ppermute | solution.py:180
  94.4 11.4 %collective-permute-start.17 = (bf16[2,96,1280]{2,1,0:T(8,128)(2,1)S(1)}, bf16[2,96,1280]{2,1,0:T(8,128)(2,1)S(1)}, u32[]{:S(2)}, u32[]{:S(2)}) collective-permute-start(bf16[2,96,1280]{2,1,0:T(8,128)(2,1)S(1)} %collective-permute-done.15.centre_1), channel_id=1, source_target_pairs={{4,0},{6,2},{8,12},{10,14},{5,1},{7,3},{9,13},{11,15},{20,16},{22,... | collective-permute-start | bytes 1474568 | tf_op jit(solution)/shard_map/ppermute | solution.py:180
  102.1 17.7 %collective-permute-start.22 = (f16[2,96,1280]{2,1,0:T(8,128)(2,1)}, f16[2,96,1280]{2,1,0:T(8,128)(2,1)}, u32[]{:S(2)}, u32[]{:S(2)}) collective-permute-start(f16[2,96,1280]{2,1,0:T(8,128)(2,1)} %get-tuple-element.179), channel_id=1, source_target_pairs={{0,4},{2,6},{12,8},{14,10},{4,0},{6,2},{8,12},{10,14},{1,5},{3,7},... | collective-permute-start | bytes 1474568 | tf_op jit(solution)/shard_map/ppermute | solution.py:180
  104.3 15.5 %collective-permute-start.23 = (f16[2,96,1280]{2,1,0:T(8,128)(2,1)}, f16[2,96,1280]{2,1,0:T(8,128)(2,1)}, u32[]{:S(2)}, u32[]{:S(2)}) collective-permute-start(f16[2,96,1280]{2,1,0:T(8,128)(2,1)} %get-tuple-element.180), channel_id=1, source_target_pairs={{4,8},{6,10},{8,4},{10,6},{5,9},{7,11},{9,5},{11,7},{20,24},{22,26... | collective-permute-start | bytes 1474568 | tf_op jit(solution)/shard_map/ppermute | solution.py:180
  105.7 5.3 %copy-start.12 = (bf16[2,96,1280]{2,1,0:T(8,128)(2,1)}, bf16[2,96,1280]{2,1,0:T(8,128)(2,1)S(1)}, u32[]{:S(2)}) copy-start(bf16[2,96,1280]{2,1,0:T(8,128)(2,1)S(1)} %collective-permute-done.18.share_2) | copy-start | bytes 1474564
  105.7 5.3 %copy-start.14 = (bf16[2,96,1280]{2,1,0:T(8,128)(2,1)}, bf16[2,96,1280]{2,1,0:T(8,128)(2,1)S(1)}, u32[]{:S(2)}) copy-start(bf16[2,96,1280]{2,1,0:T(8,128)(2,1)S(1)} %collective-permute-done.17.out_2) | copy-start | bytes 1474564
  105.7 21.7 %collective-permute-start.21 = (bf16[2,96,1280]{2,1,0:T(8,128)(2,1)S(1)}, bf16[2,96,1280]{2,1,0:T(8,128)(2,1)S(1)}, u32[]{:S(2)}, u32[]{:S(2)}) collective-permute-start(bf16[2,96,1280]{2,1,0:T(8,128)(2,1)S(1)} %collective-permute-done.18.share_2), channel_id=1, source_target_pairs={{4,0},{6,2},{8,12},{10,14},{5,1},{7,3},{9,13},{11,15},{20,16},{22,... | collective-permute-start | bytes 1474568 | tf_op jit(solution)/shard_map/ppermute | solution.py:180
  109.4 10.4 %copy-start.1 = (f32[4,2,96,1280]{3,2,1,0:T(8,128)S(1)}, f32[4,2,96,1280]{3,2,1,0:T(8,128)}, u32[]{:S(2)}) copy-start(f32[4,2,96,1280]{3,2,1,0:T(8,128)} %copy-done) | copy-start | bytes 11796484
  112.2 9.6 %copy-start.22 = (bf16[96,1792]{1,0:T(8,128)(2,1)S(1)}, bf16[96,1792]{1,0:T(8,128)(2,1)}, u32[]{:S(2)}) copy-start(bf16[96,1792]{1,0:T(8,128)(2,1)} %get-tuple-element.200) | copy-start | bytes 1032196
  112.3 17.4 %collective-permute-start.26 = (f16[2,192,512]{2,1,0:T(8,128)(2,1)S(1)}, f16[2,192,512]{2,1,0:T(8,128)(2,1)S(1)}, u32[]{:S(2)}, u32[]{:S(2)}) collective-permute-start(f16[2,192,512]{2,1,0:T(8,128)(2,1)S(1)} %fusion.39), channel_id=1, source_target_pairs={{0,4},{2,6},{12,8},{14,10},{1,5},{3,7},{13,9},{15,11},{16,20},{18,... | collective-permute-start | bytes 1179656 | tf_op jit(solution)/shard_map/ppermute | solution.py:180
  121.8 6.5 %copy-start.7 = (bf16[2,96,1280]{2,1,0:T(8,128)(2,1)S(1)}, bf16[2,96,1280]{2,1,0:T(8,128)(2,1)}, u32[]{:S(2)}) copy-start(bf16[2,96,1280]{2,1,0:T(8,128)(2,1)} %copy-done.6) | copy-start | bytes 1474564
  121.8 6.4 %copy-start.9 = (bf16[2,96,1280]{2,1,0:T(8,128)(2,1)S(1)}, bf16[2,96,1280]{2,1,0:T(8,128)(2,1)}, u32[]{:S(2)}) copy-start(bf16[2,96,1280]{2,1,0:T(8,128)(2,1)} %copy-done.8) | copy-start | bytes 1474564
  121.8 6.4 %copy-start.11 = (bf16[2,96,1280]{2,1,0:T(8,128)(2,1)S(1)}, bf16[2,96,1280]{2,1,0:T(8,128)(2,1)}, u32[]{:S(2)}) copy-start(bf16[2,96,1280]{2,1,0:T(8,128)(2,1)} %copy-done.10) | copy-start | bytes 1474564
  121.8 6.4 %copy-start.13 = (bf16[2,96,1280]{2,1,0:T(8,128)(2,1)S(1)}, bf16[2,96,1280]{2,1,0:T(8,128)(2,1)}, u32[]{:S(2)}) copy-start(bf16[2,96,1280]{2,1,0:T(8,128)(2,1)} %copy-done.12) | copy-start | bytes 1474564
  121.8 6.4 %copy-start.15 = (bf16[2,96,1280]{2,1,0:T(8,128)(2,1)S(1)}, bf16[2,96,1280]{2,1,0:T(8,128)(2,1)}, u32[]{:S(2)}) copy-start(bf16[2,96,1280]{2,1,0:T(8,128)(2,1)} %copy-done.14) | copy-start | bytes 1474564
  122.9 6.7 %copy-start.4 = (bf16[2,96,1280]{2,1,0:T(8,128)(2,1)}, bf16[2,96,1280]{2,1,0:T(8,128)(2,1)S(1)}, u32[]{:S(2)}) copy-start(bf16[2,96,1280]{2,1,0:T(8,128)(2,1)S(1)} %pad_maximum_fusion.3.act) | copy-start | bytes 1474564
  122.9 13.2 %collective-permute-start.25 = (bf16[2,96,1280]{2,1,0:T(8,128)(2,1)S(1)}, bf16[2,96,1280]{2,1,0:T(8,128)(2,1)}, u32[]{:S(2)}, u32[]{:S(2)}) collective-permute-start(bf16[2,96,1280]{2,1,0:T(8,128)(2,1)S(1)} %pad_maximum_fusion.3.act), channel_id=1, source_target_pairs={{4,8},{6,10},{8,4},{10,6},{5,9},{7,11},{9,5},{11,7},{20,24},{22,26... | collective-permute-start | bytes 1474568 | tf_op jit(solution)/shard_map/ppermute | solution.py:180
  124.4 12.8 %collective-permute-start.24 = (bf16[2,96,1280]{2,1,0:T(8,128)(2,1)S(1)}, bf16[2,96,1280]{2,1,0:T(8,128)(2,1)}, u32[]{:S(2)}, u32[]{:S(2)}) collective-permute-start(bf16[2,96,1280]{2,1,0:T(8,128)(2,1)S(1)} %pad_maximum_fusion.3.act), channel_id=1, source_target_pairs={{0,4},{2,6},{12,8},{14,10},{4,0},{6,2},{8,12},{10,14},{1,5},{3,7},... | collective-permute-start | bytes 1474568 | tf_op jit(solution)/shard_map/ppermute | solution.py:180
  131.4 8.5 %collective-permute-start.30 = (f16[2,192,512]{2,1,0:T(8,128)(2,1)S(1)}, f16[2,192,512]{2,1,0:T(8,128)(2,1)S(1)}, u32[]{:S(2)}, u32[]{:S(2)}) collective-permute-start(f16[2,192,512]{2,1,0:T(8,128)(2,1)S(1)} %fusion.19), channel_id=1, source_target_pairs={{4,8},{6,10},{8,4},{10,6},{5,9},{7,11},{9,5},{11,7},{20,24},{22,26... | collective-permute-start | bytes 1179656 | tf_op jit(solution)/shard_map/ppermute | solution.py:180
  132.1 13.5 %collective-permute-start.29 = (f16[2,192,512]{2,1,0:T(8,128)(2,1)S(1)}, f16[2,192,512]{2,1,0:T(8,128)(2,1)S(1)}, u32[]{:S(2)}, u32[]{:S(2)}) collective-permute-start(f16[2,192,512]{2,1,0:T(8,128)(2,1)S(1)} %fusion.40), channel_id=1, source_target_pairs={{0,4},{2,6},{12,8},{14,10},{1,5},{3,7},{13,9},{15,11},{16,20},{18,... | collective-permute-start | bytes 1179656 | tf_op jit(solution)/shard_map/ppermute | solution.py:180
  137.1 14.4 %collective-permute-start.28 = (bf16[2,96,1280]{2,1,0:T(8,128)(2,1)}, bf16[2,96,1280]{2,1,0:T(8,128)(2,1)}, u32[]{:S(2)}, u32[]{:S(2)}) collective-permute-start(bf16[2,96,1280]{2,1,0:T(8,128)(2,1)} %collective-permute-done.24.side_1), channel_id=1, source_target_pairs={{4,8},{6,10},{8,4},{10,6},{5,9},{7,11},{9,5},{11,7},{20,24},{22,26... | collective-permute-start | bytes 1474568 | tf_op jit(solution)/shard_map/ppermute | solution.py:180
  138.6 13.0 %collective-permute-start.27 = (bf16[2,96,1280]{2,1,0:T(8,128)(2,1)}, bf16[2,96,1280]{2,1,0:T(8,128)(2,1)}, u32[]{:S(2)}, u32[]{:S(2)}) collective-permute-start(bf16[2,96,1280]{2,1,0:T(8,128)(2,1)} %collective-permute-done.25.centre_1), channel_id=1, source_target_pairs={{4,0},{6,2},{8,12},{10,14},{5,1},{7,3},{9,13},{11,15},{20,16},{22,... | collective-permute-start | bytes 1474568 | tf_op jit(solution)/shard_map/ppermute | solution.py:180
  146.8 8.6 %collective-permute-start.31 = (f16[2,192,512]{2,1,0:T(8,128)(2,1)}, f16[2,192,512]{2,1,0:T(8,128)(2,1)}, u32[]{:S(2)}, u32[]{:S(2)}) collective-permute-start(f16[2,192,512]{2,1,0:T(8,128)(2,1)} %get-tuple-element.183), channel_id=1, source_target_pairs={{0,4},{2,6},{12,8},{14,10},{4,0},{6,2},{8,12},{10,14},{1,5},{3,7},... | collective-permute-start | bytes 1179656 | tf_op jit(solution)/shard_map/ppermute | solution.py:180
  149.1 6.3 %collective-permute-start.32 = (f16[2,192,512]{2,1,0:T(8,128)(2,1)}, f16[2,192,512]{2,1,0:T(8,128)(2,1)}, u32[]{:S(2)}, u32[]{:S(2)}) collective-permute-start(f16[2,192,512]{2,1,0:T(8,128)(2,1)} %get-tuple-element.184), channel_id=1, source_target_pairs={{4,8},{6,10},{8,4},{10,6},{5,9},{7,11},{9,5},{11,7},{20,24},{22,26... | collective-permute-start | bytes 1179656 | tf_op jit(solution)/shard_map/ppermute | solution.py:180
  151.6 26.8 %collective-permute-start.36 = (bf16[2,96,1280]{2,1,0:T(8,128)(2,1)}, bf16[2,96,1280]{2,1,0:T(8,128)(2,1)}, u32[]{:S(2)}, u32[]{:S(2)}) collective-permute-start(bf16[2,96,1280]{2,1,0:T(8,128)(2,1)} %collective-permute-done.28.share_2), channel_id=1, source_target_pairs={{4,0},{6,2},{8,12},{10,14},{5,1},{7,3},{9,13},{11,15},{20,16},{22,... | collective-permute-start | bytes 1474568 | tf_op jit(solution)/shard_map/ppermute | solution.py:180
  157.3 12.2 %copy-start.24 = (bf16[1,96,1280]{2,1,0:T(8,128)(2,1)S(1)}, bf16[1,96,1280]{2,1,0:T(8,128)(2,1)}, u32[]{:S(2)}) copy-start(bf16[1,96,1280]{2,1,0:T(8,128)(2,1)} %get-tuple-element.189) | copy-start | bytes 737284
  157.3 12.2 %copy-start.25 = (bf16[1,96,1280]{2,1,0:T(8,128)(2,1)S(1)}, bf16[1,96,1280]{2,1,0:T(8,128)(2,1)}, u32[]{:S(2)}) copy-start(bf16[1,96,1280]{2,1,0:T(8,128)(2,1)} %get-tuple-element.190) | copy-start | bytes 737284
  158.4 25.6 %collective-permute-start.34 = (bf16[2,192,512]{2,1,0:T(8,128)(2,1)}, bf16[2,192,512]{2,1,0:T(8,128)(2,1)}, u32[]{:S(2)}, u32[]{:S(2)}) collective-permute-start(bf16[2,192,512]{2,1,0:T(8,128)(2,1)} %pad_maximum_fusion.4.act), channel_id=1, source_target_pairs={{4,8},{6,10},{8,4},{10,6},{5,9},{7,11},{9,5},{11,7},{20,24},{22,26... | collective-permute-start | bytes 1179656 | tf_op jit(solution)/shard_map/ppermute | solution.py:180
  159.8 24.1 %collective-permute-start.33 = (bf16[2,192,512]{2,1,0:T(8,128)(2,1)}, bf16[2,192,512]{2,1,0:T(8,128)(2,1)}, u32[]{:S(2)}, u32[]{:S(2)}) collective-permute-start(bf16[2,192,512]{2,1,0:T(8,128)(2,1)} %pad_maximum_fusion.4.act), channel_id=1, source_target_pairs={{0,4},{2,6},{12,8},{14,10},{4,0},{6,2},{8,12},{10,14},{1,5},{3,7},... | collective-permute-start | bytes 1179656 | tf_op jit(solution)/shard_map/ppermute | solution.py:180
  170.5 10.0 %collective-permute-start.35 = (bf16[2,48,1792]{2,1,0:T(8,128)(2,1)}, bf16[2,48,1792]{2,1,0:T(8,128)(2,1)}, u32[]{:S(2)}, u32[]{:S(2)}) collective-permute-start(bf16[2,48,1792]{2,1,0:T(8,128)(2,1)} %get-tuple-element.198), channel_id=1, source_target_pairs={{0,2},{2,0},{4,6},{6,4},{8,10},{10,8},{12,14},{14,12},{1,3},{3,1},... | collective-permute-start | bytes 1032200 | tf_op jit(solution)/shard_map/ppermute | solution.py:180
  178.4 20.2 %collective-permute-start.40 = (bf16[4,2,96,1280]{3,2,1,0:T(8,128)(2,1)S(1)}, bf16[4,2,96,1280]{3,2,1,0:T(8,128)(2,1)S(1)}, u32[]{:S(2)}, u32[]{:S(2)}) collective-permute-start(bf16[4,2,96,1280]{3,2,1,0:T(8,128)(2,1)S(1)} %shard_map.72), channel_id=1, source_target_pairs={{0,2},{2,0},{4,6},{6,4},{8,10},{10,8},{12,14},{14,12},{1,3},{3,1},... | collective-permute-start | bytes 5898248 | tf_op jit(solution)/shard_map/ppermute | solution.py:180
  181.5 4.4 %copy-start.23 = (bf16[2,48,1792]{2,1,0:T(8,128)(2,1)S(1)}, bf16[2,48,1792]{2,1,0:T(8,128)(2,1)}, u32[]{:S(2)}) copy-start(bf16[2,48,1792]{2,1,0:T(8,128)(2,1)} %get-tuple-element.165) | copy-start | bytes 1032196
  183.5 15.1 %collective-permute-start.41 = (bf16[4,2,96,1280]{3,2,1,0:T(8,128)(2,1)S(1)}, bf16[4,2,96,1280]{3,2,1,0:T(8,128)(2,1)S(1)}, u32[]{:S(2)}, u32[]{:S(2)}) collective-permute-start(bf16[4,2,96,1280]{3,2,1,0:T(8,128)(2,1)S(1)} %shard_map.73), channel_id=1, source_target_pairs={{0,2},{2,0},{4,6},{6,4},{8,10},{10,8},{12,14},{14,12},{1,3},{3,1},... | collective-permute-start | bytes 5898248 | tf_op jit(solution)/shard_map/ppermute | solution.py:180
  183.9 12.2 %collective-permute-start.37 = (bf16[2,192,512]{2,1,0:T(8,128)(2,1)}, bf16[2,192,512]{2,1,0:T(8,128)(2,1)S(1)}, u32[]{:S(2)}, u32[]{:S(2)}) collective-permute-start(bf16[2,192,512]{2,1,0:T(8,128)(2,1)} %collective-permute-done.34.centre_1), channel_id=1, source_target_pairs={{4,0},{6,2},{8,12},{10,14},{5,1},{7,3},{9,13},{11,15},{20,16},{22,... | collective-permute-start | bytes 1179656 | tf_op jit(solution)/shard_map/ppermute | solution.py:180
  185.2 9.2 %collective-permute-start.38 = (bf16[2,192,512]{2,1,0:T(8,128)(2,1)}, bf16[2,192,512]{2,1,0:T(8,128)(2,1)S(1)}, u32[]{:S(2)}, u32[]{:S(2)}) collective-permute-start(bf16[2,192,512]{2,1,0:T(8,128)(2,1)} %collective-permute-done.33.side_1), channel_id=1, source_target_pairs={{4,8},{6,10},{8,4},{10,6},{5,9},{7,11},{9,5},{11,7},{20,24},{22,26... | collective-permute-start | bytes 1179656 | tf_op jit(solution)/shard_map/ppermute | solution.py:180
  187.2 10.4 %collective-permute-start.42 = (bf16[48,3584]{1,0:T(8,128)(2,1)S(1)}, bf16[48,3584]{1,0:T(8,128)(2,1)S(1)}, u32[]{:S(2)}, u32[]{:S(2)}) collective-permute-start(bf16[48,3584]{1,0:T(8,128)(2,1)S(1)} %get-tuple-element.196), channel_id=1, source_target_pairs={{0,1},{1,0},{2,3},{3,2},{4,5},{5,4},{6,7},{7,6},{8,9},{9,8},{10,11... | collective-permute-start | bytes 1032200 | tf_op jit(solution)/shard_map/ppermute | solution.py:322
  196.1 12.0 %collective-permute-start.39 = (bf16[2,192,512]{2,1,0:T(8,128)(2,1)S(1)}, bf16[2,192,512]{2,1,0:T(8,128)(2,1)S(1)}, u32[]{:S(2)}, u32[]{:S(2)}) collective-permute-start(bf16[2,192,512]{2,1,0:T(8,128)(2,1)S(1)} %collective-permute-done.38.share_2), channel_id=1, source_target_pairs={{4,0},{6,2},{8,12},{10,14},{5,1},{7,3},{9,13},{11,15},{20,16},{22,... | collective-permute-start | bytes 1179656 | tf_op jit(solution)/shard_map/ppermute | solution.py:180
  209.6 5.9 %collective-permute-start.43 = (bf16[4,2,192,512]{3,2,1,0:T(8,128)(2,1)S(1)}, bf16[4,2,192,512]{3,2,1,0:T(8,128)(2,1)S(1)}, u32[]{:S(2)}, u32[]{:S(2)}) collective-permute-start(bf16[4,2,192,512]{3,2,1,0:T(8,128)(2,1)S(1)} %shard_map.76), channel_id=1, source_target_pairs={{0,2},{2,0},{4,6},{6,4},{8,10},{10,8},{12,14},{14,12},{1,3},{3,1},... | collective-permute-start | bytes 4718600 | tf_op jit(solution)/shard_map/ppermute | solution.py:180
  (7 other events, 8.4 us)

commit v19 on v18

--- a/solution.py
+++ b/solution.py
@@ -289,8 +289,7 @@
                 merged.append(merge(*hops))
                 terms = tie(terms, merged[-1][0])
             if k == 0:
-                products[2] = all_features(tokens, 2, act)
-                terms = tie(terms, products[2])
+                terms = tie(terms, far_weights, tokens[1])
             near = take(tie(terms, in_1) if gathering else terms, 2).astype(WIRE)
             far = add(take(tie(terms, near), 3), in_1).astype(WIRE)
             centre_2, in_2 = send(far, centre), send(near, inward)
@@ -306,6 +305,9 @@
         if gathering:
             side_1, centre_1 = tie((side_1, centre_1), before)
             out_2, share_2 = send(centre_1, outward), send(side_1, centre)
+        if k == 0:
+            products[2] = all_features(tokens, 2, (side_1, centre_1, far, near))
+            terms = tie(terms, products[2])
         if k < 0:
             products[1] = (own((far, near), LONG), send(theirs, pairs))
             cotangent = tie(grad_hidden[0], far, near)

time: 220 us -> 217 us (0.986)
  starting transfers between devices: 90.2 us -> 87.7 us
  waiting for transfers between devices: 35.9 us -> 38.2 us
    ppermute x39, starting transfers between devices: 86.5 us -> 82.8 us  [send(): return lax.ppermute(value, 'col', route)]
    ppermute x39, waiting for transfers between devices: 20.6 us -> 22.9 us  [send(): return lax.ppermute(value, 'col', route)]
    unnamed x54 -> x52, local copies, waits for them, and re-layouts: 7.74 us -> 6.27 us
  transfers between devices with their start and end apart: 44 -> 44, of which waited for: 11 -> 14; matrix products, arithmetic and copies ran while one was open for 14% -> 14% of each run, Pallas kernels for 18% -> 18%
where the time goes in v19:
time: 217 us; the launch traced here: 216 us
  starting transfers between devices  87.7 us (40%)
  Pallas kernels  47.9 us (22%)
  waiting for transfers between devices  38.2 us (18%)
  other arithmetic  26.9 us (12%)
  local copies, waits for them, and re-layouts  14.1 us (6%)
    ppermute x39, starting transfers between devices, send(): return lax.ppermute(value, 'col', route)  82.8 us
    pallas_call x5, Pallas kernels, forward(): pl.pallas_call(functools.partial(forward_kernel, scale, start, cores), ou...  23.2 us
    ppermute x39, waiting for transfers between devices, send(): return lax.ppermute(value, 'col', route)  22.9 us
    pallas_call x4, Pallas kernels, gradient(): pl.pallas_call(functools.partial(gradient_kernel, len(acts)), out_shape=(...  20.9 us
    ppermute x1, waiting for transfers between devices, local(): over_depth = lax.ppermute(mine, 'depth', swap)  7.84 us
    unnamed x52, local copies, waits for them, and re-layouts  6.27 us
    ppermute x1, waiting for transfers between devices, local(): lax.ppermute(columns_of(cotangent, (1 - part) * half, half), 'depth', swap)  5.16 us
    convert_element_type x3, other arithmetic, local(): swapped = swapped.astype(WIRE)  5.1 us
  transfers between devices with their start and end apart: 44, of which 14 were waited for; matrix products, arithmetic and copies ran while one was open for 14% of the time, Pallas kernels for 18%

profile of v19, /device:TPU:1, one launch (start us, length us, event | category | flops | bytes accessed | tf_op | source)
XLA Modules:
  0.0 216.1 jit_solution(3588506129362111446)
XLA Ops:
  0.6 2.1 collective-permute-start.1
  2.8 1.2 collective-permute-start
  4.0 7.8 %collective-permute-done.1 = bf16[384,512]{1,0:T(8,128)(2,1)S(1)} collective-permute-done((bf16[384,512]{1,0:T(8,128)(2,1)}, bf16[384,512]{1,0:T(8,128)(2,1)S(1)}, u32[]{:S(2)}, u32[]{:S(2)}) %collective-permute-start.1) | collective-permute-done | bytes 393248 | tf_op jit(solution)/shard_map/ppermute | solution.py:214
  12.6 1.3 maximum_select_fusion
  14.2 4.2 %shard_map.67 = f32[4,2,96,1280]{3,2,1,0:T(8,128)S(1)} custom-call(s32[1]{0:T(128)} %bitcast.6.place_ref, bf16[384,1024]{1,0:T(8,128)(2,1)S(1)} %bitcast.154, bf16[1024,7168]{1,0:T(8,128)(2,1)} %refs_2_.9, bf16[1024,7168]{1,0:T(8,128)(2,1)} %refs_3_.1), custom_call_target="tpu_custom_call" | custom-call | tf_op jit(solution)/shard_map/pallas_call | solution.py:57
  18.4 1.5 convert_element_type.194
  19.9 1.9 collective-permute-start.2
  21.8 4.2 %shard_map.68 = f32[4,2,96,1280]{3,2,1,0:T(8,128)S(1)} custom-call(s32[1]{0:T(128)} %bitcast.1.place_ref, bf16[384,1024]{1,0:T(8,128)(2,1)S(1)} %bitcast.155, bf16[1024,7168]{1,0:T(8,128)(2,1)} %refs_2_.9, bf16[1024,7168]{1,0:T(8,128)(2,1)} %refs_3_.1), custom_call_target="tpu_custom_call" | custom-call | flops 6000000000 | tf_op jit(solution)/shard_map/pallas_call | solution.py:57
  26.9 4.1 %collective-permute-start.4 = (f16[2,96,1280]{2,1,0:T(8,128)(2,1)}, f16[2,96,1280]{2,1,0:T(8,128)(2,1)}, u32[]{:S(2)}, u32[]{:S(2)}) collective-permute-start(f16[2,96,1280]{2,1,0:T(8,128)(2,1)} %fusion.33), channel_id=1, source_target_pairs={{0,4},{2,6},{12,8},{14,10},{1,5},{3,7},{13,9},{15,11},{16,20},{18,... | collective-permute-start | bytes 1474568 | tf_op jit(solution)/shard_map/ppermute | solution.py:180
  31.0 1.5 collective-permute-done.3
  32.9 4.2 %shard_map.69 = f32[4,2,96,1280]{3,2,1,0:T(8,128)S(1)} custom-call(s32[1]{0:T(128)} %bitcast.6.place_ref, bf16[384,1024]{1,0:T(8,128)(2,1)S(1)} %bitcast.158, bf16[1024,7168]{1,0:T(8,128)(2,1)} %refs_2_.9, bf16[1024,7168]{1,0:T(8,128)(2,1)} %refs_3_.1), custom_call_target="tpu_custom_call" | custom-call | tf_op jit(solution)/shard_map/pallas_call | solution.py:57
  39.1 4.0 %collective-permute-start.7 = (f16[2,96,1280]{2,1,0:T(8,128)(2,1)}, f16[2,96,1280]{2,1,0:T(8,128)(2,1)}, u32[]{:S(2)}, u32[]{:S(2)}) collective-permute-start(f16[2,96,1280]{2,1,0:T(8,128)(2,1)} %fusion.30), channel_id=1, source_target_pairs={{0,4},{2,6},{12,8},{14,10},{1,5},{3,7},{13,9},{15,11},{16,20},{18,... | collective-permute-start | bytes 1474568 | tf_op jit(solution)/shard_map/ppermute | solution.py:180
  43.1 2.0 fusion.13
  45.1 1.4 collective-permute-start.8
  47.5 4.2 %shard_map.70 = f32[4,2,96,1280]{3,2,1,0:T(8,128)S(1)} custom-call(s32[1]{0:T(128)} %bitcast.1.place_ref, bf16[384,1024]{1,0:T(8,128)(2,1)S(1)} %bitcast.159, bf16[1024,7168]{1,0:T(8,128)(2,1)} %refs_2_.9, bf16[1024,7168]{1,0:T(8,128)(2,1)} %refs_3_.1), custom_call_target="tpu_custom_call" | custom-call | flops 6000000000 | tf_op jit(solution)/shard_map/pallas_call | solution.py:57
  51.7 5.2 %collective-permute-done.5 = bf16[48,3584]{1,0:T(8,128)(2,1)S(1)} collective-permute-done((bf16[48,3584]{1,0:T(8,128)(2,1)}, bf16[48,3584]{1,0:T(8,128)(2,1)S(1)}, u32[]{:S(2)}, u32[]{:S(2)}) %collective-permute-start.5) | collective-permute-done | bytes 344096 | tf_op jit(solution)/shard_map/ppermute | solution.py:316
  56.9 2.3 %fusion.8 = (f16[2,96,1280]{2,1,0:T(8,128)(2,1)S(1)}, f16[2,96,1280]{2,1,0:T(8,128)(2,1)S(1)}) fusion(f16[2,96,1280]{2,1,0:T(8,128)(2,1)} %collective-permute-done.8, f32[4,2,96,1280]{3,2,1,0:T(8,128)S(1)} %shard_map.68, pred[]{:T(512)S(6)} %or.3, f16[4,2,96,1280]{3,2,1,0:T(8,128)(2,1)S(1)} %collective-permute-done.2, ...), kind=kLoop, calls=%fused_computation.22 | loop fusion | flops 3194880 | bytes 6389761 | tf_op jit(solution)/shard_map/convert_element_type | solution.py:332
  59.2 1.3 collective-permute-start.11
  61.3 2.4 %collective-permute-start.9 = (bf16[2,48,1792]{2,1,0:T(8,128)(2,1)S(1)}, bf16[2,48,1792]{2,1,0:T(8,128)(2,1)S(1)}, u32[]{:S(2)}, u32[]{:S(2)}) collective-permute-start(bf16[2,48,1792]{2,1,0:T(8,128)(2,1)S(1)} %get-tuple-element.206), channel_id=1, source_target_pairs={{0,2},{2,0},{4,6},{6,4},{8,10},{10,8},{12,14},{14,12},{1,3},{3,1},... | collective-permute-start | bytes 1032200 | tf_op jit(solution)/shard_map/ppermute | solution.py:180
  63.8 4.5 %collective-permute-start.15 = (f16[2,96,1280]{2,1,0:T(8,128)(2,1)S(1)}, f16[2,96,1280]{2,1,0:T(8,128)(2,1)S(1)}, u32[]{:S(2)}, u32[]{:S(2)}) collective-permute-start(f16[2,96,1280]{2,1,0:T(8,128)(2,1)S(1)} %fusion.31), channel_id=1, source_target_pairs={{0,4},{2,6},{12,8},{14,10},{1,5},{3,7},{13,9},{15,11},{16,20},{18,... | collective-permute-start | bytes 1474568 | tf_op jit(solution)/shard_map/ppermute | solution.py:180
  68.3 1.7 dynamic-slice_bitcast_fusion
  74.6 3.8 %collective-permute-start.13 = (bf16[2,96,1280]{2,1,0:T(8,128)(2,1)S(1)}, bf16[2,96,1280]{2,1,0:T(8,128)(2,1)S(1)}, u32[]{:S(2)}, u32[]{:S(2)}) collective-permute-start(bf16[2,96,1280]{2,1,0:T(8,128)(2,1)S(1)} %pad_maximum_fusion.2.act), channel_id=1, source_target_pairs={{0,4},{2,6},{12,8},{14,10},{4,0},{6,2},{8,12},{10,14},{1,5},{3,7},... | collective-permute-start | bytes 1474568 | tf_op jit(solution)/shard_map/ppermute | solution.py:180
  81.4 6.6 %collective-permute-start.19 = (f16[2,96,1280]{2,1,0:T(8,128)(2,1)}, f16[2,96,1280]{2,1,0:T(8,128)(2,1)S(1)}, u32[]{:S(2)}, u32[]{:S(2)}) collective-permute-start(f16[2,96,1280]{2,1,0:T(8,128)(2,1)} %fusion.32), channel_id=1, source_target_pairs={{0,4},{2,6},{12,8},{14,10},{1,5},{3,7},{13,9},{15,11},{16,20},{18,... | collective-permute-start | bytes 1474568 | tf_op jit(solution)/shard_map/ppermute | solution.py:180
  88.1 2.0 collective-permute-done.13.side_1
  90.8 1.3 collective-permute-start.17
  92.4 1.4 copy-done.3
  93.8 6.5 %shard_map.71 = f32[4,2,192,512]{3,2,1,0:T(8,128)} custom-call(s32[1]{0:T(128)} %bitcast.1.place_ref, bf16[768,1024]{1,0:T(8,128)(2,1)S(1)} %bitcast.163, bf16[768,1024]{1,0:T(8,128)(2,1)S(1)} %bitcast.164, bf16[1024,7168]{1,0:T(8,128)(2,1)} %refs_2_.9, bf16[1024,7168]{1,0:T(8,128)(2,1)} %refs_3_.1, bf16[2,1024,512]{2,1,0:T(8,128)(2,1)S(1)} %copy-done.3, ...), custom_call_target="tpu_custom_call" | custom-call | tf_op jit(solution)/shard_map/pallas_call | solution.py:57
  100.8 1.5 fusion.4
  102.2 4.4 %collective-permute-start.22 = (f16[2,96,1280]{2,1,0:T(8,128)(2,1)}, f16[2,96,1280]{2,1,0:T(8,128)(2,1)}, u32[]{:S(2)}, u32[]{:S(2)}) collective-permute-start(f16[2,96,1280]{2,1,0:T(8,128)(2,1)} %get-tuple-element.183), channel_id=1, source_target_pairs={{0,4},{2,6},{12,8},{14,10},{4,0},{6,2},{8,12},{10,14},{1,5},{3,7},... | collective-permute-start | bytes 1474568 | tf_op jit(solution)/shard_map/ppermute | solution.py:180
  106.6 1.4 collective-permute-start.23
  108.1 1.3 collective-permute-start.21
  111.7 1.6 maximum_bitcast_fusion.features_ref
  114.6 4.2 %collective-permute-start.26 = (f16[2,192,512]{2,1,0:T(8,128)(2,1)S(1)}, f16[2,192,512]{2,1,0:T(8,128)(2,1)S(1)}, u32[]{:S(2)}, u32[]{:S(2)}) collective-permute-start(f16[2,192,512]{2,1,0:T(8,128)(2,1)S(1)} %fusion.39), channel_id=1, source_target_pairs={{0,4},{2,6},{12,8},{14,10},{1,5},{3,7},{13,9},{15,11},{16,20},{18,... | collective-permute-start | bytes 1179656 | tf_op jit(solution)/shard_map/ppermute | solution.py:180
  118.8 1.9 fusion.2
  121.8 1.5 collective-permute-start.25
  123.3 2.2 %collective-permute-done.21.out_3 = bf16[2,96,1280]{2,1,0:T(8,128)(2,1)S(1)} collective-permute-done((bf16[2,96,1280]{2,1,0:T(8,128)(2,1)S(1)}, bf16[2,96,1280]{2,1,0:T(8,128)(2,1)S(1)}, u32[]{:S(2)}, u32[]{:S(2)}) %collective-permute-start.21) | collective-permute-done | bytes 491552 | tf_op jit(solution)/shard_map/ppermute | solution.py:180
  127.7 1.6 copy-done.18
  130.1 2.6 %collective-permute-start.29 = (f16[2,192,512]{2,1,0:T(8,128)(2,1)S(1)}, f16[2,192,512]{2,1,0:T(8,128)(2,1)S(1)}, u32[]{:S(2)}, u32[]{:S(2)}) collective-permute-start(f16[2,192,512]{2,1,0:T(8,128)(2,1)S(1)} %fusion.40), channel_id=1, source_target_pairs={{0,4},{2,6},{12,8},{14,10},{1,5},{3,7},{13,9},{15,11},{16,20},{18,... | collective-permute-start | bytes 1179656 | tf_op jit(solution)/shard_map/ppermute | solution.py:180
  132.7 4.0 %collective-permute-done.24.side_1 = bf16[2,96,1280]{2,1,0:T(8,128)(2,1)} collective-permute-done((bf16[2,96,1280]{2,1,0:T(8,128)(2,1)S(1)}, bf16[2,96,1280]{2,1,0:T(8,128)(2,1)}, u32[]{:S(2)}, u32[]{:S(2)}) %collective-permute-start.24) | collective-permute-done | bytes 491552 | tf_op jit(solution)/shard_map/ppermute | solution.py:180
  136.7 1.5 collective-permute-start.28
  138.2 1.3 collective-permute-start.27
  139.5 2.2 %collective-permute-done.29 = f16[2,192,512]{2,1,0:T(8,128)(2,1)S(1)} collective-permute-done((f16[2,192,512]{2,1,0:T(8,128)(2,1)S(1)}, f16[2,192,512]{2,1,0:T(8,128)(2,1)S(1)}, u32[]{:S(2)}, u32[]{:S(2)}) %collective-permute-start.29) | collective-permute-done | bytes 393248 | tf_op jit(solution)/shard_map/ppermute | solution.py:180
  141.7 1.3 fusion.16
  143.0 2.3 %collective-permute-start.31 = (f16[2,192,512]{2,1,0:T(8,128)(2,1)}, f16[2,192,512]{2,1,0:T(8,128)(2,1)}, u32[]{:S(2)}, u32[]{:S(2)}) collective-permute-start(f16[2,192,512]{2,1,0:T(8,128)(2,1)} %get-tuple-element.187), channel_id=1, source_target_pairs={{0,4},{2,6},{12,8},{14,10},{4,0},{6,2},{8,12},{10,14},{1,5},{3,7},... | collective-permute-start | bytes 1179656 | tf_op jit(solution)/shard_map/ppermute | solution.py:180
  145.3 1.4 collective-permute-start.32
  148.1 1.3 collective-permute-start.36
  149.4 3.7 %collective-permute-done.31 = f16[2,192,512]{2,1,0:T(8,128)(2,1)} collective-permute-done((f16[2,192,512]{2,1,0:T(8,128)(2,1)}, f16[2,192,512]{2,1,0:T(8,128)(2,1)}, u32[]{:S(2)}, u32[]{:S(2)}) %collective-permute-start.31) | collective-permute-done | bytes 393248 | tf_op jit(solution)/shard_map/ppermute | solution.py:180
  153.1 1.9 fusion.18
  156.0 1.4 collective-permute-start.34
  157.4 7.4 %collective-permute-start.33 = (bf16[2,192,512]{2,1,0:T(8,128)(2,1)}, bf16[2,192,512]{2,1,0:T(8,128)(2,1)}, u32[]{:S(2)}, u32[]{:S(2)}) collective-permute-start(bf16[2,192,512]{2,1,0:T(8,128)(2,1)} %pad_maximum_fusion.4.act), channel_id=1, source_target_pairs={{0,4},{2,6},{12,8},{14,10},{4,0},{6,2},{8,12},{10,14},{1,5},{3,7},... | collective-permute-start | bytes 1179656 | tf_op jit(solution)/shard_map/ppermute | solution.py:180
  165.9 8.3 %collective-permute-start.35 = (bf16[2,48,1792]{2,1,0:T(8,128)(2,1)}, bf16[2,48,1792]{2,1,0:T(8,128)(2,1)}, u32[]{:S(2)}, u32[]{:S(2)}) collective-permute-start(bf16[2,48,1792]{2,1,0:T(8,128)(2,1)} %get-tuple-element.202), channel_id=1, source_target_pairs={{0,2},{2,0},{4,6},{6,4},{8,10},{10,8},{12,14},{14,12},{1,3},{3,1},... | collective-permute-start | bytes 1032200 | tf_op jit(solution)/shard_map/ppermute | solution.py:180
  174.2 2.1 collective-permute-done.35
  177.3 2.0 shard_map.73
  180.3 1.3 collective-permute-start.37
  182.3 1.2 maximum_select_fusion.3
  183.6 1.3 collective-permute-start.42
  184.9 7.0 %shard_map.74 = (f32[1024,3584]{1,0:T(8,128)}, f32[1024,3584]{1,0:T(8,128)}) custom-call(s32[1]{0:T(128)} %bitcast.59.place_ref, bf16[1024,768]{1,0:T(8,128)(2,1)S(1)} %maximum_bitcast_fusion.features_ref, bf16[4,1,2,96,1280]{4,3,2,1,0:T(8,128)(2,1)S(1)} %bitcast.165, bf16[4,1,2,96,1280]{4,3,2,1,0:T(8,128)(2,1)S(1)} %bitcast.167), custom_call_target="tpu_custom_call" | custom-call | flops 4026531840 | bytes 15990784 | tf_op jit(solution)/shard_map/pallas_call | solution.py:101
  191.9 1.5 collective-permute-start.39
  194.5 7.0 %shard_map.75 = (f32[1024,3584]{1,0:T(8,128)}, f32[1024,3584]{1,0:T(8,128)}) custom-call(s32[1]{0:T(128)} %bitcast.62.place_ref, bf16[1024,768]{1,0:T(8,128)(2,1)S(1)} %maximum_bitcast_fusion.features_ref, bf16[4,1,2,96,1280]{4,3,2,1,0:T(8,128)(2,1)S(1)} %bitcast.166, ...), custom_call_target="tpu_custom_call", output_to_operand_aliasing={{0}: (4, {}), {1}: (5, {})} | custom-call | flops 4026531840 | bytes 15990784 | tf_op jit(solution)/shard_map/pallas_call | solution.py:101
  201.5 4.6 %collective-permute-done.39.out_3 = bf16[2,192,512]{2,1,0:T(8,128)(2,1)S(1)} collective-permute-done((bf16[2,192,512]{2,1,0:T(8,128)(2,1)S(1)}, bf16[2,192,512]{2,1,0:T(8,128)(2,1)S(1)}, u32[]{:S(2)}, u32[]{:S(2)}) %collective-permute-start.39) | collective-permute-done | bytes 393248 | tf_op jit(solution)/shard_map/ppermute | solution.py:180
  206.1 1.5 shard_map.76
  207.6 1.7 collective-permute-start.43
  209.3 3.4 %shard_map.77 = (f32[1024,3584]{1,0:T(8,128)}, f32[1024,3584]{1,0:T(8,128)}) custom-call(s32[1]{0:T(128)} %bitcast.59.place_ref, bf16[1024,768]{1,0:T(8,128)(2,1)S(1)} %maximum_bitcast_fusion.features_ref, bf16[4,1,2,192,512]{4,3,2,1,0:T(8,128)(2,1)S(1)} %bitcast.162, ...), custom_call_target="tpu_custom_call", output_to_operand_aliasing={{0}: (3, {}), {1}: (4, {})} | custom-call | flops 1610612736 | bytes 7340032 | tf_op jit(solution)/shard_map/pallas_call | solution.py:101
  212.7 3.4 %shard_map.78 = (f32[1024,3584]{1,0:T(8,128)}, f32[1024,3584]{1,0:T(8,128)}) custom-call(s32[1]{0:T(128)} %bitcast.62.place_ref, bf16[1024,768]{1,0:T(8,128)(2,1)S(1)} %maximum_bitcast_fusion.features_ref, bf16[4,1,2,192,512]{4,3,2,1,0:T(8,128)(2,1)S(1)} %bitcast.169, ...), custom_call_target="tpu_custom_call", output_to_operand_aliasing={{0}: (3, {}), {1}: (4, {})} | custom-call | flops 1610612736 | bytes 7340032 | tf_op jit(solution)/shard_map/pallas_call | solution.py:101
  (136 shorter events, 30.0 us)
Async XLA Ops:
  0.6 11.2 %collective-permute-start.1 = (bf16[384,512]{1,0:T(8,128)(2,1)}, bf16[384,512]{1,0:T(8,128)(2,1)S(1)}, u32[]{:S(2)}, u32[]{:S(2)}) collective-permute-start(bf16[384,512]{1,0:T(8,128)(2,1)} %bitcast.177), channel_id=1, source_target_pairs={{0,1},{1,0},{2,3},{3,2},{4,5},{5,4},{6,7},{7,6},{8,9},{9,8},{10,11... | collective-permute-start | bytes 1179656 | tf_op jit(solution)/shard_map/ppermute | solution.py:214
  2.8 9.9 %collective-permute-start = (bf16[384,512]{1,0:T(8,128)(2,1)}, bf16[384,512]{1,0:T(8,128)(2,1)S(1)}, u32[]{:S(2)}, u32[]{:S(2)}) collective-permute-start(bf16[384,512]{1,0:T(8,128)(2,1)} %bitcast.178), channel_id=1, source_target_pairs={{0,16},{16,0},{1,17},{17,1},{2,18},{18,2},{3,19},{19,3},{4,20},{20... | collective-permute-start | bytes 1179656 | tf_op jit(solution)/shard_map/ppermute | solution.py:213
  19.9 6.1 %collective-permute-start.2 = (f16[4,2,96,1280]{3,2,1,0:T(8,128)(2,1)}, f16[4,2,96,1280]{3,2,1,0:T(8,128)(2,1)S(1)}, u32[]{:S(2)}, u32[]{:S(2)}) collective-permute-start(f16[4,2,96,1280]{3,2,1,0:T(8,128)(2,1)} %convert_element_type.194), channel_id=1, source_target_pairs={{0,2},{2,0},{4,6},{6,4},{8,10},{10,8},{12,14},{14,12},{1,3},{3,1},... | collective-permute-start | bytes 5898248 | tf_op jit(solution)/shard_map/ppermute | solution.py:180
  21.7 10.7 %collective-permute-start.3 = (bf16[384,512]{1,0:T(8,128)(2,1)S(1)}, bf16[384,512]{1,0:T(8,128)(2,1)S(1)}, u32[]{:S(2)}, u32[]{:S(2)}) collective-permute-start(bf16[384,512]{1,0:T(8,128)(2,1)S(1)} %collective-permute-done), channel_id=1, source_target_pairs={{0,1},{1,0},{2,3},{3,2},{4,5},{5,4},{6,7},{7,6},{8,9},{9,8},{10,11... | collective-permute-start | bytes 1179656 | tf_op jit(solution)/shard_map/ppermute | solution.py:215
  26.9 16.2 %collective-permute-start.4 = (f16[2,96,1280]{2,1,0:T(8,128)(2,1)}, f16[2,96,1280]{2,1,0:T(8,128)(2,1)}, u32[]{:S(2)}, u32[]{:S(2)}) collective-permute-start(f16[2,96,1280]{2,1,0:T(8,128)(2,1)} %fusion.33), channel_id=1, source_target_pairs={{0,4},{2,6},{12,8},{14,10},{1,5},{3,7},{13,9},{15,11},{16,20},{18,... | collective-permute-start | bytes 1474568 | tf_op jit(solution)/shard_map/ppermute | solution.py:180
  37.3 9.2 %copy-start.25 = (bf16[1,48,7168]{2,1,0:T(8,128)(2,1)S(1)}, bf16[1,48,7168]{2,1,0:T(8,128)(2,1)}, u32[]{:S(2)}) copy-start(bf16[1,48,7168]{2,1,0:T(8,128)(2,1)} %param.7) | copy-start | bytes 2064388
  37.3 19.5 %collective-permute-start.6 = (f16[4,2,96,1280]{3,2,1,0:T(8,128)(2,1)S(1)}, f16[4,2,96,1280]{3,2,1,0:T(8,128)(2,1)S(1)}, u32[]{:S(2)}, u32[]{:S(2)}) collective-permute-start(f16[4,2,96,1280]{3,2,1,0:T(8,128)(2,1)S(1)} %convert_element_type.198), channel_id=1, source_target_pairs={{0,2},{2,0},{4,6},{6,4},{8,10},{10,8},{12,14},{14,12},{1,3},{3,1},... | collective-permute-start | bytes 5898248 | tf_op jit(solution)/shard_map/ppermute | solution.py:180
  39.1 17.8 %collective-permute-start.7 = (f16[2,96,1280]{2,1,0:T(8,128)(2,1)}, f16[2,96,1280]{2,1,0:T(8,128)(2,1)}, u32[]{:S(2)}, u32[]{:S(2)}) collective-permute-start(f16[2,96,1280]{2,1,0:T(8,128)(2,1)} %fusion.30), channel_id=1, source_target_pairs={{0,4},{2,6},{12,8},{14,10},{1,5},{3,7},{13,9},{15,11},{16,20},{18,... | collective-permute-start | bytes 1474568 | tf_op jit(solution)/shard_map/ppermute | solution.py:180
  45.1 11.8 %collective-permute-start.8 = (f16[2,96,1280]{2,1,0:T(8,128)(2,1)}, f16[2,96,1280]{2,1,0:T(8,128)(2,1)}, u32[]{:S(2)}, u32[]{:S(2)}) collective-permute-start(f16[2,96,1280]{2,1,0:T(8,128)(2,1)} %fusion.13), channel_id=1, source_target_pairs={{4,8},{6,10},{8,4},{10,6},{5,9},{7,11},{9,5},{11,7},{20,24},{22,26... | collective-permute-start | bytes 1474568 | tf_op jit(solution)/shard_map/ppermute | solution.py:180
  47.3 9.6 %collective-permute-start.5 = (bf16[48,3584]{1,0:T(8,128)(2,1)}, bf16[48,3584]{1,0:T(8,128)(2,1)S(1)}, u32[]{:S(2)}, u32[]{:S(2)}) collective-permute-start(bf16[48,3584]{1,0:T(8,128)(2,1)} %get-tuple-element.207), channel_id=1, source_target_pairs={{0,1},{1,0},{2,3},{3,2},{4,5},{5,4},{6,7},{7,6},{8,9},{9,8},{10,11... | collective-permute-start | bytes 1032200 | tf_op jit(solution)/shard_map/ppermute | solution.py:316
  51.7 49.1 %copy-start = (f32[4,2,96,1280]{3,2,1,0:T(8,128)}, f32[4,2,96,1280]{3,2,1,0:T(8,128)S(1)}, u32[]{:S(2)}) copy-start(f32[4,2,96,1280]{3,2,1,0:T(8,128)S(1)} %shard_map.70) | copy-start | bytes 11796484
  56.9 43.9 %copy-start.19 = (f16[4,2,96,1280]{3,2,1,0:T(8,128)(2,1)}, f16[4,2,96,1280]{3,2,1,0:T(8,128)(2,1)S(1)}, u32[]{:S(2)}) copy-start(f16[4,2,96,1280]{3,2,1,0:T(8,128)(2,1)S(1)} %collective-permute-done.6) | copy-start | bytes 5898244
  59.2 12.7 %collective-permute-start.11 = (f16[2,96,1280]{2,1,0:T(8,128)(2,1)S(1)}, f16[2,96,1280]{2,1,0:T(8,128)(2,1)S(1)}, u32[]{:S(2)}, u32[]{:S(2)}) collective-permute-start(f16[2,96,1280]{2,1,0:T(8,128)(2,1)S(1)} %get-tuple-element.185), channel_id=1, source_target_pairs={{0,4},{2,6},{12,8},{14,10},{4,0},{6,2},{8,12},{10,14},{1,5},{3,7},... | collective-permute-start | bytes 1474568 | tf_op jit(solution)/shard_map/ppermute | solution.py:180
  60.6 11.4 %collective-permute-start.12 = (f16[2,96,1280]{2,1,0:T(8,128)(2,1)S(1)}, f16[2,96,1280]{2,1,0:T(8,128)(2,1)S(1)}, u32[]{:S(2)}, u32[]{:S(2)}) collective-permute-start(f16[2,96,1280]{2,1,0:T(8,128)(2,1)S(1)} %get-tuple-element.186), channel_id=1, source_target_pairs={{4,8},{6,10},{8,4},{10,6},{5,9},{7,11},{9,5},{11,7},{20,24},{22,26... | collective-permute-start | bytes 1474568 | tf_op jit(solution)/shard_map/ppermute | solution.py:180
  61.3 9.4 %collective-permute-start.9 = (bf16[2,48,1792]{2,1,0:T(8,128)(2,1)S(1)}, bf16[2,48,1792]{2,1,0:T(8,128)(2,1)S(1)}, u32[]{:S(2)}, u32[]{:S(2)}) collective-permute-start(bf16[2,48,1792]{2,1,0:T(8,128)(2,1)S(1)} %get-tuple-element.206), channel_id=1, source_target_pairs={{0,2},{2,0},{4,6},{6,4},{8,10},{10,8},{12,14},{14,12},{1,3},{3,1},... | collective-permute-start | bytes 1032200 | tf_op jit(solution)/shard_map/ppermute | solution.py:180
  63.8 15.8 %collective-permute-start.15 = (f16[2,96,1280]{2,1,0:T(8,128)(2,1)S(1)}, f16[2,96,1280]{2,1,0:T(8,128)(2,1)S(1)}, u32[]{:S(2)}, u32[]{:S(2)}) collective-permute-start(f16[2,96,1280]{2,1,0:T(8,128)(2,1)S(1)} %fusion.31), channel_id=1, source_target_pairs={{0,4},{2,6},{12,8},{14,10},{1,5},{3,7},{13,9},{15,11},{16,20},{18,... | collective-permute-start | bytes 1474568 | tf_op jit(solution)/shard_map/ppermute | solution.py:180
  70.2 8.2 %collective-permute-start.16 = (bf16[2,1024,512]{2,1,0:T(8,128)(2,1)S(1)}, bf16[2,1024,512]{2,1,0:T(8,128)(2,1)S(1)}, u32[]{:S(2)}, u32[]{:S(2)}) collective-permute-start(bf16[2,1024,512]{2,1,0:T(8,128)(2,1)S(1)} %pad_maximum_fusion), channel_id=1, source_target_pairs={{0,2},{2,0},{4,6},{6,4},{8,10},{10,8},{12,14},{14,12},{1,3},{3,1},... | collective-permute-start | bytes 6291464 | tf_op jit(solution)/shard_map/ppermute | solution.py:180
  70.7 7.7 %collective-permute-start.10 = (bf16[4,2,96,1024]{3,2,0,1:T(8,128)(2,1)S(1)}, bf16[4,2,96,1024]{3,2,0,1:T(8,128)(2,1)S(1)}, u32[]{:S(2)}, u32[]{:S(2)}) collective-permute-start(bf16[4,2,96,1024]{3,2,0,1:T(8,128)(2,1)S(1)} %pad_maximum_fusion.1), channel_id=1, source_target_pairs={{0,2},{2,0},{4,6},{6,4},{8,10},{10,8},{12,14},{14,12},{1,3},{3,1},... | collective-permute-start | bytes 4718600 | tf_op jit(solution)/shard_map/ppermute | solution.py:180
  73.7 7.0 %copy-start.6 = (bf16[2,96,1280]{2,1,0:T(8,128)(2,1)}, bf16[2,96,1280]{2,1,0:T(8,128)(2,1)S(1)}, u32[]{:S(2)}) copy-start(bf16[2,96,1280]{2,1,0:T(8,128)(2,1)S(1)} %pad_maximum_fusion.2.act) | copy-start | bytes 1474564
  73.7 14.4 %collective-permute-start.14 = (bf16[2,96,1280]{2,1,0:T(8,128)(2,1)S(1)}, bf16[2,96,1280]{2,1,0:T(8,128)(2,1)S(1)}, u32[]{:S(2)}, u32[]{:S(2)}) collective-permute-start(bf16[2,96,1280]{2,1,0:T(8,128)(2,1)S(1)} %pad_maximum_fusion.2.act), channel_id=1, source_target_pairs={{4,8},{6,10},{8,4},{10,6},{5,9},{7,11},{9,5},{11,7},{20,24},{22,26... | collective-permute-start | bytes 1474568 | tf_op jit(solution)/shard_map/ppermute | solution.py:180
  74.6 15.5 %collective-permute-start.13 = (bf16[2,96,1280]{2,1,0:T(8,128)(2,1)S(1)}, bf16[2,96,1280]{2,1,0:T(8,128)(2,1)S(1)}, u32[]{:S(2)}, u32[]{:S(2)}) collective-permute-start(bf16[2,96,1280]{2,1,0:T(8,128)(2,1)S(1)} %pad_maximum_fusion.2.act), channel_id=1, source_target_pairs={{0,4},{2,6},{12,8},{14,10},{4,0},{6,2},{8,12},{10,14},{1,5},{3,7},... | collective-permute-start | bytes 1474568 | tf_op jit(solution)/shard_map/ppermute | solution.py:180
  78.4 2.3 %copy-start.2 = (bf16[2,1024,512]{2,1,0:T(8,128)(2,1)}, bf16[2,1024,512]{2,1,0:T(8,128)(2,1)S(1)}, u32[]{:S(2)}) copy-start(bf16[2,1024,512]{2,1,0:T(8,128)(2,1)S(1)} %collective-permute-done.16.refs_4_.refs_5_) | copy-start | bytes 6291460
  80.7 19.7 %collective-permute-start.20 = (f16[2,96,1280]{2,1,0:T(8,128)(2,1)S(1)}, f16[2,96,1280]{2,1,0:T(8,128)(2,1)S(1)}, u32[]{:S(2)}, u32[]{:S(2)}) collective-permute-start(f16[2,96,1280]{2,1,0:T(8,128)(2,1)S(1)} %fusion.6), channel_id=1, source_target_pairs={{4,8},{6,10},{8,4},{10,6},{5,9},{7,11},{9,5},{11,7},{20,24},{22,26... | collective-permute-start | bytes 1474568 | tf_op jit(solution)/shard_map/ppermute | solution.py:180
  81.4 19.3 %collective-permute-start.19 = (f16[2,96,1280]{2,1,0:T(8,128)(2,1)}, f16[2,96,1280]{2,1,0:T(8,128)(2,1)S(1)}, u32[]{:S(2)}, u32[]{:S(2)}) collective-permute-start(f16[2,96,1280]{2,1,0:T(8,128)(2,1)} %fusion.32), channel_id=1, source_target_pairs={{0,4},{2,6},{12,8},{14,10},{1,5},{3,7},{13,9},{15,11},{16,20},{18,... | collective-permute-start | bytes 1474568 | tf_op jit(solution)/shard_map/ppermute | solution.py:180
  88.1 4.3 %copy-start.8 = (bf16[2,96,1280]{2,1,0:T(8,128)(2,1)}, bf16[2,96,1280]{2,1,0:T(8,128)(2,1)S(1)}, u32[]{:S(2)}) copy-start(bf16[2,96,1280]{2,1,0:T(8,128)(2,1)S(1)} %collective-permute-done.14.centre_1) | copy-start | bytes 1474564
  90.1 2.3 %copy-start.10 = (bf16[2,96,1280]{2,1,0:T(8,128)(2,1)}, bf16[2,96,1280]{2,1,0:T(8,128)(2,1)S(1)}, u32[]{:S(2)}) copy-start(bf16[2,96,1280]{2,1,0:T(8,128)(2,1)S(1)} %collective-permute-done.13.side_1) | copy-start | bytes 1474564
  90.1 17.9 %collective-permute-start.18 = (bf16[2,96,1280]{2,1,0:T(8,128)(2,1)S(1)}, bf16[2,96,1280]{2,1,0:T(8,128)(2,1)S(1)}, u32[]{:S(2)}, u32[]{:S(2)}) collective-permute-start(bf16[2,96,1280]{2,1,0:T(8,128)(2,1)S(1)} %collective-permute-done.13.side_1), channel_id=1, source_target_pairs={{4,8},{6,10},{8,4},{10,6},{5,9},{7,11},{9,5},{11,7},{20,24},{22,26... | collective-permute-start | bytes 1474568 | tf_op jit(solution)/shard_map/ppermute | solution.py:180
  90.8 17.2 %collective-permute-start.17 = (bf16[2,96,1280]{2,1,0:T(8,128)(2,1)S(1)}, bf16[2,96,1280]{2,1,0:T(8,128)(2,1)S(1)}, u32[]{:S(2)}, u32[]{:S(2)}) collective-permute-start(bf16[2,96,1280]{2,1,0:T(8,128)(2,1)S(1)} %collective-permute-done.14.centre_1), channel_id=1, source_target_pairs={{4,0},{6,2},{8,12},{10,14},{5,1},{7,3},{9,13},{11,15},{20,16},{22,... | collective-permute-start | bytes 1474568 | tf_op jit(solution)/shard_map/ppermute | solution.py:180
  102.2 16.5 %collective-permute-start.22 = (f16[2,96,1280]{2,1,0:T(8,128)(2,1)}, f16[2,96,1280]{2,1,0:T(8,128)(2,1)}, u32[]{:S(2)}, u32[]{:S(2)}) collective-permute-start(f16[2,96,1280]{2,1,0:T(8,128)(2,1)} %get-tuple-element.183), channel_id=1, source_target_pairs={{0,4},{2,6},{12,8},{14,10},{4,0},{6,2},{8,12},{10,14},{1,5},{3,7},... | collective-permute-start | bytes 1474568 | tf_op jit(solution)/shard_map/ppermute | solution.py:180
  106.6 12.1 %collective-permute-start.23 = (f16[2,96,1280]{2,1,0:T(8,128)(2,1)}, f16[2,96,1280]{2,1,0:T(8,128)(2,1)}, u32[]{:S(2)}, u32[]{:S(2)}) collective-permute-start(f16[2,96,1280]{2,1,0:T(8,128)(2,1)} %get-tuple-element.184), channel_id=1, source_target_pairs={{4,8},{6,10},{8,4},{10,6},{5,9},{7,11},{9,5},{11,7},{20,24},{22,26... | collective-permute-start | bytes 1474568 | tf_op jit(solution)/shard_map/ppermute | solution.py:180
  108.1 5.3 %copy-start.12 = (bf16[2,96,1280]{2,1,0:T(8,128)(2,1)}, bf16[2,96,1280]{2,1,0:T(8,128)(2,1)S(1)}, u32[]{:S(2)}) copy-start(bf16[2,96,1280]{2,1,0:T(8,128)(2,1)S(1)} %collective-permute-done.18.share_2) | copy-start | bytes 1474564
  108.1 5.3 %copy-start.14 = (bf16[2,96,1280]{2,1,0:T(8,128)(2,1)}, bf16[2,96,1280]{2,1,0:T(8,128)(2,1)S(1)}, u32[]{:S(2)}) copy-start(bf16[2,96,1280]{2,1,0:T(8,128)(2,1)S(1)} %collective-permute-done.17.out_2) | copy-start | bytes 1474564
  108.1 17.4 %collective-permute-start.21 = (bf16[2,96,1280]{2,1,0:T(8,128)(2,1)S(1)}, bf16[2,96,1280]{2,1,0:T(8,128)(2,1)S(1)}, u32[]{:S(2)}, u32[]{:S(2)}) collective-permute-start(bf16[2,96,1280]{2,1,0:T(8,128)(2,1)S(1)} %collective-permute-done.18.share_2), channel_id=1, source_target_pairs={{4,0},{6,2},{8,12},{10,14},{5,1},{7,3},{9,13},{11,15},{20,16},{22,... | collective-permute-start | bytes 1474568 | tf_op jit(solution)/shard_map/ppermute | solution.py:180
  111.7 7.1 %copy-start.1 = (f32[4,2,96,1280]{3,2,1,0:T(8,128)S(1)}, f32[4,2,96,1280]{3,2,1,0:T(8,128)}, u32[]{:S(2)}) copy-start(f32[4,2,96,1280]{3,2,1,0:T(8,128)} %copy-done) | copy-start | bytes 11796484
  114.6 6.2 %copy-start.21 = (bf16[96,1792]{1,0:T(8,128)(2,1)S(1)}, bf16[96,1792]{1,0:T(8,128)(2,1)}, u32[]{:S(2)}) copy-start(bf16[96,1792]{1,0:T(8,128)(2,1)} %get-tuple-element.204) | copy-start | bytes 1032196
  114.6 13.1 %collective-permute-start.26 = (f16[2,192,512]{2,1,0:T(8,128)(2,1)S(1)}, f16[2,192,512]{2,1,0:T(8,128)(2,1)S(1)}, u32[]{:S(2)}, u32[]{:S(2)}) collective-permute-start(f16[2,192,512]{2,1,0:T(8,128)(2,1)S(1)} %fusion.39), channel_id=1, source_target_pairs={{0,4},{2,6},{12,8},{14,10},{1,5},{3,7},{13,9},{15,11},{16,20},{18,... | collective-permute-start | bytes 1179656 | tf_op jit(solution)/shard_map/ppermute | solution.py:180
  120.7 5.6 %copy-start.7 = (bf16[2,96,1280]{2,1,0:T(8,128)(2,1)S(1)}, bf16[2,96,1280]{2,1,0:T(8,128)(2,1)}, u32[]{:S(2)}) copy-start(bf16[2,96,1280]{2,1,0:T(8,128)(2,1)} %copy-done.6) | copy-start | bytes 1474564
  120.7 5.6 %copy-start.9 = (bf16[2,96,1280]{2,1,0:T(8,128)(2,1)S(1)}, bf16[2,96,1280]{2,1,0:T(8,128)(2,1)}, u32[]{:S(2)}) copy-start(bf16[2,96,1280]{2,1,0:T(8,128)(2,1)} %copy-done.8) | copy-start | bytes 1474564
  120.8 5.5 %copy-start.11 = (bf16[2,96,1280]{2,1,0:T(8,128)(2,1)S(1)}, bf16[2,96,1280]{2,1,0:T(8,128)(2,1)}, u32[]{:S(2)}) copy-start(bf16[2,96,1280]{2,1,0:T(8,128)(2,1)} %copy-done.10) | copy-start | bytes 1474564
  120.8 5.5 %copy-start.13 = (bf16[2,96,1280]{2,1,0:T(8,128)(2,1)S(1)}, bf16[2,96,1280]{2,1,0:T(8,128)(2,1)}, u32[]{:S(2)}) copy-start(bf16[2,96,1280]{2,1,0:T(8,128)(2,1)} %copy-done.12) | copy-start | bytes 1474564
  120.8 5.5 %copy-start.15 = (bf16[2,96,1280]{2,1,0:T(8,128)(2,1)S(1)}, bf16[2,96,1280]{2,1,0:T(8,128)(2,1)}, u32[]{:S(2)}) copy-start(bf16[2,96,1280]{2,1,0:T(8,128)(2,1)} %copy-done.14) | copy-start | bytes 1474564
  121.8 5.8 %copy-start.4 = (bf16[2,96,1280]{2,1,0:T(8,128)(2,1)}, bf16[2,96,1280]{2,1,0:T(8,128)(2,1)S(1)}, u32[]{:S(2)}) copy-start(bf16[2,96,1280]{2,1,0:T(8,128)(2,1)S(1)} %pad_maximum_fusion.3.act) | copy-start | bytes 1474564
  121.8 10.9 %collective-permute-start.25 = (bf16[2,96,1280]{2,1,0:T(8,128)(2,1)S(1)}, bf16[2,96,1280]{2,1,0:T(8,128)(2,1)}, u32[]{:S(2)}, u32[]{:S(2)}) collective-permute-start(bf16[2,96,1280]{2,1,0:T(8,128)(2,1)S(1)} %pad_maximum_fusion.3.act), channel_id=1, source_target_pairs={{4,8},{6,10},{8,4},{10,6},{5,9},{7,11},{9,5},{11,7},{20,24},{22,26... | collective-permute-start | bytes 1474568 | tf_op jit(solution)/shard_map/ppermute | solution.py:180
  123.3 13.4 %collective-permute-start.24 = (bf16[2,96,1280]{2,1,0:T(8,128)(2,1)S(1)}, bf16[2,96,1280]{2,1,0:T(8,128)(2,1)}, u32[]{:S(2)}, u32[]{:S(2)}) collective-permute-start(bf16[2,96,1280]{2,1,0:T(8,128)(2,1)S(1)} %pad_maximum_fusion.3.act), channel_id=1, source_target_pairs={{0,4},{2,6},{12,8},{14,10},{4,0},{6,2},{8,12},{10,14},{1,5},{3,7},... | collective-permute-start | bytes 1474568 | tf_op jit(solution)/shard_map/ppermute | solution.py:180
  129.4 10.1 %collective-permute-start.30 = (f16[2,192,512]{2,1,0:T(8,128)(2,1)S(1)}, f16[2,192,512]{2,1,0:T(8,128)(2,1)S(1)}, u32[]{:S(2)}, u32[]{:S(2)}) collective-permute-start(f16[2,192,512]{2,1,0:T(8,128)(2,1)S(1)} %fusion.19), channel_id=1, source_target_pairs={{4,8},{6,10},{8,4},{10,6},{5,9},{7,11},{9,5},{11,7},{20,24},{22,26... | collective-permute-start | bytes 1179656 | tf_op jit(solution)/shard_map/ppermute | solution.py:180
  130.1 11.6 %collective-permute-start.29 = (f16[2,192,512]{2,1,0:T(8,128)(2,1)S(1)}, f16[2,192,512]{2,1,0:T(8,128)(2,1)S(1)}, u32[]{:S(2)}, u32[]{:S(2)}) collective-permute-start(f16[2,192,512]{2,1,0:T(8,128)(2,1)S(1)} %fusion.40), channel_id=1, source_target_pairs={{0,4},{2,6},{12,8},{14,10},{1,5},{3,7},{13,9},{15,11},{16,20},{18,... | collective-permute-start | bytes 1179656 | tf_op jit(solution)/shard_map/ppermute | solution.py:180
  136.7 10.9 %collective-permute-start.28 = (bf16[2,96,1280]{2,1,0:T(8,128)(2,1)}, bf16[2,96,1280]{2,1,0:T(8,128)(2,1)}, u32[]{:S(2)}, u32[]{:S(2)}) collective-permute-start(bf16[2,96,1280]{2,1,0:T(8,128)(2,1)} %collective-permute-done.24.side_1), channel_id=1, source_target_pairs={{4,8},{6,10},{8,4},{10,6},{5,9},{7,11},{9,5},{11,7},{20,24},{22,26... | collective-permute-start | bytes 1474568 | tf_op jit(solution)/shard_map/ppermute | solution.py:180
  138.2 9.9 %collective-permute-start.27 = (bf16[2,96,1280]{2,1,0:T(8,128)(2,1)}, bf16[2,96,1280]{2,1,0:T(8,128)(2,1)}, u32[]{:S(2)}, u32[]{:S(2)}) collective-permute-start(bf16[2,96,1280]{2,1,0:T(8,128)(2,1)} %collective-permute-done.25.centre_1), channel_id=1, source_target_pairs={{4,0},{6,2},{8,12},{10,14},{5,1},{7,3},{9,13},{11,15},{20,16},{22,... | collective-permute-start | bytes 1474568 | tf_op jit(solution)/shard_map/ppermute | solution.py:180
  143.0 10.1 %collective-permute-start.31 = (f16[2,192,512]{2,1,0:T(8,128)(2,1)}, f16[2,192,512]{2,1,0:T(8,128)(2,1)}, u32[]{:S(2)}, u32[]{:S(2)}) collective-permute-start(f16[2,192,512]{2,1,0:T(8,128)(2,1)} %get-tuple-element.187), channel_id=1, source_target_pairs={{0,4},{2,6},{12,8},{14,10},{4,0},{6,2},{8,12},{10,14},{1,5},{3,7},... | collective-permute-start | bytes 1179656 | tf_op jit(solution)/shard_map/ppermute | solution.py:180
  145.3 7.8 %collective-permute-start.32 = (f16[2,192,512]{2,1,0:T(8,128)(2,1)}, f16[2,192,512]{2,1,0:T(8,128)(2,1)}, u32[]{:S(2)}, u32[]{:S(2)}) collective-permute-start(f16[2,192,512]{2,1,0:T(8,128)(2,1)} %get-tuple-element.188), channel_id=1, source_target_pairs={{4,8},{6,10},{8,4},{10,6},{5,9},{7,11},{9,5},{11,7},{20,24},{22,26... | collective-permute-start | bytes 1179656 | tf_op jit(solution)/shard_map/ppermute | solution.py:180
  148.1 26.1 %collective-permute-start.36 = (bf16[2,96,1280]{2,1,0:T(8,128)(2,1)}, bf16[2,96,1280]{2,1,0:T(8,128)(2,1)}, u32[]{:S(2)}, u32[]{:S(2)}) collective-permute-start(bf16[2,96,1280]{2,1,0:T(8,128)(2,1)} %collective-permute-done.28.share_2), channel_id=1, source_target_pairs={{4,0},{6,2},{8,12},{10,14},{5,1},{7,3},{9,13},{11,15},{20,16},{22,... | collective-permute-start | bytes 1474568 | tf_op jit(solution)/shard_map/ppermute | solution.py:180
  154.9 10.0 %copy-start.23 = (bf16[1,96,1280]{2,1,0:T(8,128)(2,1)S(1)}, bf16[1,96,1280]{2,1,0:T(8,128)(2,1)}, u32[]{:S(2)}) copy-start(bf16[1,96,1280]{2,1,0:T(8,128)(2,1)} %get-tuple-element.193) | copy-start | bytes 737284
  154.9 10.0 %copy-start.24 = (bf16[1,96,1280]{2,1,0:T(8,128)(2,1)S(1)}, bf16[1,96,1280]{2,1,0:T(8,128)(2,1)}, u32[]{:S(2)}) copy-start(bf16[1,96,1280]{2,1,0:T(8,128)(2,1)} %get-tuple-element.194) | copy-start | bytes 737284
  156.0 24.3 %collective-permute-start.34 = (bf16[2,192,512]{2,1,0:T(8,128)(2,1)}, bf16[2,192,512]{2,1,0:T(8,128)(2,1)}, u32[]{:S(2)}, u32[]{:S(2)}) collective-permute-start(bf16[2,192,512]{2,1,0:T(8,128)(2,1)} %pad_maximum_fusion.4.act), channel_id=1, source_target_pairs={{4,8},{6,10},{8,4},{10,6},{5,9},{7,11},{9,5},{11,7},{20,24},{22,26... | collective-permute-start | bytes 1179656 | tf_op jit(solution)/shard_map/ppermute | solution.py:180
  157.4 22.9 %collective-permute-start.33 = (bf16[2,192,512]{2,1,0:T(8,128)(2,1)}, bf16[2,192,512]{2,1,0:T(8,128)(2,1)}, u32[]{:S(2)}, u32[]{:S(2)}) collective-permute-start(bf16[2,192,512]{2,1,0:T(8,128)(2,1)} %pad_maximum_fusion.4.act), channel_id=1, source_target_pairs={{0,4},{2,6},{12,8},{14,10},{4,0},{6,2},{8,12},{10,14},{1,5},{3,7},... | collective-permute-start | bytes 1179656 | tf_op jit(solution)/shard_map/ppermute | solution.py:180
  165.9 10.3 %collective-permute-start.35 = (bf16[2,48,1792]{2,1,0:T(8,128)(2,1)}, bf16[2,48,1792]{2,1,0:T(8,128)(2,1)}, u32[]{:S(2)}, u32[]{:S(2)}) collective-permute-start(bf16[2,48,1792]{2,1,0:T(8,128)(2,1)} %get-tuple-element.202), channel_id=1, source_target_pairs={{0,2},{2,0},{4,6},{6,4},{8,10},{10,8},{12,14},{14,12},{1,3},{3,1},... | collective-permute-start | bytes 1032200 | tf_op jit(solution)/shard_map/ppermute | solution.py:180
  174.2 20.3 %collective-permute-start.40 = (bf16[4,2,96,1280]{3,2,1,0:T(8,128)(2,1)S(1)}, bf16[4,2,96,1280]{3,2,1,0:T(8,128)(2,1)S(1)}, u32[]{:S(2)}, u32[]{:S(2)}) collective-permute-start(bf16[4,2,96,1280]{3,2,1,0:T(8,128)(2,1)S(1)} %shard_map.72), channel_id=1, source_target_pairs={{0,2},{2,0},{4,6},{6,4},{8,10},{10,8},{12,14},{14,12},{1,3},{3,1},... | collective-permute-start | bytes 5898248 | tf_op jit(solution)/shard_map/ppermute | solution.py:180
  177.3 5.0 %copy-start.22 = (bf16[2,48,1792]{2,1,0:T(8,128)(2,1)S(1)}, bf16[2,48,1792]{2,1,0:T(8,128)(2,1)}, u32[]{:S(2)}) copy-start(bf16[2,48,1792]{2,1,0:T(8,128)(2,1)} %get-tuple-element.169) | copy-start | bytes 1032196
  179.3 15.2 %collective-permute-start.41 = (bf16[4,2,96,1280]{3,2,1,0:T(8,128)(2,1)S(1)}, bf16[4,2,96,1280]{3,2,1,0:T(8,128)(2,1)S(1)}, u32[]{:S(2)}, u32[]{:S(2)}) collective-permute-start(bf16[4,2,96,1280]{3,2,1,0:T(8,128)(2,1)S(1)} %shard_map.73), channel_id=1, source_target_pairs={{0,2},{2,0},{4,6},{6,4},{8,10},{10,8},{12,14},{14,12},{1,3},{3,1},... | collective-permute-start | bytes 5898248 | tf_op jit(solution)/shard_map/ppermute | solution.py:180
  180.3 11.6 %collective-permute-start.37 = (bf16[2,192,512]{2,1,0:T(8,128)(2,1)}, bf16[2,192,512]{2,1,0:T(8,128)(2,1)S(1)}, u32[]{:S(2)}, u32[]{:S(2)}) collective-permute-start(bf16[2,192,512]{2,1,0:T(8,128)(2,1)} %collective-permute-done.34.centre_1), channel_id=1, source_target_pairs={{4,0},{6,2},{8,12},{10,14},{5,1},{7,3},{9,13},{11,15},{20,16},{22,... | collective-permute-start | bytes 1179656 | tf_op jit(solution)/shard_map/ppermute | solution.py:180
  181.6 10.3 %collective-permute-start.38 = (bf16[2,192,512]{2,1,0:T(8,128)(2,1)}, bf16[2,192,512]{2,1,0:T(8,128)(2,1)S(1)}, u32[]{:S(2)}, u32[]{:S(2)}) collective-permute-start(bf16[2,192,512]{2,1,0:T(8,128)(2,1)} %collective-permute-done.33.side_1), channel_id=1, source_target_pairs={{4,8},{6,10},{8,4},{10,6},{5,9},{7,11},{9,5},{11,7},{20,24},{22,26... | collective-permute-start | bytes 1179656 | tf_op jit(solution)/shard_map/ppermute | solution.py:180
  183.6 9.9 %collective-permute-start.42 = (bf16[48,3584]{1,0:T(8,128)(2,1)S(1)}, bf16[48,3584]{1,0:T(8,128)(2,1)S(1)}, u32[]{:S(2)}, u32[]{:S(2)}) collective-permute-start(bf16[48,3584]{1,0:T(8,128)(2,1)S(1)} %get-tuple-element.200), channel_id=1, source_target_pairs={{0,1},{1,0},{2,3},{3,2},{4,5},{5,4},{6,7},{7,6},{8,9},{9,8},{10,11... | collective-permute-start | bytes 1032200 | tf_op jit(solution)/shard_map/ppermute | solution.py:324
  191.9 14.2 %collective-permute-start.39 = (bf16[2,192,512]{2,1,0:T(8,128)(2,1)S(1)}, bf16[2,192,512]{2,1,0:T(8,128)(2,1)S(1)}, u32[]{:S(2)}, u32[]{:S(2)}) collective-permute-start(bf16[2,192,512]{2,1,0:T(8,128)(2,1)S(1)} %collective-permute-done.38.share_2), channel_id=1, source_target_pairs={{4,0},{6,2},{8,12},{10,14},{5,1},{7,3},{9,13},{11,15},{20,16},{22,... | collective-permute-start | bytes 1179656 | tf_op jit(solution)/shard_map/ppermute | solution.py:180
  207.6 5.1 %collective-permute-start.43 = (bf16[4,2,192,512]{3,2,1,0:T(8,128)(2,1)S(1)}, bf16[4,2,192,512]{3,2,1,0:T(8,128)(2,1)S(1)}, u32[]{:S(2)}, u32[]{:S(2)}) collective-permute-start(bf16[4,2,192,512]{3,2,1,0:T(8,128)(2,1)S(1)} %shard_map.76), channel_id=1, source_target_pairs={{0,2},{2,0},{4,6},{6,4},{8,10},{10,8},{12,14},{14,12},{1,3},{3,1},... | collective-permute-start | bytes 4718600 | tf_op jit(solution)/shard_map/ppermute | solution.py:180
  (6 other events, 7.1 us)

commit v20 on v19

--- a/solution.py
+++ b/solution.py
@@ -346,7 +346,7 @@
             far_weights = exchange_weights(2, (near, swapped))
             tokens = jnp.stack(tie(features, near, swapped), axis=1)
             tokens = (tokens, send(tokens, pairs))
-        if k == 0:
+        if k == last - 1:
             turned = [value.reshape(-1, depth) for value in tie(features, near, swapped)]
             turned = jnp.concatenate(turned).T
             terms = tie(terms, turned)

time: 217 us -> 216 us (level)
  waiting for transfers between devices: 38.2 us -> 31.2 us
  other arithmetic: 26.9 us -> 31.7 us
  starting transfers between devices: 87.7 us -> 92.1 us
  local copies, waits for them, and re-layouts: 14.1 us -> 11.1 us
    ppermute x39, waiting for transfers between devices: 22.9 us -> 15.9 us  [send(): return lax.ppermute(value, 'col', route)]
    ppermute x39, starting transfers between devices: 82.8 us -> 87.1 us  [send(): return lax.ppermute(value, 'col', route)]
    unnamed x52 -> x46, local copies, waits for them, and re-layouts: 6.27 us -> 3.39 us
  transfers between devices with their start and end apart: 44 -> 44, of which waited for: 14 -> 13; matrix products, arithmetic and copies ran while one was open for 14% -> 16% of each run, Pallas kernels for 18% -> 18%
where the time goes in v20:
time: 216 us; the launch traced here: 215 us
  starting transfers between devices  92.1 us (43%)
  Pallas kernels  48 us (22%)
  other arithmetic  31.7 us (15%)
  waiting for transfers between devices  31.2 us (14%)
  local copies, waits for them, and re-layouts  11.1 us (5%)
    ppermute x39, starting transfers between devices, send(): return lax.ppermute(value, 'col', route)  87.1 us
    pallas_call x5, Pallas kernels, forward(): pl.pallas_call(functools.partial(forward_kernel, scale, start, cores), ou...  23.2 us
    pallas_call x4, Pallas kernels, gradient(): pl.pallas_call(functools.partial(gradient_kernel, len(acts)), out_shape=(...  20.9 us
    ppermute x39, waiting for transfers between devices, send(): return lax.ppermute(value, 'col', route)  15.9 us
    ppermute x1, waiting for transfers between devices, local(): over_depth = lax.ppermute(mine, 'depth', swap)  7.84 us
    convert_element_type x3, other arithmetic, local(): swapped = swapped.astype(WIRE)  6.87 us
    ppermute x1, waiting for transfers between devices, local(): lax.ppermute(columns_of(cotangent, (1 - part) * half, half), 'depth', swap)  5.16 us
  transfers between devices with their start and end apart: 44, of which 13 were waited for; matrix products, arithmetic and copies ran while one was open for 16% of the time, Pallas kernels for 18%

profile of v20, /device:TPU:1, one launch (start us, length us, event | category | flops | bytes accessed | tf_op | source)
XLA Modules:
  0.0 215.4 jit_solution(40835417595635616)
XLA Ops:
  0.6 2.1 collective-permute-start.1
  4.0 7.8 %collective-permute-done.1 = bf16[384,512]{1,0:T(8,128)(2,1)S(1)} collective-permute-done((bf16[384,512]{1,0:T(8,128)(2,1)}, bf16[384,512]{1,0:T(8,128)(2,1)S(1)}, u32[]{:S(2)}, u32[]{:S(2)}) %collective-permute-start.1) | collective-permute-done | bytes 393248 | tf_op jit(solution)/shard_map/ppermute | solution.py:214
  12.6 1.3 maximum_select_fusion
  14.2 4.2 %shard_map.67 = f32[4,2,96,1280]{3,2,1,0:T(8,128)S(1)} custom-call(s32[1]{0:T(128)} %bitcast.6.place_ref, bf16[384,1024]{1,0:T(8,128)(2,1)S(1)} %bitcast.154, bf16[1024,7168]{1,0:T(8,128)(2,1)} %refs_2_.9, bf16[1024,7168]{1,0:T(8,128)(2,1)} %refs_3_.1), custom_call_target="tpu_custom_call" | custom-call | tf_op jit(solution)/shard_map/pallas_call | solution.py:57
  18.4 1.5 convert_element_type.194
  19.9 1.9 collective-permute-start.2
  21.8 4.2 %shard_map.68 = f32[4,2,96,1280]{3,2,1,0:T(8,128)S(1)} custom-call(s32[1]{0:T(128)} %bitcast.1.place_ref, bf16[384,1024]{1,0:T(8,128)(2,1)S(1)} %bitcast.155, bf16[1024,7168]{1,0:T(8,128)(2,1)} %refs_2_.9, bf16[1024,7168]{1,0:T(8,128)(2,1)} %refs_3_.1), custom_call_target="tpu_custom_call" | custom-call | flops 6000000000 | tf_op jit(solution)/shard_map/pallas_call | solution.py:57
  26.9 4.2 %collective-permute-start.4 = (f16[2,96,1280]{2,1,0:T(8,128)(2,1)}, f16[2,96,1280]{2,1,0:T(8,128)(2,1)}, u32[]{:S(2)}, u32[]{:S(2)}) collective-permute-start(f16[2,96,1280]{2,1,0:T(8,128)(2,1)} %fusion.33), channel_id=1, source_target_pairs={{0,4},{2,6},{12,8},{14,10},{1,5},{3,7},{13,9},{15,11},{16,20},{18,... | collective-permute-start | bytes 1474568 | tf_op jit(solution)/shard_map/ppermute | solution.py:180
  31.1 1.4 collective-permute-done.3
  32.9 4.2 %shard_map.69 = f32[4,2,96,1280]{3,2,1,0:T(8,128)S(1)} custom-call(s32[1]{0:T(128)} %bitcast.6.place_ref, bf16[384,1024]{1,0:T(8,128)(2,1)S(1)} %bitcast.158, bf16[1024,7168]{1,0:T(8,128)(2,1)} %refs_2_.9, bf16[1024,7168]{1,0:T(8,128)(2,1)} %refs_3_.1), custom_call_target="tpu_custom_call" | custom-call | tf_op jit(solution)/shard_map/pallas_call | solution.py:57
  39.1 4.0 %collective-permute-start.7 = (f16[2,96,1280]{2,1,0:T(8,128)(2,1)}, f16[2,96,1280]{2,1,0:T(8,128)(2,1)}, u32[]{:S(2)}, u32[]{:S(2)}) collective-permute-start(f16[2,96,1280]{2,1,0:T(8,128)(2,1)} %fusion.30), channel_id=1, source_target_pairs={{0,4},{2,6},{12,8},{14,10},{1,5},{3,7},{13,9},{15,11},{16,20},{18,... | collective-permute-start | bytes 1474568 | tf_op jit(solution)/shard_map/ppermute | solution.py:180
  43.1 2.0 fusion.13
  45.1 1.4 collective-permute-start.8
  47.5 4.2 %shard_map.70 = f32[4,2,96,1280]{3,2,1,0:T(8,128)S(1)} custom-call(s32[1]{0:T(128)} %bitcast.1.place_ref, bf16[384,1024]{1,0:T(8,128)(2,1)S(1)} %bitcast.159, bf16[1024,7168]{1,0:T(8,128)(2,1)} %refs_2_.9, bf16[1024,7168]{1,0:T(8,128)(2,1)} %refs_3_.1), custom_call_target="tpu_custom_call" | custom-call | flops 6000000000 | tf_op jit(solution)/shard_map/pallas_call | solution.py:57
  51.7 5.2 %collective-permute-done.5 = bf16[48,3584]{1,0:T(8,128)(2,1)S(1)} collective-permute-done((bf16[48,3584]{1,0:T(8,128)(2,1)}, bf16[48,3584]{1,0:T(8,128)(2,1)S(1)}, u32[]{:S(2)}, u32[]{:S(2)}) %collective-permute-start.5) | collective-permute-done | bytes 344096 | tf_op jit(solution)/shard_map/ppermute | solution.py:316
  56.9 2.3 %fusion.8 = (f16[2,96,1280]{2,1,0:T(8,128)(2,1)S(1)}, f16[2,96,1280]{2,1,0:T(8,128)(2,1)S(1)}) fusion(f16[2,96,1280]{2,1,0:T(8,128)(2,1)} %collective-permute-done.8, f32[4,2,96,1280]{3,2,1,0:T(8,128)S(1)} %shard_map.68, pred[]{:T(512)S(6)} %or.3, f16[4,2,96,1280]{3,2,1,0:T(8,128)(2,1)S(1)} %collective-permute-done.2, ...), kind=kLoop, calls=%fused_computation.22 | loop fusion | flops 3194880 | bytes 6389761 | tf_op jit(solution)/shard_map/convert_element_type | solution.py:332
  59.2 1.3 collective-permute-start.11
  61.3 2.4 %collective-permute-start.9 = (bf16[2,48,1792]{2,1,0:T(8,128)(2,1)S(1)}, bf16[2,48,1792]{2,1,0:T(8,128)(2,1)S(1)}, u32[]{:S(2)}, u32[]{:S(2)}) collective-permute-start(bf16[2,48,1792]{2,1,0:T(8,128)(2,1)S(1)} %get-tuple-element.204), channel_id=1, source_target_pairs={{0,2},{2,0},{4,6},{6,4},{8,10},{10,8},{12,14},{14,12},{1,3},{3,1},... | collective-permute-start | bytes 1032200 | tf_op jit(solution)/shard_map/ppermute | solution.py:180
  63.8 4.5 %collective-permute-start.15 = (f16[2,96,1280]{2,1,0:T(8,128)(2,1)S(1)}, f16[2,96,1280]{2,1,0:T(8,128)(2,1)S(1)}, u32[]{:S(2)}, u32[]{:S(2)}) collective-permute-start(f16[2,96,1280]{2,1,0:T(8,128)(2,1)S(1)} %fusion.31), channel_id=1, source_target_pairs={{0,4},{2,6},{12,8},{14,10},{1,5},{3,7},{13,9},{15,11},{16,20},{18,... | collective-permute-start | bytes 1474568 | tf_op jit(solution)/shard_map/ppermute | solution.py:180
  68.3 1.7 dynamic-slice_bitcast_fusion
  74.5 3.8 %collective-permute-start.13 = (bf16[2,96,1280]{2,1,0:T(8,128)(2,1)S(1)}, bf16[2,96,1280]{2,1,0:T(8,128)(2,1)S(1)}, u32[]{:S(2)}, u32[]{:S(2)}) collective-permute-start(bf16[2,96,1280]{2,1,0:T(8,128)(2,1)S(1)} %pad_maximum_fusion.2.act), channel_id=1, source_target_pairs={{0,4},{2,6},{12,8},{14,10},{4,0},{6,2},{8,12},{10,14},{1,5},{3,7},... | collective-permute-start | bytes 1474568 | tf_op jit(solution)/shard_map/ppermute | solution.py:180
  81.4 6.6 %collective-permute-start.19 = (f16[2,96,1280]{2,1,0:T(8,128)(2,1)}, f16[2,96,1280]{2,1,0:T(8,128)(2,1)S(1)}, u32[]{:S(2)}, u32[]{:S(2)}) collective-permute-start(f16[2,96,1280]{2,1,0:T(8,128)(2,1)} %fusion.32), channel_id=1, source_target_pairs={{0,4},{2,6},{12,8},{14,10},{1,5},{3,7},{13,9},{15,11},{16,20},{18,... | collective-permute-start | bytes 1474568 | tf_op jit(solution)/shard_map/ppermute | solution.py:180
  88.1 2.0 collective-permute-done.13.side_1
  90.8 1.3 collective-permute-start.17
  92.4 1.4 copy-done.2
  93.8 6.5 %shard_map.71 = f32[4,2,192,512]{3,2,1,0:T(8,128)} custom-call(s32[1]{0:T(128)} %bitcast.1.place_ref, bf16[768,1024]{1,0:T(8,128)(2,1)S(1)} %bitcast.163, bf16[768,1024]{1,0:T(8,128)(2,1)S(1)} %bitcast.164, bf16[1024,7168]{1,0:T(8,128)(2,1)} %refs_2_.9, bf16[1024,7168]{1,0:T(8,128)(2,1)} %refs_3_.1, bf16[2,1024,512]{2,1,0:T(8,128)(2,1)S(1)} %copy-done.2, ...), custom_call_target="tpu_custom_call" | custom-call | tf_op jit(solution)/shard_map/pallas_call | solution.py:57
  100.8 1.5 fusion.3
  102.2 4.4 %collective-permute-start.22 = (f16[2,96,1280]{2,1,0:T(8,128)(2,1)}, f16[2,96,1280]{2,1,0:T(8,128)(2,1)}, u32[]{:S(2)}, u32[]{:S(2)}) collective-permute-start(f16[2,96,1280]{2,1,0:T(8,128)(2,1)} %get-tuple-element.181), channel_id=1, source_target_pairs={{0,4},{2,6},{12,8},{14,10},{4,0},{6,2},{8,12},{10,14},{1,5},{3,7},... | collective-permute-start | bytes 1474568 | tf_op jit(solution)/shard_map/ppermute | solution.py:180
  106.6 1.5 collective-permute-start.23
  108.1 1.3 collective-permute-start.21
  110.6 4.2 %collective-permute-start.26 = (f16[2,192,512]{2,1,0:T(8,128)(2,1)S(1)}, f16[2,192,512]{2,1,0:T(8,128)(2,1)S(1)}, u32[]{:S(2)}, u32[]{:S(2)}) collective-permute-start(f16[2,192,512]{2,1,0:T(8,128)(2,1)S(1)} %fusion.39), channel_id=1, source_target_pairs={{0,4},{2,6},{12,8},{14,10},{1,5},{3,7},{13,9},{15,11},{16,20},{18,... | collective-permute-start | bytes 1179656 | tf_op jit(solution)/shard_map/ppermute | solution.py:180
  115.1 2.4 %fusion.5 = f32[2,96,1280]{2,1,0:T(8,128)S(1)} fusion(f16[2,96,1280]{2,1,0:T(8,128)(2,1)} %collective-permute-done.23, f16[2,96,1280]{2,1,0:T(8,128)(2,1)} %collective-permute-done.22, f32[4,2,96,1280]{3,2,1,0:T(8,128)} %copy-done, f16[4,2,96,1280]{3,2,1,0:T(8,128)(2,1)} %copy-done.15, pred[]{:T(512)S(6)} %or.3), kind=kLoop, calls=%fused_computation.16 | loop fusion | flops 2457600 | bytes 4915201 | tf_op jit(solution)/shard_map/mul | solution.py:260
  119.4 1.5 collective-permute-start.25
  120.8 3.2 %collective-permute-start.24 = (bf16[2,96,1280]{2,1,0:T(8,128)(2,1)}, bf16[2,96,1280]{2,1,0:T(8,128)(2,1)}, u32[]{:S(2)}, u32[]{:S(2)}) collective-permute-start(bf16[2,96,1280]{2,1,0:T(8,128)(2,1)} %pad_maximum_fusion.3.act), channel_id=1, source_target_pairs={{0,4},{2,6},{12,8},{14,10},{4,0},{6,2},{8,12},{10,14},{1,5},{3,7},... | collective-permute-start | bytes 1474568 | tf_op jit(solution)/shard_map/ppermute | solution.py:180
  124.0 1.5 collective-permute-done.21.out_3
  125.9 1.5 copy-done.13
  129.1 1.4 collective-permute-start.28
  130.5 2.6 %collective-permute-start.27 = (f16[2,192,512]{2,1,0:T(8,128)(2,1)}, f16[2,192,512]{2,1,0:T(8,128)(2,1)}, u32[]{:S(2)}, u32[]{:S(2)}) collective-permute-start(f16[2,192,512]{2,1,0:T(8,128)(2,1)} %fusion.40), channel_id=1, source_target_pairs={{0,4},{2,6},{12,8},{14,10},{1,5},{3,7},{13,9},{15,11},{16,20},{18,... | collective-permute-start | bytes 1179656 | tf_op jit(solution)/shard_map/ppermute | solution.py:180
  133.1 3.0 %collective-permute-done.24.side_1 = bf16[2,96,1280]{2,1,0:T(8,128)(2,1)} collective-permute-done((bf16[2,96,1280]{2,1,0:T(8,128)(2,1)}, bf16[2,96,1280]{2,1,0:T(8,128)(2,1)}, u32[]{:S(2)}, u32[]{:S(2)}) %collective-permute-start.24) | collective-permute-done | bytes 491552 | tf_op jit(solution)/shard_map/ppermute | solution.py:180
  136.2 1.5 collective-permute-start.30
  137.6 1.3 collective-permute-start.29
  138.9 2.7 %collective-permute-done.27 = f16[2,192,512]{2,1,0:T(8,128)(2,1)} collective-permute-done((f16[2,192,512]{2,1,0:T(8,128)(2,1)}, f16[2,192,512]{2,1,0:T(8,128)(2,1)}, u32[]{:S(2)}, u32[]{:S(2)}) %collective-permute-start.27) | collective-permute-done | bytes 393248 | tf_op jit(solution)/shard_map/ppermute | solution.py:180
  141.6 3.1 %fusion.18 = (f16[2,192,512]{2,1,0:T(8,128)(2,1)}, f16[2,192,512]{2,1,0:T(8,128)(2,1)}) fusion(f16[2,192,512]{2,1,0:T(8,128)(2,1)} %collective-permute-done.28, f32[4,2,192,512]{3,2,1,0:T(8,128)} %shard_map.71, pred[]{:T(512)S(6)} %or.3, f16[2,192,512]{2,1,0:T(8,128)(2,1)} %collective-permute-done.27), kind=kLoop, calls=%fused_computation.46 | loop fusion | flops 1376256 | bytes 3932161 | tf_op jit(solution)/shard_map/convert_element_type | solution.py:332
  144.6 2.2 %collective-permute-start.31 = (f16[2,192,512]{2,1,0:T(8,128)(2,1)}, f16[2,192,512]{2,1,0:T(8,128)(2,1)}, u32[]{:S(2)}, u32[]{:S(2)}) collective-permute-start(f16[2,192,512]{2,1,0:T(8,128)(2,1)} %get-tuple-element.185), channel_id=1, source_target_pairs={{0,4},{2,6},{12,8},{14,10},{4,0},{6,2},{8,12},{10,14},{1,5},{3,7},... | collective-permute-start | bytes 1179656 | tf_op jit(solution)/shard_map/ppermute | solution.py:180
  146.8 1.4 collective-permute-start.32
  152.3 1.6 maximum_bitcast_fusion.features_ref
  153.9 1.4 collective-permute-start.36
  155.4 1.4 fusion.15
  157.9 1.4 collective-permute-start.34
  159.3 6.7 %collective-permute-start.33 = (bf16[2,192,512]{2,1,0:T(8,128)(2,1)}, bf16[2,192,512]{2,1,0:T(8,128)(2,1)}, u32[]{:S(2)}, u32[]{:S(2)}) collective-permute-start(bf16[2,192,512]{2,1,0:T(8,128)(2,1)} %pad_maximum_fusion.4.act), channel_id=1, source_target_pairs={{0,4},{2,6},{12,8},{14,10},{4,0},{6,2},{8,12},{10,14},{1,5},{3,7},... | collective-permute-start | bytes 1179656 | tf_op jit(solution)/shard_map/ppermute | solution.py:180
  167.1 6.9 %collective-permute-start.35 = (bf16[2,48,1792]{2,1,0:T(8,128)(2,1)}, bf16[2,48,1792]{2,1,0:T(8,128)(2,1)}, u32[]{:S(2)}, u32[]{:S(2)}) collective-permute-start(bf16[2,48,1792]{2,1,0:T(8,128)(2,1)} %get-tuple-element.200), channel_id=1, source_target_pairs={{0,2},{2,0},{4,6},{6,4},{8,10},{10,8},{12,14},{14,12},{1,3},{3,1},... | collective-permute-start | bytes 1032200 | tf_op jit(solution)/shard_map/ppermute | solution.py:180
  174.0 2.0 collective-permute-done.35
  176.0 2.1 shard_map.73
  178.1 1.5 collective-permute-start.41
  179.6 1.3 collective-permute-start.37
  182.9 1.3 collective-permute-start.42
  184.2 7.0 %shard_map.74 = (f32[1024,3584]{1,0:T(8,128)}, f32[1024,3584]{1,0:T(8,128)}) custom-call(s32[1]{0:T(128)} %bitcast.59.place_ref, bf16[1024,768]{1,0:T(8,128)(2,1)S(1)} %maximum_bitcast_fusion.features_ref, bf16[4,1,2,96,1280]{4,3,2,1,0:T(8,128)(2,1)S(1)} %bitcast.165, bf16[4,1,2,96,1280]{4,3,2,1,0:T(8,128)(2,1)S(1)} %bitcast.167), custom_call_target="tpu_custom_call" | custom-call | flops 4026531840 | bytes 15990784 | tf_op jit(solution)/shard_map/pallas_call | solution.py:101
  191.2 1.5 collective-permute-start.39
  193.8 7.0 %shard_map.75 = (f32[1024,3584]{1,0:T(8,128)}, f32[1024,3584]{1,0:T(8,128)}) custom-call(s32[1]{0:T(128)} %bitcast.62.place_ref, bf16[1024,768]{1,0:T(8,128)(2,1)S(1)} %maximum_bitcast_fusion.features_ref, bf16[4,1,2,96,1280]{4,3,2,1,0:T(8,128)(2,1)S(1)} %bitcast.166, ...), custom_call_target="tpu_custom_call", output_to_operand_aliasing={{0}: (4, {}), {1}: (5, {})} | custom-call | flops 4026531840 | bytes 15990784 | tf_op jit(solution)/shard_map/pallas_call | solution.py:101
  200.8 2.7 %collective-permute-done.39.out_3 = bf16[2,192,512]{2,1,0:T(8,128)(2,1)S(1)} collective-permute-done((bf16[2,192,512]{2,1,0:T(8,128)(2,1)S(1)}, bf16[2,192,512]{2,1,0:T(8,128)(2,1)S(1)}, u32[]{:S(2)}, u32[]{:S(2)}) %collective-permute-start.39) | collective-permute-done | bytes 393248 | tf_op jit(solution)/shard_map/ppermute | solution.py:180
  203.5 1.5 shard_map.76
  204.9 3.6 %collective-permute-start.43 = (bf16[4,2,192,512]{3,2,1,0:T(8,128)(2,1)S(1)}, bf16[4,2,192,512]{3,2,1,0:T(8,128)(2,1)S(1)}, u32[]{:S(2)}, u32[]{:S(2)}) collective-permute-start(bf16[4,2,192,512]{3,2,1,0:T(8,128)(2,1)S(1)} %shard_map.76), channel_id=1, source_target_pairs={{0,2},{2,0},{4,6},{6,4},{8,10},{10,8},{12,14},{14,12},{1,3},{3,1},... | collective-permute-start | bytes 4718600 | tf_op jit(solution)/shard_map/ppermute | solution.py:180
  208.5 3.4 %shard_map.77 = (f32[1024,3584]{1,0:T(8,128)}, f32[1024,3584]{1,0:T(8,128)}) custom-call(s32[1]{0:T(128)} %bitcast.59.place_ref, bf16[1024,768]{1,0:T(8,128)(2,1)S(1)} %maximum_bitcast_fusion.features_ref, bf16[4,1,2,192,512]{4,3,2,1,0:T(8,128)(2,1)S(1)} %bitcast.162, ...), custom_call_target="tpu_custom_call", output_to_operand_aliasing={{0}: (3, {}), {1}: (4, {})} | custom-call | flops 1610612736 | bytes 7340032 | tf_op jit(solution)/shard_map/pallas_call | solution.py:101
  212.0 3.4 %shard_map.78 = (f32[1024,3584]{1,0:T(8,128)}, f32[1024,3584]{1,0:T(8,128)}) custom-call(s32[1]{0:T(128)} %bitcast.62.place_ref, bf16[1024,768]{1,0:T(8,128)(2,1)S(1)} %maximum_bitcast_fusion.features_ref, bf16[4,1,2,192,512]{4,3,2,1,0:T(8,128)(2,1)S(1)} %bitcast.169, ...), custom_call_target="tpu_custom_call", output_to_operand_aliasing={{0}: (3, {}), {1}: (4, {})} | custom-call | flops 1610612736 | bytes 7340032 | tf_op jit(solution)/shard_map/pallas_call | solution.py:101
  (130 shorter events, 30.8 us)
Async XLA Ops:
  0.6 11.2 %collective-permute-start.1 = (bf16[384,512]{1,0:T(8,128)(2,1)}, bf16[384,512]{1,0:T(8,128)(2,1)S(1)}, u32[]{:S(2)}, u32[]{:S(2)}) collective-permute-start(bf16[384,512]{1,0:T(8,128)(2,1)} %bitcast.177), channel_id=1, source_target_pairs={{0,1},{1,0},{2,3},{3,2},{4,5},{5,4},{6,7},{7,6},{8,9},{9,8},{10,11... | collective-permute-start | bytes 1179656 | tf_op jit(solution)/shard_map/ppermute | solution.py:214
  2.8 9.9 %collective-permute-start = (bf16[384,512]{1,0:T(8,128)(2,1)}, bf16[384,512]{1,0:T(8,128)(2,1)S(1)}, u32[]{:S(2)}, u32[]{:S(2)}) collective-permute-start(bf16[384,512]{1,0:T(8,128)(2,1)} %bitcast.178), channel_id=1, source_target_pairs={{0,16},{16,0},{1,17},{17,1},{2,18},{18,2},{3,19},{19,3},{4,20},{20... | collective-permute-start | bytes 1179656 | tf_op jit(solution)/shard_map/ppermute | solution.py:213
  19.9 6.1 %collective-permute-start.2 = (f16[4,2,96,1280]{3,2,1,0:T(8,128)(2,1)}, f16[4,2,96,1280]{3,2,1,0:T(8,128)(2,1)S(1)}, u32[]{:S(2)}, u32[]{:S(2)}) collective-permute-start(f16[4,2,96,1280]{3,2,1,0:T(8,128)(2,1)} %convert_element_type.194), channel_id=1, source_target_pairs={{0,2},{2,0},{4,6},{6,4},{8,10},{10,8},{12,14},{14,12},{1,3},{3,1},... | collective-permute-start | bytes 5898248 | tf_op jit(solution)/shard_map/ppermute | solution.py:180
  21.7 10.7 %collective-permute-start.3 = (bf16[384,512]{1,0:T(8,128)(2,1)S(1)}, bf16[384,512]{1,0:T(8,128)(2,1)S(1)}, u32[]{:S(2)}, u32[]{:S(2)}) collective-permute-start(bf16[384,512]{1,0:T(8,128)(2,1)S(1)} %collective-permute-done), channel_id=1, source_target_pairs={{0,1},{1,0},{2,3},{3,2},{4,5},{5,4},{6,7},{7,6},{8,9},{9,8},{10,11... | collective-permute-start | bytes 1179656 | tf_op jit(solution)/shard_map/ppermute | solution.py:215
  26.9 16.2 %collective-permute-start.4 = (f16[2,96,1280]{2,1,0:T(8,128)(2,1)}, f16[2,96,1280]{2,1,0:T(8,128)(2,1)}, u32[]{:S(2)}, u32[]{:S(2)}) collective-permute-start(f16[2,96,1280]{2,1,0:T(8,128)(2,1)} %fusion.33), channel_id=1, source_target_pairs={{0,4},{2,6},{12,8},{14,10},{1,5},{3,7},{13,9},{15,11},{16,20},{18,... | collective-permute-start | bytes 1474568 | tf_op jit(solution)/shard_map/ppermute | solution.py:180
  37.3 9.2 %copy-start.22 = (bf16[1,48,7168]{2,1,0:T(8,128)(2,1)S(1)}, bf16[1,48,7168]{2,1,0:T(8,128)(2,1)}, u32[]{:S(2)}) copy-start(bf16[1,48,7168]{2,1,0:T(8,128)(2,1)} %param.7) | copy-start | bytes 2064388
  37.3 19.5 %collective-permute-start.6 = (f16[4,2,96,1280]{3,2,1,0:T(8,128)(2,1)S(1)}, f16[4,2,96,1280]{3,2,1,0:T(8,128)(2,1)S(1)}, u32[]{:S(2)}, u32[]{:S(2)}) collective-permute-start(f16[4,2,96,1280]{3,2,1,0:T(8,128)(2,1)S(1)} %convert_element_type.198), channel_id=1, source_target_pairs={{0,2},{2,0},{4,6},{6,4},{8,10},{10,8},{12,14},{14,12},{1,3},{3,1},... | collective-permute-start | bytes 5898248 | tf_op jit(solution)/shard_map/ppermute | solution.py:180
  39.1 17.8 %collective-permute-start.7 = (f16[2,96,1280]{2,1,0:T(8,128)(2,1)}, f16[2,96,1280]{2,1,0:T(8,128)(2,1)}, u32[]{:S(2)}, u32[]{:S(2)}) collective-permute-start(f16[2,96,1280]{2,1,0:T(8,128)(2,1)} %fusion.30), channel_id=1, source_target_pairs={{0,4},{2,6},{12,8},{14,10},{1,5},{3,7},{13,9},{15,11},{16,20},{18,... | collective-permute-start | bytes 1474568 | tf_op jit(solution)/shard_map/ppermute | solution.py:180
  45.1 11.8 %collective-permute-start.8 = (f16[2,96,1280]{2,1,0:T(8,128)(2,1)}, f16[2,96,1280]{2,1,0:T(8,128)(2,1)}, u32[]{:S(2)}, u32[]{:S(2)}) collective-permute-start(f16[2,96,1280]{2,1,0:T(8,128)(2,1)} %fusion.13), channel_id=1, source_target_pairs={{4,8},{6,10},{8,4},{10,6},{5,9},{7,11},{9,5},{11,7},{20,24},{22,26... | collective-permute-start | bytes 1474568 | tf_op jit(solution)/shard_map/ppermute | solution.py:180
  47.3 9.6 %collective-permute-start.5 = (bf16[48,3584]{1,0:T(8,128)(2,1)}, bf16[48,3584]{1,0:T(8,128)(2,1)S(1)}, u32[]{:S(2)}, u32[]{:S(2)}) collective-permute-start(bf16[48,3584]{1,0:T(8,128)(2,1)} %get-tuple-element.205), channel_id=1, source_target_pairs={{0,1},{1,0},{2,3},{3,2},{4,5},{5,4},{6,7},{7,6},{8,9},{9,8},{10,11... | collective-permute-start | bytes 1032200 | tf_op jit(solution)/shard_map/ppermute | solution.py:316
  51.7 49.1 %copy-start = (f32[4,2,96,1280]{3,2,1,0:T(8,128)}, f32[4,2,96,1280]{3,2,1,0:T(8,128)S(1)}, u32[]{:S(2)}) copy-start(f32[4,2,96,1280]{3,2,1,0:T(8,128)S(1)} %shard_map.70) | copy-start | bytes 11796484
  56.9 43.9 %copy-start.15 = (f16[4,2,96,1280]{3,2,1,0:T(8,128)(2,1)}, f16[4,2,96,1280]{3,2,1,0:T(8,128)(2,1)S(1)}, u32[]{:S(2)}) copy-start(f16[4,2,96,1280]{3,2,1,0:T(8,128)(2,1)S(1)} %collective-permute-done.6) | copy-start | bytes 5898244
  59.2 12.7 %collective-permute-start.11 = (f16[2,96,1280]{2,1,0:T(8,128)(2,1)S(1)}, f16[2,96,1280]{2,1,0:T(8,128)(2,1)S(1)}, u32[]{:S(2)}, u32[]{:S(2)}) collective-permute-start(f16[2,96,1280]{2,1,0:T(8,128)(2,1)S(1)} %get-tuple-element.183), channel_id=1, source_target_pairs={{0,4},{2,6},{12,8},{14,10},{4,0},{6,2},{8,12},{10,14},{1,5},{3,7},... | collective-permute-start | bytes 1474568 | tf_op jit(solution)/shard_map/ppermute | solution.py:180
  60.6 11.3 %collective-permute-start.12 = (f16[2,96,1280]{2,1,0:T(8,128)(2,1)S(1)}, f16[2,96,1280]{2,1,0:T(8,128)(2,1)S(1)}, u32[]{:S(2)}, u32[]{:S(2)}) collective-permute-start(f16[2,96,1280]{2,1,0:T(8,128)(2,1)S(1)} %get-tuple-element.184), channel_id=1, source_target_pairs={{4,8},{6,10},{8,4},{10,6},{5,9},{7,11},{9,5},{11,7},{20,24},{22,26... | collective-permute-start | bytes 1474568 | tf_op jit(solution)/shard_map/ppermute | solution.py:180
  61.3 9.4 %collective-permute-start.9 = (bf16[2,48,1792]{2,1,0:T(8,128)(2,1)S(1)}, bf16[2,48,1792]{2,1,0:T(8,128)(2,1)S(1)}, u32[]{:S(2)}, u32[]{:S(2)}) collective-permute-start(bf16[2,48,1792]{2,1,0:T(8,128)(2,1)S(1)} %get-tuple-element.204), channel_id=1, source_target_pairs={{0,2},{2,0},{4,6},{6,4},{8,10},{10,8},{12,14},{14,12},{1,3},{3,1},... | collective-permute-start | bytes 1032200 | tf_op jit(solution)/shard_map/ppermute | solution.py:180
  63.8 15.8 %collective-permute-start.15 = (f16[2,96,1280]{2,1,0:T(8,128)(2,1)S(1)}, f16[2,96,1280]{2,1,0:T(8,128)(2,1)S(1)}, u32[]{:S(2)}, u32[]{:S(2)}) collective-permute-start(f16[2,96,1280]{2,1,0:T(8,128)(2,1)S(1)} %fusion.31), channel_id=1, source_target_pairs={{0,4},{2,6},{12,8},{14,10},{1,5},{3,7},{13,9},{15,11},{16,20},{18,... | collective-permute-start | bytes 1474568 | tf_op jit(solution)/shard_map/ppermute | solution.py:180
  70.2 8.2 %collective-permute-start.16 = (bf16[2,1024,512]{2,1,0:T(8,128)(2,1)S(1)}, bf16[2,1024,512]{2,1,0:T(8,128)(2,1)S(1)}, u32[]{:S(2)}, u32[]{:S(2)}) collective-permute-start(bf16[2,1024,512]{2,1,0:T(8,128)(2,1)S(1)} %pad_maximum_fusion), channel_id=1, source_target_pairs={{0,2},{2,0},{4,6},{6,4},{8,10},{10,8},{12,14},{14,12},{1,3},{3,1},... | collective-permute-start | bytes 6291464 | tf_op jit(solution)/shard_map/ppermute | solution.py:180
  70.7 7.7 %collective-permute-start.10 = (bf16[4,2,96,1024]{3,2,0,1:T(8,128)(2,1)S(1)}, bf16[4,2,96,1024]{3,2,0,1:T(8,128)(2,1)S(1)}, u32[]{:S(2)}, u32[]{:S(2)}) collective-permute-start(bf16[4,2,96,1024]{3,2,0,1:T(8,128)(2,1)S(1)} %pad_maximum_fusion.1), channel_id=1, source_target_pairs={{0,2},{2,0},{4,6},{6,4},{8,10},{10,8},{12,14},{14,12},{1,3},{3,1},... | collective-permute-start | bytes 4718600 | tf_op jit(solution)/shard_map/ppermute | solution.py:180
  73.6 7.1 %copy-start.3 = (bf16[2,96,1280]{2,1,0:T(8,128)(2,1)}, bf16[2,96,1280]{2,1,0:T(8,128)(2,1)S(1)}, u32[]{:S(2)}) copy-start(bf16[2,96,1280]{2,1,0:T(8,128)(2,1)S(1)} %pad_maximum_fusion.2.act) | copy-start | bytes 1474564
  73.7 14.4 %collective-permute-start.14 = (bf16[2,96,1280]{2,1,0:T(8,128)(2,1)S(1)}, bf16[2,96,1280]{2,1,0:T(8,128)(2,1)S(1)}, u32[]{:S(2)}, u32[]{:S(2)}) collective-permute-start(bf16[2,96,1280]{2,1,0:T(8,128)(2,1)S(1)} %pad_maximum_fusion.2.act), channel_id=1, source_target_pairs={{4,8},{6,10},{8,4},{10,6},{5,9},{7,11},{9,5},{11,7},{20,24},{22,26... | collective-permute-start | bytes 1474568 | tf_op jit(solution)/shard_map/ppermute | solution.py:180
  74.5 15.6 %collective-permute-start.13 = (bf16[2,96,1280]{2,1,0:T(8,128)(2,1)S(1)}, bf16[2,96,1280]{2,1,0:T(8,128)(2,1)S(1)}, u32[]{:S(2)}, u32[]{:S(2)}) collective-permute-start(bf16[2,96,1280]{2,1,0:T(8,128)(2,1)S(1)} %pad_maximum_fusion.2.act), channel_id=1, source_target_pairs={{0,4},{2,6},{12,8},{14,10},{4,0},{6,2},{8,12},{10,14},{1,5},{3,7},... | collective-permute-start | bytes 1474568 | tf_op jit(solution)/shard_map/ppermute | solution.py:180
  78.4 2.3 %copy-start.1 = (bf16[2,1024,512]{2,1,0:T(8,128)(2,1)}, bf16[2,1024,512]{2,1,0:T(8,128)(2,1)S(1)}, u32[]{:S(2)}) copy-start(bf16[2,1024,512]{2,1,0:T(8,128)(2,1)S(1)} %collective-permute-done.16.refs_4_.refs_5_) | copy-start | bytes 6291460
  80.7 19.7 %collective-permute-start.20 = (f16[2,96,1280]{2,1,0:T(8,128)(2,1)S(1)}, f16[2,96,1280]{2,1,0:T(8,128)(2,1)S(1)}, u32[]{:S(2)}, u32[]{:S(2)}) collective-permute-start(f16[2,96,1280]{2,1,0:T(8,128)(2,1)S(1)} %fusion.6), channel_id=1, source_target_pairs={{4,8},{6,10},{8,4},{10,6},{5,9},{7,11},{9,5},{11,7},{20,24},{22,26... | collective-permute-start | bytes 1474568 | tf_op jit(solution)/shard_map/ppermute | solution.py:180
  81.4 19.3 %collective-permute-start.19 = (f16[2,96,1280]{2,1,0:T(8,128)(2,1)}, f16[2,96,1280]{2,1,0:T(8,128)(2,1)S(1)}, u32[]{:S(2)}, u32[]{:S(2)}) collective-permute-start(f16[2,96,1280]{2,1,0:T(8,128)(2,1)} %fusion.32), channel_id=1, source_target_pairs={{0,4},{2,6},{12,8},{14,10},{1,5},{3,7},{13,9},{15,11},{16,20},{18,... | collective-permute-start | bytes 1474568 | tf_op jit(solution)/shard_map/ppermute | solution.py:180
  88.1 4.3 %copy-start.5 = (bf16[2,96,1280]{2,1,0:T(8,128)(2,1)}, bf16[2,96,1280]{2,1,0:T(8,128)(2,1)S(1)}, u32[]{:S(2)}) copy-start(bf16[2,96,1280]{2,1,0:T(8,128)(2,1)S(1)} %collective-permute-done.14.centre_1) | copy-start | bytes 1474564
  90.1 2.3 %copy-start.7 = (bf16[2,96,1280]{2,1,0:T(8,128)(2,1)}, bf16[2,96,1280]{2,1,0:T(8,128)(2,1)S(1)}, u32[]{:S(2)}) copy-start(bf16[2,96,1280]{2,1,0:T(8,128)(2,1)S(1)} %collective-permute-done.13.side_1) | copy-start | bytes 1474564
  90.1 18.0 %collective-permute-start.18 = (bf16[2,96,1280]{2,1,0:T(8,128)(2,1)S(1)}, bf16[2,96,1280]{2,1,0:T(8,128)(2,1)S(1)}, u32[]{:S(2)}, u32[]{:S(2)}) collective-permute-start(bf16[2,96,1280]{2,1,0:T(8,128)(2,1)S(1)} %collective-permute-done.13.side_1), channel_id=1, source_target_pairs={{4,8},{6,10},{8,4},{10,6},{5,9},{7,11},{9,5},{11,7},{20,24},{22,26... | collective-permute-start | bytes 1474568 | tf_op jit(solution)/shard_map/ppermute | solution.py:180
  90.8 17.3 %collective-permute-start.17 = (bf16[2,96,1280]{2,1,0:T(8,128)(2,1)S(1)}, bf16[2,96,1280]{2,1,0:T(8,128)(2,1)S(1)}, u32[]{:S(2)}, u32[]{:S(2)}) collective-permute-start(bf16[2,96,1280]{2,1,0:T(8,128)(2,1)S(1)} %collective-permute-done.14.centre_1), channel_id=1, source_target_pairs={{4,0},{6,2},{8,12},{10,14},{5,1},{7,3},{9,13},{11,15},{20,16},{22,... | collective-permute-start | bytes 1474568 | tf_op jit(solution)/shard_map/ppermute | solution.py:180
  102.2 12.8 %collective-permute-start.22 = (f16[2,96,1280]{2,1,0:T(8,128)(2,1)}, f16[2,96,1280]{2,1,0:T(8,128)(2,1)}, u32[]{:S(2)}, u32[]{:S(2)}) collective-permute-start(f16[2,96,1280]{2,1,0:T(8,128)(2,1)} %get-tuple-element.181), channel_id=1, source_target_pairs={{0,4},{2,6},{12,8},{14,10},{4,0},{6,2},{8,12},{10,14},{1,5},{3,7},... | collective-permute-start | bytes 1474568 | tf_op jit(solution)/shard_map/ppermute | solution.py:180
  106.6 8.5 %collective-permute-start.23 = (f16[2,96,1280]{2,1,0:T(8,128)(2,1)}, f16[2,96,1280]{2,1,0:T(8,128)(2,1)}, u32[]{:S(2)}, u32[]{:S(2)}) collective-permute-start(f16[2,96,1280]{2,1,0:T(8,128)(2,1)} %get-tuple-element.182), channel_id=1, source_target_pairs={{4,8},{6,10},{8,4},{10,6},{5,9},{7,11},{9,5},{11,7},{20,24},{22,26... | collective-permute-start | bytes 1474568 | tf_op jit(solution)/shard_map/ppermute | solution.py:180
  108.1 9.4 %copy-start.9 = (bf16[2,96,1280]{2,1,0:T(8,128)(2,1)}, bf16[2,96,1280]{2,1,0:T(8,128)(2,1)S(1)}, u32[]{:S(2)}) copy-start(bf16[2,96,1280]{2,1,0:T(8,128)(2,1)S(1)} %collective-permute-done.18.share_2) | copy-start | bytes 1474564
  108.1 9.4 %copy-start.11 = (bf16[2,96,1280]{2,1,0:T(8,128)(2,1)}, bf16[2,96,1280]{2,1,0:T(8,128)(2,1)S(1)}, u32[]{:S(2)}) copy-start(bf16[2,96,1280]{2,1,0:T(8,128)(2,1)S(1)} %collective-permute-done.17.out_2) | copy-start | bytes 1474564
  108.1 17.4 %collective-permute-start.21 = (bf16[2,96,1280]{2,1,0:T(8,128)(2,1)S(1)}, bf16[2,96,1280]{2,1,0:T(8,128)(2,1)S(1)}, u32[]{:S(2)}, u32[]{:S(2)}) collective-permute-start(bf16[2,96,1280]{2,1,0:T(8,128)(2,1)S(1)} %collective-permute-done.18.share_2), channel_id=1, source_target_pairs={{4,0},{6,2},{8,12},{10,14},{5,1},{7,3},{9,13},{11,15},{20,16},{22,... | collective-permute-start | bytes 1474568 | tf_op jit(solution)/shard_map/ppermute | solution.py:180
  110.6 6.9 %copy-start.17 = (bf16[96,1792]{1,0:T(8,128)(2,1)S(1)}, bf16[96,1792]{1,0:T(8,128)(2,1)}, u32[]{:S(2)}) copy-start(bf16[96,1792]{1,0:T(8,128)(2,1)} %get-tuple-element.202) | copy-start | bytes 1032196
  110.6 15.3 %collective-permute-start.26 = (f16[2,192,512]{2,1,0:T(8,128)(2,1)S(1)}, f16[2,192,512]{2,1,0:T(8,128)(2,1)S(1)}, u32[]{:S(2)}, u32[]{:S(2)}) collective-permute-start(f16[2,192,512]{2,1,0:T(8,128)(2,1)S(1)} %fusion.39), channel_id=1, source_target_pairs={{0,4},{2,6},{12,8},{14,10},{1,5},{3,7},{13,9},{15,11},{16,20},{18,... | collective-permute-start | bytes 1179656 | tf_op jit(solution)/shard_map/ppermute | solution.py:180
  117.5 8.0 %copy-start.4 = (bf16[2,96,1280]{2,1,0:T(8,128)(2,1)S(1)}, bf16[2,96,1280]{2,1,0:T(8,128)(2,1)}, u32[]{:S(2)}) copy-start(bf16[2,96,1280]{2,1,0:T(8,128)(2,1)} %copy-done.3) | copy-start | bytes 1474564
  117.5 8.0 %copy-start.6 = (bf16[2,96,1280]{2,1,0:T(8,128)(2,1)S(1)}, bf16[2,96,1280]{2,1,0:T(8,128)(2,1)}, u32[]{:S(2)}) copy-start(bf16[2,96,1280]{2,1,0:T(8,128)(2,1)} %copy-done.5) | copy-start | bytes 1474564
  117.5 8.0 %copy-start.8 = (bf16[2,96,1280]{2,1,0:T(8,128)(2,1)S(1)}, bf16[2,96,1280]{2,1,0:T(8,128)(2,1)}, u32[]{:S(2)}) copy-start(bf16[2,96,1280]{2,1,0:T(8,128)(2,1)} %copy-done.7) | copy-start | bytes 1474564
  117.5 8.0 %copy-start.10 = (bf16[2,96,1280]{2,1,0:T(8,128)(2,1)S(1)}, bf16[2,96,1280]{2,1,0:T(8,128)(2,1)}, u32[]{:S(2)}) copy-start(bf16[2,96,1280]{2,1,0:T(8,128)(2,1)} %copy-done.9) | copy-start | bytes 1474564
  117.6 8.0 %copy-start.12 = (bf16[2,96,1280]{2,1,0:T(8,128)(2,1)S(1)}, bf16[2,96,1280]{2,1,0:T(8,128)(2,1)}, u32[]{:S(2)}) copy-start(bf16[2,96,1280]{2,1,0:T(8,128)(2,1)} %copy-done.11) | copy-start | bytes 1474564
  119.4 13.7 %collective-permute-start.25 = (bf16[2,96,1280]{2,1,0:T(8,128)(2,1)}, bf16[2,96,1280]{2,1,0:T(8,128)(2,1)}, u32[]{:S(2)}, u32[]{:S(2)}) collective-permute-start(bf16[2,96,1280]{2,1,0:T(8,128)(2,1)} %pad_maximum_fusion.3.act), channel_id=1, source_target_pairs={{4,8},{6,10},{8,4},{10,6},{5,9},{7,11},{9,5},{11,7},{20,24},{22,26... | collective-permute-start | bytes 1474568 | tf_op jit(solution)/shard_map/ppermute | solution.py:180
  120.8 15.3 %collective-permute-start.24 = (bf16[2,96,1280]{2,1,0:T(8,128)(2,1)}, bf16[2,96,1280]{2,1,0:T(8,128)(2,1)}, u32[]{:S(2)}, u32[]{:S(2)}) collective-permute-start(bf16[2,96,1280]{2,1,0:T(8,128)(2,1)} %pad_maximum_fusion.3.act), channel_id=1, source_target_pairs={{0,4},{2,6},{12,8},{14,10},{4,0},{6,2},{8,12},{10,14},{1,5},{3,7},... | collective-permute-start | bytes 1474568 | tf_op jit(solution)/shard_map/ppermute | solution.py:180
  129.1 9.8 %collective-permute-start.28 = (f16[2,192,512]{2,1,0:T(8,128)(2,1)}, f16[2,192,512]{2,1,0:T(8,128)(2,1)}, u32[]{:S(2)}, u32[]{:S(2)}) collective-permute-start(f16[2,192,512]{2,1,0:T(8,128)(2,1)} %fusion.16), channel_id=1, source_target_pairs={{4,8},{6,10},{8,4},{10,6},{5,9},{7,11},{9,5},{11,7},{20,24},{22,26... | collective-permute-start | bytes 1179656 | tf_op jit(solution)/shard_map/ppermute | solution.py:180
  130.5 11.0 %collective-permute-start.27 = (f16[2,192,512]{2,1,0:T(8,128)(2,1)}, f16[2,192,512]{2,1,0:T(8,128)(2,1)}, u32[]{:S(2)}, u32[]{:S(2)}) collective-permute-start(f16[2,192,512]{2,1,0:T(8,128)(2,1)} %fusion.40), channel_id=1, source_target_pairs={{0,4},{2,6},{12,8},{14,10},{1,5},{3,7},{13,9},{15,11},{16,20},{18,... | collective-permute-start | bytes 1179656 | tf_op jit(solution)/shard_map/ppermute | solution.py:180
  136.2 17.8 %collective-permute-start.30 = (bf16[2,96,1280]{2,1,0:T(8,128)(2,1)}, bf16[2,96,1280]{2,1,0:T(8,128)(2,1)}, u32[]{:S(2)}, u32[]{:S(2)}) collective-permute-start(bf16[2,96,1280]{2,1,0:T(8,128)(2,1)} %collective-permute-done.24.side_1), channel_id=1, source_target_pairs={{4,8},{6,10},{8,4},{10,6},{5,9},{7,11},{9,5},{11,7},{20,24},{22,26... | collective-permute-start | bytes 1474568 | tf_op jit(solution)/shard_map/ppermute | solution.py:180
  137.6 16.3 %collective-permute-start.29 = (bf16[2,96,1280]{2,1,0:T(8,128)(2,1)}, bf16[2,96,1280]{2,1,0:T(8,128)(2,1)}, u32[]{:S(2)}, u32[]{:S(2)}) collective-permute-start(bf16[2,96,1280]{2,1,0:T(8,128)(2,1)} %collective-permute-done.25.centre_1), channel_id=1, source_target_pairs={{4,0},{6,2},{8,12},{10,14},{5,1},{7,3},{9,13},{11,15},{20,16},{22,... | collective-permute-start | bytes 1474568 | tf_op jit(solution)/shard_map/ppermute | solution.py:180
  144.6 10.7 %collective-permute-start.31 = (f16[2,192,512]{2,1,0:T(8,128)(2,1)}, f16[2,192,512]{2,1,0:T(8,128)(2,1)}, u32[]{:S(2)}, u32[]{:S(2)}) collective-permute-start(f16[2,192,512]{2,1,0:T(8,128)(2,1)} %get-tuple-element.185), channel_id=1, source_target_pairs={{0,4},{2,6},{12,8},{14,10},{4,0},{6,2},{8,12},{10,14},{1,5},{3,7},... | collective-permute-start | bytes 1179656 | tf_op jit(solution)/shard_map/ppermute | solution.py:180
  146.8 8.5 %collective-permute-start.32 = (f16[2,192,512]{2,1,0:T(8,128)(2,1)}, f16[2,192,512]{2,1,0:T(8,128)(2,1)}, u32[]{:S(2)}, u32[]{:S(2)}) collective-permute-start(f16[2,192,512]{2,1,0:T(8,128)(2,1)} %get-tuple-element.186), channel_id=1, source_target_pairs={{4,8},{6,10},{8,4},{10,6},{5,9},{7,11},{9,5},{11,7},{20,24},{22,26... | collective-permute-start | bytes 1179656 | tf_op jit(solution)/shard_map/ppermute | solution.py:180
  152.3 3.1 %copy-start.14 = (f32[4,2,192,512]{3,2,1,0:T(8,128)S(1)}, f32[4,2,192,512]{3,2,1,0:T(8,128)}, u32[]{:S(2)}) copy-start(f32[4,2,192,512]{3,2,1,0:T(8,128)} %shard_map.71) | copy-start | bytes 9437188
  153.9 2.9 %copy-start.21 = (bf16[1,2,96,512]{3,2,1,0:T(8,128)(2,1)S(1)}, bf16[1,2,96,512]{3,2,1,0:T(8,128)(2,1)}, u32[]{:S(2)}) copy-start(bf16[1,2,96,512]{3,2,1,0:T(8,128)(2,1)} %pad_maximum_fusion.5) | copy-start | bytes 589828
  153.9 20.0 %collective-permute-start.36 = (bf16[2,96,1280]{2,1,0:T(8,128)(2,1)}, bf16[2,96,1280]{2,1,0:T(8,128)(2,1)}, u32[]{:S(2)}, u32[]{:S(2)}) collective-permute-start(bf16[2,96,1280]{2,1,0:T(8,128)(2,1)} %collective-permute-done.30.share_2), channel_id=1, source_target_pairs={{4,0},{6,2},{8,12},{10,14},{5,1},{7,3},{9,13},{11,15},{20,16},{22,... | collective-permute-start | bytes 1474568 | tf_op jit(solution)/shard_map/ppermute | solution.py:180
  156.8 9.3 %copy-start.19 = (bf16[1,96,1280]{2,1,0:T(8,128)(2,1)S(1)}, bf16[1,96,1280]{2,1,0:T(8,128)(2,1)}, u32[]{:S(2)}) copy-start(bf16[1,96,1280]{2,1,0:T(8,128)(2,1)} %get-tuple-element.191) | copy-start | bytes 737284
  156.8 9.3 %copy-start.20 = (bf16[1,96,1280]{2,1,0:T(8,128)(2,1)S(1)}, bf16[1,96,1280]{2,1,0:T(8,128)(2,1)}, u32[]{:S(2)}) copy-start(bf16[1,96,1280]{2,1,0:T(8,128)(2,1)} %get-tuple-element.192) | copy-start | bytes 737284
  157.9 21.7 %collective-permute-start.34 = (bf16[2,192,512]{2,1,0:T(8,128)(2,1)}, bf16[2,192,512]{2,1,0:T(8,128)(2,1)}, u32[]{:S(2)}, u32[]{:S(2)}) collective-permute-start(bf16[2,192,512]{2,1,0:T(8,128)(2,1)} %pad_maximum_fusion.4.act), channel_id=1, source_target_pairs={{4,8},{6,10},{8,4},{10,6},{5,9},{7,11},{9,5},{11,7},{20,24},{22,26... | collective-permute-start | bytes 1179656 | tf_op jit(solution)/shard_map/ppermute | solution.py:180
  159.3 20.3 %collective-permute-start.33 = (bf16[2,192,512]{2,1,0:T(8,128)(2,1)}, bf16[2,192,512]{2,1,0:T(8,128)(2,1)}, u32[]{:S(2)}, u32[]{:S(2)}) collective-permute-start(bf16[2,192,512]{2,1,0:T(8,128)(2,1)} %pad_maximum_fusion.4.act), channel_id=1, source_target_pairs={{0,4},{2,6},{12,8},{14,10},{4,0},{6,2},{8,12},{10,14},{1,5},{3,7},... | collective-permute-start | bytes 1179656 | tf_op jit(solution)/shard_map/ppermute | solution.py:180
  167.1 8.9 %collective-permute-start.35 = (bf16[2,48,1792]{2,1,0:T(8,128)(2,1)}, bf16[2,48,1792]{2,1,0:T(8,128)(2,1)}, u32[]{:S(2)}, u32[]{:S(2)}) collective-permute-start(bf16[2,48,1792]{2,1,0:T(8,128)(2,1)} %get-tuple-element.200), channel_id=1, source_target_pairs={{0,2},{2,0},{4,6},{6,4},{8,10},{10,8},{12,14},{14,12},{1,3},{3,1},... | collective-permute-start | bytes 1032200 | tf_op jit(solution)/shard_map/ppermute | solution.py:180
  174.0 7.6 %copy-start.18 = (bf16[2,48,1792]{2,1,0:T(8,128)(2,1)S(1)}, bf16[2,48,1792]{2,1,0:T(8,128)(2,1)}, u32[]{:S(2)}) copy-start(bf16[2,48,1792]{2,1,0:T(8,128)(2,1)} %get-tuple-element.167) | copy-start | bytes 1032196
  174.0 19.8 %collective-permute-start.40 = (bf16[4,2,96,1280]{3,2,1,0:T(8,128)(2,1)S(1)}, bf16[4,2,96,1280]{3,2,1,0:T(8,128)(2,1)S(1)}, u32[]{:S(2)}, u32[]{:S(2)}) collective-permute-start(bf16[4,2,96,1280]{3,2,1,0:T(8,128)(2,1)S(1)} %shard_map.72), channel_id=1, source_target_pairs={{0,2},{2,0},{4,6},{6,4},{8,10},{10,8},{12,14},{14,12},{1,3},{3,1},... | collective-permute-start | bytes 5898248 | tf_op jit(solution)/shard_map/ppermute | solution.py:180
  178.1 15.7 %collective-permute-start.41 = (bf16[4,2,96,1280]{3,2,1,0:T(8,128)(2,1)S(1)}, bf16[4,2,96,1280]{3,2,1,0:T(8,128)(2,1)S(1)}, u32[]{:S(2)}, u32[]{:S(2)}) collective-permute-start(bf16[4,2,96,1280]{3,2,1,0:T(8,128)(2,1)S(1)} %shard_map.73), channel_id=1, source_target_pairs={{0,2},{2,0},{4,6},{6,4},{8,10},{10,8},{12,14},{14,12},{1,3},{3,1},... | collective-permute-start | bytes 5898248 | tf_op jit(solution)/shard_map/ppermute | solution.py:180
  179.6 11.6 %collective-permute-start.37 = (bf16[2,192,512]{2,1,0:T(8,128)(2,1)}, bf16[2,192,512]{2,1,0:T(8,128)(2,1)S(1)}, u32[]{:S(2)}, u32[]{:S(2)}) collective-permute-start(bf16[2,192,512]{2,1,0:T(8,128)(2,1)} %collective-permute-done.34.centre_1), channel_id=1, source_target_pairs={{4,0},{6,2},{8,12},{10,14},{5,1},{7,3},{9,13},{11,15},{20,16},{22,... | collective-permute-start | bytes 1179656 | tf_op jit(solution)/shard_map/ppermute | solution.py:180
  180.9 10.3 %collective-permute-start.38 = (bf16[2,192,512]{2,1,0:T(8,128)(2,1)}, bf16[2,192,512]{2,1,0:T(8,128)(2,1)S(1)}, u32[]{:S(2)}, u32[]{:S(2)}) collective-permute-start(bf16[2,192,512]{2,1,0:T(8,128)(2,1)} %collective-permute-done.33.side_1), channel_id=1, source_target_pairs={{4,8},{6,10},{8,4},{10,6},{5,9},{7,11},{9,5},{11,7},{20,24},{22,26... | collective-permute-start | bytes 1179656 | tf_op jit(solution)/shard_map/ppermute | solution.py:180
  182.9 9.9 %collective-permute-start.42 = (bf16[48,3584]{1,0:T(8,128)(2,1)S(1)}, bf16[48,3584]{1,0:T(8,128)(2,1)S(1)}, u32[]{:S(2)}, u32[]{:S(2)}) collective-permute-start(bf16[48,3584]{1,0:T(8,128)(2,1)S(1)} %get-tuple-element.198), channel_id=1, source_target_pairs={{0,1},{1,0},{2,3},{3,2},{4,5},{5,4},{6,7},{7,6},{8,9},{9,8},{10,11... | collective-permute-start | bytes 1032200 | tf_op jit(solution)/shard_map/ppermute | solution.py:324
  191.2 12.2 %collective-permute-start.39 = (bf16[2,192,512]{2,1,0:T(8,128)(2,1)S(1)}, bf16[2,192,512]{2,1,0:T(8,128)(2,1)S(1)}, u32[]{:S(2)}, u32[]{:S(2)}) collective-permute-start(bf16[2,192,512]{2,1,0:T(8,128)(2,1)S(1)} %collective-permute-done.38.share_2), channel_id=1, source_target_pairs={{4,0},{6,2},{8,12},{10,14},{5,1},{7,3},{9,13},{11,15},{20,16},{22,... | collective-permute-start | bytes 1179656 | tf_op jit(solution)/shard_map/ppermute | solution.py:180
  204.9 7.0 %collective-permute-start.43 = (bf16[4,2,192,512]{3,2,1,0:T(8,128)(2,1)S(1)}, bf16[4,2,192,512]{3,2,1,0:T(8,128)(2,1)S(1)}, u32[]{:S(2)}, u32[]{:S(2)}) collective-permute-start(bf16[4,2,192,512]{3,2,1,0:T(8,128)(2,1)S(1)} %shard_map.76), channel_id=1, source_target_pairs={{0,2},{2,0},{4,6},{6,4},{8,10},{10,8},{12,14},{14,12},{1,3},{3,1},... | collective-permute-start | bytes 4718600 | tf_op jit(solution)/shard_map/ppermute | solution.py:180
  (3 other events, 4.2 us)

commit v21 on v20

--- a/solution.py
+++ b/solution.py
@@ -305,9 +305,6 @@
         if gathering:
             side_1, centre_1 = tie((side_1, centre_1), before)
             out_2, share_2 = send(centre_1, outward), send(side_1, centre)
-        if k == 0:
-            products[2] = all_features(tokens, 2, (side_1, centre_1, far, near))
-            terms = tie(terms, products[2])
         if k < 0:
             products[1] = (own((far, near), LONG), send(theirs, pairs))
             cotangent = tie(grad_hidden[0], far, near)
@@ -331,6 +328,8 @@
             swapped = jnp.where(at_end, take(terms, 1), add(take(terms, 0), centre_2))
             swapped = swapped.astype(WIRE)
             centre_3, side_3 = send(near, centre), send(swapped, side)
+            if k == 0:
+                products[2] = all_features(tokens, 2, (near, swapped))
             if k + 2 <= last:
                 payload = take(tie(products[k + 2], near, swapped), 3).astype(WIRE)
                 in_1 = send(payload, inward)

time: 216 us -> 223 us (1.032)
  waiting for transfers between devices: 31.2 us -> 38.4 us
  local copies, waits for them, and re-layouts: 11.1 us -> 14.1 us
  starting transfers between devices: 92.1 us -> 89.5 us
    ppermute x39, waiting for transfers between devices: 15.9 us -> 22.9 us  [send(): return lax.ppermute(value, 'col', route)]
    ppermute x39, starting transfers between devices: 87.1 us -> 84.6 us  [send(): return lax.ppermute(value, 'col', route)]
    unnamed x46 -> x58, local copies, waits for them, and re-layouts: 3.39 us -> 4.85 us
  transfers between devices with their start and end apart: 44 -> 44, of which waited for: 13 -> 11; matrix products, arithmetic and copies ran while one was open for 16% -> 15% of each run, Pallas kernels for 18% -> 18%
where the time goes in v21:
time: 223 us; the launch traced here: 222 us
  starting transfers between devices  89.5 us (40%)
  Pallas kernels  48.1 us (22%)
  waiting for transfers between devices  38.4 us (17%)
  other arithmetic  30 us (13%)
  local copies, waits for them, and re-layouts  14.1 us (6%)
    ppermute x39, starting transfers between devices, send(): return lax.ppermute(value, 'col', route)  84.6 us
    pallas_call x5, Pallas kernels, forward(): pl.pallas_call(functools.partial(forward_kernel, scale, start, cores), ou...  23.3 us
    ppermute x39, waiting for transfers between devices, send(): return lax.ppermute(value, 'col', route)  22.9 us
    pallas_call x4, Pallas kernels, gradient(): pl.pallas_call(functools.partial(gradient_kernel, len(acts)), out_shape=(...  20.9 us
    ppermute x1, waiting for transfers between devices, local(): over_depth = lax.ppermute(mine, 'depth', swap)  7.84 us
    convert_element_type x3, other arithmetic, local(): swapped = swapped.astype(WIRE)  6.87 us
    ppermute x1, waiting for transfers between devices, local(): lax.ppermute(columns_of(cotangent, (1 - part) * half, half), 'depth', swap)  5.16 us
    unnamed x58, local copies, waits for them, and re-layouts  4.85 us
  transfers between devices with their start and end apart: 44, of which 11 were waited for; matrix products, arithmetic and copies ran while one was open for 15% of the time, Pallas kernels for 18%

profile of v21, /device:TPU:1, one launch (start us, length us, event | category | flops | bytes accessed | tf_op | source)
XLA Modules:
  0.0 221.6 jit_solution(15013852995834558856)
XLA Ops:
  0.6 2.1 collective-permute-start.1
  2.8 1.2 collective-permute-start
  4.0 7.8 %collective-permute-done.1 = bf16[384,512]{1,0:T(8,128)(2,1)S(1)} collective-permute-done((bf16[384,512]{1,0:T(8,128)(2,1)}, bf16[384,512]{1,0:T(8,128)(2,1)S(1)}, u32[]{:S(2)}, u32[]{:S(2)}) %collective-permute-start.1) | collective-permute-done | bytes 393248 | tf_op jit(solution)/shard_map/ppermute | solution.py:214
  13.4 1.3 maximum_select_fusion
  14.9 4.2 %shard_map.67 = f32[4,2,96,1280]{3,2,1,0:T(8,128)S(1)} custom-call(s32[1]{0:T(128)} %bitcast.6.place_ref, bf16[384,1024]{1,0:T(8,128)(2,1)S(1)} %bitcast.154, bf16[1024,7168]{1,0:T(8,128)(2,1)} %refs_2_.9, bf16[1024,7168]{1,0:T(8,128)(2,1)} %refs_3_.1), custom_call_target="tpu_custom_call" | custom-call | tf_op jit(solution)/shard_map/pallas_call | solution.py:57
  19.1 1.5 convert_element_type.194
  20.6 1.9 collective-permute-start.2
  22.6 4.2 %shard_map.68 = f32[4,2,96,1280]{3,2,1,0:T(8,128)S(1)} custom-call(s32[1]{0:T(128)} %bitcast.1.place_ref, bf16[384,1024]{1,0:T(8,128)(2,1)S(1)} %bitcast.155, bf16[1024,7168]{1,0:T(8,128)(2,1)} %refs_2_.9, bf16[1024,7168]{1,0:T(8,128)(2,1)} %refs_3_.1), custom_call_target="tpu_custom_call" | custom-call | flops 6000000000 | tf_op jit(solution)/shard_map/pallas_call | solution.py:57
  27.6 4.1 %collective-permute-start.4 = (f16[2,96,1280]{2,1,0:T(8,128)(2,1)}, f16[2,96,1280]{2,1,0:T(8,128)(2,1)}, u32[]{:S(2)}, u32[]{:S(2)}) collective-permute-start(f16[2,96,1280]{2,1,0:T(8,128)(2,1)} %fusion.33), channel_id=1, source_target_pairs={{0,4},{2,6},{12,8},{14,10},{1,5},{3,7},{13,9},{15,11},{16,20},{18,... | collective-permute-start | bytes 1474568 | tf_op jit(solution)/shard_map/ppermute | solution.py:180
  31.8 1.7 collective-permute-done.3
  33.9 4.2 %shard_map.69 = f32[4,2,96,1280]{3,2,1,0:T(8,128)S(1)} custom-call(s32[1]{0:T(128)} %bitcast.6.place_ref, bf16[384,1024]{1,0:T(8,128)(2,1)S(1)} %bitcast.158, bf16[1024,7168]{1,0:T(8,128)(2,1)} %refs_2_.9, bf16[1024,7168]{1,0:T(8,128)(2,1)} %refs_3_.1), custom_call_target="tpu_custom_call" | custom-call | tf_op jit(solution)/shard_map/pallas_call | solution.py:57
  40.0 4.0 %collective-permute-start.7 = (f16[2,96,1280]{2,1,0:T(8,128)(2,1)}, f16[2,96,1280]{2,1,0:T(8,128)(2,1)}, u32[]{:S(2)}, u32[]{:S(2)}) collective-permute-start(f16[2,96,1280]{2,1,0:T(8,128)(2,1)} %fusion.30), channel_id=1, source_target_pairs={{0,4},{2,6},{12,8},{14,10},{1,5},{3,7},{13,9},{15,11},{16,20},{18,... | collective-permute-start | bytes 1474568 | tf_op jit(solution)/shard_map/ppermute | solution.py:180
  44.0 2.0 fusion.13
  46.0 1.4 collective-permute-start.8
  48.5 4.2 %shard_map.70 = f32[4,2,96,1280]{3,2,1,0:T(8,128)S(1)} custom-call(s32[1]{0:T(128)} %bitcast.1.place_ref, bf16[384,1024]{1,0:T(8,128)(2,1)S(1)} %bitcast.159, bf16[1024,7168]{1,0:T(8,128)(2,1)} %refs_2_.9, bf16[1024,7168]{1,0:T(8,128)(2,1)} %refs_3_.1), custom_call_target="tpu_custom_call" | custom-call | flops 6000000000 | tf_op jit(solution)/shard_map/pallas_call | solution.py:57
  52.6 5.2 %collective-permute-done.5 = bf16[48,3584]{1,0:T(8,128)(2,1)S(1)} collective-permute-done((bf16[48,3584]{1,0:T(8,128)(2,1)}, bf16[48,3584]{1,0:T(8,128)(2,1)S(1)}, u32[]{:S(2)}, u32[]{:S(2)}) %collective-permute-start.5) | collective-permute-done | bytes 344096 | tf_op jit(solution)/shard_map/ppermute | solution.py:313
  57.8 2.3 %fusion.8 = (f16[2,96,1280]{2,1,0:T(8,128)(2,1)S(1)}, f16[2,96,1280]{2,1,0:T(8,128)(2,1)S(1)}) fusion(f16[2,96,1280]{2,1,0:T(8,128)(2,1)} %collective-permute-done.8, f32[4,2,96,1280]{3,2,1,0:T(8,128)S(1)} %shard_map.68, pred[]{:T(512)S(6)} %or.3, f16[4,2,96,1280]{3,2,1,0:T(8,128)(2,1)S(1)} %collective-permute-done.2, ...), kind=kLoop, calls=%fused_computation.22 | loop fusion | flops 3194880 | bytes 6389761 | tf_op jit(solution)/shard_map/convert_element_type | solution.py:329
  62.1 2.4 %collective-permute-start.9 = (bf16[2,48,1792]{2,1,0:T(8,128)(2,1)S(1)}, bf16[2,48,1792]{2,1,0:T(8,128)(2,1)S(1)}, u32[]{:S(2)}, u32[]{:S(2)}) collective-permute-start(bf16[2,48,1792]{2,1,0:T(8,128)(2,1)S(1)} %get-tuple-element.200), channel_id=1, source_target_pairs={{0,2},{2,0},{4,6},{6,4},{8,10},{10,8},{12,14},{14,12},{1,3},{3,1},... | collective-permute-start | bytes 1032200 | tf_op jit(solution)/shard_map/ppermute | solution.py:180
  64.6 4.5 %collective-permute-start.16 = (f16[2,96,1280]{2,1,0:T(8,128)(2,1)S(1)}, f16[2,96,1280]{2,1,0:T(8,128)(2,1)S(1)}, u32[]{:S(2)}, u32[]{:S(2)}) collective-permute-start(f16[2,96,1280]{2,1,0:T(8,128)(2,1)S(1)} %fusion.31), channel_id=1, source_target_pairs={{0,4},{2,6},{12,8},{14,10},{1,5},{3,7},{13,9},{15,11},{16,20},{18,... | collective-permute-start | bytes 1474568 | tf_op jit(solution)/shard_map/ppermute | solution.py:180
  69.0 1.7 dynamic-slice_bitcast_fusion
  75.4 4.1 %collective-permute-start.14 = (bf16[2,96,1280]{2,1,0:T(8,128)(2,1)S(1)}, bf16[2,96,1280]{2,1,0:T(8,128)(2,1)S(1)}, u32[]{:S(2)}, u32[]{:S(2)}) collective-permute-start(bf16[2,96,1280]{2,1,0:T(8,128)(2,1)S(1)} %pad_maximum_fusion.2.act), channel_id=1, source_target_pairs={{0,4},{2,6},{12,8},{14,10},{4,0},{6,2},{8,12},{10,14},{1,5},{3,7},... | collective-permute-start | bytes 1474568 | tf_op jit(solution)/shard_map/ppermute | solution.py:180
  82.1 6.0 %collective-permute-start.17 = (f16[2,96,1280]{2,1,0:T(8,128)(2,1)S(1)}, f16[2,96,1280]{2,1,0:T(8,128)(2,1)S(1)}, u32[]{:S(2)}, u32[]{:S(2)}) collective-permute-start(f16[2,96,1280]{2,1,0:T(8,128)(2,1)S(1)} %fusion.32), channel_id=1, source_target_pairs={{0,4},{2,6},{12,8},{14,10},{1,5},{3,7},{13,9},{15,11},{16,20},{18,... | collective-permute-start | bytes 1474568 | tf_op jit(solution)/shard_map/ppermute | solution.py:180
  88.1 2.8 %collective-permute-done.14.side_1 = bf16[2,96,1280]{2,1,0:T(8,128)(2,1)S(1)} collective-permute-done((bf16[2,96,1280]{2,1,0:T(8,128)(2,1)S(1)}, bf16[2,96,1280]{2,1,0:T(8,128)(2,1)S(1)}, u32[]{:S(2)}, u32[]{:S(2)}) %collective-permute-start.14) | collective-permute-done | bytes 491552 | tf_op jit(solution)/shard_map/ppermute | solution.py:180
  91.6 1.3 collective-permute-start.19
  92.9 8.5 %collective-permute-done.17 = f16[2,96,1280]{2,1,0:T(8,128)(2,1)S(1)} collective-permute-done((f16[2,96,1280]{2,1,0:T(8,128)(2,1)S(1)}, f16[2,96,1280]{2,1,0:T(8,128)(2,1)S(1)}, u32[]{:S(2)}, u32[]{:S(2)}) %collective-permute-start.17) | collective-permute-done | bytes 491552 | tf_op jit(solution)/shard_map/ppermute | solution.py:180
  101.4 1.5 fusion.5
  102.9 2.2 collective-permute-start.22
  105.1 1.5 collective-permute-start.23
  106.6 1.6 collective-permute-start.21
  108.1 1.5 copy.25
  109.9 1.4 copy-done.3
  111.3 6.7 %shard_map.71 = f32[4,2,192,512]{3,2,1,0:T(8,128)} custom-call(s32[1]{0:T(128)} %bitcast.1.place_ref, bf16[768,1024]{1,0:T(8,128)(2,1)S(1)} %bitcast.163, bf16[768,1024]{1,0:T(8,128)(2,1)S(1)} %bitcast.164, bf16[1024,7168]{1,0:T(8,128)(2,1)} %refs_2_.9, bf16[1024,7168]{1,0:T(8,128)(2,1)} %refs_3_.1, bf16[2,1024,512]{2,1,0:T(8,128)(2,1)S(1)} %copy-done.3, ...), custom_call_target="tpu_custom_call" | custom-call | tf_op jit(solution)/shard_map/pallas_call | solution.py:57
  118.0 1.2 fusion.39
  119.2 4.2 %collective-permute-start.26 = (f16[2,192,512]{2,1,0:T(8,128)(2,1)S(1)}, f16[2,192,512]{2,1,0:T(8,128)(2,1)S(1)}, u32[]{:S(2)}, u32[]{:S(2)}) collective-permute-start(f16[2,192,512]{2,1,0:T(8,128)(2,1)S(1)} %fusion.39), channel_id=1, source_target_pairs={{0,4},{2,6},{12,8},{14,10},{1,5},{3,7},{13,9},{15,11},{16,20},{18,... | collective-permute-start | bytes 1179656 | tf_op jit(solution)/shard_map/ppermute | solution.py:180
  123.4 1.5 fusion.2
  126.8 1.5 collective-permute-start.25
  129.8 1.5 copy-done.14
  133.0 1.4 collective-permute-start.28
  134.4 4.8 %collective-permute-start.27 = (f16[2,192,512]{2,1,0:T(8,128)(2,1)}, f16[2,192,512]{2,1,0:T(8,128)(2,1)}, u32[]{:S(2)}, u32[]{:S(2)}) collective-permute-start(f16[2,192,512]{2,1,0:T(8,128)(2,1)} %fusion.40), channel_id=1, source_target_pairs={{0,4},{2,6},{12,8},{14,10},{1,5},{3,7},{13,9},{15,11},{16,20},{18,... | collective-permute-start | bytes 1179656 | tf_op jit(solution)/shard_map/ppermute | solution.py:180
  139.3 1.4 collective-permute-start.30
  140.7 1.3 collective-permute-start.29
  142.0 5.7 %collective-permute-done.27 = f16[2,192,512]{2,1,0:T(8,128)(2,1)} collective-permute-done((f16[2,192,512]{2,1,0:T(8,128)(2,1)}, f16[2,192,512]{2,1,0:T(8,128)(2,1)}, u32[]{:S(2)}, u32[]{:S(2)}) %collective-permute-start.27) | collective-permute-done | bytes 393248 | tf_op jit(solution)/shard_map/ppermute | solution.py:180
  147.7 3.1 %fusion.18 = (f16[2,192,512]{2,1,0:T(8,128)(2,1)}, f16[2,192,512]{2,1,0:T(8,128)(2,1)}) fusion(f16[2,192,512]{2,1,0:T(8,128)(2,1)} %collective-permute-done.28, f32[4,2,192,512]{3,2,1,0:T(8,128)} %shard_map.71, pred[]{:T(512)S(6)} %or.3, f16[2,192,512]{2,1,0:T(8,128)(2,1)} %collective-permute-done.27), kind=kLoop, calls=%fused_computation.46 | loop fusion | flops 1376256 | bytes 3932161 | tf_op jit(solution)/shard_map/convert_element_type | solution.py:329
  150.8 2.2 collective-permute-start.31
  153.0 1.4 collective-permute-start.32
  158.4 1.6 maximum_bitcast_fusion.features_ref
  160.1 1.4 collective-permute-start.36
  161.5 1.4 fusion.15
  164.0 1.4 collective-permute-start.34
  165.4 5.6 %collective-permute-start.33 = (bf16[2,192,512]{2,1,0:T(8,128)(2,1)}, bf16[2,192,512]{2,1,0:T(8,128)(2,1)}, u32[]{:S(2)}, u32[]{:S(2)}) collective-permute-start(bf16[2,192,512]{2,1,0:T(8,128)(2,1)} %pad_maximum_fusion.4.act), channel_id=1, source_target_pairs={{0,4},{2,6},{12,8},{14,10},{4,0},{6,2},{8,12},{10,14},{1,5},{3,7},... | collective-permute-start | bytes 1179656 | tf_op jit(solution)/shard_map/ppermute | solution.py:180
  172.1 8.1 %collective-permute-start.35 = (bf16[2,48,1792]{2,1,0:T(8,128)(2,1)}, bf16[2,48,1792]{2,1,0:T(8,128)(2,1)}, u32[]{:S(2)}, u32[]{:S(2)}) collective-permute-start(bf16[2,48,1792]{2,1,0:T(8,128)(2,1)} %get-tuple-element.196), channel_id=1, source_target_pairs={{0,2},{2,0},{4,6},{6,4},{8,10},{10,8},{12,14},{14,12},{1,3},{3,1},... | collective-permute-start | bytes 1032200 | tf_op jit(solution)/shard_map/ppermute | solution.py:180
  180.3 2.0 collective-permute-done.35
  182.3 2.1 shard_map.73
  185.5 1.3 collective-permute-start.37
  187.5 1.2 maximum_select_fusion.3
  188.8 1.3 collective-permute-start.42
  190.1 7.0 %shard_map.74 = (f32[1024,3584]{1,0:T(8,128)}, f32[1024,3584]{1,0:T(8,128)}) custom-call(s32[1]{0:T(128)} %bitcast.59.place_ref, bf16[1024,768]{1,0:T(8,128)(2,1)S(1)} %maximum_bitcast_fusion.features_ref, bf16[4,1,2,96,1280]{4,3,2,1,0:T(8,128)(2,1)S(1)} %bitcast.165, bf16[4,1,2,96,1280]{4,3,2,1,0:T(8,128)(2,1)S(1)} %bitcast.167), custom_call_target="tpu_custom_call" | custom-call | flops 4026531840 | bytes 15990784 | tf_op jit(solution)/shard_map/pallas_call | solution.py:101
  197.2 1.5 collective-permute-start.39
  199.7 7.0 %shard_map.75 = (f32[1024,3584]{1,0:T(8,128)}, f32[1024,3584]{1,0:T(8,128)}) custom-call(s32[1]{0:T(128)} %bitcast.62.place_ref, bf16[1024,768]{1,0:T(8,128)(2,1)S(1)} %maximum_bitcast_fusion.features_ref, bf16[4,1,2,96,1280]{4,3,2,1,0:T(8,128)(2,1)S(1)} %bitcast.166, ...), custom_call_target="tpu_custom_call", output_to_operand_aliasing={{0}: (4, {}), {1}: (5, {})} | custom-call | flops 4026531840 | bytes 15990784 | tf_op jit(solution)/shard_map/pallas_call | solution.py:101
  206.7 2.9 %collective-permute-done.39.out_3 = bf16[2,192,512]{2,1,0:T(8,128)(2,1)S(1)} collective-permute-done((bf16[2,192,512]{2,1,0:T(8,128)(2,1)S(1)}, bf16[2,192,512]{2,1,0:T(8,128)(2,1)S(1)}, u32[]{:S(2)}, u32[]{:S(2)}) %collective-permute-start.39) | collective-permute-done | bytes 393248 | tf_op jit(solution)/shard_map/ppermute | solution.py:180
  209.6 1.5 shard_map.76
  211.1 3.6 %collective-permute-start.43 = (bf16[4,2,192,512]{3,2,1,0:T(8,128)(2,1)S(1)}, bf16[4,2,192,512]{3,2,1,0:T(8,128)(2,1)S(1)}, u32[]{:S(2)}, u32[]{:S(2)}) collective-permute-start(bf16[4,2,192,512]{3,2,1,0:T(8,128)(2,1)S(1)} %shard_map.76), channel_id=1, source_target_pairs={{0,2},{2,0},{4,6},{6,4},{8,10},{10,8},{12,14},{14,12},{1,3},{3,1},... | collective-permute-start | bytes 4718600 | tf_op jit(solution)/shard_map/ppermute | solution.py:180
  214.7 3.4 %shard_map.77 = (f32[1024,3584]{1,0:T(8,128)}, f32[1024,3584]{1,0:T(8,128)}) custom-call(s32[1]{0:T(128)} %bitcast.59.place_ref, bf16[1024,768]{1,0:T(8,128)(2,1)S(1)} %maximum_bitcast_fusion.features_ref, bf16[4,1,2,192,512]{4,3,2,1,0:T(8,128)(2,1)S(1)} %bitcast.162, ...), custom_call_target="tpu_custom_call", output_to_operand_aliasing={{0}: (3, {}), {1}: (4, {})} | custom-call | flops 1610612736 | bytes 7340032 | tf_op jit(solution)/shard_map/pallas_call | solution.py:101
  218.2 3.4 %shard_map.78 = (f32[1024,3584]{1,0:T(8,128)}, f32[1024,3584]{1,0:T(8,128)}) custom-call(s32[1]{0:T(128)} %bitcast.62.place_ref, bf16[1024,768]{1,0:T(8,128)(2,1)S(1)} %maximum_bitcast_fusion.features_ref, bf16[4,1,2,192,512]{4,3,2,1,0:T(8,128)(2,1)S(1)} %bitcast.169, ...), custom_call_target="tpu_custom_call", output_to_operand_aliasing={{0}: (3, {}), {1}: (4, {})} | custom-call | flops 1610612736 | bytes 7340032 | tf_op jit(solution)/shard_map/pallas_call | solution.py:101
  (142 shorter events, 30.2 us)
Async XLA Ops:
  0.6 11.2 %collective-permute-start.1 = (bf16[384,512]{1,0:T(8,128)(2,1)}, bf16[384,512]{1,0:T(8,128)(2,1)S(1)}, u32[]{:S(2)}, u32[]{:S(2)}) collective-permute-start(bf16[384,512]{1,0:T(8,128)(2,1)} %bitcast.177), channel_id=1, source_target_pairs={{0,1},{1,0},{2,3},{3,2},{4,5},{5,4},{6,7},{7,6},{8,9},{9,8},{10,11... | collective-permute-start | bytes 1179656 | tf_op jit(solution)/shard_map/ppermute | solution.py:214
  2.8 9.9 %collective-permute-start = (bf16[384,512]{1,0:T(8,128)(2,1)}, bf16[384,512]{1,0:T(8,128)(2,1)S(1)}, u32[]{:S(2)}, u32[]{:S(2)}) collective-permute-start(bf16[384,512]{1,0:T(8,128)(2,1)} %bitcast.178), channel_id=1, source_target_pairs={{0,16},{16,0},{1,17},{17,1},{2,18},{18,2},{3,19},{19,3},{4,20},{20... | collective-permute-start | bytes 1179656 | tf_op jit(solution)/shard_map/ppermute | solution.py:213
  20.6 6.1 %collective-permute-start.2 = (f16[4,2,96,1280]{3,2,1,0:T(8,128)(2,1)}, f16[4,2,96,1280]{3,2,1,0:T(8,128)(2,1)S(1)}, u32[]{:S(2)}, u32[]{:S(2)}) collective-permute-start(f16[4,2,96,1280]{3,2,1,0:T(8,128)(2,1)} %convert_element_type.194), channel_id=1, source_target_pairs={{0,2},{2,0},{4,6},{6,4},{8,10},{10,8},{12,14},{14,12},{1,3},{3,1},... | collective-permute-start | bytes 5898248 | tf_op jit(solution)/shard_map/ppermute | solution.py:180
  22.5 11.0 %collective-permute-start.3 = (bf16[384,512]{1,0:T(8,128)(2,1)}, bf16[384,512]{1,0:T(8,128)(2,1)S(1)}, u32[]{:S(2)}, u32[]{:S(2)}) collective-permute-start(bf16[384,512]{1,0:T(8,128)(2,1)} %copy-done.28), channel_id=1, source_target_pairs={{0,1},{1,0},{2,3},{3,2},{4,5},{5,4},{6,7},{7,6},{8,9},{9,8},{10,11... | collective-permute-start | bytes 1179656 | tf_op jit(solution)/shard_map/ppermute | solution.py:215
  27.6 16.4 %collective-permute-start.4 = (f16[2,96,1280]{2,1,0:T(8,128)(2,1)}, f16[2,96,1280]{2,1,0:T(8,128)(2,1)}, u32[]{:S(2)}, u32[]{:S(2)}) collective-permute-start(f16[2,96,1280]{2,1,0:T(8,128)(2,1)} %fusion.33), channel_id=1, source_target_pairs={{0,4},{2,6},{12,8},{14,10},{1,5},{3,7},{13,9},{15,11},{16,20},{18,... | collective-permute-start | bytes 1474568 | tf_op jit(solution)/shard_map/ppermute | solution.py:180
  38.3 9.2 %copy-start.27 = (bf16[1,48,7168]{2,1,0:T(8,128)(2,1)S(1)}, bf16[1,48,7168]{2,1,0:T(8,128)(2,1)}, u32[]{:S(2)}) copy-start(bf16[1,48,7168]{2,1,0:T(8,128)(2,1)} %param.7) | copy-start | bytes 2064388
  38.3 19.5 %collective-permute-start.6 = (f16[4,2,96,1280]{3,2,1,0:T(8,128)(2,1)S(1)}, f16[4,2,96,1280]{3,2,1,0:T(8,128)(2,1)S(1)}, u32[]{:S(2)}, u32[]{:S(2)}) collective-permute-start(f16[4,2,96,1280]{3,2,1,0:T(8,128)(2,1)S(1)} %convert_element_type.198), channel_id=1, source_target_pairs={{0,2},{2,0},{4,6},{6,4},{8,10},{10,8},{12,14},{14,12},{1,3},{3,1},... | collective-permute-start | bytes 5898248 | tf_op jit(solution)/shard_map/ppermute | solution.py:180
  40.0 17.8 %collective-permute-start.7 = (f16[2,96,1280]{2,1,0:T(8,128)(2,1)}, f16[2,96,1280]{2,1,0:T(8,128)(2,1)}, u32[]{:S(2)}, u32[]{:S(2)}) collective-permute-start(f16[2,96,1280]{2,1,0:T(8,128)(2,1)} %fusion.30), channel_id=1, source_target_pairs={{0,4},{2,6},{12,8},{14,10},{1,5},{3,7},{13,9},{15,11},{16,20},{18,... | collective-permute-start | bytes 1474568 | tf_op jit(solution)/shard_map/ppermute | solution.py:180
  46.0 11.8 %collective-permute-start.8 = (f16[2,96,1280]{2,1,0:T(8,128)(2,1)}, f16[2,96,1280]{2,1,0:T(8,128)(2,1)}, u32[]{:S(2)}, u32[]{:S(2)}) collective-permute-start(f16[2,96,1280]{2,1,0:T(8,128)(2,1)} %fusion.13), channel_id=1, source_target_pairs={{4,8},{6,10},{8,4},{10,6},{5,9},{7,11},{9,5},{11,7},{20,24},{22,26... | collective-permute-start | bytes 1474568 | tf_op jit(solution)/shard_map/ppermute | solution.py:180
  48.2 9.6 %collective-permute-start.5 = (bf16[48,3584]{1,0:T(8,128)(2,1)}, bf16[48,3584]{1,0:T(8,128)(2,1)S(1)}, u32[]{:S(2)}, u32[]{:S(2)}) collective-permute-start(bf16[48,3584]{1,0:T(8,128)(2,1)} %get-tuple-element.201), channel_id=1, source_target_pairs={{0,1},{1,0},{2,3},{3,2},{4,5},{5,4},{6,7},{7,6},{8,9},{9,8},{10,11... | collective-permute-start | bytes 1032200 | tf_op jit(solution)/shard_map/ppermute | solution.py:313
  52.6 48.8 %copy-start = (f32[4,2,96,1280]{3,2,1,0:T(8,128)}, f32[4,2,96,1280]{3,2,1,0:T(8,128)S(1)}, u32[]{:S(2)}) copy-start(f32[4,2,96,1280]{3,2,1,0:T(8,128)S(1)} %shard_map.70) | copy-start | bytes 11796484
  57.8 43.6 %copy-start.16 = (f16[4,2,96,1280]{3,2,1,0:T(8,128)(2,1)}, f16[4,2,96,1280]{3,2,1,0:T(8,128)(2,1)S(1)}, u32[]{:S(2)}) copy-start(f16[4,2,96,1280]{3,2,1,0:T(8,128)(2,1)S(1)} %collective-permute-done.6) | copy-start | bytes 5898244
  60.2 12.6 %collective-permute-start.12 = (f16[2,96,1280]{2,1,0:T(8,128)(2,1)S(1)}, f16[2,96,1280]{2,1,0:T(8,128)(2,1)S(1)}, u32[]{:S(2)}, u32[]{:S(2)}) collective-permute-start(f16[2,96,1280]{2,1,0:T(8,128)(2,1)S(1)} %get-tuple-element.179), channel_id=1, source_target_pairs={{0,4},{2,6},{12,8},{14,10},{4,0},{6,2},{8,12},{10,14},{1,5},{3,7},... | collective-permute-start | bytes 1474568 | tf_op jit(solution)/shard_map/ppermute | solution.py:180
  61.3 11.4 %collective-permute-start.13 = (f16[2,96,1280]{2,1,0:T(8,128)(2,1)S(1)}, f16[2,96,1280]{2,1,0:T(8,128)(2,1)S(1)}, u32[]{:S(2)}, u32[]{:S(2)}) collective-permute-start(f16[2,96,1280]{2,1,0:T(8,128)(2,1)S(1)} %get-tuple-element.180), channel_id=1, source_target_pairs={{4,8},{6,10},{8,4},{10,6},{5,9},{7,11},{9,5},{11,7},{20,24},{22,26... | collective-permute-start | bytes 1474568 | tf_op jit(solution)/shard_map/ppermute | solution.py:180
  62.1 9.4 %collective-permute-start.9 = (bf16[2,48,1792]{2,1,0:T(8,128)(2,1)S(1)}, bf16[2,48,1792]{2,1,0:T(8,128)(2,1)S(1)}, u32[]{:S(2)}, u32[]{:S(2)}) collective-permute-start(bf16[2,48,1792]{2,1,0:T(8,128)(2,1)S(1)} %get-tuple-element.200), channel_id=1, source_target_pairs={{0,2},{2,0},{4,6},{6,4},{8,10},{10,8},{12,14},{14,12},{1,3},{3,1},... | collective-permute-start | bytes 1032200 | tf_op jit(solution)/shard_map/ppermute | solution.py:180
  64.6 15.8 %collective-permute-start.16 = (f16[2,96,1280]{2,1,0:T(8,128)(2,1)S(1)}, f16[2,96,1280]{2,1,0:T(8,128)(2,1)S(1)}, u32[]{:S(2)}, u32[]{:S(2)}) collective-permute-start(f16[2,96,1280]{2,1,0:T(8,128)(2,1)S(1)} %fusion.31), channel_id=1, source_target_pairs={{0,4},{2,6},{12,8},{14,10},{1,5},{3,7},{13,9},{15,11},{16,20},{18,... | collective-permute-start | bytes 1474568 | tf_op jit(solution)/shard_map/ppermute | solution.py:180
  70.9 8.6 %collective-permute-start.11 = (bf16[2,1024,512]{2,1,0:T(8,128)(2,1)S(1)}, bf16[2,1024,512]{2,1,0:T(8,128)(2,1)S(1)}, u32[]{:S(2)}, u32[]{:S(2)}) collective-permute-start(bf16[2,1024,512]{2,1,0:T(8,128)(2,1)S(1)} %pad_maximum_fusion), channel_id=1, source_target_pairs={{0,2},{2,0},{4,6},{6,4},{8,10},{10,8},{12,14},{14,12},{1,3},{3,1},... | collective-permute-start | bytes 6291464 | tf_op jit(solution)/shard_map/ppermute | solution.py:180
  71.5 8.1 %collective-permute-start.10 = (bf16[4,2,96,1024]{3,2,0,1:T(8,128)(2,1)S(1)}, bf16[4,2,96,1024]{3,2,0,1:T(8,128)(2,1)S(1)}, u32[]{:S(2)}, u32[]{:S(2)}) collective-permute-start(bf16[4,2,96,1024]{3,2,0,1:T(8,128)(2,1)S(1)} %pad_maximum_fusion.1), channel_id=1, source_target_pairs={{0,2},{2,0},{4,6},{6,4},{8,10},{10,8},{12,14},{14,12},{1,3},{3,1},... | collective-permute-start | bytes 4718600 | tf_op jit(solution)/shard_map/ppermute | solution.py:180
  74.5 6.2 %copy-start.4 = (bf16[2,96,1280]{2,1,0:T(8,128)(2,1)}, bf16[2,96,1280]{2,1,0:T(8,128)(2,1)S(1)}, u32[]{:S(2)}) copy-start(bf16[2,96,1280]{2,1,0:T(8,128)(2,1)S(1)} %pad_maximum_fusion.2.act) | copy-start | bytes 1474564
  74.5 13.5 %collective-permute-start.15 = (bf16[2,96,1280]{2,1,0:T(8,128)(2,1)S(1)}, bf16[2,96,1280]{2,1,0:T(8,128)(2,1)S(1)}, u32[]{:S(2)}, u32[]{:S(2)}) collective-permute-start(bf16[2,96,1280]{2,1,0:T(8,128)(2,1)S(1)} %pad_maximum_fusion.2.act), channel_id=1, source_target_pairs={{4,8},{6,10},{8,4},{10,6},{5,9},{7,11},{9,5},{11,7},{20,24},{22,26... | collective-permute-start | bytes 1474568 | tf_op jit(solution)/shard_map/ppermute | solution.py:180
  75.4 15.5 %collective-permute-start.14 = (bf16[2,96,1280]{2,1,0:T(8,128)(2,1)S(1)}, bf16[2,96,1280]{2,1,0:T(8,128)(2,1)S(1)}, u32[]{:S(2)}, u32[]{:S(2)}) collective-permute-start(bf16[2,96,1280]{2,1,0:T(8,128)(2,1)S(1)} %pad_maximum_fusion.2.act), channel_id=1, source_target_pairs={{0,4},{2,6},{12,8},{14,10},{4,0},{6,2},{8,12},{10,14},{1,5},{3,7},... | collective-permute-start | bytes 1474568 | tf_op jit(solution)/shard_map/ppermute | solution.py:180
  81.4 11.5 %collective-permute-start.18 = (f16[2,96,1280]{2,1,0:T(8,128)(2,1)S(1)}, f16[2,96,1280]{2,1,0:T(8,128)(2,1)S(1)}, u32[]{:S(2)}, u32[]{:S(2)}) collective-permute-start(f16[2,96,1280]{2,1,0:T(8,128)(2,1)S(1)} %fusion.3), channel_id=1, source_target_pairs={{4,8},{6,10},{8,4},{10,6},{5,9},{7,11},{9,5},{11,7},{20,24},{22,26... | collective-permute-start | bytes 1474568 | tf_op jit(solution)/shard_map/ppermute | solution.py:180
  82.1 19.3 %collective-permute-start.17 = (f16[2,96,1280]{2,1,0:T(8,128)(2,1)S(1)}, f16[2,96,1280]{2,1,0:T(8,128)(2,1)S(1)}, u32[]{:S(2)}, u32[]{:S(2)}) collective-permute-start(f16[2,96,1280]{2,1,0:T(8,128)(2,1)S(1)} %fusion.32), channel_id=1, source_target_pairs={{0,4},{2,6},{12,8},{14,10},{1,5},{3,7},{13,9},{15,11},{16,20},{18,... | collective-permute-start | bytes 1474568 | tf_op jit(solution)/shard_map/ppermute | solution.py:180
  88.1 14.8 %copy-start.6 = (bf16[2,96,1280]{2,1,0:T(8,128)(2,1)}, bf16[2,96,1280]{2,1,0:T(8,128)(2,1)S(1)}, u32[]{:S(2)}) copy-start(bf16[2,96,1280]{2,1,0:T(8,128)(2,1)S(1)} %collective-permute-done.15.centre_1) | copy-start | bytes 1474564
  90.9 12.0 %copy-start.8 = (bf16[2,96,1280]{2,1,0:T(8,128)(2,1)}, bf16[2,96,1280]{2,1,0:T(8,128)(2,1)S(1)}, u32[]{:S(2)}) copy-start(bf16[2,96,1280]{2,1,0:T(8,128)(2,1)S(1)} %collective-permute-done.14.side_1) | copy-start | bytes 1474564
  90.9 15.7 %collective-permute-start.20 = (bf16[2,96,1280]{2,1,0:T(8,128)(2,1)S(1)}, bf16[2,96,1280]{2,1,0:T(8,128)(2,1)S(1)}, u32[]{:S(2)}, u32[]{:S(2)}) collective-permute-start(bf16[2,96,1280]{2,1,0:T(8,128)(2,1)S(1)} %collective-permute-done.14.side_1), channel_id=1, source_target_pairs={{4,8},{6,10},{8,4},{10,6},{5,9},{7,11},{9,5},{11,7},{20,24},{22,26... | collective-permute-start | bytes 1474568 | tf_op jit(solution)/shard_map/ppermute | solution.py:180
  91.6 15.0 %collective-permute-start.19 = (bf16[2,96,1280]{2,1,0:T(8,128)(2,1)S(1)}, bf16[2,96,1280]{2,1,0:T(8,128)(2,1)S(1)}, u32[]{:S(2)}, u32[]{:S(2)}) collective-permute-start(bf16[2,96,1280]{2,1,0:T(8,128)(2,1)S(1)} %collective-permute-done.15.centre_1), channel_id=1, source_target_pairs={{4,0},{6,2},{8,12},{10,14},{5,1},{7,3},{9,13},{11,15},{20,16},{22,... | collective-permute-start | bytes 1474568 | tf_op jit(solution)/shard_map/ppermute | solution.py:180
  102.9 20.5 %collective-permute-start.22 = (f16[2,96,1280]{2,1,0:T(8,128)(2,1)}, f16[2,96,1280]{2,1,0:T(8,128)(2,1)}, u32[]{:S(2)}, u32[]{:S(2)}) collective-permute-start(f16[2,96,1280]{2,1,0:T(8,128)(2,1)} %get-tuple-element.177), channel_id=1, source_target_pairs={{0,4},{2,6},{12,8},{14,10},{4,0},{6,2},{8,12},{10,14},{1,5},{3,7},... | collective-permute-start | bytes 1474568 | tf_op jit(solution)/shard_map/ppermute | solution.py:180
  105.1 18.3 %collective-permute-start.23 = (f16[2,96,1280]{2,1,0:T(8,128)(2,1)}, f16[2,96,1280]{2,1,0:T(8,128)(2,1)}, u32[]{:S(2)}, u32[]{:S(2)}) collective-permute-start(f16[2,96,1280]{2,1,0:T(8,128)(2,1)} %get-tuple-element.178), channel_id=1, source_target_pairs={{4,8},{6,10},{8,4},{10,6},{5,9},{7,11},{9,5},{11,7},{20,24},{22,26... | collective-permute-start | bytes 1474568 | tf_op jit(solution)/shard_map/ppermute | solution.py:180
  106.6 3.3 %copy-start.10 = (bf16[2,96,1280]{2,1,0:T(8,128)(2,1)}, bf16[2,96,1280]{2,1,0:T(8,128)(2,1)S(1)}, u32[]{:S(2)}) copy-start(bf16[2,96,1280]{2,1,0:T(8,128)(2,1)S(1)} %collective-permute-done.20.share_2) | copy-start | bytes 1474564
  106.6 3.3 %copy-start.12 = (bf16[2,96,1280]{2,1,0:T(8,128)(2,1)}, bf16[2,96,1280]{2,1,0:T(8,128)(2,1)S(1)}, u32[]{:S(2)}) copy-start(bf16[2,96,1280]{2,1,0:T(8,128)(2,1)S(1)} %collective-permute-done.19.out_2) | copy-start | bytes 1474564
  106.6 22.8 %collective-permute-start.21 = (bf16[2,96,1280]{2,1,0:T(8,128)(2,1)S(1)}, bf16[2,96,1280]{2,1,0:T(8,128)(2,1)S(1)}, u32[]{:S(2)}, u32[]{:S(2)}) collective-permute-start(bf16[2,96,1280]{2,1,0:T(8,128)(2,1)S(1)} %collective-permute-done.20.share_2), channel_id=1, source_target_pairs={{4,0},{6,2},{8,12},{10,14},{5,1},{7,3},{9,13},{11,15},{20,16},{22,... | collective-permute-start | bytes 1474568 | tf_op jit(solution)/shard_map/ppermute | solution.py:180
  111.3 12.1 %copy-start.1 = (f32[4,2,96,1280]{3,2,1,0:T(8,128)S(1)}, f32[4,2,96,1280]{3,2,1,0:T(8,128)}, u32[]{:S(2)}) copy-start(f32[4,2,96,1280]{3,2,1,0:T(8,128)} %copy-done) | copy-start | bytes 11796484
  111.3 12.1 %copy-start.17 = (f16[4,2,96,1280]{3,2,1,0:T(8,128)(2,1)S(1)}, f16[4,2,96,1280]{3,2,1,0:T(8,128)(2,1)}, u32[]{:S(2)}) copy-start(f16[4,2,96,1280]{3,2,1,0:T(8,128)(2,1)} %copy-done.16) | copy-start | bytes 5898244
  119.2 5.8 %copy-start.22 = (bf16[96,1792]{1,0:T(8,128)(2,1)S(1)}, bf16[96,1792]{1,0:T(8,128)(2,1)}, u32[]{:S(2)}) copy-start(bf16[96,1792]{1,0:T(8,128)(2,1)} %get-tuple-element.198) | copy-start | bytes 1032196
  119.2 10.6 %collective-permute-start.26 = (f16[2,192,512]{2,1,0:T(8,128)(2,1)S(1)}, f16[2,192,512]{2,1,0:T(8,128)(2,1)S(1)}, u32[]{:S(2)}, u32[]{:S(2)}) collective-permute-start(f16[2,192,512]{2,1,0:T(8,128)(2,1)S(1)} %fusion.39), channel_id=1, source_target_pairs={{0,4},{2,6},{12,8},{14,10},{1,5},{3,7},{13,9},{15,11},{16,20},{18,... | collective-permute-start | bytes 1179656 | tf_op jit(solution)/shard_map/ppermute | solution.py:180
  124.9 4.5 %copy-start.5 = (bf16[2,96,1280]{2,1,0:T(8,128)(2,1)S(1)}, bf16[2,96,1280]{2,1,0:T(8,128)(2,1)}, u32[]{:S(2)}) copy-start(bf16[2,96,1280]{2,1,0:T(8,128)(2,1)} %copy-done.4) | copy-start | bytes 1474564
  124.9 4.5 %copy-start.7 = (bf16[2,96,1280]{2,1,0:T(8,128)(2,1)S(1)}, bf16[2,96,1280]{2,1,0:T(8,128)(2,1)}, u32[]{:S(2)}) copy-start(bf16[2,96,1280]{2,1,0:T(8,128)(2,1)} %copy-done.6) | copy-start | bytes 1474564
  124.9 4.5 %copy-start.9 = (bf16[2,96,1280]{2,1,0:T(8,128)(2,1)S(1)}, bf16[2,96,1280]{2,1,0:T(8,128)(2,1)}, u32[]{:S(2)}) copy-start(bf16[2,96,1280]{2,1,0:T(8,128)(2,1)} %copy-done.8) | copy-start | bytes 1474564
  124.9 4.5 %copy-start.11 = (bf16[2,96,1280]{2,1,0:T(8,128)(2,1)S(1)}, bf16[2,96,1280]{2,1,0:T(8,128)(2,1)}, u32[]{:S(2)}) copy-start(bf16[2,96,1280]{2,1,0:T(8,128)(2,1)} %copy-done.10) | copy-start | bytes 1474564
  124.9 4.5 %copy-start.13 = (bf16[2,96,1280]{2,1,0:T(8,128)(2,1)S(1)}, bf16[2,96,1280]{2,1,0:T(8,128)(2,1)}, u32[]{:S(2)}) copy-start(bf16[2,96,1280]{2,1,0:T(8,128)(2,1)} %copy-done.12) | copy-start | bytes 1474564
  126.8 12.4 %collective-permute-start.25 = (bf16[2,96,1280]{2,1,0:T(8,128)(2,1)}, bf16[2,96,1280]{2,1,0:T(8,128)(2,1)}, u32[]{:S(2)}, u32[]{:S(2)}) collective-permute-start(bf16[2,96,1280]{2,1,0:T(8,128)(2,1)} %pad_maximum_fusion.3.act), channel_id=1, source_target_pairs={{4,8},{6,10},{8,4},{10,6},{5,9},{7,11},{9,5},{11,7},{20,24},{22,26... | collective-permute-start | bytes 1474568 | tf_op jit(solution)/shard_map/ppermute | solution.py:180
  128.2 11.0 %collective-permute-start.24 = (bf16[2,96,1280]{2,1,0:T(8,128)(2,1)}, bf16[2,96,1280]{2,1,0:T(8,128)(2,1)}, u32[]{:S(2)}, u32[]{:S(2)}) collective-permute-start(bf16[2,96,1280]{2,1,0:T(8,128)(2,1)} %pad_maximum_fusion.3.act), channel_id=1, source_target_pairs={{0,4},{2,6},{12,8},{14,10},{4,0},{6,2},{8,12},{10,14},{1,5},{3,7},... | collective-permute-start | bytes 1474568 | tf_op jit(solution)/shard_map/ppermute | solution.py:180
  133.0 9.0 %collective-permute-start.28 = (f16[2,192,512]{2,1,0:T(8,128)(2,1)}, f16[2,192,512]{2,1,0:T(8,128)(2,1)}, u32[]{:S(2)}, u32[]{:S(2)}) collective-permute-start(f16[2,192,512]{2,1,0:T(8,128)(2,1)} %fusion.16), channel_id=1, source_target_pairs={{4,8},{6,10},{8,4},{10,6},{5,9},{7,11},{9,5},{11,7},{20,24},{22,26... | collective-permute-start | bytes 1179656 | tf_op jit(solution)/shard_map/ppermute | solution.py:180
  134.4 13.3 %collective-permute-start.27 = (f16[2,192,512]{2,1,0:T(8,128)(2,1)}, f16[2,192,512]{2,1,0:T(8,128)(2,1)}, u32[]{:S(2)}, u32[]{:S(2)}) collective-permute-start(f16[2,192,512]{2,1,0:T(8,128)(2,1)} %fusion.40), channel_id=1, source_target_pairs={{0,4},{2,6},{12,8},{14,10},{1,5},{3,7},{13,9},{15,11},{16,20},{18,... | collective-permute-start | bytes 1179656 | tf_op jit(solution)/shard_map/ppermute | solution.py:180
  139.3 20.8 %collective-permute-start.30 = (bf16[2,96,1280]{2,1,0:T(8,128)(2,1)}, bf16[2,96,1280]{2,1,0:T(8,128)(2,1)}, u32[]{:S(2)}, u32[]{:S(2)}) collective-permute-start(bf16[2,96,1280]{2,1,0:T(8,128)(2,1)} %collective-permute-done.24.side_1), channel_id=1, source_target_pairs={{4,8},{6,10},{8,4},{10,6},{5,9},{7,11},{9,5},{11,7},{20,24},{22,26... | collective-permute-start | bytes 1474568 | tf_op jit(solution)/shard_map/ppermute | solution.py:180
  140.7 19.3 %collective-permute-start.29 = (bf16[2,96,1280]{2,1,0:T(8,128)(2,1)}, bf16[2,96,1280]{2,1,0:T(8,128)(2,1)}, u32[]{:S(2)}, u32[]{:S(2)}) collective-permute-start(bf16[2,96,1280]{2,1,0:T(8,128)(2,1)} %collective-permute-done.25.centre_1), channel_id=1, source_target_pairs={{4,0},{6,2},{8,12},{10,14},{5,1},{7,3},{9,13},{11,15},{20,16},{22,... | collective-permute-start | bytes 1474568 | tf_op jit(solution)/shard_map/ppermute | solution.py:180
  150.8 10.7 %collective-permute-start.31 = (f16[2,192,512]{2,1,0:T(8,128)(2,1)}, f16[2,192,512]{2,1,0:T(8,128)(2,1)}, u32[]{:S(2)}, u32[]{:S(2)}) collective-permute-start(f16[2,192,512]{2,1,0:T(8,128)(2,1)} %get-tuple-element.181), channel_id=1, source_target_pairs={{0,4},{2,6},{12,8},{14,10},{4,0},{6,2},{8,12},{10,14},{1,5},{3,7},... | collective-permute-start | bytes 1179656 | tf_op jit(solution)/shard_map/ppermute | solution.py:180
  153.0 8.5 %collective-permute-start.32 = (f16[2,192,512]{2,1,0:T(8,128)(2,1)}, f16[2,192,512]{2,1,0:T(8,128)(2,1)}, u32[]{:S(2)}, u32[]{:S(2)}) collective-permute-start(f16[2,192,512]{2,1,0:T(8,128)(2,1)} %get-tuple-element.182), channel_id=1, source_target_pairs={{4,8},{6,10},{8,4},{10,6},{5,9},{7,11},{9,5},{11,7},{20,24},{22,26... | collective-permute-start | bytes 1179656 | tf_op jit(solution)/shard_map/ppermute | solution.py:180
  158.4 3.1 %copy-start.15 = (f32[4,2,192,512]{3,2,1,0:T(8,128)S(1)}, f32[4,2,192,512]{3,2,1,0:T(8,128)}, u32[]{:S(2)}) copy-start(f32[4,2,192,512]{3,2,1,0:T(8,128)} %shard_map.71) | copy-start | bytes 9437188
  160.1 20.2 %collective-permute-start.36 = (bf16[2,96,1280]{2,1,0:T(8,128)(2,1)}, bf16[2,96,1280]{2,1,0:T(8,128)(2,1)}, u32[]{:S(2)}, u32[]{:S(2)}) collective-permute-start(bf16[2,96,1280]{2,1,0:T(8,128)(2,1)} %collective-permute-done.30.share_2), channel_id=1, source_target_pairs={{4,0},{6,2},{8,12},{10,14},{5,1},{7,3},{9,13},{11,15},{20,16},{22,... | collective-permute-start | bytes 1474568 | tf_op jit(solution)/shard_map/ppermute | solution.py:180
  162.9 8.2 %copy-start.24 = (bf16[1,96,1280]{2,1,0:T(8,128)(2,1)S(1)}, bf16[1,96,1280]{2,1,0:T(8,128)(2,1)}, u32[]{:S(2)}) copy-start(bf16[1,96,1280]{2,1,0:T(8,128)(2,1)} %get-tuple-element.187) | copy-start | bytes 737284
  162.9 8.2 %copy-start.25 = (bf16[1,96,1280]{2,1,0:T(8,128)(2,1)S(1)}, bf16[1,96,1280]{2,1,0:T(8,128)(2,1)}, u32[]{:S(2)}) copy-start(bf16[1,96,1280]{2,1,0:T(8,128)(2,1)} %get-tuple-element.188) | copy-start | bytes 737284
  164.0 21.6 %collective-permute-start.34 = (bf16[2,192,512]{2,1,0:T(8,128)(2,1)}, bf16[2,192,512]{2,1,0:T(8,128)(2,1)}, u32[]{:S(2)}, u32[]{:S(2)}) collective-permute-start(bf16[2,192,512]{2,1,0:T(8,128)(2,1)} %pad_maximum_fusion.4.act), channel_id=1, source_target_pairs={{4,8},{6,10},{8,4},{10,6},{5,9},{7,11},{9,5},{11,7},{20,24},{22,26... | collective-permute-start | bytes 1179656 | tf_op jit(solution)/shard_map/ppermute | solution.py:180
  165.4 20.2 %collective-permute-start.33 = (bf16[2,192,512]{2,1,0:T(8,128)(2,1)}, bf16[2,192,512]{2,1,0:T(8,128)(2,1)}, u32[]{:S(2)}, u32[]{:S(2)}) collective-permute-start(bf16[2,192,512]{2,1,0:T(8,128)(2,1)} %pad_maximum_fusion.4.act), channel_id=1, source_target_pairs={{0,4},{2,6},{12,8},{14,10},{4,0},{6,2},{8,12},{10,14},{1,5},{3,7},... | collective-permute-start | bytes 1179656 | tf_op jit(solution)/shard_map/ppermute | solution.py:180
  172.1 10.2 %collective-permute-start.35 = (bf16[2,48,1792]{2,1,0:T(8,128)(2,1)}, bf16[2,48,1792]{2,1,0:T(8,128)(2,1)}, u32[]{:S(2)}, u32[]{:S(2)}) collective-permute-start(bf16[2,48,1792]{2,1,0:T(8,128)(2,1)} %get-tuple-element.196), channel_id=1, source_target_pairs={{0,2},{2,0},{4,6},{6,4},{8,10},{10,8},{12,14},{14,12},{1,3},{3,1},... | collective-permute-start | bytes 1032200 | tf_op jit(solution)/shard_map/ppermute | solution.py:180
  180.3 7.3 %copy-start.23 = (bf16[2,48,1792]{2,1,0:T(8,128)(2,1)S(1)}, bf16[2,48,1792]{2,1,0:T(8,128)(2,1)}, u32[]{:S(2)}) copy-start(bf16[2,48,1792]{2,1,0:T(8,128)(2,1)} %get-tuple-element.163) | copy-start | bytes 1032196
  180.3 19.4 %collective-permute-start.40 = (bf16[4,2,96,1280]{3,2,1,0:T(8,128)(2,1)S(1)}, bf16[4,2,96,1280]{3,2,1,0:T(8,128)(2,1)S(1)}, u32[]{:S(2)}, u32[]{:S(2)}) collective-permute-start(bf16[4,2,96,1280]{3,2,1,0:T(8,128)(2,1)S(1)} %shard_map.72), channel_id=1, source_target_pairs={{0,2},{2,0},{4,6},{6,4},{8,10},{10,8},{12,14},{14,12},{1,3},{3,1},... | collective-permute-start | bytes 5898248 | tf_op jit(solution)/shard_map/ppermute | solution.py:180
  184.4 15.3 %collective-permute-start.41 = (bf16[4,2,96,1280]{3,2,1,0:T(8,128)(2,1)S(1)}, bf16[4,2,96,1280]{3,2,1,0:T(8,128)(2,1)S(1)}, u32[]{:S(2)}, u32[]{:S(2)}) collective-permute-start(bf16[4,2,96,1280]{3,2,1,0:T(8,128)(2,1)S(1)} %shard_map.73), channel_id=1, source_target_pairs={{0,2},{2,0},{4,6},{6,4},{8,10},{10,8},{12,14},{14,12},{1,3},{3,1},... | collective-permute-start | bytes 5898248 | tf_op jit(solution)/shard_map/ppermute | solution.py:180
  185.5 11.6 %collective-permute-start.37 = (bf16[2,192,512]{2,1,0:T(8,128)(2,1)}, bf16[2,192,512]{2,1,0:T(8,128)(2,1)S(1)}, u32[]{:S(2)}, u32[]{:S(2)}) collective-permute-start(bf16[2,192,512]{2,1,0:T(8,128)(2,1)} %collective-permute-done.34.centre_1), channel_id=1, source_target_pairs={{4,0},{6,2},{8,12},{10,14},{5,1},{7,3},{9,13},{11,15},{20,16},{22,... | collective-permute-start | bytes 1179656 | tf_op jit(solution)/shard_map/ppermute | solution.py:180
  186.8 10.3 %collective-permute-start.38 = (bf16[2,192,512]{2,1,0:T(8,128)(2,1)}, bf16[2,192,512]{2,1,0:T(8,128)(2,1)S(1)}, u32[]{:S(2)}, u32[]{:S(2)}) collective-permute-start(bf16[2,192,512]{2,1,0:T(8,128)(2,1)} %collective-permute-done.33.side_1), channel_id=1, source_target_pairs={{4,8},{6,10},{8,4},{10,6},{5,9},{7,11},{9,5},{11,7},{20,24},{22,26... | collective-permute-start | bytes 1179656 | tf_op jit(solution)/shard_map/ppermute | solution.py:180
  188.8 9.9 %collective-permute-start.42 = (bf16[48,3584]{1,0:T(8,128)(2,1)S(1)}, bf16[48,3584]{1,0:T(8,128)(2,1)S(1)}, u32[]{:S(2)}, u32[]{:S(2)}) collective-permute-start(bf16[48,3584]{1,0:T(8,128)(2,1)S(1)} %get-tuple-element.194), channel_id=1, source_target_pairs={{0,1},{1,0},{2,3},{3,2},{4,5},{5,4},{6,7},{7,6},{8,9},{9,8},{10,11... | collective-permute-start | bytes 1032200 | tf_op jit(solution)/shard_map/ppermute | solution.py:321
  197.2 12.5 %collective-permute-start.39 = (bf16[2,192,512]{2,1,0:T(8,128)(2,1)S(1)}, bf16[2,192,512]{2,1,0:T(8,128)(2,1)S(1)}, u32[]{:S(2)}, u32[]{:S(2)}) collective-permute-start(bf16[2,192,512]{2,1,0:T(8,128)(2,1)S(1)} %collective-permute-done.38.share_2), channel_id=1, source_target_pairs={{4,0},{6,2},{8,12},{10,14},{5,1},{7,3},{9,13},{11,15},{20,16},{22,... | collective-permute-start | bytes 1179656 | tf_op jit(solution)/shard_map/ppermute | solution.py:180
  211.1 7.0 %collective-permute-start.43 = (bf16[4,2,192,512]{3,2,1,0:T(8,128)(2,1)S(1)}, bf16[4,2,192,512]{3,2,1,0:T(8,128)(2,1)S(1)}, u32[]{:S(2)}, u32[]{:S(2)}) collective-permute-start(bf16[4,2,192,512]{3,2,1,0:T(8,128)(2,1)S(1)} %shard_map.76), channel_id=1, source_target_pairs={{0,2},{2,0},{4,6},{6,4},{8,10},{10,8},{12,14},{14,12},{1,3},{3,1},... | collective-permute-start | bytes 4718600 | tf_op jit(solution)/shard_map/ppermute | solution.py:180
  (9 other events, 15.7 us)
